TPU v7x, 32 devices: a whole 2x2x4 slice. The times are simulated.
32 devices in a mesh: cand: 2 (over y), gz: 4 (over x, core), yx: 4 (over z).
Axes of the slice: x: 2, y: 2, z: 4, core: 2. Of those that a mesh axis runs over, the one named last changes fastest.
Arguments:
- features: bfloat16 [128, 64, 16, 128], P(('cand', 'gz'), 'yx'), parts along dimension 0, may hold values from -20 to 20
- conv_weight: bfloat16 [3, 3, 3, 128, 128], replicated, may hold values from -0.109375 to 0.109375
- gain_mid: float32 [128], replicated, may hold values from 0.5 to 1.5
- offset_mid: float32 [128], replicated, may hold values from -3 to 3
- deep_weight: bfloat16 [3, 3, 3, 128, 256], P(None, None, None, None, 'yx'), may hold values from -0.109375 to 0.109375
- gain_deep: float32 [256], replicated, may hold values from 0.5 to 1.5
- offset_deep: float32 [256], replicated, may hold values from -3 to 3
- up_weight: bfloat16 [256, 128], replicated, may hold values from -0.375 to 0.375
Outputs:
- decoded: bfloat16 [128, 64, 16, 128], P(('cand', 'gz'), 'yx'), parts along dimension 0
There are 2 independent parts, one for each index of `cand`. A program takes and returns all parts, laid end to end along the dimension named above; an argument that names none is the same for every part. Nothing has to cross between parts.
All inputs are finite; a program needn't handle non-finite values.
Results may differ from a plain program's by a relative error of at most 0.01.
Values may be sent and summed in bfloat16 or wider, within the bound.
No kernel may reach another device: no remote copies, remote signals or barrier semaphores. Data moves between devices by JAX's collectives and lax.ppermute only.
A program may use at most 64 MiB of HBM per device.

v0:
```python
import math

import jax
import jax.numpy as jnp
from jax import lax
from jax.sharding import PartitionSpec as P

GROUPS = 32


EPSILON = 1e-05
LAYOUT = ("NDHWC", "DHWIO", "NDHWC")


def padded_2(x, sides, width):
    for axis, dim in sides:
        size, length = (lax.axis_size(axis), x.shape[dim])
        up = [(i, (i + 1) % size) for i in range(size - 1)]
        down = [(j, i) for i, j in up]
        last = lax.slice_in_dim(x, length - width, length, axis=dim)
        initial = lax.slice_in_dim(x, 0, width, axis=dim)
        before = lax.ppermute(last, axis, up)
        after = lax.ppermute(initial, axis, down)
        x = jnp.concatenate([before, x, after], axis=dim)
    return x


def from_behind(block, axis, distance):
    devices = range(lax.axis_size(axis))
    route = [(i - distance, i) for i in devices if i - distance in devices]
    return lax.ppermute(block, axis, route)


def convolve(padded, weight):
    result = lax.conv_general_dilated(
        padded[None],
        weight,
        (1, 1, 1),
        "VALID",
        dimension_numbers=LAYOUT,
        preferred_element_type=jnp.float32,
    )
    return result[0]


def extend_depth(volume):
    return padded_2(volume, (("gz", 0),), 1)


def extend_plane(volume):
    tile_side = math.isqrt(lax.axis_size("yx"))
    column = lax.axis_index("yx") % tile_side
    for axis_dim, stride in ((1, tile_side), (2, 1)):
        length = volume.shape[axis_dim]
        low_edge = lax.slice_in_dim(volume, length - 1, length, axis=axis_dim)
        high_edge = lax.slice_in_dim(volume, 0, 1, axis=axis_dim)
        received = []
        for offset, edge_piece in ((stride, low_edge), (-stride, high_edge)):
            received.append(from_behind(edge_piece, "yx", offset))
        before, after_rim = received
        if stride == 1:
            before = jnp.where(column > 0, before, jnp.zeros_like(before))
            after_rim = jnp.where(column < tile_side - 1, after_rim, jnp.zeros_like(after_rim))
        volume = jnp.concatenate([before, volume, after_rim], axis=axis_dim)
    return volume


def cube_sum(terms):
    return lax.psum(terms, ("gz", "yx"))


def group_norm(values, gain, offset_term, group_width, reduce_sum, count):
    channels = values.shape[-1]
    flat = values.reshape(-1, channels)
    total = reduce_sum(jnp.sum(flat, axis=0).reshape(-1, group_width).sum(axis=1))
    mean_value = total / count
    centered = flat - jnp.repeat(mean_value, group_width)
    spread = (
        reduce_sum(jnp.sum(centered * centered, axis=0).reshape(-1, group_width).sum(axis=1))
        / count
    )
    scaled = centered * jnp.repeat(lax.rsqrt(spread + EPSILON), group_width)
    return jax.nn.silu(scaled.reshape(values.shape) * gain + offset_term).astype(jnp.bfloat16)


def body(
    features, conv_weight, gain_mid, offset_mid, deep_weight, gain_deep, offset_deep, up_weight
):
    edge_len = features.shape[0]
    channels = features.shape[3]
    deep_channels = gain_deep.shape[0]
    tiles_count = lax.axis_size("yx")
    group_mid = channels // GROUPS
    group_deep = deep_channels // GROUPS
    devices_part = lax.axis_size("gz") * tiles_count
    padded = extend_plane(extend_depth(features))
    mid_act = convolve(padded, conv_weight)
    mid_out = group_norm(
        mid_act,
        gain_mid,
        offset_mid,
        group_mid,
        cube_sum,
        float(edge_len**3 * devices_part * group_mid),
    )
    half_edge = edge_len // 2
    pooled = mid_out.astype(jnp.float32).reshape(half_edge, 2, half_edge, 2, half_edge, 2, channels)
    pooled = pooled.mean(axis=(1, 3, 5)).astype(jnp.bfloat16)
    deep_count = float(half_edge**3 * devices_part * group_deep)
    full_kernel = lax.all_gather(deep_weight, "yx", axis=4, tiled=True)
    deep_padded = extend_plane(extend_depth(pooled))
    deep_act = convolve(deep_padded, full_kernel)
    deep_out = group_norm(deep_act, gain_deep, offset_deep, group_deep, cube_sum, deep_count)
    lifted = jnp.dot(
        deep_out.reshape(-1, deep_channels), up_weight, preferred_element_type=jnp.float32
    )
    lifted = lifted.reshape(half_edge, half_edge, half_edge, channels)
    widened = jnp.broadcast_to(
        lifted[:, None, :, None, :, None, :], (half_edge, 2, half_edge, 2, half_edge, 2, channels)
    )
    widened = widened.reshape(edge_len, edge_len, edge_len, channels)
    return (mid_out.astype(jnp.float32) + widened).astype(jnp.bfloat16)


def solution(mesh):
    placed = (
        P(("cand", "gz"), "yx", None, None),
        P(),
        P(),
        P(),
        P(None, None, None, None, "yx"),
        P(),
        P(),
        P(),
    )
    return jax.shard_map(
        body,
        mesh=mesh,
        in_specs=placed,
        out_specs=P(("cand", "gz"), "yx", None, None),
        check_vma=False,
    )
```

profile of v0, /device:TPU:0, one launch (start us, length us, event | category | flops | bytes accessed | tf_op | source)
XLA Modules:
  0.0 236.7 jit_solution(9804729858773444709)
XLA Ops:
  6.5 1.0 fusion.31
  7.5 2.4 collective-permute-start
  9.9 1.3 collective-permute-start.1
  11.2 1.5 constant_dynamic-update-slice_fusion.1
  12.7 2.4 %collective-permute-done.1 = bf16[1,16,16,128]{3,2,1,0:T(8,128)(2,1)S(1)} collective-permute-done((bf16[1,16,16,128]{3,2,1,0:T(8,128)(2,1)S(1)}, bf16[1,16,16,128]{3,2,1,0:T(8,128)(2,1)S(1)}, u32[]{:S(2)}, u32[]{:S(2)}) %collective-permute-start.1) | collective-permute-done | bytes 65568 | tf_op jit(solution)/shard_map/ppermute | solution.py:23
  15.2 4.5 %collective-permute-start.2 = (bf16[18,1,16,128]{3,2,1,0:T(8,128)(2,1)S(1)}, bf16[18,1,16,128]{3,2,1,0:T(8,128)(2,1)S(1)}, u32[]{:S(2)}, u32[]{:S(2)}) collective-permute-start(bf16[18,1,16,128]{3,2,1,0:T(8,128)(2,1)S(1)} %get-tuple-element.7), channel_id=1, source_target_pairs={{0,2},{1,3},{4,6},{5,7},{8,10},{9,11},{12,14},{13,15},{16,18},{17,... | collective-permute-start | bytes 221192 | tf_op jit(solution)/shard_map/ppermute | solution.py:31
  19.7 1.3 collective-permute-start.3
  21.0 0.7 collective-permute-done.2
  21.6 5.2 %collective-permute-done.3 = bf16[18,1,16,128]{3,2,1,0:T(8,128)(2,1)S(1)} collective-permute-done((bf16[18,1,16,128]{3,2,1,0:T(8,128)(2,1)S(1)}, bf16[18,1,16,128]{3,2,1,0:T(8,128)(2,1)S(1)}, u32[]{:S(2)}, u32[]{:S(2)}) %collective-permute-start.3) | collective-permute-done | bytes 73760 | tf_op jit(solution)/shard_map/ppermute | solution.py:31
  26.8 0.3 pad_maximum_fusion.2
  27.1 1.3 collective-permute-start.5
  28.5 4.6 %collective-permute-start.4 = (bf16[18,18,1,128]{3,1,2,0:T(8,128)(2,1)S(1)}, bf16[18,18,1,128]{3,1,2,0:T(8,128)(2,1)S(1)}, u32[]{:S(2)}, u32[]{:S(2)}) collective-permute-start(bf16[18,18,1,128]{3,1,2,0:T(8,128)(2,1)S(1)} %copy.49), channel_id=1, source_target_pairs={{0,1},{1,2},{2,3},{4,5},{5,6},{6,7},{8,9},{9,10},{10,11},{12,13},{... | collective-permute-start | bytes 248840 | tf_op jit(solution)/shard_map/ppermute | solution.py:31
  33.0 1.3 collective-permute-done.5
  34.3 0.2 broadcast_select_fusion
  34.5 1.6 collective-permute-done.4
  36.1 0.2 broadcast_select_fusion.1
  36.3 1.2 maximum_bitcast_fusion
  37.5 1.6 pad
  39.2 5.3 %reshape.107 = bf16[18,18,1,8,3,128]{5,4,3,1,0,2:T(4,128)(2,1)S(1)} reshape(bf16[18,18,1,24,128]{4,3,1,0,2:T(8,128)(2,1)} %pad) | data formatting | bytes 3981312 | tf_op jit(solution)/shard_map/conv_general_dilated | solution.py:35
  44.5 0.3 copy.54
  44.8 0.3 slice.52
  45.2 0.3 copy-done.8
  45.5 13.4 %select_reduce_fusion.1 = (f32[128]{0:T(128)S(1)}, f32[16,16,8,3,128]{4,2,3,1,0:T(8,128)}) fusion(pred[8,3]{0,1:T(4,128)(4,1)S(1)} %copy-done.8, bf16[3,3,3,128,128]{4,3,2,1,0:T(8,128)(2,1)S(1)} %copy-done, bf16[18,18,1,7,2,128]{5,3,4,1,0,2:T(8,128)(2,1)S(1)} %slice.52, bf16[18,18,1,8,3,128]{5,3,4,1,0,2:T(8,128)(2,1)S(1)} %copy.54), kind=kOutput, calls=%fused_computation.9 | convolution fusion | flops 5448130560 | bytes 7182872 | tf_op jit(solution)/shard_map/conv_general_dilated | solution.py:35
  58.9 0.1 reshape.100
  59.0 0.1 reduce_sum.82
  59.1 32.7 %psum.28 = f32[32]{0:T(128)S(1)} all-reduce(f32[32]{0:T(128)S(1)} %reduce_sum.82), channel_id=1, replica_groups=mesh['cand'=2,'gz'=4,'yx'=4] {'gz','yx'}, use_global_device_ids=true, to_apply=%region_2.3 | all-reduce | flops 32 | bytes 256 | tf_op jit(solution)/shard_map/psum | solution.py:69
  91.8 0.1 broadcast_in_dim.28
  91.9 0.1 sub.44
  92.0 4.3 %copy.55 = f32[16,16,8,3,128]{4,1,3,2,0:T(8,128)} copy(f32[16,16,8,3,128]{4,2,3,1,0:T(8,128)} %get-tuple-element.18) | data formatting | bytes 6291456 | tf_op jit(solution)/shard_map/conv_general_dilated | solution.py:35
  96.3 0.9 select_reduce_fusion
  97.1 0.1 reshape.101
  97.2 0.1 reduce_sum.84
  97.4 30.2 %psum.29 = f32[32]{0:T(128)S(1)} all-reduce(f32[32]{0:T(128)S(1)} %reduce_sum.84), channel_id=1, replica_groups=mesh['cand'=2,'gz'=4,'yx'=4] {'gz','yx'}, use_global_device_ids=true, to_apply=%region_5.6 | all-reduce | flops 32 | bytes 256 | tf_op jit(solution)/shard_map/psum | solution.py:69
  127.6 0.1 mul.89
  127.7 1.7 slice.53
  129.5 2.1 convert_reduce_fusion
  131.7 1.3 collective-permute-start.6
  133.0 1.3 collective-permute-start.7
  134.3 3.4 %collective-permute-done.7 = bf16[1,8,8,128]{3,1,2,0:T(8,128)(2,1)S(1)} collective-permute-done((bf16[1,8,8,128]{3,1,2,0:T(8,128)(2,1)S(1)}, bf16[1,8,8,128]{3,1,2,0:T(8,128)(2,1)S(1)}, u32[]{:S(2)}, u32[]{:S(2)}) %collective-permute-start.7) | collective-permute-done | bytes 16416 | tf_op jit(solution)/shard_map/ppermute | solution.py:23
  137.7 1.5 collective-permute-start.8
  139.2 1.3 collective-permute-start.9
  140.5 0.4 collective-permute-done.8
  140.9 5.1 %collective-permute-done.9 = bf16[10,1,8,128]{3,1,2,0:T(2,128)(2,1)S(1)} collective-permute-done((bf16[10,1,8,128]{3,1,2,0:T(2,128)(2,1)S(1)}, bf16[10,1,8,128]{3,1,2,0:T(2,128)(2,1)S(1)}, u32[]{:S(2)}, u32[]{:S(2)}) %collective-permute-start.9) | collective-permute-done | bytes 20512 | tf_op jit(solution)/shard_map/ppermute | solution.py:31
  146.1 4.2 %collective-permute-start.10 = (bf16[10,10,1,128]{3,1,2,0:T(8,128)(2,1)S(1)}, bf16[10,10,1,128]{3,1,2,0:T(8,128)(2,1)S(1)}, u32[]{:S(2)}, u32[]{:S(2)}) collective-permute-start(bf16[10,10,1,128]{3,1,2,0:T(8,128)(2,1)S(1)} %get-tuple-element.11), channel_id=1, source_target_pairs={{0,1},{1,2},{2,3},{4,5},{5,6},{6,7},{8,9},{9,10},{10,11},{12,13},{... | collective-permute-start | bytes 76808 | tf_op jit(solution)/shard_map/ppermute | solution.py:31
  150.3 1.3 collective-permute-start.11
  151.6 0.5 collective-permute-done.10
  152.2 4.3 %collective-permute-done.11 = bf16[10,10,1,128]{3,1,2,0:T(8,128)(2,1)S(1)} collective-permute-done((bf16[10,10,1,128]{3,1,2,0:T(8,128)(2,1)S(1)}, bf16[10,10,1,128]{3,1,2,0:T(8,128)(2,1)S(1)}, u32[]{:S(2)}, u32[]{:S(2)}) %collective-permute-start.11) | collective-permute-done | bytes 25632 | tf_op jit(solution)/shard_map/ppermute | solution.py:31
  156.5 0.2 maximum_bitcast_fusion.1
  156.7 6.2 %fusion.33 = (f32[256]{0:T(256)S(1)}, f32[1,8,8,8,256]{4,0,3,2,1:T(1,128)S(1)}) fusion(bf16[3,3,3,128,256]{3,4,2,1,0:T(8,128)(2,1)} %all-gather.2.cloned.1.call-done, bf16[1,10,10,10,128]{4,2,3,1,0:T(8,128)(2,1)S(1)} %maximum_bitcast_fusion.1), kind=kOutput, calls=%fused_computation.67 | convolution fusion | flops 906100480 | bytes 2550784 | tf_op jit(solution)/shard_map/conv_general_dilated | solution.py:35
  163.0 0.1 reshape.102
  163.1 0.1 reduce_sum.87
  163.2 29.8 %psum.30 = f32[32]{0:T(128)S(1)} all-reduce(f32[32]{0:T(128)S(1)} %reduce_sum.87), channel_id=1, replica_groups=mesh['cand'=2,'gz'=4,'yx'=4] {'gz','yx'}, use_global_device_ids=true, to_apply=%region_9.10 | all-reduce | flops 32 | bytes 256 | tf_op jit(solution)/shard_map/psum | solution.py:69
  193.0 0.1 sub.51
  193.1 0.6 multiply_reduce_fusion
  193.7 0.1 reshape.103
  193.8 0.1 reduce_sum.89
  193.9 31.8 %psum.31 = f32[32]{0:T(128)S(1)} all-reduce(f32[32]{0:T(128)S(1)} %reduce_sum.89), channel_id=1, replica_groups=mesh['cand'=2,'gz'=4,'yx'=4] {'gz','yx'}, use_global_device_ids=true, to_apply=%region_12.13 | all-reduce | flops 32 | bytes 256 | tf_op jit(solution)/shard_map/psum | solution.py:69
  225.9 0.1 mul.101
  226.0 0.2 multiply_convert_fusion.2
  226.2 0.2 fusion.24
  226.4 0.7 broadcast_in_dim.33
  227.1 0.7 copy-done.1
  227.9 0.8 add_convert_fusion
  228.6 1.2 copy.62
  (39 shorter events, 0.6 us)
Async XLA Ops:
  6.5 38.6 %copy-start = (bf16[3,3,3,128,128]{4,3,2,1,0:T(8,128)(2,1)S(1)}, bf16[3,3,3,128,128]{4,3,2,1,0:T(8,128)(2,1)}, u32[]{:S(2)}) copy-start(bf16[3,3,3,128,128]{4,3,2,1,0:T(8,128)(2,1)} %param.9) | copy-start | bytes 2654212
  6.5 150.2 %all-gather.2.cloned.1.call-start = ((), (), s32[]{:S(2)}) async-start(), calls=%async_computation | async-start | bytes 2211840 | tf_op jit(solution)/shard_map/all_gather | solution.py:110
  7.5 3.7 %collective-permute-start = (bf16[1,16,16,128]{3,2,1,0:T(8,128)(2,1)S(1)}, bf16[1,16,16,128]{3,2,1,0:T(8,128)(2,1)S(1)}, u32[]{:S(2)}, u32[]{:S(2)}) collective-permute-start(bf16[1,16,16,128]{3,2,1,0:T(8,128)(2,1)S(1)} %get-tuple-element.10), channel_id=1, source_target_pairs={{0,4},{4,8},{8,12},{1,5},{5,9},{9,13},{2,6},{6,10},{10,14},{3,7},{... | collective-permute-start | bytes 196616 | tf_op jit(solution)/shard_map/ppermute | solution.py:22
  9.9 5.3 %collective-permute-start.1 = (bf16[1,16,16,128]{3,2,1,0:T(8,128)(2,1)S(1)}, bf16[1,16,16,128]{3,2,1,0:T(8,128)(2,1)S(1)}, u32[]{:S(2)}, u32[]{:S(2)}) collective-permute-start(bf16[1,16,16,128]{3,2,1,0:T(8,128)(2,1)S(1)} %get-tuple-element.9), channel_id=1, source_target_pairs={{4,0},{8,4},{12,8},{5,1},{9,5},{13,9},{6,2},{10,6},{14,10},{7,3},{... | collective-permute-start | bytes 196616 | tf_op jit(solution)/shard_map/ppermute | solution.py:23
  15.2 6.5 %collective-permute-start.2 = (bf16[18,1,16,128]{3,2,1,0:T(8,128)(2,1)S(1)}, bf16[18,1,16,128]{3,2,1,0:T(8,128)(2,1)S(1)}, u32[]{:S(2)}, u32[]{:S(2)}) collective-permute-start(bf16[18,1,16,128]{3,2,1,0:T(8,128)(2,1)S(1)} %get-tuple-element.7), channel_id=1, source_target_pairs={{0,2},{1,3},{4,6},{5,7},{8,10},{9,11},{12,14},{13,15},{16,18},{17,... | collective-permute-start | bytes 221192 | tf_op jit(solution)/shard_map/ppermute | solution.py:31
  19.7 7.1 %collective-permute-start.3 = (bf16[18,1,16,128]{3,2,1,0:T(8,128)(2,1)S(1)}, bf16[18,1,16,128]{3,2,1,0:T(8,128)(2,1)S(1)}, u32[]{:S(2)}, u32[]{:S(2)}) collective-permute-start(bf16[18,1,16,128]{3,2,1,0:T(8,128)(2,1)S(1)} %get-tuple-element.8), channel_id=1, source_target_pairs={{2,0},{3,1},{6,4},{7,5},{10,8},{11,9},{14,12},{15,13},{18,16},{19,... | collective-permute-start | bytes 221192 | tf_op jit(solution)/shard_map/ppermute | solution.py:31
  27.1 7.2 %collective-permute-start.5 = (bf16[18,18,1,128]{3,1,2,0:T(8,128)(2,1)S(1)}, bf16[18,18,1,128]{3,1,2,0:T(8,128)(2,1)S(1)}, u32[]{:S(2)}, u32[]{:S(2)}) collective-permute-start(bf16[18,18,1,128]{3,1,2,0:T(8,128)(2,1)S(1)} %copy.51), channel_id=1, source_target_pairs={{1,0},{2,1},{3,2},{5,4},{6,5},{7,6},{9,8},{10,9},{11,10},{13,12},{... | collective-permute-start | bytes 248840 | tf_op jit(solution)/shard_map/ppermute | solution.py:31
  28.5 7.7 %collective-permute-start.4 = (bf16[18,18,1,128]{3,1,2,0:T(8,128)(2,1)S(1)}, bf16[18,18,1,128]{3,1,2,0:T(8,128)(2,1)S(1)}, u32[]{:S(2)}, u32[]{:S(2)}) collective-permute-start(bf16[18,18,1,128]{3,1,2,0:T(8,128)(2,1)S(1)} %copy.49), channel_id=1, source_target_pairs={{0,1},{1,2},{2,3},{4,5},{5,6},{6,7},{8,9},{9,10},{10,11},{12,13},{... | collective-permute-start | bytes 248840 | tf_op jit(solution)/shard_map/ppermute | solution.py:31
  44.8 0.7 copy-start.8
  92.0 4.3 %copy-start.2 = (f32[16,16,8,3,128]{4,2,3,1,0:T(8,128)S(1)}, f32[16,16,8,3,128]{4,2,3,1,0:T(8,128)}, u32[]{:S(2)}) copy-start(f32[16,16,8,3,128]{4,2,3,1,0:T(8,128)} %get-tuple-element.18) | copy-start | bytes 9437188
  127.7 1.8 copy-start.4
  127.7 1.8 copy-start.5
  131.7 2.6 %collective-permute-start.6 = (bf16[1,8,8,128]{3,1,2,0:T(8,128)(2,1)S(1)}, bf16[1,8,8,128]{3,1,2,0:T(8,128)(2,1)S(1)}, u32[]{:S(2)}, u32[]{:S(2)}) collective-permute-start(bf16[1,8,8,128]{3,1,2,0:T(8,128)(2,1)S(1)} %get-tuple-element.15), channel_id=1, source_target_pairs={{0,4},{4,8},{8,12},{1,5},{5,9},{9,13},{2,6},{6,10},{10,14},{3,7},{... | collective-permute-start | bytes 49160 | tf_op jit(solution)/shard_map/ppermute | solution.py:22
  133.0 4.7 %collective-permute-start.7 = (bf16[1,8,8,128]{3,1,2,0:T(8,128)(2,1)S(1)}, bf16[1,8,8,128]{3,1,2,0:T(8,128)(2,1)S(1)}, u32[]{:S(2)}, u32[]{:S(2)}) collective-permute-start(bf16[1,8,8,128]{3,1,2,0:T(8,128)(2,1)S(1)} %get-tuple-element.16), channel_id=1, source_target_pairs={{4,0},{8,4},{12,8},{5,1},{9,5},{13,9},{6,2},{10,6},{14,10},{7,3},{... | collective-permute-start | bytes 49160 | tf_op jit(solution)/shard_map/ppermute | solution.py:23
  137.7 3.2 %collective-permute-start.8 = (bf16[10,1,8,128]{3,1,2,0:T(2,128)(2,1)S(1)}, bf16[10,1,8,128]{3,1,2,0:T(2,128)(2,1)S(1)}, u32[]{:S(2)}, u32[]{:S(2)}) collective-permute-start(bf16[10,1,8,128]{3,1,2,0:T(2,128)(2,1)S(1)} %get-tuple-element.13), channel_id=1, source_target_pairs={{0,2},{1,3},{4,6},{5,7},{8,10},{9,11},{12,14},{13,15},{16,18},{17,... | collective-permute-start | bytes 61448 | tf_op jit(solution)/shard_map/ppermute | solution.py:31
  139.2 6.8 %collective-permute-start.9 = (bf16[10,1,8,128]{3,1,2,0:T(2,128)(2,1)S(1)}, bf16[10,1,8,128]{3,1,2,0:T(2,128)(2,1)S(1)}, u32[]{:S(2)}, u32[]{:S(2)}) collective-permute-start(bf16[10,1,8,128]{3,1,2,0:T(2,128)(2,1)S(1)} %get-tuple-element.14), channel_id=1, source_target_pairs={{2,0},{3,1},{6,4},{7,5},{10,8},{11,9},{14,12},{15,13},{18,16},{19,... | collective-permute-start | bytes 61448 | tf_op jit(solution)/shard_map/ppermute | solution.py:31
  146.1 6.1 %collective-permute-start.10 = (bf16[10,10,1,128]{3,1,2,0:T(8,128)(2,1)S(1)}, bf16[10,10,1,128]{3,1,2,0:T(8,128)(2,1)S(1)}, u32[]{:S(2)}, u32[]{:S(2)}) collective-permute-start(bf16[10,10,1,128]{3,1,2,0:T(8,128)(2,1)S(1)} %get-tuple-element.11), channel_id=1, source_target_pairs={{0,1},{1,2},{2,3},{4,5},{5,6},{6,7},{8,9},{9,10},{10,11},{12,13},{... | collective-permute-start | bytes 76808 | tf_op jit(solution)/shard_map/ppermute | solution.py:31
  150.3 6.1 %collective-permute-start.11 = (bf16[10,10,1,128]{3,1,2,0:T(8,128)(2,1)S(1)}, bf16[10,10,1,128]{3,1,2,0:T(8,128)(2,1)S(1)}, u32[]{:S(2)}, u32[]{:S(2)}) collective-permute-start(bf16[10,10,1,128]{3,1,2,0:T(8,128)(2,1)S(1)} %get-tuple-element.12), channel_id=1, source_target_pairs={{1,0},{2,1},{3,2},{5,4},{6,5},{7,6},{9,8},{10,9},{11,10},{13,12},{... | collective-permute-start | bytes 76808 | tf_op jit(solution)/shard_map/ppermute | solution.py:31
  156.7 69.3 %copy-start.6 = (f32[256]{0:T(256)S(1)}, f32[256]{0:T(256)}, u32[]{:S(2)}) copy-start(f32[256]{0:T(256)} %param.14) | copy-start | bytes 3076
  156.7 69.3 %copy-start.7 = (f32[256]{0:T(256)S(1)}, f32[256]{0:T(256)}, u32[]{:S(2)}) copy-start(f32[256]{0:T(256)} %param.13) | copy-start | bytes 3076
  156.7 69.5 %copy-start.3 = (bf16[256,128]{1,0:T(8,128)(2,1)S(1)}, bf16[256,128]{1,0:T(8,128)(2,1)}, u32[]{:S(2)}) copy-start(bf16[256,128]{1,0:T(8,128)(2,1)} %param.15) | copy-start | bytes 196612
  226.0 1.9 copy-start.1
Sparse Core Ops, SparseCore 0:
  28.5 43.2 all-gather.1
where the time goes:
time: 237 us
  blocking collectives  124 us (52%)
  starting transfers between devices  26.2 us (11%)
  waiting for transfers between devices  24.9 us (11%)
  local copies, waits for them, and re-layouts  20.2 us (9%)
  matrix products  19.9 us (8%)
  between operations  13.8 us (6%)
  other arithmetic  7.25 us (3%)
    psum x4, blocking collectives, cube_sum(): return lax.psum(terms, ('gz', 'yx'))  124 us
    ppermute x8, starting transfers between devices, from_behind(): return lax.ppermute(block, axis, route)  19.9 us
    conv_general_dilated x2, matrix products, convolve(): lax.conv_general_dilated(padded[None], weight, (1, 1, 1), 'VALID', dimens...  19.7 us
    ppermute x8, waiting for transfers between devices, from_behind(): return lax.ppermute(block, axis, route)  19.1 us
    conv_general_dilated x5, local copies, waits for them, and re-layouts, convolve(): lax.conv_general_dilated(padded[None], weight, (1, 1, 1), 'VALID', dimens...  12 us
    ppermute x2, waiting for transfers between devices, padded_2(): after = lax.ppermute(initial, axis, down)  5.77 us
  transfers between devices with their start and end apart: 13, of which 10 were waited for; matrix products, arithmetic and copies ran while one was open for 15% of the time, Pallas kernels for 0%

commit v1 on v0

v1 whole, which is shorter than its diff:
```python
import math

import jax
import jax.numpy as jnp
from jax import lax
from jax.sharding import PartitionSpec as P

GROUPS = 32


EPSILON = 1e-05
LAYOUT = ("NDHWC", "DHWIO", "NDHWC")
PART = ("gz", "yx")


def send(block, axis, distance):
    size = lax.axis_size(axis)
    route = [(i, i + distance) for i in range(size) if 0 <= i + distance < size]
    return lax.ppermute(block, axis, route)


def convolve(padded, weight):
    result = lax.conv_general_dilated(
        padded[None],
        weight,
        (1, 1, 1),
        "VALID",
        dimension_numbers=LAYOUT,
        preferred_element_type=jnp.float32,
    )
    return result[0]


def extend_depth(volume):
    before = send(volume[-1:], "gz", 1)
    after = send(volume[:1], "gz", -1)
    return jnp.concatenate([before, volume, after], axis=0)


def plane_sides(low, high, place, stride, side):
    if side == 2:
        route = [(i, i + stride if (i // stride) % 2 == 0 else i - stride) for i in range(4)]
        got = lax.ppermute(jnp.where(place == 0, high, low), "yx", route)
        none = jnp.zeros_like(got)
        return jnp.where(place == 1, got, none), jnp.where(place == 0, got, none)
    before, after = send(high, "yx", stride), send(low, "yx", -stride)
    none = jnp.zeros_like(before)
    return jnp.where(place > 0, before, none), jnp.where(place < side - 1, after, none)


def extend_plane(volume):
    side = math.isqrt(lax.axis_size("yx"))
    tile = lax.axis_index("yx")
    for dim, stride, place in ((1, side, tile // side), (2, 1, tile % side)):
        length = volume.shape[dim]
        high = lax.slice_in_dim(volume, length - 1, length, axis=dim)
        low = lax.slice_in_dim(volume, 0, 1, axis=dim)
        before, after = plane_sides(low, high, place, stride, side)
        volume = jnp.concatenate([before, volume, after], axis=dim)
    return volume


def group_norm(values, gain, offset_term, width):
    channels = values.shape[-1]
    flat = values.reshape(-1, channels)
    rows = flat.shape[0]
    devices = lax.axis_size("gz") * lax.axis_size("yx")
    mean = jnp.sum(flat, axis=0) / rows
    spread = jnp.sum(jnp.square(flat - mean), axis=0)
    mine = jnp.stack([mean, spread])
    every = lax.all_to_all(jnp.broadcast_to(mine[None], (devices, 2, channels)), PART, 0, 0)
    means = every[:, 0].reshape(devices, -1, width)
    mean = means.mean(axis=(0, 2))
    total = every[:, 1].reshape(devices, -1, width).sum(axis=(0, 2))
    total = total + rows * jnp.square(means - mean[:, None]).sum(axis=(0, 2))
    scale = lax.rsqrt(total / (rows * devices * width) + EPSILON)
    scaled = (flat - jnp.repeat(mean, width)) * jnp.repeat(scale, width)
    return jax.nn.silu(scaled.reshape(values.shape) * gain + offset_term).astype(jnp.bfloat16)


def whole_kernel(weight):
    n = lax.axis_size("yx")
    shards = [weight]
    for k in range(1, n):
        shards.append(lax.ppermute(weight, "yx", [(i, (i + k) % n) for i in range(n)]))
    stack = jnp.stack(shards)
    order = (lax.axis_index("yx") - jnp.arange(n)) % n
    stack = jnp.take(stack, order, axis=0)
    return jnp.moveaxis(stack, 0, 4).reshape(weight.shape[:4] + (n * weight.shape[4],))


def body(
    features, conv_weight, gain_mid, offset_mid, deep_weight, gain_deep, offset_deep, up_weight
):
    edge_len = features.shape[0]
    channels = features.shape[3]
    deep_channels = gain_deep.shape[0]
    padded = extend_plane(extend_depth(features))
    full_kernel = whole_kernel(deep_weight)
    mid_act = convolve(padded, conv_weight)
    mid_out = group_norm(mid_act, gain_mid, offset_mid, channels // GROUPS)
    half_edge = edge_len // 2
    pooled = mid_out.astype(jnp.float32).reshape(half_edge, 2, half_edge, 2, half_edge, 2, channels)
    pooled = pooled.mean(axis=(1, 3, 5)).astype(jnp.bfloat16)
    deep_padded = extend_plane(extend_depth(pooled))
    deep_act = convolve(deep_padded, full_kernel)
    deep_out = group_norm(deep_act, gain_deep, offset_deep, deep_channels // GROUPS)
    lifted = jnp.dot(
        deep_out.reshape(-1, deep_channels), up_weight, preferred_element_type=jnp.float32
    )
    lifted = lifted.reshape(half_edge, half_edge, half_edge, channels)
    widened = jnp.broadcast_to(
        lifted[:, None, :, None, :, None, :], (half_edge, 2, half_edge, 2, half_edge, 2, channels)
    )
    widened = widened.reshape(edge_len, edge_len, edge_len, channels)
    return (mid_out.astype(jnp.float32) + widened).astype(jnp.bfloat16)


def solution(mesh):
    placed = (
        P(("cand", "gz"), "yx", None, None),
        P(),
        P(),
        P(),
        P(None, None, None, None, "yx"),
        P(),
        P(),
        P(),
    )
    return jax.shard_map(
        body,
        mesh=mesh,
        in_specs=placed,
        out_specs=P(("cand", "gz"), "yx", None, None),
        check_vma=False,
    )
```

time: 237 us -> 129 us (0.54)
  blocking collectives: 124 us -> 9.97 us
  waiting for transfers between devices: 24.9 us -> 39.8 us
  between operations: 13.8 us -> 0.49 us
  other arithmetic: 7.25 us -> 11.6 us
  local copies, waits for them, and re-layouts: 20.2 us -> 23.9 us
  matrix products: 19.9 us -> 17.5 us
    psum x4 -> x0, blocking collectives: 124 us -> none  [cube_sum(): return lax.psum(terms, ('gz', 'yx'))]
    ppermute x12 -> x11, waiting for transfers between devices: 24.9 us -> 39.8 us  [the longest x4 33.9 us: plane_sides(): got = lax.ppermute(jnp.where(place == 0, high, low), 'yx', route)]
    all_to_all x0 -> x1, blocking collectives: none -> 9.97 us  [group_norm(): lax.all_to_all(jnp.broadcast_to(mine[None], (devices, 2, channels)), PART...]
    ppermute x12 -> x11, starting transfers between devices: 26.2 us -> 17.9 us  [the longest x4 6.79 us: plane_sides(): got = lax.ppermute(jnp.where(place == 0, high, low), 'yx', route)]
    all_to_all x0 -> x1, starting transfers between devices: none -> 7.49 us  [group_norm(): lax.all_to_all(jnp.broadcast_to(mine[None], (devices, 2, channels)), PART...]
    unnamed x20 -> x26, local copies, waits for them, and re-layouts: 2.58 us -> 6.67 us
    conv_general_dilated x5, local copies, waits for them, and re-layouts: 12 us -> 8.59 us  [convolve(): lax.conv_general_dilated(padded[None], weight, (1, 1, 1), 'VALID', dimens...]
    conv_general_dilated x2, matrix products: 19.7 us -> 17.3 us  [convolve(): lax.conv_general_dilated(padded[None], weight, (1, 1, 1), 'VALID', dimens...]
  transfers between devices with their start and end apart: 13 -> 12, of which waited for: 10 -> 6; matrix products, arithmetic and copies ran while one was open for 15% -> 7% of each run, Pallas kernels for 0% -> 0%
where the time goes in v1:
time: 129 us
  waiting for transfers between devices  39.8 us (31%)
  starting transfers between devices  25.4 us (20%)
  local copies, waits for them, and re-layouts  23.9 us (19%)
  matrix products  17.5 us (14%)
  other arithmetic  11.6 us (9%)
  blocking collectives  9.97 us (8%)
    ppermute x4, waiting for transfers between devices, plane_sides(): got = lax.ppermute(jnp.where(place == 0, high, low), 'yx', route)  33.9 us
    conv_general_dilated x2, matrix products, convolve(): lax.conv_general_dilated(padded[None], weight, (1, 1, 1), 'VALID', dimens...  17.3 us
    all_to_all x1, blocking collectives, group_norm(): lax.all_to_all(jnp.broadcast_to(mine[None], (devices, 2, channels)), PART...  9.97 us
    conv_general_dilated x5, local copies, waits for them, and re-layouts, convolve(): lax.conv_general_dilated(padded[None], weight, (1, 1, 1), 'VALID', dimens...  8.59 us
    all_to_all x1, starting transfers between devices, group_norm(): lax.all_to_all(jnp.broadcast_to(mine[None], (devices, 2, channels)), PART...  7.49 us
    ppermute x4, starting transfers between devices, plane_sides(): got = lax.ppermute(jnp.where(place == 0, high, low), 'yx', route)  6.79 us
    unnamed x26, local copies, waits for them, and re-layouts  6.67 us
    ppermute x4, starting transfers between devices, send(): return lax.ppermute(block, axis, route)  6.23 us
  transfers between devices with their start and end apart: 12, of which 6 were waited for; matrix products, arithmetic and copies ran while one was open for 7% of the time, Pallas kernels for 0%

profile of v1, /device:TPU:0, one launch (start us, length us, event | category | flops | bytes accessed | tf_op | source)
XLA Modules:
  0.0 128.7 jit_solution(1912945858927735246)
XLA Ops:
  0.0 1.0 fusion.37
  1.0 2.4 %collective-permute-start = (bf16[1,16,16,128]{3,2,1,0:T(8,128)(2,1)S(1)}, bf16[1,16,16,128]{3,2,1,0:T(8,128)(2,1)S(1)}, u32[]{:S(2)}, u32[]{:S(2)}) collective-permute-start(bf16[1,16,16,128]{3,2,1,0:T(8,128)(2,1)S(1)} %get-tuple-element.8), channel_id=1, source_target_pairs={{0,4},{4,8},{8,12},{1,5},{5,9},{9,13},{2,6},{6,10},{10,14},{3,7},{... | collective-permute-start | bytes 196616 | tf_op jit(solution)/shard_map/ppermute | solution.py:19
  3.3 1.3 %collective-permute-start.1 = (bf16[1,16,16,128]{3,2,1,0:T(8,128)(2,1)S(1)}, bf16[1,16,16,128]{3,2,1,0:T(8,128)(2,1)S(1)}, u32[]{:S(2)}, u32[]{:S(2)}) collective-permute-start(bf16[1,16,16,128]{3,2,1,0:T(8,128)(2,1)S(1)} %get-tuple-element.7), channel_id=1, source_target_pairs={{4,0},{8,4},{12,8},{5,1},{9,5},{13,9},{6,2},{10,6},{14,10},{7,3},{... | collective-permute-start | bytes 196616 | tf_op jit(solution)/shard_map/ppermute | solution.py:19
  4.7 1.5 %constant_dynamic-update-slice_fusion.1 = bf16[18,16,16,128]{3,2,1,0:T(8,128)(2,1)S(1)} fusion(bf16[18,16,16,128]{3,2,1,0:T(8,128)(2,1)S(1)} %constant_dynamic-update-slice_fusion.2, bf16[16,16,16,128]{3,2,1,0:T(8,128)(2,1)} %param.8), kind=kLoop, calls=%fused_computation.68 | loop fusion | bytes 2097152
  6.2 2.4 %collective-permute-done.1 = bf16[1,16,16,128]{3,2,1,0:T(8,128)(2,1)S(1)} collective-permute-done((bf16[1,16,16,128]{3,2,1,0:T(8,128)(2,1)S(1)}, bf16[1,16,16,128]{3,2,1,0:T(8,128)(2,1)S(1)}, u32[]{:S(2)}, u32[]{:S(2)}) %collective-permute-start.1) | collective-permute-done | bytes 65568 | tf_op jit(solution)/shard_map/ppermute | solution.py:19
  8.6 2.7 %collective-permute-start.2 = (bf16[18,1,16,128]{3,2,1,0:T(8,128)(2,1)S(1)}, bf16[18,1,16,128]{3,2,1,0:T(8,128)(2,1)S(1)}, u32[]{:S(2)}, u32[]{:S(2)}) collective-permute-start(bf16[18,1,16,128]{3,2,1,0:T(8,128)(2,1)S(1)} %slice_select_fusion), channel_id=1, source_target_pairs={{0,2},{1,3},{2,0},{3,1},{4,6},{5,7},{6,4},{7,5},{8,10},{9,11},{10,... | collective-permute-start | bytes 221192 | tf_op jit(solution)/shard_map/ppermute | solution.py:43
  11.3 2.7 %collective-permute-done.2 = bf16[18,1,16,128]{3,2,1,0:T(8,128)(2,1)S(1)} collective-permute-done((bf16[18,1,16,128]{3,2,1,0:T(8,128)(2,1)S(1)}, bf16[18,1,16,128]{3,2,1,0:T(8,128)(2,1)S(1)}, u32[]{:S(2)}, u32[]{:S(2)}) %collective-permute-start.2) | collective-permute-done | bytes 73760 | tf_op jit(solution)/shard_map/ppermute | solution.py:43
  14.0 0.3 broadcast_select_fusion.1
  14.3 1.6 %collective-permute-start.3 = (bf16[18,18,1,128]{3,1,2,0:T(8,128)(2,1)S(1)}, bf16[18,18,1,128]{3,1,2,0:T(8,128)(2,1)S(1)}, u32[]{:S(2)}, u32[]{:S(2)}) collective-permute-start(bf16[18,18,1,128]{3,1,2,0:T(8,128)(2,1)S(1)} %copy.89), channel_id=1, source_target_pairs={{0,1},{1,0},{2,3},{3,2},{4,5},{5,4},{6,7},{7,6},{8,9},{9,8},{10,11... | collective-permute-start | bytes 248840 | tf_op jit(solution)/shard_map/ppermute | solution.py:43
  15.9 3.5 %collective-permute-done.3 = bf16[18,18,1,128]{3,1,2,0:T(8,128)(2,1)S(1)} collective-permute-done((bf16[18,18,1,128]{3,1,2,0:T(8,128)(2,1)S(1)}, bf16[18,18,1,128]{3,1,2,0:T(8,128)(2,1)S(1)}, u32[]{:S(2)}, u32[]{:S(2)}) %collective-permute-start.3) | collective-permute-done | bytes 82976 | tf_op jit(solution)/shard_map/ppermute | solution.py:43
  19.4 0.3 broadcast_select_fusion.2
  19.7 1.2 maximum_bitcast_fusion
  20.9 1.6 %pad = bf16[18,18,1,24,128]{4,3,1,0,2:T(8,128)(2,1)} pad(bf16[18,18,1,18,128]{4,3,1,0,2:T(8,128)(2,1)S(1)} %maximum_bitcast_fusion, bf16[]{:T(256)} %constant.86.clone.1), padding=0_0x0_0x0_0x0_6x0_0 | pad | bytes 3483650 | tf_op jit(solution)/shard_map/broadcast_in_dim | solution.py:24
  22.6 5.3 %reshape.183 = bf16[18,18,1,8,3,128]{5,4,3,1,0,2:T(4,128)(2,1)S(1)} reshape(bf16[18,18,1,24,128]{4,3,1,0,2:T(8,128)(2,1)} %pad) | data formatting | bytes 3981312 | tf_op jit(solution)/shard_map/conv_general_dilated | solution.py:23
  27.8 0.3 copy.93
  28.2 0.3 slice.70
  28.6 0.3 copy-done.11
  28.9 12.4 %select_reduce_fusion.1 = (f32[128]{0:T(128)S(1)}, f32[16,16,8,3,128]{4,2,3,1,0:T(8,128)S(1)}) fusion(pred[8,3]{0,1:T(4,128)(4,1)S(1)} %copy-done.11, bf16[3,3,3,128,128]{4,3,2,1,0:T(8,128)(2,1)S(1)} %copy-done, bf16[18,18,1,7,2,128]{5,3,4,1,0,2:T(8,128)(2,1)S(1)} %slice.70, bf16[18,18,1,8,3,128]{5,3,4,1,0,2:T(8,128)(2,1)S(1)} %copy.93), kind=kOutput, calls=%fused_computation.10 | convolution fusion | flops 5448130560 | bytes 7182872 | tf_op jit(solution)/shard_map/conv_general_dilated | solution.py:23
  41.3 1.6 %copy-done.3 = f32[16,16,8,3,128]{4,2,3,1,0:T(8,128)} copy-done((f32[16,16,8,3,128]{4,2,3,1,0:T(8,128)}, f32[16,16,8,3,128]{4,2,3,1,0:T(8,128)S(1)}, u32[]{:S(2)}) %copy-start.3) | copy-done | bytes 3145752
  42.9 0.9 select_reduce_fusion
  43.8 0.6 broadcast_in_dim.66
  44.5 7.5 %all-to-all-start = ((f32[16,2,128]{2,1,0:T(2,128)}), f32[16,2,128]{2,1,0:T(2,128)S(1)}, u32[]{:S(2)}, u32[]{:S(2)}) async-start(f32[16,2,128]{2,1,0:T(2,128)} %broadcast_in_dim.66), calls=%async_computation | async-start | bytes 32768 | tf_op jit(solution)/shard_map/all_to_all | solution.py:71
  52.0 2.0 %collective-permute-start.8 = (bf16[3,3,3,128,64]{3,4,2,1,0:T(8,128)(2,1)S(1)}, bf16[3,3,3,128,64]{3,4,2,1,0:T(8,128)(2,1)}, u32[]{:S(2)}, u32[]{:S(2)}) collective-permute-start(bf16[3,3,3,128,64]{3,4,2,1,0:T(8,128)(2,1)S(1)} %copy-done.4), channel_id=1, source_target_pairs={{0,1},{1,2},{2,3},{3,0},{4,5},{5,6},{6,7},{7,4},{8,9},{9,10},{10,1... | collective-permute-start | bytes 1327112 | tf_op jit(solution)/shard_map/ppermute | solution.py:85
  53.9 1.9 %collective-permute-start.10 = (bf16[3,3,3,128,64]{3,4,2,1,0:T(8,128)(2,1)S(1)}, bf16[3,3,3,128,64]{3,4,2,1,0:T(8,128)(2,1)}, u32[]{:S(2)}, u32[]{:S(2)}) collective-permute-start(bf16[3,3,3,128,64]{3,4,2,1,0:T(8,128)(2,1)S(1)} %copy-done.4), channel_id=1, source_target_pairs={{0,3},{1,0},{2,1},{3,2},{4,7},{5,4},{6,5},{7,6},{8,11},{9,8},{10,9... | collective-permute-start | bytes 1327112 | tf_op jit(solution)/shard_map/ppermute | solution.py:85
  55.8 1.0 collective-permute-start.9
  56.9 2.4 %copy.94 = f32[16,16,8,3,128]{4,1,3,2,0:T(8,128)S(1)} copy(f32[16,16,8,3,128]{4,2,3,1,0:T(8,128)} %copy-done.3) | data formatting | bytes 6291456 | tf_op jit(solution)/shard_map/conv_general_dilated | solution.py:23
  59.3 1.7 %copy-done.1 = f32[16,16,8,3,128]{4,1,3,2,0:T(8,128)} copy-done((f32[16,16,8,3,128]{4,1,3,2,0:T(8,128)}, f32[16,16,8,3,128]{4,1,3,2,0:T(8,128)S(1)}, u32[]{:S(2)}) %copy-start.1) | copy-done | bytes 3145752
  61.0 0.2 slice.71
  61.3 0.1 reduce_sum.118
  61.4 0.1 reduce_sum.119
  61.6 0.1 sub.97
  61.7 0.1 reduce_sum.150
  61.8 0.1 reduce_sum.151
  61.9 0.1 reduce_sum.124
  62.0 0.1 reduce_sum.148
  62.2 0.1 mul.94
  62.4 2.0 %convert_reduce_fusion = f32[8,8,8,128]{3,2,1,0:T(8,128)S(1)} fusion(f32[128]{0:T(128)S(1)} %copy-done.7, f32[128]{0:T(128)S(1)} %copy-done.8, f32[128]{0:T(128)S(1)} %mul.94, f32[128]{0:T(128)S(1)} %sub.97, f32[8,2,8,2,8,2,128]{6,3,2,5,4,1,0:T(2,128)S(1)} %bitcast.66), kind=kLoop, calls=%fused_computation.20 | loop fusion | flops 5701632 | bytes 2361344 | tf_op jit(solution)/shard_map/reduce_sum | solution.py:104
  64.5 1.3 %collective-permute-start.4 = (bf16[1,8,8,128]{3,1,2,0:T(8,128)(2,1)S(1)}, bf16[1,8,8,128]{3,1,2,0:T(8,128)(2,1)S(1)}, u32[]{:S(2)}, u32[]{:S(2)}) collective-permute-start(bf16[1,8,8,128]{3,1,2,0:T(8,128)(2,1)S(1)} %get-tuple-element.9), channel_id=1, source_target_pairs={{0,4},{4,8},{8,12},{1,5},{5,9},{9,13},{2,6},{6,10},{10,14},{3,7},{... | collective-permute-start | bytes 49160 | tf_op jit(solution)/shard_map/ppermute | solution.py:19
  65.8 1.3 %collective-permute-start.5 = (bf16[1,8,8,128]{3,1,2,0:T(8,128)(2,1)S(1)}, bf16[1,8,8,128]{3,1,2,0:T(8,128)(2,1)S(1)}, u32[]{:S(2)}, u32[]{:S(2)}) collective-permute-start(bf16[1,8,8,128]{3,1,2,0:T(8,128)(2,1)S(1)} %get-tuple-element.10), channel_id=1, source_target_pairs={{4,0},{8,4},{12,8},{5,1},{9,5},{13,9},{6,2},{10,6},{14,10},{7,3},{... | collective-permute-start | bytes 49160 | tf_op jit(solution)/shard_map/ppermute | solution.py:19
  67.1 3.4 %collective-permute-done.5 = bf16[1,8,8,128]{3,1,2,0:T(8,128)(2,1)S(1)} collective-permute-done((bf16[1,8,8,128]{3,1,2,0:T(8,128)(2,1)S(1)}, bf16[1,8,8,128]{3,1,2,0:T(8,128)(2,1)S(1)}, u32[]{:S(2)}, u32[]{:S(2)}) %collective-permute-start.5) | collective-permute-done | bytes 16416 | tf_op jit(solution)/shard_map/ppermute | solution.py:19
  70.6 2.4 %collective-permute-start.6 = (bf16[10,1,8,128]{3,1,2,0:T(2,128)(2,1)S(1)}, bf16[10,1,8,128]{3,1,2,0:T(2,128)(2,1)S(1)}, u32[]{:S(2)}, u32[]{:S(2)}) collective-permute-start(bf16[10,1,8,128]{3,1,2,0:T(2,128)(2,1)S(1)} %broadcast_select_fusion.4), channel_id=1, source_target_pairs={{0,2},{1,3},{2,0},{3,1},{4,6},{5,7},{6,4},{7,5},{8,10},{9,11},{10,... | collective-permute-start | bytes 61448 | tf_op jit(solution)/shard_map/ppermute | solution.py:43
  73.0 23.7 %collective-permute-done.6 = bf16[10,1,8,128]{3,1,2,0:T(2,128)(2,1)S(1)} collective-permute-done((bf16[10,1,8,128]{3,1,2,0:T(2,128)(2,1)S(1)}, bf16[10,1,8,128]{3,1,2,0:T(2,128)(2,1)S(1)}, u32[]{:S(2)}, u32[]{:S(2)}) %collective-permute-start.6) | collective-permute-done | bytes 20512 | tf_op jit(solution)/shard_map/ppermute | solution.py:43
  97.0 4.0 %collective-permute-done.7 = bf16[10,10,1,128]{3,1,2,0:T(8,128)(2,1)S(1)} collective-permute-done((bf16[10,10,1,128]{3,1,2,0:T(8,128)(2,1)S(1)}, bf16[10,10,1,128]{3,1,2,0:T(8,128)(2,1)S(1)}, u32[]{:S(2)}, u32[]{:S(2)}) %collective-permute-start.7) | collective-permute-done | bytes 25632 | tf_op jit(solution)/shard_map/ppermute | solution.py:43
  101.0 1.0 maximum_bitcast_fusion.1
  102.0 1.5 %pad_maximum_fusion = bf16[4,3,3,3,128,64]{4,5,3,2,1,0:T(8,128)(2,1)S(1)} fusion(bf16[1,3,3,3,128,64]{4,5,3,2,1,0:T(8,128)(2,1)} %bitcast.12, bf16[1,3,3,3,128,64]{4,5,3,2,1,0:T(8,128)(2,1)} %bitcast.11, bf16[1,3,3,3,128,64]{4,5,3,2,1,0:T(8,128)(2,1)} %bitcast.10, bf16[1,3,3,3,128,64]{4,5,3,2,1,0:T(8,128)(2,1)S(1)} %bitcast.68), kind=kLoop, calls=%fused_computation.24 | loop fusion | flops 2654208 | bytes 3538944 | tf_op jit(solution)/shard_map/stack | solution.py:86
  103.5 2.0 %gather_fusion = bf16[4,3,3,3,128,64]{4,5,3,2,1,0:T(8,128)(2,1)} fusion(bf16[4,3,3,3,128,64]{4,5,3,2,1,0:T(8,128)(2,1)S(1)} %pad_maximum_fusion, s32[1024]{0:T(1024)S(1)} %pad_clamp_fusion), kind=kCustom, calls=%fused_computation | custom fusion | bytes 3538960 | tf_op jit(solution)/shard_map/jit(_take)/gather | solution.py:88
  105.5 1.7 %select_bitcast_fusion = bf16[3,3,3,128,4,64]{3,5,2,1,0,4:T(8,128)(2,1)S(1)} fusion(bf16[4,3,3,3,128,64]{4,5,3,2,1,0:T(8,128)(2,1)} %gather_fusion, pred[4]{0:T(512)(128)(4,1)S(1)} %compare_and_fusion), kind=kLoop, calls=%fused_computation.25 | loop fusion | flops 884736 | bytes 3538948 | tf_op jit(solution)/shard_map/jit(_take)/select_n | solution.py:88
  107.2 0.2 copy.101
  107.4 0.8 copy-done.5
  108.2 4.9 %fusion.40 = (f32[256]{0:T(256)S(1)}, f32[1,8,8,8,256]{4,0,3,2,1:T(1,128)S(1)}) fusion(bf16[3,3,3,128,256]{3,4,2,1,0:T(8,128)(2,1)S(1)} %bitcast.67, bf16[1,10,10,10,128]{4,2,3,1,0:T(8,128)(2,1)S(1)} %copy-done.5), kind=kOutput, calls=%fused_computation.99 | convolution fusion | flops 906100480 | bytes 2550784 | tf_op jit(solution)/shard_map/conv_general_dilated | solution.py:23
  113.1 0.6 multiply_reduce_fusion
  113.7 10.0 %all_to_all.10 = f32[16,2,256]{2,1,0:T(2,128)S(1)} all-to-all(f32[16,2,256]{2,1,0:T(2,128)S(1)} %broadcast_in_dim.74), channel_id=1, replica_groups=mesh['cand'=2,'gz'=4,'yx'=4] {'gz','yx'}, dimensions={0} | all-to-all | bytes 65536 | tf_op jit(solution)/shard_map/all_to_all | solution.py:71
  123.7 0.1 reduce_sum.156
  123.8 0.1 reduce_sum.157
  124.0 0.1 sub.110
  124.2 0.1 reduce_sum.163
  124.4 0.1 reduce_sum.160
  124.6 0.1 mul.107
  124.8 0.2 multiply_convert_fusion.2
  125.0 0.2 fusion.24
  125.2 0.7 broadcast_in_dim.77
  125.9 0.7 copy-done.2
  126.7 0.8 add_convert_fusion
  127.4 1.2 copy.106
  (61 shorter events, 1.1 us)
Async XLA Ops:
  0.0 28.6 %copy-start = (bf16[3,3,3,128,128]{4,3,2,1,0:T(8,128)(2,1)S(1)}, bf16[3,3,3,128,128]{4,3,2,1,0:T(8,128)(2,1)}, u32[]{:S(2)}) copy-start(bf16[3,3,3,128,128]{4,3,2,1,0:T(8,128)(2,1)} %param.9) | copy-start | bytes 2654212
  1.0 3.7 %collective-permute-start = (bf16[1,16,16,128]{3,2,1,0:T(8,128)(2,1)S(1)}, bf16[1,16,16,128]{3,2,1,0:T(8,128)(2,1)S(1)}, u32[]{:S(2)}, u32[]{:S(2)}) collective-permute-start(bf16[1,16,16,128]{3,2,1,0:T(8,128)(2,1)S(1)} %get-tuple-element.8), channel_id=1, source_target_pairs={{0,4},{4,8},{8,12},{1,5},{5,9},{9,13},{2,6},{6,10},{10,14},{3,7},{... | collective-permute-start | bytes 196616 | tf_op jit(solution)/shard_map/ppermute | solution.py:19
  3.3 5.3 %collective-permute-start.1 = (bf16[1,16,16,128]{3,2,1,0:T(8,128)(2,1)S(1)}, bf16[1,16,16,128]{3,2,1,0:T(8,128)(2,1)S(1)}, u32[]{:S(2)}, u32[]{:S(2)}) collective-permute-start(bf16[1,16,16,128]{3,2,1,0:T(8,128)(2,1)S(1)} %get-tuple-element.7), channel_id=1, source_target_pairs={{4,0},{8,4},{12,8},{5,1},{9,5},{13,9},{6,2},{10,6},{14,10},{7,3},{... | collective-permute-start | bytes 196616 | tf_op jit(solution)/shard_map/ppermute | solution.py:19
  8.6 5.3 %collective-permute-start.2 = (bf16[18,1,16,128]{3,2,1,0:T(8,128)(2,1)S(1)}, bf16[18,1,16,128]{3,2,1,0:T(8,128)(2,1)S(1)}, u32[]{:S(2)}, u32[]{:S(2)}) collective-permute-start(bf16[18,1,16,128]{3,2,1,0:T(8,128)(2,1)S(1)} %slice_select_fusion), channel_id=1, source_target_pairs={{0,2},{1,3},{2,0},{3,1},{4,6},{5,7},{6,4},{7,5},{8,10},{9,11},{10,... | collective-permute-start | bytes 221192 | tf_op jit(solution)/shard_map/ppermute | solution.py:43
  14.3 5.2 %collective-permute-start.3 = (bf16[18,18,1,128]{3,1,2,0:T(8,128)(2,1)S(1)}, bf16[18,18,1,128]{3,1,2,0:T(8,128)(2,1)S(1)}, u32[]{:S(2)}, u32[]{:S(2)}) collective-permute-start(bf16[18,18,1,128]{3,1,2,0:T(8,128)(2,1)S(1)} %copy.89), channel_id=1, source_target_pairs={{0,1},{1,0},{2,3},{3,2},{4,5},{5,4},{6,7},{7,6},{8,9},{9,8},{10,11... | collective-permute-start | bytes 248840 | tf_op jit(solution)/shard_map/ppermute | solution.py:43
  28.2 0.7 copy-start.11
  41.3 1.7 %copy-start.3 = (f32[16,16,8,3,128]{4,2,3,1,0:T(8,128)}, f32[16,16,8,3,128]{4,2,3,1,0:T(8,128)S(1)}, u32[]{:S(2)}) copy-start(f32[16,16,8,3,128]{4,2,3,1,0:T(8,128)S(1)} %get-tuple-element.25) | copy-start | bytes 9437188
  41.3 10.7 %copy-start.4 = (bf16[3,3,3,128,64]{3,4,2,1,0:T(8,128)(2,1)S(1)}, bf16[3,3,3,128,64]{3,4,2,1,0:T(8,128)(2,1)}, u32[]{:S(2)}) copy-start(bf16[3,3,3,128,64]{3,4,2,1,0:T(8,128)(2,1)} %param.12) | copy-start | bytes 1327108
  44.5 16.7 %all-to-all-start = ((f32[16,2,128]{2,1,0:T(2,128)}), f32[16,2,128]{2,1,0:T(2,128)S(1)}, u32[]{:S(2)}, u32[]{:S(2)}) async-start(f32[16,2,128]{2,1,0:T(2,128)} %broadcast_in_dim.66), calls=%async_computation | async-start | bytes 32768 | tf_op jit(solution)/shard_map/all_to_all | solution.py:71
  52.0 50.0 %collective-permute-start.8 = (bf16[3,3,3,128,64]{3,4,2,1,0:T(8,128)(2,1)S(1)}, bf16[3,3,3,128,64]{3,4,2,1,0:T(8,128)(2,1)}, u32[]{:S(2)}, u32[]{:S(2)}) collective-permute-start(bf16[3,3,3,128,64]{3,4,2,1,0:T(8,128)(2,1)S(1)} %copy-done.4), channel_id=1, source_target_pairs={{0,1},{1,2},{2,3},{3,0},{4,5},{5,6},{6,7},{7,4},{8,9},{9,10},{10,1... | collective-permute-start | bytes 1327112 | tf_op jit(solution)/shard_map/ppermute | solution.py:85
  53.9 48.0 %collective-permute-start.10 = (bf16[3,3,3,128,64]{3,4,2,1,0:T(8,128)(2,1)S(1)}, bf16[3,3,3,128,64]{3,4,2,1,0:T(8,128)(2,1)}, u32[]{:S(2)}, u32[]{:S(2)}) collective-permute-start(bf16[3,3,3,128,64]{3,4,2,1,0:T(8,128)(2,1)S(1)} %copy-done.4), channel_id=1, source_target_pairs={{0,3},{1,0},{2,1},{3,2},{4,7},{5,4},{6,5},{7,6},{8,11},{9,8},{10,9... | collective-permute-start | bytes 1327112 | tf_op jit(solution)/shard_map/ppermute | solution.py:85
  55.8 46.1 %collective-permute-start.9 = (bf16[3,3,3,128,64]{3,4,2,1,0:T(8,128)(2,1)S(1)}, bf16[3,3,3,128,64]{3,4,2,1,0:T(8,128)(2,1)}, u32[]{:S(2)}, u32[]{:S(2)}) collective-permute-start(bf16[3,3,3,128,64]{3,4,2,1,0:T(8,128)(2,1)S(1)} %copy-done.4), channel_id=1, source_target_pairs={{0,2},{1,3},{2,0},{3,1},{4,6},{5,7},{6,4},{7,5},{8,10},{9,11},{10,... | collective-permute-start | bytes 1327112 | tf_op jit(solution)/shard_map/ppermute | solution.py:85
  59.3 1.7 %copy-start.1 = (f32[16,16,8,3,128]{4,1,3,2,0:T(8,128)}, f32[16,16,8,3,128]{4,1,3,2,0:T(8,128)S(1)}, u32[]{:S(2)}) copy-start(f32[16,16,8,3,128]{4,1,3,2,0:T(8,128)S(1)} %copy.94) | copy-start | bytes 9437188
  61.0 1.4 %copy-start.7 = (f32[128]{0:T(128)S(1)}, f32[128]{0:T(128)}, u32[]{:S(2)}) copy-start(f32[128]{0:T(128)} %param.11) | copy-start | bytes 1540
  61.0 1.4 %copy-start.8 = (f32[128]{0:T(128)S(1)}, f32[128]{0:T(128)}, u32[]{:S(2)}) copy-start(f32[128]{0:T(128)} %param.10) | copy-start | bytes 1540
  64.5 2.6 %collective-permute-start.4 = (bf16[1,8,8,128]{3,1,2,0:T(8,128)(2,1)S(1)}, bf16[1,8,8,128]{3,1,2,0:T(8,128)(2,1)S(1)}, u32[]{:S(2)}, u32[]{:S(2)}) collective-permute-start(bf16[1,8,8,128]{3,1,2,0:T(8,128)(2,1)S(1)} %get-tuple-element.9), channel_id=1, source_target_pairs={{0,4},{4,8},{8,12},{1,5},{5,9},{9,13},{2,6},{6,10},{10,14},{3,7},{... | collective-permute-start | bytes 49160 | tf_op jit(solution)/shard_map/ppermute | solution.py:19
  65.8 4.8 %collective-permute-start.5 = (bf16[1,8,8,128]{3,1,2,0:T(8,128)(2,1)S(1)}, bf16[1,8,8,128]{3,1,2,0:T(8,128)(2,1)S(1)}, u32[]{:S(2)}, u32[]{:S(2)}) collective-permute-start(bf16[1,8,8,128]{3,1,2,0:T(8,128)(2,1)S(1)} %get-tuple-element.10), channel_id=1, source_target_pairs={{4,0},{8,4},{12,8},{5,1},{9,5},{13,9},{6,2},{10,6},{14,10},{7,3},{... | collective-permute-start | bytes 49160 | tf_op jit(solution)/shard_map/ppermute | solution.py:19
  70.6 26.2 %collective-permute-start.6 = (bf16[10,1,8,128]{3,1,2,0:T(2,128)(2,1)S(1)}, bf16[10,1,8,128]{3,1,2,0:T(2,128)(2,1)S(1)}, u32[]{:S(2)}, u32[]{:S(2)}) collective-permute-start(bf16[10,1,8,128]{3,1,2,0:T(2,128)(2,1)S(1)} %broadcast_select_fusion.4), channel_id=1, source_target_pairs={{0,2},{1,3},{2,0},{3,1},{4,6},{5,7},{6,4},{7,5},{8,10},{9,11},{10,... | collective-permute-start | bytes 61448 | tf_op jit(solution)/shard_map/ppermute | solution.py:43
  96.9 4.1 %collective-permute-start.7 = (bf16[10,10,1,128]{3,1,2,0:T(8,128)(2,1)S(1)}, bf16[10,10,1,128]{3,1,2,0:T(8,128)(2,1)S(1)}, u32[]{:S(2)}, u32[]{:S(2)}) collective-permute-start(bf16[10,10,1,128]{3,1,2,0:T(8,128)(2,1)S(1)} %fusion.27), channel_id=1, source_target_pairs={{0,1},{1,0},{2,3},{3,2},{4,5},{5,4},{6,7},{7,6},{8,9},{9,8},{10,11... | collective-permute-start | bytes 76808 | tf_op jit(solution)/shard_map/ppermute | solution.py:43
  107.2 1.0 copy-start.5
  108.2 16.6 %copy-start.9 = (f32[256]{0:T(256)S(1)}, f32[256]{0:T(256)}, u32[]{:S(2)}) copy-start(f32[256]{0:T(256)} %param.14) | copy-start | bytes 3076
  108.2 16.6 %copy-start.10 = (f32[256]{0:T(256)S(1)}, f32[256]{0:T(256)}, u32[]{:S(2)}) copy-start(f32[256]{0:T(256)} %param.13) | copy-start | bytes 3076
  108.2 16.8 %copy-start.6 = (bf16[256,128]{1,0:T(8,128)(2,1)S(1)}, bf16[256,128]{1,0:T(8,128)(2,1)}, u32[]{:S(2)}) copy-start(bf16[256,128]{1,0:T(8,128)(2,1)} %param.15) | copy-start | bytes 196612
  124.8 1.9 %copy-start.2 = (f32[16,16,8,3,128]{4,1,3,2,0:T(8,128)S(1)}, f32[16,16,8,3,128]{4,1,3,2,0:T(8,128)}, u32[]{:S(2)}) copy-start(f32[16,16,8,3,128]{4,1,3,2,0:T(8,128)} %copy-done.1) | copy-start | bytes 9437188

commit v2 on v1

v2 whole, which is shorter than its diff:
```python
import functools
import math

import jax
import jax.numpy as jnp
from jax import lax
from jax.experimental import pallas as pl
from jax.experimental.pallas import tpu as pltpu
from jax.sharding import PartitionSpec as P

GROUPS = 32
EPSILON = 1e-05
PART = ("gz", "yx")
VMEM_BYTES = 32 * 1024 * 1024
HIGHEST = lax.Precision.HIGHEST


class Square:
    def __init__(self):
        self.tiles = lax.axis_size("yx")
        self.side = math.isqrt(self.tiles)
        tile = lax.axis_index("yx")
        self.row, self.column = tile // self.side, tile % self.side
        self.folded = self.side == 2
        self.steps = (0,) if self.folded else (-1, 1)

    def low_sides(self):
        if self.folded:
            return [self.row], [self.column]
        return [1, 0], [1, 0]

    def route(self, down, right):
        pairs = []
        for tile in range(self.tiles):
            row, column = tile // self.side + down, tile % self.side + right
            if 0 <= row < self.side and 0 <= column < self.side:
                pairs.append((tile, row * self.side + column))
        return pairs

    def swap_route(self, mask):
        return [(tile, tile ^ mask) for tile in range(self.tiles)]

    def halos(self, y_edges, x_edges, corners):
        if self.folded:
            y = lax.ppermute(y_edges[0], "yx", self.swap_route(2))
            x = lax.ppermute(x_edges[0], "yx", self.swap_route(1))
            corner = lax.ppermute(corners[0], "yx", self.swap_route(3))
            return [y], [x], [corner]
        y = [lax.ppermute(y_edges[k], "yx", self.route((1, -1)[1 - k], 0)) for k in (1, 0)]
        x = [lax.ppermute(x_edges[k], "yx", self.route(0, (1, -1)[1 - k])) for k in (1, 0)]
        corner = [
            lax.ppermute(corners[2 * k + j], "yx", self.route((1, -1)[1 - k], (1, -1)[1 - j]))
            for k in (1, 0)
            for j in (1, 0)
        ]
        return y, x, corner

    def edges(self, volume):
        if self.folded:
            low_y, low_x = self.row == 1, self.column == 1
            y = jnp.where(low_y, volume[:, 0], volume[:, -1])
            x = jnp.where(low_x, volume[:, :, 0], volume[:, :, -1])
            corner = jnp.where(low_x, y[:, 0], y[:, -1])
            return [y], [x], [corner]
        y = [volume[:, 0], volume[:, -1]]
        x = [volume[:, :, 0], volume[:, :, -1]]
        return y, x, [row[:, k] for row in y for k in (0, -1)]


def swap_depth(low, high):
    size = lax.axis_size("gz")
    up = [(i, i + 1) for i in range(size - 1)]
    return lax.ppermute(high, "gz", up), lax.ppermute(low, "gz", [(j, i) for i, j in up])


def depth_face(volume, y, x, corner, at):
    edge, channels = volume.shape[2:]
    pad = jnp.zeros((edge - len(corner), channels), volume.dtype)
    last = jnp.concatenate([piece[at][None] for piece in corner] + [pad])
    rows = [volume[at]] + [piece[at][None] for piece in y + x] + [last[None]]
    return jnp.concatenate(rows)


def gather_shards(weight):
    tiles = lax.axis_size("yx")
    half = weight.shape[1] // 2
    odd = lax.axis_index("gz") % 2
    mine = weight
    if half % 16 == 0:
        mine = jnp.where(odd == 1, weight[:, half:], weight[:, :half])
    got = [
        lax.ppermute(mine, "yx", [(i, (i + k) % tiles) for i in range(tiles)]) for k in range(1, tiles)
    ]
    return got


def swap_halves(got, whole):
    if whole:
        return got
    pairs = [(i, i ^ 1) for i in range(lax.axis_size("gz"))]
    return lax.ppermute(got, "gz", pairs)


def share(statistics):
    return lax.all_to_all(statistics, PART, 0, 0)


def call(kernel, outs, scratch, scalars, *arrays, flops=0, nbytes=0):
    smem, vmem = pl.BlockSpec(memory_space=pltpu.SMEM), pl.BlockSpec(memory_space=pltpu.VMEM)
    return pl.pallas_call(
        kernel,
        out_shape=[jax.ShapeDtypeStruct(shape, dtype) for shape, dtype in outs],
        in_specs=[smem] + [vmem] * len(arrays),
        out_specs=[vmem] * len(outs),
        scratch_shapes=[pltpu.VMEM(shape, dtype) for shape, dtype in scratch],
        compiler_params=pltpu.CompilerParams(vmem_limit_bytes=VMEM_BYTES),
        cost_estimate=pl.CostEstimate(flops=flops, bytes_accessed=nbytes, transcendentals=0),
    )(scalars, *arrays)


def mid_kernel(ny, nx, pos, x, *refs):
    y_halos, x_halos, corners = refs[0], refs[1], refs[2]
    front, back, weight, act, stats, grid, taps, column, flanks = refs[3:]
    edge = x.shape[0]
    f32 = jnp.float32
    for dz in range(3):
        for dy in range(3):
            row = (dz * 3 + dy) * 128
            for dx in range(3):
                taps[row : row + 128, dx * 128 : dx * 128 + 128] = weight[dz * 9 + dy * 3 + dx]
    grid[1 : edge + 1, 1 : edge + 1] = x[...]
    grid[0, 1 : edge + 1] = front[0:edge]
    grid[edge + 1, 1 : edge + 1] = back[0:edge]
    blank = jnp.zeros((edge + 2,) + grid.shape[2:], grid.dtype)
    grid[:, 0] = blank
    grid[:, edge + 1] = blank
    for i in range(ny):
        at = jnp.where(pos[i] == 1, 0, edge + 1)
        grid[1 : edge + 1, at] = y_halos[i]
        grid[0, at] = front[edge + i]
        grid[edge + 1, at] = back[edge + i]

    act[...] = jnp.zeros(act.shape, f32)
    flat = act.reshape(edge**3, 128)
    for j in range(nx):
        column[:, 0:8] = jnp.zeros((edge + 2, 8, 128), f32)
        column[:, 8 + edge :] = jnp.zeros((edge + 2, 8, 128), f32)
        column[1 : edge + 1, 8 : 8 + edge] = x_halos[j].astype(f32)
        column[0, 8 : 8 + edge] = front[edge + ny + j].astype(f32)
        column[edge + 1, 8 : 8 + edge] = back[edge + ny + j].astype(f32)
        rows = edge + 16
        lines = column.reshape((edge + 2) * rows, 128)
        for i in range(ny):
            k = i * nx + j
            ends = [front[edge + ny + nx, k : k + 1], corners[k], back[edge + ny + nx, k : k + 1]]
            ends = jnp.concatenate([e.astype(f32) for e in ends], axis=0)
            low = pos[i] == 1
            if ny == 1:
                lines[pl.ds(7, edge + 2, stride=rows), :] = jnp.where(low, ends, 0.0)
                lines[pl.ds(8 + edge, edge + 2, stride=rows), :] = jnp.where(low, 0.0, ends)
            else:
                lines[pl.ds(7 if i == 0 else 8 + edge, edge + 2, stride=rows), :] = ends
        for dy in range(3):
            piece = column[:, 7 + dy : 7 + dy + edge].astype(jnp.bfloat16)
            flanks[:, :, dy * 128 : dy * 128 + 128] = piece
        left = jnp.concatenate(
            [flanks[dz : dz + edge].reshape(edge * edge, 384) for dz in range(3)], axis=1
        )
        right = jnp.concatenate([taps[:, 0:128], taps[:, 256:384]], axis=1)
        extra = jnp.dot(left, right, preferred_element_type=f32)
        low = pos[ny + j] == 1
        if nx == 1:
            flat[pl.ds(0, edge * edge, stride=edge), :] = jnp.where(low, extra[:, :128], 0.0)
            flat[pl.ds(edge - 1, edge * edge, stride=edge), :] = jnp.where(low, 0.0, extra[:, 128:])
        elif j == 0:
            flat[pl.ds(0, edge * edge, stride=edge), :] = extra[:, :128]
        else:
            flat[pl.ds(edge - 1, edge * edge, stride=edge), :] = extra[:, 128:]

    planes = 2
    rows = planes * edge * edge
    place = lax.broadcasted_iota(jnp.int32, (planes * edge, edge, 128), 1)

    def step(k, carry):
        z = k * planes
        left = jnp.concatenate(
            [
                grid[pl.ds(z + dz, planes), dy : dy + edge].reshape(rows, 128)
                for dz in range(3)
                for dy in range(3)
            ],
            axis=1,
        )
        wide = jnp.dot(left, taps[...], preferred_element_type=f32)
        wide = wide.reshape(planes * edge, edge, 384)
        after = jnp.where(place > 0, pltpu.roll(wide[:, :, :128], 1, 1), 0.0)
        before = jnp.where(place < edge - 1, pltpu.roll(wide[:, :, 256:], edge - 1, 1), 0.0)
        old = act[pl.ds(z, planes)].reshape(planes * edge, edge, 128)
        new = old + wide[:, :, 128:256] + after + before
        act[pl.ds(z, planes)] = new.reshape(planes, edge, edge, 128)
        return carry + jnp.sum(new.reshape(rows // 8, 8, 128), axis=0)

    total = lax.fori_loop(0, edge // planes, step, jnp.zeros((8, 128), f32))
    mean = jnp.sum(total, axis=0, keepdims=True) / edge**3

    def spread_step(k, carry):
        off = act[pl.ds(k * planes, planes)].reshape(rows // 8, 8, 128) - mean
        return carry + jnp.sum(off * off, axis=0)

    total = lax.fori_loop(0, edge // planes, spread_step, jnp.zeros((8, 128), f32))
    spread = jnp.sum(total, axis=0, keepdims=True)
    put_stats(stats, mean, spread)


def put_stats(stats, mean, spread):
    line = lax.broadcasted_iota(jnp.int32, stats.shape[1:], 0)
    both = jnp.where(line == 0, mean, spread)
    stats[...] = jnp.broadcast_to(both[None], stats.shape)


def read_stats(stats, rows):
    devices, _, channels = stats.shape
    width = channels // GROUPS
    means = stats[:, 0, :]
    spreads = stats[:, 1, :]
    line = lax.broadcasted_iota(jnp.int32, (channels, channels), 0) // width
    same = line == lax.broadcasted_iota(jnp.int32, (channels, channels), 1) // width
    same = same.astype(jnp.float32)

    def grouped(row):
        row = jnp.broadcast_to(row, (8, channels))
        return jnp.dot(row, same, precision=HIGHEST, preferred_element_type=jnp.float32)[0:1]

    mean = grouped(jnp.sum(means, axis=0, keepdims=True)) / (devices * width)
    off = means - mean
    total = grouped(jnp.sum(spreads + rows * (off * off), axis=0, keepdims=True))
    return mean, lax.rsqrt(total / (rows * devices * width) + EPSILON)


def silu(u):
    return u / (1.0 + jnp.exp(-u))


def norm_kernel(ny, nx, pos, act, stats, gain, offset, out, pooled, *refs):
    y_edges, x_edges, corners, half, fine = refs
    edge = act.shape[0]
    deep = edge // 2
    f32 = jnp.float32
    mean, scale = read_stats(stats, float(edge**3))
    scale = scale * gain[...]
    shift = offset[...]

    def step(k, _):
        value = silu((act[pl.ds(2 * k, 2)] - mean) * scale + shift).astype(jnp.bfloat16)
        out[pl.ds(2 * k, 2)] = value
        value = value.astype(f32)
        value = value[0] + value[1]
        value = value.reshape(deep, 2, edge, 128)
        half[...] = (value[:, 0] + value[:, 1]).reshape(deep * edge, 128)
        pair = half[pl.ds(0, deep * deep, stride=2), :] + half[pl.ds(1, deep * deep, stride=2), :]
        pair = (pair * 0.125).astype(jnp.bfloat16).astype(f32)
        fine[pl.ds(k, 1)] = pair.reshape(1, deep, deep, 128)
        return 0

    lax.fori_loop(0, deep, step, 0)
    pooled[...] = fine[...]
    lines = fine.reshape(deep**3, 128)
    low, high = ((pos[0] == 1, pos[1] == 1) if ny == 1 else (None, None))
    first_x = lines[pl.ds(0, deep * deep, stride=deep), :].reshape(deep, deep, 128)
    last_x = lines[pl.ds(deep - 1, deep * deep, stride=deep), :].reshape(deep, deep, 128)
    ends = []
    for y in (0, deep - 1):
        for x in (0, deep - 1):
            ends.append(lines[pl.ds(y * deep + x, deep, stride=deep * deep), :])
    if ny == 1:
        y_edges[0] = jnp.where(low, fine[:, 0], fine[:, deep - 1])
        x_edges[0] = jnp.where(high, first_x, last_x)
        corners[0] = jnp.where(
            low, jnp.where(high, ends[0], ends[1]), jnp.where(high, ends[2], ends[3])
        )
    else:
        y_edges[0], y_edges[1] = fine[:, 0], fine[:, deep - 1]
        x_edges[0], x_edges[1] = first_x, last_x
        for k in range(4):
            corners[k] = ends[k]


def deep_kernel(ny, nx, tiles, pos, pooled, y_halos, x_halos, corners, front, back, own, got, partner, *refs):
    act, stats, grid, packed, kernel = refs
    deep = pooled.shape[0]
    f32 = jnp.float32
    shard = own.shape[1]
    part = shard // 2
    tile, odd = pos[ny + nx], pos[ny + nx + 1]

    def place(rows, at):
        for tap in range(27):
            lane = (tap % 9) * 128
            kernel[tap // 9, pl.ds(at, rows.shape[1]), lane : lane + 128] = rows[tap]

    place(own, pl.multiple_of(tile * shard, shard))
    for k in range(1, tiles):
        base = lax.rem(tile + tiles - k, tiles) * shard
        if got.shape[2] == shard:
            place(got.at[k - 1], pl.multiple_of(base, shard))
            continue
        place(got.at[k - 1], pl.multiple_of(base + odd * part, part))
        place(partner.at[k - 1], pl.multiple_of(base + (1 - odd) * part, part))

    grid[...] = jnp.zeros(grid.shape, f32)
    grid[1 : deep + 1, 1 : deep + 1, 8:16] = pooled[...]
    grid[0, 1 : deep + 1, 8:16] = front[0:deep]
    grid[deep + 1, 1 : deep + 1, 8:16] = back[0:deep]
    for i in range(ny):
        at = jnp.where(pos[i] == 1, 0, deep + 1)
        grid[1 : deep + 1, at, 8:16] = y_halos[i]
        grid[0, at, 8:16] = front[deep + i]
        grid[deep + 1, at, 8:16] = back[deep + i]
    for j in range(nx):
        for z in range(deep + 2):
            if z == 0:
                line, rim = front[deep + ny + j], front
            elif z == deep + 1:
                line, rim = back[deep + ny + j], back
            else:
                line, rim = x_halos[j, z - 1], None
            lines = grid.at[z].reshape((deep + 2) * 24, 128)
            left = pos[ny + j] == 1
            for side, here in ((7, left), (16, jnp.logical_not(left))):
                if nx == 2 and side != (7, 16)[j]:
                    continue
                kept = line if nx == 2 else jnp.where(here, line, 0.0)
                lines[pl.ds(24 + side, deep, stride=24), :] = kept
                for i in range(ny):
                    k = i * nx + j
                    end = corners[k, z - 1 : z] if rim is None else rim[deep + ny + nx, k : k + 1]
                    above = pos[i] == 1
                    for y, there in ((0, above), (deep + 1, jnp.logical_not(above))):
                        if ny == 2 and y != (0, deep + 1)[i]:
                            continue
                        kept = end
                        if nx == 1:
                            kept = jnp.where(jnp.logical_and(here, there), end, 0.0)
                        grid[z, y, side : side + 1] = kept

    for dx in range(3):
        plane = grid[:, :, 7 + dx : 15 + dx]
        for y in range(deep + 1):
            both = jnp.concatenate([plane[:, y], plane[:, y + 1]], axis=1)
            packed[:, y // 2, y % 2, :, dx * 128 : dx * 128 + 128] = both.astype(jnp.bfloat16)

    rows = deep**3
    total = None
    for dz in range(3):
        left = jnp.concatenate(
            [
                packed[dz : dz + deep, dy // 2 : dy // 2 + deep // 2, dy % 2].reshape(rows, 384)
                for dy in range(3)
            ],
            axis=1,
        )
        term = lax.dot_general(
            left, kernel[dz], (((1,), (1,)), ((), ())), preferred_element_type=f32
        )
        total = term if total is None else total + term
    act[...] = total
    mean = jnp.sum(total, axis=0, keepdims=True) / rows
    off = total - mean
    put_stats(stats, mean, jnp.sum(off * off, axis=0, keepdims=True))


def final_kernel(_, act, stats, gain, offset, up, mid, out, wide):
    edge = mid.shape[0]
    deep = edge // 2
    f32 = jnp.float32
    mean, scale = read_stats(stats, float(deep**3))
    value = silu((act[...] - mean) * (scale * gain[...]) + offset[...]).astype(jnp.bfloat16)
    lifted = jnp.dot(value, up[...], preferred_element_type=f32)
    rows = deep**3
    wide[pl.ds(0, rows, stride=2), :] = lifted
    wide[pl.ds(1, rows, stride=2), :] = lifted

    def step(k, _):
        size = deep * edge
        add = wide[pl.ds(pl.multiple_of(k * size, size), size), :].reshape(1, deep, 1, edge, 128)
        old = mid[pl.ds(2 * k, 2)].astype(f32).reshape(2, deep, 2, edge, 128)
        out[pl.ds(2 * k, 2)] = (old + add).astype(jnp.bfloat16).reshape(2, edge, edge, 128)
        return 0

    lax.fori_loop(0, deep, step, 0)


def body(
    features, conv_weight, gain_mid, offset_mid, deep_weight, gain_deep, offset_deep, up_weight
):
    f32, bf16 = jnp.float32, jnp.bfloat16
    edge, channels = features.shape[0], features.shape[3]
    deep = edge // 2
    deep_channels = gain_deep.shape[0]
    square = Square()
    tiles = square.tiles
    devices = lax.axis_size("gz") * tiles
    y_low, x_low = square.low_sides()
    ny, nx = len(y_low), len(x_low)
    pos = jnp.stack(
        [jnp.asarray(v, jnp.int32) for v in y_low + x_low + [lax.axis_index("yx"), lax.axis_index("gz") % 2]]
    )

    y, x, corner = square.halos(*square.edges(features))
    own = jnp.moveaxis(deep_weight, 4, 3).reshape(27, deep_weight.shape[4], deep_weight.shape[3])
    got = gather_shards(own)
    front, back = swap_depth(
        depth_face(features, y, x, corner, 0), depth_face(features, y, x, corner, -1)
    )
    act, stats = call(
        functools.partial(mid_kernel, ny, nx),
        [((edge, edge, edge, channels), f32), ((devices, 8, channels), f32)],
        [
            ((edge + 2, edge + 2, edge, channels), bf16),
            ((9 * channels, 3 * channels), bf16),
            ((edge + 2, edge + 16, channels), f32),
            ((edge + 2, edge, 3 * channels), bf16),
        ],
        pos,
        features,
        jnp.stack(y),
        jnp.stack(x),
        jnp.stack(corner),
        front,
        back,
        conv_weight.reshape(27, channels, channels),
        flops=2 * 27 * channels * channels * edge**3,
        nbytes=6 << 20,
    )
    stats, *got = lax.optimization_barrier((stats, *got))
    got = jnp.stack(got)
    partner = swap_halves(got, got.shape[2] == own.shape[1])
    stats = share(stats)
    out, pooled, *edges = call(
        functools.partial(norm_kernel, ny, nx),
        [
            ((edge, edge, edge, channels), bf16),
            ((deep, deep, deep, channels), f32),
            ((ny, deep, deep, channels), f32),
            ((nx, deep, deep, channels), f32),
            ((ny * nx, deep, channels), f32),
        ],
        [((deep * edge, channels), f32), ((deep, deep, deep, channels), f32)],
        pos,
        act,
        stats,
        gain_mid.reshape(1, channels),
        offset_mid.reshape(1, channels),
        flops=20 * channels * edge**3,
        nbytes=3 << 20,
    )
    y, x, corner = square.halos(*([piece[i] for i in range(piece.shape[0])] for piece in edges))
    front, back = swap_depth(
        depth_face(pooled, y, x, corner, 0), depth_face(pooled, y, x, corner, -1)
    )
    deep_act, stats = call(
        functools.partial(deep_kernel, ny, nx, tiles),
        [((deep**3, deep_channels), f32), ((devices, 8, deep_channels), f32)],
        [
            ((deep + 2, deep + 2, 24, channels), f32),
            ((deep + 2, deep // 2 + 1, 2, 16, 3 * channels), bf16),
            ((3, deep_channels, 9 * channels), bf16),
        ],
        pos,
        pooled,
        jnp.stack(y),
        jnp.stack(x),
        jnp.stack(corner),
        front,
        back,
        own,
        got,
        partner,
        flops=2 * 27 * channels * deep_channels * deep**3,
        nbytes=4 << 20,
    )
    stats = share(stats)
    (decoded,) = call(
        final_kernel,
        [((edge, edge, edge, channels), bf16)],
        [((2 * deep**3, channels), f32)],
        pos,
        deep_act,
        stats,
        gain_deep.reshape(1, deep_channels),
        offset_deep.reshape(1, deep_channels),
        up_weight,
        out,
        flops=4 * deep_channels * channels * deep**3,
        nbytes=3 << 20,
    )
    return decoded


def solution(mesh):
    placed = (
        P(("cand", "gz"), "yx", None, None),
        P(),
        P(),
        P(),
        P(None, None, None, None, "yx"),
        P(),
        P(),
        P(),
    )
    return jax.shard_map(
        body,
        mesh=mesh,
        in_specs=placed,
        out_specs=P(("cand", "gz"), "yx", None, None),
        check_vma=False,
    )
```

time: 129 us -> 96.2 us (0.75)
  local copies, waits for them, and re-layouts: 23.9 us -> 4.45 us
  matrix products: 17.5 us -> 0 us
  waiting for transfers between devices: 39.8 us -> 22.6 us
  Pallas kernels: 0 us -> 16.6 us
  starting transfers between devices: 25.4 us -> 35.2 us
  other arithmetic: 11.6 us -> 2.71 us
  blocking collectives: 9.97 us -> 13.8 us
    ppermute x11 -> x14, waiting for transfers between devices: 39.8 us -> 17.7 us  [the longest x2 8.55 us: halos(): corner = lax.ppermute(corners[0], 'yx', self.swap_route(3))]
    conv_general_dilated x2 -> x0, matrix products: 17.3 us -> none  [convolve(): lax.conv_general_dilated(padded[None], weight, (1, 1, 1), 'VALID', dimens...]
    pallas_call x0 -> x4, Pallas kernels: none -> 16.6 us  [call(): pl.pallas_call(kernel, out_shape=[jax.ShapeDtypeStruct(shape, dtype) for...]
    ppermute x11 -> x14, starting transfers between devices: 17.9 us -> 27.1 us  [the longest x2 6.44 us: halos(): x = lax.ppermute(x_edges[0], 'yx', self.swap_route(1))]
    conv_general_dilated x5 -> x0, local copies, waits for them, and re-layouts: 8.59 us -> none  [convolve(): lax.conv_general_dilated(padded[None], weight, (1, 1, 1), 'VALID', dimens...]
    unnamed x26 -> x20, local copies, waits for them, and re-layouts: 6.67 us -> 1.21 us
    all_to_all x1, waiting for transfers between devices: 0.01 us -> 4.93 us  [share(): return lax.all_to_all(statistics, PART, 0, 0)]
    reduce_sum x14 -> x0, other arithmetic: 4.34 us -> none  [the longest x1 2 us: body(): pooled = pooled.mean(axis=(1, 3, 5)).astype(jnp.bfloat16)]
  transfers between devices with their start and end apart: 12 -> 15, of which waited for: 6 -> 7; matrix products, arithmetic and copies ran while one was open for 7% -> 5% of each run, Pallas kernels for 0% -> 12%
where the time goes in v2:
time: 96.2 us; the launch traced here: 95.6 us
  starting transfers between devices  35.2 us (37%)
  waiting for transfers between devices  22.6 us (23%)
  Pallas kernels  16.6 us (17%)
  blocking collectives  13.8 us (14%)
  local copies, waits for them, and re-layouts  4.45 us (5%)
  other arithmetic  2.71 us (3%)
    pallas_call x4, Pallas kernels, call(): pl.pallas_call(kernel, out_shape=[jax.ShapeDtypeStruct(shape, dtype) for...  16.6 us
    all_to_all x1, blocking collectives, share(): return lax.all_to_all(statistics, PART, 0, 0)  13.8 us
    ppermute x2, waiting for transfers between devices, halos(): corner = lax.ppermute(corners[0], 'yx', self.swap_route(3))  8.55 us
    all_to_all x1, starting transfers between devices, share(): return lax.all_to_all(statistics, PART, 0, 0)  8.12 us
    ppermute x2, starting transfers between devices, halos(): x = lax.ppermute(x_edges[0], 'yx', self.swap_route(1))  6.44 us
    ppermute x2, waiting for transfers between devices, swap_depth(): lax.ppermute(low, 'gz', [(j, i) for i, j in up])  6.26 us
    ppermute x3, starting transfers between devices, gather_shards(): lax.ppermute(mine, 'yx', [(i, (i + k) % tiles) for i in range(tiles)])  6.11 us
    ppermute x2, starting transfers between devices, halos(): y = lax.ppermute(y_edges[0], 'yx', self.swap_route(2))  5.2 us
  transfers between devices with their start and end apart: 15, of which 7 were waited for; matrix products, arithmetic and copies ran while one was open for 5% of the time, Pallas kernels for 12%

profile of v2, /device:TPU:0, one launch (start us, length us, event | category | flops | bytes accessed | tf_op | source)
XLA Modules:
  0.0 95.6 jit_solution(2062160137030228876)
XLA Ops:
  0.0 0.0 copy-start.9
  0.0 0.0 copy-start.1
  0.0 1.2 %slice_select_fusion = bf16[27,32,128]{2,1,0:T(8,128)(2,1)S(1)} fusion(bf16[27,64,128]{2,1,0:T(8,128)(2,1)} %bitcast.46, pred[]{:T(512)S(6)} %eq.15), kind=kLoop, calls=%fused_computation.1 | loop fusion | flops 110592 | bytes 663553 | tf_op jit(solution)/shard_map/jit(_where)/select_n | solution.py:90
  1.2 5.1 %collective-permute-start.7 = (bf16[27,32,128]{2,1,0:T(8,128)(2,1)S(1)}, bf16[27,32,128]{2,1,0:T(8,128)(2,1)}, u32[]{:S(2)}, u32[]{:S(2)}) collective-permute-start(bf16[27,32,128]{2,1,0:T(8,128)(2,1)S(1)} %slice_select_fusion), channel_id=1, source_target_pairs={{0,3},{1,0},{2,1},{3,2},{4,7},{5,4},{6,5},{7,6},{8,11},{9,8},{10,9... | collective-permute-start | bytes 663560 | tf_op jit(solution)/shard_map/ppermute | solution.py:92
  6.3 0.0 collective-permute-start.6
  6.3 1.0 %collective-permute-start.5 = (bf16[27,32,128]{2,1,0:T(8,128)(2,1)S(1)}, bf16[27,32,128]{2,1,0:T(8,128)(2,1)}, u32[]{:S(2)}, u32[]{:S(2)}) collective-permute-start(bf16[27,32,128]{2,1,0:T(8,128)(2,1)S(1)} %slice_select_fusion), channel_id=1, source_target_pairs={{0,1},{1,2},{2,3},{3,0},{4,5},{5,6},{6,7},{7,4},{8,9},{9,10},{10,1... | collective-permute-start | bytes 663560 | tf_op jit(solution)/shard_map/ppermute | solution.py:92
  7.3 0.9 fusion.4
  8.2 2.0 %collective-permute-start = (bf16[16,16,128]{2,0,1:T(8,128)(2,1)S(1)}, bf16[16,16,128]{2,0,1:T(8,128)(2,1)S(1)}, u32[]{:S(2)}, u32[]{:S(2)}) collective-permute-start(bf16[16,16,128]{2,0,1:T(8,128)(2,1)S(1)} %fusion.1), channel_id=1, source_target_pairs={{0,2},{1,3},{2,0},{3,1},{4,6},{5,7},{6,4},{7,5},{8,10},{9,11},{10,... | collective-permute-start | bytes 196616 | tf_op jit(solution)/shard_map/ppermute | solution.py:45
  10.2 2.9 %collective-permute-start.2 = (bf16[16,128]{1,0:T(8,128)(2,1)S(1)}, bf16[16,128]{1,0:T(8,128)(2,1)S(1)}, u32[]{:S(2)}, u32[]{:S(2)}) collective-permute-start(bf16[16,128]{1,0:T(8,128)(2,1)S(1)} %fusion.2), channel_id=1, source_target_pairs={{0,3},{1,2},{2,1},{3,0},{4,7},{5,6},{6,5},{7,4},{8,11},{9,10},{10,... | collective-permute-start | bytes 12296 | tf_op jit(solution)/shard_map/ppermute | solution.py:47
  13.1 0.9 slice_bitcast_fusion
  14.0 1.4 %fusion.3 = (bf16[16,16,1,128]{3,2,1,0:T(2,128)(2,1)S(1)}, bf16[16,16,1,128]{3,2,1,0:T(2,128)(2,1)S(1)}) fusion(bf16[16,16,16,128]{3,2,1,0:T(8,128)(2,1)} %x.5), kind=kLoop, calls=%fused_computation.21 | loop fusion | bytes 262144 | tf_op jit(solution)/shard_map/slice | solution.py:62
  15.4 7.5 %collective-permute-done.2 = bf16[16,128]{1,0:T(8,128)(2,1)S(1)} collective-permute-done((bf16[16,128]{1,0:T(8,128)(2,1)S(1)}, bf16[16,128]{1,0:T(8,128)(2,1)S(1)}, u32[]{:S(2)}, u32[]{:S(2)}) %collective-permute-start.2) | collective-permute-done | bytes 4128 | tf_op jit(solution)/shard_map/ppermute | solution.py:47
  22.9 6.0 %collective-permute-start.1 = (bf16[16,16,128]{2,1,0:T(8,128)(2,1)S(1)}, bf16[16,16,128]{2,1,0:T(8,128)(2,1)S(1)}, u32[]{:S(2)}, u32[]{:S(2)}) collective-permute-start(bf16[16,16,128]{2,1,0:T(8,128)(2,1)S(1)} %fusion), channel_id=1, source_target_pairs={{0,1},{1,0},{2,3},{3,2},{4,5},{5,4},{6,7},{7,6},{8,9},{9,8},{10,11... | collective-permute-start | bytes 196616 | tf_op jit(solution)/shard_map/ppermute | solution.py:46
  28.9 0.0 copy-done.9
  28.9 0.1 select_bitcast_fusion.1
  29.0 0.0 collective-permute-done
  29.1 2.1 %collective-permute-done.1 = bf16[16,16,128]{2,1,0:T(8,128)(2,1)S(1)} collective-permute-done((bf16[16,16,128]{2,1,0:T(8,128)(2,1)S(1)}, bf16[16,16,128]{2,1,0:T(8,128)(2,1)S(1)}, u32[]{:S(2)}, u32[]{:S(2)}) %collective-permute-start.1) | collective-permute-done | bytes 65568 | tf_op jit(solution)/shard_map/ppermute | solution.py:46
  31.2 1.3 %collective-permute-start.3 = (bf16[19,16,128]{2,1,0:T(8,128)(2,1)S(1)}, bf16[19,16,128]{2,1,0:T(8,128)(2,1)S(1)}, u32[]{:S(2)}, u32[]{:S(2)}) collective-permute-start(bf16[19,16,128]{2,1,0:T(8,128)(2,1)S(1)} %pad_maximum_fusion.1), channel_id=1, source_target_pairs={{0,4},{4,8},{8,12},{1,5},{5,9},{9,13},{2,6},{6,10},{10,14},{3,7},{... | collective-permute-start | bytes 233480 | tf_op jit(solution)/shard_map/ppermute | solution.py:73
  32.5 1.3 %collective-permute-start.4 = (bf16[19,16,128]{2,1,0:T(8,128)(2,1)S(1)}, bf16[19,16,128]{2,1,0:T(8,128)(2,1)S(1)}, u32[]{:S(2)}, u32[]{:S(2)}) collective-permute-start(bf16[19,16,128]{2,1,0:T(8,128)(2,1)S(1)} %pad_maximum_fusion.2), channel_id=1, source_target_pairs={{4,0},{8,4},{12,8},{5,1},{9,5},{13,9},{6,2},{10,6},{14,10},{7,3},{... | collective-permute-start | bytes 233480 | tf_op jit(solution)/shard_map/ppermute | solution.py:73
  33.8 0.1 pad_add_fusion.pos._
  33.9 0.0 collective-permute-done.3.refs_3_
  33.9 3.5 %collective-permute-done.4.refs_4_ = bf16[19,16,128]{2,1,0:T(8,128)(2,1)S(1)} collective-permute-done((bf16[19,16,128]{2,1,0:T(8,128)(2,1)S(1)}, bf16[19,16,128]{2,1,0:T(8,128)(2,1)S(1)}, u32[]{:S(2)}, u32[]{:S(2)}) %collective-permute-start.4) | collective-permute-done | bytes 77856 | tf_op jit(solution)/shard_map/ppermute | solution.py:73
  37.4 0.0 copy-done.1
  37.4 0.0 copy-start.7
  37.4 1.2 %copy-done.7 = bf16[3,3,3,128,128]{4,3,2,1,0:T(8,128)(2,1)S(1)} copy-done((bf16[3,3,3,128,128]{4,3,2,1,0:T(8,128)(2,1)S(1)}, bf16[3,3,3,128,128]{4,3,2,1,0:T(8,128)(2,1)}, u32[]{:S(2)}) %copy-start.7) | copy-done | bytes 884760
  38.6 0.0 copy-start.5
  38.6 0.0 copy-start.6
  38.6 9.1 %shard_map.82 = (f32[16,16,16,128]{3,2,1,0:T(8,128)S(1)}, f32[16,8,128]{2,1,0:T(8,128)}) custom-call(s32[4]{0:T(128)S(1)} %pad_add_fusion.pos._, bf16[16,16,16,128]{3,2,1,0:T(8,128)(2,1)S(1)} %copy-done.1, bf16[1,16,16,128]{3,2,1,0:T(8,128)(2,1)S(1)} %copy.15.refs_0_, bf16[1,16,16,128]{3,2,1,0:T(8,128)(2,1)S(1)} %bitcast.54, ...), custom_call_target="tpu_custom_call" | custom-call | flops 3623878656 | bytes 6291456 | tf_op jit(solution)/shard_map/pallas_call | solution.py:110
  47.7 0.0 copy-start.8
  47.7 0.0 copy-start
  47.7 0.0 collective-permute-done.7
  47.7 0.0 collective-permute-done.6
  47.7 0.0 collective-permute-done.5
  47.7 8.1 %all-to-all-start = ((f32[16,8,128]{2,1,0:T(8,128)}), f32[16,8,128]{2,1,0:T(8,128)S(1)}, u32[]{:S(2)}, u32[]{:S(2)}) async-start(f32[16,8,128]{2,1,0:T(8,128)} %get-tuple-element.20), calls=%async_computation | async-start | bytes 131072 | tf_op jit(solution)/shard_map/all_to_all | solution.py:105
  55.9 1.2 %pad_maximum_fusion.got = bf16[3,27,32,128]{3,2,1,0:T(8,128)(2,1)S(1)} fusion(bf16[1,27,32,128]{3,2,1,0:T(8,128)(2,1)} %bitcast.32, bf16[1,27,32,128]{3,2,1,0:T(8,128)(2,1)} %bitcast.31, bf16[1,27,32,128]{3,2,1,0:T(8,128)(2,1)} %bitcast.30), kind=kLoop, calls=%fused_computation | loop fusion | flops 663552 | bytes 1327104 | tf_op jit(solution)/shard_map/stack | solution.py:436
  57.1 0.5 collective-permute-start.13
  57.6 4.9 %all-to-all-done.stats = f32[16,8,128]{2,1,0:T(8,128)S(1)} async-done(((f32[16,8,128]{2,1,0:T(8,128)}), f32[16,8,128]{2,1,0:T(8,128)S(1)}, u32[]{:S(2)}, u32[]{:S(2)}) %all-to-all-start) | async-done | bytes 65568 | tf_op jit(solution)/shard_map/all_to_all | solution.py:105
  62.5 0.0 copy-done.5
  62.5 0.0 copy-done.6
  62.5 2.0 %shard_map.83 = (bf16[16,16,16,128]{3,2,1,0:T(8,128)(2,1)S(1)}, f32[8,8,8,128]{3,2,1,0:T(8,128)S(1)}, f32[1,8,8,128]{3,2,1,0:T(8,128)S(1)}, f32[1,8,8,128]{3,2,1,0:T(8,128)S(1)}, f32[1,8,128]{2,1,0:T(8,128)S(1)}) custom-call(s32[4]{0:T(128)S(1)} %pad_add_fusion.pos._, f32[16,16,16,128]{3,2,1,0:T(8,128)S(1)} %get-tuple-element.18.act, ...), custom_call_target="tpu_custom_call" | custom-call | flops 10485760 | bytes 3145728 | tf_op jit(solution)/shard_map/pallas_call | solution.py:110
  64.5 0.0 copy-start.2
  64.6 0.0 copy-start.3
  64.6 0.0 copy-start.4
  64.6 0.8 collective-permute-start.10
  65.4 0.4 collective-permute-start.9
  65.8 3.2 %collective-permute-start.8 = (f32[8,8,128]{2,1,0:T(8,128)S(1)}, f32[8,8,128]{2,1,0:T(8,128)S(1)}, u32[]{:S(2)}, u32[]{:S(2)}) collective-permute-start(f32[8,8,128]{2,1,0:T(8,128)S(1)} %bitcast.58), channel_id=1, source_target_pairs={{0,2},{1,3},{2,0},{3,1},{4,6},{5,7},{6,4},{7,5},{8,10},{9,11},{10,... | collective-permute-start | bytes 98312 | tf_op jit(solution)/shard_map/ppermute | solution.py:45
  69.0 1.1 %collective-permute-done.10 = f32[8,128]{1,0:T(8,128)S(1)} collective-permute-done((f32[8,128]{1,0:T(8,128)S(1)}, f32[8,128]{1,0:T(8,128)S(1)}, u32[]{:S(2)}, u32[]{:S(2)}) %collective-permute-start.10) | collective-permute-done | bytes 4128 | tf_op jit(solution)/shard_map/ppermute | solution.py:47
  70.1 0.0 copy-done.8
  70.1 0.1 select_bitcast_fusion
  70.2 0.0 collective-permute-done.9
  70.2 0.7 collective-permute-done.8
  70.9 1.3 %collective-permute-start.11 = (f32[11,8,128]{2,1,0:T(8,128)S(1)}, f32[11,8,128]{2,1,0:T(8,128)S(1)}, u32[]{:S(2)}, u32[]{:S(2)}) collective-permute-start(f32[11,8,128]{2,1,0:T(8,128)S(1)} %pad_maximum_fusion.3), channel_id=1, source_target_pairs={{0,4},{4,8},{8,12},{1,5},{5,9},{9,13},{2,6},{6,10},{10,14},{3,7},{... | collective-permute-start | bytes 135176 | tf_op jit(solution)/shard_map/ppermute | solution.py:73
  72.2 1.3 %collective-permute-start.12 = (f32[11,8,128]{2,1,0:T(8,128)S(1)}, f32[11,8,128]{2,1,0:T(8,128)S(1)}, u32[]{:S(2)}, u32[]{:S(2)}) collective-permute-start(f32[11,8,128]{2,1,0:T(8,128)S(1)} %pad_maximum_fusion.4), channel_id=1, source_target_pairs={{4,0},{8,4},{12,8},{5,1},{9,5},{13,9},{6,2},{10,6},{14,10},{7,3},{... | collective-permute-start | bytes 135176 | tf_op jit(solution)/shard_map/ppermute | solution.py:73
  73.5 0.0 collective-permute-done.11.front
  73.5 2.8 %collective-permute-done.12.back = f32[11,8,128]{2,1,0:T(8,128)S(1)} collective-permute-done((f32[11,8,128]{2,1,0:T(8,128)S(1)}, f32[11,8,128]{2,1,0:T(8,128)S(1)}, u32[]{:S(2)}, u32[]{:S(2)}) %collective-permute-start.12) | collective-permute-done | bytes 45088 | tf_op jit(solution)/shard_map/ppermute | solution.py:73
  76.3 0.0 collective-permute-done.13.partner
  76.3 0.0 copy-done
  76.3 2.8 %shard_map.84 = (f32[512,256]{1,0:T(8,128)S(1)}, f32[16,8,256]{2,1,0:T(8,128)S(1)}) custom-call(s32[4]{0:T(128)S(1)} %pad_add_fusion.pos._, f32[8,8,8,128]{3,2,1,0:T(8,128)S(1)} %get-tuple-element.21.pooled, f32[1,8,8,128]{3,2,1,0:T(8,128)S(1)} %bitcast.51, f32[1,8,8,128]{3,2,1,0:T(8,128)S(1)} %bitcast.50, f32[1,8,128]{2,1,0:T(8,128)S(1)} %bitcast.49, ...), custom_call_target="tpu_custom_call" | custom-call | flops 905969664 | bytes 4194304 | tf_op jit(solution)/shard_map/pallas_call | solution.py:110
  79.2 13.8 %all_to_all.10.stats = f32[16,8,256]{2,1,0:T(8,128)S(1)} all-to-all(f32[16,8,256]{2,1,0:T(8,128)S(1)} %get-tuple-element.29), channel_id=1, replica_groups=mesh['cand'=2,'gz'=4,'yx'=4] {'gz','yx'}, dimensions={0} | all-to-all | bytes 262144 | tf_op jit(solution)/shard_map/all_to_all | solution.py:105
  93.0 0.0 copy-done.2
  93.0 0.0 copy-done.3
  93.0 0.0 copy-done.4
  93.0 2.7 %shard_map.85 = bf16[16,16,16,128]{3,2,1,0:T(8,128)(2,1)} custom-call(s32[4]{0:T(128)S(1)} %pad_add_fusion.pos._, f32[512,256]{1,0:T(8,128)S(1)} %get-tuple-element.28.act, f32[16,8,256]{2,1,0:T(8,128)S(1)} %all_to_all.10.stats, f32[1,256]{1,0:T(1,128)S(1)} %bitcast.52, f32[1,256]{1,0:T(1,128)S(1)} %bitcast.53, bf16[256,128]{1,0:T(8,128)(2,1)S(1)} %copy-done.2, ...), custom_call_target="tpu_custom_call" | custom-call | flops 67108864 | bytes 3145728 | tf_op jit(solution)/shard_map/pallas_call | solution.py:110
  (19 shorter events, 0.2 us)
Async XLA Ops:
  0.0 28.9 %copy-start.9 = (pred[16]{0:T(512)(128)(4,1)S(1)}, pred[16]{0:T(512)(128)(4,1)}, u32[]{:S(2)}) copy-start(pred[16]{0:T(512)(128)(4,1)} %constant.43.clone.1) | copy-start | bytes 52
  0.0 37.4 %copy-start.1 = (bf16[16,16,16,128]{3,2,1,0:T(8,128)(2,1)S(1)}, bf16[16,16,16,128]{3,2,1,0:T(8,128)(2,1)}, u32[]{:S(2)}) copy-start(bf16[16,16,16,128]{3,2,1,0:T(8,128)(2,1)} %x.5) | copy-start | bytes 3145732
  1.2 46.6 %collective-permute-start.7 = (bf16[27,32,128]{2,1,0:T(8,128)(2,1)S(1)}, bf16[27,32,128]{2,1,0:T(8,128)(2,1)}, u32[]{:S(2)}, u32[]{:S(2)}) collective-permute-start(bf16[27,32,128]{2,1,0:T(8,128)(2,1)S(1)} %slice_select_fusion), channel_id=1, source_target_pairs={{0,3},{1,0},{2,1},{3,2},{4,7},{5,4},{6,5},{7,6},{8,11},{9,8},{10,9... | collective-permute-start | bytes 663560 | tf_op jit(solution)/shard_map/ppermute | solution.py:92
  6.3 41.5 %collective-permute-start.6 = (bf16[27,32,128]{2,1,0:T(8,128)(2,1)S(1)}, bf16[27,32,128]{2,1,0:T(8,128)(2,1)}, u32[]{:S(2)}, u32[]{:S(2)}) collective-permute-start(bf16[27,32,128]{2,1,0:T(8,128)(2,1)S(1)} %slice_select_fusion), channel_id=1, source_target_pairs={{0,2},{1,3},{2,0},{3,1},{4,6},{5,7},{6,4},{7,5},{8,10},{9,11},{10,... | collective-permute-start | bytes 663560 | tf_op jit(solution)/shard_map/ppermute | solution.py:92
  6.3 41.5 %collective-permute-start.5 = (bf16[27,32,128]{2,1,0:T(8,128)(2,1)S(1)}, bf16[27,32,128]{2,1,0:T(8,128)(2,1)}, u32[]{:S(2)}, u32[]{:S(2)}) collective-permute-start(bf16[27,32,128]{2,1,0:T(8,128)(2,1)S(1)} %slice_select_fusion), channel_id=1, source_target_pairs={{0,1},{1,2},{2,3},{3,0},{4,5},{5,6},{6,7},{7,4},{8,9},{9,10},{10,1... | collective-permute-start | bytes 663560 | tf_op jit(solution)/shard_map/ppermute | solution.py:92
  8.2 20.8 %collective-permute-start = (bf16[16,16,128]{2,0,1:T(8,128)(2,1)S(1)}, bf16[16,16,128]{2,0,1:T(8,128)(2,1)S(1)}, u32[]{:S(2)}, u32[]{:S(2)}) collective-permute-start(bf16[16,16,128]{2,0,1:T(8,128)(2,1)S(1)} %fusion.1), channel_id=1, source_target_pairs={{0,2},{1,3},{2,0},{3,1},{4,6},{5,7},{6,4},{7,5},{8,10},{9,11},{10,... | collective-permute-start | bytes 196616 | tf_op jit(solution)/shard_map/ppermute | solution.py:45
  10.2 12.7 %collective-permute-start.2 = (bf16[16,128]{1,0:T(8,128)(2,1)S(1)}, bf16[16,128]{1,0:T(8,128)(2,1)S(1)}, u32[]{:S(2)}, u32[]{:S(2)}) collective-permute-start(bf16[16,128]{1,0:T(8,128)(2,1)S(1)} %fusion.2), channel_id=1, source_target_pairs={{0,3},{1,2},{2,1},{3,0},{4,7},{5,6},{6,5},{7,4},{8,11},{9,10},{10,... | collective-permute-start | bytes 12296 | tf_op jit(solution)/shard_map/ppermute | solution.py:47
  22.9 8.2 %collective-permute-start.1 = (bf16[16,16,128]{2,1,0:T(8,128)(2,1)S(1)}, bf16[16,16,128]{2,1,0:T(8,128)(2,1)S(1)}, u32[]{:S(2)}, u32[]{:S(2)}) collective-permute-start(bf16[16,16,128]{2,1,0:T(8,128)(2,1)S(1)} %fusion), channel_id=1, source_target_pairs={{0,1},{1,0},{2,3},{3,2},{4,5},{5,4},{6,7},{7,6},{8,9},{9,8},{10,11... | collective-permute-start | bytes 196616 | tf_op jit(solution)/shard_map/ppermute | solution.py:46
  31.2 2.7 %collective-permute-start.3 = (bf16[19,16,128]{2,1,0:T(8,128)(2,1)S(1)}, bf16[19,16,128]{2,1,0:T(8,128)(2,1)S(1)}, u32[]{:S(2)}, u32[]{:S(2)}) collective-permute-start(bf16[19,16,128]{2,1,0:T(8,128)(2,1)S(1)} %pad_maximum_fusion.1), channel_id=1, source_target_pairs={{0,4},{4,8},{8,12},{1,5},{5,9},{9,13},{2,6},{6,10},{10,14},{3,7},{... | collective-permute-start | bytes 233480 | tf_op jit(solution)/shard_map/ppermute | solution.py:73
  32.5 4.9 %collective-permute-start.4 = (bf16[19,16,128]{2,1,0:T(8,128)(2,1)S(1)}, bf16[19,16,128]{2,1,0:T(8,128)(2,1)S(1)}, u32[]{:S(2)}, u32[]{:S(2)}) collective-permute-start(bf16[19,16,128]{2,1,0:T(8,128)(2,1)S(1)} %pad_maximum_fusion.2), channel_id=1, source_target_pairs={{4,0},{8,4},{12,8},{5,1},{9,5},{13,9},{6,2},{10,6},{14,10},{7,3},{... | collective-permute-start | bytes 233480 | tf_op jit(solution)/shard_map/ppermute | solution.py:73
  37.4 1.2 %copy-start.7 = (bf16[3,3,3,128,128]{4,3,2,1,0:T(8,128)(2,1)S(1)}, bf16[3,3,3,128,128]{4,3,2,1,0:T(8,128)(2,1)}, u32[]{:S(2)}) copy-start(bf16[3,3,3,128,128]{4,3,2,1,0:T(8,128)(2,1)} %param.9) | copy-start | bytes 2654212
  38.6 23.9 %copy-start.5 = (f32[128]{0:T(128)S(1)}, f32[128]{0:T(128)}, u32[]{:S(2)}) copy-start(f32[128]{0:T(128)} %param.10) | copy-start | bytes 1540
  38.6 23.9 %copy-start.6 = (f32[128]{0:T(128)S(1)}, f32[128]{0:T(128)}, u32[]{:S(2)}) copy-start(f32[128]{0:T(128)} %param.11) | copy-start | bytes 1540
  47.7 22.4 %copy-start.8 = (pred[8]{0:T(512)(128)(4,1)S(1)}, pred[8]{0:T(512)(128)(4,1)}, u32[]{:S(2)}) copy-start(pred[8]{0:T(512)(128)(4,1)} %constant.45.clone.1) | copy-start | bytes 28
  47.7 28.6 %copy-start = (bf16[3,3,3,128,64]{3,4,2,1,0:T(8,128)(2,1)S(1)}, bf16[3,3,3,128,64]{3,4,2,1,0:T(8,128)(2,1)}, u32[]{:S(2)}) copy-start(bf16[3,3,3,128,64]{3,4,2,1,0:T(8,128)(2,1)} %param.12) | copy-start | bytes 1327108
  47.7 14.8 %all-to-all-start = ((f32[16,8,128]{2,1,0:T(8,128)}), f32[16,8,128]{2,1,0:T(8,128)S(1)}, u32[]{:S(2)}, u32[]{:S(2)}) async-start(f32[16,8,128]{2,1,0:T(8,128)} %get-tuple-element.20), calls=%async_computation | async-start | bytes 131072 | tf_op jit(solution)/shard_map/all_to_all | solution.py:105
  57.1 19.2 %collective-permute-start.13 = (bf16[3,27,32,128]{3,2,1,0:T(8,128)(2,1)S(1)}, bf16[3,27,32,128]{3,2,1,0:T(8,128)(2,1)}, u32[]{:S(2)}, u32[]{:S(2)}) collective-permute-start(bf16[3,27,32,128]{3,2,1,0:T(8,128)(2,1)S(1)} %pad_maximum_fusion.got), channel_id=1, source_target_pairs={{0,4},{4,0},{8,12},{12,8},{1,5},{5,1},{9,13},{13,9},{2,6},{6,2},{1... | collective-permute-start | bytes 1990664 | tf_op jit(solution)/shard_map/ppermute | solution.py:101
  64.5 28.4 %copy-start.2 = (bf16[256,128]{1,0:T(8,128)(2,1)S(1)}, bf16[256,128]{1,0:T(8,128)(2,1)}, u32[]{:S(2)}) copy-start(bf16[256,128]{1,0:T(8,128)(2,1)} %up.1) | copy-start | bytes 196612
  64.6 28.4 %copy-start.3 = (f32[256]{0:T(256)S(1)}, f32[256]{0:T(256)}, u32[]{:S(2)}) copy-start(f32[256]{0:T(256)} %param.13) | copy-start | bytes 3076
  64.6 28.4 %copy-start.4 = (f32[256]{0:T(256)S(1)}, f32[256]{0:T(256)}, u32[]{:S(2)}) copy-start(f32[256]{0:T(256)} %param.14) | copy-start | bytes 3076
  64.6 5.5 %collective-permute-start.10 = (f32[8,128]{1,0:T(8,128)S(1)}, f32[8,128]{1,0:T(8,128)S(1)}, u32[]{:S(2)}, u32[]{:S(2)}) collective-permute-start(f32[8,128]{1,0:T(8,128)S(1)} %bitcast.60), channel_id=1, source_target_pairs={{0,3},{1,2},{2,1},{3,0},{4,7},{5,6},{6,5},{7,4},{8,11},{9,10},{10,... | collective-permute-start | bytes 12296 | tf_op jit(solution)/shard_map/ppermute | solution.py:47
  65.4 4.8 %collective-permute-start.9 = (f32[8,8,128]{2,1,0:T(8,128)S(1)}, f32[8,8,128]{2,1,0:T(8,128)S(1)}, u32[]{:S(2)}, u32[]{:S(2)}) collective-permute-start(f32[8,8,128]{2,1,0:T(8,128)S(1)} %bitcast.59), channel_id=1, source_target_pairs={{0,1},{1,0},{2,3},{3,2},{4,5},{5,4},{6,7},{7,6},{8,9},{9,8},{10,11... | collective-permute-start | bytes 98312 | tf_op jit(solution)/shard_map/ppermute | solution.py:46
  65.8 5.1 %collective-permute-start.8 = (f32[8,8,128]{2,1,0:T(8,128)S(1)}, f32[8,8,128]{2,1,0:T(8,128)S(1)}, u32[]{:S(2)}, u32[]{:S(2)}) collective-permute-start(f32[8,8,128]{2,1,0:T(8,128)S(1)} %bitcast.58), channel_id=1, source_target_pairs={{0,2},{1,3},{2,0},{3,1},{4,6},{5,7},{6,4},{7,5},{8,10},{9,11},{10,... | collective-permute-start | bytes 98312 | tf_op jit(solution)/shard_map/ppermute | solution.py:45
  70.9 2.6 %collective-permute-start.11 = (f32[11,8,128]{2,1,0:T(8,128)S(1)}, f32[11,8,128]{2,1,0:T(8,128)S(1)}, u32[]{:S(2)}, u32[]{:S(2)}) collective-permute-start(f32[11,8,128]{2,1,0:T(8,128)S(1)} %pad_maximum_fusion.3), channel_id=1, source_target_pairs={{0,4},{4,8},{8,12},{1,5},{5,9},{9,13},{2,6},{6,10},{10,14},{3,7},{... | collective-permute-start | bytes 135176 | tf_op jit(solution)/shard_map/ppermute | solution.py:73
  72.2 4.1 %collective-permute-start.12 = (f32[11,8,128]{2,1,0:T(8,128)S(1)}, f32[11,8,128]{2,1,0:T(8,128)S(1)}, u32[]{:S(2)}, u32[]{:S(2)}) collective-permute-start(f32[11,8,128]{2,1,0:T(8,128)S(1)} %pad_maximum_fusion.4), channel_id=1, source_target_pairs={{4,0},{8,4},{12,8},{5,1},{9,5},{13,9},{6,2},{10,6},{14,10},{7,3},{... | collective-permute-start | bytes 135176 | tf_op jit(solution)/shard_map/ppermute | solution.py:73

commit v3 on v2

--- a/solution.py
+++ b/solution.py
@@ -82,27 +82,23 @@
 
 
 def gather_shards(weight):
-    tiles = lax.axis_size("yx")
-    half = weight.shape[1] // 2
-    odd = lax.axis_index("gz") % 2
-    mine = weight
-    if half % 16 == 0:
-        mine = jnp.where(odd == 1, weight[:, half:], weight[:, :half])
-    got = [
-        lax.ppermute(mine, "yx", [(i, (i + k) % tiles) for i in range(tiles)]) for k in range(1, tiles)
-    ]
-    return got
-
-
-def swap_halves(got, whole):
-    if whole:
-        return got
-    pairs = [(i, i ^ 1) for i in range(lax.axis_size("gz"))]
-    return lax.ppermute(got, "gz", pairs)
+    depth = lax.axis_size("gz")
+    part = weight.shape[1] // depth
+    if part % 16:
+        return lax.all_gather(weight, "yx")
+    mine = lax.dynamic_slice_in_dim(weight, lax.axis_index("gz") * part, part, axis=1)
+    return lax.all_gather(mine, PART)
 
 
 def share(statistics):
     return lax.all_to_all(statistics, PART, 0, 0)
+
+
+def share_by_axis(statistics):
+    tiles = lax.all_to_all(statistics, "yx", 0, 0)
+    depth = lax.axis_size("gz")
+    every = lax.all_to_all(jnp.broadcast_to(tiles[None], (depth,) + tiles.shape), "gz", 0, 0)
+    return every.reshape((-1,) + statistics.shape[1:])
 
 
 def call(kernel, outs, scratch, scalars, *arrays, flops=0, nbytes=0):
@@ -118,30 +114,94 @@
     )(scalars, *arrays)
 
 
-def mid_kernel(ny, nx, pos, x, *refs):
-    y_halos, x_halos, corners = refs[0], refs[1], refs[2]
-    front, back, weight, act, stats, grid, taps, column, flanks = refs[3:]
+def spread_taps(weight, taps):
+    for tap in range(27):
+        row, lane = tap // 3 * 128, tap % 3 * 128
+        taps[row : row + 128, lane : lane + 128] = weight[tap]
+
+
+def join_x(wide, edge):
+    place = lax.broadcasted_iota(jnp.int32, wide.shape[:2] + (128,), 1)
+    after = jnp.where(place > 0, pltpu.roll(wide[:, :, :128], 1, 1), 0.0)
+    before = jnp.where(place < edge - 1, pltpu.roll(wide[:, :, 256:], edge - 1, 1), 0.0)
+    return wide[:, :, 128:256] + after + before
+
+
+def local_planes(x, lo, count, taps, grid, act):
     edge = x.shape[0]
-    f32 = jnp.float32
-    for dz in range(3):
-        for dy in range(3):
-            row = (dz * 3 + dy) * 128
-            for dx in range(3):
-                taps[row : row + 128, dx * 128 : dx * 128 + 128] = weight[dz * 9 + dy * 3 + dx]
-    grid[1 : edge + 1, 1 : edge + 1] = x[...]
-    grid[0, 1 : edge + 1] = front[0:edge]
-    grid[edge + 1, 1 : edge + 1] = back[0:edge]
-    blank = jnp.zeros((edge + 2,) + grid.shape[2:], grid.dtype)
+    blank = jnp.zeros((count + 2,) + grid.shape[2:], grid.dtype)
     grid[:, 0] = blank
     grid[:, edge + 1] = blank
+    first, last = max(lo - 1, 0), min(lo + count + 1, edge)
+    if first > lo - 1:
+        grid[0] = jnp.zeros(grid.shape[1:], grid.dtype)
+    if last < lo + count + 1:
+        grid[count + 1] = jnp.zeros(grid.shape[1:], grid.dtype)
+    grid[first - lo + 1 : last - lo + 1, 1 : edge + 1] = x[first:last]
+    planes = 2
+    rows = planes * edge * edge
+    for z in range(0, count, planes):
+        left = jnp.concatenate(
+            [
+                grid[z + dz : z + dz + planes, dy : dy + edge].reshape(rows, 128)
+                for dz in range(3)
+                for dy in range(3)
+            ],
+            axis=1,
+        )
+        wide = jnp.dot(left, taps[...], preferred_element_type=jnp.float32)
+        new = join_x(wide.reshape(planes * edge, edge, 384), edge)
+        act[z : z + planes] = new.reshape(planes, edge, edge, 128)
+
+
+def front_half_kernel(_, x, weight, act, taps, grid):
+    spread_taps(weight, taps)
+    local_planes(x, 0, act.shape[0], taps, grid, act)
+
+
+def back_half_kernel(_, x, taps, after, act, grid):
+    del after
+    local_planes(x, x.shape[0] - act.shape[0], act.shape[0], taps, grid, act)
+
+
+def rim_kernel(ny, nx, pos, *refs):
+    near, far, y_halos, x_halos, corners, front, back, taps, act, stats, column, flanks = refs
+    edge = act.shape[0]
+    half = edge // 2
+    f32, bf16 = jnp.float32, jnp.bfloat16
+    act[0:half] = near[...]
+    act[half:edge] = far[...]
+    flat = act.reshape(edge**3, 128)
+
+    for plane, face, dz in ((0, front, 0), (edge - 1, back, 2)):
+        inner = face[0:edge]
+        blank = jnp.zeros((1, edge, 128), bf16)
+        lines = [
+            jnp.concatenate([blank, inner[: edge - 1]], axis=0),
+            inner,
+            jnp.concatenate([inner[1:], blank], axis=0),
+        ]
+        left = jnp.concatenate([line.reshape(edge * edge, 128) for line in lines], axis=1)
+        wide = jnp.dot(left, taps[dz * 384 : dz * 384 + 384, :], preferred_element_type=f32)
+        act[plane] += join_x(wide.reshape(edge, edge, 384), edge)
+
     for i in range(ny):
-        at = jnp.where(pos[i] == 1, 0, edge + 1)
-        grid[1 : edge + 1, at] = y_halos[i]
-        grid[0, at] = front[edge + i]
-        grid[edge + 1, at] = back[edge + i]
-
-    act[...] = jnp.zeros(act.shape, f32)
-    flat = act.reshape(edge**3, 128)
+        low = pos[i] == 1
+        inner = y_halos[i]
+        ends = [front[edge + i][None], back[edge + i][None]]
+        lines = [
+            jnp.concatenate([ends[0], inner[: edge - 1]], axis=0),
+            inner,
+            jnp.concatenate([inner[1:], ends[1]], axis=0),
+        ]
+        left = jnp.concatenate([line.reshape(edge * edge, 128) for line in lines], axis=1)
+        start = jnp.where(low, 0, 256)
+        right = jnp.concatenate(
+            [taps[pl.ds(pl.multiple_of(start + dz * 384, 128), 128), :] for dz in range(3)], axis=0
+        )
+        wide = jnp.dot(left, right, preferred_element_type=f32)
+        act[:, jnp.where(low, 0, edge - 1)] += join_x(wide.reshape(edge, edge, 384), edge)
+
     for j in range(nx):
         column[:, 0:8] = jnp.zeros((edge + 2, 8, 128), f32)
         column[:, 8 + edge :] = jnp.zeros((edge + 2, 8, 128), f32)
@@ -161,7 +221,7 @@
             else:
                 lines[pl.ds(7 if i == 0 else 8 + edge, edge + 2, stride=rows), :] = ends
         for dy in range(3):
-            piece = column[:, 7 + dy : 7 + dy + edge].astype(jnp.bfloat16)
+            piece = column[:, 7 + dy : 7 + dy + edge].astype(bf16)
             flanks[:, :, dy * 128 : dy * 128 + 128] = piece
         left = jnp.concatenate(
             [flanks[dz : dz + edge].reshape(edge * edge, 384) for dz in range(3)], axis=1
@@ -169,47 +229,26 @@
         right = jnp.concatenate([taps[:, 0:128], taps[:, 256:384]], axis=1)
         extra = jnp.dot(left, right, preferred_element_type=f32)
         low = pos[ny + j] == 1
+        first, last = extra[:, :128], extra[:, 128:]
         if nx == 1:
-            flat[pl.ds(0, edge * edge, stride=edge), :] = jnp.where(low, extra[:, :128], 0.0)
-            flat[pl.ds(edge - 1, edge * edge, stride=edge), :] = jnp.where(low, 0.0, extra[:, 128:])
-        elif j == 0:
-            flat[pl.ds(0, edge * edge, stride=edge), :] = extra[:, :128]
-        else:
-            flat[pl.ds(edge - 1, edge * edge, stride=edge), :] = extra[:, 128:]
-
-    planes = 2
-    rows = planes * edge * edge
-    place = lax.broadcasted_iota(jnp.int32, (planes * edge, edge, 128), 1)
-
-    def step(k, carry):
-        z = k * planes
-        left = jnp.concatenate(
-            [
-                grid[pl.ds(z + dz, planes), dy : dy + edge].reshape(rows, 128)
-                for dz in range(3)
-                for dy in range(3)
-            ],
-            axis=1,
-        )
-        wide = jnp.dot(left, taps[...], preferred_element_type=f32)
-        wide = wide.reshape(planes * edge, edge, 384)
-        after = jnp.where(place > 0, pltpu.roll(wide[:, :, :128], 1, 1), 0.0)
-        before = jnp.where(place < edge - 1, pltpu.roll(wide[:, :, 256:], edge - 1, 1), 0.0)
-        old = act[pl.ds(z, planes)].reshape(planes * edge, edge, 128)
-        new = old + wide[:, :, 128:256] + after + before
-        act[pl.ds(z, planes)] = new.reshape(planes, edge, edge, 128)
-        return carry + jnp.sum(new.reshape(rows // 8, 8, 128), axis=0)
-
-    total = lax.fori_loop(0, edge // planes, step, jnp.zeros((8, 128), f32))
+            first, last = jnp.where(low, first, 0.0), jnp.where(low, 0.0, last)
+        if nx == 1 or j == 0:
+            flat[pl.ds(0, edge * edge, stride=edge), :] += first
+        if nx == 1 or j == 1:
+            flat[pl.ds(edge - 1, edge * edge, stride=edge), :] += last
+
+    def sum_step(k, carry):
+        return carry + jnp.sum(act[k].reshape(edge * 2, 8, 128), axis=0)
+
+    total = lax.fori_loop(0, edge, sum_step, jnp.zeros((8, 128), f32), unroll=4)
     mean = jnp.sum(total, axis=0, keepdims=True) / edge**3
 
     def spread_step(k, carry):
-        off = act[pl.ds(k * planes, planes)].reshape(rows // 8, 8, 128) - mean
+        off = act[k].reshape(edge * 2, 8, 128) - mean
         return carry + jnp.sum(off * off, axis=0)
 
-    total = lax.fori_loop(0, edge // planes, spread_step, jnp.zeros((8, 128), f32))
-    spread = jnp.sum(total, axis=0, keepdims=True)
-    put_stats(stats, mean, spread)
+    total = lax.fori_loop(0, edge, spread_step, jnp.zeros((8, 128), f32), unroll=4)
+    put_stats(stats, mean, jnp.sum(total, axis=0, keepdims=True))
 
 
 def put_stats(stats, mean, spread):
@@ -237,8 +276,8 @@
     return mean, lax.rsqrt(total / (rows * devices * width) + EPSILON)
 
 
-def silu(u):
-    return u / (1.0 + jnp.exp(-u))
+def silu_of_double(h):
+    return h + h * jnp.tanh(h)
 
 
 def norm_kernel(ny, nx, pos, act, stats, gain, offset, out, pooled, *refs):
@@ -247,11 +286,11 @@
     deep = edge // 2
     f32 = jnp.float32
     mean, scale = read_stats(stats, float(edge**3))
-    scale = scale * gain[...]
-    shift = offset[...]
+    scale = scale * (0.5 * gain[...])
+    shift = 0.5 * offset[...]
 
     def step(k, _):
-        value = silu((act[pl.ds(2 * k, 2)] - mean) * scale + shift).astype(jnp.bfloat16)
+        value = silu_of_double((act[pl.ds(2 * k, 2)] - mean) * scale + shift).astype(jnp.bfloat16)
         out[pl.ds(2 * k, 2)] = value
         value = value.astype(f32)
         value = value[0] + value[1]
@@ -285,28 +324,20 @@
             corners[k] = ends[k]
 
 
-def deep_kernel(ny, nx, tiles, pos, pooled, y_halos, x_halos, corners, front, back, own, got, partner, *refs):
-    act, stats, grid, packed, kernel = refs
+def place_kernel(tiles, _, got, after, kernel):
+    del after
+    pieces, _, part, _ = got.shape
+    for i in range(pieces):
+        at = (i % tiles * (pieces // tiles) + i // tiles) * part
+        for tap in range(27):
+            lane = tap % 9 * 128
+            kernel[tap // 9, at : at + part, lane : lane + 128] = got[i, tap]
+
+
+def deep_kernel(ny, nx, pos, pooled, y_halos, x_halos, corners, front, back, kernel, *refs):
+    act, stats, grid, packed = refs
     deep = pooled.shape[0]
     f32 = jnp.float32
-    shard = own.shape[1]
-    part = shard // 2
-    tile, odd = pos[ny + nx], pos[ny + nx + 1]
-
-    def place(rows, at):
-        for tap in range(27):
-            lane = (tap % 9) * 128
-            kernel[tap // 9, pl.ds(at, rows.shape[1]), lane : lane + 128] = rows[tap]
-
-    place(own, pl.multiple_of(tile * shard, shard))
-    for k in range(1, tiles):
-        base = lax.rem(tile + tiles - k, tiles) * shard
-        if got.shape[2] == shard:
-            place(got.at[k - 1], pl.multiple_of(base, shard))
-            continue
-        place(got.at[k - 1], pl.multiple_of(base + odd * part, part))
-        place(partner.at[k - 1], pl.multiple_of(base + (1 - odd) * part, part))
-
     grid[...] = jnp.zeros(grid.shape, f32)
     grid[1 : deep + 1, 1 : deep + 1, 8:16] = pooled[...]
     grid[0, 1 : deep + 1, 8:16] = front[0:deep]
@@ -374,7 +405,8 @@
     deep = edge // 2
     f32 = jnp.float32
     mean, scale = read_stats(stats, float(deep**3))
-    value = silu((act[...] - mean) * (scale * gain[...]) + offset[...]).astype(jnp.bfloat16)
+    scale = scale * (0.5 * gain[...])
+    value = silu_of_double((act[...] - mean) * scale + 0.5 * offset[...]).astype(jnp.bfloat16)
     lifted = jnp.dot(value, up[...], preferred_element_type=f32)
     rows = deep**3
     wide[pl.ds(0, rows, stride=2), :] = lifted
@@ -403,7 +435,7 @@
     y_low, x_low = square.low_sides()
     ny, nx = len(y_low), len(x_low)
     pos = jnp.stack(
-        [jnp.asarray(v, jnp.int32) for v in y_low + x_low + [lax.axis_index("yx"), lax.axis_index("gz") % 2]]
+        [jnp.asarray(v, jnp.int32) for v in y_low + x_low]
     )
 
     y, x, corner = square.halos(*square.edges(features))
@@ -412,29 +444,46 @@
     front, back = swap_depth(
         depth_face(features, y, x, corner, 0), depth_face(features, y, x, corner, -1)
     )
+    half_act = ((deep, edge, edge, channels), f32)
+    half_grid = ((deep + 2, edge + 2, edge, channels), bf16)
+    conv_flops = 27 * channels * channels * edge**3
+    near, taps = call(
+        front_half_kernel,
+        [half_act, ((9 * channels, 3 * channels), bf16)],
+        [half_grid],
+        pos,
+        features,
+        conv_weight.reshape(27, channels, channels),
+        flops=conv_flops,
+        nbytes=2 << 20,
+    )
+    (far,) = call(
+        back_half_kernel,
+        [half_act],
+        [half_grid],
+        pos,
+        features,
+        taps,
+        corner[0],
+        flops=conv_flops,
+        nbytes=2 << 20,
+    )
     act, stats = call(
-        functools.partial(mid_kernel, ny, nx),
+        functools.partial(rim_kernel, ny, nx),
         [((edge, edge, edge, channels), f32), ((devices, 8, channels), f32)],
-        [
-            ((edge + 2, edge + 2, edge, channels), bf16),
-            ((9 * channels, 3 * channels), bf16),
-            ((edge + 2, edge + 16, channels), f32),
-            ((edge + 2, edge, 3 * channels), bf16),
-        ],
-        pos,
-        features,
+        [((edge + 2, edge + 16, channels), f32), ((edge + 2, edge, 3 * channels), bf16)],
+        pos,
+        near,
+        far,
         jnp.stack(y),
         jnp.stack(x),
         jnp.stack(corner),
         front,
         back,
-        conv_weight.reshape(27, channels, channels),
-        flops=2 * 27 * channels * channels * edge**3,
-        nbytes=6 << 20,
-    )
-    stats, *got = lax.optimization_barrier((stats, *got))
-    got = jnp.stack(got)
-    partner = swap_halves(got, got.shape[2] == own.shape[1])
+        taps,
+        flops=conv_flops // 8,
+        nbytes=5 << 20,
+    )
     stats = share(stats)
     out, pooled, *edges = call(
         functools.partial(norm_kernel, ny, nx),
@@ -458,13 +507,21 @@
     front, back = swap_depth(
         depth_face(pooled, y, x, corner, 0), depth_face(pooled, y, x, corner, -1)
     )
+    (kernel,) = call(
+        functools.partial(place_kernel, tiles),
+        [((3, deep_channels, 9 * channels), bf16)],
+        [],
+        pos,
+        got,
+        corner[0],
+        nbytes=4 << 20,
+    )
     deep_act, stats = call(
-        functools.partial(deep_kernel, ny, nx, tiles),
-        [((deep**3, deep_channels), f32), ((devices, 8, deep_channels), f32)],
+        functools.partial(deep_kernel, ny, nx),
+        [((deep**3, deep_channels), f32), ((tiles, 8, deep_channels), f32)],
         [
             ((deep + 2, deep + 2, 24, channels), f32),
             ((deep + 2, deep // 2 + 1, 2, 16, 3 * channels), bf16),
-            ((3, deep_channels, 9 * channels), bf16),
         ],
         pos,
         pooled,
@@ -473,13 +530,11 @@
         jnp.stack(corner),
         front,
         back,
-        own,
-        got,
-        partner,
+        kernel,
         flops=2 * 27 * channels * deep_channels * deep**3,
         nbytes=4 << 20,
     )
-    stats = share(stats)
+    stats = share_by_axis(stats)
     (decoded,) = call(
         final_kernel,
         [((edge, edge, edge, channels), bf16)],

time: 96.2 us -> 86.2 us (0.90)
  waiting for transfers between devices: 22.6 us -> 3.96 us
  starting transfers between devices: 35.2 us -> 17.1 us
  blocking collectives: 13.8 us -> 30.2 us
  between operations: 0.21 us -> 13.7 us
  other arithmetic: 2.71 us -> 0.32 us
    all_to_all x0 -> x2, blocking collectives: none -> 15.9 us  [the longest x1 8.72 us: share_by_axis(): tiles = lax.all_to_all(statistics, 'yx', 0, 0)]
    all_to_all x1 -> x0, starting transfers between devices: 8.12 us -> none  [share(): return lax.all_to_all(statistics, PART, 0, 0)]
    ppermute x2, waiting for transfers between devices: 8.55 us -> 1.03 us  [halos(): corner = lax.ppermute(corners[0], 'yx', self.swap_route(3))]
    ppermute x4 -> x0, starting transfers between devices: 6.59 us -> none  [the longest x3 6.11 us: gather_shards(): lax.ppermute(mine, 'yx', [(i, (i + k) % tiles) for i in range(tiles)])]
    ppermute x2, waiting for transfers between devices: 6.26 us -> 0.22 us  [swap_depth(): lax.ppermute(low, 'gz', [(j, i) for i, j in up])]
    all_to_all x1 -> x0, waiting for transfers between devices: 4.93 us -> none  [share(): return lax.all_to_all(statistics, PART, 0, 0)]
    ppermute x2, starting transfers between devices: 6.44 us -> 3.04 us  [halos(): x = lax.ppermute(x_edges[0], 'yx', self.swap_route(1))]
    ppermute x2, starting transfers between devices: 2.57 us -> 4.33 us  [swap_depth(): lax.ppermute(high, 'gz', up)]
  transfers between devices with their start and end apart: 15 -> 11, of which waited for: 7 -> 5; matrix products, arithmetic and copies ran while one was open for 5% -> 3% of each run, Pallas kernels for 12% -> 13%
where the time goes in v3:
time: 86.2 us; the launch traced here: 85.9 us
  blocking collectives  30.2 us (35%)
  starting transfers between devices  17.1 us (20%)
  Pallas kernels  15.8 us (18%)
  between operations  13.7 us (16%)
  local copies, waits for them, and re-layouts  4.72 us (5%)
  waiting for transfers between devices  3.96 us (5%)
    pallas_call x7, Pallas kernels, call(): pl.pallas_call(kernel, out_shape=[jax.ShapeDtypeStruct(shape, dtype) for...  15.8 us
    all_to_all x1, blocking collectives, share(): return lax.all_to_all(statistics, PART, 0, 0)  14.3 us
    all_to_all x1, blocking collectives, share_by_axis(): tiles = lax.all_to_all(statistics, 'yx', 0, 0)  8.72 us
    all_to_all x1, blocking collectives, share_by_axis(): lax.all_to_all(jnp.broadcast_to(tiles[None], (depth,) + tiles.shape), 'gz...  7.2 us
    ppermute x2, starting transfers between devices, halos(): y = lax.ppermute(y_edges[0], 'yx', self.swap_route(2))  5.17 us
    ppermute x2, starting transfers between devices, swap_depth(): lax.ppermute(high, 'gz', up)  4.33 us
    ppermute x2, starting transfers between devices, halos(): x = lax.ppermute(x_edges[0], 'yx', self.swap_route(1))  3.04 us
    ppermute x2, starting transfers between devices, swap_depth(): lax.ppermute(low, 'gz', [(j, i) for i, j in up])  2.57 us
  transfers between devices with their start and end apart: 11, of which 5 were waited for; matrix products, arithmetic and copies ran while one was open for 3% of the time, Pallas kernels for 13%

profile of v3, /device:TPU:0, one launch (start us, length us, event | category | flops | bytes accessed | tf_op | source)
XLA Modules:
  0.0 85.9 jit_solution(12866123761745357806)
XLA Ops:
  6.5 0.0 copy-start
  6.5 0.0 copy-start.2
  6.5 0.0 copy-start.8
  6.5 0.0 all-gather.3.cloned.1.call-start
  6.6 1.0 %fusion.4 = (bf16[16,1,16,128]{3,2,1,0:T(8,128)(2,1)S(1)}, bf16[16,1,16,128]{3,2,1,0:T(8,128)(2,1)S(1)}) fusion(bf16[16,16,16,128]{3,2,1,0:T(8,128)(2,1)} %x.7), kind=kLoop, calls=%fused_computation.21 | loop fusion | bytes 262144 | tf_op jit(solution)/shard_map/slice | solution.py:61
  7.6 4.1 %collective-permute-start.1 = (bf16[16,16,128]{2,0,1:T(8,128)(2,1)S(1)}, bf16[16,16,128]{2,0,1:T(8,128)(2,1)S(1)}, u32[]{:S(2)}, u32[]{:S(2)}) collective-permute-start(bf16[16,16,128]{2,0,1:T(8,128)(2,1)S(1)} %fusion.1), channel_id=1, source_target_pairs={{0,2},{1,3},{2,0},{3,1},{4,6},{5,7},{6,4},{7,5},{8,10},{9,11},{10,... | collective-permute-start | bytes 196616 | tf_op jit(solution)/shard_map/ppermute | solution.py:45
  11.7 1.3 %collective-permute-start = (bf16[16,128]{1,0:T(8,128)(2,1)S(1)}, bf16[16,128]{1,0:T(8,128)(2,1)S(1)}, u32[]{:S(2)}, u32[]{:S(2)}) collective-permute-start(bf16[16,128]{1,0:T(8,128)(2,1)S(1)} %fusion.2), channel_id=1, source_target_pairs={{0,3},{1,2},{2,1},{3,0},{4,7},{5,6},{6,5},{7,4},{8,11},{9,10},{10,... | collective-permute-start | bytes 12296 | tf_op jit(solution)/shard_map/ppermute | solution.py:47
  13.1 0.0 copy-done
  13.1 0.7 constant_dynamic-slice_fusion
  13.8 0.0 all-gather.3.cloned.1.call-update
  13.8 1.4 %fusion.3 = (bf16[16,16,1,128]{3,2,1,0:T(2,128)(2,1)S(1)}, bf16[16,16,1,128]{3,2,1,0:T(2,128)(2,1)S(1)}) fusion(bf16[16,16,16,128]{3,2,1,0:T(8,128)(2,1)} %x.7), kind=kLoop, calls=%fused_computation.20 | loop fusion | bytes 262144 | tf_op jit(solution)/shard_map/slice | solution.py:62
  15.2 0.3 collective-permute-start.2
  15.5 0.1 pad_add_fusion._.pos
  15.6 0.0 copy-done.2
  15.6 0.0 copy-done.8
  15.6 0.0 copy-start.10
  15.6 3.4 %shard_map.82 = (f32[8,16,16,128]{3,2,1,0:T(8,128)S(1)}, bf16[1152,384]{1,0:T(8,128)(2,1)S(1)}) custom-call(s32[2]{0:T(128)S(1)} %pad_add_fusion._.pos, bf16[16,16,16,128]{3,2,1,0:T(8,128)(2,1)S(1)} %copy-done.2, bf16[27,128,128]{2,1,0:T(8,128)(2,1)S(1)} %bitcast.55), custom_call_target="tpu_custom_call" | custom-call | flops 1811939328 | bytes 2097152 | tf_op jit(solution)/shard_map/pallas_call | solution.py:106
  19.1 0.0 collective-permute-done.after
  19.1 0.0 copy-done.10
  19.1 0.1 select_bitcast_fusion.1
  19.2 0.0 collective-permute-done.1
  19.2 0.3 collective-permute-done.2
  19.6 1.3 %collective-permute-start.3 = (bf16[19,16,128]{2,1,0:T(8,128)(2,1)S(1)}, bf16[19,16,128]{2,1,0:T(8,128)(2,1)S(1)}, u32[]{:S(2)}, u32[]{:S(2)}) collective-permute-start(bf16[19,16,128]{2,1,0:T(8,128)(2,1)S(1)} %pad_maximum_fusion), channel_id=1, source_target_pairs={{0,4},{4,8},{8,12},{1,5},{5,9},{9,13},{2,6},{6,10},{10,14},{3,7},{... | collective-permute-start | bytes 233480 | tf_op jit(solution)/shard_map/ppermute | solution.py:73
  20.9 1.3 %collective-permute-start.4 = (bf16[19,16,128]{2,1,0:T(8,128)(2,1)S(1)}, bf16[19,16,128]{2,1,0:T(8,128)(2,1)S(1)}, u32[]{:S(2)}, u32[]{:S(2)}) collective-permute-start(bf16[19,16,128]{2,1,0:T(8,128)(2,1)S(1)} %pad_maximum_fusion.1), channel_id=1, source_target_pairs={{4,0},{8,4},{12,8},{5,1},{9,5},{13,9},{6,2},{10,6},{14,10},{7,3},{... | collective-permute-start | bytes 233480 | tf_op jit(solution)/shard_map/ppermute | solution.py:73
  22.2 3.3 %shard_map.83.refs_1_ = f32[8,16,16,128]{3,2,1,0:T(8,128)S(1)} custom-call(s32[2]{0:T(128)S(1)} %pad_add_fusion._.pos, bf16[16,16,16,128]{3,2,1,0:T(8,128)(2,1)S(1)} %copy-done.2, bf16[1152,384]{1,0:T(8,128)(2,1)S(1)} %get-tuple-element.17.taps.refs_7_, bf16[16,128]{1,0:T(8,128)(2,1)S(1)} %collective-permute-done.after), custom_call_target="tpu_custom_call" | custom-call | flops 1811939328 | bytes 2097152 | tf_op jit(solution)/shard_map/pallas_call | solution.py:106
  25.5 0.0 copy-start.6
  25.5 0.0 copy-start.7
  25.6 0.0 collective-permute-done.3.refs_5_
  25.6 0.2 collective-permute-done.4.refs_6_
  25.8 1.9 %shard_map.84 = (f32[16,16,16,128]{3,2,1,0:T(8,128)S(1)}, f32[16,8,128]{2,1,0:T(8,128)S(1)}) custom-call(s32[2]{0:T(128)S(1)} %pad_add_fusion._.pos, f32[8,16,16,128]{3,2,1,0:T(8,128)S(1)} %get-tuple-element.16.refs_0_, f32[8,16,16,128]{3,2,1,0:T(8,128)S(1)} %shard_map.83.refs_1_, bf16[1,16,16,128]{3,2,1,0:T(8,128)(2,1)S(1)} %copy.22.refs_2_, ...), custom_call_target="tpu_custom_call" | custom-call | flops 226492416 | bytes 5242880 | tf_op jit(solution)/shard_map/pallas_call | solution.py:106
  27.7 0.0 copy-start.9
  27.7 14.3 %all_to_all.15.stats = f32[16,8,128]{2,1,0:T(8,128)S(1)} all-to-all(f32[16,8,128]{2,1,0:T(8,128)S(1)} %get-tuple-element.19), channel_id=1, replica_groups=mesh['cand'=2,'gz'=4,'yx'=4] {'gz','yx'}, dimensions={0} | all-to-all | bytes 131072 | tf_op jit(solution)/shard_map/all_to_all | solution.py:94
  42.0 0.0 copy-done.6
  42.0 0.0 copy-done.7
  42.0 1.8 %shard_map.85 = (bf16[16,16,16,128]{3,2,1,0:T(8,128)(2,1)S(1)}, f32[8,8,8,128]{3,2,1,0:T(8,128)S(1)}, f32[1,8,8,128]{3,2,1,0:T(8,128)S(1)}, f32[1,8,8,128]{3,2,1,0:T(8,128)S(1)}, f32[1,8,128]{2,1,0:T(8,128)S(1)}) custom-call(s32[2]{0:T(128)S(1)} %pad_add_fusion._.pos, f32[16,16,16,128]{3,2,1,0:T(8,128)S(1)} %get-tuple-element.18.act, ...), custom_call_target="tpu_custom_call" | custom-call | flops 10485760 | bytes 3145728 | tf_op jit(solution)/shard_map/pallas_call | solution.py:106
  43.8 0.6 collective-permute-start.7
  44.5 1.1 %collective-permute-start.5 = (f32[8,8,128]{2,1,0:T(8,128)S(1)}, f32[8,8,128]{2,1,0:T(8,128)S(1)}, u32[]{:S(2)}, u32[]{:S(2)}) collective-permute-start(f32[8,8,128]{2,1,0:T(8,128)S(1)} %bitcast.57), channel_id=1, source_target_pairs={{0,2},{1,3},{2,0},{3,1},{4,6},{5,7},{6,4},{7,5},{8,10},{9,11},{10,... | collective-permute-start | bytes 98312 | tf_op jit(solution)/shard_map/ppermute | solution.py:45
  45.5 2.7 %collective-permute-start.6 = (f32[8,8,128]{2,1,0:T(8,128)S(1)}, f32[8,8,128]{2,1,0:T(8,128)S(1)}, u32[]{:S(2)}, u32[]{:S(2)}) collective-permute-start(f32[8,8,128]{2,1,0:T(8,128)S(1)} %bitcast.56), channel_id=1, source_target_pairs={{0,1},{1,0},{2,3},{3,2},{4,5},{5,4},{6,7},{7,6},{8,9},{9,8},{10,11... | collective-permute-start | bytes 98312 | tf_op jit(solution)/shard_map/ppermute | solution.py:46
  48.3 1.0 %collective-permute-done.7.after = f32[8,128]{1,0:T(8,128)S(1)} collective-permute-done((f32[8,128]{1,0:T(8,128)S(1)}, f32[8,128]{1,0:T(8,128)S(1)}, u32[]{:S(2)}, u32[]{:S(2)}) %collective-permute-start.7) | collective-permute-done | bytes 4128 | tf_op jit(solution)/shard_map/ppermute | solution.py:47
  49.3 0.0 copy-done.9
  49.3 0.1 select_bitcast_fusion
  49.4 1.6 %collective-permute-done.5 = f32[8,8,128]{2,1,0:T(8,128)S(1)} collective-permute-done((f32[8,8,128]{2,1,0:T(8,128)S(1)}, f32[8,8,128]{2,1,0:T(8,128)S(1)}, u32[]{:S(2)}, u32[]{:S(2)}) %collective-permute-start.5) | collective-permute-done | bytes 32800 | tf_op jit(solution)/shard_map/ppermute | solution.py:45
  51.0 0.7 collective-permute-done.6
  51.8 1.3 %collective-permute-start.9 = (f32[11,8,128]{2,1,0:T(8,128)S(1)}, f32[11,8,128]{2,1,0:T(8,128)S(1)}, u32[]{:S(2)}, u32[]{:S(2)}) collective-permute-start(f32[11,8,128]{2,1,0:T(8,128)S(1)} %pad_maximum_fusion.3), channel_id=1, source_target_pairs={{4,0},{8,4},{12,8},{5,1},{9,5},{13,9},{6,2},{10,6},{14,10},{7,3},{... | collective-permute-start | bytes 135176 | tf_op jit(solution)/shard_map/ppermute | solution.py:73
  53.1 3.0 %collective-permute-start.8 = (f32[11,8,128]{2,1,0:T(8,128)S(1)}, f32[11,8,128]{2,1,0:T(8,128)S(1)}, u32[]{:S(2)}, u32[]{:S(2)}) collective-permute-start(f32[11,8,128]{2,1,0:T(8,128)S(1)} %pad_maximum_fusion.2), channel_id=1, source_target_pairs={{0,4},{4,8},{8,12},{1,5},{5,9},{9,13},{2,6},{6,10},{10,14},{3,7},{... | collective-permute-start | bytes 135176 | tf_op jit(solution)/shard_map/ppermute | solution.py:73
  56.1 0.0 all-gather.3.cloned.1.call-done
  56.1 0.0 copy-start.1
  56.1 1.5 %copy-done.1 = bf16[432,16,128]{2,1,0:T(8,128)(2,1)S(1)} copy-done((bf16[432,16,128]{2,1,0:T(8,128)(2,1)S(1)}, bf16[432,16,128]{2,1,0:T(8,128)(2,1)}, u32[]{:S(2)}) %copy-start.1) | copy-done | bytes 1769496
  57.6 0.8 shard_map.86.kernel
  58.5 0.0 collective-permute-done.9.back
  58.5 0.0 collective-permute-done.8.front
  58.5 0.0 copy-start.3
  58.5 0.0 copy-start.4
  58.5 0.0 copy-start.5
  58.5 2.0 %shard_map.87 = (f32[512,256]{1,0:T(8,128)S(1)}, f32[4,8,256]{2,1,0:T(8,128)S(1)}) custom-call(s32[2]{0:T(128)S(1)} %pad_add_fusion._.pos, f32[8,8,8,128]{3,2,1,0:T(8,128)S(1)} %get-tuple-element.20.pooled, f32[1,8,8,128]{3,2,1,0:T(8,128)S(1)} %bitcast.49, f32[1,8,8,128]{3,2,1,0:T(8,128)S(1)} %bitcast.50, f32[1,8,128]{2,1,0:T(8,128)S(1)} %bitcast.48, ...), custom_call_target="tpu_custom_call" | custom-call | flops 905969664 | bytes 4194304 | tf_op jit(solution)/shard_map/pallas_call | solution.py:106
  60.5 8.7 %all_to_all.16 = f32[4,8,256]{2,1,0:T(8,128)S(1)} all-to-all(f32[4,8,256]{2,1,0:T(8,128)S(1)} %get-tuple-element.25), channel_id=1, replica_groups=mesh['cand'=2,'gz'=4,'yx'=4] {'yx'}, dimensions={0} | all-to-all | bytes 65536 | tf_op jit(solution)/shard_map/all_to_all | solution.py:98
  69.2 7.2 %all_to_all.17 = f32[4,4,8,256]{3,2,1,0:T(8,128)S(1)} all-to-all(f32[4,4,8,256]{3,2,1,0:T(8,128)S(1)} %broadcast_in_dim.22), channel_id=1, replica_groups=mesh['cand'=2,'gz'=4,'yx'=4] {'gz'}, dimensions={0} | all-to-all | bytes 262144 | tf_op jit(solution)/shard_map/all_to_all | solution.py:100
  76.4 0.0 copy-done.3
  76.4 0.0 copy-done.4
  76.4 0.0 copy-done.5
  76.4 2.6 %shard_map.88 = bf16[16,16,16,128]{3,2,1,0:T(8,128)(2,1)} custom-call(s32[2]{0:T(128)S(1)} %pad_add_fusion._.pos, f32[512,256]{1,0:T(8,128)S(1)} %get-tuple-element.24.act, f32[16,8,256]{2,1,0:T(8,128)S(1)} %bitcast.45, f32[1,256]{1,0:T(1,128)S(1)} %bitcast.51, f32[1,256]{1,0:T(1,128)S(1)} %bitcast.52, bf16[256,128]{1,0:T(8,128)(2,1)S(1)} %copy-done.3, ...), custom_call_target="tpu_custom_call" | custom-call | flops 67108864 | bytes 3145728 | tf_op jit(solution)/shard_map/pallas_call | solution.py:106
  (21 shorter events, 0.2 us)
Async XLA Ops:
  6.5 6.6 %copy-start = (bf16[3,3,3,128,64]{3,4,2,1,0:T(8,128)(2,1)S(1)}, bf16[3,3,3,128,64]{3,4,2,1,0:T(8,128)(2,1)}, u32[]{:S(2)}) copy-start(bf16[3,3,3,128,64]{3,4,2,1,0:T(8,128)(2,1)} %param.12) | copy-start | bytes 1327108
  6.5 9.1 %copy-start.2 = (bf16[16,16,16,128]{3,2,1,0:T(8,128)(2,1)S(1)}, bf16[16,16,16,128]{3,2,1,0:T(8,128)(2,1)}, u32[]{:S(2)}) copy-start(bf16[16,16,16,128]{3,2,1,0:T(8,128)(2,1)} %x.7) | copy-start | bytes 3145732
  6.5 9.1 %copy-start.8 = (bf16[3,3,3,128,128]{4,3,2,1,0:T(8,128)(2,1)S(1)}, bf16[3,3,3,128,128]{4,3,2,1,0:T(8,128)(2,1)}, u32[]{:S(2)}) copy-start(bf16[3,3,3,128,128]{4,3,2,1,0:T(8,128)(2,1)} %param.9) | copy-start | bytes 2654212
  6.5 49.6 %all-gather.3.cloned.1.call-start = ((), (), s32[]{:S(2)}) async-start(), calls=%async_computation.3 | async-start | bytes 1880064 | tf_op jit(solution)/shard_map/all_gather | solution.py:90
  7.6 11.6 %collective-permute-start.1 = (bf16[16,16,128]{2,0,1:T(8,128)(2,1)S(1)}, bf16[16,16,128]{2,0,1:T(8,128)(2,1)S(1)}, u32[]{:S(2)}, u32[]{:S(2)}) collective-permute-start(bf16[16,16,128]{2,0,1:T(8,128)(2,1)S(1)} %fusion.1), channel_id=1, source_target_pairs={{0,2},{1,3},{2,0},{3,1},{4,6},{5,7},{6,4},{7,5},{8,10},{9,11},{10,... | collective-permute-start | bytes 196616 | tf_op jit(solution)/shard_map/ppermute | solution.py:45
  11.7 7.3 %collective-permute-start = (bf16[16,128]{1,0:T(8,128)(2,1)S(1)}, bf16[16,128]{1,0:T(8,128)(2,1)S(1)}, u32[]{:S(2)}, u32[]{:S(2)}) collective-permute-start(bf16[16,128]{1,0:T(8,128)(2,1)S(1)} %fusion.2), channel_id=1, source_target_pairs={{0,3},{1,2},{2,1},{3,0},{4,7},{5,6},{6,5},{7,4},{8,11},{9,10},{10,... | collective-permute-start | bytes 12296 | tf_op jit(solution)/shard_map/ppermute | solution.py:47
  15.2 4.3 %collective-permute-start.2 = (bf16[16,16,128]{2,1,0:T(8,128)(2,1)S(1)}, bf16[16,16,128]{2,1,0:T(8,128)(2,1)S(1)}, u32[]{:S(2)}, u32[]{:S(2)}) collective-permute-start(bf16[16,16,128]{2,1,0:T(8,128)(2,1)S(1)} %fusion), channel_id=1, source_target_pairs={{0,1},{1,0},{2,3},{3,2},{4,5},{5,4},{6,7},{7,6},{8,9},{9,8},{10,11... | collective-permute-start | bytes 196616 | tf_op jit(solution)/shard_map/ppermute | solution.py:46
  15.6 3.5 %copy-start.10 = (pred[16]{0:T(512)(128)(4,1)S(1)}, pred[16]{0:T(512)(128)(4,1)}, u32[]{:S(2)}) copy-start(pred[16]{0:T(512)(128)(4,1)} %constant.39.clone.1) | copy-start | bytes 52
  19.6 6.0 %collective-permute-start.3 = (bf16[19,16,128]{2,1,0:T(8,128)(2,1)S(1)}, bf16[19,16,128]{2,1,0:T(8,128)(2,1)S(1)}, u32[]{:S(2)}, u32[]{:S(2)}) collective-permute-start(bf16[19,16,128]{2,1,0:T(8,128)(2,1)S(1)} %pad_maximum_fusion), channel_id=1, source_target_pairs={{0,4},{4,8},{8,12},{1,5},{5,9},{9,13},{2,6},{6,10},{10,14},{3,7},{... | collective-permute-start | bytes 233480 | tf_op jit(solution)/shard_map/ppermute | solution.py:73
  20.9 4.9 %collective-permute-start.4 = (bf16[19,16,128]{2,1,0:T(8,128)(2,1)S(1)}, bf16[19,16,128]{2,1,0:T(8,128)(2,1)S(1)}, u32[]{:S(2)}, u32[]{:S(2)}) collective-permute-start(bf16[19,16,128]{2,1,0:T(8,128)(2,1)S(1)} %pad_maximum_fusion.1), channel_id=1, source_target_pairs={{4,0},{8,4},{12,8},{5,1},{9,5},{13,9},{6,2},{10,6},{14,10},{7,3},{... | collective-permute-start | bytes 233480 | tf_op jit(solution)/shard_map/ppermute | solution.py:73
  25.5 16.5 %copy-start.6 = (f32[128]{0:T(128)S(1)}, f32[128]{0:T(128)}, u32[]{:S(2)}) copy-start(f32[128]{0:T(128)} %param.10) | copy-start | bytes 1540
  25.5 16.5 %copy-start.7 = (f32[128]{0:T(128)S(1)}, f32[128]{0:T(128)}, u32[]{:S(2)}) copy-start(f32[128]{0:T(128)} %param.11) | copy-start | bytes 1540
  27.7 21.6 %copy-start.9 = (pred[8]{0:T(512)(128)(4,1)S(1)}, pred[8]{0:T(512)(128)(4,1)}, u32[]{:S(2)}) copy-start(pred[8]{0:T(512)(128)(4,1)} %constant.41.clone.1) | copy-start | bytes 28
  43.8 5.5 %collective-permute-start.7 = (f32[8,128]{1,0:T(8,128)S(1)}, f32[8,128]{1,0:T(8,128)S(1)}, u32[]{:S(2)}, u32[]{:S(2)}) collective-permute-start(f32[8,128]{1,0:T(8,128)S(1)} %bitcast.58), channel_id=1, source_target_pairs={{0,3},{1,2},{2,1},{3,0},{4,7},{5,6},{6,5},{7,4},{8,11},{9,10},{10,... | collective-permute-start | bytes 12296 | tf_op jit(solution)/shard_map/ppermute | solution.py:47
  44.5 6.5 %collective-permute-start.5 = (f32[8,8,128]{2,1,0:T(8,128)S(1)}, f32[8,8,128]{2,1,0:T(8,128)S(1)}, u32[]{:S(2)}, u32[]{:S(2)}) collective-permute-start(f32[8,8,128]{2,1,0:T(8,128)S(1)} %bitcast.57), channel_id=1, source_target_pairs={{0,2},{1,3},{2,0},{3,1},{4,6},{5,7},{6,4},{7,5},{8,10},{9,11},{10,... | collective-permute-start | bytes 98312 | tf_op jit(solution)/shard_map/ppermute | solution.py:45
  45.5 6.2 %collective-permute-start.6 = (f32[8,8,128]{2,1,0:T(8,128)S(1)}, f32[8,8,128]{2,1,0:T(8,128)S(1)}, u32[]{:S(2)}, u32[]{:S(2)}) collective-permute-start(f32[8,8,128]{2,1,0:T(8,128)S(1)} %bitcast.56), channel_id=1, source_target_pairs={{0,1},{1,0},{2,3},{3,2},{4,5},{5,4},{6,7},{7,6},{8,9},{9,8},{10,11... | collective-permute-start | bytes 98312 | tf_op jit(solution)/shard_map/ppermute | solution.py:46
  51.8 6.7 %collective-permute-start.9 = (f32[11,8,128]{2,1,0:T(8,128)S(1)}, f32[11,8,128]{2,1,0:T(8,128)S(1)}, u32[]{:S(2)}, u32[]{:S(2)}) collective-permute-start(f32[11,8,128]{2,1,0:T(8,128)S(1)} %pad_maximum_fusion.3), channel_id=1, source_target_pairs={{4,0},{8,4},{12,8},{5,1},{9,5},{13,9},{6,2},{10,6},{14,10},{7,3},{... | collective-permute-start | bytes 135176 | tf_op jit(solution)/shard_map/ppermute | solution.py:73
  53.1 5.4 %collective-permute-start.8 = (f32[11,8,128]{2,1,0:T(8,128)S(1)}, f32[11,8,128]{2,1,0:T(8,128)S(1)}, u32[]{:S(2)}, u32[]{:S(2)}) collective-permute-start(f32[11,8,128]{2,1,0:T(8,128)S(1)} %pad_maximum_fusion.2), channel_id=1, source_target_pairs={{0,4},{4,8},{8,12},{1,5},{5,9},{9,13},{2,6},{6,10},{10,14},{3,7},{... | collective-permute-start | bytes 135176 | tf_op jit(solution)/shard_map/ppermute | solution.py:73
  56.1 1.5 %copy-start.1 = (bf16[432,16,128]{2,1,0:T(8,128)(2,1)S(1)}, bf16[432,16,128]{2,1,0:T(8,128)(2,1)}, u32[]{:S(2)}) copy-start(bf16[432,16,128]{2,1,0:T(8,128)(2,1)} %all-gather.3.cloned.1.call-done) | copy-start | bytes 5308420
  58.5 17.9 %copy-start.3 = (bf16[256,128]{1,0:T(8,128)(2,1)S(1)}, bf16[256,128]{1,0:T(8,128)(2,1)}, u32[]{:S(2)}) copy-start(bf16[256,128]{1,0:T(8,128)(2,1)} %up.1) | copy-start | bytes 196612
  58.5 17.9 %copy-start.4 = (f32[256]{0:T(256)S(1)}, f32[256]{0:T(256)}, u32[]{:S(2)}) copy-start(f32[256]{0:T(256)} %param.13) | copy-start | bytes 3076
  58.5 17.9 %copy-start.5 = (f32[256]{0:T(256)S(1)}, f32[256]{0:T(256)}, u32[]{:S(2)}) copy-start(f32[256]{0:T(256)} %param.14) | copy-start | bytes 3076
Sparse Core Ops, SparseCore 0:
  13.9 41.1 all-gather.2

commit v4 on v3

--- a/solution.py
+++ b/solution.py
@@ -55,17 +55,6 @@
         ]
         return y, x, corner
 
-    def edges(self, volume):
-        if self.folded:
-            low_y, low_x = self.row == 1, self.column == 1
-            y = jnp.where(low_y, volume[:, 0], volume[:, -1])
-            x = jnp.where(low_x, volume[:, :, 0], volume[:, :, -1])
-            corner = jnp.where(low_x, y[:, 0], y[:, -1])
-            return [y], [x], [corner]
-        y = [volume[:, 0], volume[:, -1]]
-        x = [volume[:, :, 0], volume[:, :, -1]]
-        return y, x, [row[:, k] for row in y for k in (0, -1)]
-
 
 def swap_depth(low, high):
     size = lax.axis_size("gz")
@@ -81,43 +70,98 @@
     return jnp.concatenate(rows)
 
 
-def gather_shards(weight):
-    depth = lax.axis_size("gz")
-    part = weight.shape[1] // depth
-    if part % 16:
-        return lax.all_gather(weight, "yx")
-    mine = lax.dynamic_slice_in_dim(weight, lax.axis_index("gz") * part, part, axis=1)
-    return lax.all_gather(mine, PART)
-
-
-def share(statistics):
-    return lax.all_to_all(statistics, PART, 0, 0)
-
-
-def share_by_axis(statistics):
-    tiles = lax.all_to_all(statistics, "yx", 0, 0)
-    depth = lax.axis_size("gz")
-    every = lax.all_to_all(jnp.broadcast_to(tiles[None], (depth,) + tiles.shape), "gz", 0, 0)
-    return every.reshape((-1,) + statistics.shape[1:])
-
-
-def call(kernel, outs, scratch, scalars, *arrays, flops=0, nbytes=0):
+def split_axes(rows):
+    return ("cand", "gz")[: 2 if rows % 64 == 0 else 0]
+
+
+def share_pieces(got, axes):
+    held = stack(*got)[None]
+    for axis in axes:
+        held = stack(held, swap(held, axis, 1))
+        held = held.reshape((-1,) + held.shape[2:])
+    return held
+
+
+def rotate_shards(piece):
+    tiles = lax.axis_size("yx")
+    return [
+        lax.ppermute(piece, "yx", [(i, (i + k) % tiles) for i in range(tiles)]) for k in range(1, tiles)
+    ]
+
+
+def swap(block, axis, mask):
+    return lax.ppermute(block, axis, [(i, i ^ mask) for i in range(lax.axis_size(axis))])
+
+
+def merge(stats, rows, axes):
+    for axis in axes:
+        mask = 1
+        while mask < lax.axis_size(axis):
+            other = swap(stats, axis, mask)
+            off = stats[0] - other[0]
+            mean = 0.5 * (stats[0] + other[0])
+            stats = jnp.stack([mean, stats[1] + other[1] + (0.5 * rows) * (off * off)])
+            rows, mask = 2 * rows, 2 * mask
+    return stats, rows
+
+
+def call(kernel, outs, scratch, scalars, *arrays, flops=0, nbytes=0, copied_out=False):
     smem, vmem = pl.BlockSpec(memory_space=pltpu.SMEM), pl.BlockSpec(memory_space=pltpu.VMEM)
+    out_spec = pl.BlockSpec(memory_space=pl.ANY) if copied_out else vmem
     return pl.pallas_call(
         kernel,
         out_shape=[jax.ShapeDtypeStruct(shape, dtype) for shape, dtype in outs],
         in_specs=[smem] + [vmem] * len(arrays),
-        out_specs=[vmem] * len(outs),
-        scratch_shapes=[pltpu.VMEM(shape, dtype) for shape, dtype in scratch],
+        out_specs=[out_spec] * len(outs),
+        scratch_shapes=[pltpu.VMEM(*entry) if isinstance(entry, tuple) else entry for entry in scratch],
         compiler_params=pltpu.CompilerParams(vmem_limit_bytes=VMEM_BYTES),
         cost_estimate=pl.CostEstimate(flops=flops, bytes_accessed=nbytes, transcendentals=0),
     )(scalars, *arrays)
+
+
+def edge_kernel(ny, nx, pos, x, y_edges, x_edges, corners, lines):
+    edge = x.shape[0]
+    f32, bf16 = jnp.float32, jnp.bfloat16
+    for i in range(ny):
+        at = jnp.where(pos[i] == 1, 0, edge - 1) if ny == 1 else (0, edge - 1)[i]
+        y_edges[i] = x[:, at]
+    flat = lines.reshape(edge * edge * 8, 128)
+    for j in range(nx):
+        first = x[:, :, 0:8].astype(f32)
+        last = x[:, :, edge - 8 : edge].astype(f32)
+        if nx == 1:
+            low = pos[ny] == 1
+            turned = pltpu.roll(last.reshape(edge * edge, 8, 128), 1, 1)
+            kept = jnp.where(low, first.reshape(edge * edge, 8, 128), turned)
+        else:
+            kept = (first, pltpu.roll(last.reshape(edge * edge, 8, 128), 1, 1))[j]
+        lines[...] = kept.reshape(edge * edge, 8, 128)
+        column = flat[pl.ds(0, edge * edge, stride=8), :]
+        x_edges[j] = column.astype(bf16).reshape(edge, edge, 128)
+        for i in range(ny):
+            first_y = flat[pl.ds(0, edge, stride=8 * edge), :]
+            last_y = flat[pl.ds(8 * (edge - 1), edge, stride=8 * edge), :]
+            kept = jnp.where(pos[i] == 1, first_y, last_y) if ny == 1 else (first_y, last_y)[i]
+            corners[i * nx + j] = kept.astype(bf16)
 
 
 def spread_taps(weight, taps):
     for tap in range(27):
         row, lane = tap // 3 * 128, tap % 3 * 128
         taps[row : row + 128, lane : lane + 128] = weight[tap]
+
+
+def pair_taps(weight, pairs):
+    for dz in range(3):
+        for line in range(4):
+            row = (dz * 4 + line) * 128
+            for out in range(2):
+                lane = out * 128
+                if 0 <= line - out < 3:
+                    block = weight[dz * 9 + (line - out) * 3 + 2]
+                else:
+                    block = jnp.zeros((128, 128), pairs.dtype)
+                pairs[row : row + 128, lane : lane + 128] = block
 
 
 def join_x(wide, edge):
@@ -127,7 +171,7 @@
     return wide[:, :, 128:256] + after + before
 
 
-def local_planes(x, lo, count, taps, grid, act):
+def local_planes(x, lo, count, taps, pairs, grid, act):
     edge = x.shape[0]
     blank = jnp.zeros((count + 2,) + grid.shape[2:], grid.dtype)
     grid[:, 0] = blank
@@ -140,6 +184,8 @@
     grid[first - lo + 1 : last - lo + 1, 1 : edge + 1] = x[first:last]
     planes = 2
     rows = planes * edge * edge
+    place = lax.broadcasted_iota(jnp.int32, (planes * edge, edge, 128), 1)
+    halved = grid.reshape(count + 2, edge // 2 + 1, 2, edge, 128)
     for z in range(0, count, planes):
         left = jnp.concatenate(
             [
@@ -149,19 +195,42 @@
             ],
             axis=1,
         )
-        wide = jnp.dot(left, taps[...], preferred_element_type=jnp.float32)
-        new = join_x(wide.reshape(planes * edge, edge, 384), edge)
+        wide = jnp.dot(left, taps[:, 0:256], preferred_element_type=jnp.float32)
+        wide = wide.reshape(planes * edge, edge, 256)
+        left = jnp.concatenate(
+            [
+                halved[z + dz : z + dz + planes, line // 2 : line // 2 + edge // 2, line % 2].reshape(
+                    rows // 2, 128
+                )
+                for dz in range(3)
+                for line in range(4)
+            ],
+            axis=1,
+        )
+        two = jnp.dot(left, pairs[...], preferred_element_type=jnp.float32)
+        two = two.reshape(planes * edge // 2, edge, 256)
+        two = jnp.stack([two[:, :, :128], two[:, :, 128:]], axis=1).reshape(planes * edge, edge, 128)
+        after = jnp.where(place > 0, pltpu.roll(wide[:, :, :128], 1, 1), 0.0)
+        before = jnp.where(place < edge - 1, pltpu.roll(two, edge - 1, 1), 0.0)
+        new = wide[:, :, 128:256] + after + before
         act[z : z + planes] = new.reshape(planes, edge, edge, 128)
 
 
-def front_half_kernel(_, x, weight, act, taps, grid):
+def front_half_kernel(pos, x, weight, deep_weight, after, act, taps, pairs, piece, grid):
+    del after
     spread_taps(weight, taps)
-    local_planes(x, 0, act.shape[0], taps, grid, act)
-
-
-def back_half_kernel(_, x, taps, after, act, grid):
+    pair_taps(weight, pairs)
+    size = piece.shape[1]
+    if size < deep_weight.shape[1]:
+        piece[...] = deep_weight[:, pl.ds(pl.multiple_of(pos[pos.shape[0] - 1] * size, size), size)]
+    else:
+        piece[...] = deep_weight[...]
+    local_planes(x, 0, act.shape[0], taps, pairs, grid, act)
+
+
+def back_half_kernel(_, x, taps, pairs, after, act, grid):
     del after
-    local_planes(x, x.shape[0] - act.shape[0], act.shape[0], taps, grid, act)
+    local_planes(x, x.shape[0] - act.shape[0], act.shape[0], taps, pairs, grid, act)
 
 
 def rim_kernel(ny, nx, pos, *refs):
@@ -252,16 +321,13 @@
 
 
 def put_stats(stats, mean, spread):
-    line = lax.broadcasted_iota(jnp.int32, stats.shape[1:], 0)
-    both = jnp.where(line == 0, mean, spread)
-    stats[...] = jnp.broadcast_to(both[None], stats.shape)
+    stats[0:1] = mean
+    stats[1:2] = spread
 
 
 def read_stats(stats, rows):
-    devices, _, channels = stats.shape
+    channels = stats.shape[1]
     width = channels // GROUPS
-    means = stats[:, 0, :]
-    spreads = stats[:, 1, :]
     line = lax.broadcasted_iota(jnp.int32, (channels, channels), 0) // width
     same = line == lax.broadcasted_iota(jnp.int32, (channels, channels), 1) // width
     same = same.astype(jnp.float32)
@@ -270,74 +336,97 @@
         row = jnp.broadcast_to(row, (8, channels))
         return jnp.dot(row, same, precision=HIGHEST, preferred_element_type=jnp.float32)[0:1]
 
-    mean = grouped(jnp.sum(means, axis=0, keepdims=True)) / (devices * width)
+    means = stats[0:1]
+    mean = grouped(means) / width
     off = means - mean
-    total = grouped(jnp.sum(spreads + rows * (off * off), axis=0, keepdims=True))
-    return mean, lax.rsqrt(total / (rows * devices * width) + EPSILON)
+    total = grouped(stats[1:2] + rows * (off * off))
+    return mean, lax.rsqrt(total / (rows * width) + EPSILON)
 
 
 def silu_of_double(h):
     return h + h * jnp.tanh(h)
 
 
-def norm_kernel(ny, nx, pos, act, stats, gain, offset, out, pooled, *refs):
-    y_edges, x_edges, corners, half, fine = refs
+def norm_kernel(ny, nx, rows, pos, act, stats, gain, offset, out, pooled, *refs):
+    y_edges, x_edges, corners, half = refs
     edge = act.shape[0]
     deep = edge // 2
-    f32 = jnp.float32
-    mean, scale = read_stats(stats, float(edge**3))
+    f32, bf16 = jnp.float32, jnp.bfloat16
+    mean, scale = read_stats(stats, rows)
     scale = scale * (0.5 * gain[...])
     shift = 0.5 * offset[...]
-
-    def step(k, _):
-        value = silu_of_double((act[pl.ds(2 * k, 2)] - mean) * scale + shift).astype(jnp.bfloat16)
-        out[pl.ds(2 * k, 2)] = value
+    for k in range(deep):
+        value = silu_of_double((act[2 * k : 2 * k + 2] - mean) * scale + shift).astype(bf16)
+        out[2 * k : 2 * k + 2] = value
         value = value.astype(f32)
-        value = value[0] + value[1]
-        value = value.reshape(deep, 2, edge, 128)
-        half[...] = (value[:, 0] + value[:, 1]).reshape(deep * edge, 128)
-        pair = half[pl.ds(0, deep * deep, stride=2), :] + half[pl.ds(1, deep * deep, stride=2), :]
-        pair = (pair * 0.125).astype(jnp.bfloat16).astype(f32)
-        fine[pl.ds(k, 1)] = pair.reshape(1, deep, deep, 128)
-        return 0
-
-    lax.fori_loop(0, deep, step, 0)
-    pooled[...] = fine[...]
-    lines = fine.reshape(deep**3, 128)
-    low, high = ((pos[0] == 1, pos[1] == 1) if ny == 1 else (None, None))
-    first_x = lines[pl.ds(0, deep * deep, stride=deep), :].reshape(deep, deep, 128)
-    last_x = lines[pl.ds(deep - 1, deep * deep, stride=deep), :].reshape(deep, deep, 128)
+        value = (value[0] + value[1]).reshape(deep, 2, edge, 128)
+        half[k] = (value[:, 0] + value[:, 1]).reshape(deep * edge, 128)
+        lines = half.at[k]
+        pair = lines[pl.ds(0, deep * deep, stride=2), :] + lines[pl.ds(1, deep * deep, stride=2), :]
+        pooled[k] = (pair * 0.125).astype(bf16).astype(f32).reshape(deep, deep, 128)
+    lines = pooled.reshape(deep**3, 128)
+    first_x = lines[pl.ds(0, deep * deep, stride=deep), :]
+    last_x = lines[pl.ds(deep - 1, deep * deep, stride=deep), :]
+    first_y, last_y = (pooled[:, y].reshape(deep * deep, 128) for y in (0, deep - 1))
     ends = []
     for y in (0, deep - 1):
         for x in (0, deep - 1):
             ends.append(lines[pl.ds(y * deep + x, deep, stride=deep * deep), :])
     if ny == 1:
-        y_edges[0] = jnp.where(low, fine[:, 0], fine[:, deep - 1])
-        x_edges[0] = jnp.where(high, first_x, last_x)
+        above, left = pos[0] == 1, pos[1] == 1
+        y_edges[0] = jnp.where(above, first_y, last_y).astype(bf16)
+        x_edges[0] = jnp.where(left, first_x, last_x).astype(bf16)
         corners[0] = jnp.where(
-            low, jnp.where(high, ends[0], ends[1]), jnp.where(high, ends[2], ends[3])
+            above, jnp.where(left, ends[0], ends[1]), jnp.where(left, ends[2], ends[3])
         )
     else:
-        y_edges[0], y_edges[1] = fine[:, 0], fine[:, deep - 1]
-        x_edges[0], x_edges[1] = first_x, last_x
+        y_edges[0], y_edges[1] = first_y.astype(bf16), last_y.astype(bf16)
+        x_edges[0], x_edges[1] = first_x.astype(bf16), last_x.astype(bf16)
         for k in range(4):
             corners[k] = ends[k]
 
 
-def place_kernel(tiles, _, got, after, kernel):
-    del after
-    pieces, _, part, _ = got.shape
-    for i in range(pieces):
-        at = (i % tiles * (pieces // tiles) + i // tiles) * part
+def stack_kernel(*refs):
+    out = refs[-1]
+    for k in range(out.shape[0]):
+        out[k] = refs[k][...]
+
+
+def stack(*arrays):
+    vmem = pl.BlockSpec(memory_space=pltpu.VMEM)
+    return pl.pallas_call(
+        stack_kernel,
+        out_shape=jax.ShapeDtypeStruct((len(arrays),) + arrays[0].shape, arrays[0].dtype),
+        in_specs=[vmem] * len(arrays),
+        out_specs=vmem,
+        compiler_params=pltpu.CompilerParams(vmem_limit_bytes=VMEM_BYTES),
+    )(*arrays)
+
+
+def place_kernel(tiles, pos, own, held, kernel):
+    shard, part = own.shape[1], held.shape[3]
+    tile, mine = pos[pos.shape[0] - 2], pos[pos.shape[0] - 1]
+
+    def place(rows, at):
         for tap in range(27):
             lane = tap % 9 * 128
-            kernel[tap // 9, at : at + part, lane : lane + 128] = got[i, tap]
+            kernel[tap // 9, pl.ds(at, rows.shape[1]), lane : lane + 128] = rows[tap]
+
+    place(own, pl.multiple_of(tile * shard, shard))
+    for piece in range(held.shape[0]):
+        at = jnp.bitwise_xor(mine, piece) * part
+        for k in range(1, tiles):
+            base = lax.rem(tile + tiles - k, tiles) * shard
+            place(held.at[piece, k - 1], pl.multiple_of(base + at, part))
 
 
 def deep_kernel(ny, nx, pos, pooled, y_halos, x_halos, corners, front, back, kernel, *refs):
     act, stats, grid, packed = refs
     deep = pooled.shape[0]
     f32 = jnp.float32
+    front, back = (face[...].astype(f32).reshape(-1, deep, 128) for face in (front, back))
+    y_halos = [y_halos[i].astype(f32).reshape(deep, deep, 128) for i in range(ny)]
+    x_halos = [x_halos[i].astype(f32).reshape(deep, deep, 128) for i in range(nx)]
     grid[...] = jnp.zeros(grid.shape, f32)
     grid[1 : deep + 1, 1 : deep + 1, 8:16] = pooled[...]
     grid[0, 1 : deep + 1, 8:16] = front[0:deep]
@@ -354,7 +443,7 @@
             elif z == deep + 1:
                 line, rim = back[deep + ny + j], back
             else:
-                line, rim = x_halos[j, z - 1], None
+                line, rim = x_halos[j][z - 1], None
             lines = grid.at[z].reshape((deep + 2) * 24, 128)
             left = pos[ny + j] == 1
             for side, here in ((7, left), (16, jnp.logical_not(left))):
@@ -400,26 +489,29 @@
     put_stats(stats, mean, jnp.sum(off * off, axis=0, keepdims=True))
 
 
-def final_kernel(_, act, stats, gain, offset, up, mid, out, wide):
+def final_kernel(rows, _, act, stats, gain, offset, up, mid, out, wide, held, sems):
     edge = mid.shape[0]
     deep = edge // 2
     f32 = jnp.float32
-    mean, scale = read_stats(stats, float(deep**3))
+    mean, scale = read_stats(stats, rows)
     scale = scale * (0.5 * gain[...])
     value = silu_of_double((act[...] - mean) * scale + 0.5 * offset[...]).astype(jnp.bfloat16)
     lifted = jnp.dot(value, up[...], preferred_element_type=f32)
-    rows = deep**3
-    wide[pl.ds(0, rows, stride=2), :] = lifted
-    wide[pl.ds(1, rows, stride=2), :] = lifted
-
-    def step(k, _):
-        size = deep * edge
-        add = wide[pl.ds(pl.multiple_of(k * size, size), size), :].reshape(1, deep, 1, edge, 128)
-        old = mid[pl.ds(2 * k, 2)].astype(f32).reshape(2, deep, 2, edge, 128)
-        out[pl.ds(2 * k, 2)] = (old + add).astype(jnp.bfloat16).reshape(2, edge, edge, 128)
-        return 0
-
-    lax.fori_loop(0, deep, step, 0)
+    wide[pl.ds(0, deep**3, stride=2), :] = lifted
+    wide[pl.ds(1, deep**3, stride=2), :] = lifted
+    size = deep * edge
+    copies = []
+    for k in range(deep):
+        add = wide[k * size : k * size + size, :].reshape(1, deep, 1, edge, 128)
+        old = mid[2 * k : 2 * k + 2].astype(f32).reshape(2, deep, 2, edge, 128)
+        held[2 * k : 2 * k + 2] = (old + add).astype(jnp.bfloat16).reshape(2, edge, edge, 128)
+        copy = pltpu.make_async_copy(
+            held.at[2 * k : 2 * k + 2], out.at[2 * k : 2 * k + 2], sems.at[k]
+        )
+        copy.start()
+        copies.append(copy)
+    for copy in copies:
+        copy.wait()
 
 
 def body(
@@ -434,29 +526,50 @@
     devices = lax.axis_size("gz") * tiles
     y_low, x_low = square.low_sides()
     ny, nx = len(y_low), len(x_low)
-    pos = jnp.stack(
-        [jnp.asarray(v, jnp.int32) for v in y_low + x_low]
-    )
-
-    y, x, corner = square.halos(*square.edges(features))
-    own = jnp.moveaxis(deep_weight, 4, 3).reshape(27, deep_weight.shape[4], deep_weight.shape[3])
-    got = gather_shards(own)
-    front, back = swap_depth(
-        depth_face(features, y, x, corner, 0), depth_face(features, y, x, corner, -1)
-    )
+    axes = split_axes(deep_weight.shape[4])
+    mine = sum(lax.axis_index(axis) % 2 * 2**k for k, axis in enumerate(axes))
+    pos = y_low + x_low + [lax.axis_index("yx"), mine]
+    pos = jnp.stack([jnp.asarray(v, jnp.int32) for v in pos])
+
+    edges = call(
+        functools.partial(edge_kernel, ny, nx),
+        [
+            ((ny, edge, edge, channels), bf16),
+            ((nx, edge, edge, channels), bf16),
+            ((ny * nx, edge, channels), bf16),
+        ],
+        [((edge * edge, 8, channels), f32)],
+        pos,
+        features,
+        nbytes=1 << 20,
+    )
+    halos = square.halos(*(list(piece) for piece in edges))
+    own = jnp.moveaxis(deep_weight, 4, 3).reshape(27, deep_weight.shape[4], channels)
     half_act = ((deep, edge, edge, channels), f32)
     half_grid = ((deep + 2, edge + 2, edge, channels), bf16)
     conv_flops = 27 * channels * channels * edge**3
-    near, taps = call(
+    near, taps, pairs, piece = call(
         front_half_kernel,
-        [half_act, ((9 * channels, 3 * channels), bf16)],
+        [
+            half_act,
+            ((9 * channels, 3 * channels), bf16),
+            ((12 * channels, 2 * channels), bf16),
+            ((27, own.shape[1] // 2 ** len(axes), channels), bf16),
+        ],
         [half_grid],
         pos,
         features,
         conv_weight.reshape(27, channels, channels),
+        own,
+        edges[2],
         flops=conv_flops,
-        nbytes=2 << 20,
-    )
+        nbytes=3 << 20,
+    )
+    piece, (y, x, corner) = lax.optimization_barrier((piece, halos))
+    front, back = swap_depth(
+        depth_face(features, y, x, corner, 0), depth_face(features, y, x, corner, -1)
+    )
+    got = rotate_shards(piece)
     (far,) = call(
         back_half_kernel,
         [half_act],
@@ -464,13 +577,14 @@
         pos,
         features,
         taps,
+        pairs,
         corner[0],
         flops=conv_flops,
-        nbytes=2 << 20,
+        nbytes=3 << 20,
     )
     act, stats = call(
         functools.partial(rim_kernel, ny, nx),
-        [((edge, edge, edge, channels), f32), ((devices, 8, channels), f32)],
+        [((edge, edge, edge, channels), f32), ((2, channels), f32)],
         [((edge + 2, edge + 16, channels), f32), ((edge + 2, edge, 3 * channels), bf16)],
         pos,
         near,
@@ -481,20 +595,21 @@
         front,
         back,
         taps,
-        flops=conv_flops // 8,
-        nbytes=5 << 20,
-    )
-    stats = share(stats)
+    )
+    stats, *got = lax.optimization_barrier((stats, *got))
+    stats, rows = merge(stats, float(edge**3), ("gz",))
+    stats, _ = merge(stats, rows, ("yx",))
+    held = share_pieces(got, axes)
     out, pooled, *edges = call(
-        functools.partial(norm_kernel, ny, nx),
+        functools.partial(norm_kernel, ny, nx, float(edge**3 * devices)),
         [
             ((edge, edge, edge, channels), bf16),
             ((deep, deep, deep, channels), f32),
-            ((ny, deep, deep, channels), f32),
-            ((nx, deep, deep, channels), f32),
+            ((ny, deep * deep, channels), bf16),
+            ((nx, deep * deep, channels), bf16),
             ((ny * nx, deep, channels), f32),
         ],
-        [((deep * edge, channels), f32), ((deep, deep, deep, channels), f32)],
+        [((deep, deep * edge, channels), f32)],
         pos,
         act,
         stats,
@@ -503,22 +618,29 @@
         flops=20 * channels * edge**3,
         nbytes=3 << 20,
     )
-    y, x, corner = square.halos(*([piece[i] for i in range(piece.shape[0])] for piece in edges))
-    front, back = swap_depth(
-        depth_face(pooled, y, x, corner, 0), depth_face(pooled, y, x, corner, -1)
-    )
+    y, x, corner = square.halos(*(list(piece) for piece in edges))
+
+    def face(at):
+        plane = pooled[at].astype(bf16).reshape(deep * deep, channels)
+        rims = [piece.reshape(deep, deep, channels)[at] for piece in y + x]
+        ends = [piece[at][None].astype(bf16) for piece in corner]
+        rows = deep * deep + deep * (ny + nx) + len(ends)
+        pad = jnp.zeros((-rows % 16, channels), bf16)
+        return jnp.concatenate([plane] + rims + ends + [pad])
+
+    front, back = swap_depth(face(0), face(-1))
     (kernel,) = call(
         functools.partial(place_kernel, tiles),
         [((3, deep_channels, 9 * channels), bf16)],
         [],
         pos,
-        got,
-        corner[0],
+        own,
+        held,
         nbytes=4 << 20,
     )
     deep_act, stats = call(
         functools.partial(deep_kernel, ny, nx),
-        [((deep**3, deep_channels), f32), ((tiles, 8, deep_channels), f32)],
+        [((deep**3, deep_channels), f32), ((2, deep_channels), f32)],
         [
             ((deep + 2, deep + 2, 24, channels), f32),
             ((deep + 2, deep // 2 + 1, 2, 16, 3 * channels), bf16),
@@ -534,11 +656,15 @@
         flops=2 * 27 * channels * deep_channels * deep**3,
         nbytes=4 << 20,
     )
-    stats = share_by_axis(stats)
+    stats, _ = merge(stats, float(deep**3), PART)
     (decoded,) = call(
-        final_kernel,
+        functools.partial(final_kernel, float(deep**3 * devices)),
         [((edge, edge, edge, channels), bf16)],
-        [((2 * deep**3, channels), f32)],
+        [
+            ((2 * deep**3, channels), f32),
+            ((edge, edge, edge, channels), bf16),
+            pltpu.SemaphoreType.DMA((deep,)),
+        ],
         pos,
         deep_act,
         stats,
@@ -548,6 +674,7 @@
         out,
         flops=4 * deep_channels * channels * deep**3,
         nbytes=3 << 20,
+        copied_out=True,
     )
     return decoded
 

time: 86.2 us -> 74.1 us (0.86)
  blocking collectives: 30.2 us -> 0 us
  starting transfers between devices: 17.1 us -> 37.5 us
  between operations: 13.7 us -> 0.38 us
  waiting for transfers between devices: 3.96 us -> 16 us
  local copies, waits for them, and re-layouts: 4.72 us -> 3.81 us
    all_to_all x3 -> x0, blocking collectives: 30.2 us -> none  [the longest x1 14.3 us: share(): return lax.all_to_all(statistics, PART, 0, 0)]
    ppermute x0 -> x13, starting transfers between devices: none -> 18.7 us  [the longest x10 13.9 us: swap(): lax.ppermute(block, axis, [(i, i ^ mask) for i in range(lax.axis_size(axi...]
    ppermute x0 -> x13, waiting for transfers between devices: none -> 14 us  [the longest x10 14 us: swap(): lax.ppermute(block, axis, [(i, i ^ mask) for i in range(lax.axis_size(axi...]
    slice x2 -> x3, local copies, waits for them, and re-layouts: 2.45 us -> 0.01 us  [the longest x1 0.01 us: face(): ends = [piece[at][None].astype(bf16) for piece in corner]]
    unnamed x22 -> x20, local copies, waits for them, and re-layouts: 1.53 us -> 3.44 us
    ppermute x2, starting transfers between devices: 4.33 us -> 6.07 us  [swap_depth(): lax.ppermute(high, 'gz', up)]
    ppermute x2, starting transfers between devices: 5.17 us -> 6.68 us  [halos(): y = lax.ppermute(y_edges[0], 'yx', self.swap_route(2))]
    ppermute x2, waiting for transfers between devices: 1.05 us -> 0.01 us  [halos(): x = lax.ppermute(x_edges[0], 'yx', self.swap_route(1))]
  transfers between devices with their start and end apart: 11 -> 23, of which waited for: 5 -> 11; matrix products, arithmetic and copies ran while one was open for 3% -> 1% of each run, Pallas kernels for 13% -> 14%
where the time goes in v4:
time: 74.1 us; the launch traced here: 73.8 us
  starting transfers between devices  37.5 us (51%)
  waiting for transfers between devices  16 us (22%)
  Pallas kernels  15.8 us (21%)
  local copies, waits for them, and re-layouts  3.81 us (5%)
    pallas_call x8, Pallas kernels, call(): pl.pallas_call(kernel, out_shape=[jax.ShapeDtypeStruct(shape, dtype) for...  15.7 us
    ppermute x10, waiting for transfers between devices, swap(): lax.ppermute(block, axis, [(i, i ^ mask) for i in range(lax.axis_size(axi...  14 us
    ppermute x10, starting transfers between devices, swap(): lax.ppermute(block, axis, [(i, i ^ mask) for i in range(lax.axis_size(axi...  13.9 us
    ppermute x2, starting transfers between devices, halos(): y = lax.ppermute(y_edges[0], 'yx', self.swap_route(2))  6.68 us
    ppermute x2, starting transfers between devices, swap_depth(): lax.ppermute(high, 'gz', up)  6.07 us
    ppermute x3, starting transfers between devices, rotate_shards(): lax.ppermute(piece, 'yx', [(i, (i + k) % tiles) for i in range(tiles)])  4.82 us
    unnamed x20, local copies, waits for them, and re-layouts  3.44 us
    ppermute x2, starting transfers between devices, swap_depth(): lax.ppermute(low, 'gz', [(j, i) for i, j in up])  2.58 us
  transfers between devices with their start and end apart: 23, of which 11 were waited for; matrix products, arithmetic and copies ran while one was open for 1% of the time, Pallas kernels for 14%

profile of v4, /device:TPU:0, one launch (start us, length us, event | category | flops | bytes accessed | tf_op | source)
XLA Modules:
  0.0 73.8 jit_solution(822075691333312349)
XLA Ops:
  0.0 0.1 pad_add_fusion.pos._
  0.1 1.2 %copy-done = bf16[16,16,16,128]{3,2,1,0:T(8,128)(2,1)S(1)} copy-done((bf16[16,16,16,128]{3,2,1,0:T(8,128)(2,1)S(1)}, bf16[16,16,16,128]{3,2,1,0:T(8,128)(2,1)}, u32[]{:S(2)}) %copy-start) | copy-done | bytes 1048600
  1.3 0.8 %shard_map.82 = (bf16[1,16,16,128]{3,2,1,0:T(8,128)(2,1)S(1)}, bf16[1,16,16,128]{3,2,1,0:T(8,128)(2,1)S(1)}, bf16[1,16,128]{2,1,0:T(8,128)(2,1)S(1)}) custom-call(s32[4]{0:T(128)S(1)} %pad_add_fusion.pos._, bf16[16,16,16,128]{3,2,1,0:T(8,128)(2,1)S(1)} %copy-done), custom_call_target="tpu_custom_call" | custom-call | bytes 1048576 | tf_op jit(solution)/shard_map/pallas_call | solution.py:111
  2.1 4.1 %collective-permute-start = (bf16[16,16,128]{2,1,0:T(8,128)(2,1)S(1)}, bf16[16,16,128]{2,1,0:T(8,128)(2,1)S(1)}, u32[]{:S(2)}, u32[]{:S(2)}) collective-permute-start(bf16[16,16,128]{2,1,0:T(8,128)(2,1)S(1)} %bitcast.58), channel_id=1, source_target_pairs={{0,2},{1,3},{2,0},{3,1},{4,6},{5,7},{6,4},{7,5},{8,10},{9,11},{10,... | collective-permute-start | bytes 196616 | tf_op jit(solution)/shard_map/ppermute | solution.py:45
  6.2 1.6 %collective-permute-start.1 = (bf16[16,16,128]{2,1,0:T(8,128)(2,1)S(1)}, bf16[16,16,128]{2,1,0:T(8,128)(2,1)S(1)}, u32[]{:S(2)}, u32[]{:S(2)}) collective-permute-start(bf16[16,16,128]{2,1,0:T(8,128)(2,1)S(1)} %bitcast.57), channel_id=1, source_target_pairs={{0,1},{1,0},{2,3},{3,2},{4,5},{5,4},{6,7},{7,6},{8,9},{9,8},{10,11... | collective-permute-start | bytes 196616 | tf_op jit(solution)/shard_map/ppermute | solution.py:46
  7.8 0.0 copy-start.1
  7.9 1.0 %copy-done.1 = bf16[3,3,3,128,64]{3,4,2,1,0:T(8,128)(2,1)S(1)} copy-done((bf16[3,3,3,128,64]{3,4,2,1,0:T(8,128)(2,1)S(1)}, bf16[3,3,3,128,64]{3,4,2,1,0:T(8,128)(2,1)}, u32[]{:S(2)}) %copy-start.1) | copy-done | bytes 442392
  8.9 1.2 %copy-done.8 = bf16[3,3,3,128,128]{4,3,2,1,0:T(8,128)(2,1)S(1)} copy-done((bf16[3,3,3,128,128]{4,3,2,1,0:T(8,128)(2,1)S(1)}, bf16[3,3,3,128,128]{4,3,2,1,0:T(8,128)(2,1)}, u32[]{:S(2)}) %copy-start.8) | copy-done | bytes 884760
  10.0 3.1 %shard_map.83 = (f32[8,16,16,128]{3,2,1,0:T(8,128)S(1)}, bf16[1152,384]{1,0:T(8,128)(2,1)S(1)}, bf16[1536,256]{1,0:T(8,128)(2,1)S(1)}, bf16[27,16,128]{2,1,0:T(8,128)(2,1)S(1)}) custom-call(s32[4]{0:T(128)S(1)} %pad_add_fusion.pos._, bf16[16,16,16,128]{3,2,1,0:T(8,128)(2,1)S(1)} %copy-done, bf16[27,128,128]{2,1,0:T(8,128)(2,1)S(1)} %bitcast.56, ...), custom_call_target="tpu_custom_call" | custom-call | flops 1811939328 | bytes 3145728 | tf_op jit(solution)/shard_map/pallas_call | solution.py:111
  13.1 0.1 collective-permute-done.2.after
  13.2 0.0 collective-permute-done
  13.2 0.0 collective-permute-done.1
  13.2 0.9 %collective-permute-start.5 = (bf16[27,16,128]{2,1,0:T(8,128)(2,1)S(1)}, bf16[27,16,128]{2,1,0:T(8,128)(2,1)S(1)}, u32[]{:S(2)}, u32[]{:S(2)}) collective-permute-start(bf16[27,16,128]{2,1,0:T(8,128)(2,1)S(1)} %get-tuple-element.41), channel_id=1, source_target_pairs={{0,1},{1,2},{2,3},{3,0},{4,5},{5,6},{6,7},{7,4},{8,9},{9,10},{10,1... | collective-permute-start | bytes 331784 | tf_op jit(solution)/shard_map/ppermute | solution.py:88
  14.1 3.5 %collective-permute-start.6 = (bf16[27,16,128]{2,1,0:T(8,128)(2,1)S(1)}, bf16[27,16,128]{2,1,0:T(8,128)(2,1)S(1)}, u32[]{:S(2)}, u32[]{:S(2)}) collective-permute-start(bf16[27,16,128]{2,1,0:T(8,128)(2,1)S(1)} %get-tuple-element.41), channel_id=1, source_target_pairs={{0,2},{1,3},{2,0},{3,1},{4,6},{5,7},{6,4},{7,5},{8,10},{9,11},{10,... | collective-permute-start | bytes 331784 | tf_op jit(solution)/shard_map/ppermute | solution.py:88
  17.6 0.4 collective-permute-start.7
  18.1 0.1 select_bitcast_fusion
  18.2 1.3 %collective-permute-start.4 = (bf16[19,16,128]{2,1,0:T(8,128)(2,1)S(1)}, bf16[19,16,128]{2,1,0:T(8,128)(2,1)S(1)}, u32[]{:S(2)}, u32[]{:S(2)}) collective-permute-start(bf16[19,16,128]{2,1,0:T(8,128)(2,1)S(1)} %pad_maximum_fusion.1), channel_id=1, source_target_pairs={{4,0},{8,4},{12,8},{5,1},{9,5},{13,9},{6,2},{10,6},{14,10},{7,3},{... | collective-permute-start | bytes 233480 | tf_op jit(solution)/shard_map/ppermute | solution.py:62
  19.5 3.0 %collective-permute-start.3 = (bf16[19,16,128]{2,1,0:T(8,128)(2,1)S(1)}, bf16[19,16,128]{2,1,0:T(8,128)(2,1)S(1)}, u32[]{:S(2)}, u32[]{:S(2)}) collective-permute-start(bf16[19,16,128]{2,1,0:T(8,128)(2,1)S(1)} %pad_maximum_fusion), channel_id=1, source_target_pairs={{0,4},{4,8},{8,12},{1,5},{5,9},{9,13},{2,6},{6,10},{10,14},{3,7},{... | collective-permute-start | bytes 233480 | tf_op jit(solution)/shard_map/ppermute | solution.py:62
  22.5 2.9 %shard_map.84.refs_1_ = f32[8,16,16,128]{3,2,1,0:T(8,128)S(1)} custom-call(s32[4]{0:T(128)S(1)} %pad_add_fusion.pos._, bf16[16,16,16,128]{3,2,1,0:T(8,128)(2,1)S(1)} %copy-done, bf16[1152,384]{1,0:T(8,128)(2,1)S(1)} %get-tuple-element.31.taps.refs_7_, bf16[1536,256]{1,0:T(8,128)(2,1)S(1)} %get-tuple-element.32.pairs, ...), custom_call_target="tpu_custom_call" | custom-call | flops 1811939328 | bytes 3145728 | tf_op jit(solution)/shard_map/pallas_call | solution.py:111
  25.5 0.0 collective-permute-done.3.refs_5_
  25.5 0.0 copy-start.6
  25.5 0.0 copy-start.7
  25.5 1.9 %shard_map.85 = (f32[16,16,16,128]{3,2,1,0:T(8,128)S(1)}, f32[2,128]{1,0:T(2,128)S(1)}) custom-call(s32[4]{0:T(128)S(1)} %pad_add_fusion.pos._, f32[8,16,16,128]{3,2,1,0:T(8,128)S(1)} %get-tuple-element.30.refs_0_, f32[8,16,16,128]{3,2,1,0:T(8,128)S(1)} %shard_map.84.refs_1_, bf16[1,16,16,128]{3,2,1,0:T(8,128)(2,1)S(1)} %bitcast.46, ...), custom_call_target="tpu_custom_call" | custom-call | tf_op jit(solution)/shard_map/pallas_call | solution.py:111
  27.5 0.0 collective-permute-done.6.refs_1_
  27.5 0.0 collective-permute-done.7.refs_2_
  27.5 1.2 %collective-permute-start.8 = (f32[2,128]{1,0:T(2,128)S(1)}, f32[2,128]{1,0:T(2,128)S(1)}, u32[]{:S(2)}, u32[]{:S(2)}) collective-permute-start(f32[2,128]{1,0:T(2,128)S(1)} %get-tuple-element.42), channel_id=1, source_target_pairs={{0,4},{4,0},{8,12},{12,8},{1,5},{5,1},{9,13},{13,9},{2,6},{6,2},{1... | collective-permute-start | bytes 3080 | tf_op jit(solution)/shard_map/ppermute | solution.py:93
  28.6 0.8 %collective-permute-done.8 = f32[2,128]{1,0:T(2,128)S(1)} collective-permute-done((f32[2,128]{1,0:T(2,128)S(1)}, f32[2,128]{1,0:T(2,128)S(1)}, u32[]{:S(2)}, u32[]{:S(2)}) %collective-permute-start.8) | collective-permute-done | bytes 1056 | tf_op jit(solution)/shard_map/ppermute | solution.py:93
  29.5 1.1 %collective-permute-start.9 = (f32[2,128]{1,0:T(2,128)S(1)}, f32[2,128]{1,0:T(2,128)S(1)}, u32[]{:S(2)}, u32[]{:S(2)}) collective-permute-start(f32[2,128]{1,0:T(2,128)S(1)} %pad_maximum_fusion.6), channel_id=1, source_target_pairs={{0,8},{4,12},{8,0},{12,4},{1,9},{5,13},{9,1},{13,5},{2,10},{6,14},... | collective-permute-start | bytes 3080 | tf_op jit(solution)/shard_map/ppermute | solution.py:93
  30.6 2.5 %collective-permute-done.9 = f32[2,128]{1,0:T(2,128)S(1)} collective-permute-done((f32[2,128]{1,0:T(2,128)S(1)}, f32[2,128]{1,0:T(2,128)S(1)}, u32[]{:S(2)}, u32[]{:S(2)}) %collective-permute-start.9) | collective-permute-done | bytes 1056 | tf_op jit(solution)/shard_map/ppermute | solution.py:93
  33.1 1.6 %collective-permute-start.10 = (f32[2,128]{1,0:T(2,128)S(1)}, f32[2,128]{1,0:T(2,128)S(1)}, u32[]{:S(2)}, u32[]{:S(2)}) collective-permute-start(f32[2,128]{1,0:T(2,128)S(1)} %pad_maximum_fusion.7), channel_id=1, source_target_pairs={{0,1},{1,0},{2,3},{3,2},{4,5},{5,4},{6,7},{7,6},{8,9},{9,8},{10,11... | collective-permute-start | bytes 3080 | tf_op jit(solution)/shard_map/ppermute | solution.py:93
  34.8 2.0 %collective-permute-done.10 = f32[2,128]{1,0:T(2,128)S(1)} collective-permute-done((f32[2,128]{1,0:T(2,128)S(1)}, f32[2,128]{1,0:T(2,128)S(1)}, u32[]{:S(2)}, u32[]{:S(2)}) %collective-permute-start.10) | collective-permute-done | bytes 1056 | tf_op jit(solution)/shard_map/ppermute | solution.py:93
  36.8 1.3 %collective-permute-start.11 = (f32[2,128]{1,0:T(2,128)S(1)}, f32[2,128]{1,0:T(2,128)S(1)}, u32[]{:S(2)}, u32[]{:S(2)}) collective-permute-start(f32[2,128]{1,0:T(2,128)S(1)} %pad_maximum_fusion.8), channel_id=1, source_target_pairs={{0,2},{1,3},{2,0},{3,1},{4,6},{5,7},{6,4},{7,5},{8,10},{9,11},{10,... | collective-permute-start | bytes 3080 | tf_op jit(solution)/shard_map/ppermute | solution.py:93
  38.1 1.6 %collective-permute-start.17 = (bf16[1,3,27,16,128]{4,3,2,1,0:T(8,128)(2,1)S(1)}, bf16[1,3,27,16,128]{4,3,2,1,0:T(8,128)(2,1)S(1)}, u32[]{:S(2)}, u32[]{:S(2)}) collective-permute-start(bf16[1,3,27,16,128]{4,3,2,1,0:T(8,128)(2,1)S(1)} %bitcast.42), channel_id=1, source_target_pairs={{0,16},{16,0},{1,17},{17,1},{2,18},{18,2},{3,19},{19,3},{4,20},{20... | collective-permute-start | bytes 995336 | tf_op jit(solution)/shard_map/ppermute | solution.py:93
  39.7 1.6 %collective-permute-done.11 = f32[2,128]{1,0:T(2,128)S(1)} collective-permute-done((f32[2,128]{1,0:T(2,128)S(1)}, f32[2,128]{1,0:T(2,128)S(1)}, u32[]{:S(2)}, u32[]{:S(2)}) %collective-permute-start.11) | collective-permute-done | bytes 1056 | tf_op jit(solution)/shard_map/ppermute | solution.py:93
  41.4 1.7 %shard_map.86 = (bf16[16,16,16,128]{3,2,1,0:T(8,128)(2,1)S(1)}, f32[8,8,8,128]{3,2,1,0:T(8,128)S(1)}, bf16[1,64,128]{2,1,0:T(8,128)(2,1)S(1)}, bf16[1,64,128]{2,1,0:T(8,128)(2,1)S(1)}, f32[1,8,128]{2,1,0:T(8,128)S(1)}) custom-call(s32[4]{0:T(128)S(1)} %pad_add_fusion.pos._, f32[16,16,16,128]{3,2,1,0:T(8,128)S(1)} %get-tuple-element.39.act, ...), custom_call_target="tpu_custom_call" | custom-call | flops 10485760 | bytes 3145728 | tf_op jit(solution)/shard_map/pallas_call | solution.py:111
  43.1 1.2 %collective-permute-start.14 = (f32[8,128]{1,0:T(8,128)S(1)}, f32[8,128]{1,0:T(8,128)S(1)}, u32[]{:S(2)}, u32[]{:S(2)}) collective-permute-start(f32[8,128]{1,0:T(8,128)S(1)} %bitcast.61), channel_id=1, source_target_pairs={{0,3},{1,2},{2,1},{3,0},{4,7},{5,6},{6,5},{7,4},{8,11},{9,10},{10,... | collective-permute-start | bytes 12296 | tf_op jit(solution)/shard_map/ppermute | solution.py:47
  44.2 0.7 collective-permute-start.13
  44.9 2.6 %collective-permute-start.12 = (bf16[64,128]{1,0:T(8,128)(2,1)S(1)}, bf16[64,128]{1,0:T(8,128)(2,1)S(1)}, u32[]{:S(2)}, u32[]{:S(2)}) collective-permute-start(bf16[64,128]{1,0:T(8,128)(2,1)S(1)} %bitcast.59), channel_id=1, source_target_pairs={{0,2},{1,3},{2,0},{3,1},{4,6},{5,7},{6,4},{7,5},{8,10},{9,11},{10,... | collective-permute-start | bytes 49160 | tf_op jit(solution)/shard_map/ppermute | solution.py:45
  47.5 1.0 %collective-permute-done.14 = f32[8,128]{1,0:T(8,128)S(1)} collective-permute-done((f32[8,128]{1,0:T(8,128)S(1)}, f32[8,128]{1,0:T(8,128)S(1)}, u32[]{:S(2)}, u32[]{:S(2)}) %collective-permute-start.14) | collective-permute-done | bytes 4128 | tf_op jit(solution)/shard_map/ppermute | solution.py:47
  48.5 0.0 collective-permute-done.17.refs_1_
  48.6 0.1 collective-permute-start.18
  48.7 0.9 %collective-permute-done.12 = bf16[64,128]{1,0:T(8,128)(2,1)S(1)} collective-permute-done((bf16[64,128]{1,0:T(8,128)(2,1)S(1)}, bf16[64,128]{1,0:T(8,128)(2,1)S(1)}, u32[]{:S(2)}, u32[]{:S(2)}) %collective-permute-start.12) | collective-permute-done | bytes 16416 | tf_op jit(solution)/shard_map/ppermute | solution.py:45
  49.6 0.2 concatenate.23
  49.7 1.3 %collective-permute-start.16 = (bf16[96,128]{1,0:T(8,128)(2,1)S(1)}, bf16[96,128]{1,0:T(8,128)(2,1)S(1)}, u32[]{:S(2)}, u32[]{:S(2)}) collective-permute-start(bf16[96,128]{1,0:T(8,128)(2,1)S(1)} %concatenate.23), channel_id=1, source_target_pairs={{4,0},{8,4},{12,8},{5,1},{9,5},{13,9},{6,2},{10,6},{14,10},{7,3},{... | collective-permute-start | bytes 73736 | tf_op jit(solution)/shard_map/ppermute | solution.py:62
  51.0 0.2 concatenate.22
  51.2 3.0 %collective-permute-start.15 = (bf16[96,128]{1,0:T(8,128)(2,1)S(1)}, bf16[96,128]{1,0:T(8,128)(2,1)S(1)}, u32[]{:S(2)}, u32[]{:S(2)}) collective-permute-start(bf16[96,128]{1,0:T(8,128)(2,1)S(1)} %concatenate.22), channel_id=1, source_target_pairs={{0,4},{4,8},{8,12},{1,5},{5,9},{9,13},{2,6},{6,10},{10,14},{3,7},{... | collective-permute-start | bytes 73736 | tf_op jit(solution)/shard_map/ppermute | solution.py:62
  54.3 0.0 collective-permute-done.18.refs_1_
  54.3 0.1 shard_map.89
  54.4 0.8 %shard_map.90.kernel = bf16[3,256,1152]{2,1,0:T(8,128)(2,1)S(1)} custom-call(s32[4]{0:T(128)S(1)} %pad_add_fusion.pos._, bf16[27,64,128]{2,1,0:T(8,128)(2,1)S(1)} %bitcast.45, bf16[4,3,27,16,128]{4,3,2,1,0:T(8,128)(2,1)S(1)} %bitcast.39), custom_call_target="tpu_custom_call" | custom-call | bytes 4194304 | tf_op jit(solution)/shard_map/pallas_call | solution.py:111
  55.2 0.0 copy-start.3
  55.2 0.0 copy-start.4
  55.2 0.0 copy-start.5
  55.3 0.0 collective-permute-done.16.back
  55.3 0.0 collective-permute-done.15.front
  55.3 2.0 %shard_map.91 = (f32[512,256]{1,0:T(8,128)S(1)}, f32[2,256]{1,0:T(2,128)S(1)}) custom-call(s32[4]{0:T(128)S(1)} %pad_add_fusion.pos._, f32[8,8,8,128]{3,2,1,0:T(8,128)S(1)} %get-tuple-element.43.pooled, bf16[1,64,128]{2,1,0:T(8,128)(2,1)S(1)} %bitcast.53, bf16[1,64,128]{2,1,0:T(8,128)(2,1)S(1)} %bitcast.52, f32[1,8,128]{2,1,0:T(8,128)S(1)} %bitcast.49, ...), custom_call_target="tpu_custom_call" | custom-call | flops 905969664 | bytes 4194304 | tf_op jit(solution)/shard_map/pallas_call | solution.py:111
  57.3 0.9 %collective-permute-start.19 = (f32[2,256]{1,0:T(2,128)S(1)}, f32[2,256]{1,0:T(2,128)S(1)}, u32[]{:S(2)}, u32[]{:S(2)}) collective-permute-start(f32[2,256]{1,0:T(2,128)S(1)} %get-tuple-element.51), channel_id=1, source_target_pairs={{0,4},{4,0},{8,12},{12,8},{1,5},{5,1},{9,13},{13,9},{2,6},{6,2},{1... | collective-permute-start | bytes 6152 | tf_op jit(solution)/shard_map/ppermute | solution.py:93
  58.2 0.8 %collective-permute-done.19 = f32[2,256]{1,0:T(2,128)S(1)} collective-permute-done((f32[2,256]{1,0:T(2,128)S(1)}, f32[2,256]{1,0:T(2,128)S(1)}, u32[]{:S(2)}, u32[]{:S(2)}) %collective-permute-start.19) | collective-permute-done | bytes 2080 | tf_op jit(solution)/shard_map/ppermute | solution.py:93
  59.0 2.5 %collective-permute-start.20 = (f32[2,256]{1,0:T(2,128)S(1)}, f32[2,256]{1,0:T(2,128)S(1)}, u32[]{:S(2)}, u32[]{:S(2)}) collective-permute-start(f32[2,256]{1,0:T(2,128)S(1)} %pad_maximum_fusion.2), channel_id=1, source_target_pairs={{0,8},{4,12},{8,0},{12,4},{1,9},{5,13},{9,1},{13,5},{2,10},{6,14},... | collective-permute-start | bytes 6152 | tf_op jit(solution)/shard_map/ppermute | solution.py:93
  61.5 1.6 %collective-permute-done.20 = f32[2,256]{1,0:T(2,128)S(1)} collective-permute-done((f32[2,256]{1,0:T(2,128)S(1)}, f32[2,256]{1,0:T(2,128)S(1)}, u32[]{:S(2)}, u32[]{:S(2)}) %collective-permute-start.20) | collective-permute-done | bytes 2080 | tf_op jit(solution)/shard_map/ppermute | solution.py:93
  63.1 1.1 %collective-permute-start.21 = (f32[2,256]{1,0:T(2,128)S(1)}, f32[2,256]{1,0:T(2,128)S(1)}, u32[]{:S(2)}, u32[]{:S(2)}) collective-permute-start(f32[2,256]{1,0:T(2,128)S(1)} %pad_maximum_fusion.3), channel_id=1, source_target_pairs={{0,1},{1,0},{2,3},{3,2},{4,5},{5,4},{6,7},{7,6},{8,9},{9,8},{10,11... | collective-permute-start | bytes 6152 | tf_op jit(solution)/shard_map/ppermute | solution.py:93
  64.3 2.5 %collective-permute-done.21 = f32[2,256]{1,0:T(2,128)S(1)} collective-permute-done((f32[2,256]{1,0:T(2,128)S(1)}, f32[2,256]{1,0:T(2,128)S(1)}, u32[]{:S(2)}, u32[]{:S(2)}) %collective-permute-start.21) | collective-permute-done | bytes 2080 | tf_op jit(solution)/shard_map/ppermute | solution.py:93
  66.8 2.4 %collective-permute-start.22 = (f32[2,256]{1,0:T(2,128)S(1)}, f32[2,256]{1,0:T(2,128)S(1)}, u32[]{:S(2)}, u32[]{:S(2)}) collective-permute-start(f32[2,256]{1,0:T(2,128)S(1)} %pad_maximum_fusion.4), channel_id=1, source_target_pairs={{0,2},{1,3},{2,0},{3,1},{4,6},{5,7},{6,4},{7,5},{8,10},{9,11},{10,... | collective-permute-start | bytes 6152 | tf_op jit(solution)/shard_map/ppermute | solution.py:93
  69.2 2.1 %collective-permute-done.22 = f32[2,256]{1,0:T(2,128)S(1)} collective-permute-done((f32[2,256]{1,0:T(2,128)S(1)}, f32[2,256]{1,0:T(2,128)S(1)}, u32[]{:S(2)}, u32[]{:S(2)}) %collective-permute-start.22) | collective-permute-done | bytes 2080 | tf_op jit(solution)/shard_map/ppermute | solution.py:93
  71.4 2.4 %shard_map.92 = bf16[16,16,16,128]{3,2,1,0:T(8,128)(2,1)} custom-call(s32[4]{0:T(128)S(1)} %pad_add_fusion.pos._, f32[512,256]{1,0:T(8,128)S(1)} %get-tuple-element.50.act, f32[2,256]{1,0:T(2,128)S(1)} %pad_maximum_fusion.5.stats, f32[1,256]{1,0:T(1,128)S(1)} %bitcast.50, f32[1,256]{1,0:T(1,128)S(1)} %bitcast.51, bf16[256,128]{1,0:T(8,128)(2,1)S(1)} %copy-done.3, ...), custom_call_target="tpu_custom_call" | custom-call | flops 67108864 | bytes 3145728 | tf_op jit(solution)/shard_map/pallas_call | solution.py:111
  (46 shorter events, 0.3 us)
Async XLA Ops:
  0.1 1.2 %copy-start = (bf16[16,16,16,128]{3,2,1,0:T(8,128)(2,1)S(1)}, bf16[16,16,16,128]{3,2,1,0:T(8,128)(2,1)}, u32[]{:S(2)}) copy-start(bf16[16,16,16,128]{3,2,1,0:T(8,128)(2,1)} %x.7) | copy-start | bytes 3145732
  2.1 11.1 %collective-permute-start = (bf16[16,16,128]{2,1,0:T(8,128)(2,1)S(1)}, bf16[16,16,128]{2,1,0:T(8,128)(2,1)S(1)}, u32[]{:S(2)}, u32[]{:S(2)}) collective-permute-start(bf16[16,16,128]{2,1,0:T(8,128)(2,1)S(1)} %bitcast.58), channel_id=1, source_target_pairs={{0,2},{1,3},{2,0},{3,1},{4,6},{5,7},{6,4},{7,5},{8,10},{9,11},{10,... | collective-permute-start | bytes 196616 | tf_op jit(solution)/shard_map/ppermute | solution.py:45
  6.2 7.0 %collective-permute-start.1 = (bf16[16,16,128]{2,1,0:T(8,128)(2,1)S(1)}, bf16[16,16,128]{2,1,0:T(8,128)(2,1)S(1)}, u32[]{:S(2)}, u32[]{:S(2)}) collective-permute-start(bf16[16,16,128]{2,1,0:T(8,128)(2,1)S(1)} %bitcast.57), channel_id=1, source_target_pairs={{0,1},{1,0},{2,3},{3,2},{4,5},{5,4},{6,7},{7,6},{8,9},{9,8},{10,11... | collective-permute-start | bytes 196616 | tf_op jit(solution)/shard_map/ppermute | solution.py:46
  7.8 5.4 %collective-permute-start.2 = (bf16[16,128]{1,0:T(8,128)(2,1)S(1)}, bf16[16,128]{1,0:T(8,128)(2,1)S(1)}, u32[]{:S(2)}, u32[]{:S(2)}) collective-permute-start(bf16[16,128]{1,0:T(8,128)(2,1)S(1)} %bitcast.62), channel_id=1, source_target_pairs={{0,3},{1,2},{2,1},{3,0},{4,7},{5,6},{6,5},{7,4},{8,11},{9,10},{10,... | collective-permute-start | bytes 12296 | tf_op jit(solution)/shard_map/ppermute | solution.py:47
  7.8 1.0 %copy-start.1 = (bf16[3,3,3,128,64]{3,4,2,1,0:T(8,128)(2,1)S(1)}, bf16[3,3,3,128,64]{3,4,2,1,0:T(8,128)(2,1)}, u32[]{:S(2)}) copy-start(bf16[3,3,3,128,64]{3,4,2,1,0:T(8,128)(2,1)} %param.12) | copy-start | bytes 1327108
  8.9 1.2 %copy-start.8 = (bf16[3,3,3,128,128]{4,3,2,1,0:T(8,128)(2,1)S(1)}, bf16[3,3,3,128,128]{4,3,2,1,0:T(8,128)(2,1)}, u32[]{:S(2)}) copy-start(bf16[3,3,3,128,128]{4,3,2,1,0:T(8,128)(2,1)} %param.9) | copy-start | bytes 2654212
  10.0 8.0 %copy-start.9 = (pred[16]{0:T(512)(128)(4,1)S(1)}, pred[16]{0:T(512)(128)(4,1)}, u32[]{:S(2)}) copy-start(pred[16]{0:T(512)(128)(4,1)} %constant.58.clone.1) | copy-start | bytes 52
  13.2 14.2 %collective-permute-start.5 = (bf16[27,16,128]{2,1,0:T(8,128)(2,1)S(1)}, bf16[27,16,128]{2,1,0:T(8,128)(2,1)S(1)}, u32[]{:S(2)}, u32[]{:S(2)}) collective-permute-start(bf16[27,16,128]{2,1,0:T(8,128)(2,1)S(1)} %get-tuple-element.41), channel_id=1, source_target_pairs={{0,1},{1,2},{2,3},{3,0},{4,5},{5,6},{6,7},{7,4},{8,9},{9,10},{10,1... | collective-permute-start | bytes 331784 | tf_op jit(solution)/shard_map/ppermute | solution.py:88
  14.1 13.3 %collective-permute-start.6 = (bf16[27,16,128]{2,1,0:T(8,128)(2,1)S(1)}, bf16[27,16,128]{2,1,0:T(8,128)(2,1)S(1)}, u32[]{:S(2)}, u32[]{:S(2)}) collective-permute-start(bf16[27,16,128]{2,1,0:T(8,128)(2,1)S(1)} %get-tuple-element.41), channel_id=1, source_target_pairs={{0,2},{1,3},{2,0},{3,1},{4,6},{5,7},{6,4},{7,5},{8,10},{9,11},{10,... | collective-permute-start | bytes 331784 | tf_op jit(solution)/shard_map/ppermute | solution.py:88
  17.6 9.9 %collective-permute-start.7 = (bf16[27,16,128]{2,1,0:T(8,128)(2,1)S(1)}, bf16[27,16,128]{2,1,0:T(8,128)(2,1)S(1)}, u32[]{:S(2)}, u32[]{:S(2)}) collective-permute-start(bf16[27,16,128]{2,1,0:T(8,128)(2,1)S(1)} %get-tuple-element.41), channel_id=1, source_target_pairs={{0,3},{1,0},{2,1},{3,2},{4,7},{5,4},{6,5},{7,6},{8,11},{9,8},{10,9... | collective-permute-start | bytes 331784 | tf_op jit(solution)/shard_map/ppermute | solution.py:88
  18.2 7.3 %collective-permute-start.4 = (bf16[19,16,128]{2,1,0:T(8,128)(2,1)S(1)}, bf16[19,16,128]{2,1,0:T(8,128)(2,1)S(1)}, u32[]{:S(2)}, u32[]{:S(2)}) collective-permute-start(bf16[19,16,128]{2,1,0:T(8,128)(2,1)S(1)} %pad_maximum_fusion.1), channel_id=1, source_target_pairs={{4,0},{8,4},{12,8},{5,1},{9,5},{13,9},{6,2},{10,6},{14,10},{7,3},{... | collective-permute-start | bytes 233480 | tf_op jit(solution)/shard_map/ppermute | solution.py:62
  19.5 6.0 %collective-permute-start.3 = (bf16[19,16,128]{2,1,0:T(8,128)(2,1)S(1)}, bf16[19,16,128]{2,1,0:T(8,128)(2,1)S(1)}, u32[]{:S(2)}, u32[]{:S(2)}) collective-permute-start(bf16[19,16,128]{2,1,0:T(8,128)(2,1)S(1)} %pad_maximum_fusion), channel_id=1, source_target_pairs={{0,4},{4,8},{8,12},{1,5},{5,9},{9,13},{2,6},{6,10},{10,14},{3,7},{... | collective-permute-start | bytes 233480 | tf_op jit(solution)/shard_map/ppermute | solution.py:62
  25.5 15.8 %copy-start.6 = (f32[128]{0:T(128)S(1)}, f32[128]{0:T(128)}, u32[]{:S(2)}) copy-start(f32[128]{0:T(128)} %param.10) | copy-start | bytes 1540
  25.5 15.8 %copy-start.7 = (f32[128]{0:T(128)S(1)}, f32[128]{0:T(128)}, u32[]{:S(2)}) copy-start(f32[128]{0:T(128)} %param.11) | copy-start | bytes 1540
  27.5 2.0 %collective-permute-start.8 = (f32[2,128]{1,0:T(2,128)S(1)}, f32[2,128]{1,0:T(2,128)S(1)}, u32[]{:S(2)}, u32[]{:S(2)}) collective-permute-start(f32[2,128]{1,0:T(2,128)S(1)} %get-tuple-element.42), channel_id=1, source_target_pairs={{0,4},{4,0},{8,12},{12,8},{1,5},{5,1},{9,13},{13,9},{2,6},{6,2},{1... | collective-permute-start | bytes 3080 | tf_op jit(solution)/shard_map/ppermute | solution.py:93
  29.5 3.6 %collective-permute-start.9 = (f32[2,128]{1,0:T(2,128)S(1)}, f32[2,128]{1,0:T(2,128)S(1)}, u32[]{:S(2)}, u32[]{:S(2)}) collective-permute-start(f32[2,128]{1,0:T(2,128)S(1)} %pad_maximum_fusion.6), channel_id=1, source_target_pairs={{0,8},{4,12},{8,0},{12,4},{1,9},{5,13},{9,1},{13,5},{2,10},{6,14},... | collective-permute-start | bytes 3080 | tf_op jit(solution)/shard_map/ppermute | solution.py:93
  33.1 3.6 %collective-permute-start.10 = (f32[2,128]{1,0:T(2,128)S(1)}, f32[2,128]{1,0:T(2,128)S(1)}, u32[]{:S(2)}, u32[]{:S(2)}) collective-permute-start(f32[2,128]{1,0:T(2,128)S(1)} %pad_maximum_fusion.7), channel_id=1, source_target_pairs={{0,1},{1,0},{2,3},{3,2},{4,5},{5,4},{6,7},{7,6},{8,9},{9,8},{10,11... | collective-permute-start | bytes 3080 | tf_op jit(solution)/shard_map/ppermute | solution.py:93
  36.8 4.5 %collective-permute-start.11 = (f32[2,128]{1,0:T(2,128)S(1)}, f32[2,128]{1,0:T(2,128)S(1)}, u32[]{:S(2)}, u32[]{:S(2)}) collective-permute-start(f32[2,128]{1,0:T(2,128)S(1)} %pad_maximum_fusion.8), channel_id=1, source_target_pairs={{0,2},{1,3},{2,0},{3,1},{4,6},{5,7},{6,4},{7,5},{8,10},{9,11},{10,... | collective-permute-start | bytes 3080 | tf_op jit(solution)/shard_map/ppermute | solution.py:93
  38.1 10.4 %collective-permute-start.17 = (bf16[1,3,27,16,128]{4,3,2,1,0:T(8,128)(2,1)S(1)}, bf16[1,3,27,16,128]{4,3,2,1,0:T(8,128)(2,1)S(1)}, u32[]{:S(2)}, u32[]{:S(2)}) collective-permute-start(bf16[1,3,27,16,128]{4,3,2,1,0:T(8,128)(2,1)S(1)} %bitcast.42), channel_id=1, source_target_pairs={{0,16},{16,0},{1,17},{17,1},{2,18},{18,2},{3,19},{19,3},{4,20},{20... | collective-permute-start | bytes 995336 | tf_op jit(solution)/shard_map/ppermute | solution.py:93
  43.1 5.5 %collective-permute-start.14 = (f32[8,128]{1,0:T(8,128)S(1)}, f32[8,128]{1,0:T(8,128)S(1)}, u32[]{:S(2)}, u32[]{:S(2)}) collective-permute-start(f32[8,128]{1,0:T(8,128)S(1)} %bitcast.61), channel_id=1, source_target_pairs={{0,3},{1,2},{2,1},{3,0},{4,7},{5,6},{6,5},{7,4},{8,11},{9,10},{10,... | collective-permute-start | bytes 12296 | tf_op jit(solution)/shard_map/ppermute | solution.py:47
  44.2 4.5 %collective-permute-start.13 = (bf16[64,128]{1,0:T(8,128)(2,1)S(1)}, bf16[64,128]{1,0:T(8,128)(2,1)S(1)}, u32[]{:S(2)}, u32[]{:S(2)}) collective-permute-start(bf16[64,128]{1,0:T(8,128)(2,1)S(1)} %bitcast.60), channel_id=1, source_target_pairs={{0,1},{1,0},{2,3},{3,2},{4,5},{5,4},{6,7},{7,6},{8,9},{9,8},{10,11... | collective-permute-start | bytes 49160 | tf_op jit(solution)/shard_map/ppermute | solution.py:46
  44.9 4.6 %collective-permute-start.12 = (bf16[64,128]{1,0:T(8,128)(2,1)S(1)}, bf16[64,128]{1,0:T(8,128)(2,1)S(1)}, u32[]{:S(2)}, u32[]{:S(2)}) collective-permute-start(bf16[64,128]{1,0:T(8,128)(2,1)S(1)} %bitcast.59), channel_id=1, source_target_pairs={{0,2},{1,3},{2,0},{3,1},{4,6},{5,7},{6,4},{7,5},{8,10},{9,11},{10,... | collective-permute-start | bytes 49160 | tf_op jit(solution)/shard_map/ppermute | solution.py:45
  48.5 5.8 %copy-start.2 = (bf16[3,3,3,128,64]{3,4,2,1,0:T(8,128)(2,1)S(1)}, bf16[3,3,3,128,64]{3,4,2,1,0:T(8,128)(2,1)}, u32[]{:S(2)}) copy-start(bf16[3,3,3,128,64]{3,4,2,1,0:T(8,128)(2,1)} %param.12) | copy-start | bytes 1327108
  48.6 5.7 %collective-permute-start.18 = (bf16[2,3,27,16,128]{4,3,2,1,0:T(8,128)(2,1)S(1)}, bf16[2,3,27,16,128]{4,3,2,1,0:T(8,128)(2,1)S(1)}, u32[]{:S(2)}, u32[]{:S(2)}) collective-permute-start(bf16[2,3,27,16,128]{4,3,2,1,0:T(8,128)(2,1)S(1)} %bitcast.40), channel_id=1, source_target_pairs={{0,4},{4,0},{8,12},{12,8},{1,5},{5,1},{9,13},{13,9},{2,6},{6,2},{1... | collective-permute-start | bytes 1990664 | tf_op jit(solution)/shard_map/ppermute | solution.py:93
  49.7 5.5 %collective-permute-start.16 = (bf16[96,128]{1,0:T(8,128)(2,1)S(1)}, bf16[96,128]{1,0:T(8,128)(2,1)S(1)}, u32[]{:S(2)}, u32[]{:S(2)}) collective-permute-start(bf16[96,128]{1,0:T(8,128)(2,1)S(1)} %concatenate.23), channel_id=1, source_target_pairs={{4,0},{8,4},{12,8},{5,1},{9,5},{13,9},{6,2},{10,6},{14,10},{7,3},{... | collective-permute-start | bytes 73736 | tf_op jit(solution)/shard_map/ppermute | solution.py:62
  51.2 4.1 %collective-permute-start.15 = (bf16[96,128]{1,0:T(8,128)(2,1)S(1)}, bf16[96,128]{1,0:T(8,128)(2,1)S(1)}, u32[]{:S(2)}, u32[]{:S(2)}) collective-permute-start(bf16[96,128]{1,0:T(8,128)(2,1)S(1)} %concatenate.22), channel_id=1, source_target_pairs={{0,4},{4,8},{8,12},{1,5},{5,9},{9,13},{2,6},{6,10},{10,14},{3,7},{... | collective-permute-start | bytes 73736 | tf_op jit(solution)/shard_map/ppermute | solution.py:62
  55.2 16.1 %copy-start.3 = (bf16[256,128]{1,0:T(8,128)(2,1)S(1)}, bf16[256,128]{1,0:T(8,128)(2,1)}, u32[]{:S(2)}) copy-start(bf16[256,128]{1,0:T(8,128)(2,1)} %up.1) | copy-start | bytes 196612
  55.2 16.1 %copy-start.4 = (f32[256]{0:T(256)S(1)}, f32[256]{0:T(256)}, u32[]{:S(2)}) copy-start(f32[256]{0:T(256)} %param.13) | copy-start | bytes 3076
  55.2 16.1 %copy-start.5 = (f32[256]{0:T(256)S(1)}, f32[256]{0:T(256)}, u32[]{:S(2)}) copy-start(f32[256]{0:T(256)} %param.14) | copy-start | bytes 3076
  57.3 1.8 %collective-permute-start.19 = (f32[2,256]{1,0:T(2,128)S(1)}, f32[2,256]{1,0:T(2,128)S(1)}, u32[]{:S(2)}, u32[]{:S(2)}) collective-permute-start(f32[2,256]{1,0:T(2,128)S(1)} %get-tuple-element.51), channel_id=1, source_target_pairs={{0,4},{4,0},{8,12},{12,8},{1,5},{5,1},{9,13},{13,9},{2,6},{6,2},{1... | collective-permute-start | bytes 6152 | tf_op jit(solution)/shard_map/ppermute | solution.py:93
  59.0 4.0 %collective-permute-start.20 = (f32[2,256]{1,0:T(2,128)S(1)}, f32[2,256]{1,0:T(2,128)S(1)}, u32[]{:S(2)}, u32[]{:S(2)}) collective-permute-start(f32[2,256]{1,0:T(2,128)S(1)} %pad_maximum_fusion.2), channel_id=1, source_target_pairs={{0,8},{4,12},{8,0},{12,4},{1,9},{5,13},{9,1},{13,5},{2,10},{6,14},... | collective-permute-start | bytes 6152 | tf_op jit(solution)/shard_map/ppermute | solution.py:93
  63.1 3.7 %collective-permute-start.21 = (f32[2,256]{1,0:T(2,128)S(1)}, f32[2,256]{1,0:T(2,128)S(1)}, u32[]{:S(2)}, u32[]{:S(2)}) collective-permute-start(f32[2,256]{1,0:T(2,128)S(1)} %pad_maximum_fusion.3), channel_id=1, source_target_pairs={{0,1},{1,0},{2,3},{3,2},{4,5},{5,4},{6,7},{7,6},{8,9},{9,8},{10,11... | collective-permute-start | bytes 6152 | tf_op jit(solution)/shard_map/ppermute | solution.py:93
  66.8 4.5 %collective-permute-start.22 = (f32[2,256]{1,0:T(2,128)S(1)}, f32[2,256]{1,0:T(2,128)S(1)}, u32[]{:S(2)}, u32[]{:S(2)}) collective-permute-start(f32[2,256]{1,0:T(2,128)S(1)} %pad_maximum_fusion.4), channel_id=1, source_target_pairs={{0,2},{1,3},{2,0},{3,1},{4,6},{5,7},{6,4},{7,5},{8,10},{9,11},{10,... | collective-permute-start | bytes 6152 | tf_op jit(solution)/shard_map/ppermute | solution.py:93

commit v5 on v4

v5 whole, which is shorter than its diff:
```python
import functools
import math

import jax
import jax.numpy as jnp
from jax import lax
from jax.experimental import pallas as pl
from jax.experimental.pallas import tpu as pltpu
from jax.sharding import PartitionSpec as P

GROUPS = 32
EPSILON = 1e-05
PART = ("gz", "yx")
VMEM_BYTES = 32 * 1024 * 1024


class Square:
    def __init__(self):
        self.tiles = lax.axis_size("yx")
        self.side = math.isqrt(self.tiles)
        tile = lax.axis_index("yx")
        self.row, self.column = tile // self.side, tile % self.side
        self.folded = self.side == 2
        self.steps = (0,) if self.folded else (-1, 1)

    def low_sides(self):
        if self.folded:
            return [self.row], [self.column]
        return [1, 0], [1, 0]

    def route(self, down, right):
        pairs = []
        for tile in range(self.tiles):
            row, column = tile // self.side + down, tile % self.side + right
            if 0 <= row < self.side and 0 <= column < self.side:
                pairs.append((tile, row * self.side + column))
        return pairs

    def swap_route(self, mask):
        return [(tile, tile ^ mask) for tile in range(self.tiles)]

    def halos(self, y_edges, x_edges, corners):
        if self.folded:
            y = lax.ppermute(y_edges[0], "yx", self.swap_route(2))
            x = lax.ppermute(x_edges[0], "yx", self.swap_route(1))
            corner = lax.ppermute(corners[0], "yx", self.swap_route(3))
            return [y], [x], [corner]
        y = [lax.ppermute(y_edges[k], "yx", self.route((1, -1)[1 - k], 0)) for k in (1, 0)]
        x = [lax.ppermute(x_edges[k], "yx", self.route(0, (1, -1)[1 - k])) for k in (1, 0)]
        corner = [
            lax.ppermute(corners[2 * k + j], "yx", self.route((1, -1)[1 - k], (1, -1)[1 - j]))
            for k in (1, 0)
            for j in (1, 0)
        ]
        return y, x, corner


def swap_depth(low, high):
    size = lax.axis_size("gz")
    up = [(i, i + 1) for i in range(size - 1)]
    return lax.ppermute(high, "gz", up), lax.ppermute(low, "gz", [(j, i) for i, j in up])


def split_axes(rows):
    return ("cand", "gz")[: 2 if rows % 64 == 0 else 0]


def rotate_shards(piece):
    tiles = lax.axis_size("yx")
    return [
        lax.ppermute(piece, "yx", [(i, (i + k) % tiles) for i in range(tiles)]) for k in range(1, tiles)
    ]


def swap(block, axis, mask):
    return lax.ppermute(block, axis, [(i, i ^ mask) for i in range(lax.axis_size(axis))])


def share(stats):
    return lax.all_to_all(stats, PART, 0, 0)


def call(kernel, outs, scratch, scalars, *arrays, flops=0, nbytes=0, in_hbm=False, out_hbm=False):
    smem, vmem, hbm = (
        pl.BlockSpec(memory_space=space) for space in (pltpu.SMEM, pltpu.VMEM, pltpu.HBM)
    )
    return pl.pallas_call(
        kernel,
        out_shape=[jax.ShapeDtypeStruct(shape, dtype) for shape, dtype in outs],
        in_specs=[smem] + [hbm if in_hbm else vmem] * len(arrays),
        out_specs=[hbm if out_hbm else vmem] * len(outs),
        scratch_shapes=[pltpu.VMEM(*entry) if isinstance(entry, tuple) else entry for entry in scratch],
        compiler_params=pltpu.CompilerParams(vmem_limit_bytes=VMEM_BYTES),
        cost_estimate=pl.CostEstimate(flops=flops, bytes_accessed=nbytes, transcendentals=0),
    )(scalars, *arrays)


def start_kernel(ny, nx, pos, x_in, w_in, d_in, y_edges, x_edges, corners, x, w, d, lines, sems):
    edge = x.shape[0]
    size = edge // 4
    first = [
        pltpu.make_async_copy(x_in.at[pl.ds(k * size, size)], x.at[pl.ds(k * size, size)], sems.at[k])
        for k in range(4)
    ]
    later = [pltpu.make_async_copy(w_in, w, sems.at[4]), pltpu.make_async_copy(d_in, d, sems.at[5])]
    for copy in first + later:
        copy.start()
    for copy in first:
        copy.wait()
    f32, bf16 = jnp.float32, jnp.bfloat16
    for i in range(ny):
        at = jnp.where(pos[i] == 1, 0, edge - 1) if ny == 1 else (0, edge - 1)[i]
        y_edges[i] = x[:, at]
    flat = lines.reshape(edge * edge * 8, 128)
    for j in range(nx):
        first = x[:, :, 0:8].astype(f32)
        last = x[:, :, edge - 8 : edge].astype(f32)
        if nx == 1:
            low = pos[ny] == 1
            turned = pltpu.roll(last.reshape(edge * edge, 8, 128), 1, 1)
            kept = jnp.where(low, first.reshape(edge * edge, 8, 128), turned)
        else:
            kept = (first, pltpu.roll(last.reshape(edge * edge, 8, 128), 1, 1))[j]
        lines[...] = kept.reshape(edge * edge, 8, 128)
        column = flat[pl.ds(0, edge * edge, stride=8), :]
        x_edges[j] = column.astype(bf16).reshape(edge, edge, 128)
        for i in range(ny):
            first_y = flat[pl.ds(0, edge, stride=8 * edge), :]
            last_y = flat[pl.ds(8 * (edge - 1), edge, stride=8 * edge), :]
            kept = jnp.where(pos[i] == 1, first_y, last_y) if ny == 1 else (first_y, last_y)[i]
            corners[i * nx + j] = kept.astype(bf16)
    for copy in later:
        copy.wait()


def face_kernel(ny, nx, _, x, y_halos, x_halos, corners, low, high):
    edge = x.shape[0]
    wide = edge + ny + nx
    for face, at in ((low, 0), (high, edge - 3)):
        for k in range(3):
            row = k * wide
            face[row : row + edge] = x[at + k]
            for i in range(ny):
                face[row + edge + i] = y_halos[i, at + k]
            for j in range(nx):
                face[row + edge + ny + j] = x_halos[j, at + k]
        for k in range(ny * nx):
            face[3 * wide + k] = corners[k]


def spread_taps(weight, taps):
    for tap in range(27):
        row, lane = tap // 3 * 128, tap % 3 * 128
        taps[row : row + 128, lane : lane + 128] = weight[tap]


def pair_taps(weight, pairs):
    for dz in range(3):
        for line in range(4):
            row = (dz * 4 + line) * 128
            for out in range(2):
                lane = out * 128
                if 0 <= line - out < 3:
                    block = weight[dz * 9 + (line - out) * 3 + 2]
                else:
                    block = jnp.zeros((128, 128), pairs.dtype)
                pairs[row : row + 128, lane : lane + 128] = block


def join_x(wide, edge):
    place = lax.broadcasted_iota(jnp.int32, wide.shape[:2] + (128,), 1)
    after = jnp.where(place > 0, pltpu.roll(wide[:, :, :128], 1, 1), 0.0)
    before = jnp.where(place < edge - 1, pltpu.roll(wide[:, :, 256:], edge - 1, 1), 0.0)
    return wide[:, :, 128:256] + after + before


def convolve(grid, count, taps, pairs, put):
    edge = grid.shape[2]
    planes = 2
    rows = planes * edge * edge
    place = lax.broadcasted_iota(jnp.int32, (planes * edge, edge, 128), 1)
    halved = grid.reshape(grid.shape[0], edge // 2 + 1, 2, edge, 128)
    for z in range(0, count, planes):
        left = jnp.concatenate(
            [
                grid[z + dz : z + dz + planes, dy : dy + edge].reshape(rows, 128)
                for dz in range(3)
                for dy in range(3)
            ],
            axis=1,
        )
        wide = jnp.dot(left, taps[:, 0:256], preferred_element_type=jnp.float32)
        wide = wide.reshape(planes * edge, edge, 256)
        left = jnp.concatenate(
            [
                halved[z + dz : z + dz + planes, line // 2 : line // 2 + edge // 2, line % 2].reshape(
                    rows // 2, 128
                )
                for dz in range(3)
                for line in range(4)
            ],
            axis=1,
        )
        two = jnp.dot(left, pairs[...], preferred_element_type=jnp.float32)
        two = two.reshape(planes * edge // 2, edge, 256)
        two = jnp.stack([two[:, :, :128], two[:, :, 128:]], axis=1).reshape(planes * edge, edge, 128)
        after = jnp.where(place > 0, pltpu.roll(wide[:, :, :128], 1, 1), 0.0)
        before = jnp.where(place < edge - 1, pltpu.roll(two, edge - 1, 1), 0.0)
        new = wide[:, :, 128:256] + after + before
        put(z, new.reshape(planes, edge, edge, 128))


def clear_sides(grid):
    blank = jnp.zeros(grid.shape[:1] + grid.shape[2:], grid.dtype)
    grid[:, 0] = blank
    grid[:, grid.shape[1] - 1] = blank


def local_planes(x, lo, count, taps, pairs, grid, act):
    edge = x.shape[0]
    clear_sides(grid)
    first, last = max(lo - 1, 0), min(lo + count + 1, edge)
    if first > lo - 1:
        grid[0] = jnp.zeros(grid.shape[1:], grid.dtype)
    if last < lo + count + 1:
        grid[count + 1] = jnp.zeros(grid.shape[1:], grid.dtype)
    grid[first - lo + 1 : last - lo + 1, 1 : edge + 1] = x[first:last]

    def put(z, new):
        act[z : z + new.shape[0]] = new

    convolve(grid, count, taps, pairs, put)


def front_half_kernel(pos, x, weight, deep_weight, act, taps, pairs, piece, grid):
    spread_taps(weight, taps)
    pair_taps(weight, pairs)
    size = piece.shape[1]
    if size < deep_weight.shape[1]:
        piece[...] = deep_weight[:, pl.ds(pl.multiple_of(pos[pos.shape[0] - 1] * size, size), size)]
    else:
        piece[...] = deep_weight[...]
    local_planes(x, 0, act.shape[0], taps, pairs, grid, act)


def back_half_kernel(_, x, taps, pairs, after, act, grid):
    del after
    local_planes(x, x.shape[0] - act.shape[0], act.shape[0], taps, pairs, grid, act)


def rim_kernel(ny, nx, pos, *refs):
    x, near, far, y_halos, x_halos, corners, front, back, taps, pairs, act, stats, grid, column, flanks = refs
    edge = x.shape[0]
    half = edge // 2
    wide_face = edge + ny + nx
    depth = edge + 4
    f32, bf16 = jnp.float32, jnp.bfloat16
    act[2 : 2 + half] = near[...]
    act[2 + half : 2 + edge] = far[...]

    clear_sides(grid)
    for face, halo_at, own_at, own, out_at, touched, dz in (
        (front, 0, 3, 0, 0, 2, 0),
        (back, 1, 0, edge - 1, depth - 2, depth - 3, 2),
    ):
        for k in range(3):
            grid[halo_at + k, 1 : edge + 1] = face[k * wide_face : k * wide_face + edge]
        grid[own_at, 1 : edge + 1] = x[own]

        def put(z, new):
            act[out_at + z : out_at + z + new.shape[0]] = new

        convolve(grid, 2, taps, pairs, put)
        beside = halo_at + (2 if dz == 0 else 0)
        left = jnp.concatenate(
            [grid[beside, dy : dy + edge].reshape(edge * edge, 128) for dy in range(3)], axis=1
        )
        wide = jnp.dot(left, taps[dz * 384 : dz * 384 + 384, :], preferred_element_type=f32)
        act[touched] += join_x(wide.reshape(edge, edge, 384), edge)

    def rim(face, row):
        return jnp.stack([face[k * wide_face + edge + row] for k in range(3)])

    for i in range(ny):
        low = pos[i] == 1
        line = jnp.concatenate([rim(front, i), y_halos[i], rim(back, i)], axis=0)
        left = jnp.concatenate(
            [line[dz : dz + depth].reshape(depth * edge, 128) for dz in range(3)], axis=1
        )
        start = jnp.where(low, 0, 256)
        right = jnp.concatenate(
            [taps[pl.ds(pl.multiple_of(start + dz * 384, 128), 128), :] for dz in range(3)], axis=0
        )
        wide = jnp.dot(left, right, preferred_element_type=f32)
        act[:, jnp.where(low, 0, edge - 1)] += join_x(wide.reshape(depth, edge, 384), edge)

    flat = act.reshape(depth * edge * edge, 128)
    for j in range(nx):
        column[:, 0:8] = jnp.zeros((depth + 2, 8, 128), f32)
        column[:, 8 + edge :] = jnp.zeros((depth + 2, 8, 128), f32)
        column[3 : edge + 3, 8 : 8 + edge] = x_halos[j].astype(f32)
        column[0:3, 8 : 8 + edge] = rim(front, ny + j).astype(f32)
        column[edge + 3 :, 8 : 8 + edge] = rim(back, ny + j).astype(f32)
        rows = edge + 16
        lines = column.reshape((depth + 2) * rows, 128)
        for i in range(ny):
            k = i * nx + j
            low = pos[i] == 1
            for at, count, ends in (
                (0, 3, front[3 * wide_face + k].astype(f32)[edge - 3 :]),
                (3, edge, corners[k].astype(f32)),
                (edge + 3, 3, back[3 * wide_face + k].astype(f32)[:3]),
            ):
                first, last = ends, ends
                if ny == 1:
                    first, last = jnp.where(low, ends, 0.0), jnp.where(low, 0.0, ends)
                if ny == 1 or i == 0:
                    lines[pl.ds(at * rows + 7, count, stride=rows), :] = first
                if ny == 1 or i == 1:
                    lines[pl.ds(at * rows + 8 + edge, count, stride=rows), :] = last
        for dy in range(3):
            piece = column[:, 7 + dy : 7 + dy + edge].astype(bf16)
            flanks[:, :, dy * 128 : dy * 128 + 128] = piece
        left = jnp.concatenate(
            [flanks[dz : dz + depth].reshape(depth * edge, 384) for dz in range(3)], axis=1
        )
        right = jnp.concatenate([taps[:, 0:128], taps[:, 256:384]], axis=1)
        extra = jnp.dot(left, right, preferred_element_type=f32)
        low = pos[ny + j] == 1
        first, last = extra[:, :128], extra[:, 128:]
        if nx == 1:
            first, last = jnp.where(low, first, 0.0), jnp.where(low, 0.0, last)
        if nx == 1 or j == 0:
            flat[pl.ds(0, depth * edge, stride=edge), :] += first
        if nx == 1 or j == 1:
            flat[pl.ds(edge - 1, depth * edge, stride=edge), :] += last

    def sum_step(k, carry):
        return carry + jnp.sum(act[k].reshape(edge * 2, 8, 128), axis=0)

    total = lax.fori_loop(2, edge + 2, sum_step, jnp.zeros((8, 128), f32), unroll=4)
    mean = jnp.sum(total, axis=0, keepdims=True) / edge**3

    def spread_step(k, carry):
        off = act[k].reshape(edge * 2, 8, 128) - mean
        return carry + jnp.sum(off * off, axis=0)

    total = lax.fori_loop(2, edge + 2, spread_step, jnp.zeros((8, 128), f32), unroll=4)
    put_stats(stats, mean, jnp.sum(total, axis=0, keepdims=True))


def put_stats(stats, mean, spread):
    both = jnp.concatenate([mean, spread], axis=0)
    stats[...] = jnp.broadcast_to(both[None], stats.shape)


def group_sums(row, width):
    lane = lax.broadcasted_iota(jnp.int32, row.shape, 1)
    size, step = row.shape[1], 1
    while step < width:
        above, below = pltpu.roll(row, size - step, 1), pltpu.roll(row, step, 1)
        row = row + jnp.where(jnp.bitwise_and(lane, step) == 0, above, below)
        step *= 2
    return row


def read_stats(stats, rows):
    devices, _, channels = stats.shape
    width = channels // GROUPS
    means, spreads = stats[:, 0, :], stats[:, 1, :]

    def grouped(row):
        return group_sums(jnp.broadcast_to(row, (8, channels)), width)[0:1]

    mean = grouped(jnp.sum(means, axis=0, keepdims=True)) / (devices * width)
    off = means - mean
    total = grouped(jnp.sum(spreads + rows * (off * off), axis=0, keepdims=True))
    return mean, lax.rsqrt(total / (rows * devices * width) + EPSILON)


def silu_of_double(h):
    return h + h * jnp.tanh(h)


def norm_kernel(ny, nx, pos, act, stats, gain, offset, out, pooled, *refs):
    y_edges, x_edges, corners, half = refs
    depth, edge = act.shape[0], act.shape[1]
    deep, deep_depth = edge // 2, depth // 2
    f32, bf16 = jnp.float32, jnp.bfloat16
    mean, scale = read_stats(stats, float(edge**3))
    scale = scale * (0.5 * gain[...])
    shift = 0.5 * offset[...]
    for k in range(deep_depth):
        value = silu_of_double((act[2 * k : 2 * k + 2] - mean) * scale + shift).astype(bf16)
        if 0 < k < deep_depth - 1:
            out[2 * k - 2 : 2 * k] = value
        value = value.astype(f32)
        value = (value[0] + value[1]).reshape(deep, 2, edge, 128)
        half[k] = (value[:, 0] + value[:, 1]).reshape(deep * edge, 128)
        lines = half.at[k]
        pair = lines[pl.ds(0, deep * deep, stride=2), :] + lines[pl.ds(1, deep * deep, stride=2), :]
        pair = (pair * 0.125).astype(bf16).astype(f32).reshape(deep, deep, 128)
        if k == 0 or k == deep_depth - 1:
            inside = pos[ny + nx + (0 if k == 0 else 1)] == 1
            pair = jnp.where(inside, pair, 0.0)
        pooled[k] = pair
    lines = pooled.reshape(deep_depth * deep * deep, 128)
    rows = deep_depth * deep
    first_x = lines[pl.ds(0, rows, stride=deep), :]
    last_x = lines[pl.ds(deep - 1, rows, stride=deep), :]
    first_y, last_y = (pooled[:, y].reshape(rows, 128) for y in (0, deep - 1))
    ends = []
    for y in (0, deep - 1):
        for x in (0, deep - 1):
            ends.append(lines[pl.ds(y * deep + x, deep_depth, stride=deep * deep), :])
    if ny == 1:
        above, left = pos[0] == 1, pos[1] == 1
        y_edges[0] = jnp.where(above, first_y, last_y).astype(bf16)
        x_edges[0] = jnp.where(left, first_x, last_x).astype(bf16)
        corners[0, 0:deep_depth] = jnp.where(
            above, jnp.where(left, ends[0], ends[1]), jnp.where(left, ends[2], ends[3])
        )
    else:
        y_edges[0], y_edges[1] = first_y.astype(bf16), last_y.astype(bf16)
        x_edges[0], x_edges[1] = first_x.astype(bf16), last_x.astype(bf16)
        for k in range(4):
            corners[k, 0:deep_depth] = ends[k]


def stack_kernel(*refs):
    out = refs[-1]
    for k in range(out.shape[0]):
        out[k] = refs[k][...]


def stack(*arrays):
    vmem = pl.BlockSpec(memory_space=pltpu.VMEM)
    return pl.pallas_call(
        stack_kernel,
        out_shape=jax.ShapeDtypeStruct((len(arrays),) + arrays[0].shape, arrays[0].dtype),
        in_specs=[vmem] * len(arrays),
        out_specs=vmem,
        compiler_params=pltpu.CompilerParams(vmem_limit_bytes=VMEM_BYTES),
    )(*arrays)


def place_kernel(tiles, pos, own, held, kernel):
    shard, part = own.shape[1], held.shape[3]
    tile, mine = pos[pos.shape[0] - 2], pos[pos.shape[0] - 1]

    def place(rows, at):
        for tap in range(27):
            lane = tap % 9 * 128
            kernel[tap // 9, pl.ds(at, rows.shape[1]), lane : lane + 128] = rows[tap]

    place(own, pl.multiple_of(tile * shard, shard))
    for piece in range(held.shape[0]):
        at = jnp.bitwise_xor(mine, piece) * part
        for k in range(1, tiles):
            base = lax.rem(tile + tiles - k, tiles) * shard
            place(held.at[piece, k - 1], pl.multiple_of(base + at, part))


def deep_kernel(ny, nx, pos, pooled, y_halos, x_halos, corners, kernel, *refs):
    act, stats, grid, packed = refs
    depth, deep = pooled.shape[0], pooled.shape[1]
    f32 = jnp.float32
    grid[...] = jnp.zeros(grid.shape, f32)
    grid[:, 1 : deep + 1, 8:16] = pooled[...]
    for i in range(ny):
        at = jnp.where(pos[i] == 1, 0, deep + 1)
        grid[:, at, 8:16] = y_halos[i].astype(f32).reshape(depth, deep, 128)
    pitch = (deep + 2) * 24
    flat = grid.reshape(depth * pitch, 128)
    for j in range(nx):
        left = pos[ny + j] == 1
        column = x_halos[j].astype(f32).reshape(depth, deep, 128)
        for side, here in ((7, left), (16, jnp.logical_not(left))):
            if nx == 2 and side != (7, 16)[j]:
                continue
            for z in range(depth):
                kept = column[z] if nx == 2 else jnp.where(here, column[z], 0.0)
                flat[pl.ds(z * pitch + 24 + side, deep, stride=24), :] = kept
            for i in range(ny):
                end = corners[i * nx + j, 0:depth]
                above = pos[i] == 1
                for y, there in ((0, above), (deep + 1, jnp.logical_not(above))):
                    if ny == 2 and y != (0, deep + 1)[i]:
                        continue
                    kept = end
                    if nx == 1:
                        kept = jnp.where(jnp.logical_and(here, there), end, 0.0)
                    flat[pl.ds(y * 24 + side, depth, stride=pitch), :] = kept

    for dx in range(3):
        plane = grid[:, :, 7 + dx : 15 + dx]
        for y in range(deep + 1):
            both = jnp.concatenate([plane[:, y], plane[:, y + 1]], axis=1)
            packed[:, y // 2, y % 2, :, dx * 128 : dx * 128 + 128] = both.astype(jnp.bfloat16)

    rows = deep**3
    total = None
    for dz in range(3):
        left = jnp.concatenate(
            [
                packed[dz : dz + deep, dy // 2 : dy // 2 + deep // 2, dy % 2].reshape(rows, 384)
                for dy in range(3)
            ],
            axis=1,
        )
        term = lax.dot_general(
            left, kernel[dz], (((1,), (1,)), ((), ())), preferred_element_type=f32
        )
        total = term if total is None else total + term
    act[...] = total
    mean = jnp.sum(total, axis=0, keepdims=True) / rows
    off = total - mean
    put_stats(stats, mean, jnp.sum(off * off, axis=0, keepdims=True))


def final_kernel(_, act, stats, gain, offset, up, mid, out, wide, held, sems):
    edge = mid.shape[0]
    deep = edge // 2
    f32 = jnp.float32
    mean, scale = read_stats(stats, float(deep**3))
    scale = scale * (0.5 * gain[...])
    value = silu_of_double((act[...] - mean) * scale + 0.5 * offset[...]).astype(jnp.bfloat16)
    lifted = jnp.dot(value, up[...], preferred_element_type=f32)
    wide[pl.ds(0, deep**3, stride=2), :] = lifted
    wide[pl.ds(1, deep**3, stride=2), :] = lifted
    size = deep * edge
    copies = []
    for k in range(deep):
        add = wide[k * size : k * size + size, :].reshape(1, deep, 1, edge, 128)
        old = mid[2 * k : 2 * k + 2].astype(f32).reshape(2, deep, 2, edge, 128)
        held[2 * k : 2 * k + 2] = (old + add).astype(jnp.bfloat16).reshape(2, edge, edge, 128)
        copy = pltpu.make_async_copy(
            held.at[2 * k : 2 * k + 2], out.at[2 * k : 2 * k + 2], sems.at[k]
        )
        copy.start()
        copies.append(copy)
    for copy in copies:
        copy.wait()


def body(
    features, conv_weight, gain_mid, offset_mid, deep_weight, gain_deep, offset_deep, up_weight
):
    f32, bf16 = jnp.float32, jnp.bfloat16
    edge, channels = features.shape[0], features.shape[3]
    deep = edge // 2
    deep_channels = gain_deep.shape[0]
    square = Square()
    tiles = square.tiles
    devices = lax.axis_size("gz") * tiles
    y_low, x_low = square.low_sides()
    ny, nx = len(y_low), len(x_low)
    axes = split_axes(deep_weight.shape[4])
    mine = sum(lax.axis_index(axis) % 2 * 2**k for k, axis in enumerate(axes))
    depth_at = lax.axis_index("gz")
    inside = [depth_at > 0, depth_at < lax.axis_size("gz") - 1]
    pos = y_low + x_low + inside + [lax.axis_index("yx"), mine]
    pos = jnp.stack([jnp.asarray(v, jnp.int32) for v in pos])

    own = jnp.moveaxis(deep_weight, 4, 3).reshape(27, deep_weight.shape[4], channels)
    conv_weight = conv_weight.reshape(27, channels, channels)
    *edges, features, conv_weight, own = call(
        functools.partial(start_kernel, ny, nx),
        [
            ((ny, edge, edge, channels), bf16),
            ((nx, edge, edge, channels), bf16),
            ((ny * nx, edge, channels), bf16),
            (features.shape, bf16),
            (conv_weight.shape, bf16),
            (own.shape, bf16),
        ],
        [((edge * edge, 8, channels), f32), pltpu.SemaphoreType.DMA((6,))],
        pos,
        features,
        conv_weight,
        own,
        nbytes=5 << 20,
        in_hbm=True,
    )
    halos = square.halos(*(list(piece) for piece in edges))
    half_act = ((deep, edge, edge, channels), f32)
    half_grid = ((deep + 2, edge + 2, edge, channels), bf16)
    conv_flops = 27 * channels * channels * edge**3
    near, taps, pairs, piece = call(
        front_half_kernel,
        [
            half_act,
            ((9 * channels, 3 * channels), bf16),
            ((12 * channels, 2 * channels), bf16),
            ((27, own.shape[1] // 2 ** len(axes), channels), bf16),
        ],
        [half_grid],
        pos,
        features,
        conv_weight,
        own,
        flops=conv_flops,
        nbytes=3 << 20,
    )
    piece, (y, x, corner) = lax.optimization_barrier((piece, halos))
    y, x, corner = jnp.stack(y), jnp.stack(x), jnp.stack(corner)
    face = ((3 * (edge + ny + nx) + ny * nx, edge, channels), bf16)
    faces = call(
        functools.partial(face_kernel, ny, nx), [face, face], [], pos, features, y, x, corner
    )
    front, back = swap_depth(*faces)
    got = rotate_shards(piece)
    (far,) = call(
        back_half_kernel,
        [half_act],
        [half_grid],
        pos,
        features,
        taps,
        pairs,
        corner,
        flops=conv_flops,
        nbytes=3 << 20,
    )
    act, stats = call(
        functools.partial(rim_kernel, ny, nx),
        [((edge + 4, edge, edge, channels), f32), ((devices, 2, channels), f32)],
        [
            ((4, edge + 2, edge, channels), bf16),
            ((edge + 6, edge + 16, channels), f32),
            ((edge + 6, edge, 3 * channels), bf16),
        ],
        pos,
        features,
        near,
        far,
        y,
        x,
        corner,
        front,
        back,
        taps,
        pairs,
    )
    stats, *got = lax.optimization_barrier((stats, *got))
    stats = share(stats)
    held = stack(*got)[None]
    for axis in axes:
        other = swap(held, axis, 1)
        if axis == "cand":
            stats, other = lax.optimization_barrier((stats, other))
        held = stack(held, other)
        held = held.reshape((-1,) + held.shape[2:])
    out, pooled, *edges = call(
        functools.partial(norm_kernel, ny, nx),
        [
            ((edge, edge, edge, channels), bf16),
            ((deep + 2, deep, deep, channels), f32),
            ((ny, (deep + 2) * deep, channels), bf16),
            ((nx, (deep + 2) * deep, channels), bf16),
            ((ny * nx, 16, channels), f32),
        ],
        [((deep + 2, deep * edge, channels), f32)],
        pos,
        act,
        stats,
        gain_mid.reshape(1, channels),
        offset_mid.reshape(1, channels),
        flops=20 * channels * edge**3,
        nbytes=3 << 20,
    )
    y, x, corner = square.halos(*(list(piece) for piece in edges))
    (kernel,) = call(
        functools.partial(place_kernel, tiles),
        [((3, deep_channels, 9 * channels), bf16)],
        [],
        pos,
        own,
        held,
        nbytes=4 << 20,
    )
    deep_act, stats = call(
        functools.partial(deep_kernel, ny, nx),
        [((deep**3, deep_channels), f32), ((devices, 2, deep_channels), f32)],
        [
            ((deep + 2, deep + 2, 24, channels), f32),
            ((deep + 2, deep // 2 + 1, 2, 16, 3 * channels), bf16),
        ],
        pos,
        pooled,
        jnp.stack(y),
        jnp.stack(x),
        jnp.stack(corner),
        kernel,
        flops=2 * 27 * channels * deep_channels * deep**3,
        nbytes=4 << 20,
    )
    stats = share(stats)
    (decoded,) = call(
        final_kernel,
        [((edge, edge, edge, channels), bf16)],
        [
            ((2 * deep**3, channels), f32),
            ((edge, edge, edge, channels), bf16),
            pltpu.SemaphoreType.DMA((deep,)),
        ],
        pos,
        deep_act,
        stats,
        gain_deep.reshape(1, deep_channels),
        offset_deep.reshape(1, deep_channels),
        up_weight,
        out,
        flops=4 * deep_channels * channels * deep**3,
        nbytes=3 << 20,
        out_hbm=True,
    )
    return decoded


def solution(mesh):
    placed = (
        P(("cand", "gz"), "yx", None, None),
        P(),
        P(),
        P(),
        P(None, None, None, None, "yx"),
        P(),
        P(),
        P(),
    )
    return jax.shard_map(
        body,
        mesh=mesh,
        in_specs=placed,
        out_specs=P(("cand", "gz"), "yx", None, None),
        check_vma=False,
    )
```

time: 74.1 us -> 68.9 us (0.930)
  blocking collectives: 0 us -> 24.9 us
  starting transfers between devices: 37.5 us -> 18.4 us
  waiting for transfers between devices: 16 us -> 3.57 us
  Pallas kernels: 15.8 us -> 18 us
    all_to_all x0 -> x2, blocking collectives: none -> 24.9 us  [share(): return lax.all_to_all(stats, PART, 0, 0)]
    ppermute x10 -> x2, waiting for transfers between devices: 14 us -> 0.01 us  [swap(): lax.ppermute(block, axis, [(i, i ^ mask) for i in range(lax.axis_size(axi...]
    ppermute x10 -> x2, starting transfers between devices: 13.9 us -> 1.77 us  [swap(): lax.ppermute(block, axis, [(i, i ^ mask) for i in range(lax.axis_size(axi...]
    ppermute x2 -> x1, starting transfers between devices: 6.07 us -> 1.3 us  [swap_depth(): lax.ppermute(high, 'gz', up)]
    ppermute x2, waiting for transfers between devices: 1.1 us -> 3.53 us  [halos(): corner = lax.ppermute(corners[0], 'yx', self.swap_route(3))]
    pallas_call x8 -> x9, Pallas kernels: 15.7 us -> 17.9 us  [call(): pl.pallas_call(kernel, out_shape=[jax.ShapeDtypeStruct(shape, dtype) for...]
    ppermute x2, starting transfers between devices: 1.16 us -> 3.26 us  [halos(): corner = lax.ppermute(corners[0], 'yx', self.swap_route(3))]
    ppermute x2, starting transfers between devices: 6.68 us -> 4.77 us  [halos(): y = lax.ppermute(y_edges[0], 'yx', self.swap_route(2))]
  transfers between devices with their start and end apart: 23 -> 13, of which waited for: 11 -> 2; matrix products, arithmetic and copies ran while one was open for 1% -> 0% of each run, Pallas kernels for 14% -> 17%
where the time goes in v5:
time: 68.9 us; the launch traced here: 68.6 us
  blocking collectives  24.9 us (36%)
  starting transfers between devices  18.4 us (27%)
  Pallas kernels  18 us (26%)
  waiting for transfers between devices  3.57 us (5%)
  local copies, waits for them, and re-layouts  3.52 us (5%)
    all_to_all x2, blocking collectives, share(): return lax.all_to_all(stats, PART, 0, 0)  24.9 us
    pallas_call x9, Pallas kernels, call(): pl.pallas_call(kernel, out_shape=[jax.ShapeDtypeStruct(shape, dtype) for...  17.9 us
    ppermute x2, starting transfers between devices, halos(): y = lax.ppermute(y_edges[0], 'yx', self.swap_route(2))  4.77 us
    ppermute x3, starting transfers between devices, rotate_shards(): lax.ppermute(piece, 'yx', [(i, (i + k) % tiles) for i in range(tiles)])  3.87 us
    ppermute x2, waiting for transfers between devices, halos(): corner = lax.ppermute(corners[0], 'yx', self.swap_route(3))  3.53 us
    unnamed x16, local copies, waits for them, and re-layouts  3.44 us
    ppermute x2, starting transfers between devices, halos(): corner = lax.ppermute(corners[0], 'yx', self.swap_route(3))  3.26 us
    ppermute x2, starting transfers between devices, halos(): x = lax.ppermute(x_edges[0], 'yx', self.swap_route(1))  2.13 us
  transfers between devices with their start and end apart: 13, of which 2 were waited for; matrix products, arithmetic and copies ran while one was open for 0% of the time, Pallas kernels for 17%

profile of v5, /device:TPU:0, one launch (start us, length us, event | category | flops | bytes accessed | tf_op | source)
XLA Modules:
  0.0 68.6 jit_solution(6636048556598111358)
XLA Ops:
  0.0 0.1 stack.53.pos._
  0.1 0.0 copy-start
  0.1 1.2 %copy-done = bf16[16,16,16,128]{3,2,1,0:T(8,128)(2,1)S(1)} copy-done((bf16[16,16,16,128]{3,2,1,0:T(8,128)(2,1)S(1)}, bf16[16,16,16,128]{3,2,1,0:T(8,128)(2,1)}, u32[]{:S(2)}) %copy-start) | copy-done | bytes 1048600
  1.3 0.0 copy-start.1
  1.3 1.2 %copy-done.1 = bf16[3,3,3,128,128]{4,3,2,1,0:T(8,128)(2,1)S(1)} copy-done((bf16[3,3,3,128,128]{4,3,2,1,0:T(8,128)(2,1)S(1)}, bf16[3,3,3,128,128]{4,3,2,1,0:T(8,128)(2,1)}, u32[]{:S(2)}) %copy-start.1) | copy-done | bytes 884760
  2.5 0.0 copy-start.2
  2.5 1.0 %copy-done.2 = bf16[3,3,3,128,64]{3,4,2,1,0:T(8,128)(2,1)S(1)} copy-done((bf16[3,3,3,128,64]{3,4,2,1,0:T(8,128)(2,1)S(1)}, bf16[3,3,3,128,64]{3,4,2,1,0:T(8,128)(2,1)}, u32[]{:S(2)}) %copy-start.2) | copy-done | bytes 442392
  3.5 1.4 %shard_map.82 = (bf16[1,16,16,128]{3,2,1,0:T(8,128)(2,1)S(1)}, bf16[1,16,16,128]{3,2,1,0:T(8,128)(2,1)S(1)}, bf16[1,16,128]{2,1,0:T(8,128)(2,1)S(1)}, bf16[16,16...) custom-call(s32[6]{0:T(128)S(1)} %stack.53.pos._, ...), custom_call_target="tpu_custom_call" | custom-call | bytes 5242880 | tf_op jit(solution)/shard_map/pallas_call | solution.py:87
  4.9 4.1 %collective-permute-start = (bf16[16,16,128]{2,1,0:T(8,128)(2,1)S(1)}, bf16[16,16,128]{2,1,0:T(8,128)(2,1)S(1)}, u32[]{:S(2)}, u32[]{:S(2)}) collective-permute-start(bf16[16,16,128]{2,1,0:T(8,128)(2,1)S(1)} %bitcast.48), channel_id=1, source_target_pairs={{0,2},{1,3},{2,0},{3,1},{4,6},{5,7},{6,4},{7,5},{8,10},{9,11},{10,... | collective-permute-start | bytes 196616 | tf_op jit(solution)/shard_map/ppermute | solution.py:44
  9.0 1.6 %collective-permute-start.1 = (bf16[16,16,128]{2,1,0:T(8,128)(2,1)S(1)}, bf16[16,16,128]{2,1,0:T(8,128)(2,1)S(1)}, u32[]{:S(2)}, u32[]{:S(2)}) collective-permute-start(bf16[16,16,128]{2,1,0:T(8,128)(2,1)S(1)} %bitcast.47), channel_id=1, source_target_pairs={{0,1},{1,0},{2,3},{3,2},{4,5},{5,4},{6,7},{7,6},{8,9},{9,8},{10,11... | collective-permute-start | bytes 196616 | tf_op jit(solution)/shard_map/ppermute | solution.py:45
  10.6 0.0 collective-permute-start.2
  10.6 3.1 %shard_map.83 = (f32[8,16,16,128]{3,2,1,0:T(8,128)S(1)}, bf16[1152,384]{1,0:T(8,128)(2,1)S(1)}, bf16[1536,256]{1,0:T(8,128)(2,1)S(1)}, bf16[27,16,128]{2,1,0:T(8,128)(2,1)S(1)}) custom-call(s32[6]{0:T(128)S(1)} %stack.53.pos._, bf16[16,16,16,128]{3,2,1,0:T(8,128)(2,1)S(1)} %get-tuple-element.36.x.refs_0_, ...), custom_call_target="tpu_custom_call" | custom-call | flops 1811939328 | bytes 3145728 | tf_op jit(solution)/shard_map/pallas_call | solution.py:87
  13.7 2.3 %collective-permute-done.2 = bf16[16,128]{1,0:T(8,128)(2,1)S(1)} collective-permute-done((bf16[16,128]{1,0:T(8,128)(2,1)S(1)}, bf16[16,128]{1,0:T(8,128)(2,1)S(1)}, u32[]{:S(2)}, u32[]{:S(2)}) %collective-permute-start.2) | collective-permute-done | bytes 4128 | tf_op jit(solution)/shard_map/ppermute | solution.py:46
  16.0 0.0 collective-permute-done
  16.0 0.0 collective-permute-done.1
  16.0 0.6 shard_map.85
  16.6 1.3 %collective-permute-start.3 = (bf16[55,16,128]{2,1,0:T(8,128)(2,1)S(1)}, bf16[55,16,128]{2,1,0:T(8,128)(2,1)S(1)}, u32[]{:S(2)}, u32[]{:S(2)}) collective-permute-start(bf16[55,16,128]{2,1,0:T(8,128)(2,1)S(1)} %get-tuple-element.49), channel_id=1, source_target_pairs={{0,4},{4,8},{8,12},{1,5},{5,9},{9,13},{2,6},{6,10},{10,14},{3,7},{... | collective-permute-start | bytes 675848 | tf_op jit(solution)/shard_map/ppermute | solution.py:61
  17.9 1.3 %collective-permute-start.4 = (bf16[55,16,128]{2,1,0:T(8,128)(2,1)S(1)}, bf16[55,16,128]{2,1,0:T(8,128)(2,1)S(1)}, u32[]{:S(2)}, u32[]{:S(2)}) collective-permute-start(bf16[55,16,128]{2,1,0:T(8,128)(2,1)S(1)} %get-tuple-element.50), channel_id=1, source_target_pairs={{4,0},{8,4},{12,8},{5,1},{9,5},{13,9},{6,2},{10,6},{14,10},{7,3},{... | collective-permute-start | bytes 675848 | tf_op jit(solution)/shard_map/ppermute | solution.py:61
  19.2 0.1 collective-permute-start.5
  19.2 2.1 %collective-permute-start.6 = (bf16[27,16,128]{2,1,0:T(8,128)(2,1)S(1)}, bf16[27,16,128]{2,1,0:T(8,128)(2,1)S(1)}, u32[]{:S(2)}, u32[]{:S(2)}) collective-permute-start(bf16[27,16,128]{2,1,0:T(8,128)(2,1)S(1)} %get-tuple-element.53), channel_id=1, source_target_pairs={{0,2},{1,3},{2,0},{3,1},{4,6},{5,7},{6,4},{7,5},{8,10},{9,11},{10,... | collective-permute-start | bytes 331784 | tf_op jit(solution)/shard_map/ppermute | solution.py:71
  21.3 1.7 %collective-permute-start.7 = (bf16[27,16,128]{2,1,0:T(8,128)(2,1)S(1)}, bf16[27,16,128]{2,1,0:T(8,128)(2,1)S(1)}, u32[]{:S(2)}, u32[]{:S(2)}) collective-permute-start(bf16[27,16,128]{2,1,0:T(8,128)(2,1)S(1)} %get-tuple-element.53), channel_id=1, source_target_pairs={{0,3},{1,0},{2,1},{3,2},{4,7},{5,4},{6,5},{7,6},{8,11},{9,8},{10,9... | collective-permute-start | bytes 331784 | tf_op jit(solution)/shard_map/ppermute | solution.py:71
  23.1 2.9 %shard_map.84.refs_2_ = f32[8,16,16,128]{3,2,1,0:T(8,128)S(1)} custom-call(s32[6]{0:T(128)S(1)} %stack.53.pos._, bf16[16,16,16,128]{3,2,1,0:T(8,128)(2,1)S(1)} %get-tuple-element.36.x.refs_0_, bf16[1152,384]{1,0:T(8,128)(2,1)S(1)} %get-tuple-element.40.taps.refs_8_, bf16[1536,256]{1,0:T(8,128)(2,1)S(1)} %get-tuple-element.41.pairs.refs_9_, ...), custom_call_target="tpu_custom_call" | custom-call | flops 1811939328 | bytes 3145728 | tf_op jit(solution)/shard_map/pallas_call | solution.py:87
  26.0 0.0 collective-permute-done.3.refs_6_
  26.0 0.0 collective-permute-done.4.refs_7_
  26.0 3.2 %shard_map.86 = (f32[20,16,16,128]{3,2,1,0:T(8,128)S(1)}, f32[16,2,128]{2,1,0:T(2,128)S(1)}) custom-call(s32[6]{0:T(128)S(1)} %stack.53.pos._, bf16[16,16,16,128]{3,2,1,0:T(8,128)(2,1)S(1)} %get-tuple-element.36.x.refs_0_, f32[8,16,16,128]{3,2,1,0:T(8,128)S(1)} %get-tuple-element.39.refs_1_, f32[8,16,16,128]{3,2,1,0:T(8,128)S(1)} %shard_map.84.refs_2_, ...), custom_call_target="tpu_custom_call" | custom-call | tf_op jit(solution)/shard_map/pallas_call | solution.py:87
  29.1 0.0 copy-start.6
  29.1 0.0 copy-start.7
  29.2 0.0 collective-permute-done.5.refs_0_
  29.2 0.0 collective-permute-done.6.refs_1_
  29.2 0.0 collective-permute-done.7.refs_2_
  29.2 1.6 %collective-permute-start.8 = (bf16[1,3,27,16,128]{4,3,2,1,0:T(8,128)(2,1)S(1)}, bf16[1,3,27,16,128]{4,3,2,1,0:T(8,128)(2,1)S(1)}, u32[]{:S(2)}, u32[]{:S(2)}) collective-permute-start(bf16[1,3,27,16,128]{4,3,2,1,0:T(8,128)(2,1)S(1)} %bitcast.32), channel_id=1, source_target_pairs={{0,16},{16,0},{1,17},{17,1},{2,18},{18,2},{3,19},{19,3},{4,20},{20... | collective-permute-start | bytes 995336 | tf_op jit(solution)/shard_map/ppermute | solution.py:76
  30.8 13.9 %all_to_all.10.stats = f32[16,2,128]{2,1,0:T(2,128)S(1)} all-to-all(f32[16,2,128]{2,1,0:T(2,128)S(1)} %get-tuple-element.54), channel_id=1, replica_groups=mesh['cand'=2,'gz'=4,'yx'=4] {'gz','yx'}, dimensions={0} | all-to-all | bytes 32768 | tf_op jit(solution)/shard_map/all_to_all | solution.py:80
  44.7 0.0 collective-permute-done.8.refs_1_
  44.8 0.2 collective-permute-start.12
  45.0 0.0 copy-done.6
  45.0 0.0 copy-done.7
  45.0 1.8 %shard_map.88 = (bf16[16,16,16,128]{3,2,1,0:T(8,128)(2,1)S(1)}, f32[10,8,8,128]{3,2,1,0:T(8,128)S(1)}, bf16[1,80,128]{2,1,0:T(8,128)(2,1)S(1)}, bf16[1,80,128]{2,1,0:T(8,128)(2,1)S(1)}, f32[1,16,128]{2,1,0:T(8,128)S(1)}) custom-call(s32[6]{0:T(128)S(1)} %stack.53.pos._, f32[20,16,16,128]{3,2,1,0:T(8,128)S(1)} %get-tuple-element.51.act, ...), custom_call_target="tpu_custom_call" | custom-call | flops 10485760 | bytes 3145728 | tf_op jit(solution)/shard_map/pallas_call | solution.py:87
  46.8 0.7 collective-permute-start.9
  47.4 0.6 collective-permute-start.10
  48.0 3.3 %collective-permute-start.11 = (f32[16,128]{1,0:T(8,128)S(1)}, f32[16,128]{1,0:T(8,128)S(1)}, u32[]{:S(2)}, u32[]{:S(2)}) collective-permute-start(f32[16,128]{1,0:T(8,128)S(1)} %bitcast.53), channel_id=1, source_target_pairs={{0,3},{1,2},{2,1},{3,0},{4,7},{5,6},{6,5},{7,4},{8,11},{9,10},{10,... | collective-permute-start | bytes 24584 | tf_op jit(solution)/shard_map/ppermute | solution.py:46
  51.3 0.0 collective-permute-done.12.refs_1_
  51.3 0.1 shard_map.90
  51.4 0.8 %shard_map.91.kernel = bf16[3,256,1152]{2,1,0:T(8,128)(2,1)S(1)} custom-call(s32[6]{0:T(128)S(1)} %stack.53.pos._, bf16[27,64,128]{2,1,0:T(8,128)(2,1)S(1)} %get-tuple-element.38.deep_weight.own, bf16[4,3,27,16,128]{4,3,2,1,0:T(8,128)(2,1)S(1)} %bitcast.29), custom_call_target="tpu_custom_call" | custom-call | bytes 4194304 | tf_op jit(solution)/shard_map/pallas_call | solution.py:87
  52.2 0.0 copy-start.3
  52.2 0.0 copy-start.4
  52.2 0.0 copy-start.5
  52.2 1.2 %collective-permute-done.11 = f32[16,128]{1,0:T(8,128)S(1)} collective-permute-done((f32[16,128]{1,0:T(8,128)S(1)}, f32[16,128]{1,0:T(8,128)S(1)}, u32[]{:S(2)}, u32[]{:S(2)}) %collective-permute-start.11) | collective-permute-done | bytes 8224 | tf_op jit(solution)/shard_map/ppermute | solution.py:46
  53.4 0.0 collective-permute-done.9
  53.5 0.0 collective-permute-done.10
  53.5 1.9 %shard_map.92 = (f32[512,256]{1,0:T(8,128)S(1)}, f32[16,2,256]{2,1,0:T(2,128)S(1)}) custom-call(s32[6]{0:T(128)S(1)} %stack.53.pos._, f32[10,8,8,128]{3,2,1,0:T(8,128)S(1)} %get-tuple-element.59.pooled, bf16[1,80,128]{2,1,0:T(8,128)(2,1)S(1)} %bitcast.50, bf16[1,80,128]{2,1,0:T(8,128)(2,1)S(1)} %bitcast.52, f32[1,16,128]{2,1,0:T(8,128)S(1)} %bitcast.54, ...), custom_call_target="tpu_custom_call" | custom-call | flops 905969664 | bytes 4194304 | tf_op jit(solution)/shard_map/pallas_call | solution.py:87
  55.4 10.9 %all_to_all.11.stats = f32[16,2,256]{2,1,0:T(2,128)S(1)} all-to-all(f32[16,2,256]{2,1,0:T(2,128)S(1)} %get-tuple-element.65), channel_id=1, replica_groups=mesh['cand'=2,'gz'=4,'yx'=4] {'gz','yx'}, dimensions={0} | all-to-all | bytes 65536 | tf_op jit(solution)/shard_map/all_to_all | solution.py:80
  66.4 0.0 copy-done.3
  66.4 0.0 copy-done.4
  66.4 0.0 copy-done.5
  66.4 2.2 %shard_map.93 = bf16[16,16,16,128]{3,2,1,0:T(8,128)(2,1)} custom-call(s32[6]{0:T(128)S(1)} %stack.53.pos._, f32[512,256]{1,0:T(8,128)S(1)} %get-tuple-element.64.act, f32[16,2,256]{2,1,0:T(2,128)S(1)} %all_to_all.11.stats, f32[1,256]{1,0:T(1,128)S(1)} %bitcast.43, f32[1,256]{1,0:T(1,128)S(1)} %bitcast.44, bf16[256,128]{1,0:T(8,128)(2,1)S(1)} %copy-done.3, ...), custom_call_target="tpu_custom_call" | custom-call | flops 67108864 | bytes 3145728 | tf_op jit(solution)/shard_map/pallas_call | solution.py:87
  (2 shorter events, 0.1 us)
Async XLA Ops:
  0.1 1.2 %copy-start = (bf16[16,16,16,128]{3,2,1,0:T(8,128)(2,1)S(1)}, bf16[16,16,16,128]{3,2,1,0:T(8,128)(2,1)}, u32[]{:S(2)}) copy-start(bf16[16,16,16,128]{3,2,1,0:T(8,128)(2,1)} %x_in.1) | copy-start | bytes 3145732
  1.3 1.2 %copy-start.1 = (bf16[3,3,3,128,128]{4,3,2,1,0:T(8,128)(2,1)S(1)}, bf16[3,3,3,128,128]{4,3,2,1,0:T(8,128)(2,1)}, u32[]{:S(2)}) copy-start(bf16[3,3,3,128,128]{4,3,2,1,0:T(8,128)(2,1)} %param.9) | copy-start | bytes 2654212
  2.5 1.0 %copy-start.2 = (bf16[3,3,3,128,64]{3,4,2,1,0:T(8,128)(2,1)S(1)}, bf16[3,3,3,128,64]{3,4,2,1,0:T(8,128)(2,1)}, u32[]{:S(2)}) copy-start(bf16[3,3,3,128,64]{3,4,2,1,0:T(8,128)(2,1)} %param.12) | copy-start | bytes 1327108
  4.9 11.1 %collective-permute-start = (bf16[16,16,128]{2,1,0:T(8,128)(2,1)S(1)}, bf16[16,16,128]{2,1,0:T(8,128)(2,1)S(1)}, u32[]{:S(2)}, u32[]{:S(2)}) collective-permute-start(bf16[16,16,128]{2,1,0:T(8,128)(2,1)S(1)} %bitcast.48), channel_id=1, source_target_pairs={{0,2},{1,3},{2,0},{3,1},{4,6},{5,7},{6,4},{7,5},{8,10},{9,11},{10,... | collective-permute-start | bytes 196616 | tf_op jit(solution)/shard_map/ppermute | solution.py:44
  9.0 7.0 %collective-permute-start.1 = (bf16[16,16,128]{2,1,0:T(8,128)(2,1)S(1)}, bf16[16,16,128]{2,1,0:T(8,128)(2,1)S(1)}, u32[]{:S(2)}, u32[]{:S(2)}) collective-permute-start(bf16[16,16,128]{2,1,0:T(8,128)(2,1)S(1)} %bitcast.47), channel_id=1, source_target_pairs={{0,1},{1,0},{2,3},{3,2},{4,5},{5,4},{6,7},{7,6},{8,9},{9,8},{10,11... | collective-permute-start | bytes 196616 | tf_op jit(solution)/shard_map/ppermute | solution.py:45
  10.6 5.4 %collective-permute-start.2 = (bf16[16,128]{1,0:T(8,128)(2,1)S(1)}, bf16[16,128]{1,0:T(8,128)(2,1)S(1)}, u32[]{:S(2)}, u32[]{:S(2)}) collective-permute-start(bf16[16,128]{1,0:T(8,128)(2,1)S(1)} %bitcast.55), channel_id=1, source_target_pairs={{0,3},{1,2},{2,1},{3,0},{4,7},{5,6},{6,5},{7,4},{8,11},{9,10},{10,... | collective-permute-start | bytes 12296 | tf_op jit(solution)/shard_map/ppermute | solution.py:46
  16.6 9.4 %collective-permute-start.3 = (bf16[55,16,128]{2,1,0:T(8,128)(2,1)S(1)}, bf16[55,16,128]{2,1,0:T(8,128)(2,1)S(1)}, u32[]{:S(2)}, u32[]{:S(2)}) collective-permute-start(bf16[55,16,128]{2,1,0:T(8,128)(2,1)S(1)} %get-tuple-element.49), channel_id=1, source_target_pairs={{0,4},{4,8},{8,12},{1,5},{5,9},{9,13},{2,6},{6,10},{10,14},{3,7},{... | collective-permute-start | bytes 675848 | tf_op jit(solution)/shard_map/ppermute | solution.py:61
  17.9 8.1 %collective-permute-start.4 = (bf16[55,16,128]{2,1,0:T(8,128)(2,1)S(1)}, bf16[55,16,128]{2,1,0:T(8,128)(2,1)S(1)}, u32[]{:S(2)}, u32[]{:S(2)}) collective-permute-start(bf16[55,16,128]{2,1,0:T(8,128)(2,1)S(1)} %get-tuple-element.50), channel_id=1, source_target_pairs={{4,0},{8,4},{12,8},{5,1},{9,5},{13,9},{6,2},{10,6},{14,10},{7,3},{... | collective-permute-start | bytes 675848 | tf_op jit(solution)/shard_map/ppermute | solution.py:61
  19.2 10.0 %collective-permute-start.5 = (bf16[27,16,128]{2,1,0:T(8,128)(2,1)S(1)}, bf16[27,16,128]{2,1,0:T(8,128)(2,1)S(1)}, u32[]{:S(2)}, u32[]{:S(2)}) collective-permute-start(bf16[27,16,128]{2,1,0:T(8,128)(2,1)S(1)} %get-tuple-element.53), channel_id=1, source_target_pairs={{0,1},{1,2},{2,3},{3,0},{4,5},{5,6},{6,7},{7,4},{8,9},{9,10},{10,1... | collective-permute-start | bytes 331784 | tf_op jit(solution)/shard_map/ppermute | solution.py:71
  19.2 9.9 %collective-permute-start.6 = (bf16[27,16,128]{2,1,0:T(8,128)(2,1)S(1)}, bf16[27,16,128]{2,1,0:T(8,128)(2,1)S(1)}, u32[]{:S(2)}, u32[]{:S(2)}) collective-permute-start(bf16[27,16,128]{2,1,0:T(8,128)(2,1)S(1)} %get-tuple-element.53), channel_id=1, source_target_pairs={{0,2},{1,3},{2,0},{3,1},{4,6},{5,7},{6,4},{7,5},{8,10},{9,11},{10,... | collective-permute-start | bytes 331784 | tf_op jit(solution)/shard_map/ppermute | solution.py:71
  21.3 7.9 %collective-permute-start.7 = (bf16[27,16,128]{2,1,0:T(8,128)(2,1)S(1)}, bf16[27,16,128]{2,1,0:T(8,128)(2,1)S(1)}, u32[]{:S(2)}, u32[]{:S(2)}) collective-permute-start(bf16[27,16,128]{2,1,0:T(8,128)(2,1)S(1)} %get-tuple-element.53), channel_id=1, source_target_pairs={{0,3},{1,0},{2,1},{3,2},{4,7},{5,4},{6,5},{7,6},{8,11},{9,8},{10,9... | collective-permute-start | bytes 331784 | tf_op jit(solution)/shard_map/ppermute | solution.py:71
  29.1 15.8 %copy-start.6 = (f32[128]{0:T(128)S(1)}, f32[128]{0:T(128)}, u32[]{:S(2)}) copy-start(f32[128]{0:T(128)} %param.10) | copy-start | bytes 1540
  29.1 15.8 %copy-start.7 = (f32[128]{0:T(128)S(1)}, f32[128]{0:T(128)}, u32[]{:S(2)}) copy-start(f32[128]{0:T(128)} %param.11) | copy-start | bytes 1540
  29.2 15.5 %collective-permute-start.8 = (bf16[1,3,27,16,128]{4,3,2,1,0:T(8,128)(2,1)S(1)}, bf16[1,3,27,16,128]{4,3,2,1,0:T(8,128)(2,1)S(1)}, u32[]{:S(2)}, u32[]{:S(2)}) collective-permute-start(bf16[1,3,27,16,128]{4,3,2,1,0:T(8,128)(2,1)S(1)} %bitcast.32), channel_id=1, source_target_pairs={{0,16},{16,0},{1,17},{17,1},{2,18},{18,2},{3,19},{19,3},{4,20},{20... | collective-permute-start | bytes 995336 | tf_op jit(solution)/shard_map/ppermute | solution.py:76
  44.8 6.5 %collective-permute-start.12 = (bf16[2,3,27,16,128]{4,3,2,1,0:T(8,128)(2,1)S(1)}, bf16[2,3,27,16,128]{4,3,2,1,0:T(8,128)(2,1)S(1)}, u32[]{:S(2)}, u32[]{:S(2)}) collective-permute-start(bf16[2,3,27,16,128]{4,3,2,1,0:T(8,128)(2,1)S(1)} %bitcast.30), channel_id=1, source_target_pairs={{0,4},{4,0},{8,12},{12,8},{1,5},{5,1},{9,13},{13,9},{2,6},{6,2},{1... | collective-permute-start | bytes 1990664 | tf_op jit(solution)/shard_map/ppermute | solution.py:76
  46.8 6.7 %collective-permute-start.9 = (bf16[80,128]{1,0:T(8,128)(2,1)S(1)}, bf16[80,128]{1,0:T(8,128)(2,1)S(1)}, u32[]{:S(2)}, u32[]{:S(2)}) collective-permute-start(bf16[80,128]{1,0:T(8,128)(2,1)S(1)} %bitcast.51), channel_id=1, source_target_pairs={{0,2},{1,3},{2,0},{3,1},{4,6},{5,7},{6,4},{7,5},{8,10},{9,11},{10,... | collective-permute-start | bytes 61448 | tf_op jit(solution)/shard_map/ppermute | solution.py:44
  47.4 6.0 %collective-permute-start.10 = (bf16[80,128]{1,0:T(8,128)(2,1)S(1)}, bf16[80,128]{1,0:T(8,128)(2,1)S(1)}, u32[]{:S(2)}, u32[]{:S(2)}) collective-permute-start(bf16[80,128]{1,0:T(8,128)(2,1)S(1)} %bitcast.49), channel_id=1, source_target_pairs={{0,1},{1,0},{2,3},{3,2},{4,5},{5,4},{6,7},{7,6},{8,9},{9,8},{10,11... | collective-permute-start | bytes 61448 | tf_op jit(solution)/shard_map/ppermute | solution.py:45
  48.0 5.4 %collective-permute-start.11 = (f32[16,128]{1,0:T(8,128)S(1)}, f32[16,128]{1,0:T(8,128)S(1)}, u32[]{:S(2)}, u32[]{:S(2)}) collective-permute-start(f32[16,128]{1,0:T(8,128)S(1)} %bitcast.53), channel_id=1, source_target_pairs={{0,3},{1,2},{2,1},{3,0},{4,7},{5,6},{6,5},{7,4},{8,11},{9,10},{10,... | collective-permute-start | bytes 24584 | tf_op jit(solution)/shard_map/ppermute | solution.py:46
  52.2 14.1 %copy-start.3 = (bf16[256,128]{1,0:T(8,128)(2,1)S(1)}, bf16[256,128]{1,0:T(8,128)(2,1)}, u32[]{:S(2)}) copy-start(bf16[256,128]{1,0:T(8,128)(2,1)} %up.1) | copy-start | bytes 196612
  52.2 14.1 %copy-start.4 = (f32[256]{0:T(256)S(1)}, f32[256]{0:T(256)}, u32[]{:S(2)}) copy-start(f32[256]{0:T(256)} %param.13) | copy-start | bytes 3076
  52.2 14.1 %copy-start.5 = (f32[256]{0:T(256)S(1)}, f32[256]{0:T(256)}, u32[]{:S(2)}) copy-start(f32[256]{0:T(256)} %param.14) | copy-start | bytes 3076

commit v6 on v5

--- a/solution.py
+++ b/solution.py
@@ -84,6 +84,8 @@
     smem, vmem, hbm = (
         pl.BlockSpec(memory_space=space) for space in (pltpu.SMEM, pltpu.VMEM, pltpu.HBM)
     )
+    if in_hbm:
+        arrays = [pltpu.with_memory_space_constraint(array, pltpu.HBM) for array in arrays]
     return pl.pallas_call(
         kernel,
         out_shape=[jax.ShapeDtypeStruct(shape, dtype) for shape, dtype in outs],
@@ -176,7 +178,7 @@
 
 def convolve(grid, count, taps, pairs, put):
     edge = grid.shape[2]
-    planes = 2
+    planes = min(count, 4)
     rows = planes * edge * edge
     place = lax.broadcasted_iota(jnp.int32, (planes * edge, edge, 128), 1)
     halved = grid.reshape(grid.shape[0], edge // 2 + 1, 2, edge, 128)
@@ -243,20 +245,15 @@
     local_planes(x, 0, act.shape[0], taps, pairs, grid, act)
 
 
-def back_half_kernel(_, x, taps, pairs, after, act, grid):
-    del after
-    local_planes(x, x.shape[0] - act.shape[0], act.shape[0], taps, pairs, grid, act)
-
-
 def rim_kernel(ny, nx, pos, *refs):
-    x, near, far, y_halos, x_halos, corners, front, back, taps, pairs, act, stats, grid, column, flanks = refs
+    x, near, y_halos, x_halos, corners, front, back, taps, pairs, act, stats, half_grid, grid, column, flanks = refs
     edge = x.shape[0]
     half = edge // 2
     wide_face = edge + ny + nx
     depth = edge + 4
     f32, bf16 = jnp.float32, jnp.bfloat16
     act[2 : 2 + half] = near[...]
-    act[2 + half : 2 + edge] = far[...]
+    local_planes(x, half, half, taps, pairs, half_grid, act.at[2 + half : 2 + edge])
 
     clear_sides(grid)
     for face, halo_at, own_at, own, out_at, touched, dz in (
@@ -524,19 +521,22 @@
     f32 = jnp.float32
     mean, scale = read_stats(stats, float(deep**3))
     scale = scale * (0.5 * gain[...])
-    value = silu_of_double((act[...] - mean) * scale + 0.5 * offset[...]).astype(jnp.bfloat16)
-    lifted = jnp.dot(value, up[...], preferred_element_type=f32)
-    wide[pl.ds(0, deep**3, stride=2), :] = lifted
-    wide[pl.ds(1, deep**3, stride=2), :] = lifted
-    size = deep * edge
+    shift = 0.5 * offset[...]
+    planes = 2
+    size = planes * deep * deep
     copies = []
-    for k in range(deep):
-        add = wide[k * size : k * size + size, :].reshape(1, deep, 1, edge, 128)
-        old = mid[2 * k : 2 * k + 2].astype(f32).reshape(2, deep, 2, edge, 128)
-        held[2 * k : 2 * k + 2] = (old + add).astype(jnp.bfloat16).reshape(2, edge, edge, 128)
-        copy = pltpu.make_async_copy(
-            held.at[2 * k : 2 * k + 2], out.at[2 * k : 2 * k + 2], sems.at[k]
-        )
+    for k in range(0, deep, planes):
+        value = act[k * deep * deep : k * deep * deep + size]
+        value = silu_of_double((value - mean) * scale + shift).astype(jnp.bfloat16)
+        lifted = jnp.dot(value, up[...], preferred_element_type=f32)
+        lines = wide.at[k // planes]
+        lines[pl.ds(0, size, stride=2), :] = lifted
+        lines[pl.ds(1, size, stride=2), :] = lifted
+        add = lines[...].reshape(planes, 1, deep, 1, edge, 128)
+        at = pl.ds(2 * k, 2 * planes)
+        old = mid[at].astype(f32).reshape(planes, 2, deep, 2, edge, 128)
+        held[at] = (old + add).astype(jnp.bfloat16).reshape(2 * planes, edge, edge, 128)
+        copy = pltpu.make_async_copy(held.at[at], out.at[at], sems.at[k // planes])
         copy.start()
         copies.append(copy)
     for copy in copies:
@@ -610,22 +610,11 @@
     )
     front, back = swap_depth(*faces)
     got = rotate_shards(piece)
-    (far,) = call(
-        back_half_kernel,
-        [half_act],
-        [half_grid],
-        pos,
-        features,
-        taps,
-        pairs,
-        corner,
-        flops=conv_flops,
-        nbytes=3 << 20,
-    )
     act, stats = call(
         functools.partial(rim_kernel, ny, nx),
         [((edge + 4, edge, edge, channels), f32), ((devices, 2, channels), f32)],
         [
+            half_grid,
             ((4, edge + 2, edge, channels), bf16),
             ((edge + 6, edge + 16, channels), f32),
             ((edge + 6, edge, 3 * channels), bf16),
@@ -633,7 +622,6 @@
         pos,
         features,
         near,
-        far,
         y,
         x,
         corner,
@@ -700,9 +688,9 @@
         final_kernel,
         [((edge, edge, edge, channels), bf16)],
         [
-            ((2 * deep**3, channels), f32),
+            ((deep // 2, 4 * deep * deep, channels), f32),
             ((edge, edge, edge, channels), bf16),
-            pltpu.SemaphoreType.DMA((deep,)),
+            pltpu.SemaphoreType.DMA((deep // 2,)),
         ],
         pos,
         deep_act,

time: 68.9 us -> 66.3 us (0.962)
  local copies, waits for them, and re-layouts: 3.52 us -> 0.11 us
  waiting for transfers between devices: 3.57 us -> 4.33 us
    unnamed x16 -> x10, local copies, waits for them, and re-layouts: 3.44 us -> 0.03 us
    ppermute x3, waiting for transfers between devices: 0.02 us -> 0.84 us  [rotate_shards(): lax.ppermute(piece, 'yx', [(i, (i + k) % tiles) for i in range(tiles)])]
    pallas_call x9 -> x8, Pallas kernels: 17.9 us -> 18 us  [call(): pl.pallas_call(kernel, out_shape=[jax.ShapeDtypeStruct(shape, dtype) for...]
  transfers between devices with their start and end apart: 13 -> 13, of which waited for: 2 -> 4; matrix products, arithmetic and copies ran while one was open for 0% -> 0% of each run, Pallas kernels for 17% -> 17%
where the time goes in v6:
time: 66.3 us; the launch traced here: 66 us
  blocking collectives  24.9 us (38%)
  starting transfers between devices  18.4 us (28%)
  Pallas kernels  18.1 us (27%)
  waiting for transfers between devices  4.33 us (7%)
    all_to_all x2, blocking collectives, share(): return lax.all_to_all(stats, PART, 0, 0)  24.9 us
    pallas_call x8, Pallas kernels, call(): pl.pallas_call(kernel, out_shape=[jax.ShapeDtypeStruct(shape, dtype) for...  18 us
    ppermute x2, starting transfers between devices, halos(): y = lax.ppermute(y_edges[0], 'yx', self.swap_route(2))  4.77 us
    ppermute x3, starting transfers between devices, rotate_shards(): lax.ppermute(piece, 'yx', [(i, (i + k) % tiles) for i in range(tiles)])  3.87 us
    ppermute x2, waiting for transfers between devices, halos(): corner = lax.ppermute(corners[0], 'yx', self.swap_route(3))  3.47 us
    ppermute x2, starting transfers between devices, halos(): corner = lax.ppermute(corners[0], 'yx', self.swap_route(3))  3.26 us
    ppermute x2, starting transfers between devices, halos(): x = lax.ppermute(x_edges[0], 'yx', self.swap_route(1))  2.13 us
    ppermute x2, starting transfers between devices, swap(): lax.ppermute(block, axis, [(i, i ^ mask) for i in range(lax.axis_size(axi...  1.77 us
  transfers between devices with their start and end apart: 13, of which 4 were waited for; matrix products, arithmetic and copies ran while one was open for 0% of the time, Pallas kernels for 17%

profile of v6, /device:TPU:0, one launch (start us, length us, event | category | flops | bytes accessed | tf_op | source)
XLA Modules:
  0.0 66.0 jit_solution(17145750393346519561)
XLA Ops:
  0.0 0.1 stack.53.pos._
  0.1 2.2 %shard_map.82 = (bf16[1,16,16,128]{3,2,1,0:T(8,128)(2,1)S(1)}, bf16[1,16,16,128]{3,2,1,0:T(8,128)(2,1)S(1)}, bf16[1,16,128]{2,1,0:T(8,128)(2,1)S(1)}, bf16[16,16...) custom-call(s32[6]{0:T(128)S(1)} %stack.53.pos._, ...), custom_call_target="tpu_custom_call" | custom-call | bytes 5242880 | tf_op jit(solution)/shard_map/pallas_call | solution.py:89
  2.3 4.1 %collective-permute-start = (bf16[16,16,128]{2,1,0:T(8,128)(2,1)S(1)}, bf16[16,16,128]{2,1,0:T(8,128)(2,1)S(1)}, u32[]{:S(2)}, u32[]{:S(2)}) collective-permute-start(bf16[16,16,128]{2,1,0:T(8,128)(2,1)S(1)} %bitcast.45), channel_id=1, source_target_pairs={{0,2},{1,3},{2,0},{3,1},{4,6},{5,7},{6,4},{7,5},{8,10},{9,11},{10,... | collective-permute-start | bytes 196616 | tf_op jit(solution)/shard_map/ppermute | solution.py:44
  6.4 1.6 %collective-permute-start.1 = (bf16[16,16,128]{2,1,0:T(8,128)(2,1)S(1)}, bf16[16,16,128]{2,1,0:T(8,128)(2,1)S(1)}, u32[]{:S(2)}, u32[]{:S(2)}) collective-permute-start(bf16[16,16,128]{2,1,0:T(8,128)(2,1)S(1)} %bitcast.44), channel_id=1, source_target_pairs={{0,1},{1,0},{2,3},{3,2},{4,5},{5,4},{6,7},{7,6},{8,9},{9,8},{10,11... | collective-permute-start | bytes 196616 | tf_op jit(solution)/shard_map/ppermute | solution.py:45
  8.0 0.0 collective-permute-start.2
  8.0 3.1 %shard_map.83 = (f32[8,16,16,128]{3,2,1,0:T(8,128)S(1)}, bf16[1152,384]{1,0:T(8,128)(2,1)S(1)}, bf16[1536,256]{1,0:T(8,128)(2,1)S(1)}, bf16[27,16,128]{2,1,0:T(8,128)(2,1)S(1)}) custom-call(s32[6]{0:T(128)S(1)} %stack.53.pos._, bf16[16,16,16,128]{3,2,1,0:T(8,128)(2,1)S(1)} %get-tuple-element.36.x.refs_0_, ...), custom_call_target="tpu_custom_call" | custom-call | flops 1811939328 | bytes 3145728 | tf_op jit(solution)/shard_map/pallas_call | solution.py:89
  11.1 2.3 %collective-permute-done.2 = bf16[16,128]{1,0:T(8,128)(2,1)S(1)} collective-permute-done((bf16[16,128]{1,0:T(8,128)(2,1)S(1)}, bf16[16,128]{1,0:T(8,128)(2,1)S(1)}, u32[]{:S(2)}, u32[]{:S(2)}) %collective-permute-start.2) | collective-permute-done | bytes 4128 | tf_op jit(solution)/shard_map/ppermute | solution.py:46
  13.4 0.0 collective-permute-done
  13.4 0.0 collective-permute-done.1
  13.4 0.6 shard_map.84
  14.0 1.3 %collective-permute-start.3 = (bf16[55,16,128]{2,1,0:T(8,128)(2,1)S(1)}, bf16[55,16,128]{2,1,0:T(8,128)(2,1)S(1)}, u32[]{:S(2)}, u32[]{:S(2)}) collective-permute-start(bf16[55,16,128]{2,1,0:T(8,128)(2,1)S(1)} %get-tuple-element.47), channel_id=1, source_target_pairs={{0,4},{4,8},{8,12},{1,5},{5,9},{9,13},{2,6},{6,10},{10,14},{3,7},{... | collective-permute-start | bytes 675848 | tf_op jit(solution)/shard_map/ppermute | solution.py:61
  15.3 1.3 %collective-permute-start.4 = (bf16[55,16,128]{2,1,0:T(8,128)(2,1)S(1)}, bf16[55,16,128]{2,1,0:T(8,128)(2,1)S(1)}, u32[]{:S(2)}, u32[]{:S(2)}) collective-permute-start(bf16[55,16,128]{2,1,0:T(8,128)(2,1)S(1)} %get-tuple-element.48), channel_id=1, source_target_pairs={{4,0},{8,4},{12,8},{5,1},{9,5},{13,9},{6,2},{10,6},{14,10},{7,3},{... | collective-permute-start | bytes 675848 | tf_op jit(solution)/shard_map/ppermute | solution.py:61
  16.6 0.1 collective-permute-start.5
  16.6 2.1 %collective-permute-start.6 = (bf16[27,16,128]{2,1,0:T(8,128)(2,1)S(1)}, bf16[27,16,128]{2,1,0:T(8,128)(2,1)S(1)}, u32[]{:S(2)}, u32[]{:S(2)}) collective-permute-start(bf16[27,16,128]{2,1,0:T(8,128)(2,1)S(1)} %get-tuple-element.53), channel_id=1, source_target_pairs={{0,2},{1,3},{2,0},{3,1},{4,6},{5,7},{6,4},{7,5},{8,10},{9,11},{10,... | collective-permute-start | bytes 331784 | tf_op jit(solution)/shard_map/ppermute | solution.py:71
  18.8 1.7 %collective-permute-start.7 = (bf16[27,16,128]{2,1,0:T(8,128)(2,1)S(1)}, bf16[27,16,128]{2,1,0:T(8,128)(2,1)S(1)}, u32[]{:S(2)}, u32[]{:S(2)}) collective-permute-start(bf16[27,16,128]{2,1,0:T(8,128)(2,1)S(1)} %get-tuple-element.53), channel_id=1, source_target_pairs={{0,3},{1,0},{2,1},{3,2},{4,7},{5,4},{6,5},{7,6},{8,11},{9,8},{10,9... | collective-permute-start | bytes 331784 | tf_op jit(solution)/shard_map/ppermute | solution.py:71
  20.4 0.0 collective-permute-done.3.refs_5_
  20.4 0.0 collective-permute-done.4.refs_6_
  20.5 5.2 %shard_map.85 = (f32[20,16,16,128]{3,2,1,0:T(8,128)S(1)}, f32[16,2,128]{2,1,0:T(2,128)S(1)}) custom-call(s32[6]{0:T(128)S(1)} %stack.53.pos._, bf16[16,16,16,128]{3,2,1,0:T(8,128)(2,1)S(1)} %get-tuple-element.36.x.refs_0_, f32[8,16,16,128]{3,2,1,0:T(8,128)S(1)} %get-tuple-element.39.refs_1_, bf16[1,16,16,128]{3,2,1,0:T(8,128)(2,1)S(1)} %bitcast.35, ...), custom_call_target="tpu_custom_call" | custom-call | tf_op jit(solution)/shard_map/pallas_call | solution.py:89
  25.7 0.0 copy-start.3
  25.7 0.0 copy-start.4
  25.7 0.0 collective-permute-done.5.refs_0_
  25.7 0.3 collective-permute-done.6.refs_1_
  26.0 0.5 collective-permute-done.7.refs_2_
  26.6 1.6 %collective-permute-start.8 = (bf16[1,3,27,16,128]{4,3,2,1,0:T(8,128)(2,1)S(1)}, bf16[1,3,27,16,128]{4,3,2,1,0:T(8,128)(2,1)S(1)}, u32[]{:S(2)}, u32[]{:S(2)}) collective-permute-start(bf16[1,3,27,16,128]{4,3,2,1,0:T(8,128)(2,1)S(1)} %bitcast.32), channel_id=1, source_target_pairs={{0,16},{16,0},{1,17},{17,1},{2,18},{18,2},{3,19},{19,3},{4,20},{20... | collective-permute-start | bytes 995336 | tf_op jit(solution)/shard_map/ppermute | solution.py:76
  28.2 14.0 %all_to_all.10.stats = f32[16,2,128]{2,1,0:T(2,128)S(1)} all-to-all(f32[16,2,128]{2,1,0:T(2,128)S(1)} %get-tuple-element.54), channel_id=1, replica_groups=mesh['cand'=2,'gz'=4,'yx'=4] {'gz','yx'}, dimensions={0} | all-to-all | bytes 32768 | tf_op jit(solution)/shard_map/all_to_all | solution.py:80
  42.1 0.0 collective-permute-done.8.refs_1_
  42.2 0.2 collective-permute-start.12
  42.4 0.0 copy-done.3
  42.4 0.0 copy-done.4
  42.4 1.8 %shard_map.87 = (bf16[16,16,16,128]{3,2,1,0:T(8,128)(2,1)S(1)}, f32[10,8,8,128]{3,2,1,0:T(8,128)S(1)}, bf16[1,80,128]{2,1,0:T(8,128)(2,1)S(1)}, bf16[1,80,128]{2,1,0:T(8,128)(2,1)S(1)}, f32[1,16,128]{2,1,0:T(8,128)S(1)}) custom-call(s32[6]{0:T(128)S(1)} %stack.53.pos._, f32[20,16,16,128]{3,2,1,0:T(8,128)S(1)} %get-tuple-element.51.act, ...), custom_call_target="tpu_custom_call" | custom-call | flops 10485760 | bytes 3145728 | tf_op jit(solution)/shard_map/pallas_call | solution.py:89
  44.2 0.7 %collective-permute-start.9 = (bf16[80,128]{1,0:T(8,128)(2,1)S(1)}, bf16[80,128]{1,0:T(8,128)(2,1)S(1)}, u32[]{:S(2)}, u32[]{:S(2)}) collective-permute-start(bf16[80,128]{1,0:T(8,128)(2,1)S(1)} %bitcast.48), channel_id=1, source_target_pairs={{0,2},{1,3},{2,0},{3,1},{4,6},{5,7},{6,4},{7,5},{8,10},{9,11},{10,... | collective-permute-start | bytes 61448 | tf_op jit(solution)/shard_map/ppermute | solution.py:44
  44.9 0.6 collective-permute-start.10
  45.4 3.3 %collective-permute-start.11 = (f32[16,128]{1,0:T(8,128)S(1)}, f32[16,128]{1,0:T(8,128)S(1)}, u32[]{:S(2)}, u32[]{:S(2)}) collective-permute-start(f32[16,128]{1,0:T(8,128)S(1)} %bitcast.50), channel_id=1, source_target_pairs={{0,3},{1,2},{2,1},{3,0},{4,7},{5,6},{6,5},{7,4},{8,11},{9,10},{10,... | collective-permute-start | bytes 24584 | tf_op jit(solution)/shard_map/ppermute | solution.py:46
  48.7 0.0 collective-permute-done.12.refs_1_
  48.7 0.1 shard_map.89
  48.8 0.8 %shard_map.90.kernel = bf16[3,256,1152]{2,1,0:T(8,128)(2,1)S(1)} custom-call(s32[6]{0:T(128)S(1)} %stack.53.pos._, bf16[27,64,128]{2,1,0:T(8,128)(2,1)S(1)} %get-tuple-element.38.deep_weight.own, bf16[4,3,27,16,128]{4,3,2,1,0:T(8,128)(2,1)S(1)} %bitcast.29), custom_call_target="tpu_custom_call" | custom-call | bytes 4194304 | tf_op jit(solution)/shard_map/pallas_call | solution.py:89
  49.6 0.0 copy-start
  49.6 0.0 copy-start.1
  49.6 0.0 copy-start.2
  49.7 1.2 %collective-permute-done.11 = f32[16,128]{1,0:T(8,128)S(1)} collective-permute-done((f32[16,128]{1,0:T(8,128)S(1)}, f32[16,128]{1,0:T(8,128)S(1)}, u32[]{:S(2)}, u32[]{:S(2)}) %collective-permute-start.11) | collective-permute-done | bytes 8224 | tf_op jit(solution)/shard_map/ppermute | solution.py:46
  50.9 0.0 collective-permute-done.9
  50.9 0.0 collective-permute-done.10
  50.9 1.9 %shard_map.91 = (f32[512,256]{1,0:T(8,128)S(1)}, f32[16,2,256]{2,1,0:T(2,128)S(1)}) custom-call(s32[6]{0:T(128)S(1)} %stack.53.pos._, f32[10,8,8,128]{3,2,1,0:T(8,128)S(1)} %get-tuple-element.59.pooled, bf16[1,80,128]{2,1,0:T(8,128)(2,1)S(1)} %bitcast.47, bf16[1,80,128]{2,1,0:T(8,128)(2,1)S(1)} %bitcast.49, f32[1,16,128]{2,1,0:T(8,128)S(1)} %bitcast.51, ...), custom_call_target="tpu_custom_call" | custom-call | flops 905969664 | bytes 4194304 | tf_op jit(solution)/shard_map/pallas_call | solution.py:89
  52.8 10.9 %all_to_all.11.stats = f32[16,2,256]{2,1,0:T(2,128)S(1)} all-to-all(f32[16,2,256]{2,1,0:T(2,128)S(1)} %get-tuple-element.65), channel_id=1, replica_groups=mesh['cand'=2,'gz'=4,'yx'=4] {'gz','yx'}, dimensions={0} | all-to-all | bytes 65536 | tf_op jit(solution)/shard_map/all_to_all | solution.py:80
  63.8 0.0 copy-done
  63.8 0.0 copy-done.1
  63.8 0.0 copy-done.2
  63.8 2.3 %shard_map.92 = bf16[16,16,16,128]{3,2,1,0:T(8,128)(2,1)} custom-call(s32[6]{0:T(128)S(1)} %stack.53.pos._, f32[512,256]{1,0:T(8,128)S(1)} %get-tuple-element.64.act, f32[16,2,256]{2,1,0:T(2,128)S(1)} %all_to_all.11.stats, f32[1,256]{1,0:T(1,128)S(1)} %bitcast.40, f32[1,256]{1,0:T(1,128)S(1)} %bitcast.41, bf16[256,128]{1,0:T(8,128)(2,1)S(1)} %copy-done, ...), custom_call_target="tpu_custom_call" | custom-call | flops 67108864 | bytes 3145728 | tf_op jit(solution)/shard_map/pallas_call | solution.py:89
  (2 shorter events, 0.1 us)
Async XLA Ops:
  2.3 11.1 %collective-permute-start = (bf16[16,16,128]{2,1,0:T(8,128)(2,1)S(1)}, bf16[16,16,128]{2,1,0:T(8,128)(2,1)S(1)}, u32[]{:S(2)}, u32[]{:S(2)}) collective-permute-start(bf16[16,16,128]{2,1,0:T(8,128)(2,1)S(1)} %bitcast.45), channel_id=1, source_target_pairs={{0,2},{1,3},{2,0},{3,1},{4,6},{5,7},{6,4},{7,5},{8,10},{9,11},{10,... | collective-permute-start | bytes 196616 | tf_op jit(solution)/shard_map/ppermute | solution.py:44
  6.4 7.0 %collective-permute-start.1 = (bf16[16,16,128]{2,1,0:T(8,128)(2,1)S(1)}, bf16[16,16,128]{2,1,0:T(8,128)(2,1)S(1)}, u32[]{:S(2)}, u32[]{:S(2)}) collective-permute-start(bf16[16,16,128]{2,1,0:T(8,128)(2,1)S(1)} %bitcast.44), channel_id=1, source_target_pairs={{0,1},{1,0},{2,3},{3,2},{4,5},{5,4},{6,7},{7,6},{8,9},{9,8},{10,11... | collective-permute-start | bytes 196616 | tf_op jit(solution)/shard_map/ppermute | solution.py:45
  8.0 5.4 %collective-permute-start.2 = (bf16[16,128]{1,0:T(8,128)(2,1)S(1)}, bf16[16,128]{1,0:T(8,128)(2,1)S(1)}, u32[]{:S(2)}, u32[]{:S(2)}) collective-permute-start(bf16[16,128]{1,0:T(8,128)(2,1)S(1)} %bitcast.52), channel_id=1, source_target_pairs={{0,3},{1,2},{2,1},{3,0},{4,7},{5,6},{6,5},{7,4},{8,11},{9,10},{10,... | collective-permute-start | bytes 12296 | tf_op jit(solution)/shard_map/ppermute | solution.py:46
  14.0 6.5 %collective-permute-start.3 = (bf16[55,16,128]{2,1,0:T(8,128)(2,1)S(1)}, bf16[55,16,128]{2,1,0:T(8,128)(2,1)S(1)}, u32[]{:S(2)}, u32[]{:S(2)}) collective-permute-start(bf16[55,16,128]{2,1,0:T(8,128)(2,1)S(1)} %get-tuple-element.47), channel_id=1, source_target_pairs={{0,4},{4,8},{8,12},{1,5},{5,9},{9,13},{2,6},{6,10},{10,14},{3,7},{... | collective-permute-start | bytes 675848 | tf_op jit(solution)/shard_map/ppermute | solution.py:61
  15.3 5.2 %collective-permute-start.4 = (bf16[55,16,128]{2,1,0:T(8,128)(2,1)S(1)}, bf16[55,16,128]{2,1,0:T(8,128)(2,1)S(1)}, u32[]{:S(2)}, u32[]{:S(2)}) collective-permute-start(bf16[55,16,128]{2,1,0:T(8,128)(2,1)S(1)} %get-tuple-element.48), channel_id=1, source_target_pairs={{4,0},{8,4},{12,8},{5,1},{9,5},{13,9},{6,2},{10,6},{14,10},{7,3},{... | collective-permute-start | bytes 675848 | tf_op jit(solution)/shard_map/ppermute | solution.py:61
  16.6 9.2 %collective-permute-start.5 = (bf16[27,16,128]{2,1,0:T(8,128)(2,1)S(1)}, bf16[27,16,128]{2,1,0:T(8,128)(2,1)S(1)}, u32[]{:S(2)}, u32[]{:S(2)}) collective-permute-start(bf16[27,16,128]{2,1,0:T(8,128)(2,1)S(1)} %get-tuple-element.53), channel_id=1, source_target_pairs={{0,1},{1,2},{2,3},{3,0},{4,5},{5,6},{6,7},{7,4},{8,9},{9,10},{10,1... | collective-permute-start | bytes 331784 | tf_op jit(solution)/shard_map/ppermute | solution.py:71
  16.6 9.4 %collective-permute-start.6 = (bf16[27,16,128]{2,1,0:T(8,128)(2,1)S(1)}, bf16[27,16,128]{2,1,0:T(8,128)(2,1)S(1)}, u32[]{:S(2)}, u32[]{:S(2)}) collective-permute-start(bf16[27,16,128]{2,1,0:T(8,128)(2,1)S(1)} %get-tuple-element.53), channel_id=1, source_target_pairs={{0,2},{1,3},{2,0},{3,1},{4,6},{5,7},{6,4},{7,5},{8,10},{9,11},{10,... | collective-permute-start | bytes 331784 | tf_op jit(solution)/shard_map/ppermute | solution.py:71
  18.8 7.8 %collective-permute-start.7 = (bf16[27,16,128]{2,1,0:T(8,128)(2,1)S(1)}, bf16[27,16,128]{2,1,0:T(8,128)(2,1)S(1)}, u32[]{:S(2)}, u32[]{:S(2)}) collective-permute-start(bf16[27,16,128]{2,1,0:T(8,128)(2,1)S(1)} %get-tuple-element.53), channel_id=1, source_target_pairs={{0,3},{1,0},{2,1},{3,2},{4,7},{5,4},{6,5},{7,6},{8,11},{9,8},{10,9... | collective-permute-start | bytes 331784 | tf_op jit(solution)/shard_map/ppermute | solution.py:71
  25.7 16.7 %copy-start.3 = (f32[128]{0:T(128)S(1)}, f32[128]{0:T(128)}, u32[]{:S(2)}) copy-start(f32[128]{0:T(128)} %param.10) | copy-start | bytes 1540
  25.7 16.7 %copy-start.4 = (f32[128]{0:T(128)S(1)}, f32[128]{0:T(128)}, u32[]{:S(2)}) copy-start(f32[128]{0:T(128)} %param.11) | copy-start | bytes 1540
  26.6 15.6 %collective-permute-start.8 = (bf16[1,3,27,16,128]{4,3,2,1,0:T(8,128)(2,1)S(1)}, bf16[1,3,27,16,128]{4,3,2,1,0:T(8,128)(2,1)S(1)}, u32[]{:S(2)}, u32[]{:S(2)}) collective-permute-start(bf16[1,3,27,16,128]{4,3,2,1,0:T(8,128)(2,1)S(1)} %bitcast.32), channel_id=1, source_target_pairs={{0,16},{16,0},{1,17},{17,1},{2,18},{18,2},{3,19},{19,3},{4,20},{20... | collective-permute-start | bytes 995336 | tf_op jit(solution)/shard_map/ppermute | solution.py:76
  42.2 6.5 %collective-permute-start.12 = (bf16[2,3,27,16,128]{4,3,2,1,0:T(8,128)(2,1)S(1)}, bf16[2,3,27,16,128]{4,3,2,1,0:T(8,128)(2,1)S(1)}, u32[]{:S(2)}, u32[]{:S(2)}) collective-permute-start(bf16[2,3,27,16,128]{4,3,2,1,0:T(8,128)(2,1)S(1)} %bitcast.30), channel_id=1, source_target_pairs={{0,4},{4,0},{8,12},{12,8},{1,5},{5,1},{9,13},{13,9},{2,6},{6,2},{1... | collective-permute-start | bytes 1990664 | tf_op jit(solution)/shard_map/ppermute | solution.py:76
  44.2 6.7 %collective-permute-start.9 = (bf16[80,128]{1,0:T(8,128)(2,1)S(1)}, bf16[80,128]{1,0:T(8,128)(2,1)S(1)}, u32[]{:S(2)}, u32[]{:S(2)}) collective-permute-start(bf16[80,128]{1,0:T(8,128)(2,1)S(1)} %bitcast.48), channel_id=1, source_target_pairs={{0,2},{1,3},{2,0},{3,1},{4,6},{5,7},{6,4},{7,5},{8,10},{9,11},{10,... | collective-permute-start | bytes 61448 | tf_op jit(solution)/shard_map/ppermute | solution.py:44
  44.9 6.0 %collective-permute-start.10 = (bf16[80,128]{1,0:T(8,128)(2,1)S(1)}, bf16[80,128]{1,0:T(8,128)(2,1)S(1)}, u32[]{:S(2)}, u32[]{:S(2)}) collective-permute-start(bf16[80,128]{1,0:T(8,128)(2,1)S(1)} %bitcast.46), channel_id=1, source_target_pairs={{0,1},{1,0},{2,3},{3,2},{4,5},{5,4},{6,7},{7,6},{8,9},{9,8},{10,11... | collective-permute-start | bytes 61448 | tf_op jit(solution)/shard_map/ppermute | solution.py:45
  45.4 5.4 %collective-permute-start.11 = (f32[16,128]{1,0:T(8,128)S(1)}, f32[16,128]{1,0:T(8,128)S(1)}, u32[]{:S(2)}, u32[]{:S(2)}) collective-permute-start(f32[16,128]{1,0:T(8,128)S(1)} %bitcast.50), channel_id=1, source_target_pairs={{0,3},{1,2},{2,1},{3,0},{4,7},{5,6},{6,5},{7,4},{8,11},{9,10},{10,... | collective-permute-start | bytes 24584 | tf_op jit(solution)/shard_map/ppermute | solution.py:46
  49.6 14.1 %copy-start = (bf16[256,128]{1,0:T(8,128)(2,1)S(1)}, bf16[256,128]{1,0:T(8,128)(2,1)}, u32[]{:S(2)}) copy-start(bf16[256,128]{1,0:T(8,128)(2,1)} %up.1) | copy-start | bytes 196612
  49.6 14.1 %copy-start.1 = (f32[256]{0:T(256)S(1)}, f32[256]{0:T(256)}, u32[]{:S(2)}) copy-start(f32[256]{0:T(256)} %param.13) | copy-start | bytes 3076
  49.6 14.1 %copy-start.2 = (f32[256]{0:T(256)S(1)}, f32[256]{0:T(256)}, u32[]{:S(2)}) copy-start(f32[256]{0:T(256)} %param.14) | copy-start | bytes 3076

commit v7 on v6

--- a/solution.py
+++ b/solution.py
@@ -61,8 +61,21 @@
     return lax.ppermute(high, "gz", up), lax.ppermute(low, "gz", [(j, i) for i, j in up])
 
 
-def split_axes(rows):
-    return ("cand", "gz")[: 2 if rows % 64 == 0 else 0]
+class Riders:
+    STEPS = (("cand", 1), ("gz", 2), ("gz", 1))
+
+    def __init__(self, rows):
+        self.tiles = 27 * rows // 16
+        self.fits = (
+            lax.axis_size("yx") == 4
+            and lax.axis_size("cand") % 2 == 0
+            and lax.axis_size("gz") % 4 == 0
+            and self.tiles >= 8
+        )
+        self.size = -(-self.tiles // 8) if self.fits else 0
+        self.mine = sum(
+            lax.axis_index(axis) // mask % 2 * 2**k for k, (axis, mask) in enumerate(self.STEPS)
+        )
 
 
 def rotate_shards(piece):
@@ -80,74 +93,97 @@
     return lax.all_to_all(stats, PART, 0, 0)
 
 
-def call(kernel, outs, scratch, scalars, *arrays, flops=0, nbytes=0, in_hbm=False, out_hbm=False):
+def call(kernel, outs, scratch, scalars, *arrays, flops=0, nbytes=0, in_hbm=0, out_hbm=False):
     smem, vmem, hbm = (
         pl.BlockSpec(memory_space=space) for space in (pltpu.SMEM, pltpu.VMEM, pltpu.HBM)
     )
-    if in_hbm:
-        arrays = [pltpu.with_memory_space_constraint(array, pltpu.HBM) for array in arrays]
+    far, near = arrays[:in_hbm], arrays[in_hbm:]
+    far = [pltpu.with_memory_space_constraint(array, pltpu.HBM) for array in far]
     return pl.pallas_call(
         kernel,
         out_shape=[jax.ShapeDtypeStruct(shape, dtype) for shape, dtype in outs],
-        in_specs=[smem] + [hbm if in_hbm else vmem] * len(arrays),
+        in_specs=[smem] + [hbm] * len(far) + [vmem] * len(near),
         out_specs=[hbm if out_hbm else vmem] * len(outs),
         scratch_shapes=[pltpu.VMEM(*entry) if isinstance(entry, tuple) else entry for entry in scratch],
         compiler_params=pltpu.CompilerParams(vmem_limit_bytes=VMEM_BYTES),
         cost_estimate=pl.CostEstimate(flops=flops, bytes_accessed=nbytes, transcendentals=0),
-    )(scalars, *arrays)
-
-
-def start_kernel(ny, nx, pos, x_in, w_in, d_in, y_edges, x_edges, corners, x, w, d, lines, sems):
-    edge = x.shape[0]
-    size = edge // 4
+    )(scalars, *far, *near)
+
+
+def start_kernel(ny, nx, size, pos, x_in, w_in, d_in, y_out, x_out, corners, x, w, lines, sems):
+    edge = x_in.shape[0]
+    f32, bf16 = jnp.float32, jnp.bfloat16
+    chunks = 4
+    planes = edge // chunks
     first = [
-        pltpu.make_async_copy(x_in.at[pl.ds(k * size, size)], x.at[pl.ds(k * size, size)], sems.at[k])
-        for k in range(4)
+        pltpu.make_async_copy(
+            x_in.at[pl.ds(k * planes, planes)],
+            x.at[pl.ds(1 + k * planes, planes), pl.ds(1, edge)],
+            sems.at[k],
+        )
+        for k in range(chunks)
     ]
-    later = [pltpu.make_async_copy(w_in, w, sems.at[4]), pltpu.make_async_copy(d_in, d, sems.at[5])]
+    later = [pltpu.make_async_copy(w_in, w, sems.at[chunks])]
+    if size:
+        at = jnp.minimum(pos[pos.shape[0] - 1] * size, d_in.shape[0] - size)
+        for k, (out, begin) in enumerate(((y_out, edge), (x_out, edge), (corners, 1))):
+            later.append(
+                pltpu.make_async_copy(
+                    d_in.at[pl.ds(at, size)], out.at[0, pl.ds(begin, size)], sems.at[chunks + 1 + k]
+                )
+            )
     for copy in first + later:
         copy.start()
-    for copy in first:
-        copy.wait()
-    f32, bf16 = jnp.float32, jnp.bfloat16
+    x[0] = jnp.zeros(x.shape[1:], bf16)
+    x[edge + 1] = jnp.zeros(x.shape[1:], bf16)
+    blank = jnp.zeros((edge,) + x.shape[2:], bf16)
+    x[1 : edge + 1, 0] = blank
+    x[1 : edge + 1, edge + 1] = blank
+    flat = lines.reshape(nx * edge * edge * 8, 128)
+    part = planes * edge
+    for k in range(chunks):
+        first[k].wait()
+        at, here = pl.ds(k * planes, planes), pl.ds(1 + k * planes, planes)
+        for i in range(ny):
+            row = jnp.where(pos[i] == 1, 1, edge) if ny == 1 else (1, edge)[i]
+            y_out[i, at] = x[here, row]
+        for j in range(nx):
+            low = x[here, 1 : edge + 1, 0:8].astype(f32).reshape(part, 8, 128)
+            high = x[here, 1 : edge + 1, edge - 8 : edge].astype(f32).reshape(part, 8, 128)
+            high = pltpu.roll(high, 1, 1)
+            kept = jnp.where(pos[ny] == 1, low, high) if nx == 1 else (low, high)[j]
+            lines[j, k * part : k * part + part] = kept
+            begin = (j * edge * edge + k * part) * 8
+            column = flat[pl.ds(begin, part, stride=8), :]
+            x_out[j, at] = column.astype(bf16).reshape(planes, edge, 128)
     for i in range(ny):
-        at = jnp.where(pos[i] == 1, 0, edge - 1) if ny == 1 else (0, edge - 1)[i]
-        y_edges[i] = x[:, at]
-    flat = lines.reshape(edge * edge * 8, 128)
-    for j in range(nx):
-        first = x[:, :, 0:8].astype(f32)
-        last = x[:, :, edge - 8 : edge].astype(f32)
-        if nx == 1:
-            low = pos[ny] == 1
-            turned = pltpu.roll(last.reshape(edge * edge, 8, 128), 1, 1)
-            kept = jnp.where(low, first.reshape(edge * edge, 8, 128), turned)
-        else:
-            kept = (first, pltpu.roll(last.reshape(edge * edge, 8, 128), 1, 1))[j]
-        lines[...] = kept.reshape(edge * edge, 8, 128)
-        column = flat[pl.ds(0, edge * edge, stride=8), :]
-        x_edges[j] = column.astype(bf16).reshape(edge, edge, 128)
-        for i in range(ny):
-            first_y = flat[pl.ds(0, edge, stride=8 * edge), :]
-            last_y = flat[pl.ds(8 * (edge - 1), edge, stride=8 * edge), :]
-            kept = jnp.where(pos[i] == 1, first_y, last_y) if ny == 1 else (first_y, last_y)[i]
-            corners[i * nx + j] = kept.astype(bf16)
+        for j in range(nx):
+            begin = j * edge * edge * 8
+            low = flat[pl.ds(begin, edge, stride=8 * edge), :]
+            high = flat[pl.ds(begin + 8 * (edge - 1), edge, stride=8 * edge), :]
+            kept = jnp.where(pos[i] == 1, low, high) if ny == 1 else (low, high)[i]
+            corners[i * nx + j, 0] = kept.astype(bf16)
     for copy in later:
         copy.wait()
 
 
-def face_kernel(ny, nx, _, x, y_halos, x_halos, corners, low, high):
-    edge = x.shape[0]
+def face_kernel(ny, nx, size, _, x, y_halos, x_halos, corners, low, high, *riders):
+    edge = low.shape[1]
     wide = edge + ny + nx
     for face, at in ((low, 0), (high, edge - 3)):
         for k in range(3):
             row = k * wide
-            face[row : row + edge] = x[at + k]
+            face[row : row + edge] = x[1 + at + k, 1 : edge + 1]
             for i in range(ny):
                 face[row + edge + i] = y_halos[i, at + k]
             for j in range(nx):
                 face[row + edge + ny + j] = x_halos[j, at + k]
         for k in range(ny * nx):
-            face[3 * wide + k] = corners[k]
+            face[3 * wide + k] = corners[k, 0]
+    if size:
+        riders[0][0] = x_halos[0, edge : edge + size]
+        riders[0][1] = y_halos[0, edge : edge + size]
+        riders[0][2] = corners[0, 1 : 1 + size]
 
 
 def spread_taps(weight, taps):
@@ -212,57 +248,39 @@
         put(z, new.reshape(planes, edge, edge, 128))
 
 
-def clear_sides(grid):
-    blank = jnp.zeros(grid.shape[:1] + grid.shape[2:], grid.dtype)
-    grid[:, 0] = blank
-    grid[:, grid.shape[1] - 1] = blank
-
-
-def local_planes(x, lo, count, taps, pairs, grid, act):
-    edge = x.shape[0]
-    clear_sides(grid)
-    first, last = max(lo - 1, 0), min(lo + count + 1, edge)
-    if first > lo - 1:
-        grid[0] = jnp.zeros(grid.shape[1:], grid.dtype)
-    if last < lo + count + 1:
-        grid[count + 1] = jnp.zeros(grid.shape[1:], grid.dtype)
-    grid[first - lo + 1 : last - lo + 1, 1 : edge + 1] = x[first:last]
+def conv_kernel(_, x, weight, act, taps, pairs, sums):
+    edge = act.shape[0]
+    spread_taps(weight, taps)
+    pair_taps(weight, pairs)
+    totals = []
 
     def put(z, new):
         act[z : z + new.shape[0]] = new
-
-    convolve(grid, count, taps, pairs, put)
-
-
-def front_half_kernel(pos, x, weight, deep_weight, act, taps, pairs, piece, grid):
-    spread_taps(weight, taps)
-    pair_taps(weight, pairs)
-    size = piece.shape[1]
-    if size < deep_weight.shape[1]:
-        piece[...] = deep_weight[:, pl.ds(pl.multiple_of(pos[pos.shape[0] - 1] * size, size), size)]
-    else:
-        piece[...] = deep_weight[...]
-    local_planes(x, 0, act.shape[0], taps, pairs, grid, act)
+        totals.append(jnp.sum(new.reshape(-1, 8, 128), axis=0))
+
+    convolve(x, edge, taps, pairs, put)
+    sums[...] = functools.reduce(jnp.add, totals)
 
 
 def rim_kernel(ny, nx, pos, *refs):
-    x, near, y_halos, x_halos, corners, front, back, taps, pairs, act, stats, half_grid, grid, column, flanks = refs
-    edge = x.shape[0]
-    half = edge // 2
+    x, own, sums, y_halos, x_halos, corners, front, back, taps, pairs, act, stats, grid, column, flanks = refs
+    edge = own.shape[0]
     wide_face = edge + ny + nx
     depth = edge + 4
     f32, bf16 = jnp.float32, jnp.bfloat16
-    act[2 : 2 + half] = near[...]
-    local_planes(x, half, half, taps, pairs, half_grid, act.at[2 + half : 2 + edge])
-
-    clear_sides(grid)
-    for face, halo_at, own_at, own, out_at, touched, dz in (
+    total = sums[...]
+    act[2 : 2 + edge] = own[...]
+
+    blank = jnp.zeros(grid.shape[:1] + grid.shape[2:], grid.dtype)
+    grid[:, 0] = blank
+    grid[:, edge + 1] = blank
+    for face, halo_at, own_at, plane, out_at, touched, dz in (
         (front, 0, 3, 0, 0, 2, 0),
         (back, 1, 0, edge - 1, depth - 2, depth - 3, 2),
     ):
         for k in range(3):
             grid[halo_at + k, 1 : edge + 1] = face[k * wide_face : k * wide_face + edge]
-        grid[own_at, 1 : edge + 1] = x[own]
+        grid[own_at, 1 : edge + 1] = x[1 + plane, 1 : edge + 1]
 
         def put(z, new):
             act[out_at + z : out_at + z + new.shape[0]] = new
@@ -273,14 +291,16 @@
             [grid[beside, dy : dy + edge].reshape(edge * edge, 128) for dy in range(3)], axis=1
         )
         wide = jnp.dot(left, taps[dz * 384 : dz * 384 + 384, :], preferred_element_type=f32)
-        act[touched] += join_x(wide.reshape(edge, edge, 384), edge)
+        new = join_x(wide.reshape(edge, edge, 384), edge)
+        total = total + jnp.sum(new.reshape(-1, 8, 128), axis=0)
+        act[touched] += new
 
     def rim(face, row):
         return jnp.stack([face[k * wide_face + edge + row] for k in range(3)])
 
     for i in range(ny):
         low = pos[i] == 1
-        line = jnp.concatenate([rim(front, i), y_halos[i], rim(back, i)], axis=0)
+        line = jnp.concatenate([rim(front, i), y_halos[i, 0:edge], rim(back, i)], axis=0)
         left = jnp.concatenate(
             [line[dz : dz + depth].reshape(depth * edge, 128) for dz in range(3)], axis=1
         )
@@ -289,13 +309,15 @@
             [taps[pl.ds(pl.multiple_of(start + dz * 384, 128), 128), :] for dz in range(3)], axis=0
         )
         wide = jnp.dot(left, right, preferred_element_type=f32)
-        act[:, jnp.where(low, 0, edge - 1)] += join_x(wide.reshape(depth, edge, 384), edge)
+        new = join_x(wide.reshape(depth, edge, 384), edge)
+        total = total + jnp.sum(new[2 : 2 + edge].reshape(-1, 8, 128), axis=0)
+        act[:, jnp.where(low, 0, edge - 1)] += new
 
     flat = act.reshape(depth * edge * edge, 128)
     for j in range(nx):
         column[:, 0:8] = jnp.zeros((depth + 2, 8, 128), f32)
         column[:, 8 + edge :] = jnp.zeros((depth + 2, 8, 128), f32)
-        column[3 : edge + 3, 8 : 8 + edge] = x_halos[j].astype(f32)
+        column[3 : edge + 3, 8 : 8 + edge] = x_halos[j, 0:edge].astype(f32)
         column[0:3, 8 : 8 + edge] = rim(front, ny + j).astype(f32)
         column[edge + 3 :, 8 : 8 + edge] = rim(back, ny + j).astype(f32)
         rows = edge + 16
@@ -305,7 +327,7 @@
             low = pos[i] == 1
             for at, count, ends in (
                 (0, 3, front[3 * wide_face + k].astype(f32)[edge - 3 :]),
-                (3, edge, corners[k].astype(f32)),
+                (3, edge, corners[k, 0].astype(f32)),
                 (edge + 3, 3, back[3 * wide_face + k].astype(f32)[:3]),
             ):
                 first, last = ends, ends
@@ -327,52 +349,59 @@
         first, last = extra[:, :128], extra[:, 128:]
         if nx == 1:
             first, last = jnp.where(low, first, 0.0), jnp.where(low, 0.0, last)
+        line = lax.broadcasted_iota(jnp.int32, (8, 128), 0)
+        inner = slice(2 * edge, 2 * edge + edge * edge)
         if nx == 1 or j == 0:
             flat[pl.ds(0, depth * edge, stride=edge), :] += first
+            total = total + jnp.where(line == 0, jnp.sum(first[inner], axis=0, keepdims=True), 0.0)
         if nx == 1 or j == 1:
             flat[pl.ds(edge - 1, depth * edge, stride=edge), :] += last
-
-    def sum_step(k, carry):
-        return carry + jnp.sum(act[k].reshape(edge * 2, 8, 128), axis=0)
-
-    total = lax.fori_loop(2, edge + 2, sum_step, jnp.zeros((8, 128), f32), unroll=4)
-    mean = jnp.sum(total, axis=0, keepdims=True) / edge**3
+            total = total + jnp.where(line == 7, jnp.sum(last[inner], axis=0, keepdims=True), 0.0)
+
+    rows = edge**3 // 8
+    mean = total / rows
 
     def spread_step(k, carry):
         off = act[k].reshape(edge * 2, 8, 128) - mean
         return carry + jnp.sum(off * off, axis=0)
 
-    total = lax.fori_loop(2, edge + 2, spread_step, jnp.zeros((8, 128), f32), unroll=4)
-    put_stats(stats, mean, jnp.sum(total, axis=0, keepdims=True))
-
-
-def put_stats(stats, mean, spread):
-    both = jnp.concatenate([mean, spread], axis=0)
+    spread = lax.fori_loop(2, edge + 2, spread_step, jnp.zeros((8, 128), f32), unroll=4)
+    put_stats(stats, mean, spread, rows)
+
+
+def merge(mean, spread, rows, other_mean, other_spread):
+    off = mean - other_mean
+    return 0.5 * (mean + other_mean), spread + other_spread + (0.5 * rows) * (off * off)
+
+
+def put_stats(stats, mean, spread, rows):
+    for step in (1, 2, 4):
+        others = pltpu.roll(mean, step, 0), pltpu.roll(spread, step, 0)
+        mean, spread = merge(mean, spread, float(rows * step), *others)
+    both = jnp.concatenate([mean[0:1], spread[0:1]], axis=0)
     stats[...] = jnp.broadcast_to(both[None], stats.shape)
-
-
-def group_sums(row, width):
-    lane = lax.broadcasted_iota(jnp.int32, row.shape, 1)
-    size, step = row.shape[1], 1
-    while step < width:
-        above, below = pltpu.roll(row, size - step, 1), pltpu.roll(row, step, 1)
-        row = row + jnp.where(jnp.bitwise_and(lane, step) == 0, above, below)
-        step *= 2
-    return row
 
 
 def read_stats(stats, rows):
     devices, _, channels = stats.shape
-    width = channels // GROUPS
-    means, spreads = stats[:, 0, :], stats[:, 1, :]
-
-    def grouped(row):
-        return group_sums(jnp.broadcast_to(row, (8, channels)), width)[0:1]
-
-    mean = grouped(jnp.sum(means, axis=0, keepdims=True)) / (devices * width)
-    off = means - mean
-    total = grouped(jnp.sum(spreads + rows * (off * off), axis=0, keepdims=True))
-    return mean, lax.rsqrt(total / (rows * devices * width) + EPSILON)
+    shape = (8, channels)
+    means = [jnp.broadcast_to(stats[k, 0:1, :], shape) for k in range(devices)]
+    spreads = [jnp.broadcast_to(stats[k, 1:2, :], shape) for k in range(devices)]
+    mean = functools.reduce(jnp.add, means) / devices
+    spread = functools.reduce(jnp.add, spreads)
+    spread = spread + rows * functools.reduce(jnp.add, [(m - mean) * (m - mean) for m in means])
+    rows = rows * devices
+    lane = lax.broadcasted_iota(jnp.int32, shape, 1)
+    step = 1
+    while step < channels // GROUPS:
+        low = jnp.bitwise_and(lane, step) == 0
+        others = [
+            jnp.where(low, pltpu.roll(row, channels - step, 1), pltpu.roll(row, step, 1))
+            for row in (mean, spread)
+        ]
+        mean, spread = merge(mean, spread, rows, *others)
+        rows, step = 2.0 * rows, 2 * step
+    return mean, lax.rsqrt(spread / rows + EPSILON)
 
 
 def silu_of_double(h):
@@ -388,7 +417,9 @@
     scale = scale * (0.5 * gain[...])
     shift = 0.5 * offset[...]
     for k in range(deep_depth):
-        value = silu_of_double((act[2 * k : 2 * k + 2] - mean) * scale + shift).astype(bf16)
+        value = act[2 * k : 2 * k + 2].reshape(edge * edge // 4, 8, 128)
+        value = silu_of_double((value - mean) * scale + shift)
+        value = value.reshape(2, edge, edge, 128).astype(bf16)
         if 0 < k < deep_depth - 1:
             out[2 * k - 2 : 2 * k] = value
         value = value.astype(f32)
@@ -441,21 +472,21 @@
     )(*arrays)
 
 
-def place_kernel(tiles, pos, own, held, kernel):
-    shard, part = own.shape[1], held.shape[3]
+def place_kernel(pos, own, *refs):
+    *held, out, sem = refs
     tile, mine = pos[pos.shape[0] - 2], pos[pos.shape[0] - 1]
-
-    def place(rows, at):
-        for tap in range(27):
-            lane = tap % 9 * 128
-            kernel[tap // 9, pl.ds(at, rows.shape[1]), lane : lane + 128] = rows[tap]
-
-    place(own, pl.multiple_of(tile * shard, shard))
-    for piece in range(held.shape[0]):
-        at = jnp.bitwise_xor(mine, piece) * part
-        for k in range(1, tiles):
-            base = lax.rem(tile + tiles - k, tiles) * shard
-            place(held.at[piece, k - 1], pl.multiple_of(base + at, part))
+    copy = pltpu.make_async_copy(own, out.at[tile], sem)
+    copy.start()
+    if len(held) == 1:
+        pieces, others, size = held[0].shape[:3]
+        for piece in range(pieces):
+            at = jnp.minimum(jnp.bitwise_xor(mine, piece) * size, own.shape[0] - size)
+            for k in range(others):
+                out[jnp.bitwise_xor(tile, k + 1), pl.ds(at, size)] = held[0][piece, k]
+    else:
+        for k, shard in enumerate(held):
+            out[lax.rem(tile + len(held) - k, len(held) + 1)] = shard[...]
+    copy.wait()
 
 
 def deep_kernel(ny, nx, pos, pooled, y_halos, x_halos, corners, kernel, *refs):
@@ -505,14 +536,19 @@
             ],
             axis=1,
         )
+        right = jnp.concatenate(
+            [kernel[:, dz * 9 + tap].reshape(-1, 128) for tap in range(9)], axis=1
+        )
         term = lax.dot_general(
-            left, kernel[dz], (((1,), (1,)), ((), ())), preferred_element_type=f32
+            left, right, (((1,), (1,)), ((), ())), preferred_element_type=f32
         )
         total = term if total is None else total + term
     act[...] = total
-    mean = jnp.sum(total, axis=0, keepdims=True) / rows
+    total = total.reshape(rows // 8, 8, -1)
+    rows = rows // 8
+    mean = jnp.sum(total, axis=0) / rows
     off = total - mean
-    put_stats(stats, mean, jnp.sum(off * off, axis=0, keepdims=True))
+    put_stats(stats, mean, jnp.sum(off * off, axis=0), rows)
 
 
 def final_kernel(_, act, stats, gain, offset, up, mid, out, wide, held, sems):
@@ -526,8 +562,9 @@
     size = planes * deep * deep
     copies = []
     for k in range(0, deep, planes):
-        value = act[k * deep * deep : k * deep * deep + size]
-        value = silu_of_double((value - mean) * scale + shift).astype(jnp.bfloat16)
+        value = act[k * deep * deep : k * deep * deep + size].reshape(size // 8, 8, -1)
+        value = silu_of_double((value - mean) * scale + shift)
+        value = value.reshape(size, -1).astype(jnp.bfloat16)
         lifted = jnp.dot(value, up[...], preferred_element_type=f32)
         lines = wide.at[k // planes]
         lines[pl.ds(0, size, stride=2), :] = lifted
@@ -555,73 +592,80 @@
     devices = lax.axis_size("gz") * tiles
     y_low, x_low = square.low_sides()
     ny, nx = len(y_low), len(x_low)
-    axes = split_axes(deep_weight.shape[4])
-    mine = sum(lax.axis_index(axis) % 2 * 2**k for k, axis in enumerate(axes))
+    riders = Riders(deep_weight.shape[4])
     depth_at = lax.axis_index("gz")
     inside = [depth_at > 0, depth_at < lax.axis_size("gz") - 1]
-    pos = y_low + x_low + inside + [lax.axis_index("yx"), mine]
+    pos = y_low + x_low + inside + [lax.axis_index("yx"), riders.mine]
     pos = jnp.stack([jnp.asarray(v, jnp.int32) for v in pos])
 
-    own = jnp.moveaxis(deep_weight, 4, 3).reshape(27, deep_weight.shape[4], channels)
+    own = jnp.moveaxis(deep_weight, 4, 3).reshape(-1, 16, channels)
     conv_weight = conv_weight.reshape(27, channels, channels)
-    *edges, features, conv_weight, own = call(
-        functools.partial(start_kernel, ny, nx),
+    *edges, field, conv_weight = call(
+        functools.partial(start_kernel, ny, nx, riders.size),
         [
-            ((ny, edge, edge, channels), bf16),
-            ((nx, edge, edge, channels), bf16),
-            ((ny * nx, edge, channels), bf16),
-            (features.shape, bf16),
+            ((ny, edge + riders.size, edge, channels), bf16),
+            ((nx, edge + riders.size, edge, channels), bf16),
+            ((ny * nx, 1 + riders.size, edge, channels), bf16),
+            ((edge + 2, edge + 2, edge, channels), bf16),
             (conv_weight.shape, bf16),
-            (own.shape, bf16),
         ],
-        [((edge * edge, 8, channels), f32), pltpu.SemaphoreType.DMA((6,))],
+        [((nx, edge * edge, 8, channels), f32), pltpu.SemaphoreType.DMA((8,))],
         pos,
         features,
         conv_weight,
         own,
         nbytes=5 << 20,
-        in_hbm=True,
+        in_hbm=3,
     )
     halos = square.halos(*(list(piece) for piece in edges))
-    half_act = ((deep, edge, edge, channels), f32)
-    half_grid = ((deep + 2, edge + 2, edge, channels), bf16)
-    conv_flops = 27 * channels * channels * edge**3
-    near, taps, pairs, piece = call(
-        front_half_kernel,
+    conv_flops = 54 * channels * channels * edge**3
+    act, taps, pairs, sums = call(
+        conv_kernel,
         [
-            half_act,
+            ((edge, edge, edge, channels), f32),
             ((9 * channels, 3 * channels), bf16),
             ((12 * channels, 2 * channels), bf16),
-            ((27, own.shape[1] // 2 ** len(axes), channels), bf16),
+            ((8, channels), f32),
         ],
-        [half_grid],
+        [],
         pos,
-        features,
+        field,
         conv_weight,
-        own,
         flops=conv_flops,
-        nbytes=3 << 20,
-    )
-    piece, (y, x, corner) = lax.optimization_barrier((piece, halos))
+        nbytes=6 << 20,
+    )
+    (y, x, corner), act = lax.optimization_barrier((halos, act))
     y, x, corner = jnp.stack(y), jnp.stack(x), jnp.stack(corner)
     face = ((3 * (edge + ny + nx) + ny * nx, edge, channels), bf16)
-    faces = call(
-        functools.partial(face_kernel, ny, nx), [face, face], [], pos, features, y, x, corner
-    )
-    front, back = swap_depth(*faces)
-    got = rotate_shards(piece)
+    held = [((3, riders.size, 16, channels), bf16)] if riders.size else []
+    low, high, *held = call(
+        functools.partial(face_kernel, ny, nx, riders.size),
+        [face, face] + held,
+        [],
+        pos,
+        field,
+        y,
+        x,
+        corner,
+    )
+    front, back = swap_depth(low, high)
+    if riders.size:
+        held = held[0][None]
+        other = swap(held, *riders.STEPS[0])
+    else:
+        held = rotate_shards(own)
     act, stats = call(
         functools.partial(rim_kernel, ny, nx),
         [((edge + 4, edge, edge, channels), f32), ((devices, 2, channels), f32)],
         [
-            half_grid,
             ((4, edge + 2, edge, channels), bf16),
             ((edge + 6, edge + 16, channels), f32),
             ((edge + 6, edge, 3 * channels), bf16),
         ],
         pos,
-        features,
-        near,
+        field,
+        act,
+        sums,
         y,
         x,
         corner,
@@ -629,16 +673,20 @@
         back,
         taps,
         pairs,
-    )
-    stats, *got = lax.optimization_barrier((stats, *got))
-    stats = share(stats)
-    held = stack(*got)[None]
-    for axis in axes:
-        other = swap(held, axis, 1)
-        if axis == "cand":
-            stats, other = lax.optimization_barrier((stats, other))
-        held = stack(held, other)
-        held = held.reshape((-1,) + held.shape[2:])
+        flops=conv_flops // 2,
+        nbytes=6 << 20,
+    )
+    if riders.size:
+        stats, other = lax.optimization_barrier((stats, other))
+        held = stack(held, other).reshape((-1,) + held.shape[1:])
+        other = swap(held, *riders.STEPS[1])
+        stats = share(stats)
+        stats, other = lax.optimization_barrier((stats, other))
+        held = stack(held, other).reshape((-1,) + held.shape[1:])
+        other = swap(held, *riders.STEPS[2])
+        held = [stack(held, other).reshape((-1,) + held.shape[1:])]
+    else:
+        stats = share(stats)
     out, pooled, *edges = call(
         functools.partial(norm_kernel, ny, nx),
         [
@@ -659,14 +707,16 @@
     )
     y, x, corner = square.halos(*(list(piece) for piece in edges))
     (kernel,) = call(
-        functools.partial(place_kernel, tiles),
-        [((3, deep_channels, 9 * channels), bf16)],
-        [],
+        place_kernel,
+        [((tiles,) + own.shape, bf16)],
+        [pltpu.SemaphoreType.DMA],
         pos,
         own,
-        held,
+        *held,
         nbytes=4 << 20,
-    )
+        in_hbm=1,
+    )
+    kernel = kernel.reshape(tiles, 27, deep_weight.shape[4], channels)
     deep_act, stats = call(
         functools.partial(deep_kernel, ny, nx),
         [((deep**3, deep_channels), f32), ((devices, 2, deep_channels), f32)],

time: 66.3 us -> 64.4 us (0.971)
  blocking collectives: 24.9 us -> 22.3 us
    ppermute x2 -> x3, starting transfers between devices: 1.77 us -> 5.97 us  [swap(): lax.ppermute(block, axis, [(i, i ^ mask) for i in range(lax.axis_size(axi...]
    ppermute x3 -> x0, starting transfers between devices: 3.87 us -> none  [rotate_shards(): lax.ppermute(piece, 'yx', [(i, (i + k) % tiles) for i in range(tiles)])]
    all_to_all x2, blocking collectives: 24.9 us -> 22.3 us  [share(): return lax.all_to_all(stats, PART, 0, 0)]
    ppermute x1, waiting for transfers between devices: 0.01 us -> 2.2 us  [swap_depth(): lax.ppermute(low, 'gz', [(j, i) for i, j in up])]
    ppermute x2, waiting for transfers between devices: 3.47 us -> 2.12 us  [halos(): corner = lax.ppermute(corners[0], 'yx', self.swap_route(3))]
    ppermute x3 -> x0, waiting for transfers between devices: 0.84 us -> none  [rotate_shards(): lax.ppermute(piece, 'yx', [(i, (i + k) % tiles) for i in range(tiles)])]
  transfers between devices with their start and end apart: 13 -> 11, of which waited for: 4 -> 3; matrix products, arithmetic and copies ran while one was open for 0% -> 0% of each run, Pallas kernels for 17% -> 18%
where the time goes in v7:
time: 64.4 us; the launch traced here: 64.1 us
  blocking collectives  22.3 us (35%)
  starting transfers between devices  18.7 us (29%)
  Pallas kernels  18.4 us (29%)
  waiting for transfers between devices  4.34 us (7%)
    all_to_all x2, blocking collectives, share(): return lax.all_to_all(stats, PART, 0, 0)  22.3 us
    pallas_call x8, Pallas kernels, call(): pl.pallas_call(kernel, out_shape=[jax.ShapeDtypeStruct(shape, dtype) for...  18.2 us
    ppermute x3, starting transfers between devices, swap(): lax.ppermute(block, axis, [(i, i ^ mask) for i in range(lax.axis_size(axi...  5.97 us
    ppermute x2, starting transfers between devices, halos(): y = lax.ppermute(y_edges[0], 'yx', self.swap_route(2))  4.77 us
    ppermute x2, starting transfers between devices, halos(): corner = lax.ppermute(corners[0], 'yx', self.swap_route(3))  3.26 us
    ppermute x1, waiting for transfers between devices, swap_depth(): lax.ppermute(low, 'gz', [(j, i) for i, j in up])  2.2 us
    ppermute x2, starting transfers between devices, halos(): x = lax.ppermute(x_edges[0], 'yx', self.swap_route(1))  2.13 us
    ppermute x2, waiting for transfers between devices, halos(): corner = lax.ppermute(corners[0], 'yx', self.swap_route(3))  2.12 us
  transfers between devices with their start and end apart: 11, of which 3 were waited for; matrix products, arithmetic and copies ran while one was open for 0% of the time, Pallas kernels for 18%

profile of v7, /device:TPU:0, one launch (start us, length us, event | category | flops | bytes accessed | tf_op | source)
XLA Modules:
  0.0 64.1 jit_solution(5115409932785305771)
XLA Ops:
  0.0 0.1 stack.53.pos._
  0.1 2.1 %shard_map.82 = (bf16[1,30,16,128]{3,2,1,0:T(8,128)(2,1)S(1)}, bf16[1,30,16,128]{3,2,1,0:T(8,128)(2,1)S(1)}, bf16[1,15,16,128]{3,2,1,0:T(8,128)(2,1)S(1)}, bf16[...) custom-call(s32[6]{0:T(128)S(1)} %stack.53.pos._, bf16[16,16,16,128]{3,2,1,0:T(8,128)(2,1)} %x_in.1, ...), custom_call_target="tpu_custom_call" | custom-call | bytes 5242880 | tf_op jit(solution)/shard_map/pallas_call | solution.py:102
  2.2 4.1 %collective-permute-start = (bf16[30,16,128]{2,1,0:T(8,128)(2,1)S(1)}, bf16[30,16,128]{2,1,0:T(8,128)(2,1)S(1)}, u32[]{:S(2)}, u32[]{:S(2)}) collective-permute-start(bf16[30,16,128]{2,1,0:T(8,128)(2,1)S(1)} %bitcast.50), channel_id=1, source_target_pairs={{0,2},{1,3},{2,0},{3,1},{4,6},{5,7},{6,4},{7,5},{8,10},{9,11},{10,... | collective-permute-start | bytes 368648 | tf_op jit(solution)/shard_map/ppermute | solution.py:44
  6.3 1.6 %collective-permute-start.1 = (bf16[30,16,128]{2,1,0:T(8,128)(2,1)S(1)}, bf16[30,16,128]{2,1,0:T(8,128)(2,1)S(1)}, u32[]{:S(2)}, u32[]{:S(2)}) collective-permute-start(bf16[30,16,128]{2,1,0:T(8,128)(2,1)S(1)} %bitcast.49), channel_id=1, source_target_pairs={{0,1},{1,0},{2,3},{3,2},{4,5},{5,4},{6,7},{7,6},{8,9},{9,8},{10,11... | collective-permute-start | bytes 368648 | tf_op jit(solution)/shard_map/ppermute | solution.py:45
  7.9 0.0 collective-permute-start.2
  7.9 5.3 %shard_map.83 = (f32[16,16,16,128]{3,2,1,0:T(8,128)S(1)}, bf16[1152,384]{1,0:T(8,128)(2,1)S(1)}, bf16[1536,256]{1,0:T(8,128)(2,1)S(1)}, f32[8,128]{1,0:T(8,128)S(1)}) custom-call(s32[6]{0:T(128)S(1)} %stack.53.pos._, bf16[18,18,16,128]{3,2,1,0:T(8,128)(2,1)S(1)} %get-tuple-element.34.x.refs_0_, bf16[27,128,128]{2,1,0:T(8,128)(2,1)S(1)} %get-tuple-element.38.weight), custom_call_target="tpu_custom_call" | custom-call | flops 3623878656 | bytes 6291456 | tf_op jit(solution)/shard_map/pallas_call | solution.py:102
  13.1 1.6 %collective-permute-done.2 = bf16[15,16,128]{2,1,0:T(8,128)(2,1)S(1)} collective-permute-done((bf16[15,16,128]{2,1,0:T(8,128)(2,1)S(1)}, bf16[15,16,128]{2,1,0:T(8,128)(2,1)S(1)}, u32[]{:S(2)}, u32[]{:S(2)}) %collective-permute-start.2) | collective-permute-done | bytes 61472 | tf_op jit(solution)/shard_map/ppermute | solution.py:46
  14.8 0.0 collective-permute-done
  14.8 0.0 collective-permute-done.1
  14.8 0.6 shard_map.84
  15.4 1.3 %collective-permute-start.3 = (bf16[55,16,128]{2,1,0:T(8,128)(2,1)S(1)}, bf16[55,16,128]{2,1,0:T(8,128)(2,1)S(1)}, u32[]{:S(2)}, u32[]{:S(2)}) collective-permute-start(bf16[55,16,128]{2,1,0:T(8,128)(2,1)S(1)} %get-tuple-element.45), channel_id=1, source_target_pairs={{0,4},{4,8},{8,12},{1,5},{5,9},{9,13},{2,6},{6,10},{10,14},{3,7},{... | collective-permute-start | bytes 675848 | tf_op jit(solution)/shard_map/ppermute | solution.py:61
  16.7 1.3 %collective-permute-start.4 = (bf16[55,16,128]{2,1,0:T(8,128)(2,1)S(1)}, bf16[55,16,128]{2,1,0:T(8,128)(2,1)S(1)}, u32[]{:S(2)}, u32[]{:S(2)}) collective-permute-start(bf16[55,16,128]{2,1,0:T(8,128)(2,1)S(1)} %get-tuple-element.46), channel_id=1, source_target_pairs={{4,0},{8,4},{12,8},{5,1},{9,5},{13,9},{6,2},{10,6},{14,10},{7,3},{... | collective-permute-start | bytes 675848 | tf_op jit(solution)/shard_map/ppermute | solution.py:61
  18.0 1.6 %collective-permute-start.5 = (bf16[1,3,14,16,128]{4,3,2,1,0:T(8,128)(2,1)S(1)}, bf16[1,3,14,16,128]{4,3,2,1,0:T(8,128)(2,1)S(1)}, u32[]{:S(2)}, u32[]{:S(2)}) collective-permute-start(bf16[1,3,14,16,128]{4,3,2,1,0:T(8,128)(2,1)S(1)} %bitcast.37), channel_id=1, source_target_pairs={{0,16},{16,0},{1,17},{17,1},{2,18},{18,2},{3,19},{19,3},{4,20},{20... | collective-permute-start | bytes 516104 | tf_op jit(solution)/shard_map/ppermute | solution.py:89
  19.6 0.0 collective-permute-done.3.refs_6_
  19.6 2.2 %collective-permute-done.4.refs_7_ = bf16[55,16,128]{2,1,0:T(8,128)(2,1)S(1)} collective-permute-done((bf16[55,16,128]{2,1,0:T(8,128)(2,1)S(1)}, bf16[55,16,128]{2,1,0:T(8,128)(2,1)S(1)}, u32[]{:S(2)}, u32[]{:S(2)}) %collective-permute-start.4) | collective-permute-done | bytes 225312 | tf_op jit(solution)/shard_map/ppermute | solution.py:61
  21.8 3.0 %shard_map.85 = (f32[20,16,16,128]{3,2,1,0:T(8,128)S(1)}, f32[16,2,128]{2,1,0:T(2,128)S(1)}) custom-call(s32[6]{0:T(128)S(1)} %stack.53.pos._, bf16[18,18,16,128]{3,2,1,0:T(8,128)(2,1)S(1)} %get-tuple-element.34.x.refs_0_, f32[16,16,16,128]{3,2,1,0:T(8,128)S(1)} %get-tuple-element.40.refs_1_, f32[8,128]{1,0:T(8,128)S(1)} %get-tuple-element.41.refs_2_, ...), custom_call_target="tpu_custom_call" | custom-call | flops 1811939328 | bytes 6291456 | tf_op jit(solution)/shard_map/pallas_call | solution.py:102
  24.8 0.0 copy-start.3
  24.8 0.0 copy-start.4
  24.8 0.0 collective-permute-done.5.refs_1_
  24.9 4.2 %collective-permute-start.6 = (bf16[2,3,14,16,128]{4,3,2,1,0:T(8,128)(2,1)S(1)}, bf16[2,3,14,16,128]{4,3,2,1,0:T(8,128)(2,1)S(1)}, u32[]{:S(2)}, u32[]{:S(2)}) collective-permute-start(bf16[2,3,14,16,128]{4,3,2,1,0:T(8,128)(2,1)S(1)} %bitcast.35), channel_id=1, source_target_pairs={{0,8},{4,12},{8,0},{12,4},{1,9},{5,13},{9,1},{13,5},{2,10},{6,14},... | collective-permute-start | bytes 1032200 | tf_op jit(solution)/shard_map/ppermute | solution.py:89
  29.1 11.4 %all_to_all.10.stats = f32[16,2,128]{2,1,0:T(2,128)S(1)} all-to-all(f32[16,2,128]{2,1,0:T(2,128)S(1)} %get-tuple-element.52), channel_id=1, replica_groups=mesh['cand'=2,'gz'=4,'yx'=4] {'gz','yx'}, dimensions={0} | all-to-all | bytes 32768 | tf_op jit(solution)/shard_map/all_to_all | solution.py:93
  40.5 0.0 collective-permute-done.6.refs_1_
  40.5 0.2 collective-permute-start.10
  40.7 0.0 copy-done.3
  40.7 0.0 copy-done.4
  40.7 1.7 %shard_map.87 = (bf16[16,16,16,128]{3,2,1,0:T(8,128)(2,1)S(1)}, f32[10,8,8,128]{3,2,1,0:T(8,128)S(1)}, bf16[1,80,128]{2,1,0:T(8,128)(2,1)S(1)}, bf16[1,80,128]{2,1,0:T(8,128)(2,1)S(1)}, f32[1,16,128]{2,1,0:T(8,128)S(1)}) custom-call(s32[6]{0:T(128)S(1)} %stack.53.pos._, f32[20,16,16,128]{3,2,1,0:T(8,128)S(1)} %get-tuple-element.49.act, ...), custom_call_target="tpu_custom_call" | custom-call | flops 10485760 | bytes 3145728 | tf_op jit(solution)/shard_map/pallas_call | solution.py:102
  42.4 0.7 %collective-permute-start.7 = (bf16[80,128]{1,0:T(8,128)(2,1)S(1)}, bf16[80,128]{1,0:T(8,128)(2,1)S(1)}, u32[]{:S(2)}, u32[]{:S(2)}) collective-permute-start(bf16[80,128]{1,0:T(8,128)(2,1)S(1)} %bitcast.54), channel_id=1, source_target_pairs={{0,2},{1,3},{2,0},{3,1},{4,6},{5,7},{6,4},{7,5},{8,10},{9,11},{10,... | collective-permute-start | bytes 61448 | tf_op jit(solution)/shard_map/ppermute | solution.py:44
  43.1 0.6 collective-permute-start.8
  43.6 3.3 %collective-permute-start.9 = (f32[16,128]{1,0:T(8,128)S(1)}, f32[16,128]{1,0:T(8,128)S(1)}, u32[]{:S(2)}, u32[]{:S(2)}) collective-permute-start(f32[16,128]{1,0:T(8,128)S(1)} %bitcast.56), channel_id=1, source_target_pairs={{0,3},{1,2},{2,1},{3,0},{4,7},{5,6},{6,5},{7,4},{8,11},{9,10},{10,... | collective-permute-start | bytes 24584 | tf_op jit(solution)/shard_map/ppermute | solution.py:46
  46.9 0.0 collective-permute-done.10.refs_1_
  46.9 0.1 shard_map.89
  47.0 1.6 %shard_map.90 = bf16[4,108,16,128]{3,2,1,0:T(8,128)(2,1)S(1)} custom-call(s32[6]{0:T(128)S(1)} %stack.53.pos._, bf16[108,16,128]{2,1,0:T(8,128)(2,1)} %bitcast.59, bf16[8,3,14,16,128]{4,3,2,1,0:T(8,128)(2,1)S(1)} %bitcast.31), custom_call_target="tpu_custom_call" | custom-call | bytes 4194304 | tf_op jit(solution)/shard_map/pallas_call | solution.py:102
  48.6 0.0 copy-start
  48.6 0.0 copy-start.1
  48.6 0.0 copy-start.2
  48.6 0.5 collective-permute-done.9
  49.1 0.0 collective-permute-done.7
  49.1 0.0 collective-permute-done.8
  49.1 1.9 %shard_map.91 = (f32[512,256]{1,0:T(8,128)S(1)}, f32[16,2,256]{2,1,0:T(2,128)S(1)}) custom-call(s32[6]{0:T(128)S(1)} %stack.53.pos._, f32[10,8,8,128]{3,2,1,0:T(8,128)S(1)} %get-tuple-element.55.pooled, bf16[1,80,128]{2,1,0:T(8,128)(2,1)S(1)} %bitcast.53, bf16[1,80,128]{2,1,0:T(8,128)(2,1)S(1)} %bitcast.55, f32[1,16,128]{2,1,0:T(8,128)S(1)} %bitcast.57, ...), custom_call_target="tpu_custom_call" | custom-call | flops 905969664 | bytes 4194304 | tf_op jit(solution)/shard_map/pallas_call | solution.py:102
  51.0 10.9 %all_to_all.11.stats = f32[16,2,256]{2,1,0:T(2,128)S(1)} all-to-all(f32[16,2,256]{2,1,0:T(2,128)S(1)} %get-tuple-element.61), channel_id=1, replica_groups=mesh['cand'=2,'gz'=4,'yx'=4] {'gz','yx'}, dimensions={0} | all-to-all | bytes 65536 | tf_op jit(solution)/shard_map/all_to_all | solution.py:93
  62.0 0.0 copy-done
  62.0 0.0 copy-done.1
  62.0 0.0 copy-done.2
  62.0 2.1 %shard_map.92 = bf16[16,16,16,128]{3,2,1,0:T(8,128)(2,1)} custom-call(s32[6]{0:T(128)S(1)} %stack.53.pos._, f32[512,256]{1,0:T(8,128)S(1)} %get-tuple-element.60.act, f32[16,2,256]{2,1,0:T(2,128)S(1)} %all_to_all.11.stats, f32[1,256]{1,0:T(1,128)S(1)} %bitcast.45, f32[1,256]{1,0:T(1,128)S(1)} %bitcast.46, bf16[256,128]{1,0:T(8,128)(2,1)S(1)} %copy-done, ...), custom_call_target="tpu_custom_call" | custom-call | flops 67108864 | bytes 3145728 | tf_op jit(solution)/shard_map/pallas_call | solution.py:102
  (2 shorter events, 0.1 us)
Async XLA Ops:
  2.2 12.6 %collective-permute-start = (bf16[30,16,128]{2,1,0:T(8,128)(2,1)S(1)}, bf16[30,16,128]{2,1,0:T(8,128)(2,1)S(1)}, u32[]{:S(2)}, u32[]{:S(2)}) collective-permute-start(bf16[30,16,128]{2,1,0:T(8,128)(2,1)S(1)} %bitcast.50), channel_id=1, source_target_pairs={{0,2},{1,3},{2,0},{3,1},{4,6},{5,7},{6,4},{7,5},{8,10},{9,11},{10,... | collective-permute-start | bytes 368648 | tf_op jit(solution)/shard_map/ppermute | solution.py:44
  6.3 8.5 %collective-permute-start.1 = (bf16[30,16,128]{2,1,0:T(8,128)(2,1)S(1)}, bf16[30,16,128]{2,1,0:T(8,128)(2,1)S(1)}, u32[]{:S(2)}, u32[]{:S(2)}) collective-permute-start(bf16[30,16,128]{2,1,0:T(8,128)(2,1)S(1)} %bitcast.49), channel_id=1, source_target_pairs={{0,1},{1,0},{2,3},{3,2},{4,5},{5,4},{6,7},{7,6},{8,9},{9,8},{10,11... | collective-permute-start | bytes 368648 | tf_op jit(solution)/shard_map/ppermute | solution.py:45
  7.9 6.9 %collective-permute-start.2 = (bf16[15,16,128]{2,1,0:T(8,128)(2,1)S(1)}, bf16[15,16,128]{2,1,0:T(8,128)(2,1)S(1)}, u32[]{:S(2)}, u32[]{:S(2)}) collective-permute-start(bf16[15,16,128]{2,1,0:T(8,128)(2,1)S(1)} %bitcast.51), channel_id=1, source_target_pairs={{0,3},{1,2},{2,1},{3,0},{4,7},{5,6},{6,5},{7,4},{8,11},{9,10},{10,... | collective-permute-start | bytes 184328 | tf_op jit(solution)/shard_map/ppermute | solution.py:46
  15.4 4.2 %collective-permute-start.3 = (bf16[55,16,128]{2,1,0:T(8,128)(2,1)S(1)}, bf16[55,16,128]{2,1,0:T(8,128)(2,1)S(1)}, u32[]{:S(2)}, u32[]{:S(2)}) collective-permute-start(bf16[55,16,128]{2,1,0:T(8,128)(2,1)S(1)} %get-tuple-element.45), channel_id=1, source_target_pairs={{0,4},{4,8},{8,12},{1,5},{5,9},{9,13},{2,6},{6,10},{10,14},{3,7},{... | collective-permute-start | bytes 675848 | tf_op jit(solution)/shard_map/ppermute | solution.py:61
  16.7 5.1 %collective-permute-start.4 = (bf16[55,16,128]{2,1,0:T(8,128)(2,1)S(1)}, bf16[55,16,128]{2,1,0:T(8,128)(2,1)S(1)}, u32[]{:S(2)}, u32[]{:S(2)}) collective-permute-start(bf16[55,16,128]{2,1,0:T(8,128)(2,1)S(1)} %get-tuple-element.46), channel_id=1, source_target_pairs={{4,0},{8,4},{12,8},{5,1},{9,5},{13,9},{6,2},{10,6},{14,10},{7,3},{... | collective-permute-start | bytes 675848 | tf_op jit(solution)/shard_map/ppermute | solution.py:61
  18.0 6.8 %collective-permute-start.5 = (bf16[1,3,14,16,128]{4,3,2,1,0:T(8,128)(2,1)S(1)}, bf16[1,3,14,16,128]{4,3,2,1,0:T(8,128)(2,1)S(1)}, u32[]{:S(2)}, u32[]{:S(2)}) collective-permute-start(bf16[1,3,14,16,128]{4,3,2,1,0:T(8,128)(2,1)S(1)} %bitcast.37), channel_id=1, source_target_pairs={{0,16},{16,0},{1,17},{17,1},{2,18},{18,2},{3,19},{19,3},{4,20},{20... | collective-permute-start | bytes 516104 | tf_op jit(solution)/shard_map/ppermute | solution.py:89
  24.8 15.9 %copy-start.3 = (f32[128]{0:T(128)S(1)}, f32[128]{0:T(128)}, u32[]{:S(2)}) copy-start(f32[128]{0:T(128)} %param.10) | copy-start | bytes 1540
  24.8 15.9 %copy-start.4 = (f32[128]{0:T(128)S(1)}, f32[128]{0:T(128)}, u32[]{:S(2)}) copy-start(f32[128]{0:T(128)} %param.11) | copy-start | bytes 1540
  24.9 15.6 %collective-permute-start.6 = (bf16[2,3,14,16,128]{4,3,2,1,0:T(8,128)(2,1)S(1)}, bf16[2,3,14,16,128]{4,3,2,1,0:T(8,128)(2,1)S(1)}, u32[]{:S(2)}, u32[]{:S(2)}) collective-permute-start(bf16[2,3,14,16,128]{4,3,2,1,0:T(8,128)(2,1)S(1)} %bitcast.35), channel_id=1, source_target_pairs={{0,8},{4,12},{8,0},{12,4},{1,9},{5,13},{9,1},{13,5},{2,10},{6,14},... | collective-permute-start | bytes 1032200 | tf_op jit(solution)/shard_map/ppermute | solution.py:89
  40.5 6.4 %collective-permute-start.10 = (bf16[4,3,14,16,128]{4,3,2,1,0:T(8,128)(2,1)S(1)}, bf16[4,3,14,16,128]{4,3,2,1,0:T(8,128)(2,1)S(1)}, u32[]{:S(2)}, u32[]{:S(2)}) collective-permute-start(bf16[4,3,14,16,128]{4,3,2,1,0:T(8,128)(2,1)S(1)} %bitcast.32), channel_id=1, source_target_pairs={{0,4},{4,0},{8,12},{12,8},{1,5},{5,1},{9,13},{13,9},{2,6},{6,2},{1... | collective-permute-start | bytes 2064392 | tf_op jit(solution)/shard_map/ppermute | solution.py:89
  42.4 6.7 %collective-permute-start.7 = (bf16[80,128]{1,0:T(8,128)(2,1)S(1)}, bf16[80,128]{1,0:T(8,128)(2,1)S(1)}, u32[]{:S(2)}, u32[]{:S(2)}) collective-permute-start(bf16[80,128]{1,0:T(8,128)(2,1)S(1)} %bitcast.54), channel_id=1, source_target_pairs={{0,2},{1,3},{2,0},{3,1},{4,6},{5,7},{6,4},{7,5},{8,10},{9,11},{10,... | collective-permute-start | bytes 61448 | tf_op jit(solution)/shard_map/ppermute | solution.py:44
  43.1 6.0 %collective-permute-start.8 = (bf16[80,128]{1,0:T(8,128)(2,1)S(1)}, bf16[80,128]{1,0:T(8,128)(2,1)S(1)}, u32[]{:S(2)}, u32[]{:S(2)}) collective-permute-start(bf16[80,128]{1,0:T(8,128)(2,1)S(1)} %bitcast.52), channel_id=1, source_target_pairs={{0,1},{1,0},{2,3},{3,2},{4,5},{5,4},{6,7},{7,6},{8,9},{9,8},{10,11... | collective-permute-start | bytes 61448 | tf_op jit(solution)/shard_map/ppermute | solution.py:45
  43.6 5.4 %collective-permute-start.9 = (f32[16,128]{1,0:T(8,128)S(1)}, f32[16,128]{1,0:T(8,128)S(1)}, u32[]{:S(2)}, u32[]{:S(2)}) collective-permute-start(f32[16,128]{1,0:T(8,128)S(1)} %bitcast.56), channel_id=1, source_target_pairs={{0,3},{1,2},{2,1},{3,0},{4,7},{5,6},{6,5},{7,4},{8,11},{9,10},{10,... | collective-permute-start | bytes 24584 | tf_op jit(solution)/shard_map/ppermute | solution.py:46
  48.6 13.4 %copy-start = (bf16[256,128]{1,0:T(8,128)(2,1)S(1)}, bf16[256,128]{1,0:T(8,128)(2,1)}, u32[]{:S(2)}) copy-start(bf16[256,128]{1,0:T(8,128)(2,1)} %up.1) | copy-start | bytes 196612
  48.6 13.4 %copy-start.1 = (f32[256]{0:T(256)S(1)}, f32[256]{0:T(256)}, u32[]{:S(2)}) copy-start(f32[256]{0:T(256)} %param.13) | copy-start | bytes 3076
  48.6 13.4 %copy-start.2 = (f32[256]{0:T(256)S(1)}, f32[256]{0:T(256)}, u32[]{:S(2)}) copy-start(f32[256]{0:T(256)} %param.14) | copy-start | bytes 3076

commit v8 on v7

--- a/solution.py
+++ b/solution.py
@@ -55,10 +55,12 @@
         return y, x, corner
 
 
-def swap_depth(low, high):
+def swap_depth(outer, inner):
     size = lax.axis_size("gz")
-    up = [(i, i + 1) for i in range(size - 1)]
-    return lax.ppermute(high, "gz", up), lax.ppermute(low, "gz", [(j, i) for i, j in up])
+    routes = [[], []]
+    for low in range(size - 1):
+        routes[low % 2] += [(low, low + 1), (low + 1, low)]
+    return lax.ppermute(outer, "gz", routes[1]), lax.ppermute(inner, "gz", routes[0])
 
 
 class Riders:
@@ -113,7 +115,7 @@
 def start_kernel(ny, nx, size, pos, x_in, w_in, d_in, y_out, x_out, corners, x, w, lines, sems):
     edge = x_in.shape[0]
     f32, bf16 = jnp.float32, jnp.bfloat16
-    chunks = 4
+    chunks = 8
     planes = edge // chunks
     first = [
         pltpu.make_async_copy(
@@ -123,15 +125,20 @@
         )
         for k in range(chunks)
     ]
-    later = [pltpu.make_async_copy(w_in, w, sems.at[chunks])]
+    later = []
     if size:
         at = jnp.minimum(pos[pos.shape[0] - 1] * size, d_in.shape[0] - size)
         for k, (out, begin) in enumerate(((y_out, edge), (x_out, edge), (corners, 1))):
             later.append(
                 pltpu.make_async_copy(
-                    d_in.at[pl.ds(at, size)], out.at[0, pl.ds(begin, size)], sems.at[chunks + 1 + k]
+                    d_in.at[pl.ds(at, size)], out.at[0, pl.ds(begin, size)], sems.at[chunks + k]
                 )
             )
+    for k in range(9):
+        three = pl.ds(3 * k, 3)
+        later.append(
+            pltpu.make_async_copy(w_in.at[three], w.at[three], sems.at[chunks + 3 + k])
+        )
     for copy in first + later:
         copy.start()
     x[0] = jnp.zeros(x.shape[1:], bf16)
@@ -167,10 +174,12 @@
         copy.wait()
 
 
-def face_kernel(ny, nx, size, _, x, y_halos, x_halos, corners, low, high, *riders):
-    edge = low.shape[1]
+def face_kernel(ny, nx, size, pos, x, y_halos, x_halos, corners, outer, inner, *riders):
+    edge = outer.shape[1]
     wide = edge + ny + nx
-    for face, at in ((low, 0), (high, edge - 3)):
+    odd = pos[ny + nx + 2]
+    far = edge - 3
+    for face, at in ((outer, odd * far), (inner, (1 - odd) * far)):
         for k in range(3):
             row = k * wide
             face[row : row + edge] = x[1 + at + k, 1 : edge + 1]
@@ -248,125 +257,170 @@
         put(z, new.reshape(planes, edge, edge, 128))
 
 
-def conv_kernel(_, x, weight, act, taps, pairs, sums):
+def conv_kernel(_, x, weight, act, taps, pairs):
     edge = act.shape[0]
     spread_taps(weight, taps)
     pair_taps(weight, pairs)
-    totals = []
 
     def put(z, new):
         act[z : z + new.shape[0]] = new
-        totals.append(jnp.sum(new.reshape(-1, 8, 128), axis=0))
 
     convolve(x, edge, taps, pairs, put)
-    sums[...] = functools.reduce(jnp.add, totals)
-
-
-def rim_kernel(ny, nx, pos, *refs):
-    x, own, sums, y_halos, x_halos, corners, front, back, taps, pairs, act, stats, grid, column, flanks = refs
+
+
+def y_terms(line, low, taps):
+    planes, edge = line.shape[0] - 2, line.shape[1]
+    left = jnp.concatenate(
+        [line[dz : dz + planes].reshape(planes * edge, 128) for dz in range(3)], axis=1
+    )
+    start = jnp.where(low, 0, 256)
+    right = jnp.concatenate(
+        [taps[pl.ds(pl.multiple_of(start + dz * 384, 128), 128), :] for dz in range(3)], axis=0
+    )
+    wide = jnp.dot(left, right, preferred_element_type=jnp.float32)
+    return join_x(wide.reshape(planes, edge, 384), edge)
+
+
+def x_terms(column, taps):
+    planes, edge = column.shape[0] - 2, column.shape[1] - 16
+    lines = [column[:, 7 + dy : 7 + dy + edge].astype(jnp.bfloat16) for dy in range(3)]
+    left = jnp.concatenate(
+        [line[dz : dz + planes].reshape(planes * edge, 128) for dz in range(3) for line in lines],
+        axis=1,
+    )
+    right = jnp.concatenate([taps[:, 0:128], taps[:, 256:384]], axis=1)
+    both = jnp.dot(left, right, preferred_element_type=jnp.float32)
+    return both[:, :128], both[:, 128:]
+
+
+def fill_column(column, at, voxels, ends, above):
+    count, edge = voxels.shape[:2]
+    rows = edge + 16
+    lines = column.reshape(column.shape[0] * rows, 128)
+    column[at : at + count, 8 : 8 + edge] = voxels.astype(jnp.float32)
+    for i, end in enumerate(ends):
+        first = last = end.astype(jnp.float32)
+        if len(ends) == 1:
+            first, last = jnp.where(above[0], first, 0.0), jnp.where(above[0], 0.0, last)
+        if len(ends) == 1 or i == 0:
+            lines[pl.ds(at * rows + 7, count, stride=rows), :] = first
+        if len(ends) == 1 or i == 1:
+            lines[pl.ds(at * rows + 8 + edge, count, stride=rows), :] = last
+
+
+def add_column(act, terms, j, nx, low):
+    planes, edge = act.shape[:2]
+    flat = act.reshape(planes * edge * edge, 128)
+    first, last = terms
+    if nx == 1:
+        first, last = jnp.where(low, first, 0.0), jnp.where(low, 0.0, last)
+    if nx == 1 or j == 0:
+        flat[pl.ds(0, planes * edge, stride=edge), :] += first
+    if nx == 1 or j == 1:
+        flat[pl.ds(edge - 1, planes * edge, stride=edge), :] += last
+
+
+def moments(planes):
+    count, edge = planes.shape[:2]
+    zero = jnp.zeros((8, 128), jnp.float32)
+
+    def sum_step(k, carry):
+        return carry + jnp.sum(planes[k].reshape(edge * 2, 8, 128), axis=0)
+
+    mean = lax.fori_loop(0, count, sum_step, zero, unroll=True) / (count * edge * edge // 8)
+
+    def spread_step(k, carry):
+        off = planes[k].reshape(edge * 2, 8, 128) - mean
+        return carry + jnp.sum(off * off, axis=0)
+
+    return mean, lax.fori_loop(0, count, spread_step, zero, unroll=True)
+
+
+def side_kernel(ny, nx, pos, own, y_halos, x_halos, corners, taps, inner, ends, stats, act, column):
     edge = own.shape[0]
+    act[0] = jnp.zeros(act.shape[1:], jnp.float32)
+    act[edge + 1] = jnp.zeros(act.shape[1:], jnp.float32)
+    act[1 : edge + 1] = own[...]
+    above = [pos[i] == 1 for i in range(ny)]
+    blank = jnp.zeros((2, edge, 128), jnp.bfloat16)
+    for i in range(ny):
+        line = jnp.concatenate([blank, y_halos[i, 0:edge], blank], axis=0)
+        act[:, jnp.where(above[i], 0, edge - 1)] += y_terms(line, above[i], taps)
+    for j in range(nx):
+        column[...] = jnp.zeros(column.shape, jnp.float32)
+        fill_column(
+            column, 2, x_halos[j, 0:edge], [corners[i * nx + j, 0] for i in range(ny)], above
+        )
+        add_column(act, x_terms(column, taps), j, nx, pos[ny + j] == 1)
+    inner[...] = act[2:edge]
+    ends[0:2] = act[0:2]
+    ends[2:4] = act[edge : edge + 2]
+    mean, spread = moments(act.at[2:edge])
+    stats[0:8] = mean
+    stats[8:16] = spread
+
+
+def end_kernel(ny, nx, pos, *refs):
+    x, inner_stats, partial, outer_face, inner_face, taps, pairs, act, stats, faces, grid, column = refs
+    edge = x.shape[2]
     wide_face = edge + ny + nx
-    depth = edge + 4
-    f32, bf16 = jnp.float32, jnp.bfloat16
-    total = sums[...]
-    act[2 : 2 + edge] = own[...]
-
+    f32 = jnp.float32
+    odd = pos[ny + nx + 2] == 1
+    faces[0] = jnp.where(odd, inner_face[...], outer_face[...])
+    faces[1] = jnp.where(odd, outer_face[...], inner_face[...])
+    above = [pos[i] == 1 for i in range(ny)]
     blank = jnp.zeros(grid.shape[:1] + grid.shape[2:], grid.dtype)
     grid[:, 0] = blank
     grid[:, edge + 1] = blank
-    for face, halo_at, own_at, plane, out_at, touched, dz in (
-        (front, 0, 3, 0, 0, 2, 0),
-        (back, 1, 0, edge - 1, depth - 2, depth - 3, 2),
+    gap = jnp.zeros((2, edge, 128), grid.dtype)
+    for side, halo_at, own_at, plane, at, beyond, own, beside, dz in (
+        (0, 0, 3, 1, 0, 0, 2, 2, 0),
+        (1, 1, 0, edge, 3, 4, 3, 1, 2),
     ):
         for k in range(3):
-            grid[halo_at + k, 1 : edge + 1] = face[k * wide_face : k * wide_face + edge]
-        grid[own_at, 1 : edge + 1] = x[1 + plane, 1 : edge + 1]
+            begin = k * wide_face
+            grid[halo_at + k, 1 : edge + 1] = faces[side, begin : begin + edge]
+        grid[own_at, 1 : edge + 1] = x[plane, 1 : edge + 1]
 
         def put(z, new):
-            act[out_at + z : out_at + z + new.shape[0]] = new
+            act[beyond + z : beyond + z + new.shape[0]] = new
 
         convolve(grid, 2, taps, pairs, put)
-        beside = halo_at + (2 if dz == 0 else 0)
         left = jnp.concatenate(
             [grid[beside, dy : dy + edge].reshape(edge * edge, 128) for dy in range(3)], axis=1
         )
         wide = jnp.dot(left, taps[dz * 384 : dz * 384 + 384, :], preferred_element_type=f32)
-        new = join_x(wide.reshape(edge, edge, 384), edge)
-        total = total + jnp.sum(new.reshape(-1, 8, 128), axis=0)
-        act[touched] += new
-
-    def rim(face, row):
-        return jnp.stack([face[k * wide_face + edge + row] for k in range(3)])
-
-    for i in range(ny):
-        low = pos[i] == 1
-        line = jnp.concatenate([rim(front, i), y_halos[i, 0:edge], rim(back, i)], axis=0)
-        left = jnp.concatenate(
-            [line[dz : dz + depth].reshape(depth * edge, 128) for dz in range(3)], axis=1
-        )
-        start = jnp.where(low, 0, 256)
-        right = jnp.concatenate(
-            [taps[pl.ds(pl.multiple_of(start + dz * 384, 128), 128), :] for dz in range(3)], axis=0
-        )
-        wide = jnp.dot(left, right, preferred_element_type=f32)
-        new = join_x(wide.reshape(depth, edge, 384), edge)
-        total = total + jnp.sum(new[2 : 2 + edge].reshape(-1, 8, 128), axis=0)
-        act[:, jnp.where(low, 0, edge - 1)] += new
-
-    flat = act.reshape(depth * edge * edge, 128)
-    for j in range(nx):
-        column[:, 0:8] = jnp.zeros((depth + 2, 8, 128), f32)
-        column[:, 8 + edge :] = jnp.zeros((depth + 2, 8, 128), f32)
-        column[3 : edge + 3, 8 : 8 + edge] = x_halos[j, 0:edge].astype(f32)
-        column[0:3, 8 : 8 + edge] = rim(front, ny + j).astype(f32)
-        column[edge + 3 :, 8 : 8 + edge] = rim(back, ny + j).astype(f32)
-        rows = edge + 16
-        lines = column.reshape((depth + 2) * rows, 128)
+        own_part = partial[1 if side == 0 else 2]
+        act[own] = own_part + join_x(wide.reshape(edge, edge, 384), edge)
+        near = 1 if side == 0 else 4
+        act[near] += partial[0 if side == 0 else 3]
+
+        def rim(row):
+            planes = [faces[side, k * wide_face + edge + row] for k in range(3)]
+            return jnp.stack(planes)
+
+        three = act.at[at : at + 3]
         for i in range(ny):
-            k = i * nx + j
-            low = pos[i] == 1
-            for at, count, ends in (
-                (0, 3, front[3 * wide_face + k].astype(f32)[edge - 3 :]),
-                (3, edge, corners[k, 0].astype(f32)),
-                (edge + 3, 3, back[3 * wide_face + k].astype(f32)[:3]),
-            ):
-                first, last = ends, ends
-                if ny == 1:
-                    first, last = jnp.where(low, ends, 0.0), jnp.where(low, 0.0, ends)
-                if ny == 1 or i == 0:
-                    lines[pl.ds(at * rows + 7, count, stride=rows), :] = first
-                if ny == 1 or i == 1:
-                    lines[pl.ds(at * rows + 8 + edge, count, stride=rows), :] = last
-        for dy in range(3):
-            piece = column[:, 7 + dy : 7 + dy + edge].astype(bf16)
-            flanks[:, :, dy * 128 : dy * 128 + 128] = piece
-        left = jnp.concatenate(
-            [flanks[dz : dz + depth].reshape(depth * edge, 384) for dz in range(3)], axis=1
-        )
-        right = jnp.concatenate([taps[:, 0:128], taps[:, 256:384]], axis=1)
-        extra = jnp.dot(left, right, preferred_element_type=f32)
-        low = pos[ny + j] == 1
-        first, last = extra[:, :128], extra[:, 128:]
-        if nx == 1:
-            first, last = jnp.where(low, first, 0.0), jnp.where(low, 0.0, last)
-        line = lax.broadcasted_iota(jnp.int32, (8, 128), 0)
-        inner = slice(2 * edge, 2 * edge + edge * edge)
-        if nx == 1 or j == 0:
-            flat[pl.ds(0, depth * edge, stride=edge), :] += first
-            total = total + jnp.where(line == 0, jnp.sum(first[inner], axis=0, keepdims=True), 0.0)
-        if nx == 1 or j == 1:
-            flat[pl.ds(edge - 1, depth * edge, stride=edge), :] += last
-            total = total + jnp.where(line == 7, jnp.sum(last[inner], axis=0, keepdims=True), 0.0)
-
-    rows = edge**3 // 8
-    mean = total / rows
-
-    def spread_step(k, carry):
-        off = act[k].reshape(edge * 2, 8, 128) - mean
-        return carry + jnp.sum(off * off, axis=0)
-
-    spread = lax.fori_loop(2, edge + 2, spread_step, jnp.zeros((8, 128), f32), unroll=4)
-    put_stats(stats, mean, spread, rows)
+            line = [rim(i), gap] if side == 0 else [gap, rim(i)]
+            three[:, jnp.where(above[i], 0, edge - 1)] += y_terms(
+                jnp.concatenate(line, axis=0), above[i], taps
+            )
+        for j in range(nx):
+            column[...] = jnp.zeros(column.shape, f32)
+            ends = []
+            for i in range(ny):
+                tile = faces[side, 3 * wide_face + i * nx + j].astype(f32)
+                ends.append(tile[edge - 3 :] if side == 0 else tile[:3])
+            fill_column(column, 0 if side == 0 else 2, rim(ny + j), ends, above)
+            add_column(three, x_terms(column, taps), j, nx, pos[ny + j] == 1)
+
+    mean, spread = moments(act.at[2:4])
+    few, many = edge * edge // 4, (edge - 2) * edge * edge // 8
+    inner_mean, inner_spread = inner_stats[0:8], inner_stats[8:16]
+    off = inner_mean - mean
+    share_of = few / (few + many)
+    spread = spread + inner_spread + (many * share_of) * (off * off)
+    put_stats(stats, inner_mean - share_of * off, spread, few + many)
 
 
 def merge(mean, spread, rows, other_mean, other_spread):
@@ -408,16 +462,20 @@
     return h + h * jnp.tanh(h)
 
 
-def norm_kernel(ny, nx, pos, act, stats, gain, offset, out, pooled, *refs):
+def norm_kernel(ny, nx, pos, inner, ends, stats, gain, offset, out, pooled, *refs):
     y_edges, x_edges, corners, half = refs
-    depth, edge = act.shape[0], act.shape[1]
+    depth, edge = inner.shape[0] + 6, inner.shape[1]
     deep, deep_depth = edge // 2, depth // 2
     f32, bf16 = jnp.float32, jnp.bfloat16
     mean, scale = read_stats(stats, float(edge**3))
     scale = scale * (0.5 * gain[...])
     shift = 0.5 * offset[...]
     for k in range(deep_depth):
-        value = act[2 * k : 2 * k + 2].reshape(edge * edge // 4, 8, 128)
+        value = [
+            ends[z] if z < 3 else inner[z - 3] if z < depth - 3 else ends[z - depth + 6]
+            for z in (2 * k, 2 * k + 1)
+        ]
+        value = jnp.stack(value).reshape(edge * edge // 4, 8, 128)
         value = silu_of_double((value - mean) * scale + shift)
         value = value.reshape(2, edge, edge, 128).astype(bf16)
         if 0 < k < deep_depth - 1:
@@ -595,7 +653,7 @@
     riders = Riders(deep_weight.shape[4])
     depth_at = lax.axis_index("gz")
     inside = [depth_at > 0, depth_at < lax.axis_size("gz") - 1]
-    pos = y_low + x_low + inside + [lax.axis_index("yx"), riders.mine]
+    pos = y_low + x_low + inside + [depth_at % 2, lax.axis_index("yx"), riders.mine]
     pos = jnp.stack([jnp.asarray(v, jnp.int32) for v in pos])
 
     own = jnp.moveaxis(deep_weight, 4, 3).reshape(-1, 16, channels)
@@ -609,7 +667,7 @@
             ((edge + 2, edge + 2, edge, channels), bf16),
             (conv_weight.shape, bf16),
         ],
-        [((nx, edge * edge, 8, channels), f32), pltpu.SemaphoreType.DMA((8,))],
+        [((nx, edge * edge, 8, channels), f32), pltpu.SemaphoreType.DMA((20,))],
         pos,
         features,
         conv_weight,
@@ -619,13 +677,12 @@
     )
     halos = square.halos(*(list(piece) for piece in edges))
     conv_flops = 54 * channels * channels * edge**3
-    act, taps, pairs, sums = call(
+    act, taps, pairs = call(
         conv_kernel,
         [
             ((edge, edge, edge, channels), f32),
             ((9 * channels, 3 * channels), bf16),
             ((12 * channels, 2 * channels), bf16),
-            ((8, channels), f32),
         ],
         [],
         pos,
@@ -638,7 +695,7 @@
     y, x, corner = jnp.stack(y), jnp.stack(x), jnp.stack(corner)
     face = ((3 * (edge + ny + nx) + ny * nx, edge, channels), bf16)
     held = [((3, riders.size, 16, channels), bf16)] if riders.size else []
-    low, high, *held = call(
+    outer, inner, *held = call(
         functools.partial(face_kernel, ny, nx, riders.size),
         [face, face] + held,
         [],
@@ -648,33 +705,49 @@
         x,
         corner,
     )
-    front, back = swap_depth(low, high)
+    outer, inner = swap_depth(outer, inner)
     if riders.size:
         held = held[0][None]
         other = swap(held, *riders.STEPS[0])
     else:
         held = rotate_shards(own)
-    act, stats = call(
-        functools.partial(rim_kernel, ny, nx),
-        [((edge + 4, edge, edge, channels), f32), ((devices, 2, channels), f32)],
+    six = ((6, edge, edge, channels), f32)
+    column = (edge + 16, channels)
+    middle, partial, stats = call(
+        functools.partial(side_kernel, ny, nx),
         [
+            ((edge - 2, edge, edge, channels), f32),
+            ((4, edge, edge, channels), f32),
+            ((16, channels), f32),
+        ],
+        [((edge + 2, edge, edge, channels), f32), ((edge + 4,) + column, f32)],
+        pos,
+        act,
+        y,
+        x,
+        corner,
+        taps,
+        flops=conv_flops // 4,
+        nbytes=6 << 20,
+    )
+    ends, stats = call(
+        functools.partial(end_kernel, ny, nx),
+        [six, ((devices, 2, channels), f32)],
+        [
+            ((2,) + face[0], bf16),
             ((4, edge + 2, edge, channels), bf16),
-            ((edge + 6, edge + 16, channels), f32),
-            ((edge + 6, edge, 3 * channels), bf16),
+            ((5,) + column, f32),
         ],
         pos,
         field,
-        act,
-        sums,
-        y,
-        x,
-        corner,
-        front,
-        back,
+        stats,
+        partial,
+        outer,
+        inner,
         taps,
         pairs,
         flops=conv_flops // 2,
-        nbytes=6 << 20,
+        nbytes=3 << 20,
     )
     if riders.size:
         stats, other = lax.optimization_barrier((stats, other))
@@ -698,7 +771,8 @@
         ],
         [((deep + 2, deep * edge, channels), f32)],
         pos,
-        act,
+        middle,
+        ends,
         stats,
         gain_mid.reshape(1, channels),
         offset_mid.reshape(1, channels),

time: 64.4 us -> 61 us (0.947)
  blocking collectives: 22.3 us -> 19.8 us
  starting transfers between devices: 18.7 us -> 17 us
  Pallas kernels: 18.4 us -> 19.8 us
    ppermute x2, starting transfers between devices: 3.26 us -> 8.05 us  [halos(): corner = lax.ppermute(corners[0], 'yx', self.swap_route(3))]
    ppermute x2, starting transfers between devices: 4.77 us -> 1.88 us  [halos(): y = lax.ppermute(y_edges[0], 'yx', self.swap_route(2))]
    ppermute x3, starting transfers between devices: 5.97 us -> 3.2 us  [swap(): lax.ppermute(block, axis, [(i, i ^ mask) for i in range(lax.axis_size(axi...]
    all_to_all x2, blocking collectives: 22.3 us -> 19.8 us  [share(): return lax.all_to_all(stats, PART, 0, 0)]
    ppermute x2, waiting for transfers between devices: 2.2 us -> 0.01 us  [the longest x1 0.01 us: swap_depth(): lax.ppermute(inner, 'gz', routes[0])]
    ppermute x2, starting transfers between devices: 2.13 us -> 0.31 us  [halos(): x = lax.ppermute(x_edges[0], 'yx', self.swap_route(1))]
    ppermute x2, waiting for transfers between devices: 0.01 us -> 1.59 us  [halos(): y = lax.ppermute(y_edges[0], 'yx', self.swap_route(2))]
    pallas_call x8 -> x9, Pallas kernels: 18.2 us -> 19.6 us  [call(): pl.pallas_call(kernel, out_shape=[jax.ShapeDtypeStruct(shape, dtype) for...]
  transfers between devices with their start and end apart: 11 -> 11, of which waited for: 3 -> 4; matrix products, arithmetic and copies ran while one was open for 0% -> 0% of each run, Pallas kernels for 18% -> 21%
where the time goes in v8:
time: 61 us; the launch traced here: 60.8 us
  Pallas kernels  19.8 us (32%)
  blocking collectives  19.8 us (32%)
  starting transfers between devices  17 us (28%)
  waiting for transfers between devices  3.86 us (6%)
    all_to_all x2, blocking collectives, share(): return lax.all_to_all(stats, PART, 0, 0)  19.8 us
    pallas_call x9, Pallas kernels, call(): pl.pallas_call(kernel, out_shape=[jax.ShapeDtypeStruct(shape, dtype) for...  19.6 us
    ppermute x2, starting transfers between devices, halos(): corner = lax.ppermute(corners[0], 'yx', self.swap_route(3))  8.05 us
    ppermute x3, starting transfers between devices, swap(): lax.ppermute(block, axis, [(i, i ^ mask) for i in range(lax.axis_size(axi...  3.2 us
    ppermute x1, starting transfers between devices, swap_depth(): lax.ppermute(inner, 'gz', routes[0])  2.92 us
    ppermute x2, starting transfers between devices, halos(): y = lax.ppermute(y_edges[0], 'yx', self.swap_route(2))  1.88 us
    ppermute x2, waiting for transfers between devices, halos(): y = lax.ppermute(y_edges[0], 'yx', self.swap_route(2))  1.59 us
  transfers between devices with their start and end apart: 11, of which 4 were waited for; matrix products, arithmetic and copies ran while one was open for 0% of the time, Pallas kernels for 21%

profile of v8, /device:TPU:0, one launch (start us, length us, event | category | flops | bytes accessed | tf_op | source)
XLA Modules:
  0.0 60.8 jit_solution(18246202576527353899)
XLA Ops:
  0.0 0.1 stack.57.pos._
  0.1 2.3 %shard_map.82 = (bf16[1,30,16,128]{3,2,1,0:T(8,128)(2,1)S(1)}, bf16[1,30,16,128]{3,2,1,0:T(8,128)(2,1)S(1)}, bf16[1,15,16,128]{3,2,1,0:T(8,128)(2,1)S(1)}, bf16[...) custom-call(s32[7]{0:T(128)S(1)} %stack.57.pos._, bf16[16,16,16,128]{3,2,1,0:T(8,128)(2,1)} %x_in.1, ...), custom_call_target="tpu_custom_call" | custom-call | bytes 5242880 | tf_op jit(solution)/shard_map/pallas_call | solution.py:104
  2.4 5.1 %collective-permute-start.2 = (bf16[15,16,128]{2,1,0:T(8,128)(2,1)S(1)}, bf16[15,16,128]{2,1,0:T(8,128)(2,1)S(1)}, u32[]{:S(2)}, u32[]{:S(2)}) collective-permute-start(bf16[15,16,128]{2,1,0:T(8,128)(2,1)S(1)} %bitcast.52), channel_id=1, source_target_pairs={{0,3},{1,2},{2,1},{3,0},{4,7},{5,6},{6,5},{7,4},{8,11},{9,10},{10,... | collective-permute-start | bytes 184328 | tf_op jit(solution)/shard_map/ppermute | solution.py:46
  7.5 0.0 collective-permute-start.1
  7.5 0.6 %collective-permute-start = (bf16[30,16,128]{2,1,0:T(8,128)(2,1)S(1)}, bf16[30,16,128]{2,1,0:T(8,128)(2,1)S(1)}, u32[]{:S(2)}, u32[]{:S(2)}) collective-permute-start(bf16[30,16,128]{2,1,0:T(8,128)(2,1)S(1)} %bitcast.50), channel_id=1, source_target_pairs={{0,2},{1,3},{2,0},{3,1},{4,6},{5,7},{6,4},{7,5},{8,10},{9,11},{10,... | collective-permute-start | bytes 368648 | tf_op jit(solution)/shard_map/ppermute | solution.py:44
  8.2 5.3 %shard_map.83 = (f32[16,16,16,128]{3,2,1,0:T(8,128)S(1)}, bf16[1152,384]{1,0:T(8,128)(2,1)S(1)}, bf16[1536,256]{1,0:T(8,128)(2,1)S(1)}) custom-call(s32[7]{0:T(128)S(1)} %stack.57.pos._, bf16[18,18,16,128]{3,2,1,0:T(8,128)(2,1)S(1)} %get-tuple-element.39.x.refs_0_, bf16[27,128,128]{2,1,0:T(8,128)(2,1)S(1)} %get-tuple-element.40.weight), custom_call_target="tpu_custom_call" | custom-call | flops 3623878656 | bytes 6291456 | tf_op jit(solution)/shard_map/pallas_call | solution.py:104
  13.4 0.0 collective-permute-done.2
  13.5 0.8 %collective-permute-done.1 = bf16[30,16,128]{2,1,0:T(8,128)(2,1)S(1)} collective-permute-done((bf16[30,16,128]{2,1,0:T(8,128)(2,1)S(1)}, bf16[30,16,128]{2,1,0:T(8,128)(2,1)S(1)}, u32[]{:S(2)}, u32[]{:S(2)}) %collective-permute-start.1) | collective-permute-done | bytes 122912 | tf_op jit(solution)/shard_map/ppermute | solution.py:45
  14.3 1.6 %collective-permute-done = bf16[30,16,128]{2,1,0:T(8,128)(2,1)S(1)} collective-permute-done((bf16[30,16,128]{2,1,0:T(8,128)(2,1)S(1)}, bf16[30,16,128]{2,1,0:T(8,128)(2,1)S(1)}, u32[]{:S(2)}, u32[]{:S(2)}) %collective-permute-start) | collective-permute-done | bytes 122912 | tf_op jit(solution)/shard_map/ppermute | solution.py:44
  15.9 0.6 shard_map.85
  16.5 0.7 %collective-permute-start.3 = (bf16[55,16,128]{2,1,0:T(8,128)(2,1)S(1)}, bf16[55,16,128]{2,1,0:T(8,128)(2,1)S(1)}, u32[]{:S(2)}, u32[]{:S(2)}) collective-permute-start(bf16[55,16,128]{2,1,0:T(8,128)(2,1)S(1)} %get-tuple-element.50), channel_id=1, source_target_pairs={{4,8},{8,4},{5,9},{9,5},{6,10},{10,6},{7,11},{11,7},{20,24},{24,20... | collective-permute-start | bytes 675848 | tf_op jit(solution)/shard_map/ppermute | solution.py:63
  17.2 2.9 %collective-permute-start.4 = (bf16[55,16,128]{2,1,0:T(8,128)(2,1)S(1)}, bf16[55,16,128]{2,1,0:T(8,128)(2,1)S(1)}, u32[]{:S(2)}, u32[]{:S(2)}) collective-permute-start(bf16[55,16,128]{2,1,0:T(8,128)(2,1)S(1)} %get-tuple-element.51), channel_id=1, source_target_pairs={{0,4},{4,0},{8,12},{12,8},{1,5},{5,1},{9,13},{13,9},{2,6},{6,2},{1... | collective-permute-start | bytes 675848 | tf_op jit(solution)/shard_map/ppermute | solution.py:63
  20.1 1.5 %collective-permute-start.5 = (bf16[1,3,14,16,128]{4,3,2,1,0:T(8,128)(2,1)S(1)}, bf16[1,3,14,16,128]{4,3,2,1,0:T(8,128)(2,1)S(1)}, u32[]{:S(2)}, u32[]{:S(2)}) collective-permute-start(bf16[1,3,14,16,128]{4,3,2,1,0:T(8,128)(2,1)S(1)} %bitcast.38), channel_id=1, source_target_pairs={{0,16},{16,0},{1,17},{17,1},{2,18},{18,2},{3,19},{19,3},{4,20},{20... | collective-permute-start | bytes 516104 | tf_op jit(solution)/shard_map/ppermute | solution.py:91
  21.6 1.6 %shard_map.84 = (f32[14,16,16,128]{3,2,1,0:T(8,128)S(1)}, f32[4,16,16,128]{3,2,1,0:T(8,128)S(1)}, f32[16,128]{1,0:T(8,128)S(1)}) custom-call(s32[7]{0:T(128)S(1)} %stack.57.pos._, f32[16,16,16,128]{3,2,1,0:T(8,128)S(1)} %get-tuple-element.42.own, bf16[1,30,16,128]{3,2,1,0:T(8,128)(2,1)S(1)} %bitcast.43, bf16[1,30,16,128]{3,2,1,0:T(8,128)(2,1)S(1)} %bitcast.41, ...), custom_call_target="tpu_custom_call" | custom-call | flops 905969664 | bytes 6291456 | tf_op jit(solution)/shard_map/pallas_call | solution.py:104
  23.2 0.0 collective-permute-done.3.refs_3_
  23.2 0.0 collective-permute-done.4.refs_4_
  23.3 2.5 %shard_map.86 = (f32[6,16,16,128]{3,2,1,0:T(8,128)S(1)}, f32[16,2,128]{2,1,0:T(2,128)S(1)}) custom-call(s32[7]{0:T(128)S(1)} %stack.57.pos._, bf16[18,18,16,128]{3,2,1,0:T(8,128)(2,1)S(1)} %get-tuple-element.39.x.refs_0_, f32[16,128]{1,0:T(8,128)S(1)} %get-tuple-element.48.refs_1_, f32[4,16,16,128]{3,2,1,0:T(8,128)S(1)} %get-tuple-element.49.refs_2_, ...), custom_call_target="tpu_custom_call" | custom-call | flops 1811939328 | bytes 3145728 | tf_op jit(solution)/shard_map/pallas_call | solution.py:104
  25.8 0.0 copy-start.3
  25.8 0.0 copy-start.4
  25.8 0.6 %collective-permute-done.5.refs_1_ = bf16[1,3,14,16,128]{4,3,2,1,0:T(8,128)(2,1)S(1)} collective-permute-done((bf16[1,3,14,16,128]{4,3,2,1,0:T(8,128)(2,1)S(1)}, bf16[1,3,14,16,128]{4,3,2,1,0:T(8,128)(2,1)S(1)}, u32[]{:S(2)}, u32[]{:S(2)}) %collective-permute-start.5) | collective-permute-done | bytes 172064 | tf_op jit(solution)/shard_map/ppermute | solution.py:91
  26.5 1.5 %collective-permute-start.6 = (bf16[2,3,14,16,128]{4,3,2,1,0:T(8,128)(2,1)S(1)}, bf16[2,3,14,16,128]{4,3,2,1,0:T(8,128)(2,1)S(1)}, u32[]{:S(2)}, u32[]{:S(2)}) collective-permute-start(bf16[2,3,14,16,128]{4,3,2,1,0:T(8,128)(2,1)S(1)} %bitcast.36), channel_id=1, source_target_pairs={{0,8},{4,12},{8,0},{12,4},{1,9},{5,13},{9,1},{13,5},{2,10},{6,14},... | collective-permute-start | bytes 1032200 | tf_op jit(solution)/shard_map/ppermute | solution.py:91
  28.0 9.2 %all_to_all.10.stats = f32[16,2,128]{2,1,0:T(2,128)S(1)} all-to-all(f32[16,2,128]{2,1,0:T(2,128)S(1)} %get-tuple-element.56), channel_id=1, replica_groups=mesh['cand'=2,'gz'=4,'yx'=4] {'gz','yx'}, dimensions={0} | all-to-all | bytes 32768 | tf_op jit(solution)/shard_map/all_to_all | solution.py:95
  37.2 0.0 collective-permute-done.6.refs_1_
  37.2 0.2 collective-permute-start.10
  37.4 0.0 copy-done.3
  37.4 0.0 copy-done.4
  37.4 1.7 %shard_map.88 = (bf16[16,16,16,128]{3,2,1,0:T(8,128)(2,1)S(1)}, f32[10,8,8,128]{3,2,1,0:T(8,128)S(1)}, bf16[1,80,128]{2,1,0:T(8,128)(2,1)S(1)}, bf16[1,80,128]{2,1,0:T(8,128)(2,1)S(1)}, f32[1,16,128]{2,1,0:T(8,128)S(1)}) custom-call(s32[7]{0:T(128)S(1)} %stack.57.pos._, f32[14,16,16,128]{3,2,1,0:T(8,128)S(1)} %get-tuple-element.47.inner, ...), custom_call_target="tpu_custom_call" | custom-call | flops 10485760 | bytes 3145728 | tf_op jit(solution)/shard_map/pallas_call | solution.py:104
  39.1 1.2 %collective-permute-start.7 = (bf16[80,128]{1,0:T(8,128)(2,1)S(1)}, bf16[80,128]{1,0:T(8,128)(2,1)S(1)}, u32[]{:S(2)}, u32[]{:S(2)}) collective-permute-start(bf16[80,128]{1,0:T(8,128)(2,1)S(1)} %bitcast.55), channel_id=1, source_target_pairs={{0,2},{1,3},{2,0},{3,1},{4,6},{5,7},{6,4},{7,5},{8,10},{9,11},{10,... | collective-permute-start | bytes 61448 | tf_op jit(solution)/shard_map/ppermute | solution.py:44
  40.3 0.3 collective-permute-start.8
  40.7 2.9 %collective-permute-start.9 = (f32[16,128]{1,0:T(8,128)S(1)}, f32[16,128]{1,0:T(8,128)S(1)}, u32[]{:S(2)}, u32[]{:S(2)}) collective-permute-start(f32[16,128]{1,0:T(8,128)S(1)} %bitcast.57), channel_id=1, source_target_pairs={{0,3},{1,2},{2,1},{3,0},{4,7},{5,6},{6,5},{7,4},{8,11},{9,10},{10,... | collective-permute-start | bytes 24584 | tf_op jit(solution)/shard_map/ppermute | solution.py:46
  43.6 0.0 collective-permute-done.10.refs_1_
  43.6 0.1 shard_map.90
  43.7 1.6 %shard_map.91 = bf16[4,108,16,128]{3,2,1,0:T(8,128)(2,1)S(1)} custom-call(s32[7]{0:T(128)S(1)} %stack.57.pos._, bf16[108,16,128]{2,1,0:T(8,128)(2,1)} %bitcast.60, bf16[8,3,14,16,128]{4,3,2,1,0:T(8,128)(2,1)S(1)} %bitcast.32), custom_call_target="tpu_custom_call" | custom-call | bytes 4194304 | tf_op jit(solution)/shard_map/pallas_call | solution.py:104
  45.3 0.0 copy-start
  45.3 0.0 copy-start.1
  45.3 0.0 copy-start.2
  45.3 0.8 %collective-permute-done.9 = f32[16,128]{1,0:T(8,128)S(1)} collective-permute-done((f32[16,128]{1,0:T(8,128)S(1)}, f32[16,128]{1,0:T(8,128)S(1)}, u32[]{:S(2)}, u32[]{:S(2)}) %collective-permute-start.9) | collective-permute-done | bytes 8224 | tf_op jit(solution)/shard_map/ppermute | solution.py:46
  46.1 0.0 collective-permute-done.7
  46.1 0.0 collective-permute-done.8
  46.1 1.9 %shard_map.92 = (f32[512,256]{1,0:T(8,128)S(1)}, f32[16,2,256]{2,1,0:T(2,128)S(1)}) custom-call(s32[7]{0:T(128)S(1)} %stack.57.pos._, f32[10,8,8,128]{3,2,1,0:T(8,128)S(1)} %get-tuple-element.59.pooled, bf16[1,80,128]{2,1,0:T(8,128)(2,1)S(1)} %bitcast.54, bf16[1,80,128]{2,1,0:T(8,128)(2,1)S(1)} %bitcast.56, f32[1,16,128]{2,1,0:T(8,128)S(1)} %bitcast.58, ...), custom_call_target="tpu_custom_call" | custom-call | flops 905969664 | bytes 4194304 | tf_op jit(solution)/shard_map/pallas_call | solution.py:104
  48.1 10.6 %all_to_all.11.stats = f32[16,2,256]{2,1,0:T(2,128)S(1)} all-to-all(f32[16,2,256]{2,1,0:T(2,128)S(1)} %get-tuple-element.65), channel_id=1, replica_groups=mesh['cand'=2,'gz'=4,'yx'=4] {'gz','yx'}, dimensions={0} | all-to-all | bytes 65536 | tf_op jit(solution)/shard_map/all_to_all | solution.py:95
  58.7 0.0 copy-done
  58.7 0.0 copy-done.1
  58.7 0.0 copy-done.2
  58.7 2.1 %shard_map.93 = bf16[16,16,16,128]{3,2,1,0:T(8,128)(2,1)} custom-call(s32[7]{0:T(128)S(1)} %stack.57.pos._, f32[512,256]{1,0:T(8,128)S(1)} %get-tuple-element.64.act, f32[16,2,256]{2,1,0:T(2,128)S(1)} %all_to_all.11.stats, f32[1,256]{1,0:T(1,128)S(1)} %bitcast.46, f32[1,256]{1,0:T(1,128)S(1)} %bitcast.47, bf16[256,128]{1,0:T(8,128)(2,1)S(1)} %copy-done, ...), custom_call_target="tpu_custom_call" | custom-call | flops 67108864 | bytes 3145728 | tf_op jit(solution)/shard_map/pallas_call | solution.py:104
  (2 shorter events, 0.1 us)
Async XLA Ops:
  2.4 11.0 %collective-permute-start.2 = (bf16[15,16,128]{2,1,0:T(8,128)(2,1)S(1)}, bf16[15,16,128]{2,1,0:T(8,128)(2,1)S(1)}, u32[]{:S(2)}, u32[]{:S(2)}) collective-permute-start(bf16[15,16,128]{2,1,0:T(8,128)(2,1)S(1)} %bitcast.52), channel_id=1, source_target_pairs={{0,3},{1,2},{2,1},{3,0},{4,7},{5,6},{6,5},{7,4},{8,11},{9,10},{10,... | collective-permute-start | bytes 184328 | tf_op jit(solution)/shard_map/ppermute | solution.py:46
  7.5 6.8 %collective-permute-start.1 = (bf16[30,16,128]{2,1,0:T(8,128)(2,1)S(1)}, bf16[30,16,128]{2,1,0:T(8,128)(2,1)S(1)}, u32[]{:S(2)}, u32[]{:S(2)}) collective-permute-start(bf16[30,16,128]{2,1,0:T(8,128)(2,1)S(1)} %bitcast.51), channel_id=1, source_target_pairs={{0,1},{1,0},{2,3},{3,2},{4,5},{5,4},{6,7},{7,6},{8,9},{9,8},{10,11... | collective-permute-start | bytes 368648 | tf_op jit(solution)/shard_map/ppermute | solution.py:45
  7.5 8.4 %collective-permute-start = (bf16[30,16,128]{2,1,0:T(8,128)(2,1)S(1)}, bf16[30,16,128]{2,1,0:T(8,128)(2,1)S(1)}, u32[]{:S(2)}, u32[]{:S(2)}) collective-permute-start(bf16[30,16,128]{2,1,0:T(8,128)(2,1)S(1)} %bitcast.50), channel_id=1, source_target_pairs={{0,2},{1,3},{2,0},{3,1},{4,6},{5,7},{6,4},{7,5},{8,10},{9,11},{10,... | collective-permute-start | bytes 368648 | tf_op jit(solution)/shard_map/ppermute | solution.py:44
  16.5 6.8 %collective-permute-start.3 = (bf16[55,16,128]{2,1,0:T(8,128)(2,1)S(1)}, bf16[55,16,128]{2,1,0:T(8,128)(2,1)S(1)}, u32[]{:S(2)}, u32[]{:S(2)}) collective-permute-start(bf16[55,16,128]{2,1,0:T(8,128)(2,1)S(1)} %get-tuple-element.50), channel_id=1, source_target_pairs={{4,8},{8,4},{5,9},{9,5},{6,10},{10,6},{7,11},{11,7},{20,24},{24,20... | collective-permute-start | bytes 675848 | tf_op jit(solution)/shard_map/ppermute | solution.py:63
  17.2 6.1 %collective-permute-start.4 = (bf16[55,16,128]{2,1,0:T(8,128)(2,1)S(1)}, bf16[55,16,128]{2,1,0:T(8,128)(2,1)S(1)}, u32[]{:S(2)}, u32[]{:S(2)}) collective-permute-start(bf16[55,16,128]{2,1,0:T(8,128)(2,1)S(1)} %get-tuple-element.51), channel_id=1, source_target_pairs={{0,4},{4,0},{8,12},{12,8},{1,5},{5,1},{9,13},{13,9},{2,6},{6,2},{1... | collective-permute-start | bytes 675848 | tf_op jit(solution)/shard_map/ppermute | solution.py:63
  20.1 6.4 %collective-permute-start.5 = (bf16[1,3,14,16,128]{4,3,2,1,0:T(8,128)(2,1)S(1)}, bf16[1,3,14,16,128]{4,3,2,1,0:T(8,128)(2,1)S(1)}, u32[]{:S(2)}, u32[]{:S(2)}) collective-permute-start(bf16[1,3,14,16,128]{4,3,2,1,0:T(8,128)(2,1)S(1)} %bitcast.38), channel_id=1, source_target_pairs={{0,16},{16,0},{1,17},{17,1},{2,18},{18,2},{3,19},{19,3},{4,20},{20... | collective-permute-start | bytes 516104 | tf_op jit(solution)/shard_map/ppermute | solution.py:91
  25.8 11.6 %copy-start.3 = (f32[128]{0:T(128)S(1)}, f32[128]{0:T(128)}, u32[]{:S(2)}) copy-start(f32[128]{0:T(128)} %param.10) | copy-start | bytes 1540
  25.8 11.6 %copy-start.4 = (f32[128]{0:T(128)S(1)}, f32[128]{0:T(128)}, u32[]{:S(2)}) copy-start(f32[128]{0:T(128)} %param.11) | copy-start | bytes 1540
  26.5 10.7 %collective-permute-start.6 = (bf16[2,3,14,16,128]{4,3,2,1,0:T(8,128)(2,1)S(1)}, bf16[2,3,14,16,128]{4,3,2,1,0:T(8,128)(2,1)S(1)}, u32[]{:S(2)}, u32[]{:S(2)}) collective-permute-start(bf16[2,3,14,16,128]{4,3,2,1,0:T(8,128)(2,1)S(1)} %bitcast.36), channel_id=1, source_target_pairs={{0,8},{4,12},{8,0},{12,4},{1,9},{5,13},{9,1},{13,5},{2,10},{6,14},... | collective-permute-start | bytes 1032200 | tf_op jit(solution)/shard_map/ppermute | solution.py:91
  37.2 6.4 %collective-permute-start.10 = (bf16[4,3,14,16,128]{4,3,2,1,0:T(8,128)(2,1)S(1)}, bf16[4,3,14,16,128]{4,3,2,1,0:T(8,128)(2,1)S(1)}, u32[]{:S(2)}, u32[]{:S(2)}) collective-permute-start(bf16[4,3,14,16,128]{4,3,2,1,0:T(8,128)(2,1)S(1)} %bitcast.33), channel_id=1, source_target_pairs={{0,4},{4,0},{8,12},{12,8},{1,5},{5,1},{9,13},{13,9},{2,6},{6,2},{1... | collective-permute-start | bytes 2064392 | tf_op jit(solution)/shard_map/ppermute | solution.py:91
  39.1 7.0 %collective-permute-start.7 = (bf16[80,128]{1,0:T(8,128)(2,1)S(1)}, bf16[80,128]{1,0:T(8,128)(2,1)S(1)}, u32[]{:S(2)}, u32[]{:S(2)}) collective-permute-start(bf16[80,128]{1,0:T(8,128)(2,1)S(1)} %bitcast.55), channel_id=1, source_target_pairs={{0,2},{1,3},{2,0},{3,1},{4,6},{5,7},{6,4},{7,5},{8,10},{9,11},{10,... | collective-permute-start | bytes 61448 | tf_op jit(solution)/shard_map/ppermute | solution.py:44
  40.3 5.8 %collective-permute-start.8 = (bf16[80,128]{1,0:T(8,128)(2,1)S(1)}, bf16[80,128]{1,0:T(8,128)(2,1)S(1)}, u32[]{:S(2)}, u32[]{:S(2)}) collective-permute-start(bf16[80,128]{1,0:T(8,128)(2,1)S(1)} %bitcast.53), channel_id=1, source_target_pairs={{0,1},{1,0},{2,3},{3,2},{4,5},{5,4},{6,7},{7,6},{8,9},{9,8},{10,11... | collective-permute-start | bytes 61448 | tf_op jit(solution)/shard_map/ppermute | solution.py:45
  40.7 5.4 %collective-permute-start.9 = (f32[16,128]{1,0:T(8,128)S(1)}, f32[16,128]{1,0:T(8,128)S(1)}, u32[]{:S(2)}, u32[]{:S(2)}) collective-permute-start(f32[16,128]{1,0:T(8,128)S(1)} %bitcast.57), channel_id=1, source_target_pairs={{0,3},{1,2},{2,1},{3,0},{4,7},{5,6},{6,5},{7,4},{8,11},{9,10},{10,... | collective-permute-start | bytes 24584 | tf_op jit(solution)/shard_map/ppermute | solution.py:46
  45.3 13.4 %copy-start = (bf16[256,128]{1,0:T(8,128)(2,1)S(1)}, bf16[256,128]{1,0:T(8,128)(2,1)}, u32[]{:S(2)}) copy-start(bf16[256,128]{1,0:T(8,128)(2,1)} %up.1) | copy-start | bytes 196612
  45.3 13.4 %copy-start.1 = (f32[256]{0:T(256)S(1)}, f32[256]{0:T(256)}, u32[]{:S(2)}) copy-start(f32[256]{0:T(256)} %param.13) | copy-start | bytes 3076
  45.3 13.4 %copy-start.2 = (f32[256]{0:T(256)S(1)}, f32[256]{0:T(256)}, u32[]{:S(2)}) copy-start(f32[256]{0:T(256)} %param.14) | copy-start | bytes 3076

commit v9 on v8

--- a/solution.py
+++ b/solution.py
@@ -25,8 +25,8 @@
 
     def low_sides(self):
         if self.folded:
-            return [self.row], [self.column]
-        return [1, 0], [1, 0]
+            return [self.row == 1], [self.column == 1]
+        return [True, False], [True, False]
 
     def route(self, down, right):
         pairs = []
@@ -75,8 +75,11 @@
             and self.tiles >= 8
         )
         self.size = -(-self.tiles // 8) if self.fits else 0
-        self.mine = sum(
-            lax.axis_index(axis) // mask % 2 * 2**k for k, (axis, mask) in enumerate(self.STEPS)
+
+    @classmethod
+    def mine(cls):
+        return sum(
+            lax.axis_index(axis) // mask % 2 * 2**k for k, (axis, mask) in enumerate(cls.STEPS)
         )
 
 
@@ -95,27 +98,26 @@
     return lax.all_to_all(stats, PART, 0, 0)
 
 
-def call(kernel, outs, scratch, scalars, *arrays, flops=0, nbytes=0, in_hbm=0, out_hbm=False):
-    smem, vmem, hbm = (
-        pl.BlockSpec(memory_space=space) for space in (pltpu.SMEM, pltpu.VMEM, pltpu.HBM)
-    )
+def call(kernel, outs, scratch, *arrays, flops=0, nbytes=0, in_hbm=0, out_hbm=False):
+    vmem, hbm = (pl.BlockSpec(memory_space=space) for space in (pltpu.VMEM, pltpu.HBM))
     far, near = arrays[:in_hbm], arrays[in_hbm:]
     far = [pltpu.with_memory_space_constraint(array, pltpu.HBM) for array in far]
     return pl.pallas_call(
         kernel,
         out_shape=[jax.ShapeDtypeStruct(shape, dtype) for shape, dtype in outs],
-        in_specs=[smem] + [hbm] * len(far) + [vmem] * len(near),
+        in_specs=[hbm] * len(far) + [vmem] * len(near),
         out_specs=[hbm if out_hbm else vmem] * len(outs),
         scratch_shapes=[pltpu.VMEM(*entry) if isinstance(entry, tuple) else entry for entry in scratch],
         compiler_params=pltpu.CompilerParams(vmem_limit_bytes=VMEM_BYTES),
         cost_estimate=pl.CostEstimate(flops=flops, bytes_accessed=nbytes, transcendentals=0),
-    )(scalars, *far, *near)
-
-
-def start_kernel(ny, nx, size, pos, x_in, w_in, d_in, y_out, x_out, corners, x, w, lines, sems):
+    )(*far, *near)
+
+
+def start_kernel(ny, nx, size, x_in, w_in, d_in, y_out, x_out, corners, x, w, lines, sems):
     edge = x_in.shape[0]
     f32, bf16 = jnp.float32, jnp.bfloat16
-    chunks = 8
+    above, left = Square().low_sides()
+    chunks = 4
     planes = edge // chunks
     first = [
         pltpu.make_async_copy(
@@ -127,18 +129,14 @@
     ]
     later = []
     if size:
-        at = jnp.minimum(pos[pos.shape[0] - 1] * size, d_in.shape[0] - size)
+        at = jnp.minimum(Riders.mine() * size, d_in.shape[0] - size)
         for k, (out, begin) in enumerate(((y_out, edge), (x_out, edge), (corners, 1))):
             later.append(
                 pltpu.make_async_copy(
                     d_in.at[pl.ds(at, size)], out.at[0, pl.ds(begin, size)], sems.at[chunks + k]
                 )
             )
-    for k in range(9):
-        three = pl.ds(3 * k, 3)
-        later.append(
-            pltpu.make_async_copy(w_in.at[three], w.at[three], sems.at[chunks + 3 + k])
-        )
+    later.append(pltpu.make_async_copy(w_in, w, sems.at[chunks + 3]))
     for copy in first + later:
         copy.start()
     x[0] = jnp.zeros(x.shape[1:], bf16)
@@ -152,13 +150,13 @@
         first[k].wait()
         at, here = pl.ds(k * planes, planes), pl.ds(1 + k * planes, planes)
         for i in range(ny):
-            row = jnp.where(pos[i] == 1, 1, edge) if ny == 1 else (1, edge)[i]
+            row = jnp.where(above[i], 1, edge)
             y_out[i, at] = x[here, row]
         for j in range(nx):
             low = x[here, 1 : edge + 1, 0:8].astype(f32).reshape(part, 8, 128)
             high = x[here, 1 : edge + 1, edge - 8 : edge].astype(f32).reshape(part, 8, 128)
             high = pltpu.roll(high, 1, 1)
-            kept = jnp.where(pos[ny] == 1, low, high) if nx == 1 else (low, high)[j]
+            kept = jnp.where(left[j], low, high)
             lines[j, k * part : k * part + part] = kept
             begin = (j * edge * edge + k * part) * 8
             column = flat[pl.ds(begin, part, stride=8), :]
@@ -168,16 +166,16 @@
             begin = j * edge * edge * 8
             low = flat[pl.ds(begin, edge, stride=8 * edge), :]
             high = flat[pl.ds(begin + 8 * (edge - 1), edge, stride=8 * edge), :]
-            kept = jnp.where(pos[i] == 1, low, high) if ny == 1 else (low, high)[i]
+            kept = jnp.where(above[i], low, high)
             corners[i * nx + j, 0] = kept.astype(bf16)
     for copy in later:
         copy.wait()
 
 
-def face_kernel(ny, nx, size, pos, x, y_halos, x_halos, corners, outer, inner, *riders):
+def face_kernel(ny, nx, size, x, y_halos, x_halos, corners, outer, inner, *riders):
     edge = outer.shape[1]
     wide = edge + ny + nx
-    odd = pos[ny + nx + 2]
+    odd = lax.axis_index("gz") % 2
     far = edge - 3
     for face, at in ((outer, odd * far), (inner, (1 - odd) * far)):
         for k in range(3):
@@ -257,7 +255,9 @@
         put(z, new.reshape(planes, edge, edge, 128))
 
 
-def conv_kernel(_, x, weight, act, taps, pairs):
+def conv_kernel(deep_in, x, weight, act, taps, pairs, deep_weight, sem):
+    copy = pltpu.make_async_copy(deep_in, deep_weight, sem)
+    copy.start()
     edge = act.shape[0]
     spread_taps(weight, taps)
     pair_taps(weight, pairs)
@@ -266,6 +266,7 @@
         act[z : z + new.shape[0]] = new
 
     convolve(x, edge, taps, pairs, put)
+    copy.wait()
 
 
 def y_terms(line, low, taps):
@@ -336,12 +337,12 @@
     return mean, lax.fori_loop(0, count, spread_step, zero, unroll=True)
 
 
-def side_kernel(ny, nx, pos, own, y_halos, x_halos, corners, taps, inner, ends, stats, act, column):
+def side_kernel(ny, nx, own, y_halos, x_halos, corners, taps, inner, ends, stats, act, column):
     edge = own.shape[0]
     act[0] = jnp.zeros(act.shape[1:], jnp.float32)
     act[edge + 1] = jnp.zeros(act.shape[1:], jnp.float32)
     act[1 : edge + 1] = own[...]
-    above = [pos[i] == 1 for i in range(ny)]
+    above, left = Square().low_sides()
     blank = jnp.zeros((2, edge, 128), jnp.bfloat16)
     for i in range(ny):
         line = jnp.concatenate([blank, y_halos[i, 0:edge], blank], axis=0)
@@ -351,7 +352,7 @@
         fill_column(
             column, 2, x_halos[j, 0:edge], [corners[i * nx + j, 0] for i in range(ny)], above
         )
-        add_column(act, x_terms(column, taps), j, nx, pos[ny + j] == 1)
+        add_column(act, x_terms(column, taps), j, nx, left[j])
     inner[...] = act[2:edge]
     ends[0:2] = act[0:2]
     ends[2:4] = act[edge : edge + 2]
@@ -360,15 +361,15 @@
     stats[8:16] = spread
 
 
-def end_kernel(ny, nx, pos, *refs):
+def end_kernel(ny, nx, *refs):
     x, inner_stats, partial, outer_face, inner_face, taps, pairs, act, stats, faces, grid, column = refs
     edge = x.shape[2]
     wide_face = edge + ny + nx
     f32 = jnp.float32
-    odd = pos[ny + nx + 2] == 1
+    odd = lax.axis_index("gz") % 2 == 1
     faces[0] = jnp.where(odd, inner_face[...], outer_face[...])
     faces[1] = jnp.where(odd, outer_face[...], inner_face[...])
-    above = [pos[i] == 1 for i in range(ny)]
+    above, left = Square().low_sides()
     blank = jnp.zeros(grid.shape[:1] + grid.shape[2:], grid.dtype)
     grid[:, 0] = blank
     grid[:, edge + 1] = blank
@@ -386,10 +387,10 @@
             act[beyond + z : beyond + z + new.shape[0]] = new
 
         convolve(grid, 2, taps, pairs, put)
-        left = jnp.concatenate(
+        stacked = jnp.concatenate(
             [grid[beside, dy : dy + edge].reshape(edge * edge, 128) for dy in range(3)], axis=1
         )
-        wide = jnp.dot(left, taps[dz * 384 : dz * 384 + 384, :], preferred_element_type=f32)
+        wide = jnp.dot(stacked, taps[dz * 384 : dz * 384 + 384, :], preferred_element_type=f32)
         own_part = partial[1 if side == 0 else 2]
         act[own] = own_part + join_x(wide.reshape(edge, edge, 384), edge)
         near = 1 if side == 0 else 4
@@ -412,7 +413,7 @@
                 tile = faces[side, 3 * wide_face + i * nx + j].astype(f32)
                 ends.append(tile[edge - 3 :] if side == 0 else tile[:3])
             fill_column(column, 0 if side == 0 else 2, rim(ny + j), ends, above)
-            add_column(three, x_terms(column, taps), j, nx, pos[ny + j] == 1)
+            add_column(three, x_terms(column, taps), j, nx, left[j])
 
     mean, spread = moments(act.at[2:4])
     few, many = edge * edge // 4, (edge - 2) * edge * edge // 8
@@ -462,11 +463,13 @@
     return h + h * jnp.tanh(h)
 
 
-def norm_kernel(ny, nx, pos, inner, ends, stats, gain, offset, out, pooled, *refs):
+def norm_kernel(ny, nx, inner, ends, stats, gain, offset, out, pooled, *refs):
     y_edges, x_edges, corners, half = refs
     depth, edge = inner.shape[0] + 6, inner.shape[1]
     deep, deep_depth = edge // 2, depth // 2
     f32, bf16 = jnp.float32, jnp.bfloat16
+    above, left = Square().low_sides()
+    depth_at = lax.axis_index("gz")
     mean, scale = read_stats(stats, float(edge**3))
     scale = scale * (0.5 * gain[...])
     shift = 0.5 * offset[...]
@@ -487,7 +490,7 @@
         pair = lines[pl.ds(0, deep * deep, stride=2), :] + lines[pl.ds(1, deep * deep, stride=2), :]
         pair = (pair * 0.125).astype(bf16).astype(f32).reshape(deep, deep, 128)
         if k == 0 or k == deep_depth - 1:
-            inside = pos[ny + nx + (0 if k == 0 else 1)] == 1
+            inside = depth_at > 0 if k == 0 else depth_at < lax.axis_size("gz") - 1
             pair = jnp.where(inside, pair, 0.0)
         pooled[k] = pair
     lines = pooled.reshape(deep_depth * deep * deep, 128)
@@ -500,7 +503,7 @@
         for x in (0, deep - 1):
             ends.append(lines[pl.ds(y * deep + x, deep_depth, stride=deep * deep), :])
     if ny == 1:
-        above, left = pos[0] == 1, pos[1] == 1
+        above, left = above[0], left[0]
         y_edges[0] = jnp.where(above, first_y, last_y).astype(bf16)
         x_edges[0] = jnp.where(left, first_x, last_x).astype(bf16)
         corners[0, 0:deep_depth] = jnp.where(
@@ -530,60 +533,44 @@
     )(*arrays)
 
 
-def place_kernel(pos, own, *refs):
-    *held, out, sem = refs
-    tile, mine = pos[pos.shape[0] - 2], pos[pos.shape[0] - 1]
-    copy = pltpu.make_async_copy(own, out.at[tile], sem)
-    copy.start()
+def place_weights(own, held, out):
+    tile = lax.axis_index("yx")
+    out[tile] = own[...]
     if len(held) == 1:
         pieces, others, size = held[0].shape[:3]
         for piece in range(pieces):
-            at = jnp.minimum(jnp.bitwise_xor(mine, piece) * size, own.shape[0] - size)
+            at = jnp.minimum(jnp.bitwise_xor(Riders.mine(), piece) * size, own.shape[0] - size)
             for k in range(others):
                 out[jnp.bitwise_xor(tile, k + 1), pl.ds(at, size)] = held[0][piece, k]
     else:
         for k, shard in enumerate(held):
             out[lax.rem(tile + len(held) - k, len(held) + 1)] = shard[...]
-    copy.wait()
-
-
-def deep_kernel(ny, nx, pos, pooled, y_halos, x_halos, corners, kernel, *refs):
-    act, stats, grid, packed = refs
+
+
+def tap_rows(weight, taps):
+    per = weight.shape[1] // 27
+    return jnp.concatenate(
+        [weight[:, pl.ds(tap * per, per)].reshape(-1, 128) for tap in taps], axis=1
+    )
+
+
+def dot_rows(left, right):
+    return lax.dot_general(
+        left, right, (((1,), (1,)), ((), ())), preferred_element_type=jnp.float32
+    )
+
+
+def deep_kernel(pooled, own, *refs):
+    *held, act, weight, grid, packed = refs
     depth, deep = pooled.shape[0], pooled.shape[1]
-    f32 = jnp.float32
-    grid[...] = jnp.zeros(grid.shape, f32)
+    place_weights(own, held, weight)
+    grid[...] = jnp.zeros(grid.shape, jnp.float32)
     grid[:, 1 : deep + 1, 8:16] = pooled[...]
-    for i in range(ny):
-        at = jnp.where(pos[i] == 1, 0, deep + 1)
-        grid[:, at, 8:16] = y_halos[i].astype(f32).reshape(depth, deep, 128)
-    pitch = (deep + 2) * 24
-    flat = grid.reshape(depth * pitch, 128)
-    for j in range(nx):
-        left = pos[ny + j] == 1
-        column = x_halos[j].astype(f32).reshape(depth, deep, 128)
-        for side, here in ((7, left), (16, jnp.logical_not(left))):
-            if nx == 2 and side != (7, 16)[j]:
-                continue
-            for z in range(depth):
-                kept = column[z] if nx == 2 else jnp.where(here, column[z], 0.0)
-                flat[pl.ds(z * pitch + 24 + side, deep, stride=24), :] = kept
-            for i in range(ny):
-                end = corners[i * nx + j, 0:depth]
-                above = pos[i] == 1
-                for y, there in ((0, above), (deep + 1, jnp.logical_not(above))):
-                    if ny == 2 and y != (0, deep + 1)[i]:
-                        continue
-                    kept = end
-                    if nx == 1:
-                        kept = jnp.where(jnp.logical_and(here, there), end, 0.0)
-                    flat[pl.ds(y * 24 + side, depth, stride=pitch), :] = kept
-
     for dx in range(3):
         plane = grid[:, :, 7 + dx : 15 + dx]
         for y in range(deep + 1):
             both = jnp.concatenate([plane[:, y], plane[:, y + 1]], axis=1)
             packed[:, y // 2, y % 2, :, dx * 128 : dx * 128 + 128] = both.astype(jnp.bfloat16)
-
     rows = deep**3
     total = None
     for dz in range(3):
@@ -594,22 +581,73 @@
             ],
             axis=1,
         )
-        right = jnp.concatenate(
-            [kernel[:, dz * 9 + tap].reshape(-1, 128) for tap in range(9)], axis=1
-        )
-        term = lax.dot_general(
-            left, right, (((1,), (1,)), ((), ())), preferred_element_type=f32
-        )
+        term = dot_rows(left, tap_rows(weight, range(dz * 9, dz * 9 + 9)))
         total = term if total is None else total + term
-    act[...] = total
-    total = total.reshape(rows // 8, 8, -1)
-    rows = rows // 8
-    mean = jnp.sum(total, axis=0) / rows
-    off = total - mean
-    put_stats(stats, mean, jnp.sum(off * off, axis=0), rows)
-
-
-def final_kernel(_, act, stats, gain, offset, up, mid, out, wide, held, sems):
+    for half in range(act.shape[0]):
+        act[half] = total[:, half * 128 : half * 128 + 128]
+
+
+def deep_rim_kernel(ny, nx, own, y_halos, x_halos, corners, weight, act, stats, line):
+    depth, deep = line.shape[0], line.shape[1] - 16
+    halves = act.shape[0]
+    f32 = jnp.float32
+    square = deep * deep
+    above, left = Square().low_sides()
+    act[...] = own[...]
+    flat = line.reshape(depth * line.shape[1], 128)
+
+    def shifts():
+        return jnp.concatenate(
+            [
+                line[dz : dz + deep, 7 + d : 7 + d + deep].reshape(square, 128).astype(jnp.bfloat16)
+                for dz in range(3)
+                for d in range(3)
+            ],
+            axis=1,
+        )
+
+    for i in range(ny):
+        line[...] = jnp.zeros(line.shape, f32)
+        line[:, 8 : 8 + deep] = y_halos[i].astype(f32).reshape(depth, deep, 128)
+        for j in range(nx):
+            end = corners[i * nx + j, 0:depth]
+            first, last = jnp.where(left[j], end, 0.0), jnp.where(left[j], 0.0, end)
+            if nx == 1 or j == 0:
+                flat[pl.ds(7, depth, stride=line.shape[1]), :] = first
+            if nx == 1 or j == 1:
+                flat[pl.ds(8 + deep, depth, stride=line.shape[1]), :] = last
+        tap = jnp.where(above[i], 0, 6)
+        taps = [tap + dz * 9 + dx for dz in range(3) for dx in range(3)]
+        terms = dot_rows(shifts(), tap_rows(weight, taps))
+        for half in range(halves):
+            rows = act.at[half].reshape(deep, deep, deep, 128)
+            term = terms[:, half * 128 : half * 128 + 128].reshape(deep, deep, 128)
+            rows[:, jnp.where(above[i], 0, deep - 1)] += term
+    for j in range(nx):
+        line[...] = jnp.zeros(line.shape, f32)
+        line[:, 8 : 8 + deep] = x_halos[j].astype(f32).reshape(depth, deep, 128)
+        tap = jnp.where(left[j], 0, 2)
+        taps = [tap + dz * 9 + dy * 3 for dz in range(3) for dy in range(3)]
+        terms = dot_rows(shifts(), tap_rows(weight, taps))
+        first, last = jnp.where(left[j], terms, 0.0), jnp.where(left[j], 0.0, terms)
+        for half in range(halves):
+            lanes, rows = slice(half * 128, half * 128 + 128), act.at[half]
+            if nx == 1 or j == 0:
+                rows[pl.ds(0, square, stride=deep), :] += first[:, lanes]
+            if nx == 1 or j == 1:
+                rows[pl.ds(deep - 1, square, stride=deep), :] += last[:, lanes]
+
+    rows = deep**3 // 8
+    means, spreads = [], []
+    for half in range(halves):
+        total = act[half].reshape(rows, 8, 128)
+        means.append(jnp.sum(total, axis=0) / rows)
+        off = total - means[-1]
+        spreads.append(jnp.sum(off * off, axis=0))
+    put_stats(stats, *(jnp.concatenate(part, axis=1) for part in (means, spreads)), rows)
+
+
+def final_kernel(act, stats, gain, offset, up, mid, out, wide, held, sems):
     edge = mid.shape[0]
     deep = edge // 2
     f32 = jnp.float32
@@ -620,7 +658,9 @@
     size = planes * deep * deep
     copies = []
     for k in range(0, deep, planes):
-        value = act[k * deep * deep : k * deep * deep + size].reshape(size // 8, 8, -1)
+        at = slice(k * deep * deep, k * deep * deep + size)
+        value = jnp.concatenate([act[half, at] for half in range(act.shape[0])], axis=1)
+        value = value.reshape(size // 8, 8, -1)
         value = silu_of_double((value - mean) * scale + shift)
         value = value.reshape(size, -1).astype(jnp.bfloat16)
         lifted = jnp.dot(value, up[...], preferred_element_type=f32)
@@ -648,13 +688,8 @@
     square = Square()
     tiles = square.tiles
     devices = lax.axis_size("gz") * tiles
-    y_low, x_low = square.low_sides()
-    ny, nx = len(y_low), len(x_low)
+    ny, nx = (len(sides) for sides in square.low_sides())
     riders = Riders(deep_weight.shape[4])
-    depth_at = lax.axis_index("gz")
-    inside = [depth_at > 0, depth_at < lax.axis_size("gz") - 1]
-    pos = y_low + x_low + inside + [depth_at % 2, lax.axis_index("yx"), riders.mine]
-    pos = jnp.stack([jnp.asarray(v, jnp.int32) for v in pos])
 
     own = jnp.moveaxis(deep_weight, 4, 3).reshape(-1, 16, channels)
     conv_weight = conv_weight.reshape(27, channels, channels)
@@ -667,8 +702,7 @@
             ((edge + 2, edge + 2, edge, channels), bf16),
             (conv_weight.shape, bf16),
         ],
-        [((nx, edge * edge, 8, channels), f32), pltpu.SemaphoreType.DMA((20,))],
-        pos,
+        [((nx, edge * edge, 8, channels), f32), pltpu.SemaphoreType.DMA((8,))],
         features,
         conv_weight,
         own,
@@ -677,19 +711,21 @@
     )
     halos = square.halos(*(list(piece) for piece in edges))
     conv_flops = 54 * channels * channels * edge**3
-    act, taps, pairs = call(
+    act, taps, pairs, own = call(
         conv_kernel,
         [
             ((edge, edge, edge, channels), f32),
             ((9 * channels, 3 * channels), bf16),
             ((12 * channels, 2 * channels), bf16),
+            (own.shape, bf16),
         ],
-        [],
-        pos,
+        [pltpu.SemaphoreType.DMA],
+        own,
         field,
         conv_weight,
         flops=conv_flops,
         nbytes=6 << 20,
+        in_hbm=1,
     )
     (y, x, corner), act = lax.optimization_barrier((halos, act))
     y, x, corner = jnp.stack(y), jnp.stack(x), jnp.stack(corner)
@@ -699,7 +735,6 @@
         functools.partial(face_kernel, ny, nx, riders.size),
         [face, face] + held,
         [],
-        pos,
         field,
         y,
         x,
@@ -721,7 +756,6 @@
             ((16, channels), f32),
         ],
         [((edge + 2, edge, edge, channels), f32), ((edge + 4,) + column, f32)],
-        pos,
         act,
         y,
         x,
@@ -738,7 +772,6 @@
             ((4, edge + 2, edge, channels), bf16),
             ((5,) + column, f32),
         ],
-        pos,
         field,
         stats,
         partial,
@@ -770,7 +803,6 @@
             ((ny * nx, 16, channels), f32),
         ],
         [((deep + 2, deep * edge, channels), f32)],
-        pos,
         middle,
         ends,
         stats,
@@ -780,32 +812,31 @@
         nbytes=3 << 20,
     )
     y, x, corner = square.halos(*(list(piece) for piece in edges))
-    (kernel,) = call(
-        place_kernel,
-        [((tiles,) + own.shape, bf16)],
-        [pltpu.SemaphoreType.DMA],
-        pos,
-        own,
-        *held,
-        nbytes=4 << 20,
-        in_hbm=1,
-    )
-    kernel = kernel.reshape(tiles, 27, deep_weight.shape[4], channels)
-    deep_act, stats = call(
-        functools.partial(deep_kernel, ny, nx),
-        [((deep**3, deep_channels), f32), ((devices, 2, deep_channels), f32)],
+    halves = ((deep_channels // 128, deep**3, 128), f32)
+    deep_act, weight = call(
+        deep_kernel,
+        [halves, ((tiles,) + own.shape, bf16)],
         [
             ((deep + 2, deep + 2, 24, channels), f32),
             ((deep + 2, deep // 2 + 1, 2, 16, 3 * channels), bf16),
         ],
-        pos,
         pooled,
+        own,
+        *held,
+        flops=54 * channels * deep_channels * deep**3,
+        nbytes=4 << 20,
+    )
+    deep_act, stats = call(
+        functools.partial(deep_rim_kernel, ny, nx),
+        [halves, ((devices, 2, deep_channels), f32)],
+        [((deep + 2, 24, channels), f32)],
+        deep_act,
         jnp.stack(y),
         jnp.stack(x),
         jnp.stack(corner),
-        kernel,
-        flops=2 * 27 * channels * deep_channels * deep**3,
-        nbytes=4 << 20,
+        weight,
+        flops=4 * channels * deep_channels * deep**3,
+        nbytes=3 << 20,
     )
     stats = share(stats)
     (decoded,) = call(
@@ -816,7 +847,6 @@
             ((edge, edge, edge, channels), bf16),
             pltpu.SemaphoreType.DMA((deep // 2,)),
         ],
-        pos,
         deep_act,
         stats,
         gain_deep.reshape(1, deep_channels),

time: 61 us -> 56 us (0.918)
  Pallas kernels: 19.8 us -> 14.4 us
  waiting for transfers between devices: 3.86 us -> 4.89 us
    pallas_call x9, Pallas kernels: 19.6 us -> 14.3 us  [call(): pl.pallas_call(kernel, out_shape=[jax.ShapeDtypeStruct(shape, dtype) for...]
    ppermute x2, starting transfers between devices: 8.05 us -> 5.77 us  [halos(): corner = lax.ppermute(corners[0], 'yx', self.swap_route(3))]
    ppermute x2, starting transfers between devices: 0.31 us -> 2.42 us  [halos(): x = lax.ppermute(x_edges[0], 'yx', self.swap_route(1))]
    ppermute x3, waiting for transfers between devices: 0.62 us -> 1.74 us  [swap(): lax.ppermute(block, axis, [(i, i ^ mask) for i in range(lax.axis_size(axi...]
    ppermute x2, waiting for transfers between devices: 0.8 us -> 0.01 us  [halos(): corner = lax.ppermute(corners[0], 'yx', self.swap_route(3))]
    ppermute x2, waiting for transfers between devices: 0.84 us -> 1.55 us  [halos(): x = lax.ppermute(x_edges[0], 'yx', self.swap_route(1))]
  transfers between devices with their start and end apart: 11 -> 11, of which waited for: 4 -> 4; matrix products, arithmetic and copies ran while one was open for 0% -> 0% of each run, Pallas kernels for 21% -> 19%
where the time goes in v9:
time: 56 us; the launch traced here: 55.8 us
  blocking collectives  19.8 us (35%)
  starting transfers between devices  16.5 us (29%)
  Pallas kernels  14.4 us (26%)
  waiting for transfers between devices  4.89 us (9%)
    all_to_all x2, blocking collectives, share(): return lax.all_to_all(stats, PART, 0, 0)  19.8 us
    pallas_call x9, Pallas kernels, call(): pl.pallas_call(kernel, out_shape=[jax.ShapeDtypeStruct(shape, dtype) for...  14.3 us
    ppermute x2, starting transfers between devices, halos(): corner = lax.ppermute(corners[0], 'yx', self.swap_route(3))  5.77 us
    ppermute x1, starting transfers between devices, swap_depth(): lax.ppermute(inner, 'gz', routes[0])  2.92 us
    ppermute x3, starting transfers between devices, swap(): lax.ppermute(block, axis, [(i, i ^ mask) for i in range(lax.axis_size(axi...  2.63 us
    ppermute x2, starting transfers between devices, halos(): x = lax.ppermute(x_edges[0], 'yx', self.swap_route(1))  2.42 us
    ppermute x2, starting transfers between devices, halos(): y = lax.ppermute(y_edges[0], 'yx', self.swap_route(2))  2.05 us
    ppermute x3, waiting for transfers between devices, swap(): lax.ppermute(block, axis, [(i, i ^ mask) for i in range(lax.axis_size(axi...  1.74 us
  transfers between devices with their start and end apart: 11, of which 4 were waited for; matrix products, arithmetic and copies ran while one was open for 0% of the time, Pallas kernels for 19%

profile of v9, /device:TPU:0, one launch (start us, length us, event | category | flops | bytes accessed | tf_op | source)
XLA Modules:
  0.0 55.8 jit_solution(4117643765310741138)
XLA Ops:
  0.0 1.6 %shard_map.82 = (bf16[1,30,16,128]{3,2,1,0:T(8,128)(2,1)S(1)}, bf16[1,30,16,128]{3,2,1,0:T(8,128)(2,1)S(1)}, bf16[1,15,16,128]{3,2,1,0:T(8,128)(2,1)S(1)}, bf16[...) custom-call(bf16[16,16,16,128]{3,2,1,0:T(8,128)(2,1)} %x_in.1, bf16[27,128,128]{2,1,0:T(8,128)(2,1)} %bitcast.50, ...), custom_call_target="tpu_custom_call" | custom-call | bytes 5242880 | tf_op jit(solution)/shard_map/pallas_call | solution.py:105
  1.6 5.1 %collective-permute-start.2 = (bf16[15,16,128]{2,1,0:T(8,128)(2,1)S(1)}, bf16[15,16,128]{2,1,0:T(8,128)(2,1)S(1)}, u32[]{:S(2)}, u32[]{:S(2)}) collective-permute-start(bf16[15,16,128]{2,1,0:T(8,128)(2,1)S(1)} %bitcast.46), channel_id=1, source_target_pairs={{0,3},{1,2},{2,1},{3,0},{4,7},{5,6},{6,5},{7,4},{8,11},{9,10},{10,... | collective-permute-start | bytes 184328 | tf_op jit(solution)/shard_map/ppermute | solution.py:46
  6.7 0.0 collective-permute-start.1
  6.7 0.6 %collective-permute-start = (bf16[30,16,128]{2,1,0:T(8,128)(2,1)S(1)}, bf16[30,16,128]{2,1,0:T(8,128)(2,1)S(1)}, u32[]{:S(2)}, u32[]{:S(2)}) collective-permute-start(bf16[30,16,128]{2,1,0:T(8,128)(2,1)S(1)} %bitcast.44), channel_id=1, source_target_pairs={{0,2},{1,3},{2,0},{3,1},{4,6},{5,7},{6,4},{7,5},{8,10},{9,11},{10,... | collective-permute-start | bytes 368648 | tf_op jit(solution)/shard_map/ppermute | solution.py:44
  7.4 4.7 %shard_map.83 = (f32[16,16,16,128]{3,2,1,0:T(8,128)S(1)}, bf16[1152,384]{1,0:T(8,128)(2,1)S(1)}, bf16[1536,256]{1,0:T(8,128)(2,1)S(1)}, bf16[108,16,128]{2,1,0:T(8,128)(2,1)S(1)}) custom-call(bf16[108,16,128]{2,1,0:T(8,128)(2,1)} %bitcast.52, bf16[18,18,16,128]{3,2,1,0:T(8,128)(2,1)S(1)} %get-tuple-element.42.x.refs_0_, ...), custom_call_target="tpu_custom_call" | custom-call | flops 3623878656 | bytes 6291456 | tf_op jit(solution)/shard_map/pallas_call | solution.py:105
  12.1 0.0 collective-permute-done.2
  12.2 1.4 %collective-permute-done.1 = bf16[30,16,128]{2,1,0:T(8,128)(2,1)S(1)} collective-permute-done((bf16[30,16,128]{2,1,0:T(8,128)(2,1)S(1)}, bf16[30,16,128]{2,1,0:T(8,128)(2,1)S(1)}, u32[]{:S(2)}, u32[]{:S(2)}) %collective-permute-start.1) | collective-permute-done | bytes 122912 | tf_op jit(solution)/shard_map/ppermute | solution.py:45
  13.5 1.6 %collective-permute-done = bf16[30,16,128]{2,1,0:T(8,128)(2,1)S(1)} collective-permute-done((bf16[30,16,128]{2,1,0:T(8,128)(2,1)S(1)}, bf16[30,16,128]{2,1,0:T(8,128)(2,1)S(1)}, u32[]{:S(2)}, u32[]{:S(2)}) %collective-permute-start) | collective-permute-done | bytes 122912 | tf_op jit(solution)/shard_map/ppermute | solution.py:44
  15.2 0.7 %collective-permute-start.3 = (bf16[55,16,128]{2,1,0:T(8,128)(2,1)S(1)}, bf16[55,16,128]{2,1,0:T(8,128)(2,1)S(1)}, u32[]{:S(2)}, u32[]{:S(2)}) collective-permute-start(bf16[55,16,128]{2,1,0:T(8,128)(2,1)S(1)} %get-tuple-element.53), channel_id=1, source_target_pairs={{4,8},{8,4},{5,9},{9,5},{6,10},{10,6},{7,11},{11,7},{20,24},{24,20... | collective-permute-start | bytes 675848 | tf_op jit(solution)/shard_map/ppermute | solution.py:63
  15.8 2.9 %collective-permute-start.4 = (bf16[55,16,128]{2,1,0:T(8,128)(2,1)S(1)}, bf16[55,16,128]{2,1,0:T(8,128)(2,1)S(1)}, u32[]{:S(2)}, u32[]{:S(2)}) collective-permute-start(bf16[55,16,128]{2,1,0:T(8,128)(2,1)S(1)} %get-tuple-element.54), channel_id=1, source_target_pairs={{0,4},{4,0},{8,12},{12,8},{1,5},{5,1},{9,13},{13,9},{2,6},{6,2},{1... | collective-permute-start | bytes 675848 | tf_op jit(solution)/shard_map/ppermute | solution.py:63
  18.8 1.5 %collective-permute-start.5 = (bf16[1,3,14,16,128]{4,3,2,1,0:T(8,128)(2,1)S(1)}, bf16[1,3,14,16,128]{4,3,2,1,0:T(8,128)(2,1)S(1)}, u32[]{:S(2)}, u32[]{:S(2)}) collective-permute-start(bf16[1,3,14,16,128]{4,3,2,1,0:T(8,128)(2,1)S(1)} %bitcast.29), channel_id=1, source_target_pairs={{0,16},{16,0},{1,17},{17,1},{2,18},{18,2},{3,19},{19,3},{4,20},{20... | collective-permute-start | bytes 516104 | tf_op jit(solution)/shard_map/ppermute | solution.py:94
  20.3 1.1 %shard_map.84 = (f32[14,16,16,128]{3,2,1,0:T(8,128)S(1)}, f32[4,16,16,128]{3,2,1,0:T(8,128)S(1)}, f32[16,128]{1,0:T(8,128)S(1)}) custom-call(f32[16,16,16,128]{3,2,1,0:T(8,128)S(1)} %get-tuple-element.45.own, bf16[1,30,16,128]{3,2,1,0:T(8,128)(2,1)S(1)} %bitcast.34, bf16[1,30,16,128]{3,2,1,0:T(8,128)(2,1)S(1)} %bitcast.32, ...), custom_call_target="tpu_custom_call" | custom-call | flops 905969664 | bytes 6291456 | tf_op jit(solution)/shard_map/pallas_call | solution.py:105
  21.4 0.0 collective-permute-done.3.refs_3_
  21.4 0.0 collective-permute-done.4.refs_4_
  21.4 2.0 %shard_map.86 = (f32[6,16,16,128]{3,2,1,0:T(8,128)S(1)}, f32[16,2,128]{2,1,0:T(2,128)S(1)}) custom-call(bf16[18,18,16,128]{3,2,1,0:T(8,128)(2,1)S(1)} %get-tuple-element.42.x.refs_0_, f32[16,128]{1,0:T(8,128)S(1)} %get-tuple-element.51.refs_1_, f32[4,16,16,128]{3,2,1,0:T(8,128)S(1)} %get-tuple-element.52.refs_2_, ...), custom_call_target="tpu_custom_call" | custom-call | flops 1811939328 | bytes 3145728 | tf_op jit(solution)/shard_map/pallas_call | solution.py:105
  23.4 0.0 copy-start.3
  23.4 0.0 copy-start.4
  23.4 1.7 %collective-permute-done.5.refs_1_ = bf16[1,3,14,16,128]{4,3,2,1,0:T(8,128)(2,1)S(1)} collective-permute-done((bf16[1,3,14,16,128]{4,3,2,1,0:T(8,128)(2,1)S(1)}, bf16[1,3,14,16,128]{4,3,2,1,0:T(8,128)(2,1)S(1)}, u32[]{:S(2)}, u32[]{:S(2)}) %collective-permute-start.5) | collective-permute-done | bytes 172064 | tf_op jit(solution)/shard_map/ppermute | solution.py:94
  25.1 0.9 %collective-permute-start.6 = (bf16[2,3,14,16,128]{4,3,2,1,0:T(8,128)(2,1)S(1)}, bf16[2,3,14,16,128]{4,3,2,1,0:T(8,128)(2,1)S(1)}, u32[]{:S(2)}, u32[]{:S(2)}) collective-permute-start(bf16[2,3,14,16,128]{4,3,2,1,0:T(8,128)(2,1)S(1)} %bitcast.27), channel_id=1, source_target_pairs={{0,8},{4,12},{8,0},{12,4},{1,9},{5,13},{9,1},{13,5},{2,10},{6,14},... | collective-permute-start | bytes 1032200 | tf_op jit(solution)/shard_map/ppermute | solution.py:94
  26.1 9.8 %all_to_all.10.stats = f32[16,2,128]{2,1,0:T(2,128)S(1)} all-to-all(f32[16,2,128]{2,1,0:T(2,128)S(1)} %get-tuple-element.59), channel_id=1, replica_groups=mesh['cand'=2,'gz'=4,'yx'=4] {'gz','yx'}, dimensions={0} | all-to-all | bytes 32768 | tf_op jit(solution)/shard_map/all_to_all | solution.py:98
  35.8 0.0 collective-permute-done.6.refs_1_
  35.9 0.2 collective-permute-start.7
  36.1 0.0 copy-done.3
  36.1 0.0 copy-done.4
  36.1 1.1 %shard_map.88 = (bf16[16,16,16,128]{3,2,1,0:T(8,128)(2,1)S(1)}, f32[10,8,8,128]{3,2,1,0:T(8,128)S(1)}, bf16[1,80,128]{2,1,0:T(8,128)(2,1)S(1)}, bf16[1,80,128]{2,1,0:T(8,128)(2,1)S(1)}, f32[1,16,128]{2,1,0:T(8,128)S(1)}) custom-call(f32[14,16,16,128]{3,2,1,0:T(8,128)S(1)} %get-tuple-element.50.inner, f32[6,16,16,128]{3,2,1,0:T(8,128)S(1)} %get-tuple-element.56.ends, ...), custom_call_target="tpu_custom_call" | custom-call | flops 10485760 | bytes 3145728 | tf_op jit(solution)/shard_map/pallas_call | solution.py:105
  37.2 0.7 %collective-permute-start.10 = (f32[16,128]{1,0:T(8,128)S(1)}, f32[16,128]{1,0:T(8,128)S(1)}, u32[]{:S(2)}, u32[]{:S(2)}) collective-permute-start(f32[16,128]{1,0:T(8,128)S(1)} %bitcast.49), channel_id=1, source_target_pairs={{0,3},{1,2},{2,1},{3,0},{4,7},{5,6},{6,5},{7,4},{8,11},{9,10},{10,... | collective-permute-start | bytes 24584 | tf_op jit(solution)/shard_map/ppermute | solution.py:46
  37.9 1.4 %collective-permute-start.8 = (bf16[80,128]{1,0:T(8,128)(2,1)S(1)}, bf16[80,128]{1,0:T(8,128)(2,1)S(1)}, u32[]{:S(2)}, u32[]{:S(2)}) collective-permute-start(bf16[80,128]{1,0:T(8,128)(2,1)S(1)} %bitcast.48), channel_id=1, source_target_pairs={{0,2},{1,3},{2,0},{3,1},{4,6},{5,7},{6,4},{7,5},{8,10},{9,11},{10,... | collective-permute-start | bytes 61448 | tf_op jit(solution)/shard_map/ppermute | solution.py:44
  39.3 2.4 %collective-permute-start.9 = (bf16[80,128]{1,0:T(8,128)(2,1)S(1)}, bf16[80,128]{1,0:T(8,128)(2,1)S(1)}, u32[]{:S(2)}, u32[]{:S(2)}) collective-permute-start(bf16[80,128]{1,0:T(8,128)(2,1)S(1)} %bitcast.47), channel_id=1, source_target_pairs={{0,1},{1,0},{2,3},{3,2},{4,5},{5,4},{6,7},{7,6},{8,9},{9,8},{10,11... | collective-permute-start | bytes 61448 | tf_op jit(solution)/shard_map/ppermute | solution.py:45
  41.7 0.0 collective-permute-done.7.refs_1_
  41.7 0.1 shard_map.90
  41.8 1.4 %shard_map.91 = (f32[2,512,128]{2,1,0:T(8,128)S(1)}, bf16[4,108,16,128]{3,2,1,0:T(8,128)(2,1)S(1)}) custom-call(f32[10,8,8,128]{3,2,1,0:T(8,128)S(1)} %get-tuple-element.62.pooled, bf16[108,16,128]{2,1,0:T(8,128)(2,1)S(1)} %get-tuple-element.63.own, bf16[8,3,14,16,128]{4,3,2,1,0:T(8,128)(2,1)S(1)} %bitcast.26), custom_call_target="tpu_custom_call" | custom-call | flops 905969664 | bytes 4194304 | tf_op jit(solution)/shard_map/pallas_call | solution.py:105
  43.2 0.0 copy-start
  43.3 0.0 copy-start.1
  43.3 0.0 copy-start.2
  43.3 0.0 collective-permute-done.10
  43.3 0.0 collective-permute-done.8
  43.3 0.2 collective-permute-done.9
  43.5 0.7 %shard_map.92 = (f32[2,512,128]{2,1,0:T(8,128)S(1)}, f32[16,2,256]{2,1,0:T(2,128)S(1)}) custom-call(f32[2,512,128]{2,1,0:T(8,128)S(1)} %get-tuple-element.65.own, bf16[1,80,128]{2,1,0:T(8,128)(2,1)S(1)} %bitcast.37, bf16[1,80,128]{2,1,0:T(8,128)(2,1)S(1)} %bitcast.38, f32[1,16,128]{2,1,0:T(8,128)S(1)} %bitcast.39, ...), custom_call_target="tpu_custom_call" | custom-call | flops 67108864 | bytes 3145728 | tf_op jit(solution)/shard_map/pallas_call | solution.py:105
  44.2 10.0 %all_to_all.11.stats = f32[16,2,256]{2,1,0:T(2,128)S(1)} all-to-all(f32[16,2,256]{2,1,0:T(2,128)S(1)} %get-tuple-element.71), channel_id=1, replica_groups=mesh['cand'=2,'gz'=4,'yx'=4] {'gz','yx'}, dimensions={0} | all-to-all | bytes 65536 | tf_op jit(solution)/shard_map/all_to_all | solution.py:98
  54.2 0.0 copy-done
  54.2 0.0 copy-done.1
  54.2 0.0 copy-done.2
  54.3 1.5 %shard_map.93 = bf16[16,16,16,128]{3,2,1,0:T(8,128)(2,1)} custom-call(f32[2,512,128]{2,1,0:T(8,128)S(1)} %get-tuple-element.70.act, f32[16,2,256]{2,1,0:T(2,128)S(1)} %all_to_all.11.stats, f32[1,256]{1,0:T(1,128)S(1)} %bitcast.40, f32[1,256]{1,0:T(1,128)S(1)} %bitcast.41, bf16[256,128]{1,0:T(8,128)(2,1)S(1)} %copy-done, ...), custom_call_target="tpu_custom_call" | custom-call | flops 67108864 | bytes 3145728 | tf_op jit(solution)/shard_map/pallas_call | solution.py:105
  (3 shorter events, 0.1 us)
Async XLA Ops:
  1.6 10.5 %collective-permute-start.2 = (bf16[15,16,128]{2,1,0:T(8,128)(2,1)S(1)}, bf16[15,16,128]{2,1,0:T(8,128)(2,1)S(1)}, u32[]{:S(2)}, u32[]{:S(2)}) collective-permute-start(bf16[15,16,128]{2,1,0:T(8,128)(2,1)S(1)} %bitcast.46), channel_id=1, source_target_pairs={{0,3},{1,2},{2,1},{3,0},{4,7},{5,6},{6,5},{7,4},{8,11},{9,10},{10,... | collective-permute-start | bytes 184328 | tf_op jit(solution)/shard_map/ppermute | solution.py:46
  6.7 6.8 %collective-permute-start.1 = (bf16[30,16,128]{2,1,0:T(8,128)(2,1)S(1)}, bf16[30,16,128]{2,1,0:T(8,128)(2,1)S(1)}, u32[]{:S(2)}, u32[]{:S(2)}) collective-permute-start(bf16[30,16,128]{2,1,0:T(8,128)(2,1)S(1)} %bitcast.45), channel_id=1, source_target_pairs={{0,1},{1,0},{2,3},{3,2},{4,5},{5,4},{6,7},{7,6},{8,9},{9,8},{10,11... | collective-permute-start | bytes 368648 | tf_op jit(solution)/shard_map/ppermute | solution.py:45
  6.7 8.4 %collective-permute-start = (bf16[30,16,128]{2,1,0:T(8,128)(2,1)S(1)}, bf16[30,16,128]{2,1,0:T(8,128)(2,1)S(1)}, u32[]{:S(2)}, u32[]{:S(2)}) collective-permute-start(bf16[30,16,128]{2,1,0:T(8,128)(2,1)S(1)} %bitcast.44), channel_id=1, source_target_pairs={{0,2},{1,3},{2,0},{3,1},{4,6},{5,7},{6,4},{7,5},{8,10},{9,11},{10,... | collective-permute-start | bytes 368648 | tf_op jit(solution)/shard_map/ppermute | solution.py:44
  15.2 6.2 %collective-permute-start.3 = (bf16[55,16,128]{2,1,0:T(8,128)(2,1)S(1)}, bf16[55,16,128]{2,1,0:T(8,128)(2,1)S(1)}, u32[]{:S(2)}, u32[]{:S(2)}) collective-permute-start(bf16[55,16,128]{2,1,0:T(8,128)(2,1)S(1)} %get-tuple-element.53), channel_id=1, source_target_pairs={{4,8},{8,4},{5,9},{9,5},{6,10},{10,6},{7,11},{11,7},{20,24},{24,20... | collective-permute-start | bytes 675848 | tf_op jit(solution)/shard_map/ppermute | solution.py:63
  15.8 5.5 %collective-permute-start.4 = (bf16[55,16,128]{2,1,0:T(8,128)(2,1)S(1)}, bf16[55,16,128]{2,1,0:T(8,128)(2,1)S(1)}, u32[]{:S(2)}, u32[]{:S(2)}) collective-permute-start(bf16[55,16,128]{2,1,0:T(8,128)(2,1)S(1)} %get-tuple-element.54), channel_id=1, source_target_pairs={{0,4},{4,0},{8,12},{12,8},{1,5},{5,1},{9,13},{13,9},{2,6},{6,2},{1... | collective-permute-start | bytes 675848 | tf_op jit(solution)/shard_map/ppermute | solution.py:63
  18.8 6.4 %collective-permute-start.5 = (bf16[1,3,14,16,128]{4,3,2,1,0:T(8,128)(2,1)S(1)}, bf16[1,3,14,16,128]{4,3,2,1,0:T(8,128)(2,1)S(1)}, u32[]{:S(2)}, u32[]{:S(2)}) collective-permute-start(bf16[1,3,14,16,128]{4,3,2,1,0:T(8,128)(2,1)S(1)} %bitcast.29), channel_id=1, source_target_pairs={{0,16},{16,0},{1,17},{17,1},{2,18},{18,2},{3,19},{19,3},{4,20},{20... | collective-permute-start | bytes 516104 | tf_op jit(solution)/shard_map/ppermute | solution.py:94
  23.4 12.7 %copy-start.3 = (f32[128]{0:T(128)S(1)}, f32[128]{0:T(128)}, u32[]{:S(2)}) copy-start(f32[128]{0:T(128)} %param.10) | copy-start | bytes 1540
  23.4 12.7 %copy-start.4 = (f32[128]{0:T(128)S(1)}, f32[128]{0:T(128)}, u32[]{:S(2)}) copy-start(f32[128]{0:T(128)} %param.11) | copy-start | bytes 1540
  25.1 10.7 %collective-permute-start.6 = (bf16[2,3,14,16,128]{4,3,2,1,0:T(8,128)(2,1)S(1)}, bf16[2,3,14,16,128]{4,3,2,1,0:T(8,128)(2,1)S(1)}, u32[]{:S(2)}, u32[]{:S(2)}) collective-permute-start(bf16[2,3,14,16,128]{4,3,2,1,0:T(8,128)(2,1)S(1)} %bitcast.27), channel_id=1, source_target_pairs={{0,8},{4,12},{8,0},{12,4},{1,9},{5,13},{9,1},{13,5},{2,10},{6,14},... | collective-permute-start | bytes 1032200 | tf_op jit(solution)/shard_map/ppermute | solution.py:94
  35.9 5.8 %collective-permute-start.7 = (bf16[4,3,14,16,128]{4,3,2,1,0:T(8,128)(2,1)S(1)}, bf16[4,3,14,16,128]{4,3,2,1,0:T(8,128)(2,1)S(1)}, u32[]{:S(2)}, u32[]{:S(2)}) collective-permute-start(bf16[4,3,14,16,128]{4,3,2,1,0:T(8,128)(2,1)S(1)} %bitcast.24), channel_id=1, source_target_pairs={{0,4},{4,0},{8,12},{12,8},{1,5},{5,1},{9,13},{13,9},{2,6},{6,2},{1... | collective-permute-start | bytes 2064392 | tf_op jit(solution)/shard_map/ppermute | solution.py:94
  37.2 6.0 %collective-permute-start.10 = (f32[16,128]{1,0:T(8,128)S(1)}, f32[16,128]{1,0:T(8,128)S(1)}, u32[]{:S(2)}, u32[]{:S(2)}) collective-permute-start(f32[16,128]{1,0:T(8,128)S(1)} %bitcast.49), channel_id=1, source_target_pairs={{0,3},{1,2},{2,1},{3,0},{4,7},{5,6},{6,5},{7,4},{8,11},{9,10},{10,... | collective-permute-start | bytes 24584 | tf_op jit(solution)/shard_map/ppermute | solution.py:46
  37.9 5.4 %collective-permute-start.8 = (bf16[80,128]{1,0:T(8,128)(2,1)S(1)}, bf16[80,128]{1,0:T(8,128)(2,1)S(1)}, u32[]{:S(2)}, u32[]{:S(2)}) collective-permute-start(bf16[80,128]{1,0:T(8,128)(2,1)S(1)} %bitcast.48), channel_id=1, source_target_pairs={{0,2},{1,3},{2,0},{3,1},{4,6},{5,7},{6,4},{7,5},{8,10},{9,11},{10,... | collective-permute-start | bytes 61448 | tf_op jit(solution)/shard_map/ppermute | solution.py:44
  39.3 4.2 %collective-permute-start.9 = (bf16[80,128]{1,0:T(8,128)(2,1)S(1)}, bf16[80,128]{1,0:T(8,128)(2,1)S(1)}, u32[]{:S(2)}, u32[]{:S(2)}) collective-permute-start(bf16[80,128]{1,0:T(8,128)(2,1)S(1)} %bitcast.47), channel_id=1, source_target_pairs={{0,1},{1,0},{2,3},{3,2},{4,5},{5,4},{6,7},{7,6},{8,9},{9,8},{10,11... | collective-permute-start | bytes 61448 | tf_op jit(solution)/shard_map/ppermute | solution.py:45
  43.2 11.0 %copy-start = (bf16[256,128]{1,0:T(8,128)(2,1)S(1)}, bf16[256,128]{1,0:T(8,128)(2,1)}, u32[]{:S(2)}) copy-start(bf16[256,128]{1,0:T(8,128)(2,1)} %up.1) | copy-start | bytes 196612
  43.3 11.0 %copy-start.1 = (f32[256]{0:T(256)S(1)}, f32[256]{0:T(256)}, u32[]{:S(2)}) copy-start(f32[256]{0:T(256)} %param.13) | copy-start | bytes 3076
  43.3 11.0 %copy-start.2 = (f32[256]{0:T(256)S(1)}, f32[256]{0:T(256)}, u32[]{:S(2)}) copy-start(f32[256]{0:T(256)} %param.14) | copy-start | bytes 3076

commit v10 on v9

--- a/solution.py
+++ b/solution.py
@@ -113,10 +113,10 @@
     )(*far, *near)
 
 
-def start_kernel(ny, nx, size, x_in, w_in, d_in, y_out, x_out, corners, x, w, lines, sems):
+def start_kernel(ny, size, x_in, w_in, d_in, y_out, rider, x, w, sems):
     edge = x_in.shape[0]
-    f32, bf16 = jnp.float32, jnp.bfloat16
-    above, left = Square().low_sides()
+    bf16 = jnp.bfloat16
+    above, _ = Square().low_sides()
     chunks = 4
     planes = edge // chunks
     first = [
@@ -130,13 +130,8 @@
     later = []
     if size:
         at = jnp.minimum(Riders.mine() * size, d_in.shape[0] - size)
-        for k, (out, begin) in enumerate(((y_out, edge), (x_out, edge), (corners, 1))):
-            later.append(
-                pltpu.make_async_copy(
-                    d_in.at[pl.ds(at, size)], out.at[0, pl.ds(begin, size)], sems.at[chunks + k]
-                )
-            )
-    later.append(pltpu.make_async_copy(w_in, w, sems.at[chunks + 3]))
+        later.append(pltpu.make_async_copy(d_in.at[pl.ds(at, size)], rider, sems.at[chunks]))
+    later.append(pltpu.make_async_copy(w_in, w, sems.at[chunks + 1]))
     for copy in first + later:
         copy.start()
     x[0] = jnp.zeros(x.shape[1:], bf16)
@@ -144,20 +139,33 @@
     blank = jnp.zeros((edge,) + x.shape[2:], bf16)
     x[1 : edge + 1, 0] = blank
     x[1 : edge + 1, edge + 1] = blank
-    flat = lines.reshape(nx * edge * edge * 8, 128)
-    part = planes * edge
+    if not size:
+        rider[...] = jnp.zeros(rider.shape, bf16)
     for k in range(chunks):
         first[k].wait()
         at, here = pl.ds(k * planes, planes), pl.ds(1 + k * planes, planes)
         for i in range(ny):
-            row = jnp.where(above[i], 1, edge)
-            y_out[i, at] = x[here, row]
+            y_out[i, at] = x[here, jnp.where(above[i], 1, edge)]
+    for copy in later:
+        copy.wait()
+    if size:
+        y_out[0, edge : edge + size] = rider[...]
+
+
+def flank_kernel(ny, nx, size, x, rider, x_out, corners, lines):
+    edge = x.shape[2]
+    f32, bf16 = jnp.float32, jnp.bfloat16
+    above, left = Square().low_sides()
+    flat = lines.reshape(nx * edge * edge * 8, 128)
+    planes = edge // 4
+    part = planes * edge
+    for k in range(4):
+        at, here = pl.ds(k * planes, planes), pl.ds(1 + k * planes, planes)
         for j in range(nx):
             low = x[here, 1 : edge + 1, 0:8].astype(f32).reshape(part, 8, 128)
             high = x[here, 1 : edge + 1, edge - 8 : edge].astype(f32).reshape(part, 8, 128)
             high = pltpu.roll(high, 1, 1)
-            kept = jnp.where(left[j], low, high)
-            lines[j, k * part : k * part + part] = kept
+            lines[j, k * part : k * part + part] = jnp.where(left[j], low, high)
             begin = (j * edge * edge + k * part) * 8
             column = flat[pl.ds(begin, part, stride=8), :]
             x_out[j, at] = column.astype(bf16).reshape(planes, edge, 128)
@@ -166,10 +174,10 @@
             begin = j * edge * edge * 8
             low = flat[pl.ds(begin, edge, stride=8 * edge), :]
             high = flat[pl.ds(begin + 8 * (edge - 1), edge, stride=8 * edge), :]
-            kept = jnp.where(above[i], low, high)
-            corners[i * nx + j, 0] = kept.astype(bf16)
-    for copy in later:
-        copy.wait()
+            corners[i * nx + j, 0] = jnp.where(above[i], low, high).astype(bf16)
+    if size:
+        x_out[0, edge : edge + size] = rider[...]
+        corners[0, 1 : 1 + size] = rider[...]
 
 
 def face_kernel(ny, nx, size, x, y_halos, x_halos, corners, outer, inner, *riders):
@@ -693,22 +701,33 @@
 
     own = jnp.moveaxis(deep_weight, 4, 3).reshape(-1, 16, channels)
     conv_weight = conv_weight.reshape(27, channels, channels)
-    *edges, field, conv_weight = call(
-        functools.partial(start_kernel, ny, nx, riders.size),
+    y, rider, field, conv_weight = call(
+        functools.partial(start_kernel, ny, riders.size),
         [
             ((ny, edge + riders.size, edge, channels), bf16),
-            ((nx, edge + riders.size, edge, channels), bf16),
-            ((ny * nx, 1 + riders.size, edge, channels), bf16),
+            ((max(riders.size, 1), 16, channels), bf16),
             ((edge + 2, edge + 2, edge, channels), bf16),
             (conv_weight.shape, bf16),
         ],
-        [((nx, edge * edge, 8, channels), f32), pltpu.SemaphoreType.DMA((8,))],
+        [pltpu.SemaphoreType.DMA((6,))],
         features,
         conv_weight,
         own,
         nbytes=5 << 20,
         in_hbm=3,
     )
+    x, corner = call(
+        functools.partial(flank_kernel, ny, nx, riders.size),
+        [
+            ((nx, edge + riders.size, edge, channels), bf16),
+            ((ny * nx, 1 + riders.size, edge, channels), bf16),
+        ],
+        [((nx, edge * edge, 8, channels), f32)],
+        field,
+        rider,
+        nbytes=2 << 20,
+    )
+    edges = y, x, corner
     halos = square.halos(*(list(piece) for piece in edges))
     conv_flops = 54 * channels * channels * edge**3
     act, taps, pairs, own = call(
@@ -744,6 +763,9 @@
     if riders.size:
         held = held[0][None]
         other = swap(held, *riders.STEPS[0])
+        act, other = lax.optimization_barrier((act, other))
+        held = stack(held, other).reshape((-1,) + held.shape[1:])
+        other = swap(held, *riders.STEPS[1])
     else:
         held = rotate_shards(own)
     six = ((6, edge, edge, channels), f32)
@@ -782,17 +804,12 @@
         flops=conv_flops // 2,
         nbytes=3 << 20,
     )
+    stats = share(stats)
     if riders.size:
-        stats, other = lax.optimization_barrier((stats, other))
-        held = stack(held, other).reshape((-1,) + held.shape[1:])
-        other = swap(held, *riders.STEPS[1])
-        stats = share(stats)
         stats, other = lax.optimization_barrier((stats, other))
         held = stack(held, other).reshape((-1,) + held.shape[1:])
         other = swap(held, *riders.STEPS[2])
         held = [stack(held, other).reshape((-1,) + held.shape[1:])]
-    else:
-        stats = share(stats)
     out, pooled, *edges = call(
         functools.partial(norm_kernel, ny, nx),
         [

time: 56 us -> 57.7 us (1.030)
  blocking collectives: 19.8 us -> 22.7 us
  waiting for transfers between devices: 4.89 us -> 2.71 us
  starting transfers between devices: 16.5 us -> 17.3 us
    ppermute x2, starting transfers between devices: 5.77 us -> 2.07 us  [halos(): corner = lax.ppermute(corners[0], 'yx', self.swap_route(3))]
    ppermute x2, starting transfers between devices: 2.05 us -> 5.51 us  [halos(): y = lax.ppermute(y_edges[0], 'yx', self.swap_route(2))]
    all_to_all x2, blocking collectives: 19.8 us -> 22.7 us  [share(): return lax.all_to_all(stats, PART, 0, 0)]
    ppermute x3, waiting for transfers between devices: 1.74 us -> 0.27 us  [swap(): lax.ppermute(block, axis, [(i, i ^ mask) for i in range(lax.axis_size(axi...]
    ppermute x3, starting transfers between devices: 2.63 us -> 3.42 us  [swap(): lax.ppermute(block, axis, [(i, i ^ mask) for i in range(lax.axis_size(axi...]
    ppermute x2, waiting for transfers between devices: 1.59 us -> 0.93 us  [halos(): y = lax.ppermute(y_edges[0], 'yx', self.swap_route(2))]
    pallas_call x9 -> x10, Pallas kernels: 14.3 us -> 14.5 us  [call(): pl.pallas_call(kernel, out_shape=[jax.ShapeDtypeStruct(shape, dtype) for...]
  transfers between devices with their start and end apart: 11 -> 11, of which waited for: 4 -> 5; matrix products, arithmetic and copies ran while one was open for 0% -> 0% of each run, Pallas kernels for 19% -> 19%
where the time goes in v10:
time: 57.7 us; the launch traced here: 57.5 us
  blocking collectives  22.7 us (39%)
  starting transfers between devices  17.3 us (30%)
  Pallas kernels  14.6 us (25%)
  waiting for transfers between devices  2.71 us (5%)
    all_to_all x2, blocking collectives, share(): return lax.all_to_all(stats, PART, 0, 0)  22.7 us
    pallas_call x10, Pallas kernels, call(): pl.pallas_call(kernel, out_shape=[jax.ShapeDtypeStruct(shape, dtype) for...  14.5 us
    ppermute x2, starting transfers between devices, halos(): y = lax.ppermute(y_edges[0], 'yx', self.swap_route(2))  5.51 us
    ppermute x3, starting transfers between devices, swap(): lax.ppermute(block, axis, [(i, i ^ mask) for i in range(lax.axis_size(axi...  3.42 us
    ppermute x1, starting transfers between devices, swap_depth(): lax.ppermute(inner, 'gz', routes[0])  2.9 us
    ppermute x2, starting transfers between devices, halos(): x = lax.ppermute(x_edges[0], 'yx', self.swap_route(1))  2.72 us
    ppermute x2, starting transfers between devices, halos(): corner = lax.ppermute(corners[0], 'yx', self.swap_route(3))  2.07 us
  transfers between devices with their start and end apart: 11, of which 5 were waited for; matrix products, arithmetic and copies ran while one was open for 0% of the time, Pallas kernels for 19%

profile of v10, /device:TPU:0, one launch (start us, length us, event | category | flops | bytes accessed | tf_op | source)
XLA Modules:
  0.0 57.5 jit_solution(2308457671204490848)
XLA Ops:
  0.0 1.6 %shard_map.82 = (bf16[1,30,16,128]{3,2,1,0:T(8,128)(2,1)S(1)}, bf16[14,16,128]{2,1,0:T(8,128)(2,1)S(1)}, bf16[18,18,16,128]{3,2,1,0:T(8,128)(2,1)S(1)}, bf16[27,128,128]{2,1,0:T(8,128)(2,1)S(1)}) custom-call(bf16[16,16,16,128]{3,2,1,0:T(8,128)(2,1)} %x_in.1, bf16[27,128,128]{2,1,0:T(8,128)(2,1)} %bitcast.50, bf16[108,16,128]{2,1,0:T(8,128)(2,1)} %bitcast.51), custom_call_target="tpu_custom_call" | custom-call | bytes 5242880 | tf_op jit(solution)/shard_map/pallas_call | solution.py:105
  1.6 4.1 %collective-permute-start = (bf16[30,16,128]{2,1,0:T(8,128)(2,1)S(1)}, bf16[30,16,128]{2,1,0:T(8,128)(2,1)S(1)}, u32[]{:S(2)}, u32[]{:S(2)}) collective-permute-start(bf16[30,16,128]{2,1,0:T(8,128)(2,1)S(1)} %bitcast.44), channel_id=1, source_target_pairs={{0,2},{1,3},{2,0},{3,1},{4,6},{5,7},{6,4},{7,5},{8,10},{9,11},{10,... | collective-permute-start | bytes 368648 | tf_op jit(solution)/shard_map/ppermute | solution.py:44
  5.7 0.3 shard_map.83
  5.9 1.4 %collective-permute-start.2 = (bf16[15,16,128]{2,1,0:T(8,128)(2,1)S(1)}, bf16[15,16,128]{2,1,0:T(8,128)(2,1)S(1)}, u32[]{:S(2)}, u32[]{:S(2)}) collective-permute-start(bf16[15,16,128]{2,1,0:T(8,128)(2,1)S(1)} %bitcast.46), channel_id=1, source_target_pairs={{0,3},{1,2},{2,1},{3,0},{4,7},{5,6},{6,5},{7,4},{8,11},{9,10},{10,... | collective-permute-start | bytes 184328 | tf_op jit(solution)/shard_map/ppermute | solution.py:46
  7.4 0.3 collective-permute-start.1
  7.7 4.7 %shard_map.84 = (f32[16,16,16,128]{3,2,1,0:T(8,128)S(1)}, bf16[1152,384]{1,0:T(8,128)(2,1)S(1)}, bf16[1536,256]{1,0:T(8,128)(2,1)S(1)}, bf16[108,16,128]{2,1,0:T(8,128)(2,1)S(1)}) custom-call(bf16[108,16,128]{2,1,0:T(8,128)(2,1)} %bitcast.52, bf16[18,18,16,128]{3,2,1,0:T(8,128)(2,1)S(1)} %get-tuple-element.41.x.refs_0_, ...), custom_call_target="tpu_custom_call" | custom-call | flops 3623878656 | bytes 6291456 | tf_op jit(solution)/shard_map/pallas_call | solution.py:105
  12.4 0.4 collective-permute-done.2
  12.7 0.9 %collective-permute-done = bf16[30,16,128]{2,1,0:T(8,128)(2,1)S(1)} collective-permute-done((bf16[30,16,128]{2,1,0:T(8,128)(2,1)S(1)}, bf16[30,16,128]{2,1,0:T(8,128)(2,1)S(1)}, u32[]{:S(2)}, u32[]{:S(2)}) %collective-permute-start) | collective-permute-done | bytes 122912 | tf_op jit(solution)/shard_map/ppermute | solution.py:44
  13.7 1.0 %collective-permute-done.1 = bf16[30,16,128]{2,1,0:T(8,128)(2,1)S(1)} collective-permute-done((bf16[30,16,128]{2,1,0:T(8,128)(2,1)S(1)}, bf16[30,16,128]{2,1,0:T(8,128)(2,1)S(1)}, u32[]{:S(2)}, u32[]{:S(2)}) %collective-permute-start.1) | collective-permute-done | bytes 122912 | tf_op jit(solution)/shard_map/ppermute | solution.py:45
  14.7 1.6 %collective-permute-start.3 = (bf16[1,3,14,16,128]{4,3,2,1,0:T(8,128)(2,1)S(1)}, bf16[1,3,14,16,128]{4,3,2,1,0:T(8,128)(2,1)S(1)}, u32[]{:S(2)}, u32[]{:S(2)}) collective-permute-start(bf16[1,3,14,16,128]{4,3,2,1,0:T(8,128)(2,1)S(1)} %bitcast.29), channel_id=1, source_target_pairs={{0,16},{16,0},{1,17},{17,1},{2,18},{18,2},{3,19},{19,3},{4,20},{20... | collective-permute-start | bytes 516104 | tf_op jit(solution)/shard_map/ppermute | solution.py:94
  16.3 0.7 %collective-permute-start.4 = (bf16[55,16,128]{2,1,0:T(8,128)(2,1)S(1)}, bf16[55,16,128]{2,1,0:T(8,128)(2,1)S(1)}, u32[]{:S(2)}, u32[]{:S(2)}) collective-permute-start(bf16[55,16,128]{2,1,0:T(8,128)(2,1)S(1)} %get-tuple-element.57), channel_id=1, source_target_pairs={{4,8},{8,4},{5,9},{9,5},{6,10},{10,6},{7,11},{11,7},{20,24},{24,20... | collective-permute-start | bytes 675848 | tf_op jit(solution)/shard_map/ppermute | solution.py:63
  17.0 2.9 %collective-permute-start.5 = (bf16[55,16,128]{2,1,0:T(8,128)(2,1)S(1)}, bf16[55,16,128]{2,1,0:T(8,128)(2,1)S(1)}, u32[]{:S(2)}, u32[]{:S(2)}) collective-permute-start(bf16[55,16,128]{2,1,0:T(8,128)(2,1)S(1)} %get-tuple-element.58), channel_id=1, source_target_pairs={{0,4},{4,0},{8,12},{12,8},{1,5},{5,1},{9,13},{13,9},{2,6},{6,2},{1... | collective-permute-start | bytes 675848 | tf_op jit(solution)/shard_map/ppermute | solution.py:63
  19.9 0.3 collective-permute-done.3.refs_1_
  20.2 1.6 %collective-permute-start.6 = (bf16[2,3,14,16,128]{4,3,2,1,0:T(8,128)(2,1)S(1)}, bf16[2,3,14,16,128]{4,3,2,1,0:T(8,128)(2,1)S(1)}, u32[]{:S(2)}, u32[]{:S(2)}) collective-permute-start(bf16[2,3,14,16,128]{4,3,2,1,0:T(8,128)(2,1)S(1)} %bitcast.27), channel_id=1, source_target_pairs={{0,8},{4,12},{8,0},{12,4},{1,9},{5,13},{9,1},{13,5},{2,10},{6,14},... | collective-permute-start | bytes 1032200 | tf_op jit(solution)/shard_map/ppermute | solution.py:94
  21.8 1.0 %shard_map.86 = (f32[14,16,16,128]{3,2,1,0:T(8,128)S(1)}, f32[4,16,16,128]{3,2,1,0:T(8,128)S(1)}, f32[16,128]{1,0:T(8,128)S(1)}) custom-call(f32[16,16,16,128]{3,2,1,0:T(8,128)S(1)} %get-tuple-element.52.own, bf16[1,30,16,128]{3,2,1,0:T(8,128)(2,1)S(1)} %bitcast.32, bf16[1,30,16,128]{3,2,1,0:T(8,128)(2,1)S(1)} %bitcast.34, ...), custom_call_target="tpu_custom_call" | custom-call | flops 905969664 | bytes 6291456 | tf_op jit(solution)/shard_map/pallas_call | solution.py:105
  22.8 0.0 collective-permute-done.4.refs_3_
  22.9 0.0 collective-permute-done.5.refs_4_
  22.9 0.0 copy-start.3
  22.9 0.0 copy-start.4
  22.9 2.0 %shard_map.87 = (f32[6,16,16,128]{3,2,1,0:T(8,128)S(1)}, f32[16,2,128]{2,1,0:T(2,128)S(1)}) custom-call(bf16[18,18,16,128]{3,2,1,0:T(8,128)(2,1)S(1)} %get-tuple-element.41.x.refs_0_, f32[16,128]{1,0:T(8,128)S(1)} %get-tuple-element.55.refs_1_, f32[4,16,16,128]{3,2,1,0:T(8,128)S(1)} %get-tuple-element.56.refs_2_, ...), custom_call_target="tpu_custom_call" | custom-call | flops 1811939328 | bytes 3145728 | tf_op jit(solution)/shard_map/pallas_call | solution.py:105
  24.9 12.6 %all_to_all.10.stats = f32[16,2,128]{2,1,0:T(2,128)S(1)} all-to-all(f32[16,2,128]{2,1,0:T(2,128)S(1)} %get-tuple-element.61), channel_id=1, replica_groups=mesh['cand'=2,'gz'=4,'yx'=4] {'gz','yx'}, dimensions={0} | all-to-all | bytes 32768 | tf_op jit(solution)/shard_map/all_to_all | solution.py:98
  37.6 0.0 collective-permute-done.6.refs_1_
  37.6 0.2 collective-permute-start.7
  37.8 0.0 copy-done.3
  37.8 0.0 copy-done.4
  37.8 1.1 %shard_map.89 = (bf16[16,16,16,128]{3,2,1,0:T(8,128)(2,1)S(1)}, f32[10,8,8,128]{3,2,1,0:T(8,128)S(1)}, bf16[1,80,128]{2,1,0:T(8,128)(2,1)S(1)}, bf16[1,80,128]{2,1,0:T(8,128)(2,1)S(1)}, f32[1,16,128]{2,1,0:T(8,128)S(1)}) custom-call(f32[14,16,16,128]{3,2,1,0:T(8,128)S(1)} %get-tuple-element.54.inner, f32[6,16,16,128]{3,2,1,0:T(8,128)S(1)} %get-tuple-element.60.ends, ...), custom_call_target="tpu_custom_call" | custom-call | flops 10485760 | bytes 3145728 | tf_op jit(solution)/shard_map/pallas_call | solution.py:105
  39.0 0.7 %collective-permute-start.10 = (f32[16,128]{1,0:T(8,128)S(1)}, f32[16,128]{1,0:T(8,128)S(1)}, u32[]{:S(2)}, u32[]{:S(2)}) collective-permute-start(f32[16,128]{1,0:T(8,128)S(1)} %bitcast.49), channel_id=1, source_target_pairs={{0,3},{1,2},{2,1},{3,0},{4,7},{5,6},{6,5},{7,4},{8,11},{9,10},{10,... | collective-permute-start | bytes 24584 | tf_op jit(solution)/shard_map/ppermute | solution.py:46
  39.6 1.4 %collective-permute-start.8 = (bf16[80,128]{1,0:T(8,128)(2,1)S(1)}, bf16[80,128]{1,0:T(8,128)(2,1)S(1)}, u32[]{:S(2)}, u32[]{:S(2)}) collective-permute-start(bf16[80,128]{1,0:T(8,128)(2,1)S(1)} %bitcast.48), channel_id=1, source_target_pairs={{0,2},{1,3},{2,0},{3,1},{4,6},{5,7},{6,4},{7,5},{8,10},{9,11},{10,... | collective-permute-start | bytes 61448 | tf_op jit(solution)/shard_map/ppermute | solution.py:44
  41.0 2.4 %collective-permute-start.9 = (bf16[80,128]{1,0:T(8,128)(2,1)S(1)}, bf16[80,128]{1,0:T(8,128)(2,1)S(1)}, u32[]{:S(2)}, u32[]{:S(2)}) collective-permute-start(bf16[80,128]{1,0:T(8,128)(2,1)S(1)} %bitcast.47), channel_id=1, source_target_pairs={{0,1},{1,0},{2,3},{3,2},{4,5},{5,4},{6,7},{7,6},{8,9},{9,8},{10,11... | collective-permute-start | bytes 61448 | tf_op jit(solution)/shard_map/ppermute | solution.py:45
  43.4 0.0 collective-permute-done.7.refs_1_
  43.4 0.1 shard_map.91
  43.5 1.4 %shard_map.92 = (f32[2,512,128]{2,1,0:T(8,128)S(1)}, bf16[4,108,16,128]{3,2,1,0:T(8,128)(2,1)S(1)}) custom-call(f32[10,8,8,128]{3,2,1,0:T(8,128)S(1)} %get-tuple-element.64.pooled, bf16[108,16,128]{2,1,0:T(8,128)(2,1)S(1)} %get-tuple-element.65.own, bf16[8,3,14,16,128]{4,3,2,1,0:T(8,128)(2,1)S(1)} %bitcast.26), custom_call_target="tpu_custom_call" | custom-call | flops 905969664 | bytes 4194304 | tf_op jit(solution)/shard_map/pallas_call | solution.py:105
  45.0 0.0 copy-start
  45.0 0.0 copy-start.1
  45.0 0.0 copy-start.2
  45.0 0.0 collective-permute-done.10
  45.0 0.0 collective-permute-done.8
  45.0 0.2 collective-permute-done.9
  45.2 0.7 %shard_map.93 = (f32[2,512,128]{2,1,0:T(8,128)S(1)}, f32[16,2,256]{2,1,0:T(2,128)S(1)}) custom-call(f32[2,512,128]{2,1,0:T(8,128)S(1)} %get-tuple-element.67.own, bf16[1,80,128]{2,1,0:T(8,128)(2,1)S(1)} %bitcast.37, bf16[1,80,128]{2,1,0:T(8,128)(2,1)S(1)} %bitcast.38, f32[1,16,128]{2,1,0:T(8,128)S(1)} %bitcast.39, ...), custom_call_target="tpu_custom_call" | custom-call | flops 67108864 | bytes 3145728 | tf_op jit(solution)/shard_map/pallas_call | solution.py:105
  45.9 10.0 %all_to_all.11.stats = f32[16,2,256]{2,1,0:T(2,128)S(1)} all-to-all(f32[16,2,256]{2,1,0:T(2,128)S(1)} %get-tuple-element.73), channel_id=1, replica_groups=mesh['cand'=2,'gz'=4,'yx'=4] {'gz','yx'}, dimensions={0} | all-to-all | bytes 65536 | tf_op jit(solution)/shard_map/all_to_all | solution.py:98
  56.0 0.0 copy-done
  56.0 0.0 copy-done.1
  56.0 0.0 copy-done.2
  56.0 1.5 %shard_map.94 = bf16[16,16,16,128]{3,2,1,0:T(8,128)(2,1)} custom-call(f32[2,512,128]{2,1,0:T(8,128)S(1)} %get-tuple-element.72.act, f32[16,2,256]{2,1,0:T(2,128)S(1)} %all_to_all.11.stats, f32[1,256]{1,0:T(1,128)S(1)} %bitcast.40, f32[1,256]{1,0:T(1,128)S(1)} %bitcast.41, bf16[256,128]{1,0:T(8,128)(2,1)S(1)} %copy-done, ...), custom_call_target="tpu_custom_call" | custom-call | flops 67108864 | bytes 3145728 | tf_op jit(solution)/shard_map/pallas_call | solution.py:105
  (3 shorter events, 0.1 us)
Async XLA Ops:
  1.6 12.1 %collective-permute-start = (bf16[30,16,128]{2,1,0:T(8,128)(2,1)S(1)}, bf16[30,16,128]{2,1,0:T(8,128)(2,1)S(1)}, u32[]{:S(2)}, u32[]{:S(2)}) collective-permute-start(bf16[30,16,128]{2,1,0:T(8,128)(2,1)S(1)} %bitcast.44), channel_id=1, source_target_pairs={{0,2},{1,3},{2,0},{3,1},{4,6},{5,7},{6,4},{7,5},{8,10},{9,11},{10,... | collective-permute-start | bytes 368648 | tf_op jit(solution)/shard_map/ppermute | solution.py:44
  5.9 6.8 %collective-permute-start.2 = (bf16[15,16,128]{2,1,0:T(8,128)(2,1)S(1)}, bf16[15,16,128]{2,1,0:T(8,128)(2,1)S(1)}, u32[]{:S(2)}, u32[]{:S(2)}) collective-permute-start(bf16[15,16,128]{2,1,0:T(8,128)(2,1)S(1)} %bitcast.46), channel_id=1, source_target_pairs={{0,3},{1,2},{2,1},{3,0},{4,7},{5,6},{6,5},{7,4},{8,11},{9,10},{10,... | collective-permute-start | bytes 184328 | tf_op jit(solution)/shard_map/ppermute | solution.py:46
  7.4 7.3 %collective-permute-start.1 = (bf16[30,16,128]{2,1,0:T(8,128)(2,1)S(1)}, bf16[30,16,128]{2,1,0:T(8,128)(2,1)S(1)}, u32[]{:S(2)}, u32[]{:S(2)}) collective-permute-start(bf16[30,16,128]{2,1,0:T(8,128)(2,1)S(1)} %bitcast.45), channel_id=1, source_target_pairs={{0,1},{1,0},{2,3},{3,2},{4,5},{5,4},{6,7},{7,6},{8,9},{9,8},{10,11... | collective-permute-start | bytes 368648 | tf_op jit(solution)/shard_map/ppermute | solution.py:45
  14.7 5.5 %collective-permute-start.3 = (bf16[1,3,14,16,128]{4,3,2,1,0:T(8,128)(2,1)S(1)}, bf16[1,3,14,16,128]{4,3,2,1,0:T(8,128)(2,1)S(1)}, u32[]{:S(2)}, u32[]{:S(2)}) collective-permute-start(bf16[1,3,14,16,128]{4,3,2,1,0:T(8,128)(2,1)S(1)} %bitcast.29), channel_id=1, source_target_pairs={{0,16},{16,0},{1,17},{17,1},{2,18},{18,2},{3,19},{19,3},{4,20},{20... | collective-permute-start | bytes 516104 | tf_op jit(solution)/shard_map/ppermute | solution.py:94
  16.3 6.5 %collective-permute-start.4 = (bf16[55,16,128]{2,1,0:T(8,128)(2,1)S(1)}, bf16[55,16,128]{2,1,0:T(8,128)(2,1)S(1)}, u32[]{:S(2)}, u32[]{:S(2)}) collective-permute-start(bf16[55,16,128]{2,1,0:T(8,128)(2,1)S(1)} %get-tuple-element.57), channel_id=1, source_target_pairs={{4,8},{8,4},{5,9},{9,5},{6,10},{10,6},{7,11},{11,7},{20,24},{24,20... | collective-permute-start | bytes 675848 | tf_op jit(solution)/shard_map/ppermute | solution.py:63
  17.0 5.9 %collective-permute-start.5 = (bf16[55,16,128]{2,1,0:T(8,128)(2,1)S(1)}, bf16[55,16,128]{2,1,0:T(8,128)(2,1)S(1)}, u32[]{:S(2)}, u32[]{:S(2)}) collective-permute-start(bf16[55,16,128]{2,1,0:T(8,128)(2,1)S(1)} %get-tuple-element.58), channel_id=1, source_target_pairs={{0,4},{4,0},{8,12},{12,8},{1,5},{5,1},{9,13},{13,9},{2,6},{6,2},{1... | collective-permute-start | bytes 675848 | tf_op jit(solution)/shard_map/ppermute | solution.py:63
  20.2 17.4 %collective-permute-start.6 = (bf16[2,3,14,16,128]{4,3,2,1,0:T(8,128)(2,1)S(1)}, bf16[2,3,14,16,128]{4,3,2,1,0:T(8,128)(2,1)S(1)}, u32[]{:S(2)}, u32[]{:S(2)}) collective-permute-start(bf16[2,3,14,16,128]{4,3,2,1,0:T(8,128)(2,1)S(1)} %bitcast.27), channel_id=1, source_target_pairs={{0,8},{4,12},{8,0},{12,4},{1,9},{5,13},{9,1},{13,5},{2,10},{6,14},... | collective-permute-start | bytes 1032200 | tf_op jit(solution)/shard_map/ppermute | solution.py:94
  22.9 14.9 %copy-start.3 = (f32[128]{0:T(128)S(1)}, f32[128]{0:T(128)}, u32[]{:S(2)}) copy-start(f32[128]{0:T(128)} %param.10) | copy-start | bytes 1540
  22.9 14.9 %copy-start.4 = (f32[128]{0:T(128)S(1)}, f32[128]{0:T(128)}, u32[]{:S(2)}) copy-start(f32[128]{0:T(128)} %param.11) | copy-start | bytes 1540
  37.6 5.8 %collective-permute-start.7 = (bf16[4,3,14,16,128]{4,3,2,1,0:T(8,128)(2,1)S(1)}, bf16[4,3,14,16,128]{4,3,2,1,0:T(8,128)(2,1)S(1)}, u32[]{:S(2)}, u32[]{:S(2)}) collective-permute-start(bf16[4,3,14,16,128]{4,3,2,1,0:T(8,128)(2,1)S(1)} %bitcast.24), channel_id=1, source_target_pairs={{0,4},{4,0},{8,12},{12,8},{1,5},{5,1},{9,13},{13,9},{2,6},{6,2},{1... | collective-permute-start | bytes 2064392 | tf_op jit(solution)/shard_map/ppermute | solution.py:94
  39.0 6.0 %collective-permute-start.10 = (f32[16,128]{1,0:T(8,128)S(1)}, f32[16,128]{1,0:T(8,128)S(1)}, u32[]{:S(2)}, u32[]{:S(2)}) collective-permute-start(f32[16,128]{1,0:T(8,128)S(1)} %bitcast.49), channel_id=1, source_target_pairs={{0,3},{1,2},{2,1},{3,0},{4,7},{5,6},{6,5},{7,4},{8,11},{9,10},{10,... | collective-permute-start | bytes 24584 | tf_op jit(solution)/shard_map/ppermute | solution.py:46
  39.6 5.4 %collective-permute-start.8 = (bf16[80,128]{1,0:T(8,128)(2,1)S(1)}, bf16[80,128]{1,0:T(8,128)(2,1)S(1)}, u32[]{:S(2)}, u32[]{:S(2)}) collective-permute-start(bf16[80,128]{1,0:T(8,128)(2,1)S(1)} %bitcast.48), channel_id=1, source_target_pairs={{0,2},{1,3},{2,0},{3,1},{4,6},{5,7},{6,4},{7,5},{8,10},{9,11},{10,... | collective-permute-start | bytes 61448 | tf_op jit(solution)/shard_map/ppermute | solution.py:44
  41.0 4.2 %collective-permute-start.9 = (bf16[80,128]{1,0:T(8,128)(2,1)S(1)}, bf16[80,128]{1,0:T(8,128)(2,1)S(1)}, u32[]{:S(2)}, u32[]{:S(2)}) collective-permute-start(bf16[80,128]{1,0:T(8,128)(2,1)S(1)} %bitcast.47), channel_id=1, source_target_pairs={{0,1},{1,0},{2,3},{3,2},{4,5},{5,4},{6,7},{7,6},{8,9},{9,8},{10,11... | collective-permute-start | bytes 61448 | tf_op jit(solution)/shard_map/ppermute | solution.py:45
  45.0 11.0 %copy-start = (bf16[256,128]{1,0:T(8,128)(2,1)S(1)}, bf16[256,128]{1,0:T(8,128)(2,1)}, u32[]{:S(2)}) copy-start(bf16[256,128]{1,0:T(8,128)(2,1)} %up.1) | copy-start | bytes 196612
  45.0 11.0 %copy-start.1 = (f32[256]{0:T(256)S(1)}, f32[256]{0:T(256)}, u32[]{:S(2)}) copy-start(f32[256]{0:T(256)} %param.13) | copy-start | bytes 3076
  45.0 11.0 %copy-start.2 = (f32[256]{0:T(256)S(1)}, f32[256]{0:T(256)}, u32[]{:S(2)}) copy-start(f32[256]{0:T(256)} %param.14) | copy-start | bytes 3076

commit v11 on v9

--- a/solution.py
+++ b/solution.py
@@ -191,6 +191,7 @@
         riders[0][0] = x_halos[0, edge : edge + size]
         riders[0][1] = y_halos[0, edge : edge + size]
         riders[0][2] = corners[0, 1 : 1 + size]
+        riders[0][3] = corners[0, 1 : 1 + size]
 
 
 def spread_taps(weight, taps):
@@ -519,14 +520,15 @@
 def stack_kernel(*refs):
     out = refs[-1]
     for k in range(out.shape[0]):
-        out[k] = refs[k][...]
-
-
-def stack(*arrays):
+        out[k] = refs[k][: out.shape[1], : out.shape[2]]
+
+
+def stack(*arrays, part=None):
     vmem = pl.BlockSpec(memory_space=pltpu.VMEM)
+    shape = (part or arrays[0].shape[:2]) + arrays[0].shape[2:]
     return pl.pallas_call(
         stack_kernel,
-        out_shape=jax.ShapeDtypeStruct((len(arrays),) + arrays[0].shape, arrays[0].dtype),
+        out_shape=jax.ShapeDtypeStruct((len(arrays),) + shape, arrays[0].dtype),
         in_specs=[vmem] * len(arrays),
         out_specs=vmem,
         compiler_params=pltpu.CompilerParams(vmem_limit_bytes=VMEM_BYTES),
@@ -730,7 +732,7 @@
     (y, x, corner), act = lax.optimization_barrier((halos, act))
     y, x, corner = jnp.stack(y), jnp.stack(x), jnp.stack(corner)
     face = ((3 * (edge + ny + nx) + ny * nx, edge, channels), bf16)
-    held = [((3, riders.size, 16, channels), bf16)] if riders.size else []
+    held = [((4, riders.size, 16, channels), bf16)] if riders.size else []
     outer, inner, *held = call(
         functools.partial(face_kernel, ny, nx, riders.size),
         [face, face] + held,
@@ -761,8 +763,6 @@
         x,
         corner,
         taps,
-        flops=conv_flops // 4,
-        nbytes=6 << 20,
     )
     ends, stats = call(
         functools.partial(end_kernel, ny, nx),
@@ -779,12 +779,10 @@
         inner,
         taps,
         pairs,
-        flops=conv_flops // 2,
-        nbytes=3 << 20,
     )
     if riders.size:
         stats, other = lax.optimization_barrier((stats, other))
-        held = stack(held, other).reshape((-1,) + held.shape[1:])
+        held = stack(held, other, part=(1, 3)).reshape((2, 3) + held.shape[2:])
         other = swap(held, *riders.STEPS[1])
         stats = share(stats)
         stats, other = lax.optimization_barrier((stats, other))

time: 56 us -> 57 us (1.018)
  starting transfers between devices: 16.5 us -> 19.8 us
  waiting for transfers between devices: 4.89 us -> 3.25 us
  blocking collectives: 19.8 us -> 19.2 us
    ppermute x3, starting transfers between devices: 2.63 us -> 5.95 us  [swap(): lax.ppermute(block, axis, [(i, i ^ mask) for i in range(lax.axis_size(axi...]
    ppermute x3, waiting for transfers between devices: 1.74 us -> 0.01 us  [swap(): lax.ppermute(block, axis, [(i, i ^ mask) for i in range(lax.axis_size(axi...]
    all_to_all x2, blocking collectives: 19.8 us -> 19.2 us  [share(): return lax.all_to_all(stats, PART, 0, 0)]
  transfers between devices with their start and end apart: 11 -> 11, of which waited for: 4 -> 4; matrix products, arithmetic and copies ran while one was open for 0% -> 0% of each run, Pallas kernels for 19% -> 18%
where the time goes in v11:
time: 57 us; the launch traced here: 56.8 us
  starting transfers between devices  19.8 us (35%)
  blocking collectives  19.2 us (34%)
  Pallas kernels  14.3 us (25%)
  waiting for transfers between devices  3.25 us (6%)
    all_to_all x2, blocking collectives, share(): return lax.all_to_all(stats, PART, 0, 0)  19.2 us
    pallas_call x9, Pallas kernels, call(): pl.pallas_call(kernel, out_shape=[jax.ShapeDtypeStruct(shape, dtype) for...  14.2 us
    ppermute x3, starting transfers between devices, swap(): lax.ppermute(block, axis, [(i, i ^ mask) for i in range(lax.axis_size(axi...  5.95 us
    ppermute x2, starting transfers between devices, halos(): corner = lax.ppermute(corners[0], 'yx', self.swap_route(3))  5.77 us
    ppermute x1, starting transfers between devices, swap_depth(): lax.ppermute(inner, 'gz', routes[0])  2.9 us
    ppermute x2, starting transfers between devices, halos(): x = lax.ppermute(x_edges[0], 'yx', self.swap_route(1))  2.42 us
    ppermute x2, starting transfers between devices, halos(): y = lax.ppermute(y_edges[0], 'yx', self.swap_route(2))  2.05 us
    ppermute x2, waiting for transfers between devices, halos(): y = lax.ppermute(y_edges[0], 'yx', self.swap_route(2))  1.59 us
  transfers between devices with their start and end apart: 11, of which 4 were waited for; matrix products, arithmetic and copies ran while one was open for 0% of the time, Pallas kernels for 18%

profile of v11, /device:TPU:0, one launch (start us, length us, event | category | flops | bytes accessed | tf_op | source)
XLA Modules:
  0.0 56.8 jit_solution(12018867670760148347)
XLA Ops:
  0.0 1.6 %shard_map.82 = (bf16[1,30,16,128]{3,2,1,0:T(8,128)(2,1)S(1)}, bf16[1,30,16,128]{3,2,1,0:T(8,128)(2,1)S(1)}, bf16[1,15,16,128]{3,2,1,0:T(8,128)(2,1)S(1)}, bf16[...) custom-call(bf16[16,16,16,128]{3,2,1,0:T(8,128)(2,1)} %x_in.1, bf16[27,128,128]{2,1,0:T(8,128)(2,1)} %bitcast.50, ...), custom_call_target="tpu_custom_call" | custom-call | bytes 5242880 | tf_op jit(solution)/shard_map/pallas_call | solution.py:105
  1.6 5.1 %collective-permute-start.2 = (bf16[15,16,128]{2,1,0:T(8,128)(2,1)S(1)}, bf16[15,16,128]{2,1,0:T(8,128)(2,1)S(1)}, u32[]{:S(2)}, u32[]{:S(2)}) collective-permute-start(bf16[15,16,128]{2,1,0:T(8,128)(2,1)S(1)} %bitcast.46), channel_id=1, source_target_pairs={{0,3},{1,2},{2,1},{3,0},{4,7},{5,6},{6,5},{7,4},{8,11},{9,10},{10,... | collective-permute-start | bytes 184328 | tf_op jit(solution)/shard_map/ppermute | solution.py:46
  6.7 0.0 collective-permute-start.1
  6.7 0.6 %collective-permute-start = (bf16[30,16,128]{2,1,0:T(8,128)(2,1)S(1)}, bf16[30,16,128]{2,1,0:T(8,128)(2,1)S(1)}, u32[]{:S(2)}, u32[]{:S(2)}) collective-permute-start(bf16[30,16,128]{2,1,0:T(8,128)(2,1)S(1)} %bitcast.44), channel_id=1, source_target_pairs={{0,2},{1,3},{2,0},{3,1},{4,6},{5,7},{6,4},{7,5},{8,10},{9,11},{10,... | collective-permute-start | bytes 368648 | tf_op jit(solution)/shard_map/ppermute | solution.py:44
  7.4 4.7 %shard_map.83 = (f32[16,16,16,128]{3,2,1,0:T(8,128)S(1)}, bf16[1152,384]{1,0:T(8,128)(2,1)S(1)}, bf16[1536,256]{1,0:T(8,128)(2,1)S(1)}, bf16[108,16,128]{2,1,0:T(8,128)(2,1)S(1)}) custom-call(bf16[108,16,128]{2,1,0:T(8,128)(2,1)} %bitcast.52, bf16[18,18,16,128]{3,2,1,0:T(8,128)(2,1)S(1)} %get-tuple-element.42.x.refs_0_, ...), custom_call_target="tpu_custom_call" | custom-call | flops 3623878656 | bytes 6291456 | tf_op jit(solution)/shard_map/pallas_call | solution.py:105
  12.1 0.0 collective-permute-done.2
  12.1 1.4 %collective-permute-done.1 = bf16[30,16,128]{2,1,0:T(8,128)(2,1)S(1)} collective-permute-done((bf16[30,16,128]{2,1,0:T(8,128)(2,1)S(1)}, bf16[30,16,128]{2,1,0:T(8,128)(2,1)S(1)}, u32[]{:S(2)}, u32[]{:S(2)}) %collective-permute-start.1) | collective-permute-done | bytes 122912 | tf_op jit(solution)/shard_map/ppermute | solution.py:45
  13.5 1.6 %collective-permute-done = bf16[30,16,128]{2,1,0:T(8,128)(2,1)S(1)} collective-permute-done((bf16[30,16,128]{2,1,0:T(8,128)(2,1)S(1)}, bf16[30,16,128]{2,1,0:T(8,128)(2,1)S(1)}, u32[]{:S(2)}, u32[]{:S(2)}) %collective-permute-start) | collective-permute-done | bytes 122912 | tf_op jit(solution)/shard_map/ppermute | solution.py:44
  15.1 0.1 shard_map.85
  15.2 1.6 %collective-permute-start.5 = (bf16[1,4,14,16,128]{4,3,2,1,0:T(8,128)(2,1)S(1)}, bf16[1,4,14,16,128]{4,3,2,1,0:T(8,128)(2,1)S(1)}, u32[]{:S(2)}, u32[]{:S(2)}) collective-permute-start(bf16[1,4,14,16,128]{4,3,2,1,0:T(8,128)(2,1)S(1)} %bitcast.35), channel_id=1, source_target_pairs={{0,16},{16,0},{1,17},{17,1},{2,18},{18,2},{3,19},{19,3},{4,20},{20... | collective-permute-start | bytes 688136 | tf_op jit(solution)/shard_map/ppermute | solution.py:94
  16.8 0.7 %collective-permute-start.3 = (bf16[55,16,128]{2,1,0:T(8,128)(2,1)S(1)}, bf16[55,16,128]{2,1,0:T(8,128)(2,1)S(1)}, u32[]{:S(2)}, u32[]{:S(2)}) collective-permute-start(bf16[55,16,128]{2,1,0:T(8,128)(2,1)S(1)} %get-tuple-element.53), channel_id=1, source_target_pairs={{4,8},{8,4},{5,9},{9,5},{6,10},{10,6},{7,11},{11,7},{20,24},{24,20... | collective-permute-start | bytes 675848 | tf_op jit(solution)/shard_map/ppermute | solution.py:63
  17.4 2.9 %collective-permute-start.4 = (bf16[55,16,128]{2,1,0:T(8,128)(2,1)S(1)}, bf16[55,16,128]{2,1,0:T(8,128)(2,1)S(1)}, u32[]{:S(2)}, u32[]{:S(2)}) collective-permute-start(bf16[55,16,128]{2,1,0:T(8,128)(2,1)S(1)} %get-tuple-element.54), channel_id=1, source_target_pairs={{0,4},{4,0},{8,12},{12,8},{1,5},{5,1},{9,13},{13,9},{2,6},{6,2},{1... | collective-permute-start | bytes 675848 | tf_op jit(solution)/shard_map/ppermute | solution.py:63
  20.3 1.0 %shard_map.84 = (f32[14,16,16,128]{3,2,1,0:T(8,128)S(1)}, f32[4,16,16,128]{3,2,1,0:T(8,128)S(1)}, f32[16,128]{1,0:T(8,128)S(1)}) custom-call(f32[16,16,16,128]{3,2,1,0:T(8,128)S(1)} %get-tuple-element.45.own, bf16[1,30,16,128]{3,2,1,0:T(8,128)(2,1)S(1)} %bitcast.32, bf16[1,30,16,128]{3,2,1,0:T(8,128)(2,1)S(1)} %bitcast.30, ...), custom_call_target="tpu_custom_call" | custom-call | tf_op jit(solution)/shard_map/pallas_call | solution.py:105
  21.4 0.0 collective-permute-done.3.refs_3_
  21.4 0.1 collective-permute-done.4.refs_4_
  21.5 2.0 %shard_map.86 = (f32[6,16,16,128]{3,2,1,0:T(8,128)S(1)}, f32[16,2,128]{2,1,0:T(2,128)S(1)}) custom-call(bf16[18,18,16,128]{3,2,1,0:T(8,128)(2,1)S(1)} %get-tuple-element.42.x.refs_0_, f32[16,128]{1,0:T(8,128)S(1)} %get-tuple-element.51.refs_1_, f32[4,16,16,128]{3,2,1,0:T(8,128)S(1)} %get-tuple-element.52.refs_2_, ...), custom_call_target="tpu_custom_call" | custom-call | tf_op jit(solution)/shard_map/pallas_call | solution.py:105
  23.4 0.0 copy-start.3
  23.4 0.0 copy-start.4
  23.4 0.0 collective-permute-done.5.refs_1_
  23.5 4.2 %collective-permute-start.6 = (bf16[2,3,14,16,128]{4,3,2,1,0:T(8,128)(2,1)S(1)}, bf16[2,3,14,16,128]{4,3,2,1,0:T(8,128)(2,1)S(1)}, u32[]{:S(2)}, u32[]{:S(2)}) collective-permute-start(bf16[2,3,14,16,128]{4,3,2,1,0:T(8,128)(2,1)S(1)} %bitcast.27), channel_id=1, source_target_pairs={{0,8},{4,12},{8,0},{12,4},{1,9},{5,13},{9,1},{13,5},{2,10},{6,14},... | collective-permute-start | bytes 1032200 | tf_op jit(solution)/shard_map/ppermute | solution.py:94
  27.7 9.2 %all_to_all.10.stats = f32[16,2,128]{2,1,0:T(2,128)S(1)} all-to-all(f32[16,2,128]{2,1,0:T(2,128)S(1)} %get-tuple-element.59), channel_id=1, replica_groups=mesh['cand'=2,'gz'=4,'yx'=4] {'gz','yx'}, dimensions={0} | all-to-all | bytes 32768 | tf_op jit(solution)/shard_map/all_to_all | solution.py:98
  36.8 0.0 collective-permute-done.6.refs_1_
  36.9 0.2 collective-permute-start.7
  37.1 0.0 copy-done.3
  37.1 0.0 copy-done.4
  37.1 1.1 %shard_map.88 = (bf16[16,16,16,128]{3,2,1,0:T(8,128)(2,1)S(1)}, f32[10,8,8,128]{3,2,1,0:T(8,128)S(1)}, bf16[1,80,128]{2,1,0:T(8,128)(2,1)S(1)}, bf16[1,80,128]{2,1,0:T(8,128)(2,1)S(1)}, f32[1,16,128]{2,1,0:T(8,128)S(1)}) custom-call(f32[14,16,16,128]{3,2,1,0:T(8,128)S(1)} %get-tuple-element.50.inner, f32[6,16,16,128]{3,2,1,0:T(8,128)S(1)} %get-tuple-element.56.ends, ...), custom_call_target="tpu_custom_call" | custom-call | flops 10485760 | bytes 3145728 | tf_op jit(solution)/shard_map/pallas_call | solution.py:105
  38.2 0.7 %collective-permute-start.10 = (f32[16,128]{1,0:T(8,128)S(1)}, f32[16,128]{1,0:T(8,128)S(1)}, u32[]{:S(2)}, u32[]{:S(2)}) collective-permute-start(f32[16,128]{1,0:T(8,128)S(1)} %bitcast.49), channel_id=1, source_target_pairs={{0,3},{1,2},{2,1},{3,0},{4,7},{5,6},{6,5},{7,4},{8,11},{9,10},{10,... | collective-permute-start | bytes 24584 | tf_op jit(solution)/shard_map/ppermute | solution.py:46
  38.9 1.4 %collective-permute-start.8 = (bf16[80,128]{1,0:T(8,128)(2,1)S(1)}, bf16[80,128]{1,0:T(8,128)(2,1)S(1)}, u32[]{:S(2)}, u32[]{:S(2)}) collective-permute-start(bf16[80,128]{1,0:T(8,128)(2,1)S(1)} %bitcast.48), channel_id=1, source_target_pairs={{0,2},{1,3},{2,0},{3,1},{4,6},{5,7},{6,4},{7,5},{8,10},{9,11},{10,... | collective-permute-start | bytes 61448 | tf_op jit(solution)/shard_map/ppermute | solution.py:44
  40.3 2.4 %collective-permute-start.9 = (bf16[80,128]{1,0:T(8,128)(2,1)S(1)}, bf16[80,128]{1,0:T(8,128)(2,1)S(1)}, u32[]{:S(2)}, u32[]{:S(2)}) collective-permute-start(bf16[80,128]{1,0:T(8,128)(2,1)S(1)} %bitcast.47), channel_id=1, source_target_pairs={{0,1},{1,0},{2,3},{3,2},{4,5},{5,4},{6,7},{7,6},{8,9},{9,8},{10,11... | collective-permute-start | bytes 61448 | tf_op jit(solution)/shard_map/ppermute | solution.py:45
  42.7 0.0 collective-permute-done.7.refs_1_
  42.7 0.1 shard_map.90
  42.8 1.4 %shard_map.91 = (f32[2,512,128]{2,1,0:T(8,128)S(1)}, bf16[4,108,16,128]{3,2,1,0:T(8,128)(2,1)S(1)}) custom-call(f32[10,8,8,128]{3,2,1,0:T(8,128)S(1)} %get-tuple-element.62.pooled, bf16[108,16,128]{2,1,0:T(8,128)(2,1)S(1)} %get-tuple-element.63.own, bf16[8,3,14,16,128]{4,3,2,1,0:T(8,128)(2,1)S(1)} %bitcast.26), custom_call_target="tpu_custom_call" | custom-call | flops 905969664 | bytes 4194304 | tf_op jit(solution)/shard_map/pallas_call | solution.py:105
  44.2 0.0 copy-start
  44.2 0.0 copy-start.1
  44.3 0.0 copy-start.2
  44.3 0.0 collective-permute-done.10
  44.3 0.0 collective-permute-done.8
  44.3 0.2 collective-permute-done.9
  44.5 0.7 %shard_map.92 = (f32[2,512,128]{2,1,0:T(8,128)S(1)}, f32[16,2,256]{2,1,0:T(2,128)S(1)}) custom-call(f32[2,512,128]{2,1,0:T(8,128)S(1)} %get-tuple-element.65.own, bf16[1,80,128]{2,1,0:T(8,128)(2,1)S(1)} %bitcast.37, bf16[1,80,128]{2,1,0:T(8,128)(2,1)S(1)} %bitcast.38, f32[1,16,128]{2,1,0:T(8,128)S(1)} %bitcast.39, ...), custom_call_target="tpu_custom_call" | custom-call | flops 67108864 | bytes 3145728 | tf_op jit(solution)/shard_map/pallas_call | solution.py:105
  45.2 10.0 %all_to_all.11.stats = f32[16,2,256]{2,1,0:T(2,128)S(1)} all-to-all(f32[16,2,256]{2,1,0:T(2,128)S(1)} %get-tuple-element.71), channel_id=1, replica_groups=mesh['cand'=2,'gz'=4,'yx'=4] {'gz','yx'}, dimensions={0} | all-to-all | bytes 65536 | tf_op jit(solution)/shard_map/all_to_all | solution.py:98
  55.2 0.0 copy-done
  55.2 0.0 copy-done.1
  55.2 0.0 copy-done.2
  55.2 1.5 %shard_map.93 = bf16[16,16,16,128]{3,2,1,0:T(8,128)(2,1)} custom-call(f32[2,512,128]{2,1,0:T(8,128)S(1)} %get-tuple-element.70.act, f32[16,2,256]{2,1,0:T(2,128)S(1)} %all_to_all.11.stats, f32[1,256]{1,0:T(1,128)S(1)} %bitcast.40, f32[1,256]{1,0:T(1,128)S(1)} %bitcast.41, bf16[256,128]{1,0:T(8,128)(2,1)S(1)} %copy-done, ...), custom_call_target="tpu_custom_call" | custom-call | flops 67108864 | bytes 3145728 | tf_op jit(solution)/shard_map/pallas_call | solution.py:105
  (2 shorter events, 0.1 us)
Async XLA Ops:
  1.6 10.5 %collective-permute-start.2 = (bf16[15,16,128]{2,1,0:T(8,128)(2,1)S(1)}, bf16[15,16,128]{2,1,0:T(8,128)(2,1)S(1)}, u32[]{:S(2)}, u32[]{:S(2)}) collective-permute-start(bf16[15,16,128]{2,1,0:T(8,128)(2,1)S(1)} %bitcast.46), channel_id=1, source_target_pairs={{0,3},{1,2},{2,1},{3,0},{4,7},{5,6},{6,5},{7,4},{8,11},{9,10},{10,... | collective-permute-start | bytes 184328 | tf_op jit(solution)/shard_map/ppermute | solution.py:46
  6.7 6.8 %collective-permute-start.1 = (bf16[30,16,128]{2,1,0:T(8,128)(2,1)S(1)}, bf16[30,16,128]{2,1,0:T(8,128)(2,1)S(1)}, u32[]{:S(2)}, u32[]{:S(2)}) collective-permute-start(bf16[30,16,128]{2,1,0:T(8,128)(2,1)S(1)} %bitcast.45), channel_id=1, source_target_pairs={{0,1},{1,0},{2,3},{3,2},{4,5},{5,4},{6,7},{7,6},{8,9},{9,8},{10,11... | collective-permute-start | bytes 368648 | tf_op jit(solution)/shard_map/ppermute | solution.py:45
  6.7 8.4 %collective-permute-start = (bf16[30,16,128]{2,1,0:T(8,128)(2,1)S(1)}, bf16[30,16,128]{2,1,0:T(8,128)(2,1)S(1)}, u32[]{:S(2)}, u32[]{:S(2)}) collective-permute-start(bf16[30,16,128]{2,1,0:T(8,128)(2,1)S(1)} %bitcast.44), channel_id=1, source_target_pairs={{0,2},{1,3},{2,0},{3,1},{4,6},{5,7},{6,4},{7,5},{8,10},{9,11},{10,... | collective-permute-start | bytes 368648 | tf_op jit(solution)/shard_map/ppermute | solution.py:44
  15.2 8.3 %collective-permute-start.5 = (bf16[1,4,14,16,128]{4,3,2,1,0:T(8,128)(2,1)S(1)}, bf16[1,4,14,16,128]{4,3,2,1,0:T(8,128)(2,1)S(1)}, u32[]{:S(2)}, u32[]{:S(2)}) collective-permute-start(bf16[1,4,14,16,128]{4,3,2,1,0:T(8,128)(2,1)S(1)} %bitcast.35), channel_id=1, source_target_pairs={{0,16},{16,0},{1,17},{17,1},{2,18},{18,2},{3,19},{19,3},{4,20},{20... | collective-permute-start | bytes 688136 | tf_op jit(solution)/shard_map/ppermute | solution.py:94
  16.8 4.6 %collective-permute-start.3 = (bf16[55,16,128]{2,1,0:T(8,128)(2,1)S(1)}, bf16[55,16,128]{2,1,0:T(8,128)(2,1)S(1)}, u32[]{:S(2)}, u32[]{:S(2)}) collective-permute-start(bf16[55,16,128]{2,1,0:T(8,128)(2,1)S(1)} %get-tuple-element.53), channel_id=1, source_target_pairs={{4,8},{8,4},{5,9},{9,5},{6,10},{10,6},{7,11},{11,7},{20,24},{24,20... | collective-permute-start | bytes 675848 | tf_op jit(solution)/shard_map/ppermute | solution.py:63
  17.4 4.0 %collective-permute-start.4 = (bf16[55,16,128]{2,1,0:T(8,128)(2,1)S(1)}, bf16[55,16,128]{2,1,0:T(8,128)(2,1)S(1)}, u32[]{:S(2)}, u32[]{:S(2)}) collective-permute-start(bf16[55,16,128]{2,1,0:T(8,128)(2,1)S(1)} %get-tuple-element.54), channel_id=1, source_target_pairs={{0,4},{4,0},{8,12},{12,8},{1,5},{5,1},{9,13},{13,9},{2,6},{6,2},{1... | collective-permute-start | bytes 675848 | tf_op jit(solution)/shard_map/ppermute | solution.py:63
  23.4 13.6 %copy-start.3 = (f32[128]{0:T(128)S(1)}, f32[128]{0:T(128)}, u32[]{:S(2)}) copy-start(f32[128]{0:T(128)} %param.10) | copy-start | bytes 1540
  23.4 13.6 %copy-start.4 = (f32[128]{0:T(128)S(1)}, f32[128]{0:T(128)}, u32[]{:S(2)}) copy-start(f32[128]{0:T(128)} %param.11) | copy-start | bytes 1540
  23.5 13.3 %collective-permute-start.6 = (bf16[2,3,14,16,128]{4,3,2,1,0:T(8,128)(2,1)S(1)}, bf16[2,3,14,16,128]{4,3,2,1,0:T(8,128)(2,1)S(1)}, u32[]{:S(2)}, u32[]{:S(2)}) collective-permute-start(bf16[2,3,14,16,128]{4,3,2,1,0:T(8,128)(2,1)S(1)} %bitcast.27), channel_id=1, source_target_pairs={{0,8},{4,12},{8,0},{12,4},{1,9},{5,13},{9,1},{13,5},{2,10},{6,14},... | collective-permute-start | bytes 1032200 | tf_op jit(solution)/shard_map/ppermute | solution.py:94
  36.9 5.8 %collective-permute-start.7 = (bf16[4,3,14,16,128]{4,3,2,1,0:T(8,128)(2,1)S(1)}, bf16[4,3,14,16,128]{4,3,2,1,0:T(8,128)(2,1)S(1)}, u32[]{:S(2)}, u32[]{:S(2)}) collective-permute-start(bf16[4,3,14,16,128]{4,3,2,1,0:T(8,128)(2,1)S(1)} %bitcast.24), channel_id=1, source_target_pairs={{0,4},{4,0},{8,12},{12,8},{1,5},{5,1},{9,13},{13,9},{2,6},{6,2},{1... | collective-permute-start | bytes 2064392 | tf_op jit(solution)/shard_map/ppermute | solution.py:94
  38.2 6.0 %collective-permute-start.10 = (f32[16,128]{1,0:T(8,128)S(1)}, f32[16,128]{1,0:T(8,128)S(1)}, u32[]{:S(2)}, u32[]{:S(2)}) collective-permute-start(f32[16,128]{1,0:T(8,128)S(1)} %bitcast.49), channel_id=1, source_target_pairs={{0,3},{1,2},{2,1},{3,0},{4,7},{5,6},{6,5},{7,4},{8,11},{9,10},{10,... | collective-permute-start | bytes 24584 | tf_op jit(solution)/shard_map/ppermute | solution.py:46
  38.9 5.4 %collective-permute-start.8 = (bf16[80,128]{1,0:T(8,128)(2,1)S(1)}, bf16[80,128]{1,0:T(8,128)(2,1)S(1)}, u32[]{:S(2)}, u32[]{:S(2)}) collective-permute-start(bf16[80,128]{1,0:T(8,128)(2,1)S(1)} %bitcast.48), channel_id=1, source_target_pairs={{0,2},{1,3},{2,0},{3,1},{4,6},{5,7},{6,4},{7,5},{8,10},{9,11},{10,... | collective-permute-start | bytes 61448 | tf_op jit(solution)/shard_map/ppermute | solution.py:44
  40.3 4.2 %collective-permute-start.9 = (bf16[80,128]{1,0:T(8,128)(2,1)S(1)}, bf16[80,128]{1,0:T(8,128)(2,1)S(1)}, u32[]{:S(2)}, u32[]{:S(2)}) collective-permute-start(bf16[80,128]{1,0:T(8,128)(2,1)S(1)} %bitcast.47), channel_id=1, source_target_pairs={{0,1},{1,0},{2,3},{3,2},{4,5},{5,4},{6,7},{7,6},{8,9},{9,8},{10,11... | collective-permute-start | bytes 61448 | tf_op jit(solution)/shard_map/ppermute | solution.py:45
  44.2 11.0 %copy-start = (bf16[256,128]{1,0:T(8,128)(2,1)S(1)}, bf16[256,128]{1,0:T(8,128)(2,1)}, u32[]{:S(2)}) copy-start(bf16[256,128]{1,0:T(8,128)(2,1)} %up.1) | copy-start | bytes 196612
  44.2 11.0 %copy-start.1 = (f32[256]{0:T(256)S(1)}, f32[256]{0:T(256)}, u32[]{:S(2)}) copy-start(f32[256]{0:T(256)} %param.13) | copy-start | bytes 3076
  44.3 11.0 %copy-start.2 = (f32[256]{0:T(256)S(1)}, f32[256]{0:T(256)}, u32[]{:S(2)}) copy-start(f32[256]{0:T(256)} %param.14) | copy-start | bytes 3076

commit v12 on v9

--- a/solution.py
+++ b/solution.py
@@ -113,7 +113,7 @@
     )(*far, *near)
 
 
-def start_kernel(ny, nx, size, x_in, w_in, d_in, y_out, x_out, corners, x, w, lines, sems):
+def start_kernel(ny, nx, size, x_in, w_in, d_in, y_out, x_out, corners, outer, inner, x, w, lines, sems):
     edge = x_in.shape[0]
     f32, bf16 = jnp.float32, jnp.bfloat16
     above, left = Square().low_sides()
@@ -168,29 +168,35 @@
             high = flat[pl.ds(begin + 8 * (edge - 1), edge, stride=8 * edge), :]
             kept = jnp.where(above[i], low, high)
             corners[i * nx + j, 0] = kept.astype(bf16)
+    odd, far = lax.axis_index("gz") % 2, edge - 3
+    for face, at in ((outer, odd * far), (inner, (1 - odd) * far)):
+        for k in range(3):
+            face[k] = x[1 + at + k, 1 : edge + 1]
     for copy in later:
         copy.wait()
 
 
-def face_kernel(ny, nx, size, x, y_halos, x_halos, corners, outer, inner, *riders):
+def turn_kernel(ny, nx, size, y_halos, x_halos, corners, outer, inner, *riders):
     edge = outer.shape[1]
-    wide = edge + ny + nx
-    odd = lax.axis_index("gz") % 2
-    far = edge - 3
+    wide = ny + nx
+    odd, far = lax.axis_index("gz") % 2, edge - 3
     for face, at in ((outer, odd * far), (inner, (1 - odd) * far)):
         for k in range(3):
             row = k * wide
-            face[row : row + edge] = x[1 + at + k, 1 : edge + 1]
             for i in range(ny):
-                face[row + edge + i] = y_halos[i, at + k]
+                face[row + i] = y_halos[i, at + k]
             for j in range(nx):
-                face[row + edge + ny + j] = x_halos[j, at + k]
+                face[row + ny + j] = x_halos[j, at + k]
         for k in range(ny * nx):
             face[3 * wide + k] = corners[k, 0]
     if size:
         riders[0][0] = x_halos[0, edge : edge + size]
         riders[0][1] = y_halos[0, edge : edge + size]
         riders[0][2] = corners[0, 1 : 1 + size]
+
+
+def in_order(odd, outer, inner):
+    return jnp.where(odd, inner, outer), jnp.where(odd, outer, inner)
 
 
 def spread_taps(weight, taps):
@@ -337,50 +343,23 @@
     return mean, lax.fori_loop(0, count, spread_step, zero, unroll=True)
 
 
-def side_kernel(ny, nx, own, y_halos, x_halos, corners, taps, inner, ends, stats, act, column):
+def side_kernel(ny, nx, *refs):
+    x, own, y_halos, x_halos, corners, outer, inner, taps, pairs, middle, ends, stats, act, grid, column = refs
     edge = own.shape[0]
-    act[0] = jnp.zeros(act.shape[1:], jnp.float32)
-    act[edge + 1] = jnp.zeros(act.shape[1:], jnp.float32)
-    act[1 : edge + 1] = own[...]
+    depth = edge + 4
+    f32 = jnp.float32
     above, left = Square().low_sides()
-    blank = jnp.zeros((2, edge, 128), jnp.bfloat16)
-    for i in range(ny):
-        line = jnp.concatenate([blank, y_halos[i, 0:edge], blank], axis=0)
-        act[:, jnp.where(above[i], 0, edge - 1)] += y_terms(line, above[i], taps)
-    for j in range(nx):
-        column[...] = jnp.zeros(column.shape, jnp.float32)
-        fill_column(
-            column, 2, x_halos[j, 0:edge], [corners[i * nx + j, 0] for i in range(ny)], above
-        )
-        add_column(act, x_terms(column, taps), j, nx, left[j])
-    inner[...] = act[2:edge]
-    ends[0:2] = act[0:2]
-    ends[2:4] = act[edge : edge + 2]
-    mean, spread = moments(act.at[2:edge])
-    stats[0:8] = mean
-    stats[8:16] = spread
-
-
-def end_kernel(ny, nx, *refs):
-    x, inner_stats, partial, outer_face, inner_face, taps, pairs, act, stats, faces, grid, column = refs
-    edge = x.shape[2]
-    wide_face = edge + ny + nx
-    f32 = jnp.float32
     odd = lax.axis_index("gz") % 2 == 1
-    faces[0] = jnp.where(odd, inner_face[...], outer_face[...])
-    faces[1] = jnp.where(odd, outer_face[...], inner_face[...])
-    above, left = Square().low_sides()
+    act[2 : 2 + edge] = own[...]
     blank = jnp.zeros(grid.shape[:1] + grid.shape[2:], grid.dtype)
     grid[:, 0] = blank
     grid[:, edge + 1] = blank
-    gap = jnp.zeros((2, edge, 128), grid.dtype)
-    for side, halo_at, own_at, plane, at, beyond, own, beside, dz in (
-        (0, 0, 3, 1, 0, 0, 2, 2, 0),
-        (1, 1, 0, edge, 3, 4, 3, 1, 2),
+    faces = in_order(odd, outer[...], inner[...])
+    for face, halo_at, own_at, plane, beyond, at, beside, dz in (
+        (faces[0], 0, 3, 1, 0, 2, 2, 0),
+        (faces[1], 1, 0, edge, edge + 2, edge + 1, 1, 2),
     ):
-        for k in range(3):
-            begin = k * wide_face
-            grid[halo_at + k, 1 : edge + 1] = faces[side, begin : begin + edge]
+        grid[halo_at : halo_at + 3, 1 : edge + 1] = face
         grid[own_at, 1 : edge + 1] = x[plane, 1 : edge + 1]
 
         def put(z, new):
@@ -391,37 +370,62 @@
             [grid[beside, dy : dy + edge].reshape(edge * edge, 128) for dy in range(3)], axis=1
         )
         wide = jnp.dot(stacked, taps[dz * 384 : dz * 384 + 384, :], preferred_element_type=f32)
-        own_part = partial[1 if side == 0 else 2]
-        act[own] = own_part + join_x(wide.reshape(edge, edge, 384), edge)
-        near = 1 if side == 0 else 4
-        act[near] += partial[0 if side == 0 else 3]
+        act[at] += join_x(wide.reshape(edge, edge, 384), edge)
+
+    gap = jnp.zeros((2, edge, 128), grid.dtype)
+    reached = act.at[1 : depth - 1]
+    for i in range(ny):
+        line = jnp.concatenate([gap, y_halos[i, 0:edge], gap], axis=0)
+        reached[:, jnp.where(above[i], 0, edge - 1)] += y_terms(line, above[i], taps)
+    for j in range(nx):
+        column[...] = jnp.zeros(column.shape, f32)
+        fill_column(
+            column, 2, x_halos[j, 0:edge], [corners[i * nx + j, 0] for i in range(ny)], above
+        )
+        add_column(reached, x_terms(column, taps), j, nx, left[j])
+    middle[...] = act[3 : depth - 3]
+    ends[0:3] = act[0:3]
+    ends[3:6] = act[depth - 3 :]
+    mean, spread = moments(act.at[3 : depth - 3])
+    stats[0:8] = mean
+    stats[8:16] = spread
+
+
+def end_kernel(ny, nx, middle_stats, ends, outer, inner, taps, act, stats, faces, column):
+    edge = act.shape[1]
+    wide = ny + nx
+    f32 = jnp.float32
+    above, left = Square().low_sides()
+    odd = lax.axis_index("gz") % 2 == 1
+    faces[0], faces[1] = in_order(odd, outer[...], inner[...])
+    act[...] = ends[...]
+    gap = jnp.zeros((2, edge, 128), faces.dtype)
+    for side in range(2):
 
         def rim(row):
-            planes = [faces[side, k * wide_face + edge + row] for k in range(3)]
-            return jnp.stack(planes)
-
-        three = act.at[at : at + 3]
+            return jnp.stack([faces[side, k * wide + row] for k in range(3)])
+
+        three = act.at[3 * side : 3 * side + 3]
         for i in range(ny):
             line = [rim(i), gap] if side == 0 else [gap, rim(i)]
-            three[:, jnp.where(above[i], 0, edge - 1)] += y_terms(
-                jnp.concatenate(line, axis=0), above[i], taps
-            )
+            line = jnp.concatenate(line, axis=0)
+            three[:, jnp.where(above[i], 0, edge - 1)] += y_terms(line, above[i], taps)
         for j in range(nx):
             column[...] = jnp.zeros(column.shape, f32)
-            ends = []
+            tails = []
             for i in range(ny):
-                tile = faces[side, 3 * wide_face + i * nx + j].astype(f32)
-                ends.append(tile[edge - 3 :] if side == 0 else tile[:3])
-            fill_column(column, 0 if side == 0 else 2, rim(ny + j), ends, above)
+                tile = faces[side, 3 * wide + i * nx + j].astype(f32)
+                tails.append(tile[edge - 3 :] if side == 0 else tile[:3])
+            fill_column(column, 0 if side == 0 else 2, rim(ny + j), tails, above)
             add_column(three, x_terms(column, taps), j, nx, left[j])
 
     mean, spread = moments(act.at[2:4])
     few, many = edge * edge // 4, (edge - 2) * edge * edge // 8
-    inner_mean, inner_spread = inner_stats[0:8], inner_stats[8:16]
-    off = inner_mean - mean
-    share_of = few / (few + many)
-    spread = spread + inner_spread + (many * share_of) * (off * off)
-    put_stats(stats, inner_mean - share_of * off, spread, few + many)
+    middle_mean, middle_spread = middle_stats[0:8], middle_stats[8:16]
+    off = middle_mean - mean
+    part = few / (few + many)
+    spread = spread + middle_spread + (many * part) * (off * off)
+    put_stats(stats, middle_mean - part * off, spread, few + many)
 
 
 def merge(mean, spread, rows, other_mean, other_spread):
@@ -693,12 +697,15 @@
 
     own = jnp.moveaxis(deep_weight, 4, 3).reshape(-1, 16, channels)
     conv_weight = conv_weight.reshape(27, channels, channels)
-    *edges, field, conv_weight = call(
+    three = ((3, edge, edge, channels), bf16)
+    *edges, outer, inner, field, conv_weight = call(
         functools.partial(start_kernel, ny, nx, riders.size),
         [
             ((ny, edge + riders.size, edge, channels), bf16),
             ((nx, edge + riders.size, edge, channels), bf16),
             ((ny * nx, 1 + riders.size, edge, channels), bf16),
+            three,
+            three,
             ((edge + 2, edge + 2, edge, channels), bf16),
             (conv_weight.shape, bf16),
         ],
@@ -710,6 +717,7 @@
         in_hbm=3,
     )
     halos = square.halos(*(list(piece) for piece in edges))
+    outer, inner = swap_depth(outer, inner)
     conv_flops = 54 * channels * channels * edge**3
     act, taps, pairs, own = call(
         conv_kernel,
@@ -729,18 +737,12 @@
     )
     (y, x, corner), act = lax.optimization_barrier((halos, act))
     y, x, corner = jnp.stack(y), jnp.stack(x), jnp.stack(corner)
-    face = ((3 * (edge + ny + nx) + ny * nx, edge, channels), bf16)
+    turn = ((3 * (ny + nx) + ny * nx, edge, channels), bf16)
     held = [((3, riders.size, 16, channels), bf16)] if riders.size else []
-    outer, inner, *held = call(
-        functools.partial(face_kernel, ny, nx, riders.size),
-        [face, face] + held,
-        [],
-        field,
-        y,
-        x,
-        corner,
-    )
-    outer, inner = swap_depth(outer, inner)
+    turns = call(
+        functools.partial(turn_kernel, ny, nx, riders.size), [turn, turn] + held, [], y, x, corner
+    )
+    turns, held = swap_depth(*turns[:2]), turns[2:]
     if riders.size:
         held = held[0][None]
         other = swap(held, *riders.STEPS[0])
@@ -748,39 +750,32 @@
         held = rotate_shards(own)
     six = ((6, edge, edge, channels), f32)
     column = (edge + 16, channels)
-    middle, partial, stats = call(
+    middle, ends, stats = call(
         functools.partial(side_kernel, ny, nx),
+        [((edge - 2, edge, edge, channels), f32), six, ((16, channels), f32)],
         [
-            ((edge - 2, edge, edge, channels), f32),
-            ((4, edge, edge, channels), f32),
-            ((16, channels), f32),
+            ((edge + 4, edge, edge, channels), f32),
+            ((4, edge + 2, edge, channels), bf16),
+            ((edge + 4,) + column, f32),
         ],
-        [((edge + 2, edge, edge, channels), f32), ((edge + 4,) + column, f32)],
+        field,
         act,
         y,
         x,
         corner,
-        taps,
-        flops=conv_flops // 4,
-        nbytes=6 << 20,
-    )
-    ends, stats = call(
-        functools.partial(end_kernel, ny, nx),
-        [six, ((devices, 2, channels), f32)],
-        [
-            ((2,) + face[0], bf16),
-            ((4, edge + 2, edge, channels), bf16),
-            ((5,) + column, f32),
-        ],
-        field,
-        stats,
-        partial,
         outer,
         inner,
         taps,
         pairs,
-        flops=conv_flops // 2,
-        nbytes=3 << 20,
+    )
+    ends, stats = call(
+        functools.partial(end_kernel, ny, nx),
+        [six, ((devices, 2, channels), f32)],
+        [((2,) + turn[0], bf16), ((5,) + column, f32)],
+        stats,
+        ends,
+        *turns,
+        taps,
     )
     if riders.size:
         stats, other = lax.optimization_barrier((stats, other))

time: 56 us -> 56.1 us (level)
  waiting for transfers between devices: 4.89 us -> 0.35 us
  starting transfers between devices: 16.5 us -> 19.1 us
  blocking collectives: 19.8 us -> 21.7 us
    ppermute x1 -> x2, starting transfers between devices: 2.92 us -> 5.21 us  [swap_depth(): lax.ppermute(inner, 'gz', routes[0])]
    all_to_all x2, blocking collectives: 19.8 us -> 21.7 us  [share(): return lax.all_to_all(stats, PART, 0, 0)]
    ppermute x3, waiting for transfers between devices: 1.74 us -> 0.01 us  [swap(): lax.ppermute(block, axis, [(i, i ^ mask) for i in range(lax.axis_size(axi...]
    ppermute x2, waiting for transfers between devices: 1.59 us -> 0.12 us  [halos(): y = lax.ppermute(y_edges[0], 'yx', self.swap_route(2))]
    ppermute x2, waiting for transfers between devices: 1.55 us -> 0.21 us  [halos(): x = lax.ppermute(x_edges[0], 'yx', self.swap_route(1))]
    ppermute x2, starting transfers between devices: 2.05 us -> 1.24 us  [halos(): y = lax.ppermute(y_edges[0], 'yx', self.swap_route(2))]
    ppermute x2, starting transfers between devices: 5.77 us -> 6.58 us  [halos(): corner = lax.ppermute(corners[0], 'yx', self.swap_route(3))]
    ppermute x1 -> x2, starting transfers between devices: 0.68 us -> 1.31 us  [swap_depth(): lax.ppermute(outer, 'gz', routes[1])]
  transfers between devices with their start and end apart: 11 -> 13, of which waited for: 4 -> 2; matrix products, arithmetic and copies ran while one was open for 0% -> 0% of each run, Pallas kernels for 19% -> 19%
where the time goes in v12:
time: 56.1 us; the launch traced here: 55.9 us
  blocking collectives  21.7 us (39%)
  starting transfers between devices  19.1 us (34%)
  Pallas kernels  14.4 us (26%)
    all_to_all x2, blocking collectives, share(): return lax.all_to_all(stats, PART, 0, 0)  21.7 us
    pallas_call x9, Pallas kernels, call(): pl.pallas_call(kernel, out_shape=[jax.ShapeDtypeStruct(shape, dtype) for...  14.3 us
    ppermute x2, starting transfers between devices, halos(): corner = lax.ppermute(corners[0], 'yx', self.swap_route(3))  6.58 us
    ppermute x2, starting transfers between devices, swap_depth(): lax.ppermute(inner, 'gz', routes[0])  5.21 us
    ppermute x2, starting transfers between devices, halos(): x = lax.ppermute(x_edges[0], 'yx', self.swap_route(1))  2.42 us
    ppermute x3, starting transfers between devices, swap(): lax.ppermute(block, axis, [(i, i ^ mask) for i in range(lax.axis_size(axi...  2.38 us
    ppermute x2, starting transfers between devices, swap_depth(): lax.ppermute(outer, 'gz', routes[1])  1.31 us
    ppermute x2, starting transfers between devices, halos(): y = lax.ppermute(y_edges[0], 'yx', self.swap_route(2))  1.24 us
  transfers between devices with their start and end apart: 13, of which 2 were waited for; matrix products, arithmetic and copies ran while one was open for 0% of the time, Pallas kernels for 19%

profile of v12, /device:TPU:0, one launch (start us, length us, event | category | flops | bytes accessed | tf_op | source)
XLA Modules:
  0.0 55.9 jit_solution(5307209350249174785)
XLA Ops:
  0.0 1.6 %shard_map.82 = (bf16[1,30,16,128]{3,2,1,0:T(8,128)(2,1)S(1)}, bf16[1,30,16,128]{3,2,1,0:T(8,128)(2,1)S(1)}, bf16[1,15,16,128]{3,2,1,0:T(8,128)(2,1)S(1)}, bf16[...) custom-call(bf16[16,16,16,128]{3,2,1,0:T(8,128)(2,1)} %x_in.1, ...), custom_call_target="tpu_custom_call" | custom-call | bytes 5242880 | tf_op jit(solution)/shard_map/pallas_call | solution.py:105
  1.6 5.1 %collective-permute-start.2 = (bf16[15,16,128]{2,1,0:T(8,128)(2,1)S(1)}, bf16[15,16,128]{2,1,0:T(8,128)(2,1)S(1)}, u32[]{:S(2)}, u32[]{:S(2)}) collective-permute-start(bf16[15,16,128]{2,1,0:T(8,128)(2,1)S(1)} %bitcast.46), channel_id=1, source_target_pairs={{0,3},{1,2},{2,1},{3,0},{4,7},{5,6},{6,5},{7,4},{8,11},{9,10},{10,... | collective-permute-start | bytes 184328 | tf_op jit(solution)/shard_map/ppermute | solution.py:46
  6.7 0.0 collective-permute-start.1
  6.7 0.6 %collective-permute-start = (bf16[30,16,128]{2,1,0:T(8,128)(2,1)S(1)}, bf16[30,16,128]{2,1,0:T(8,128)(2,1)S(1)}, u32[]{:S(2)}, u32[]{:S(2)}) collective-permute-start(bf16[30,16,128]{2,1,0:T(8,128)(2,1)S(1)} %bitcast.44), channel_id=1, source_target_pairs={{0,2},{1,3},{2,0},{3,1},{4,6},{5,7},{6,4},{7,5},{8,10},{9,11},{10,... | collective-permute-start | bytes 368648 | tf_op jit(solution)/shard_map/ppermute | solution.py:44
  7.4 0.7 %collective-permute-start.3 = (bf16[3,16,16,128]{3,2,1,0:T(8,128)(2,1)S(1)}, bf16[3,16,16,128]{3,2,1,0:T(8,128)(2,1)S(1)}, u32[]{:S(2)}, u32[]{:S(2)}) collective-permute-start(bf16[3,16,16,128]{3,2,1,0:T(8,128)(2,1)S(1)} %get-tuple-element.51), channel_id=1, source_target_pairs={{4,8},{8,4},{5,9},{9,5},{6,10},{10,6},{7,11},{11,7},{20,24},{24,20... | collective-permute-start | bytes 589832 | tf_op jit(solution)/shard_map/ppermute | solution.py:63
  8.1 3.1 %collective-permute-start.4 = (bf16[3,16,16,128]{3,2,1,0:T(8,128)(2,1)S(1)}, bf16[3,16,16,128]{3,2,1,0:T(8,128)(2,1)S(1)}, u32[]{:S(2)}, u32[]{:S(2)}) collective-permute-start(bf16[3,16,16,128]{3,2,1,0:T(8,128)(2,1)S(1)} %get-tuple-element.52), channel_id=1, source_target_pairs={{0,4},{4,0},{8,12},{12,8},{1,5},{5,1},{9,13},{13,9},{2,6},{6,2},{1... | collective-permute-start | bytes 589832 | tf_op jit(solution)/shard_map/ppermute | solution.py:63
  11.1 4.7 %shard_map.83 = (f32[16,16,16,128]{3,2,1,0:T(8,128)S(1)}, bf16[1152,384]{1,0:T(8,128)(2,1)S(1)}, bf16[1536,256]{1,0:T(8,128)(2,1)S(1)}, bf16[108,16,128]{2,1,0:T(8,128)(2,1)S(1)}) custom-call(bf16[108,16,128]{2,1,0:T(8,128)(2,1)} %bitcast.52, bf16[18,18,16,128]{3,2,1,0:T(8,128)(2,1)S(1)} %get-tuple-element.41.x.refs_0_, ...), custom_call_target="tpu_custom_call" | custom-call | flops 3623878656 | bytes 6291456 | tf_op jit(solution)/shard_map/pallas_call | solution.py:105
  15.8 0.0 collective-permute-done.2
  15.9 0.0 collective-permute-done.1
  15.9 0.0 collective-permute-done
  15.9 1.6 %collective-permute-start.7 = (bf16[1,3,14,16,128]{4,3,2,1,0:T(8,128)(2,1)S(1)}, bf16[1,3,14,16,128]{4,3,2,1,0:T(8,128)(2,1)S(1)}, u32[]{:S(2)}, u32[]{:S(2)}) collective-permute-start(bf16[1,3,14,16,128]{4,3,2,1,0:T(8,128)(2,1)S(1)} %bitcast.35), channel_id=1, source_target_pairs={{0,16},{16,0},{1,17},{17,1},{2,18},{18,2},{3,19},{19,3},{4,20},{20... | collective-permute-start | bytes 516104 | tf_op jit(solution)/shard_map/ppermute | solution.py:94
  17.5 0.7 %collective-permute-start.5 = (bf16[7,16,128]{2,1,0:T(8,128)(2,1)S(1)}, bf16[7,16,128]{2,1,0:T(8,128)(2,1)S(1)}, u32[]{:S(2)}, u32[]{:S(2)}) collective-permute-start(bf16[7,16,128]{2,1,0:T(8,128)(2,1)S(1)} %get-tuple-element.58), channel_id=1, source_target_pairs={{4,8},{8,4},{5,9},{9,5},{6,10},{10,6},{7,11},{11,7},{20,24},{24,20... | collective-permute-start | bytes 86024 | tf_op jit(solution)/shard_map/ppermute | solution.py:63
  18.1 2.2 %collective-permute-start.6 = (bf16[7,16,128]{2,1,0:T(8,128)(2,1)S(1)}, bf16[7,16,128]{2,1,0:T(8,128)(2,1)S(1)}, u32[]{:S(2)}, u32[]{:S(2)}) collective-permute-start(bf16[7,16,128]{2,1,0:T(8,128)(2,1)S(1)} %get-tuple-element.59), channel_id=1, source_target_pairs={{0,4},{4,0},{8,12},{12,8},{1,5},{5,1},{9,13},{13,9},{2,6},{6,2},{1... | collective-permute-start | bytes 86024 | tf_op jit(solution)/shard_map/ppermute | solution.py:63
  20.3 0.0 collective-permute-done.3.refs_5_
  20.3 0.0 collective-permute-done.4.refs_6_
  20.3 2.5 %shard_map.84 = (f32[14,16,16,128]{3,2,1,0:T(8,128)S(1)}, f32[6,16,16,128]{3,2,1,0:T(8,128)S(1)}, f32[16,128]{1,0:T(8,128)S(1)}) custom-call(bf16[18,18,16,128]{3,2,1,0:T(8,128)(2,1)S(1)} %get-tuple-element.41.x.refs_0_, f32[16,16,16,128]{3,2,1,0:T(8,128)S(1)} %get-tuple-element.47.refs_1_, bf16[1,30,16,128]{3,2,1,0:T(8,128)(2,1)S(1)} %bitcast.32, ...), custom_call_target="tpu_custom_call" | custom-call | tf_op jit(solution)/shard_map/pallas_call | solution.py:105
  22.8 0.0 collective-permute-done.5.outer
  22.9 0.0 collective-permute-done.6.inner
  22.9 0.0 copy-start.3
  22.9 0.0 copy-start.4
  22.9 0.6 %shard_map.86 = (f32[6,16,16,128]{3,2,1,0:T(8,128)S(1)}, f32[16,2,128]{2,1,0:T(2,128)S(1)}) custom-call(f32[16,128]{1,0:T(8,128)S(1)} %get-tuple-element.56.middle_stats, f32[6,16,16,128]{3,2,1,0:T(8,128)S(1)} %get-tuple-element.57.ends, bf16[7,16,128]{2,1,0:T(8,128)(2,1)S(1)} %collective-permute-done.5.outer, ...), custom_call_target="tpu_custom_call" | custom-call | tf_op jit(solution)/shard_map/pallas_call | solution.py:105
  23.5 0.0 collective-permute-done.7.refs_1_
  23.5 0.6 %collective-permute-start.8 = (bf16[2,3,14,16,128]{4,3,2,1,0:T(8,128)(2,1)S(1)}, bf16[2,3,14,16,128]{4,3,2,1,0:T(8,128)(2,1)S(1)}, u32[]{:S(2)}, u32[]{:S(2)}) collective-permute-start(bf16[2,3,14,16,128]{4,3,2,1,0:T(8,128)(2,1)S(1)} %bitcast.27), channel_id=1, source_target_pairs={{0,8},{4,12},{8,0},{12,4},{1,9},{5,13},{9,1},{13,5},{2,10},{6,14},... | collective-permute-start | bytes 1032200 | tf_op jit(solution)/shard_map/ppermute | solution.py:94
  24.1 11.3 %all_to_all.10.stats = f32[16,2,128]{2,1,0:T(2,128)S(1)} all-to-all(f32[16,2,128]{2,1,0:T(2,128)S(1)} %get-tuple-element.63), channel_id=1, replica_groups=mesh['cand'=2,'gz'=4,'yx'=4] {'gz','yx'}, dimensions={0} | all-to-all | bytes 32768 | tf_op jit(solution)/shard_map/all_to_all | solution.py:98
  35.4 0.0 collective-permute-done.8.refs_1_
  35.5 0.2 collective-permute-start.9
  35.7 0.0 copy-done.3
  35.7 0.0 copy-done.4
  35.7 1.1 %shard_map.88 = (bf16[16,16,16,128]{3,2,1,0:T(8,128)(2,1)S(1)}, f32[10,8,8,128]{3,2,1,0:T(8,128)S(1)}, bf16[1,80,128]{2,1,0:T(8,128)(2,1)S(1)}, bf16[1,80,128]{2,1,0:T(8,128)(2,1)S(1)}, f32[1,16,128]{2,1,0:T(8,128)S(1)}) custom-call(f32[14,16,16,128]{3,2,1,0:T(8,128)S(1)} %get-tuple-element.55.inner, f32[6,16,16,128]{3,2,1,0:T(8,128)S(1)} %get-tuple-element.60.ends, ...), custom_call_target="tpu_custom_call" | custom-call | flops 10485760 | bytes 3145728 | tf_op jit(solution)/shard_map/pallas_call | solution.py:105
  36.8 1.5 %collective-permute-start.12 = (f32[16,128]{1,0:T(8,128)S(1)}, f32[16,128]{1,0:T(8,128)S(1)}, u32[]{:S(2)}, u32[]{:S(2)}) collective-permute-start(f32[16,128]{1,0:T(8,128)S(1)} %bitcast.49), channel_id=1, source_target_pairs={{0,3},{1,2},{2,1},{3,0},{4,7},{5,6},{6,5},{7,4},{8,11},{9,10},{10,... | collective-permute-start | bytes 24584 | tf_op jit(solution)/shard_map/ppermute | solution.py:46
  38.3 0.6 %collective-permute-start.10 = (bf16[80,128]{1,0:T(8,128)(2,1)S(1)}, bf16[80,128]{1,0:T(8,128)(2,1)S(1)}, u32[]{:S(2)}, u32[]{:S(2)}) collective-permute-start(bf16[80,128]{1,0:T(8,128)(2,1)S(1)} %bitcast.48), channel_id=1, source_target_pairs={{0,2},{1,3},{2,0},{3,1},{4,6},{5,7},{6,4},{7,5},{8,10},{9,11},{10,... | collective-permute-start | bytes 61448 | tf_op jit(solution)/shard_map/ppermute | solution.py:44
  38.9 2.4 %collective-permute-start.11 = (bf16[80,128]{1,0:T(8,128)(2,1)S(1)}, bf16[80,128]{1,0:T(8,128)(2,1)S(1)}, u32[]{:S(2)}, u32[]{:S(2)}) collective-permute-start(bf16[80,128]{1,0:T(8,128)(2,1)S(1)} %bitcast.47), channel_id=1, source_target_pairs={{0,1},{1,0},{2,3},{3,2},{4,5},{5,4},{6,7},{7,6},{8,9},{9,8},{10,11... | collective-permute-start | bytes 61448 | tf_op jit(solution)/shard_map/ppermute | solution.py:45
  41.3 0.0 collective-permute-done.9.refs_1_
  41.3 0.1 shard_map.90
  41.4 1.4 %shard_map.91 = (f32[2,512,128]{2,1,0:T(8,128)S(1)}, bf16[4,108,16,128]{3,2,1,0:T(8,128)(2,1)S(1)}) custom-call(f32[10,8,8,128]{3,2,1,0:T(8,128)S(1)} %get-tuple-element.66.pooled, bf16[108,16,128]{2,1,0:T(8,128)(2,1)S(1)} %get-tuple-element.67.own, bf16[8,3,14,16,128]{4,3,2,1,0:T(8,128)(2,1)S(1)} %bitcast.26), custom_call_target="tpu_custom_call" | custom-call | flops 905969664 | bytes 4194304 | tf_op jit(solution)/shard_map/pallas_call | solution.py:105
  42.8 0.0 copy-start
  42.8 0.0 copy-start.1
  42.9 0.0 copy-start.2
  42.9 0.0 collective-permute-done.12
  42.9 0.1 collective-permute-done.10
  43.0 0.2 collective-permute-done.11
  43.2 0.7 %shard_map.92 = (f32[2,512,128]{2,1,0:T(8,128)S(1)}, f32[16,2,256]{2,1,0:T(2,128)S(1)}) custom-call(f32[2,512,128]{2,1,0:T(8,128)S(1)} %get-tuple-element.69.own, bf16[1,80,128]{2,1,0:T(8,128)(2,1)S(1)} %bitcast.37, bf16[1,80,128]{2,1,0:T(8,128)(2,1)S(1)} %bitcast.38, f32[1,16,128]{2,1,0:T(8,128)S(1)} %bitcast.39, ...), custom_call_target="tpu_custom_call" | custom-call | flops 67108864 | bytes 3145728 | tf_op jit(solution)/shard_map/pallas_call | solution.py:105
  43.9 10.4 %all_to_all.11.stats = f32[16,2,256]{2,1,0:T(2,128)S(1)} all-to-all(f32[16,2,256]{2,1,0:T(2,128)S(1)} %get-tuple-element.75), channel_id=1, replica_groups=mesh['cand'=2,'gz'=4,'yx'=4] {'gz','yx'}, dimensions={0} | all-to-all | bytes 65536 | tf_op jit(solution)/shard_map/all_to_all | solution.py:98
  54.3 0.0 copy-done
  54.3 0.0 copy-done.1
  54.3 0.0 copy-done.2
  54.4 1.5 %shard_map.93 = bf16[16,16,16,128]{3,2,1,0:T(8,128)(2,1)} custom-call(f32[2,512,128]{2,1,0:T(8,128)S(1)} %get-tuple-element.74.act, f32[16,2,256]{2,1,0:T(2,128)S(1)} %all_to_all.11.stats, f32[1,256]{1,0:T(1,128)S(1)} %bitcast.40, f32[1,256]{1,0:T(1,128)S(1)} %bitcast.41, bf16[256,128]{1,0:T(8,128)(2,1)S(1)} %copy-done, ...), custom_call_target="tpu_custom_call" | custom-call | flops 67108864 | bytes 3145728 | tf_op jit(solution)/shard_map/pallas_call | solution.py:105
  (3 shorter events, 0.1 us)
Async XLA Ops:
  1.6 14.2 %collective-permute-start.2 = (bf16[15,16,128]{2,1,0:T(8,128)(2,1)S(1)}, bf16[15,16,128]{2,1,0:T(8,128)(2,1)S(1)}, u32[]{:S(2)}, u32[]{:S(2)}) collective-permute-start(bf16[15,16,128]{2,1,0:T(8,128)(2,1)S(1)} %bitcast.46), channel_id=1, source_target_pairs={{0,3},{1,2},{2,1},{3,0},{4,7},{5,6},{6,5},{7,4},{8,11},{9,10},{10,... | collective-permute-start | bytes 184328 | tf_op jit(solution)/shard_map/ppermute | solution.py:46
  6.7 9.1 %collective-permute-start.1 = (bf16[30,16,128]{2,1,0:T(8,128)(2,1)S(1)}, bf16[30,16,128]{2,1,0:T(8,128)(2,1)S(1)}, u32[]{:S(2)}, u32[]{:S(2)}) collective-permute-start(bf16[30,16,128]{2,1,0:T(8,128)(2,1)S(1)} %bitcast.45), channel_id=1, source_target_pairs={{0,1},{1,0},{2,3},{3,2},{4,5},{5,4},{6,7},{7,6},{8,9},{9,8},{10,11... | collective-permute-start | bytes 368648 | tf_op jit(solution)/shard_map/ppermute | solution.py:45
  6.7 9.1 %collective-permute-start = (bf16[30,16,128]{2,1,0:T(8,128)(2,1)S(1)}, bf16[30,16,128]{2,1,0:T(8,128)(2,1)S(1)}, u32[]{:S(2)}, u32[]{:S(2)}) collective-permute-start(bf16[30,16,128]{2,1,0:T(8,128)(2,1)S(1)} %bitcast.44), channel_id=1, source_target_pairs={{0,2},{1,3},{2,0},{3,1},{4,6},{5,7},{6,4},{7,5},{8,10},{9,11},{10,... | collective-permute-start | bytes 368648 | tf_op jit(solution)/shard_map/ppermute | solution.py:44
  7.4 12.9 %collective-permute-start.3 = (bf16[3,16,16,128]{3,2,1,0:T(8,128)(2,1)S(1)}, bf16[3,16,16,128]{3,2,1,0:T(8,128)(2,1)S(1)}, u32[]{:S(2)}, u32[]{:S(2)}) collective-permute-start(bf16[3,16,16,128]{3,2,1,0:T(8,128)(2,1)S(1)} %get-tuple-element.51), channel_id=1, source_target_pairs={{4,8},{8,4},{5,9},{9,5},{6,10},{10,6},{7,11},{11,7},{20,24},{24,20... | collective-permute-start | bytes 589832 | tf_op jit(solution)/shard_map/ppermute | solution.py:63
  8.1 12.3 %collective-permute-start.4 = (bf16[3,16,16,128]{3,2,1,0:T(8,128)(2,1)S(1)}, bf16[3,16,16,128]{3,2,1,0:T(8,128)(2,1)S(1)}, u32[]{:S(2)}, u32[]{:S(2)}) collective-permute-start(bf16[3,16,16,128]{3,2,1,0:T(8,128)(2,1)S(1)} %get-tuple-element.52), channel_id=1, source_target_pairs={{0,4},{4,0},{8,12},{12,8},{1,5},{5,1},{9,13},{13,9},{2,6},{6,2},{1... | collective-permute-start | bytes 589832 | tf_op jit(solution)/shard_map/ppermute | solution.py:63
  15.9 7.6 %collective-permute-start.7 = (bf16[1,3,14,16,128]{4,3,2,1,0:T(8,128)(2,1)S(1)}, bf16[1,3,14,16,128]{4,3,2,1,0:T(8,128)(2,1)S(1)}, u32[]{:S(2)}, u32[]{:S(2)}) collective-permute-start(bf16[1,3,14,16,128]{4,3,2,1,0:T(8,128)(2,1)S(1)} %bitcast.35), channel_id=1, source_target_pairs={{0,16},{16,0},{1,17},{17,1},{2,18},{18,2},{3,19},{19,3},{4,20},{20... | collective-permute-start | bytes 516104 | tf_op jit(solution)/shard_map/ppermute | solution.py:94
  17.5 5.4 %collective-permute-start.5 = (bf16[7,16,128]{2,1,0:T(8,128)(2,1)S(1)}, bf16[7,16,128]{2,1,0:T(8,128)(2,1)S(1)}, u32[]{:S(2)}, u32[]{:S(2)}) collective-permute-start(bf16[7,16,128]{2,1,0:T(8,128)(2,1)S(1)} %get-tuple-element.58), channel_id=1, source_target_pairs={{4,8},{8,4},{5,9},{9,5},{6,10},{10,6},{7,11},{11,7},{20,24},{24,20... | collective-permute-start | bytes 86024 | tf_op jit(solution)/shard_map/ppermute | solution.py:63
  18.1 4.7 %collective-permute-start.6 = (bf16[7,16,128]{2,1,0:T(8,128)(2,1)S(1)}, bf16[7,16,128]{2,1,0:T(8,128)(2,1)S(1)}, u32[]{:S(2)}, u32[]{:S(2)}) collective-permute-start(bf16[7,16,128]{2,1,0:T(8,128)(2,1)S(1)} %get-tuple-element.59), channel_id=1, source_target_pairs={{0,4},{4,0},{8,12},{12,8},{1,5},{5,1},{9,13},{13,9},{2,6},{6,2},{1... | collective-permute-start | bytes 86024 | tf_op jit(solution)/shard_map/ppermute | solution.py:63
  22.9 12.8 %copy-start.3 = (f32[128]{0:T(128)S(1)}, f32[128]{0:T(128)}, u32[]{:S(2)}) copy-start(f32[128]{0:T(128)} %param.10) | copy-start | bytes 1540
  22.9 12.8 %copy-start.4 = (f32[128]{0:T(128)S(1)}, f32[128]{0:T(128)}, u32[]{:S(2)}) copy-start(f32[128]{0:T(128)} %param.11) | copy-start | bytes 1540
  23.5 11.9 %collective-permute-start.8 = (bf16[2,3,14,16,128]{4,3,2,1,0:T(8,128)(2,1)S(1)}, bf16[2,3,14,16,128]{4,3,2,1,0:T(8,128)(2,1)S(1)}, u32[]{:S(2)}, u32[]{:S(2)}) collective-permute-start(bf16[2,3,14,16,128]{4,3,2,1,0:T(8,128)(2,1)S(1)} %bitcast.27), channel_id=1, source_target_pairs={{0,8},{4,12},{8,0},{12,4},{1,9},{5,13},{9,1},{13,5},{2,10},{6,14},... | collective-permute-start | bytes 1032200 | tf_op jit(solution)/shard_map/ppermute | solution.py:94
  35.5 5.8 %collective-permute-start.9 = (bf16[4,3,14,16,128]{4,3,2,1,0:T(8,128)(2,1)S(1)}, bf16[4,3,14,16,128]{4,3,2,1,0:T(8,128)(2,1)S(1)}, u32[]{:S(2)}, u32[]{:S(2)}) collective-permute-start(bf16[4,3,14,16,128]{4,3,2,1,0:T(8,128)(2,1)S(1)} %bitcast.24), channel_id=1, source_target_pairs={{0,4},{4,0},{8,12},{12,8},{1,5},{5,1},{9,13},{13,9},{2,6},{6,2},{1... | collective-permute-start | bytes 2064392 | tf_op jit(solution)/shard_map/ppermute | solution.py:94
  36.8 6.0 %collective-permute-start.12 = (f32[16,128]{1,0:T(8,128)S(1)}, f32[16,128]{1,0:T(8,128)S(1)}, u32[]{:S(2)}, u32[]{:S(2)}) collective-permute-start(f32[16,128]{1,0:T(8,128)S(1)} %bitcast.49), channel_id=1, source_target_pairs={{0,3},{1,2},{2,1},{3,0},{4,7},{5,6},{6,5},{7,4},{8,11},{9,10},{10,... | collective-permute-start | bytes 24584 | tf_op jit(solution)/shard_map/ppermute | solution.py:46
  38.3 4.7 %collective-permute-start.10 = (bf16[80,128]{1,0:T(8,128)(2,1)S(1)}, bf16[80,128]{1,0:T(8,128)(2,1)S(1)}, u32[]{:S(2)}, u32[]{:S(2)}) collective-permute-start(bf16[80,128]{1,0:T(8,128)(2,1)S(1)} %bitcast.48), channel_id=1, source_target_pairs={{0,2},{1,3},{2,0},{3,1},{4,6},{5,7},{6,4},{7,5},{8,10},{9,11},{10,... | collective-permute-start | bytes 61448 | tf_op jit(solution)/shard_map/ppermute | solution.py:44
  38.9 4.3 %collective-permute-start.11 = (bf16[80,128]{1,0:T(8,128)(2,1)S(1)}, bf16[80,128]{1,0:T(8,128)(2,1)S(1)}, u32[]{:S(2)}, u32[]{:S(2)}) collective-permute-start(bf16[80,128]{1,0:T(8,128)(2,1)S(1)} %bitcast.47), channel_id=1, source_target_pairs={{0,1},{1,0},{2,3},{3,2},{4,5},{5,4},{6,7},{7,6},{8,9},{9,8},{10,11... | collective-permute-start | bytes 61448 | tf_op jit(solution)/shard_map/ppermute | solution.py:45
  42.8 11.5 %copy-start = (bf16[256,128]{1,0:T(8,128)(2,1)S(1)}, bf16[256,128]{1,0:T(8,128)(2,1)}, u32[]{:S(2)}) copy-start(bf16[256,128]{1,0:T(8,128)(2,1)} %up.1) | copy-start | bytes 196612
  42.8 11.5 %copy-start.1 = (f32[256]{0:T(256)S(1)}, f32[256]{0:T(256)}, u32[]{:S(2)}) copy-start(f32[256]{0:T(256)} %param.13) | copy-start | bytes 3076
  42.9 11.5 %copy-start.2 = (f32[256]{0:T(256)S(1)}, f32[256]{0:T(256)}, u32[]{:S(2)}) copy-start(f32[256]{0:T(256)} %param.14) | copy-start | bytes 3076

commit v13 on v12

--- a/solution.py
+++ b/solution.py
@@ -64,7 +64,7 @@
 
 
 class Riders:
-    STEPS = (("cand", 1), ("gz", 2), ("gz", 1))
+    STEPS = (("gz", 2), ("cand", 1), ("gz", 1))
 
     def __init__(self, rows):
         self.tiles = 27 * rows // 16

time: 56.1 us -> 56.3 us (level)
  starting transfers between devices: 19.1 us -> 19.9 us
    ppermute x2, starting transfers between devices: 6.58 us -> 5.97 us  [halos(): corner = lax.ppermute(corners[0], 'yx', self.swap_route(3))]
    ppermute x2, starting transfers between devices: 1.24 us -> 1.86 us  [halos(): y = lax.ppermute(y_edges[0], 'yx', self.swap_route(2))]
  transfers between devices with their start and end apart: 13 -> 13, of which waited for: 2 -> 1; matrix products, arithmetic and copies ran while one was open for 0% -> 0% of each run, Pallas kernels for 19% -> 19%
where the time goes in v13:
time: 56.3 us; the launch traced here: 56 us
  blocking collectives  21.2 us (38%)
  starting transfers between devices  19.9 us (35%)
  Pallas kernels  14.4 us (26%)
    all_to_all x2, blocking collectives, share(): return lax.all_to_all(stats, PART, 0, 0)  21.2 us
    pallas_call x9, Pallas kernels, call(): pl.pallas_call(kernel, out_shape=[jax.ShapeDtypeStruct(shape, dtype) for...  14.3 us
    ppermute x2, starting transfers between devices, halos(): corner = lax.ppermute(corners[0], 'yx', self.swap_route(3))  5.97 us
    ppermute x2, starting transfers between devices, swap_depth(): lax.ppermute(inner, 'gz', routes[0])  5.77 us
    ppermute x3, starting transfers between devices, swap(): lax.ppermute(block, axis, [(i, i ^ mask) for i in range(lax.axis_size(axi...  2.56 us
    ppermute x2, starting transfers between devices, halos(): x = lax.ppermute(x_edges[0], 'yx', self.swap_route(1))  2.42 us
    ppermute x2, starting transfers between devices, halos(): y = lax.ppermute(y_edges[0], 'yx', self.swap_route(2))  1.86 us
    ppermute x2, starting transfers between devices, swap_depth(): lax.ppermute(outer, 'gz', routes[1])  1.31 us
  transfers between devices with their start and end apart: 13, of which 1 were waited for; matrix products, arithmetic and copies ran while one was open for 0% of the time, Pallas kernels for 19%

profile of v13, /device:TPU:0, one launch (start us, length us, event | category | flops | bytes accessed | tf_op | source)
XLA Modules:
  0.0 56.0 jit_solution(4430823847265201717)
XLA Ops:
  0.0 1.6 %shard_map.82 = (bf16[1,30,16,128]{3,2,1,0:T(8,128)(2,1)S(1)}, bf16[1,30,16,128]{3,2,1,0:T(8,128)(2,1)S(1)}, bf16[1,15,16,128]{3,2,1,0:T(8,128)(2,1)S(1)}, bf16[...) custom-call(bf16[16,16,16,128]{3,2,1,0:T(8,128)(2,1)} %x_in.1, ...), custom_call_target="tpu_custom_call" | custom-call | bytes 5242880 | tf_op jit(solution)/shard_map/pallas_call | solution.py:105
  1.6 5.1 %collective-permute-start.2 = (bf16[15,16,128]{2,1,0:T(8,128)(2,1)S(1)}, bf16[15,16,128]{2,1,0:T(8,128)(2,1)S(1)}, u32[]{:S(2)}, u32[]{:S(2)}) collective-permute-start(bf16[15,16,128]{2,1,0:T(8,128)(2,1)S(1)} %bitcast.46), channel_id=1, source_target_pairs={{0,3},{1,2},{2,1},{3,0},{4,7},{5,6},{6,5},{7,4},{8,11},{9,10},{10,... | collective-permute-start | bytes 184328 | tf_op jit(solution)/shard_map/ppermute | solution.py:46
  6.7 0.0 collective-permute-start.1
  6.7 0.6 %collective-permute-start = (bf16[30,16,128]{2,1,0:T(8,128)(2,1)S(1)}, bf16[30,16,128]{2,1,0:T(8,128)(2,1)S(1)}, u32[]{:S(2)}, u32[]{:S(2)}) collective-permute-start(bf16[30,16,128]{2,1,0:T(8,128)(2,1)S(1)} %bitcast.44), channel_id=1, source_target_pairs={{0,2},{1,3},{2,0},{3,1},{4,6},{5,7},{6,4},{7,5},{8,10},{9,11},{10,... | collective-permute-start | bytes 368648 | tf_op jit(solution)/shard_map/ppermute | solution.py:44
  7.4 0.7 %collective-permute-start.3 = (bf16[3,16,16,128]{3,2,1,0:T(8,128)(2,1)S(1)}, bf16[3,16,16,128]{3,2,1,0:T(8,128)(2,1)S(1)}, u32[]{:S(2)}, u32[]{:S(2)}) collective-permute-start(bf16[3,16,16,128]{3,2,1,0:T(8,128)(2,1)S(1)} %get-tuple-element.51), channel_id=1, source_target_pairs={{4,8},{8,4},{5,9},{9,5},{6,10},{10,6},{7,11},{11,7},{20,24},{24,20... | collective-permute-start | bytes 589832 | tf_op jit(solution)/shard_map/ppermute | solution.py:63
  8.1 3.1 %collective-permute-start.4 = (bf16[3,16,16,128]{3,2,1,0:T(8,128)(2,1)S(1)}, bf16[3,16,16,128]{3,2,1,0:T(8,128)(2,1)S(1)}, u32[]{:S(2)}, u32[]{:S(2)}) collective-permute-start(bf16[3,16,16,128]{3,2,1,0:T(8,128)(2,1)S(1)} %get-tuple-element.52), channel_id=1, source_target_pairs={{0,4},{4,0},{8,12},{12,8},{1,5},{5,1},{9,13},{13,9},{2,6},{6,2},{1... | collective-permute-start | bytes 589832 | tf_op jit(solution)/shard_map/ppermute | solution.py:63
  11.1 4.7 %shard_map.83 = (f32[16,16,16,128]{3,2,1,0:T(8,128)S(1)}, bf16[1152,384]{1,0:T(8,128)(2,1)S(1)}, bf16[1536,256]{1,0:T(8,128)(2,1)S(1)}, bf16[108,16,128]{2,1,0:T(8,128)(2,1)S(1)}) custom-call(bf16[108,16,128]{2,1,0:T(8,128)(2,1)} %bitcast.52, bf16[18,18,16,128]{3,2,1,0:T(8,128)(2,1)S(1)} %get-tuple-element.41.x.refs_0_, ...), custom_call_target="tpu_custom_call" | custom-call | flops 3623878656 | bytes 6291456 | tf_op jit(solution)/shard_map/pallas_call | solution.py:105
  15.8 0.0 collective-permute-done.2
  15.9 0.0 collective-permute-done.1
  15.9 0.0 collective-permute-done
  15.9 0.8 %collective-permute-start.7 = (bf16[1,3,14,16,128]{4,3,2,1,0:T(8,128)(2,1)S(1)}, bf16[1,3,14,16,128]{4,3,2,1,0:T(8,128)(2,1)S(1)}, u32[]{:S(2)}, u32[]{:S(2)}) collective-permute-start(bf16[1,3,14,16,128]{4,3,2,1,0:T(8,128)(2,1)S(1)} %bitcast.35), channel_id=1, source_target_pairs={{0,8},{4,12},{8,0},{12,4},{1,9},{5,13},{9,1},{13,5},{2,10},{6,14},... | collective-permute-start | bytes 516104 | tf_op jit(solution)/shard_map/ppermute | solution.py:94
  16.7 0.7 %collective-permute-start.5 = (bf16[7,16,128]{2,1,0:T(8,128)(2,1)S(1)}, bf16[7,16,128]{2,1,0:T(8,128)(2,1)S(1)}, u32[]{:S(2)}, u32[]{:S(2)}) collective-permute-start(bf16[7,16,128]{2,1,0:T(8,128)(2,1)S(1)} %get-tuple-element.58), channel_id=1, source_target_pairs={{4,8},{8,4},{5,9},{9,5},{6,10},{10,6},{7,11},{11,7},{20,24},{24,20... | collective-permute-start | bytes 86024 | tf_op jit(solution)/shard_map/ppermute | solution.py:63
  17.4 2.7 %collective-permute-start.6 = (bf16[7,16,128]{2,1,0:T(8,128)(2,1)S(1)}, bf16[7,16,128]{2,1,0:T(8,128)(2,1)S(1)}, u32[]{:S(2)}, u32[]{:S(2)}) collective-permute-start(bf16[7,16,128]{2,1,0:T(8,128)(2,1)S(1)} %get-tuple-element.59), channel_id=1, source_target_pairs={{0,4},{4,0},{8,12},{12,8},{1,5},{5,1},{9,13},{13,9},{2,6},{6,2},{1... | collective-permute-start | bytes 86024 | tf_op jit(solution)/shard_map/ppermute | solution.py:63
  20.1 0.0 collective-permute-done.3.refs_5_
  20.1 0.0 collective-permute-done.4.refs_6_
  20.1 2.5 %shard_map.84 = (f32[14,16,16,128]{3,2,1,0:T(8,128)S(1)}, f32[6,16,16,128]{3,2,1,0:T(8,128)S(1)}, f32[16,128]{1,0:T(8,128)S(1)}) custom-call(bf16[18,18,16,128]{3,2,1,0:T(8,128)(2,1)S(1)} %get-tuple-element.41.x.refs_0_, f32[16,16,16,128]{3,2,1,0:T(8,128)S(1)} %get-tuple-element.47.refs_1_, bf16[1,30,16,128]{3,2,1,0:T(8,128)(2,1)S(1)} %bitcast.32, ...), custom_call_target="tpu_custom_call" | custom-call | tf_op jit(solution)/shard_map/pallas_call | solution.py:105
  22.6 0.0 collective-permute-done.5.outer
  22.6 0.0 collective-permute-done.6.inner
  22.6 0.0 copy-start.3
  22.6 0.0 copy-start.4
  22.7 0.6 %shard_map.86 = (f32[6,16,16,128]{3,2,1,0:T(8,128)S(1)}, f32[16,2,128]{2,1,0:T(2,128)S(1)}) custom-call(f32[16,128]{1,0:T(8,128)S(1)} %get-tuple-element.56.middle_stats, f32[6,16,16,128]{3,2,1,0:T(8,128)S(1)} %get-tuple-element.57.ends, bf16[7,16,128]{2,1,0:T(8,128)(2,1)S(1)} %collective-permute-done.5.outer, ...), custom_call_target="tpu_custom_call" | custom-call | tf_op jit(solution)/shard_map/pallas_call | solution.py:105
  23.3 0.0 collective-permute-done.7.refs_1_
  23.3 1.6 %collective-permute-start.8 = (bf16[2,3,14,16,128]{4,3,2,1,0:T(8,128)(2,1)S(1)}, bf16[2,3,14,16,128]{4,3,2,1,0:T(8,128)(2,1)S(1)}, u32[]{:S(2)}, u32[]{:S(2)}) collective-permute-start(bf16[2,3,14,16,128]{4,3,2,1,0:T(8,128)(2,1)S(1)} %bitcast.27), channel_id=1, source_target_pairs={{0,16},{16,0},{1,17},{17,1},{2,18},{18,2},{3,19},{19,3},{4,20},{20... | collective-permute-start | bytes 1032200 | tf_op jit(solution)/shard_map/ppermute | solution.py:94
  24.9 11.2 %all_to_all.10.stats = f32[16,2,128]{2,1,0:T(2,128)S(1)} all-to-all(f32[16,2,128]{2,1,0:T(2,128)S(1)} %get-tuple-element.63), channel_id=1, replica_groups=mesh['cand'=2,'gz'=4,'yx'=4] {'gz','yx'}, dimensions={0} | all-to-all | bytes 32768 | tf_op jit(solution)/shard_map/all_to_all | solution.py:98
  36.1 0.0 collective-permute-done.8.refs_1_
  36.1 0.2 collective-permute-start.9
  36.3 0.0 copy-done.3
  36.3 0.0 copy-done.4
  36.3 1.1 %shard_map.88 = (bf16[16,16,16,128]{3,2,1,0:T(8,128)(2,1)S(1)}, f32[10,8,8,128]{3,2,1,0:T(8,128)S(1)}, bf16[1,80,128]{2,1,0:T(8,128)(2,1)S(1)}, bf16[1,80,128]{2,1,0:T(8,128)(2,1)S(1)}, f32[1,16,128]{2,1,0:T(8,128)S(1)}) custom-call(f32[14,16,16,128]{3,2,1,0:T(8,128)S(1)} %get-tuple-element.55.inner, f32[6,16,16,128]{3,2,1,0:T(8,128)S(1)} %get-tuple-element.60.ends, ...), custom_call_target="tpu_custom_call" | custom-call | flops 10485760 | bytes 3145728 | tf_op jit(solution)/shard_map/pallas_call | solution.py:105
  37.5 0.9 %collective-permute-start.12 = (f32[16,128]{1,0:T(8,128)S(1)}, f32[16,128]{1,0:T(8,128)S(1)}, u32[]{:S(2)}, u32[]{:S(2)}) collective-permute-start(f32[16,128]{1,0:T(8,128)S(1)} %bitcast.49), channel_id=1, source_target_pairs={{0,3},{1,2},{2,1},{3,0},{4,7},{5,6},{6,5},{7,4},{8,11},{9,10},{10,... | collective-permute-start | bytes 24584 | tf_op jit(solution)/shard_map/ppermute | solution.py:46
  38.3 1.2 %collective-permute-start.10 = (bf16[80,128]{1,0:T(8,128)(2,1)S(1)}, bf16[80,128]{1,0:T(8,128)(2,1)S(1)}, u32[]{:S(2)}, u32[]{:S(2)}) collective-permute-start(bf16[80,128]{1,0:T(8,128)(2,1)S(1)} %bitcast.48), channel_id=1, source_target_pairs={{0,2},{1,3},{2,0},{3,1},{4,6},{5,7},{6,4},{7,5},{8,10},{9,11},{10,... | collective-permute-start | bytes 61448 | tf_op jit(solution)/shard_map/ppermute | solution.py:44
  39.5 2.4 %collective-permute-start.11 = (bf16[80,128]{1,0:T(8,128)(2,1)S(1)}, bf16[80,128]{1,0:T(8,128)(2,1)S(1)}, u32[]{:S(2)}, u32[]{:S(2)}) collective-permute-start(bf16[80,128]{1,0:T(8,128)(2,1)S(1)} %bitcast.47), channel_id=1, source_target_pairs={{0,1},{1,0},{2,3},{3,2},{4,5},{5,4},{6,7},{7,6},{8,9},{9,8},{10,11... | collective-permute-start | bytes 61448 | tf_op jit(solution)/shard_map/ppermute | solution.py:45
  42.0 0.0 collective-permute-done.9.refs_1_
  42.0 0.1 shard_map.90
  42.1 1.4 %shard_map.91 = (f32[2,512,128]{2,1,0:T(8,128)S(1)}, bf16[4,108,16,128]{3,2,1,0:T(8,128)(2,1)S(1)}) custom-call(f32[10,8,8,128]{3,2,1,0:T(8,128)S(1)} %get-tuple-element.66.pooled, bf16[108,16,128]{2,1,0:T(8,128)(2,1)S(1)} %get-tuple-element.67.own, bf16[8,3,14,16,128]{4,3,2,1,0:T(8,128)(2,1)S(1)} %bitcast.26), custom_call_target="tpu_custom_call" | custom-call | flops 905969664 | bytes 4194304 | tf_op jit(solution)/shard_map/pallas_call | solution.py:105
  43.5 0.0 copy-start
  43.5 0.0 copy-start.1
  43.5 0.0 copy-start.2
  43.5 0.0 collective-permute-done.12
  43.5 0.0 collective-permute-done.10
  43.5 0.2 collective-permute-done.11
  43.7 0.7 %shard_map.92 = (f32[2,512,128]{2,1,0:T(8,128)S(1)}, f32[16,2,256]{2,1,0:T(2,128)S(1)}) custom-call(f32[2,512,128]{2,1,0:T(8,128)S(1)} %get-tuple-element.69.own, bf16[1,80,128]{2,1,0:T(8,128)(2,1)S(1)} %bitcast.37, bf16[1,80,128]{2,1,0:T(8,128)(2,1)S(1)} %bitcast.38, f32[1,16,128]{2,1,0:T(8,128)S(1)} %bitcast.39, ...), custom_call_target="tpu_custom_call" | custom-call | flops 67108864 | bytes 3145728 | tf_op jit(solution)/shard_map/pallas_call | solution.py:105
  44.4 10.0 %all_to_all.11.stats = f32[16,2,256]{2,1,0:T(2,128)S(1)} all-to-all(f32[16,2,256]{2,1,0:T(2,128)S(1)} %get-tuple-element.75), channel_id=1, replica_groups=mesh['cand'=2,'gz'=4,'yx'=4] {'gz','yx'}, dimensions={0} | all-to-all | bytes 65536 | tf_op jit(solution)/shard_map/all_to_all | solution.py:98
  54.5 0.0 copy-done
  54.5 0.0 copy-done.1
  54.5 0.0 copy-done.2
  54.5 1.5 %shard_map.93 = bf16[16,16,16,128]{3,2,1,0:T(8,128)(2,1)} custom-call(f32[2,512,128]{2,1,0:T(8,128)S(1)} %get-tuple-element.74.act, f32[16,2,256]{2,1,0:T(2,128)S(1)} %all_to_all.11.stats, f32[1,256]{1,0:T(1,128)S(1)} %bitcast.40, f32[1,256]{1,0:T(1,128)S(1)} %bitcast.41, bf16[256,128]{1,0:T(8,128)(2,1)S(1)} %copy-done, ...), custom_call_target="tpu_custom_call" | custom-call | flops 67108864 | bytes 3145728 | tf_op jit(solution)/shard_map/pallas_call | solution.py:105
  (3 shorter events, 0.1 us)
Async XLA Ops:
  1.6 14.2 %collective-permute-start.2 = (bf16[15,16,128]{2,1,0:T(8,128)(2,1)S(1)}, bf16[15,16,128]{2,1,0:T(8,128)(2,1)S(1)}, u32[]{:S(2)}, u32[]{:S(2)}) collective-permute-start(bf16[15,16,128]{2,1,0:T(8,128)(2,1)S(1)} %bitcast.46), channel_id=1, source_target_pairs={{0,3},{1,2},{2,1},{3,0},{4,7},{5,6},{6,5},{7,4},{8,11},{9,10},{10,... | collective-permute-start | bytes 184328 | tf_op jit(solution)/shard_map/ppermute | solution.py:46
  6.7 9.1 %collective-permute-start.1 = (bf16[30,16,128]{2,1,0:T(8,128)(2,1)S(1)}, bf16[30,16,128]{2,1,0:T(8,128)(2,1)S(1)}, u32[]{:S(2)}, u32[]{:S(2)}) collective-permute-start(bf16[30,16,128]{2,1,0:T(8,128)(2,1)S(1)} %bitcast.45), channel_id=1, source_target_pairs={{0,1},{1,0},{2,3},{3,2},{4,5},{5,4},{6,7},{7,6},{8,9},{9,8},{10,11... | collective-permute-start | bytes 368648 | tf_op jit(solution)/shard_map/ppermute | solution.py:45
  6.7 9.1 %collective-permute-start = (bf16[30,16,128]{2,1,0:T(8,128)(2,1)S(1)}, bf16[30,16,128]{2,1,0:T(8,128)(2,1)S(1)}, u32[]{:S(2)}, u32[]{:S(2)}) collective-permute-start(bf16[30,16,128]{2,1,0:T(8,128)(2,1)S(1)} %bitcast.44), channel_id=1, source_target_pairs={{0,2},{1,3},{2,0},{3,1},{4,6},{5,7},{6,4},{7,5},{8,10},{9,11},{10,... | collective-permute-start | bytes 368648 | tf_op jit(solution)/shard_map/ppermute | solution.py:44
  7.4 12.7 %collective-permute-start.3 = (bf16[3,16,16,128]{3,2,1,0:T(8,128)(2,1)S(1)}, bf16[3,16,16,128]{3,2,1,0:T(8,128)(2,1)S(1)}, u32[]{:S(2)}, u32[]{:S(2)}) collective-permute-start(bf16[3,16,16,128]{3,2,1,0:T(8,128)(2,1)S(1)} %get-tuple-element.51), channel_id=1, source_target_pairs={{4,8},{8,4},{5,9},{9,5},{6,10},{10,6},{7,11},{11,7},{20,24},{24,20... | collective-permute-start | bytes 589832 | tf_op jit(solution)/shard_map/ppermute | solution.py:63
  8.1 12.0 %collective-permute-start.4 = (bf16[3,16,16,128]{3,2,1,0:T(8,128)(2,1)S(1)}, bf16[3,16,16,128]{3,2,1,0:T(8,128)(2,1)S(1)}, u32[]{:S(2)}, u32[]{:S(2)}) collective-permute-start(bf16[3,16,16,128]{3,2,1,0:T(8,128)(2,1)S(1)} %get-tuple-element.52), channel_id=1, source_target_pairs={{0,4},{4,0},{8,12},{12,8},{1,5},{5,1},{9,13},{13,9},{2,6},{6,2},{1... | collective-permute-start | bytes 589832 | tf_op jit(solution)/shard_map/ppermute | solution.py:63
  15.9 7.4 %collective-permute-start.7 = (bf16[1,3,14,16,128]{4,3,2,1,0:T(8,128)(2,1)S(1)}, bf16[1,3,14,16,128]{4,3,2,1,0:T(8,128)(2,1)S(1)}, u32[]{:S(2)}, u32[]{:S(2)}) collective-permute-start(bf16[1,3,14,16,128]{4,3,2,1,0:T(8,128)(2,1)S(1)} %bitcast.35), channel_id=1, source_target_pairs={{0,8},{4,12},{8,0},{12,4},{1,9},{5,13},{9,1},{13,5},{2,10},{6,14},... | collective-permute-start | bytes 516104 | tf_op jit(solution)/shard_map/ppermute | solution.py:94
  16.7 5.9 %collective-permute-start.5 = (bf16[7,16,128]{2,1,0:T(8,128)(2,1)S(1)}, bf16[7,16,128]{2,1,0:T(8,128)(2,1)S(1)}, u32[]{:S(2)}, u32[]{:S(2)}) collective-permute-start(bf16[7,16,128]{2,1,0:T(8,128)(2,1)S(1)} %get-tuple-element.58), channel_id=1, source_target_pairs={{4,8},{8,4},{5,9},{9,5},{6,10},{10,6},{7,11},{11,7},{20,24},{24,20... | collective-permute-start | bytes 86024 | tf_op jit(solution)/shard_map/ppermute | solution.py:63
  17.4 5.3 %collective-permute-start.6 = (bf16[7,16,128]{2,1,0:T(8,128)(2,1)S(1)}, bf16[7,16,128]{2,1,0:T(8,128)(2,1)S(1)}, u32[]{:S(2)}, u32[]{:S(2)}) collective-permute-start(bf16[7,16,128]{2,1,0:T(8,128)(2,1)S(1)} %get-tuple-element.59), channel_id=1, source_target_pairs={{0,4},{4,0},{8,12},{12,8},{1,5},{5,1},{9,13},{13,9},{2,6},{6,2},{1... | collective-permute-start | bytes 86024 | tf_op jit(solution)/shard_map/ppermute | solution.py:63
  22.6 13.7 %copy-start.3 = (f32[128]{0:T(128)S(1)}, f32[128]{0:T(128)}, u32[]{:S(2)}) copy-start(f32[128]{0:T(128)} %param.10) | copy-start | bytes 1540
  22.6 13.7 %copy-start.4 = (f32[128]{0:T(128)S(1)}, f32[128]{0:T(128)}, u32[]{:S(2)}) copy-start(f32[128]{0:T(128)} %param.11) | copy-start | bytes 1540
  23.3 12.8 %collective-permute-start.8 = (bf16[2,3,14,16,128]{4,3,2,1,0:T(8,128)(2,1)S(1)}, bf16[2,3,14,16,128]{4,3,2,1,0:T(8,128)(2,1)S(1)}, u32[]{:S(2)}, u32[]{:S(2)}) collective-permute-start(bf16[2,3,14,16,128]{4,3,2,1,0:T(8,128)(2,1)S(1)} %bitcast.27), channel_id=1, source_target_pairs={{0,16},{16,0},{1,17},{17,1},{2,18},{18,2},{3,19},{19,3},{4,20},{20... | collective-permute-start | bytes 1032200 | tf_op jit(solution)/shard_map/ppermute | solution.py:94
  36.1 5.8 %collective-permute-start.9 = (bf16[4,3,14,16,128]{4,3,2,1,0:T(8,128)(2,1)S(1)}, bf16[4,3,14,16,128]{4,3,2,1,0:T(8,128)(2,1)S(1)}, u32[]{:S(2)}, u32[]{:S(2)}) collective-permute-start(bf16[4,3,14,16,128]{4,3,2,1,0:T(8,128)(2,1)S(1)} %bitcast.24), channel_id=1, source_target_pairs={{0,4},{4,0},{8,12},{12,8},{1,5},{5,1},{9,13},{13,9},{2,6},{6,2},{1... | collective-permute-start | bytes 2064392 | tf_op jit(solution)/shard_map/ppermute | solution.py:94
  37.5 6.0 %collective-permute-start.12 = (f32[16,128]{1,0:T(8,128)S(1)}, f32[16,128]{1,0:T(8,128)S(1)}, u32[]{:S(2)}, u32[]{:S(2)}) collective-permute-start(f32[16,128]{1,0:T(8,128)S(1)} %bitcast.49), channel_id=1, source_target_pairs={{0,3},{1,2},{2,1},{3,0},{4,7},{5,6},{6,5},{7,4},{8,11},{9,10},{10,... | collective-permute-start | bytes 24584 | tf_op jit(solution)/shard_map/ppermute | solution.py:46
  38.3 5.2 %collective-permute-start.10 = (bf16[80,128]{1,0:T(8,128)(2,1)S(1)}, bf16[80,128]{1,0:T(8,128)(2,1)S(1)}, u32[]{:S(2)}, u32[]{:S(2)}) collective-permute-start(bf16[80,128]{1,0:T(8,128)(2,1)S(1)} %bitcast.48), channel_id=1, source_target_pairs={{0,2},{1,3},{2,0},{3,1},{4,6},{5,7},{6,4},{7,5},{8,10},{9,11},{10,... | collective-permute-start | bytes 61448 | tf_op jit(solution)/shard_map/ppermute | solution.py:44
  39.5 4.2 %collective-permute-start.11 = (bf16[80,128]{1,0:T(8,128)(2,1)S(1)}, bf16[80,128]{1,0:T(8,128)(2,1)S(1)}, u32[]{:S(2)}, u32[]{:S(2)}) collective-permute-start(bf16[80,128]{1,0:T(8,128)(2,1)S(1)} %bitcast.47), channel_id=1, source_target_pairs={{0,1},{1,0},{2,3},{3,2},{4,5},{5,4},{6,7},{7,6},{8,9},{9,8},{10,11... | collective-permute-start | bytes 61448 | tf_op jit(solution)/shard_map/ppermute | solution.py:45
  43.5 11.0 %copy-start = (bf16[256,128]{1,0:T(8,128)(2,1)S(1)}, bf16[256,128]{1,0:T(8,128)(2,1)}, u32[]{:S(2)}) copy-start(bf16[256,128]{1,0:T(8,128)(2,1)} %up.1) | copy-start | bytes 196612
  43.5 11.0 %copy-start.1 = (f32[256]{0:T(256)S(1)}, f32[256]{0:T(256)}, u32[]{:S(2)}) copy-start(f32[256]{0:T(256)} %param.13) | copy-start | bytes 3076
  43.5 11.0 %copy-start.2 = (f32[256]{0:T(256)S(1)}, f32[256]{0:T(256)}, u32[]{:S(2)}) copy-start(f32[256]{0:T(256)} %param.14) | copy-start | bytes 3076

commit v14 on v13

--- a/solution.py
+++ b/solution.py
@@ -60,7 +60,8 @@
     routes = [[], []]
     for low in range(size - 1):
         routes[low % 2] += [(low, low + 1), (low + 1, low)]
-    return lax.ppermute(outer, "gz", routes[1]), lax.ppermute(inner, "gz", routes[0])
+    inner = lax.ppermute(inner, "gz", routes[0])
+    return lax.ppermute(outer, "gz", routes[1]), inner
 
 
 class Riders:
@@ -344,7 +345,7 @@
 
 
 def side_kernel(ny, nx, *refs):
-    x, own, y_halos, x_halos, corners, outer, inner, taps, pairs, middle, ends, stats, act, grid, column = refs
+    x, own, y_halos, x_halos, corners, inner, outer, taps, pairs, middle, ends, stats, act, grid, column = refs
     edge = own.shape[0]
     depth = edge + 4
     f32 = jnp.float32
@@ -391,7 +392,7 @@
     stats[8:16] = spread
 
 
-def end_kernel(ny, nx, middle_stats, ends, outer, inner, taps, act, stats, faces, column):
+def end_kernel(ny, nx, middle_stats, ends, inner, outer, taps, act, stats, faces, column):
     edge = act.shape[1]
     wide = ny + nx
     f32 = jnp.float32
@@ -763,8 +764,8 @@
         y,
         x,
         corner,
+        inner,
         outer,
-        inner,
         taps,
         pairs,
     )
@@ -774,7 +775,7 @@
         [((2,) + turn[0], bf16), ((5,) + column, f32)],
         stats,
         ends,
-        *turns,
+        *turns[::-1],
         taps,
     )
     if riders.size:

time: 56.3 us -> 56.1 us (level)
  starting transfers between devices: 19.9 us -> 14.9 us
  waiting for transfers between devices: 0.22 us -> 4.14 us
  blocking collectives: 21.2 us -> 22.2 us
    ppermute x4, starting transfers between devices: 7.08 us -> 1.32 us  [the longest x2 1.31 us: swap_depth(): return (lax.ppermute(outer, 'gz', routes[1]), inner)]
    ppermute x3, waiting for transfers between devices: 0.01 us -> 1.63 us  [swap(): lax.ppermute(block, axis, [(i, i ^ mask) for i in range(lax.axis_size(axi...]
    ppermute x2, waiting for transfers between devices: 0.01 us -> 1.59 us  [halos(): y = lax.ppermute(y_edges[0], 'yx', self.swap_route(2))]
    all_to_all x2, blocking collectives: 21.2 us -> 22.2 us  [share(): return lax.all_to_all(stats, PART, 0, 0)]
    ppermute x3, starting transfers between devices: 2.56 us -> 3.34 us  [swap(): lax.ppermute(block, axis, [(i, i ^ mask) for i in range(lax.axis_size(axi...]
    ppermute x2, waiting for transfers between devices: 0.19 us -> 0.89 us  [halos(): x = lax.ppermute(x_edges[0], 'yx', self.swap_route(1))]
  transfers between devices with their start and end apart: 13 -> 13, of which waited for: 1 -> 4; matrix products, arithmetic and copies ran while one was open for 0% -> 0% of each run, Pallas kernels for 19% -> 19%
where the time goes in v14:
time: 56.1 us; the launch traced here: 55.9 us
  blocking collectives  22.2 us (40%)
  starting transfers between devices  14.9 us (27%)
  Pallas kernels  14.4 us (26%)
  waiting for transfers between devices  4.14 us (7%)
    all_to_all x2, blocking collectives, share(): return lax.all_to_all(stats, PART, 0, 0)  22.2 us
    pallas_call x9, Pallas kernels, call(): pl.pallas_call(kernel, out_shape=[jax.ShapeDtypeStruct(shape, dtype) for...  14.3 us
    ppermute x2, starting transfers between devices, halos(): corner = lax.ppermute(corners[0], 'yx', self.swap_route(3))  5.77 us
    ppermute x3, starting transfers between devices, swap(): lax.ppermute(block, axis, [(i, i ^ mask) for i in range(lax.axis_size(axi...  3.34 us
    ppermute x2, starting transfers between devices, halos(): x = lax.ppermute(x_edges[0], 'yx', self.swap_route(1))  2.42 us
    ppermute x2, starting transfers between devices, halos(): y = lax.ppermute(y_edges[0], 'yx', self.swap_route(2))  2.05 us
    ppermute x3, waiting for transfers between devices, swap(): lax.ppermute(block, axis, [(i, i ^ mask) for i in range(lax.axis_size(axi...  1.63 us
    ppermute x2, waiting for transfers between devices, halos(): y = lax.ppermute(y_edges[0], 'yx', self.swap_route(2))  1.59 us
  transfers between devices with their start and end apart: 13, of which 4 were waited for; matrix products, arithmetic and copies ran while one was open for 0% of the time, Pallas kernels for 19%

profile of v14, /device:TPU:0, one launch (start us, length us, event | category | flops | bytes accessed | tf_op | source)
XLA Modules:
  0.0 55.9 jit_solution(11213314343144552673)
XLA Ops:
  0.0 1.6 %shard_map.82 = (bf16[1,30,16,128]{3,2,1,0:T(8,128)(2,1)S(1)}, bf16[1,30,16,128]{3,2,1,0:T(8,128)(2,1)S(1)}, bf16[1,15,16,128]{3,2,1,0:T(8,128)(2,1)S(1)}, bf16[...) custom-call(bf16[16,16,16,128]{3,2,1,0:T(8,128)(2,1)} %x_in.1, ...), custom_call_target="tpu_custom_call" | custom-call | bytes 5242880 | tf_op jit(solution)/shard_map/pallas_call | solution.py:106
  1.6 5.1 %collective-permute-start.2 = (bf16[15,16,128]{2,1,0:T(8,128)(2,1)S(1)}, bf16[15,16,128]{2,1,0:T(8,128)(2,1)S(1)}, u32[]{:S(2)}, u32[]{:S(2)}) collective-permute-start(bf16[15,16,128]{2,1,0:T(8,128)(2,1)S(1)} %bitcast.46), channel_id=1, source_target_pairs={{0,3},{1,2},{2,1},{3,0},{4,7},{5,6},{6,5},{7,4},{8,11},{9,10},{10,... | collective-permute-start | bytes 184328 | tf_op jit(solution)/shard_map/ppermute | solution.py:46
  6.7 0.0 collective-permute-start.1
  6.7 0.6 %collective-permute-start = (bf16[30,16,128]{2,1,0:T(8,128)(2,1)S(1)}, bf16[30,16,128]{2,1,0:T(8,128)(2,1)S(1)}, u32[]{:S(2)}, u32[]{:S(2)}) collective-permute-start(bf16[30,16,128]{2,1,0:T(8,128)(2,1)S(1)} %bitcast.44), channel_id=1, source_target_pairs={{0,2},{1,3},{2,0},{3,1},{4,6},{5,7},{6,4},{7,5},{8,10},{9,11},{10,... | collective-permute-start | bytes 368648 | tf_op jit(solution)/shard_map/ppermute | solution.py:44
  7.4 0.0 collective-permute-start.3
  7.4 0.7 %collective-permute-start.4 = (bf16[3,16,16,128]{3,2,1,0:T(8,128)(2,1)S(1)}, bf16[3,16,16,128]{3,2,1,0:T(8,128)(2,1)S(1)}, u32[]{:S(2)}, u32[]{:S(2)}) collective-permute-start(bf16[3,16,16,128]{3,2,1,0:T(8,128)(2,1)S(1)} %get-tuple-element.52), channel_id=1, source_target_pairs={{4,8},{8,4},{5,9},{9,5},{6,10},{10,6},{7,11},{11,7},{20,24},{24,20... | collective-permute-start | bytes 589832 | tf_op jit(solution)/shard_map/ppermute | solution.py:64
  8.1 4.7 %shard_map.83 = (f32[16,16,16,128]{3,2,1,0:T(8,128)S(1)}, bf16[1152,384]{1,0:T(8,128)(2,1)S(1)}, bf16[1536,256]{1,0:T(8,128)(2,1)S(1)}, bf16[108,16,128]{2,1,0:T(8,128)(2,1)S(1)}) custom-call(bf16[108,16,128]{2,1,0:T(8,128)(2,1)} %bitcast.52, bf16[18,18,16,128]{3,2,1,0:T(8,128)(2,1)S(1)} %get-tuple-element.41.x.refs_0_, ...), custom_call_target="tpu_custom_call" | custom-call | flops 3623878656 | bytes 6291456 | tf_op jit(solution)/shard_map/pallas_call | solution.py:106
  12.8 0.0 collective-permute-done.2
  12.8 0.7 %collective-permute-done.1 = bf16[30,16,128]{2,1,0:T(8,128)(2,1)S(1)} collective-permute-done((bf16[30,16,128]{2,1,0:T(8,128)(2,1)S(1)}, bf16[30,16,128]{2,1,0:T(8,128)(2,1)S(1)}, u32[]{:S(2)}, u32[]{:S(2)}) %collective-permute-start.1) | collective-permute-done | bytes 122912 | tf_op jit(solution)/shard_map/ppermute | solution.py:45
  13.5 1.6 %collective-permute-done = bf16[30,16,128]{2,1,0:T(8,128)(2,1)S(1)} collective-permute-done((bf16[30,16,128]{2,1,0:T(8,128)(2,1)S(1)}, bf16[30,16,128]{2,1,0:T(8,128)(2,1)S(1)}, u32[]{:S(2)}, u32[]{:S(2)}) %collective-permute-start) | collective-permute-done | bytes 122912 | tf_op jit(solution)/shard_map/ppermute | solution.py:44
  15.1 1.6 %collective-permute-start.7 = (bf16[1,3,14,16,128]{4,3,2,1,0:T(8,128)(2,1)S(1)}, bf16[1,3,14,16,128]{4,3,2,1,0:T(8,128)(2,1)S(1)}, u32[]{:S(2)}, u32[]{:S(2)}) collective-permute-start(bf16[1,3,14,16,128]{4,3,2,1,0:T(8,128)(2,1)S(1)} %bitcast.35), channel_id=1, source_target_pairs={{0,8},{4,12},{8,0},{12,4},{1,9},{5,13},{9,1},{13,5},{2,10},{6,14},... | collective-permute-start | bytes 516104 | tf_op jit(solution)/shard_map/ppermute | solution.py:95
  16.7 0.0 collective-permute-start.5
  16.7 0.7 %collective-permute-start.6 = (bf16[7,16,128]{2,1,0:T(8,128)(2,1)S(1)}, bf16[7,16,128]{2,1,0:T(8,128)(2,1)S(1)}, u32[]{:S(2)}, u32[]{:S(2)}) collective-permute-start(bf16[7,16,128]{2,1,0:T(8,128)(2,1)S(1)} %get-tuple-element.59), channel_id=1, source_target_pairs={{4,8},{8,4},{5,9},{9,5},{6,10},{10,6},{7,11},{11,7},{20,24},{24,20... | collective-permute-start | bytes 86024 | tf_op jit(solution)/shard_map/ppermute | solution.py:64
  17.4 0.0 collective-permute-done.3.refs_5_
  17.4 0.0 collective-permute-done.4.refs_6_
  17.4 2.5 %shard_map.84 = (f32[14,16,16,128]{3,2,1,0:T(8,128)S(1)}, f32[6,16,16,128]{3,2,1,0:T(8,128)S(1)}, f32[16,128]{1,0:T(8,128)S(1)}) custom-call(bf16[18,18,16,128]{3,2,1,0:T(8,128)(2,1)S(1)} %get-tuple-element.41.x.refs_0_, f32[16,16,16,128]{3,2,1,0:T(8,128)S(1)} %get-tuple-element.47.refs_1_, bf16[1,30,16,128]{3,2,1,0:T(8,128)(2,1)S(1)} %bitcast.32, ...), custom_call_target="tpu_custom_call" | custom-call | tf_op jit(solution)/shard_map/pallas_call | solution.py:106
  19.9 0.0 collective-permute-done.5.inner
  19.9 0.0 collective-permute-done.6.outer
  19.9 0.0 copy-start.3
  19.9 0.0 copy-start.4
  20.0 0.6 %shard_map.86 = (f32[6,16,16,128]{3,2,1,0:T(8,128)S(1)}, f32[16,2,128]{2,1,0:T(2,128)S(1)}) custom-call(f32[16,128]{1,0:T(8,128)S(1)} %get-tuple-element.56.middle_stats, f32[6,16,16,128]{3,2,1,0:T(8,128)S(1)} %get-tuple-element.57.ends, bf16[7,16,128]{2,1,0:T(8,128)(2,1)S(1)} %collective-permute-done.5.inner, ...), custom_call_target="tpu_custom_call" | custom-call | tf_op jit(solution)/shard_map/pallas_call | solution.py:106
  20.6 1.6 %collective-permute-done.7.refs_1_ = bf16[1,3,14,16,128]{4,3,2,1,0:T(8,128)(2,1)S(1)} collective-permute-done((bf16[1,3,14,16,128]{4,3,2,1,0:T(8,128)(2,1)S(1)}, bf16[1,3,14,16,128]{4,3,2,1,0:T(8,128)(2,1)S(1)}, u32[]{:S(2)}, u32[]{:S(2)}) %collective-permute-start.7) | collective-permute-done | bytes 172064 | tf_op jit(solution)/shard_map/ppermute | solution.py:95
  22.2 1.6 %collective-permute-start.8 = (bf16[2,3,14,16,128]{4,3,2,1,0:T(8,128)(2,1)S(1)}, bf16[2,3,14,16,128]{4,3,2,1,0:T(8,128)(2,1)S(1)}, u32[]{:S(2)}, u32[]{:S(2)}) collective-permute-start(bf16[2,3,14,16,128]{4,3,2,1,0:T(8,128)(2,1)S(1)} %bitcast.27), channel_id=1, source_target_pairs={{0,16},{16,0},{1,17},{17,1},{2,18},{18,2},{3,19},{19,3},{4,20},{20... | collective-permute-start | bytes 1032200 | tf_op jit(solution)/shard_map/ppermute | solution.py:95
  23.8 12.1 %all_to_all.10.stats = f32[16,2,128]{2,1,0:T(2,128)S(1)} all-to-all(f32[16,2,128]{2,1,0:T(2,128)S(1)} %get-tuple-element.63), channel_id=1, replica_groups=mesh['cand'=2,'gz'=4,'yx'=4] {'gz','yx'}, dimensions={0} | all-to-all | bytes 32768 | tf_op jit(solution)/shard_map/all_to_all | solution.py:99
  35.9 0.0 collective-permute-done.8.refs_1_
  36.0 0.2 collective-permute-start.9
  36.2 0.0 copy-done.3
  36.2 0.0 copy-done.4
  36.2 1.1 %shard_map.88 = (bf16[16,16,16,128]{3,2,1,0:T(8,128)(2,1)S(1)}, f32[10,8,8,128]{3,2,1,0:T(8,128)S(1)}, bf16[1,80,128]{2,1,0:T(8,128)(2,1)S(1)}, bf16[1,80,128]{2,1,0:T(8,128)(2,1)S(1)}, f32[1,16,128]{2,1,0:T(8,128)S(1)}) custom-call(f32[14,16,16,128]{3,2,1,0:T(8,128)S(1)} %get-tuple-element.55.inner, f32[6,16,16,128]{3,2,1,0:T(8,128)S(1)} %get-tuple-element.60.ends, ...), custom_call_target="tpu_custom_call" | custom-call | flops 10485760 | bytes 3145728 | tf_op jit(solution)/shard_map/pallas_call | solution.py:106
  37.3 0.7 %collective-permute-start.12 = (f32[16,128]{1,0:T(8,128)S(1)}, f32[16,128]{1,0:T(8,128)S(1)}, u32[]{:S(2)}, u32[]{:S(2)}) collective-permute-start(f32[16,128]{1,0:T(8,128)S(1)} %bitcast.49), channel_id=1, source_target_pairs={{0,3},{1,2},{2,1},{3,0},{4,7},{5,6},{6,5},{7,4},{8,11},{9,10},{10,... | collective-permute-start | bytes 24584 | tf_op jit(solution)/shard_map/ppermute | solution.py:46
  38.0 1.4 %collective-permute-start.10 = (bf16[80,128]{1,0:T(8,128)(2,1)S(1)}, bf16[80,128]{1,0:T(8,128)(2,1)S(1)}, u32[]{:S(2)}, u32[]{:S(2)}) collective-permute-start(bf16[80,128]{1,0:T(8,128)(2,1)S(1)} %bitcast.48), channel_id=1, source_target_pairs={{0,2},{1,3},{2,0},{3,1},{4,6},{5,7},{6,4},{7,5},{8,10},{9,11},{10,... | collective-permute-start | bytes 61448 | tf_op jit(solution)/shard_map/ppermute | solution.py:44
  39.4 2.4 %collective-permute-start.11 = (bf16[80,128]{1,0:T(8,128)(2,1)S(1)}, bf16[80,128]{1,0:T(8,128)(2,1)S(1)}, u32[]{:S(2)}, u32[]{:S(2)}) collective-permute-start(bf16[80,128]{1,0:T(8,128)(2,1)S(1)} %bitcast.47), channel_id=1, source_target_pairs={{0,1},{1,0},{2,3},{3,2},{4,5},{5,4},{6,7},{7,6},{8,9},{9,8},{10,11... | collective-permute-start | bytes 61448 | tf_op jit(solution)/shard_map/ppermute | solution.py:45
  41.8 0.0 collective-permute-done.9.refs_1_
  41.8 0.1 shard_map.90
  41.9 1.4 %shard_map.91 = (f32[2,512,128]{2,1,0:T(8,128)S(1)}, bf16[4,108,16,128]{3,2,1,0:T(8,128)(2,1)S(1)}) custom-call(f32[10,8,8,128]{3,2,1,0:T(8,128)S(1)} %get-tuple-element.66.pooled, bf16[108,16,128]{2,1,0:T(8,128)(2,1)S(1)} %get-tuple-element.67.own, bf16[8,3,14,16,128]{4,3,2,1,0:T(8,128)(2,1)S(1)} %bitcast.26), custom_call_target="tpu_custom_call" | custom-call | flops 905969664 | bytes 4194304 | tf_op jit(solution)/shard_map/pallas_call | solution.py:106
  43.3 0.0 copy-start
  43.3 0.0 copy-start.1
  43.4 0.0 copy-start.2
  43.4 0.0 collective-permute-done.12
  43.4 0.0 collective-permute-done.10
  43.4 0.2 collective-permute-done.11
  43.6 0.7 %shard_map.92 = (f32[2,512,128]{2,1,0:T(8,128)S(1)}, f32[16,2,256]{2,1,0:T(2,128)S(1)}) custom-call(f32[2,512,128]{2,1,0:T(8,128)S(1)} %get-tuple-element.69.own, bf16[1,80,128]{2,1,0:T(8,128)(2,1)S(1)} %bitcast.37, bf16[1,80,128]{2,1,0:T(8,128)(2,1)S(1)} %bitcast.38, f32[1,16,128]{2,1,0:T(8,128)S(1)} %bitcast.39, ...), custom_call_target="tpu_custom_call" | custom-call | flops 67108864 | bytes 3145728 | tf_op jit(solution)/shard_map/pallas_call | solution.py:106
  44.3 10.0 %all_to_all.11.stats = f32[16,2,256]{2,1,0:T(2,128)S(1)} all-to-all(f32[16,2,256]{2,1,0:T(2,128)S(1)} %get-tuple-element.75), channel_id=1, replica_groups=mesh['cand'=2,'gz'=4,'yx'=4] {'gz','yx'}, dimensions={0} | all-to-all | bytes 65536 | tf_op jit(solution)/shard_map/all_to_all | solution.py:99
  54.3 0.0 copy-done
  54.3 0.0 copy-done.1
  54.3 0.0 copy-done.2
  54.3 1.5 %shard_map.93 = bf16[16,16,16,128]{3,2,1,0:T(8,128)(2,1)} custom-call(f32[2,512,128]{2,1,0:T(8,128)S(1)} %get-tuple-element.74.act, f32[16,2,256]{2,1,0:T(2,128)S(1)} %all_to_all.11.stats, f32[1,256]{1,0:T(1,128)S(1)} %bitcast.40, f32[1,256]{1,0:T(1,128)S(1)} %bitcast.41, bf16[256,128]{1,0:T(8,128)(2,1)S(1)} %copy-done, ...), custom_call_target="tpu_custom_call" | custom-call | flops 67108864 | bytes 3145728 | tf_op jit(solution)/shard_map/pallas_call | solution.py:106
  (3 shorter events, 0.1 us)
Async XLA Ops:
  1.6 11.2 %collective-permute-start.2 = (bf16[15,16,128]{2,1,0:T(8,128)(2,1)S(1)}, bf16[15,16,128]{2,1,0:T(8,128)(2,1)S(1)}, u32[]{:S(2)}, u32[]{:S(2)}) collective-permute-start(bf16[15,16,128]{2,1,0:T(8,128)(2,1)S(1)} %bitcast.46), channel_id=1, source_target_pairs={{0,3},{1,2},{2,1},{3,0},{4,7},{5,6},{6,5},{7,4},{8,11},{9,10},{10,... | collective-permute-start | bytes 184328 | tf_op jit(solution)/shard_map/ppermute | solution.py:46
  6.7 6.8 %collective-permute-start.1 = (bf16[30,16,128]{2,1,0:T(8,128)(2,1)S(1)}, bf16[30,16,128]{2,1,0:T(8,128)(2,1)S(1)}, u32[]{:S(2)}, u32[]{:S(2)}) collective-permute-start(bf16[30,16,128]{2,1,0:T(8,128)(2,1)S(1)} %bitcast.45), channel_id=1, source_target_pairs={{0,1},{1,0},{2,3},{3,2},{4,5},{5,4},{6,7},{7,6},{8,9},{9,8},{10,11... | collective-permute-start | bytes 368648 | tf_op jit(solution)/shard_map/ppermute | solution.py:45
  6.7 8.4 %collective-permute-start = (bf16[30,16,128]{2,1,0:T(8,128)(2,1)S(1)}, bf16[30,16,128]{2,1,0:T(8,128)(2,1)S(1)}, u32[]{:S(2)}, u32[]{:S(2)}) collective-permute-start(bf16[30,16,128]{2,1,0:T(8,128)(2,1)S(1)} %bitcast.44), channel_id=1, source_target_pairs={{0,2},{1,3},{2,0},{3,1},{4,6},{5,7},{6,4},{7,5},{8,10},{9,11},{10,... | collective-permute-start | bytes 368648 | tf_op jit(solution)/shard_map/ppermute | solution.py:44
  7.4 10.0 %collective-permute-start.3 = (bf16[3,16,16,128]{3,2,1,0:T(8,128)(2,1)S(1)}, bf16[3,16,16,128]{3,2,1,0:T(8,128)(2,1)S(1)}, u32[]{:S(2)}, u32[]{:S(2)}) collective-permute-start(bf16[3,16,16,128]{3,2,1,0:T(8,128)(2,1)S(1)} %get-tuple-element.51), channel_id=1, source_target_pairs={{0,4},{4,0},{8,12},{12,8},{1,5},{5,1},{9,13},{13,9},{2,6},{6,2},{1... | collective-permute-start | bytes 589832 | tf_op jit(solution)/shard_map/ppermute | solution.py:63
  7.4 10.0 %collective-permute-start.4 = (bf16[3,16,16,128]{3,2,1,0:T(8,128)(2,1)S(1)}, bf16[3,16,16,128]{3,2,1,0:T(8,128)(2,1)S(1)}, u32[]{:S(2)}, u32[]{:S(2)}) collective-permute-start(bf16[3,16,16,128]{3,2,1,0:T(8,128)(2,1)S(1)} %get-tuple-element.52), channel_id=1, source_target_pairs={{4,8},{8,4},{5,9},{9,5},{6,10},{10,6},{7,11},{11,7},{20,24},{24,20... | collective-permute-start | bytes 589832 | tf_op jit(solution)/shard_map/ppermute | solution.py:64
  15.1 7.1 %collective-permute-start.7 = (bf16[1,3,14,16,128]{4,3,2,1,0:T(8,128)(2,1)S(1)}, bf16[1,3,14,16,128]{4,3,2,1,0:T(8,128)(2,1)S(1)}, u32[]{:S(2)}, u32[]{:S(2)}) collective-permute-start(bf16[1,3,14,16,128]{4,3,2,1,0:T(8,128)(2,1)S(1)} %bitcast.35), channel_id=1, source_target_pairs={{0,8},{4,12},{8,0},{12,4},{1,9},{5,13},{9,1},{13,5},{2,10},{6,14},... | collective-permute-start | bytes 516104 | tf_op jit(solution)/shard_map/ppermute | solution.py:95
  16.7 3.2 %collective-permute-start.5 = (bf16[7,16,128]{2,1,0:T(8,128)(2,1)S(1)}, bf16[7,16,128]{2,1,0:T(8,128)(2,1)S(1)}, u32[]{:S(2)}, u32[]{:S(2)}) collective-permute-start(bf16[7,16,128]{2,1,0:T(8,128)(2,1)S(1)} %get-tuple-element.58), channel_id=1, source_target_pairs={{0,4},{4,0},{8,12},{12,8},{1,5},{5,1},{9,13},{13,9},{2,6},{6,2},{1... | collective-permute-start | bytes 86024 | tf_op jit(solution)/shard_map/ppermute | solution.py:63
  16.7 3.2 %collective-permute-start.6 = (bf16[7,16,128]{2,1,0:T(8,128)(2,1)S(1)}, bf16[7,16,128]{2,1,0:T(8,128)(2,1)S(1)}, u32[]{:S(2)}, u32[]{:S(2)}) collective-permute-start(bf16[7,16,128]{2,1,0:T(8,128)(2,1)S(1)} %get-tuple-element.59), channel_id=1, source_target_pairs={{4,8},{8,4},{5,9},{9,5},{6,10},{10,6},{7,11},{11,7},{20,24},{24,20... | collective-permute-start | bytes 86024 | tf_op jit(solution)/shard_map/ppermute | solution.py:64
  19.9 16.2 %copy-start.3 = (f32[128]{0:T(128)S(1)}, f32[128]{0:T(128)}, u32[]{:S(2)}) copy-start(f32[128]{0:T(128)} %param.10) | copy-start | bytes 1540
  19.9 16.2 %copy-start.4 = (f32[128]{0:T(128)S(1)}, f32[128]{0:T(128)}, u32[]{:S(2)}) copy-start(f32[128]{0:T(128)} %param.11) | copy-start | bytes 1540
  22.2 13.7 %collective-permute-start.8 = (bf16[2,3,14,16,128]{4,3,2,1,0:T(8,128)(2,1)S(1)}, bf16[2,3,14,16,128]{4,3,2,1,0:T(8,128)(2,1)S(1)}, u32[]{:S(2)}, u32[]{:S(2)}) collective-permute-start(bf16[2,3,14,16,128]{4,3,2,1,0:T(8,128)(2,1)S(1)} %bitcast.27), channel_id=1, source_target_pairs={{0,16},{16,0},{1,17},{17,1},{2,18},{18,2},{3,19},{19,3},{4,20},{20... | collective-permute-start | bytes 1032200 | tf_op jit(solution)/shard_map/ppermute | solution.py:95
  36.0 5.8 %collective-permute-start.9 = (bf16[4,3,14,16,128]{4,3,2,1,0:T(8,128)(2,1)S(1)}, bf16[4,3,14,16,128]{4,3,2,1,0:T(8,128)(2,1)S(1)}, u32[]{:S(2)}, u32[]{:S(2)}) collective-permute-start(bf16[4,3,14,16,128]{4,3,2,1,0:T(8,128)(2,1)S(1)} %bitcast.24), channel_id=1, source_target_pairs={{0,4},{4,0},{8,12},{12,8},{1,5},{5,1},{9,13},{13,9},{2,6},{6,2},{1... | collective-permute-start | bytes 2064392 | tf_op jit(solution)/shard_map/ppermute | solution.py:95
  37.3 6.0 %collective-permute-start.12 = (f32[16,128]{1,0:T(8,128)S(1)}, f32[16,128]{1,0:T(8,128)S(1)}, u32[]{:S(2)}, u32[]{:S(2)}) collective-permute-start(f32[16,128]{1,0:T(8,128)S(1)} %bitcast.49), channel_id=1, source_target_pairs={{0,3},{1,2},{2,1},{3,0},{4,7},{5,6},{6,5},{7,4},{8,11},{9,10},{10,... | collective-permute-start | bytes 24584 | tf_op jit(solution)/shard_map/ppermute | solution.py:46
  38.0 5.4 %collective-permute-start.10 = (bf16[80,128]{1,0:T(8,128)(2,1)S(1)}, bf16[80,128]{1,0:T(8,128)(2,1)S(1)}, u32[]{:S(2)}, u32[]{:S(2)}) collective-permute-start(bf16[80,128]{1,0:T(8,128)(2,1)S(1)} %bitcast.48), channel_id=1, source_target_pairs={{0,2},{1,3},{2,0},{3,1},{4,6},{5,7},{6,4},{7,5},{8,10},{9,11},{10,... | collective-permute-start | bytes 61448 | tf_op jit(solution)/shard_map/ppermute | solution.py:44
  39.4 4.2 %collective-permute-start.11 = (bf16[80,128]{1,0:T(8,128)(2,1)S(1)}, bf16[80,128]{1,0:T(8,128)(2,1)S(1)}, u32[]{:S(2)}, u32[]{:S(2)}) collective-permute-start(bf16[80,128]{1,0:T(8,128)(2,1)S(1)} %bitcast.47), channel_id=1, source_target_pairs={{0,1},{1,0},{2,3},{3,2},{4,5},{5,4},{6,7},{7,6},{8,9},{9,8},{10,11... | collective-permute-start | bytes 61448 | tf_op jit(solution)/shard_map/ppermute | solution.py:45
  43.3 11.0 %copy-start = (bf16[256,128]{1,0:T(8,128)(2,1)S(1)}, bf16[256,128]{1,0:T(8,128)(2,1)}, u32[]{:S(2)}) copy-start(bf16[256,128]{1,0:T(8,128)(2,1)} %up.1) | copy-start | bytes 196612
  43.3 11.0 %copy-start.1 = (f32[256]{0:T(256)S(1)}, f32[256]{0:T(256)}, u32[]{:S(2)}) copy-start(f32[256]{0:T(256)} %param.13) | copy-start | bytes 3076
  43.4 11.0 %copy-start.2 = (f32[256]{0:T(256)S(1)}, f32[256]{0:T(256)}, u32[]{:S(2)}) copy-start(f32[256]{0:T(256)} %param.14) | copy-start | bytes 3076

commit v15 on v13

--- a/solution.py
+++ b/solution.py
@@ -55,12 +55,10 @@
         return y, x, corner
 
 
-def swap_depth(outer, inner):
+def swap_depth(face, outer):
     size = lax.axis_size("gz")
-    routes = [[], []]
-    for low in range(size - 1):
-        routes[low % 2] += [(low, low + 1), (low + 1, low)]
-    return lax.ppermute(outer, "gz", routes[1]), lax.ppermute(inner, "gz", routes[0])
+    pairs = [(low, low + 1) for low in range(int(outer), size - 1, 2)]
+    return lax.ppermute(face, "gz", pairs + [pair[::-1] for pair in pairs])
 
 
 class Riders:
@@ -113,7 +111,7 @@
     )(*far, *near)
 
 
-def start_kernel(ny, nx, size, x_in, w_in, d_in, y_out, x_out, corners, outer, inner, x, w, lines, sems):
+def start_kernel(ny, nx, size, x_in, w_in, d_in, y_out, x_out, corners, outer, x, w, lines, sems):
     edge = x_in.shape[0]
     f32, bf16 = jnp.float32, jnp.bfloat16
     above, left = Square().low_sides()
@@ -169,26 +167,27 @@
             kept = jnp.where(above[i], low, high)
             corners[i * nx + j, 0] = kept.astype(bf16)
     odd, far = lax.axis_index("gz") % 2, edge - 3
-    for face, at in ((outer, odd * far), (inner, (1 - odd) * far)):
-        for k in range(3):
-            face[k] = x[1 + at + k, 1 : edge + 1]
+    for k in range(3):
+        outer[k] = x[1 + odd * far + k, 1 : edge + 1]
     for copy in later:
         copy.wait()
 
 
-def turn_kernel(ny, nx, size, y_halos, x_halos, corners, outer, inner, *riders):
+def turn_kernel(ny, nx, size, x, y_halos, x_halos, corners, outer, inner, *riders):
     edge = outer.shape[1]
     wide = ny + nx
     odd, far = lax.axis_index("gz") % 2, edge - 3
-    for face, at in ((outer, odd * far), (inner, (1 - odd) * far)):
+    for face, at, begin in ((outer, odd * far, 0), (inner, (1 - odd) * far, 3 * edge)):
         for k in range(3):
-            row = k * wide
+            row = begin + k * wide
             for i in range(ny):
                 face[row + i] = y_halos[i, at + k]
             for j in range(nx):
                 face[row + ny + j] = x_halos[j, at + k]
+            if begin:
+                face[k * edge : k * edge + edge] = x[1 + at + k, 1 : edge + 1]
         for k in range(ny * nx):
-            face[3 * wide + k] = corners[k, 0]
+            face[begin + 3 * wide + k] = corners[k, 0]
     if size:
         riders[0][0] = x_halos[0, edge : edge + size]
         riders[0][1] = y_halos[0, edge : edge + size]
@@ -343,62 +342,98 @@
     return mean, lax.fori_loop(0, count, spread_step, zero, unroll=True)
 
 
-def side_kernel(ny, nx, *refs):
-    x, own, y_halos, x_halos, corners, outer, inner, taps, pairs, middle, ends, stats, act, grid, column = refs
-    edge = own.shape[0]
-    depth = edge + 4
-    f32 = jnp.float32
-    above, left = Square().low_sides()
-    odd = lax.axis_index("gz") % 2 == 1
-    act[2 : 2 + edge] = own[...]
+def add_beyond(behind, face, x, grid, taps, pairs, ends):
+    edge = x.shape[2]
+    grid[pl.ds(jnp.where(behind, 1, 0), 3), 1 : edge + 1] = face
+    own = jnp.where(behind, edge, 1)
+    grid[jnp.where(behind, 0, 3), 1 : edge + 1] = x[own, 1 : edge + 1]
     blank = jnp.zeros(grid.shape[:1] + grid.shape[2:], grid.dtype)
     grid[:, 0] = blank
     grid[:, edge + 1] = blank
-    faces = in_order(odd, outer[...], inner[...])
-    for face, halo_at, own_at, plane, beyond, at, beside, dz in (
-        (faces[0], 0, 3, 1, 0, 2, 2, 0),
-        (faces[1], 1, 0, edge, edge + 2, edge + 1, 1, 2),
-    ):
-        grid[halo_at : halo_at + 3, 1 : edge + 1] = face
-        grid[own_at, 1 : edge + 1] = x[plane, 1 : edge + 1]
-
-        def put(z, new):
-            act[beyond + z : beyond + z + new.shape[0]] = new
-
-        convolve(grid, 2, taps, pairs, put)
-        stacked = jnp.concatenate(
-            [grid[beside, dy : dy + edge].reshape(edge * edge, 128) for dy in range(3)], axis=1
-        )
-        wide = jnp.dot(stacked, taps[dz * 384 : dz * 384 + 384, :], preferred_element_type=f32)
-        act[at] += join_x(wide.reshape(edge, edge, 384), edge)
-
+    begin = jnp.where(behind, 4, 0)
+
+    def put(z, new):
+        ends[pl.ds(begin + z, new.shape[0])] += new
+
+    convolve(grid, 2, taps, pairs, put)
+    beside = jnp.where(behind, 1, 2)
+    stacked = jnp.concatenate(
+        [grid[beside, dy : dy + edge].reshape(edge * edge, 128) for dy in range(3)], axis=1
+    )
+    rows = taps[pl.ds(pl.multiple_of(jnp.where(behind, 768, 0), 128), 384), :]
+    wide = jnp.dot(stacked, rows, preferred_element_type=jnp.float32)
+    ends[jnp.where(behind, 3, 2)] += join_x(wide.reshape(edge, edge, 384), edge)
+
+
+def side_kernel(ny, nx, x, own, y_halos, x_halos, corners, outer, taps, pairs, *refs):
+    middle, ends, stats, grid, column = refs
+    edge = own.shape[0]
+    f32 = jnp.float32
+    above, left = Square().low_sides()
+    zero = jnp.zeros((2, edge, edge, 128), f32)
+    ends[0:2] = zero
+    ends[2] = own[0]
+    ends[3] = own[edge - 1]
+    ends[4:6] = zero
+    total = jnp.zeros((8, 128), f32)
+    for z in range(edge - 2):
+        plane = own[1 + z]
+        middle[z] = plane
+        total = total + jnp.sum(plane.reshape(edge * 2, 8, 128), axis=0)
+    odd = lax.axis_index("gz") % 2 == 1
+    add_beyond(odd, outer[...], x, grid, taps, pairs, ends)
+
+    parts = ((ends.at[1:3], 0), (middle, 2), (ends.at[3:5], edge))
     gap = jnp.zeros((2, edge, 128), grid.dtype)
-    reached = act.at[1 : depth - 1]
     for i in range(ny):
         line = jnp.concatenate([gap, y_halos[i, 0:edge], gap], axis=0)
-        reached[:, jnp.where(above[i], 0, edge - 1)] += y_terms(line, above[i], taps)
+        new = y_terms(line, above[i], taps)
+        row = jnp.where(above[i], 0, edge - 1)
+        for ref, at in parts:
+            ref[:, row] += new[at : at + ref.shape[0]]
+        total = total + jnp.sum(new[2:edge].reshape(-1, 8, 128), axis=0)
+    line = lax.broadcasted_iota(jnp.int32, (8, 128), 0)
     for j in range(nx):
         column[...] = jnp.zeros(column.shape, f32)
         fill_column(
             column, 2, x_halos[j, 0:edge], [corners[i * nx + j, 0] for i in range(ny)], above
         )
-        add_column(reached, x_terms(column, taps), j, nx, left[j])
-    middle[...] = act[3 : depth - 3]
-    ends[0:3] = act[0:3]
-    ends[3:6] = act[depth - 3 :]
-    mean, spread = moments(act.at[3 : depth - 3])
+        terms = x_terms(column, taps)
+        for ref, at in parts:
+            rows = slice(at * edge, (at + ref.shape[0]) * edge)
+            add_column(ref, [term[rows] for term in terms], j, nx, left[j])
+        first, last = (
+            jnp.sum(term[2 * edge : edge * edge], axis=0, keepdims=True) for term in terms
+        )
+        total = total + jnp.where(
+            left[j], jnp.where(line == 0, first, 0.0), jnp.where(line == 7, last, 0.0)
+        )
+    mean = total / ((edge - 2) * edge * edge // 8)
+    spread = jnp.zeros((8, 128), f32)
+    for z in range(edge - 2):
+        off = middle[z].reshape(edge * 2, 8, 128) - mean
+        spread = spread + jnp.sum(off * off, axis=0)
     stats[0:8] = mean
     stats[8:16] = spread
 
 
-def end_kernel(ny, nx, middle_stats, ends, outer, inner, taps, act, stats, faces, column):
+def end_kernel(ny, nx, x, middle_stats, ends, inner, outer, taps, pairs, act, stats, faces, grid, column):
     edge = act.shape[1]
     wide = ny + nx
     f32 = jnp.float32
     above, left = Square().low_sides()
     odd = lax.axis_index("gz") % 2 == 1
-    faces[0], faces[1] = in_order(odd, outer[...], inner[...])
+    faces[0], faces[1] = in_order(odd, outer[...], inner[3 * edge :])
     act[...] = ends[...]
+    add_beyond(
+        jnp.logical_not(odd),
+        inner[0 : 3 * edge].reshape(3, edge, edge, 128),
+        x,
+        grid,
+        taps,
+        pairs,
+        act,
+    )
     gap = jnp.zeros((2, edge, 128), faces.dtype)
     for side in range(2):
 
@@ -698,13 +733,12 @@
     own = jnp.moveaxis(deep_weight, 4, 3).reshape(-1, 16, channels)
     conv_weight = conv_weight.reshape(27, channels, channels)
     three = ((3, edge, edge, channels), bf16)
-    *edges, outer, inner, field, conv_weight = call(
+    *edges, outer, field, conv_weight = call(
         functools.partial(start_kernel, ny, nx, riders.size),
         [
             ((ny, edge + riders.size, edge, channels), bf16),
             ((nx, edge + riders.size, edge, channels), bf16),
             ((ny * nx, 1 + riders.size, edge, channels), bf16),
-            three,
             three,
             ((edge + 2, edge + 2, edge, channels), bf16),
             (conv_weight.shape, bf16),
@@ -717,7 +751,7 @@
         in_hbm=3,
     )
     halos = square.halos(*(list(piece) for piece in edges))
-    outer, inner = swap_depth(outer, inner)
+    outer = swap_depth(outer, True)
     conv_flops = 54 * channels * channels * edge**3
     act, taps, pairs, own = call(
         conv_kernel,
@@ -735,14 +769,21 @@
         nbytes=6 << 20,
         in_hbm=1,
     )
-    (y, x, corner), act = lax.optimization_barrier((halos, act))
+    (y, x, corner), act, outer = lax.optimization_barrier((halos, act, outer))
     y, x, corner = jnp.stack(y), jnp.stack(x), jnp.stack(corner)
     turn = ((3 * (ny + nx) + ny * nx, edge, channels), bf16)
+    full = ((3 * edge + turn[0][0], edge, channels), bf16)
     held = [((3, riders.size, 16, channels), bf16)] if riders.size else []
-    turns = call(
-        functools.partial(turn_kernel, ny, nx, riders.size), [turn, turn] + held, [], y, x, corner
-    )
-    turns, held = swap_depth(*turns[:2]), turns[2:]
+    outer_rim, inner, *held = call(
+        functools.partial(turn_kernel, ny, nx, riders.size),
+        [turn, full] + held,
+        [],
+        field,
+        y,
+        x,
+        corner,
+    )
+    outer_rim, inner = swap_depth(outer_rim, True), swap_depth(inner, False)
     if riders.size:
         held = held[0][None]
         other = swap(held, *riders.STEPS[0])
@@ -754,7 +795,6 @@
         functools.partial(side_kernel, ny, nx),
         [((edge - 2, edge, edge, channels), f32), six, ((16, channels), f32)],
         [
-            ((edge + 4, edge, edge, channels), f32),
             ((4, edge + 2, edge, channels), bf16),
             ((edge + 4,) + column, f32),
         ],
@@ -764,18 +804,24 @@
         x,
         corner,
         outer,
-        inner,
         taps,
         pairs,
     )
     ends, stats = call(
         functools.partial(end_kernel, ny, nx),
         [six, ((devices, 2, channels), f32)],
-        [((2,) + turn[0], bf16), ((5,) + column, f32)],
+        [
+            ((2,) + turn[0], bf16),
+            ((4, edge + 2, edge, channels), bf16),
+            ((5,) + column, f32),
+        ],
+        field,
         stats,
         ends,
-        *turns,
+        inner,
+        outer_rim,
         taps,
+        pairs,
     )
     if riders.size:
         stats, other = lax.optimization_barrier((stats, other))

time: 56.3 us -> 57 us (1.012)
  starting transfers between devices: 19.9 us -> 15 us
  waiting for transfers between devices: 0.22 us -> 4.23 us
  blocking collectives: 21.2 us -> 23 us
    ppermute x4 -> x3, starting transfers between devices: 7.08 us -> 2.09 us  [swap_depth(): return lax.ppermute(face, 'gz', pairs + [pair[::-1] for pair in pairs])]
    all_to_all x2, blocking collectives: 21.2 us -> 23 us  [share(): return lax.all_to_all(stats, PART, 0, 0)]
    ppermute x3, waiting for transfers between devices: 0.01 us -> 1.73 us  [swap(): lax.ppermute(block, axis, [(i, i ^ mask) for i in range(lax.axis_size(axi...]
    ppermute x2, waiting for transfers between devices: 0.01 us -> 1.59 us  [halos(): y = lax.ppermute(y_edges[0], 'yx', self.swap_route(2))]
    ppermute x2, waiting for transfers between devices: 0.19 us -> 0.9 us  [halos(): x = lax.ppermute(x_edges[0], 'yx', self.swap_route(1))]
  transfers between devices with their start and end apart: 13 -> 12, of which waited for: 1 -> 4; matrix products, arithmetic and copies ran while one was open for 0% -> 0% of each run, Pallas kernels for 19% -> 18%
where the time goes in v15:
time: 57 us; the launch traced here: 56.8 us
  blocking collectives  23 us (40%)
  starting transfers between devices  15 us (26%)
  Pallas kernels  14.4 us (25%)
  waiting for transfers between devices  4.23 us (7%)
    all_to_all x2, blocking collectives, share(): return lax.all_to_all(stats, PART, 0, 0)  23 us
    pallas_call x9, Pallas kernels, call(): pl.pallas_call(kernel, out_shape=[jax.ShapeDtypeStruct(shape, dtype) for...  14.2 us
    ppermute x2, starting transfers between devices, halos(): corner = lax.ppermute(corners[0], 'yx', self.swap_route(3))  5.77 us
    ppermute x3, starting transfers between devices, swap(): lax.ppermute(block, axis, [(i, i ^ mask) for i in range(lax.axis_size(axi...  2.64 us
    ppermute x2, starting transfers between devices, halos(): x = lax.ppermute(x_edges[0], 'yx', self.swap_route(1))  2.42 us
    ppermute x3, starting transfers between devices, swap_depth(): return lax.ppermute(face, 'gz', pairs + [pair[::-1] for pair in pairs])  2.09 us
    ppermute x2, starting transfers between devices, halos(): y = lax.ppermute(y_edges[0], 'yx', self.swap_route(2))  2.05 us
    ppermute x3, waiting for transfers between devices, swap(): lax.ppermute(block, axis, [(i, i ^ mask) for i in range(lax.axis_size(axi...  1.73 us
  transfers between devices with their start and end apart: 12, of which 4 were waited for; matrix products, arithmetic and copies ran while one was open for 0% of the time, Pallas kernels for 18%

profile of v15, /device:TPU:0, one launch (start us, length us, event | category | flops | bytes accessed | tf_op | source)
XLA Modules:
  0.0 56.8 jit_solution(14390707183469436821)
XLA Ops:
  0.0 1.6 %shard_map.82 = (bf16[1,30,16,128]{3,2,1,0:T(8,128)(2,1)S(1)}, bf16[1,30,16,128]{3,2,1,0:T(8,128)(2,1)S(1)}, bf16[1,15,16,128]{3,2,1,0:T(8,128)(2,1)S(1)}, bf16[...) custom-call(bf16[16,16,16,128]{3,2,1,0:T(8,128)(2,1)} %x_in.1, ...), custom_call_target="tpu_custom_call" | custom-call | bytes 5242880 | tf_op jit(solution)/shard_map/pallas_call | solution.py:103
  1.6 5.1 %collective-permute-start.2 = (bf16[15,16,128]{2,1,0:T(8,128)(2,1)S(1)}, bf16[15,16,128]{2,1,0:T(8,128)(2,1)S(1)}, u32[]{:S(2)}, u32[]{:S(2)}) collective-permute-start(bf16[15,16,128]{2,1,0:T(8,128)(2,1)S(1)} %bitcast.46), channel_id=1, source_target_pairs={{0,3},{1,2},{2,1},{3,0},{4,7},{5,6},{6,5},{7,4},{8,11},{9,10},{10,... | collective-permute-start | bytes 184328 | tf_op jit(solution)/shard_map/ppermute | solution.py:46
  6.7 0.0 collective-permute-start.1
  6.7 0.6 %collective-permute-start = (bf16[30,16,128]{2,1,0:T(8,128)(2,1)S(1)}, bf16[30,16,128]{2,1,0:T(8,128)(2,1)S(1)}, u32[]{:S(2)}, u32[]{:S(2)}) collective-permute-start(bf16[30,16,128]{2,1,0:T(8,128)(2,1)S(1)} %bitcast.44), channel_id=1, source_target_pairs={{0,2},{1,3},{2,0},{3,1},{4,6},{5,7},{6,4},{7,5},{8,10},{9,11},{10,... | collective-permute-start | bytes 368648 | tf_op jit(solution)/shard_map/ppermute | solution.py:44
  7.4 0.7 %collective-permute-start.3 = (bf16[3,16,16,128]{3,2,1,0:T(8,128)(2,1)S(1)}, bf16[3,16,16,128]{3,2,1,0:T(8,128)(2,1)S(1)}, u32[]{:S(2)}, u32[]{:S(2)}) collective-permute-start(bf16[3,16,16,128]{3,2,1,0:T(8,128)(2,1)S(1)} %get-tuple-element.47), channel_id=1, source_target_pairs={{4,8},{8,4},{5,9},{9,5},{6,10},{10,6},{7,11},{11,7},{20,24},{24,20... | collective-permute-start | bytes 589832 | tf_op jit(solution)/shard_map/ppermute | solution.py:61
  8.1 4.7 %shard_map.83 = (f32[16,16,16,128]{3,2,1,0:T(8,128)S(1)}, bf16[1152,384]{1,0:T(8,128)(2,1)S(1)}, bf16[1536,256]{1,0:T(8,128)(2,1)S(1)}, bf16[108,16,128]{2,1,0:T(8,128)(2,1)S(1)}) custom-call(bf16[108,16,128]{2,1,0:T(8,128)(2,1)} %bitcast.52, bf16[18,18,16,128]{3,2,1,0:T(8,128)(2,1)S(1)} %get-tuple-element.41.x, ...), custom_call_target="tpu_custom_call" | custom-call | flops 3623878656 | bytes 6291456 | tf_op jit(solution)/shard_map/pallas_call | solution.py:103
  12.8 0.0 collective-permute-done.2
  12.8 0.7 %collective-permute-done.1 = bf16[30,16,128]{2,1,0:T(8,128)(2,1)S(1)} collective-permute-done((bf16[30,16,128]{2,1,0:T(8,128)(2,1)S(1)}, bf16[30,16,128]{2,1,0:T(8,128)(2,1)S(1)}, u32[]{:S(2)}, u32[]{:S(2)}) %collective-permute-start.1) | collective-permute-done | bytes 122912 | tf_op jit(solution)/shard_map/ppermute | solution.py:45
  13.5 1.6 %collective-permute-done = bf16[30,16,128]{2,1,0:T(8,128)(2,1)S(1)} collective-permute-done((bf16[30,16,128]{2,1,0:T(8,128)(2,1)S(1)}, bf16[30,16,128]{2,1,0:T(8,128)(2,1)S(1)}, u32[]{:S(2)}, u32[]{:S(2)}) %collective-permute-start) | collective-permute-done | bytes 122912 | tf_op jit(solution)/shard_map/ppermute | solution.py:44
  15.1 0.0 collective-permute-done.3.outer
  15.1 0.8 %collective-permute-start.4 = (bf16[55,16,128]{2,1,0:T(8,128)(2,1)S(1)}, bf16[55,16,128]{2,1,0:T(8,128)(2,1)S(1)}, u32[]{:S(2)}, u32[]{:S(2)}) collective-permute-start(bf16[55,16,128]{2,1,0:T(8,128)(2,1)S(1)} %get-tuple-element.58), channel_id=1, source_target_pairs={{0,4},{8,12},{4,0},{12,8},{1,5},{9,13},{5,1},{13,9},{2,6},{10,14},... | collective-permute-start | bytes 675848 | tf_op jit(solution)/shard_map/ppermute | solution.py:61
  15.9 0.9 %collective-permute-start.6 = (bf16[1,3,14,16,128]{4,3,2,1,0:T(8,128)(2,1)S(1)}, bf16[1,3,14,16,128]{4,3,2,1,0:T(8,128)(2,1)S(1)}, u32[]{:S(2)}, u32[]{:S(2)}) collective-permute-start(bf16[1,3,14,16,128]{4,3,2,1,0:T(8,128)(2,1)S(1)} %bitcast.35), channel_id=1, source_target_pairs={{0,8},{4,12},{8,0},{12,4},{1,9},{5,13},{9,1},{13,5},{2,10},{6,14},... | collective-permute-start | bytes 516104 | tf_op jit(solution)/shard_map/ppermute | solution.py:92
  16.8 0.7 %collective-permute-start.5 = (bf16[7,16,128]{2,1,0:T(8,128)(2,1)S(1)}, bf16[7,16,128]{2,1,0:T(8,128)(2,1)S(1)}, u32[]{:S(2)}, u32[]{:S(2)}) collective-permute-start(bf16[7,16,128]{2,1,0:T(8,128)(2,1)S(1)} %get-tuple-element.59), channel_id=1, source_target_pairs={{4,8},{8,4},{5,9},{9,5},{6,10},{10,6},{7,11},{11,7},{20,24},{24,20... | collective-permute-start | bytes 86024 | tf_op jit(solution)/shard_map/ppermute | solution.py:61
  17.5 1.7 %shard_map.84 = (f32[14,16,16,128]{3,2,1,0:T(8,128)S(1)}, f32[6,16,16,128]{3,2,1,0:T(8,128)S(1)}, f32[16,128]{1,0:T(8,128)S(1)}) custom-call(bf16[18,18,16,128]{3,2,1,0:T(8,128)(2,1)S(1)} %get-tuple-element.41.x, f32[16,16,16,128]{3,2,1,0:T(8,128)S(1)} %get-tuple-element.48.own, bf16[1,30,16,128]{3,2,1,0:T(8,128)(2,1)S(1)} %bitcast.32, ...), custom_call_target="tpu_custom_call" | custom-call | tf_op jit(solution)/shard_map/pallas_call | solution.py:103
  19.2 0.0 collective-permute-done.5.outer
  19.2 0.0 collective-permute-done.4.inner
  19.2 1.3 %shard_map.86 = (f32[6,16,16,128]{3,2,1,0:T(8,128)S(1)}, f32[16,2,128]{2,1,0:T(2,128)S(1)}) custom-call(bf16[18,18,16,128]{3,2,1,0:T(8,128)(2,1)S(1)} %get-tuple-element.41.x, f32[16,128]{1,0:T(8,128)S(1)} %get-tuple-element.56.middle_stats, f32[6,16,16,128]{3,2,1,0:T(8,128)S(1)} %get-tuple-element.57.ends, ...), custom_call_target="tpu_custom_call" | custom-call | tf_op jit(solution)/shard_map/pallas_call | solution.py:103
  20.5 0.0 copy-start.3
  20.5 0.0 copy-start.4
  20.6 1.7 %collective-permute-done.6.refs_1_ = bf16[1,3,14,16,128]{4,3,2,1,0:T(8,128)(2,1)S(1)} collective-permute-done((bf16[1,3,14,16,128]{4,3,2,1,0:T(8,128)(2,1)S(1)}, bf16[1,3,14,16,128]{4,3,2,1,0:T(8,128)(2,1)S(1)}, u32[]{:S(2)}, u32[]{:S(2)}) %collective-permute-start.6) | collective-permute-done | bytes 172064 | tf_op jit(solution)/shard_map/ppermute | solution.py:92
  22.3 1.6 %collective-permute-start.7 = (bf16[2,3,14,16,128]{4,3,2,1,0:T(8,128)(2,1)S(1)}, bf16[2,3,14,16,128]{4,3,2,1,0:T(8,128)(2,1)S(1)}, u32[]{:S(2)}, u32[]{:S(2)}) collective-permute-start(bf16[2,3,14,16,128]{4,3,2,1,0:T(8,128)(2,1)S(1)} %bitcast.27), channel_id=1, source_target_pairs={{0,16},{16,0},{1,17},{17,1},{2,18},{18,2},{3,19},{19,3},{4,20},{20... | collective-permute-start | bytes 1032200 | tf_op jit(solution)/shard_map/ppermute | solution.py:92
  23.9 12.9 %all_to_all.10.stats = f32[16,2,128]{2,1,0:T(2,128)S(1)} all-to-all(f32[16,2,128]{2,1,0:T(2,128)S(1)} %get-tuple-element.63), channel_id=1, replica_groups=mesh['cand'=2,'gz'=4,'yx'=4] {'gz','yx'}, dimensions={0} | all-to-all | bytes 32768 | tf_op jit(solution)/shard_map/all_to_all | solution.py:96
  36.8 0.0 collective-permute-done.7.refs_1_
  36.9 0.2 collective-permute-start.8
  37.1 0.0 copy-done.3
  37.1 0.0 copy-done.4
  37.1 1.1 %shard_map.88 = (bf16[16,16,16,128]{3,2,1,0:T(8,128)(2,1)S(1)}, f32[10,8,8,128]{3,2,1,0:T(8,128)S(1)}, bf16[1,80,128]{2,1,0:T(8,128)(2,1)S(1)}, bf16[1,80,128]{2,1,0:T(8,128)(2,1)S(1)}, f32[1,16,128]{2,1,0:T(8,128)S(1)}) custom-call(f32[14,16,16,128]{3,2,1,0:T(8,128)S(1)} %get-tuple-element.55.inner, f32[6,16,16,128]{3,2,1,0:T(8,128)S(1)} %get-tuple-element.60.ends, ...), custom_call_target="tpu_custom_call" | custom-call | flops 10485760 | bytes 3145728 | tf_op jit(solution)/shard_map/pallas_call | solution.py:103
  38.2 0.7 %collective-permute-start.11 = (f32[16,128]{1,0:T(8,128)S(1)}, f32[16,128]{1,0:T(8,128)S(1)}, u32[]{:S(2)}, u32[]{:S(2)}) collective-permute-start(f32[16,128]{1,0:T(8,128)S(1)} %bitcast.49), channel_id=1, source_target_pairs={{0,3},{1,2},{2,1},{3,0},{4,7},{5,6},{6,5},{7,4},{8,11},{9,10},{10,... | collective-permute-start | bytes 24584 | tf_op jit(solution)/shard_map/ppermute | solution.py:46
  38.9 1.4 %collective-permute-start.9 = (bf16[80,128]{1,0:T(8,128)(2,1)S(1)}, bf16[80,128]{1,0:T(8,128)(2,1)S(1)}, u32[]{:S(2)}, u32[]{:S(2)}) collective-permute-start(bf16[80,128]{1,0:T(8,128)(2,1)S(1)} %bitcast.48), channel_id=1, source_target_pairs={{0,2},{1,3},{2,0},{3,1},{4,6},{5,7},{6,4},{7,5},{8,10},{9,11},{10,... | collective-permute-start | bytes 61448 | tf_op jit(solution)/shard_map/ppermute | solution.py:44
  40.3 2.4 %collective-permute-start.10 = (bf16[80,128]{1,0:T(8,128)(2,1)S(1)}, bf16[80,128]{1,0:T(8,128)(2,1)S(1)}, u32[]{:S(2)}, u32[]{:S(2)}) collective-permute-start(bf16[80,128]{1,0:T(8,128)(2,1)S(1)} %bitcast.47), channel_id=1, source_target_pairs={{0,1},{1,0},{2,3},{3,2},{4,5},{5,4},{6,7},{7,6},{8,9},{9,8},{10,11... | collective-permute-start | bytes 61448 | tf_op jit(solution)/shard_map/ppermute | solution.py:45
  42.7 0.0 collective-permute-done.8.refs_1_
  42.7 0.1 shard_map.90
  42.8 1.4 %shard_map.91 = (f32[2,512,128]{2,1,0:T(8,128)S(1)}, bf16[4,108,16,128]{3,2,1,0:T(8,128)(2,1)S(1)}) custom-call(f32[10,8,8,128]{3,2,1,0:T(8,128)S(1)} %get-tuple-element.66.pooled, bf16[108,16,128]{2,1,0:T(8,128)(2,1)S(1)} %get-tuple-element.67.own, bf16[8,3,14,16,128]{4,3,2,1,0:T(8,128)(2,1)S(1)} %bitcast.26), custom_call_target="tpu_custom_call" | custom-call | flops 905969664 | bytes 4194304 | tf_op jit(solution)/shard_map/pallas_call | solution.py:103
  44.2 0.0 copy-start
  44.2 0.0 copy-start.1
  44.2 0.0 copy-start.2
  44.3 0.0 collective-permute-done.11
  44.3 0.0 collective-permute-done.9
  44.3 0.2 collective-permute-done.10
  44.5 0.7 %shard_map.92 = (f32[2,512,128]{2,1,0:T(8,128)S(1)}, f32[16,2,256]{2,1,0:T(2,128)S(1)}) custom-call(f32[2,512,128]{2,1,0:T(8,128)S(1)} %get-tuple-element.69.own, bf16[1,80,128]{2,1,0:T(8,128)(2,1)S(1)} %bitcast.37, bf16[1,80,128]{2,1,0:T(8,128)(2,1)S(1)} %bitcast.38, f32[1,16,128]{2,1,0:T(8,128)S(1)} %bitcast.39, ...), custom_call_target="tpu_custom_call" | custom-call | flops 67108864 | bytes 3145728 | tf_op jit(solution)/shard_map/pallas_call | solution.py:103
  45.2 10.0 %all_to_all.11.stats = f32[16,2,256]{2,1,0:T(2,128)S(1)} all-to-all(f32[16,2,256]{2,1,0:T(2,128)S(1)} %get-tuple-element.75), channel_id=1, replica_groups=mesh['cand'=2,'gz'=4,'yx'=4] {'gz','yx'}, dimensions={0} | all-to-all | bytes 65536 | tf_op jit(solution)/shard_map/all_to_all | solution.py:96
  55.2 0.0 copy-done
  55.2 0.0 copy-done.1
  55.2 0.0 copy-done.2
  55.2 1.5 %shard_map.93 = bf16[16,16,16,128]{3,2,1,0:T(8,128)(2,1)} custom-call(f32[2,512,128]{2,1,0:T(8,128)S(1)} %get-tuple-element.74.act, f32[16,2,256]{2,1,0:T(2,128)S(1)} %all_to_all.11.stats, f32[1,256]{1,0:T(1,128)S(1)} %bitcast.40, f32[1,256]{1,0:T(1,128)S(1)} %bitcast.41, bf16[256,128]{1,0:T(8,128)(2,1)S(1)} %copy-done, ...), custom_call_target="tpu_custom_call" | custom-call | flops 67108864 | bytes 3145728 | tf_op jit(solution)/shard_map/pallas_call | solution.py:103
  (3 shorter events, 0.1 us)
Async XLA Ops:
  1.6 11.2 %collective-permute-start.2 = (bf16[15,16,128]{2,1,0:T(8,128)(2,1)S(1)}, bf16[15,16,128]{2,1,0:T(8,128)(2,1)S(1)}, u32[]{:S(2)}, u32[]{:S(2)}) collective-permute-start(bf16[15,16,128]{2,1,0:T(8,128)(2,1)S(1)} %bitcast.46), channel_id=1, source_target_pairs={{0,3},{1,2},{2,1},{3,0},{4,7},{5,6},{6,5},{7,4},{8,11},{9,10},{10,... | collective-permute-start | bytes 184328 | tf_op jit(solution)/shard_map/ppermute | solution.py:46
  6.7 6.8 %collective-permute-start.1 = (bf16[30,16,128]{2,1,0:T(8,128)(2,1)S(1)}, bf16[30,16,128]{2,1,0:T(8,128)(2,1)S(1)}, u32[]{:S(2)}, u32[]{:S(2)}) collective-permute-start(bf16[30,16,128]{2,1,0:T(8,128)(2,1)S(1)} %bitcast.45), channel_id=1, source_target_pairs={{0,1},{1,0},{2,3},{3,2},{4,5},{5,4},{6,7},{7,6},{8,9},{9,8},{10,11... | collective-permute-start | bytes 368648 | tf_op jit(solution)/shard_map/ppermute | solution.py:45
  6.7 8.4 %collective-permute-start = (bf16[30,16,128]{2,1,0:T(8,128)(2,1)S(1)}, bf16[30,16,128]{2,1,0:T(8,128)(2,1)S(1)}, u32[]{:S(2)}, u32[]{:S(2)}) collective-permute-start(bf16[30,16,128]{2,1,0:T(8,128)(2,1)S(1)} %bitcast.44), channel_id=1, source_target_pairs={{0,2},{1,3},{2,0},{3,1},{4,6},{5,7},{6,4},{7,5},{8,10},{9,11},{10,... | collective-permute-start | bytes 368648 | tf_op jit(solution)/shard_map/ppermute | solution.py:44
  7.4 7.7 %collective-permute-start.3 = (bf16[3,16,16,128]{3,2,1,0:T(8,128)(2,1)S(1)}, bf16[3,16,16,128]{3,2,1,0:T(8,128)(2,1)S(1)}, u32[]{:S(2)}, u32[]{:S(2)}) collective-permute-start(bf16[3,16,16,128]{3,2,1,0:T(8,128)(2,1)S(1)} %get-tuple-element.47), channel_id=1, source_target_pairs={{4,8},{8,4},{5,9},{9,5},{6,10},{10,6},{7,11},{11,7},{20,24},{24,20... | collective-permute-start | bytes 589832 | tf_op jit(solution)/shard_map/ppermute | solution.py:61
  15.1 4.1 %collective-permute-start.4 = (bf16[55,16,128]{2,1,0:T(8,128)(2,1)S(1)}, bf16[55,16,128]{2,1,0:T(8,128)(2,1)S(1)}, u32[]{:S(2)}, u32[]{:S(2)}) collective-permute-start(bf16[55,16,128]{2,1,0:T(8,128)(2,1)S(1)} %get-tuple-element.58), channel_id=1, source_target_pairs={{0,4},{8,12},{4,0},{12,8},{1,5},{9,13},{5,1},{13,9},{2,6},{10,14},... | collective-permute-start | bytes 675848 | tf_op jit(solution)/shard_map/ppermute | solution.py:61
  15.9 6.4 %collective-permute-start.6 = (bf16[1,3,14,16,128]{4,3,2,1,0:T(8,128)(2,1)S(1)}, bf16[1,3,14,16,128]{4,3,2,1,0:T(8,128)(2,1)S(1)}, u32[]{:S(2)}, u32[]{:S(2)}) collective-permute-start(bf16[1,3,14,16,128]{4,3,2,1,0:T(8,128)(2,1)S(1)} %bitcast.35), channel_id=1, source_target_pairs={{0,8},{4,12},{8,0},{12,4},{1,9},{5,13},{9,1},{13,5},{2,10},{6,14},... | collective-permute-start | bytes 516104 | tf_op jit(solution)/shard_map/ppermute | solution.py:92
  16.8 2.4 %collective-permute-start.5 = (bf16[7,16,128]{2,1,0:T(8,128)(2,1)S(1)}, bf16[7,16,128]{2,1,0:T(8,128)(2,1)S(1)}, u32[]{:S(2)}, u32[]{:S(2)}) collective-permute-start(bf16[7,16,128]{2,1,0:T(8,128)(2,1)S(1)} %get-tuple-element.59), channel_id=1, source_target_pairs={{4,8},{8,4},{5,9},{9,5},{6,10},{10,6},{7,11},{11,7},{20,24},{24,20... | collective-permute-start | bytes 86024 | tf_op jit(solution)/shard_map/ppermute | solution.py:61
  20.5 16.5 %copy-start.3 = (f32[128]{0:T(128)S(1)}, f32[128]{0:T(128)}, u32[]{:S(2)}) copy-start(f32[128]{0:T(128)} %param.10) | copy-start | bytes 1540
  20.5 16.5 %copy-start.4 = (f32[128]{0:T(128)S(1)}, f32[128]{0:T(128)}, u32[]{:S(2)}) copy-start(f32[128]{0:T(128)} %param.11) | copy-start | bytes 1540
  22.3 14.5 %collective-permute-start.7 = (bf16[2,3,14,16,128]{4,3,2,1,0:T(8,128)(2,1)S(1)}, bf16[2,3,14,16,128]{4,3,2,1,0:T(8,128)(2,1)S(1)}, u32[]{:S(2)}, u32[]{:S(2)}) collective-permute-start(bf16[2,3,14,16,128]{4,3,2,1,0:T(8,128)(2,1)S(1)} %bitcast.27), channel_id=1, source_target_pairs={{0,16},{16,0},{1,17},{17,1},{2,18},{18,2},{3,19},{19,3},{4,20},{20... | collective-permute-start | bytes 1032200 | tf_op jit(solution)/shard_map/ppermute | solution.py:92
  36.9 5.8 %collective-permute-start.8 = (bf16[4,3,14,16,128]{4,3,2,1,0:T(8,128)(2,1)S(1)}, bf16[4,3,14,16,128]{4,3,2,1,0:T(8,128)(2,1)S(1)}, u32[]{:S(2)}, u32[]{:S(2)}) collective-permute-start(bf16[4,3,14,16,128]{4,3,2,1,0:T(8,128)(2,1)S(1)} %bitcast.24), channel_id=1, source_target_pairs={{0,4},{4,0},{8,12},{12,8},{1,5},{5,1},{9,13},{13,9},{2,6},{6,2},{1... | collective-permute-start | bytes 2064392 | tf_op jit(solution)/shard_map/ppermute | solution.py:92
  38.2 6.0 %collective-permute-start.11 = (f32[16,128]{1,0:T(8,128)S(1)}, f32[16,128]{1,0:T(8,128)S(1)}, u32[]{:S(2)}, u32[]{:S(2)}) collective-permute-start(f32[16,128]{1,0:T(8,128)S(1)} %bitcast.49), channel_id=1, source_target_pairs={{0,3},{1,2},{2,1},{3,0},{4,7},{5,6},{6,5},{7,4},{8,11},{9,10},{10,... | collective-permute-start | bytes 24584 | tf_op jit(solution)/shard_map/ppermute | solution.py:46
  38.9 5.4 %collective-permute-start.9 = (bf16[80,128]{1,0:T(8,128)(2,1)S(1)}, bf16[80,128]{1,0:T(8,128)(2,1)S(1)}, u32[]{:S(2)}, u32[]{:S(2)}) collective-permute-start(bf16[80,128]{1,0:T(8,128)(2,1)S(1)} %bitcast.48), channel_id=1, source_target_pairs={{0,2},{1,3},{2,0},{3,1},{4,6},{5,7},{6,4},{7,5},{8,10},{9,11},{10,... | collective-permute-start | bytes 61448 | tf_op jit(solution)/shard_map/ppermute | solution.py:44
  40.3 4.2 %collective-permute-start.10 = (bf16[80,128]{1,0:T(8,128)(2,1)S(1)}, bf16[80,128]{1,0:T(8,128)(2,1)S(1)}, u32[]{:S(2)}, u32[]{:S(2)}) collective-permute-start(bf16[80,128]{1,0:T(8,128)(2,1)S(1)} %bitcast.47), channel_id=1, source_target_pairs={{0,1},{1,0},{2,3},{3,2},{4,5},{5,4},{6,7},{7,6},{8,9},{9,8},{10,11... | collective-permute-start | bytes 61448 | tf_op jit(solution)/shard_map/ppermute | solution.py:45
  44.2 11.0 %copy-start = (bf16[256,128]{1,0:T(8,128)(2,1)S(1)}, bf16[256,128]{1,0:T(8,128)(2,1)}, u32[]{:S(2)}) copy-start(bf16[256,128]{1,0:T(8,128)(2,1)} %up.1) | copy-start | bytes 196612
  44.2 11.0 %copy-start.1 = (f32[256]{0:T(256)S(1)}, f32[256]{0:T(256)}, u32[]{:S(2)}) copy-start(f32[256]{0:T(256)} %param.13) | copy-start | bytes 3076
  44.2 11.0 %copy-start.2 = (f32[256]{0:T(256)S(1)}, f32[256]{0:T(256)}, u32[]{:S(2)}) copy-start(f32[256]{0:T(256)} %param.14) | copy-start | bytes 3076

commit v16 on v9

--- a/solution.py
+++ b/solution.py
@@ -219,40 +219,44 @@
     return wide[:, :, 128:256] + after + before
 
 
-def convolve(grid, count, taps, pairs, put):
+def convolve(grid, spans, taps, pairs):
     edge = grid.shape[2]
-    planes = min(count, 4)
-    rows = planes * edge * edge
-    place = lax.broadcasted_iota(jnp.int32, (planes * edge, edge, 128), 1)
+    rows = sum(count for _, count in spans) * edge * edge
     halved = grid.reshape(grid.shape[0], edge // 2 + 1, 2, edge, 128)
-    for z in range(0, count, planes):
-        left = jnp.concatenate(
-            [
-                grid[z + dz : z + dz + planes, dy : dy + edge].reshape(rows, 128)
-                for dz in range(3)
-                for dy in range(3)
-            ],
-            axis=1,
-        )
-        wide = jnp.dot(left, taps[:, 0:256], preferred_element_type=jnp.float32)
-        wide = wide.reshape(planes * edge, edge, 256)
-        left = jnp.concatenate(
-            [
-                halved[z + dz : z + dz + planes, line // 2 : line // 2 + edge // 2, line % 2].reshape(
-                    rows // 2, 128
-                )
-                for dz in range(3)
-                for line in range(4)
-            ],
-            axis=1,
-        )
-        two = jnp.dot(left, pairs[...], preferred_element_type=jnp.float32)
-        two = two.reshape(planes * edge // 2, edge, 256)
-        two = jnp.stack([two[:, :, :128], two[:, :, 128:]], axis=1).reshape(planes * edge, edge, 128)
-        after = jnp.where(place > 0, pltpu.roll(wide[:, :, :128], 1, 1), 0.0)
-        before = jnp.where(place < edge - 1, pltpu.roll(two, edge - 1, 1), 0.0)
-        new = wide[:, :, 128:256] + after + before
-        put(z, new.reshape(planes, edge, edge, 128))
+
+    def stacked(pieces):
+        return jnp.concatenate([piece.reshape(-1, 128) for piece in pieces], axis=0)
+
+    left = jnp.concatenate(
+        [
+            stacked([grid[z + dz : z + dz + n, dy : dy + edge] for z, n in spans])
+            for dz in range(3)
+            for dy in range(3)
+        ],
+        axis=1,
+    )
+    wide = jnp.dot(left, taps[:, 0:256], preferred_element_type=jnp.float32)
+    wide = wide.reshape(rows // edge, edge, 256)
+    left = jnp.concatenate(
+        [
+            stacked(
+                [
+                    halved[z + dz : z + dz + n, line // 2 : line // 2 + edge // 2, line % 2]
+                    for z, n in spans
+                ]
+            )
+            for dz in range(3)
+            for line in range(4)
+        ],
+        axis=1,
+    )
+    two = jnp.dot(left, pairs[...], preferred_element_type=jnp.float32)
+    two = two.reshape(rows // edge // 2, edge, 256)
+    two = jnp.stack([two[:, :, :128], two[:, :, 128:]], axis=1).reshape(rows // edge, edge, 128)
+    place = lax.broadcasted_iota(jnp.int32, two.shape, 1)
+    after = jnp.where(place > 0, pltpu.roll(wide[:, :, :128], 1, 1), 0.0)
+    before = jnp.where(place < edge - 1, pltpu.roll(two, edge - 1, 1), 0.0)
+    return (wide[:, :, 128:256] + after + before).reshape(-1, edge, edge, 128)
 
 
 def conv_kernel(deep_in, x, weight, act, taps, pairs, deep_weight, sem):
@@ -261,11 +265,9 @@
     edge = act.shape[0]
     spread_taps(weight, taps)
     pair_taps(weight, pairs)
-
-    def put(z, new):
-        act[z : z + new.shape[0]] = new
-
-    convolve(x, edge, taps, pairs, put)
+    planes = 4
+    for z in range(0, edge, planes):
+        act[z : z + planes] = convolve(x, [(z, planes)], taps, pairs)
     copy.wait()
 
 
@@ -362,45 +364,46 @@
 
 
 def end_kernel(ny, nx, *refs):
-    x, inner_stats, partial, outer_face, inner_face, taps, pairs, act, stats, faces, grid, column = refs
+    x, inner_stats, partial, outer_face, inner_face, taps, pairs, act, stats, rims, grid, column = refs
     edge = x.shape[2]
     wide_face = edge + ny + nx
     f32 = jnp.float32
+    above, left = Square().low_sides()
     odd = lax.axis_index("gz") % 2 == 1
-    faces[0] = jnp.where(odd, inner_face[...], outer_face[...])
-    faces[1] = jnp.where(odd, outer_face[...], inner_face[...])
-    above, left = Square().low_sides()
     blank = jnp.zeros(grid.shape[:1] + grid.shape[2:], grid.dtype)
     grid[:, 0] = blank
     grid[:, edge + 1] = blank
-    gap = jnp.zeros((2, edge, 128), grid.dtype)
-    for side, halo_at, own_at, plane, at, beyond, own, beside, dz in (
-        (0, 0, 3, 1, 0, 0, 2, 2, 0),
-        (1, 1, 0, edge, 3, 4, 3, 1, 2),
-    ):
+    act[0] = jnp.zeros(act.shape[1:], f32)
+    act[1:5] = partial[...]
+    act[5] = jnp.zeros(act.shape[1:], f32)
+    sides = ((outer_face, odd, 0), (inner_face, jnp.logical_not(odd), 4))
+    for face, behind, base in sides:
+        first = base + jnp.where(behind, 1, 0)
+        side = jnp.where(behind, 1, 0)
         for k in range(3):
             begin = k * wide_face
-            grid[halo_at + k, 1 : edge + 1] = faces[side, begin : begin + edge]
-        grid[own_at, 1 : edge + 1] = x[plane, 1 : edge + 1]
-
-        def put(z, new):
-            act[beyond + z : beyond + z + new.shape[0]] = new
-
-        convolve(grid, 2, taps, pairs, put)
-        stacked = jnp.concatenate(
-            [grid[beside, dy : dy + edge].reshape(edge * edge, 128) for dy in range(3)], axis=1
-        )
-        wide = jnp.dot(stacked, taps[dz * 384 : dz * 384 + 384, :], preferred_element_type=f32)
-        own_part = partial[1 if side == 0 else 2]
-        act[own] = own_part + join_x(wide.reshape(edge, edge, 384), edge)
-        near = 1 if side == 0 else 4
-        act[near] += partial[0 if side == 0 else 3]
+            grid[first + k, 1 : edge + 1] = face[begin : begin + edge]
+            rims[side, k * (ny + nx) : (k + 1) * (ny + nx)] = face[begin + edge : begin + wide_face]
+        rims[side, 3 * (ny + nx) :] = face[3 * wide_face :]
+        grid[base + jnp.where(behind, 0, 3), 1 : edge + 1] = x[
+            jnp.where(behind, edge, 1), 1 : edge + 1
+        ]
+    beyond = convolve(grid, [(0, 2), (4, 2)], taps, pairs)
+    for (_, behind, base), new in zip(sides, (beyond[0:2], beyond[2:4])):
+        act[pl.ds(jnp.where(behind, 4, 0), 2)] += new
+        beside = base + jnp.where(behind, 1, 2)
+        lines = [grid[beside, dy : dy + edge].reshape(edge * edge, 128) for dy in range(3)]
+        rows = taps[pl.ds(pl.multiple_of(jnp.where(behind, 768, 0), 128), 384), :]
+        wide = jnp.dot(jnp.concatenate(lines, axis=1), rows, preferred_element_type=f32)
+        act[jnp.where(behind, 3, 2)] += join_x(wide.reshape(edge, edge, 384), edge)
+
+    gap = jnp.zeros((2, edge, 128), grid.dtype)
+    for side in range(2):
 
         def rim(row):
-            planes = [faces[side, k * wide_face + edge + row] for k in range(3)]
-            return jnp.stack(planes)
-
-        three = act.at[at : at + 3]
+            return jnp.stack([rims[side, k * (ny + nx) + row] for k in range(3)])
+
+        three = act.at[3 * side : 3 * side + 3]
         for i in range(ny):
             line = [rim(i), gap] if side == 0 else [gap, rim(i)]
             three[:, jnp.where(above[i], 0, edge - 1)] += y_terms(
@@ -410,7 +413,7 @@
             column[...] = jnp.zeros(column.shape, f32)
             ends = []
             for i in range(ny):
-                tile = faces[side, 3 * wide_face + i * nx + j].astype(f32)
+                tile = rims[side, 3 * (ny + nx) + i * nx + j].astype(f32)
                 ends.append(tile[edge - 3 :] if side == 0 else tile[:3])
             fill_column(column, 0 if side == 0 else 2, rim(ny + j), ends, above)
             add_column(three, x_terms(column, taps), j, nx, left[j])
@@ -768,8 +771,8 @@
         functools.partial(end_kernel, ny, nx),
         [six, ((devices, 2, channels), f32)],
         [
-            ((2,) + face[0], bf16),
-            ((4, edge + 2, edge, channels), bf16),
+            ((2, 3 * (ny + nx) + ny * nx, edge, channels), bf16),
+            ((8, edge + 2, edge, channels), bf16),
             ((5,) + column, f32),
         ],
         field,

time: 56 us -> 56 us (level)
  no operation moved by 1% of the time
where the time goes in v16:
time: 56 us; the launch traced here: 55.8 us
  blocking collectives  19.8 us (35%)
  starting transfers between devices  16.5 us (29%)
  Pallas kernels  14.5 us (26%)
  waiting for transfers between devices  4.84 us (9%)
    all_to_all x2, blocking collectives, share(): return lax.all_to_all(stats, PART, 0, 0)  19.8 us
    pallas_call x9, Pallas kernels, call(): pl.pallas_call(kernel, out_shape=[jax.ShapeDtypeStruct(shape, dtype) for...  14.3 us
    ppermute x2, starting transfers between devices, halos(): corner = lax.ppermute(corners[0], 'yx', self.swap_route(3))  5.77 us
    ppermute x1, starting transfers between devices, swap_depth(): lax.ppermute(inner, 'gz', routes[0])  2.92 us
    ppermute x3, starting transfers between devices, swap(): lax.ppermute(block, axis, [(i, i ^ mask) for i in range(lax.axis_size(axi...  2.68 us
    ppermute x2, starting transfers between devices, halos(): x = lax.ppermute(x_edges[0], 'yx', self.swap_route(1))  2.42 us
    ppermute x2, starting transfers between devices, halos(): y = lax.ppermute(y_edges[0], 'yx', self.swap_route(2))  2.05 us
    ppermute x3, waiting for transfers between devices, swap(): lax.ppermute(block, axis, [(i, i ^ mask) for i in range(lax.axis_size(axi...  1.69 us
  transfers between devices with their start and end apart: 11, of which 4 were waited for; matrix products, arithmetic and copies ran while one was open for 0% of the time, Pallas kernels for 19%

profile of v16, /device:TPU:0, one launch (start us, length us, event | category | flops | bytes accessed | tf_op | source)
XLA Modules:
  0.0 55.8 jit_solution(15108810369103871949)
XLA Ops:
  0.0 1.6 %shard_map.82 = (bf16[1,30,16,128]{3,2,1,0:T(8,128)(2,1)S(1)}, bf16[1,30,16,128]{3,2,1,0:T(8,128)(2,1)S(1)}, bf16[1,15,16,128]{3,2,1,0:T(8,128)(2,1)S(1)}, bf16[...) custom-call(bf16[16,16,16,128]{3,2,1,0:T(8,128)(2,1)} %x_in.1, bf16[27,128,128]{2,1,0:T(8,128)(2,1)} %bitcast.50, ...), custom_call_target="tpu_custom_call" | custom-call | bytes 5242880 | tf_op jit(solution)/shard_map/pallas_call | solution.py:105
  1.6 5.1 %collective-permute-start.2 = (bf16[15,16,128]{2,1,0:T(8,128)(2,1)S(1)}, bf16[15,16,128]{2,1,0:T(8,128)(2,1)S(1)}, u32[]{:S(2)}, u32[]{:S(2)}) collective-permute-start(bf16[15,16,128]{2,1,0:T(8,128)(2,1)S(1)} %bitcast.46), channel_id=1, source_target_pairs={{0,3},{1,2},{2,1},{3,0},{4,7},{5,6},{6,5},{7,4},{8,11},{9,10},{10,... | collective-permute-start | bytes 184328 | tf_op jit(solution)/shard_map/ppermute | solution.py:46
  6.7 0.0 collective-permute-start.1
  6.7 0.6 %collective-permute-start = (bf16[30,16,128]{2,1,0:T(8,128)(2,1)S(1)}, bf16[30,16,128]{2,1,0:T(8,128)(2,1)S(1)}, u32[]{:S(2)}, u32[]{:S(2)}) collective-permute-start(bf16[30,16,128]{2,1,0:T(8,128)(2,1)S(1)} %bitcast.44), channel_id=1, source_target_pairs={{0,2},{1,3},{2,0},{3,1},{4,6},{5,7},{6,4},{7,5},{8,10},{9,11},{10,... | collective-permute-start | bytes 368648 | tf_op jit(solution)/shard_map/ppermute | solution.py:44
  7.4 4.7 %shard_map.83 = (f32[16,16,16,128]{3,2,1,0:T(8,128)S(1)}, bf16[1152,384]{1,0:T(8,128)(2,1)S(1)}, bf16[1536,256]{1,0:T(8,128)(2,1)S(1)}, bf16[108,16,128]{2,1,0:T(8,128)(2,1)S(1)}) custom-call(bf16[108,16,128]{2,1,0:T(8,128)(2,1)} %bitcast.52, bf16[18,18,16,128]{3,2,1,0:T(8,128)(2,1)S(1)} %get-tuple-element.42.x.refs_0_, ...), custom_call_target="tpu_custom_call" | custom-call | flops 3623878656 | bytes 6291456 | tf_op jit(solution)/shard_map/pallas_call | solution.py:105
  12.1 0.0 collective-permute-done.2
  12.2 1.4 %collective-permute-done.1 = bf16[30,16,128]{2,1,0:T(8,128)(2,1)S(1)} collective-permute-done((bf16[30,16,128]{2,1,0:T(8,128)(2,1)S(1)}, bf16[30,16,128]{2,1,0:T(8,128)(2,1)S(1)}, u32[]{:S(2)}, u32[]{:S(2)}) %collective-permute-start.1) | collective-permute-done | bytes 122912 | tf_op jit(solution)/shard_map/ppermute | solution.py:45
  13.5 1.6 %collective-permute-done = bf16[30,16,128]{2,1,0:T(8,128)(2,1)S(1)} collective-permute-done((bf16[30,16,128]{2,1,0:T(8,128)(2,1)S(1)}, bf16[30,16,128]{2,1,0:T(8,128)(2,1)S(1)}, u32[]{:S(2)}, u32[]{:S(2)}) %collective-permute-start) | collective-permute-done | bytes 122912 | tf_op jit(solution)/shard_map/ppermute | solution.py:44
  15.2 0.7 %collective-permute-start.3 = (bf16[55,16,128]{2,1,0:T(8,128)(2,1)S(1)}, bf16[55,16,128]{2,1,0:T(8,128)(2,1)S(1)}, u32[]{:S(2)}, u32[]{:S(2)}) collective-permute-start(bf16[55,16,128]{2,1,0:T(8,128)(2,1)S(1)} %get-tuple-element.53), channel_id=1, source_target_pairs={{4,8},{8,4},{5,9},{9,5},{6,10},{10,6},{7,11},{11,7},{20,24},{24,20... | collective-permute-start | bytes 675848 | tf_op jit(solution)/shard_map/ppermute | solution.py:63
  15.8 2.9 %collective-permute-start.4 = (bf16[55,16,128]{2,1,0:T(8,128)(2,1)S(1)}, bf16[55,16,128]{2,1,0:T(8,128)(2,1)S(1)}, u32[]{:S(2)}, u32[]{:S(2)}) collective-permute-start(bf16[55,16,128]{2,1,0:T(8,128)(2,1)S(1)} %get-tuple-element.54), channel_id=1, source_target_pairs={{0,4},{4,0},{8,12},{12,8},{1,5},{5,1},{9,13},{13,9},{2,6},{6,2},{1... | collective-permute-start | bytes 675848 | tf_op jit(solution)/shard_map/ppermute | solution.py:63
  18.8 1.5 %collective-permute-start.5 = (bf16[1,3,14,16,128]{4,3,2,1,0:T(8,128)(2,1)S(1)}, bf16[1,3,14,16,128]{4,3,2,1,0:T(8,128)(2,1)S(1)}, u32[]{:S(2)}, u32[]{:S(2)}) collective-permute-start(bf16[1,3,14,16,128]{4,3,2,1,0:T(8,128)(2,1)S(1)} %bitcast.29), channel_id=1, source_target_pairs={{0,16},{16,0},{1,17},{17,1},{2,18},{18,2},{3,19},{19,3},{4,20},{20... | collective-permute-start | bytes 516104 | tf_op jit(solution)/shard_map/ppermute | solution.py:94
  20.3 1.1 %shard_map.84 = (f32[14,16,16,128]{3,2,1,0:T(8,128)S(1)}, f32[4,16,16,128]{3,2,1,0:T(8,128)S(1)}, f32[16,128]{1,0:T(8,128)S(1)}) custom-call(f32[16,16,16,128]{3,2,1,0:T(8,128)S(1)} %get-tuple-element.45.own, bf16[1,30,16,128]{3,2,1,0:T(8,128)(2,1)S(1)} %bitcast.34, bf16[1,30,16,128]{3,2,1,0:T(8,128)(2,1)S(1)} %bitcast.32, ...), custom_call_target="tpu_custom_call" | custom-call | flops 905969664 | bytes 6291456 | tf_op jit(solution)/shard_map/pallas_call | solution.py:105
  21.4 0.0 collective-permute-done.3.refs_3_
  21.4 0.0 collective-permute-done.4.refs_4_
  21.4 2.0 %shard_map.86 = (f32[6,16,16,128]{3,2,1,0:T(8,128)S(1)}, f32[16,2,128]{2,1,0:T(2,128)S(1)}) custom-call(bf16[18,18,16,128]{3,2,1,0:T(8,128)(2,1)S(1)} %get-tuple-element.42.x.refs_0_, f32[16,128]{1,0:T(8,128)S(1)} %get-tuple-element.51.refs_1_, f32[4,16,16,128]{3,2,1,0:T(8,128)S(1)} %get-tuple-element.52.refs_2_, ...), custom_call_target="tpu_custom_call" | custom-call | flops 1811939328 | bytes 3145728 | tf_op jit(solution)/shard_map/pallas_call | solution.py:105
  23.4 0.0 copy-start.3
  23.4 0.0 copy-start.4
  23.4 1.7 %collective-permute-done.5.refs_1_ = bf16[1,3,14,16,128]{4,3,2,1,0:T(8,128)(2,1)S(1)} collective-permute-done((bf16[1,3,14,16,128]{4,3,2,1,0:T(8,128)(2,1)S(1)}, bf16[1,3,14,16,128]{4,3,2,1,0:T(8,128)(2,1)S(1)}, u32[]{:S(2)}, u32[]{:S(2)}) %collective-permute-start.5) | collective-permute-done | bytes 172064 | tf_op jit(solution)/shard_map/ppermute | solution.py:94
  25.1 1.0 %collective-permute-start.6 = (bf16[2,3,14,16,128]{4,3,2,1,0:T(8,128)(2,1)S(1)}, bf16[2,3,14,16,128]{4,3,2,1,0:T(8,128)(2,1)S(1)}, u32[]{:S(2)}, u32[]{:S(2)}) collective-permute-start(bf16[2,3,14,16,128]{4,3,2,1,0:T(8,128)(2,1)S(1)} %bitcast.27), channel_id=1, source_target_pairs={{0,8},{4,12},{8,0},{12,4},{1,9},{5,13},{9,1},{13,5},{2,10},{6,14},... | collective-permute-start | bytes 1032200 | tf_op jit(solution)/shard_map/ppermute | solution.py:94
  26.1 9.7 %all_to_all.10.stats = f32[16,2,128]{2,1,0:T(2,128)S(1)} all-to-all(f32[16,2,128]{2,1,0:T(2,128)S(1)} %get-tuple-element.59), channel_id=1, replica_groups=mesh['cand'=2,'gz'=4,'yx'=4] {'gz','yx'}, dimensions={0} | all-to-all | bytes 32768 | tf_op jit(solution)/shard_map/all_to_all | solution.py:98
  35.8 0.0 collective-permute-done.6.refs_1_
  35.9 0.2 collective-permute-start.7
  36.1 0.0 copy-done.3
  36.1 0.0 copy-done.4
  36.1 1.1 %shard_map.88 = (bf16[16,16,16,128]{3,2,1,0:T(8,128)(2,1)S(1)}, f32[10,8,8,128]{3,2,1,0:T(8,128)S(1)}, bf16[1,80,128]{2,1,0:T(8,128)(2,1)S(1)}, bf16[1,80,128]{2,1,0:T(8,128)(2,1)S(1)}, f32[1,16,128]{2,1,0:T(8,128)S(1)}) custom-call(f32[14,16,16,128]{3,2,1,0:T(8,128)S(1)} %get-tuple-element.50.inner, f32[6,16,16,128]{3,2,1,0:T(8,128)S(1)} %get-tuple-element.56.ends, ...), custom_call_target="tpu_custom_call" | custom-call | flops 10485760 | bytes 3145728 | tf_op jit(solution)/shard_map/pallas_call | solution.py:105
  37.2 0.7 %collective-permute-start.10 = (f32[16,128]{1,0:T(8,128)S(1)}, f32[16,128]{1,0:T(8,128)S(1)}, u32[]{:S(2)}, u32[]{:S(2)}) collective-permute-start(f32[16,128]{1,0:T(8,128)S(1)} %bitcast.49), channel_id=1, source_target_pairs={{0,3},{1,2},{2,1},{3,0},{4,7},{5,6},{6,5},{7,4},{8,11},{9,10},{10,... | collective-permute-start | bytes 24584 | tf_op jit(solution)/shard_map/ppermute | solution.py:46
  37.9 1.4 %collective-permute-start.8 = (bf16[80,128]{1,0:T(8,128)(2,1)S(1)}, bf16[80,128]{1,0:T(8,128)(2,1)S(1)}, u32[]{:S(2)}, u32[]{:S(2)}) collective-permute-start(bf16[80,128]{1,0:T(8,128)(2,1)S(1)} %bitcast.48), channel_id=1, source_target_pairs={{0,2},{1,3},{2,0},{3,1},{4,6},{5,7},{6,4},{7,5},{8,10},{9,11},{10,... | collective-permute-start | bytes 61448 | tf_op jit(solution)/shard_map/ppermute | solution.py:44
  39.3 2.4 %collective-permute-start.9 = (bf16[80,128]{1,0:T(8,128)(2,1)S(1)}, bf16[80,128]{1,0:T(8,128)(2,1)S(1)}, u32[]{:S(2)}, u32[]{:S(2)}) collective-permute-start(bf16[80,128]{1,0:T(8,128)(2,1)S(1)} %bitcast.47), channel_id=1, source_target_pairs={{0,1},{1,0},{2,3},{3,2},{4,5},{5,4},{6,7},{7,6},{8,9},{9,8},{10,11... | collective-permute-start | bytes 61448 | tf_op jit(solution)/shard_map/ppermute | solution.py:45
  41.7 0.0 collective-permute-done.7.refs_1_
  41.7 0.1 shard_map.90
  41.8 1.4 %shard_map.91 = (f32[2,512,128]{2,1,0:T(8,128)S(1)}, bf16[4,108,16,128]{3,2,1,0:T(8,128)(2,1)S(1)}) custom-call(f32[10,8,8,128]{3,2,1,0:T(8,128)S(1)} %get-tuple-element.62.pooled, bf16[108,16,128]{2,1,0:T(8,128)(2,1)S(1)} %get-tuple-element.63.own, bf16[8,3,14,16,128]{4,3,2,1,0:T(8,128)(2,1)S(1)} %bitcast.26), custom_call_target="tpu_custom_call" | custom-call | flops 905969664 | bytes 4194304 | tf_op jit(solution)/shard_map/pallas_call | solution.py:105
  43.2 0.0 copy-start
  43.3 0.0 copy-start.1
  43.3 0.0 copy-start.2
  43.3 0.0 collective-permute-done.10
  43.3 0.0 collective-permute-done.8
  43.3 0.2 collective-permute-done.9
  43.5 0.7 %shard_map.92 = (f32[2,512,128]{2,1,0:T(8,128)S(1)}, f32[16,2,256]{2,1,0:T(2,128)S(1)}) custom-call(f32[2,512,128]{2,1,0:T(8,128)S(1)} %get-tuple-element.65.own, bf16[1,80,128]{2,1,0:T(8,128)(2,1)S(1)} %bitcast.37, bf16[1,80,128]{2,1,0:T(8,128)(2,1)S(1)} %bitcast.38, f32[1,16,128]{2,1,0:T(8,128)S(1)} %bitcast.39, ...), custom_call_target="tpu_custom_call" | custom-call | flops 67108864 | bytes 3145728 | tf_op jit(solution)/shard_map/pallas_call | solution.py:105
  44.2 10.0 %all_to_all.11.stats = f32[16,2,256]{2,1,0:T(2,128)S(1)} all-to-all(f32[16,2,256]{2,1,0:T(2,128)S(1)} %get-tuple-element.71), channel_id=1, replica_groups=mesh['cand'=2,'gz'=4,'yx'=4] {'gz','yx'}, dimensions={0} | all-to-all | bytes 65536 | tf_op jit(solution)/shard_map/all_to_all | solution.py:98
  54.2 0.0 copy-done
  54.2 0.0 copy-done.1
  54.2 0.0 copy-done.2
  54.3 1.5 %shard_map.93 = bf16[16,16,16,128]{3,2,1,0:T(8,128)(2,1)} custom-call(f32[2,512,128]{2,1,0:T(8,128)S(1)} %get-tuple-element.70.act, f32[16,2,256]{2,1,0:T(2,128)S(1)} %all_to_all.11.stats, f32[1,256]{1,0:T(1,128)S(1)} %bitcast.40, f32[1,256]{1,0:T(1,128)S(1)} %bitcast.41, bf16[256,128]{1,0:T(8,128)(2,1)S(1)} %copy-done, ...), custom_call_target="tpu_custom_call" | custom-call | flops 67108864 | bytes 3145728 | tf_op jit(solution)/shard_map/pallas_call | solution.py:105
  (3 shorter events, 0.1 us)
Async XLA Ops:
  1.6 10.5 %collective-permute-start.2 = (bf16[15,16,128]{2,1,0:T(8,128)(2,1)S(1)}, bf16[15,16,128]{2,1,0:T(8,128)(2,1)S(1)}, u32[]{:S(2)}, u32[]{:S(2)}) collective-permute-start(bf16[15,16,128]{2,1,0:T(8,128)(2,1)S(1)} %bitcast.46), channel_id=1, source_target_pairs={{0,3},{1,2},{2,1},{3,0},{4,7},{5,6},{6,5},{7,4},{8,11},{9,10},{10,... | collective-permute-start | bytes 184328 | tf_op jit(solution)/shard_map/ppermute | solution.py:46
  6.7 6.8 %collective-permute-start.1 = (bf16[30,16,128]{2,1,0:T(8,128)(2,1)S(1)}, bf16[30,16,128]{2,1,0:T(8,128)(2,1)S(1)}, u32[]{:S(2)}, u32[]{:S(2)}) collective-permute-start(bf16[30,16,128]{2,1,0:T(8,128)(2,1)S(1)} %bitcast.45), channel_id=1, source_target_pairs={{0,1},{1,0},{2,3},{3,2},{4,5},{5,4},{6,7},{7,6},{8,9},{9,8},{10,11... | collective-permute-start | bytes 368648 | tf_op jit(solution)/shard_map/ppermute | solution.py:45
  6.7 8.4 %collective-permute-start = (bf16[30,16,128]{2,1,0:T(8,128)(2,1)S(1)}, bf16[30,16,128]{2,1,0:T(8,128)(2,1)S(1)}, u32[]{:S(2)}, u32[]{:S(2)}) collective-permute-start(bf16[30,16,128]{2,1,0:T(8,128)(2,1)S(1)} %bitcast.44), channel_id=1, source_target_pairs={{0,2},{1,3},{2,0},{3,1},{4,6},{5,7},{6,4},{7,5},{8,10},{9,11},{10,... | collective-permute-start | bytes 368648 | tf_op jit(solution)/shard_map/ppermute | solution.py:44
  15.2 6.2 %collective-permute-start.3 = (bf16[55,16,128]{2,1,0:T(8,128)(2,1)S(1)}, bf16[55,16,128]{2,1,0:T(8,128)(2,1)S(1)}, u32[]{:S(2)}, u32[]{:S(2)}) collective-permute-start(bf16[55,16,128]{2,1,0:T(8,128)(2,1)S(1)} %get-tuple-element.53), channel_id=1, source_target_pairs={{4,8},{8,4},{5,9},{9,5},{6,10},{10,6},{7,11},{11,7},{20,24},{24,20... | collective-permute-start | bytes 675848 | tf_op jit(solution)/shard_map/ppermute | solution.py:63
  15.8 5.5 %collective-permute-start.4 = (bf16[55,16,128]{2,1,0:T(8,128)(2,1)S(1)}, bf16[55,16,128]{2,1,0:T(8,128)(2,1)S(1)}, u32[]{:S(2)}, u32[]{:S(2)}) collective-permute-start(bf16[55,16,128]{2,1,0:T(8,128)(2,1)S(1)} %get-tuple-element.54), channel_id=1, source_target_pairs={{0,4},{4,0},{8,12},{12,8},{1,5},{5,1},{9,13},{13,9},{2,6},{6,2},{1... | collective-permute-start | bytes 675848 | tf_op jit(solution)/shard_map/ppermute | solution.py:63
  18.8 6.4 %collective-permute-start.5 = (bf16[1,3,14,16,128]{4,3,2,1,0:T(8,128)(2,1)S(1)}, bf16[1,3,14,16,128]{4,3,2,1,0:T(8,128)(2,1)S(1)}, u32[]{:S(2)}, u32[]{:S(2)}) collective-permute-start(bf16[1,3,14,16,128]{4,3,2,1,0:T(8,128)(2,1)S(1)} %bitcast.29), channel_id=1, source_target_pairs={{0,16},{16,0},{1,17},{17,1},{2,18},{18,2},{3,19},{19,3},{4,20},{20... | collective-permute-start | bytes 516104 | tf_op jit(solution)/shard_map/ppermute | solution.py:94
  23.4 12.7 %copy-start.3 = (f32[128]{0:T(128)S(1)}, f32[128]{0:T(128)}, u32[]{:S(2)}) copy-start(f32[128]{0:T(128)} %param.10) | copy-start | bytes 1540
  23.4 12.7 %copy-start.4 = (f32[128]{0:T(128)S(1)}, f32[128]{0:T(128)}, u32[]{:S(2)}) copy-start(f32[128]{0:T(128)} %param.11) | copy-start | bytes 1540
  25.1 10.7 %collective-permute-start.6 = (bf16[2,3,14,16,128]{4,3,2,1,0:T(8,128)(2,1)S(1)}, bf16[2,3,14,16,128]{4,3,2,1,0:T(8,128)(2,1)S(1)}, u32[]{:S(2)}, u32[]{:S(2)}) collective-permute-start(bf16[2,3,14,16,128]{4,3,2,1,0:T(8,128)(2,1)S(1)} %bitcast.27), channel_id=1, source_target_pairs={{0,8},{4,12},{8,0},{12,4},{1,9},{5,13},{9,1},{13,5},{2,10},{6,14},... | collective-permute-start | bytes 1032200 | tf_op jit(solution)/shard_map/ppermute | solution.py:94
  35.9 5.8 %collective-permute-start.7 = (bf16[4,3,14,16,128]{4,3,2,1,0:T(8,128)(2,1)S(1)}, bf16[4,3,14,16,128]{4,3,2,1,0:T(8,128)(2,1)S(1)}, u32[]{:S(2)}, u32[]{:S(2)}) collective-permute-start(bf16[4,3,14,16,128]{4,3,2,1,0:T(8,128)(2,1)S(1)} %bitcast.24), channel_id=1, source_target_pairs={{0,4},{4,0},{8,12},{12,8},{1,5},{5,1},{9,13},{13,9},{2,6},{6,2},{1... | collective-permute-start | bytes 2064392 | tf_op jit(solution)/shard_map/ppermute | solution.py:94
  37.2 6.0 %collective-permute-start.10 = (f32[16,128]{1,0:T(8,128)S(1)}, f32[16,128]{1,0:T(8,128)S(1)}, u32[]{:S(2)}, u32[]{:S(2)}) collective-permute-start(f32[16,128]{1,0:T(8,128)S(1)} %bitcast.49), channel_id=1, source_target_pairs={{0,3},{1,2},{2,1},{3,0},{4,7},{5,6},{6,5},{7,4},{8,11},{9,10},{10,... | collective-permute-start | bytes 24584 | tf_op jit(solution)/shard_map/ppermute | solution.py:46
  37.9 5.4 %collective-permute-start.8 = (bf16[80,128]{1,0:T(8,128)(2,1)S(1)}, bf16[80,128]{1,0:T(8,128)(2,1)S(1)}, u32[]{:S(2)}, u32[]{:S(2)}) collective-permute-start(bf16[80,128]{1,0:T(8,128)(2,1)S(1)} %bitcast.48), channel_id=1, source_target_pairs={{0,2},{1,3},{2,0},{3,1},{4,6},{5,7},{6,4},{7,5},{8,10},{9,11},{10,... | collective-permute-start | bytes 61448 | tf_op jit(solution)/shard_map/ppermute | solution.py:44
  39.3 4.2 %collective-permute-start.9 = (bf16[80,128]{1,0:T(8,128)(2,1)S(1)}, bf16[80,128]{1,0:T(8,128)(2,1)S(1)}, u32[]{:S(2)}, u32[]{:S(2)}) collective-permute-start(bf16[80,128]{1,0:T(8,128)(2,1)S(1)} %bitcast.47), channel_id=1, source_target_pairs={{0,1},{1,0},{2,3},{3,2},{4,5},{5,4},{6,7},{7,6},{8,9},{9,8},{10,11... | collective-permute-start | bytes 61448 | tf_op jit(solution)/shard_map/ppermute | solution.py:45
  43.2 11.0 %copy-start = (bf16[256,128]{1,0:T(8,128)(2,1)S(1)}, bf16[256,128]{1,0:T(8,128)(2,1)}, u32[]{:S(2)}) copy-start(bf16[256,128]{1,0:T(8,128)(2,1)} %up.1) | copy-start | bytes 196612
  43.3 11.0 %copy-start.1 = (f32[256]{0:T(256)S(1)}, f32[256]{0:T(256)}, u32[]{:S(2)}) copy-start(f32[256]{0:T(256)} %param.13) | copy-start | bytes 3076
  43.3 11.0 %copy-start.2 = (f32[256]{0:T(256)S(1)}, f32[256]{0:T(256)}, u32[]{:S(2)}) copy-start(f32[256]{0:T(256)} %param.14) | copy-start | bytes 3076

commit v17 on v11

--- a/solution.py
+++ b/solution.py
@@ -187,6 +187,8 @@
                 face[row + edge + ny + j] = x_halos[j, at + k]
         for k in range(ny * nx):
             face[3 * wide + k] = corners[k, 0]
+    for k in range(inner.shape[0], outer.shape[0]):
+        outer[k] = corners[0, 0]
     if size:
         riders[0][0] = x_halos[0, edge : edge + size]
         riders[0][1] = y_halos[0, edge : edge + size]
@@ -368,8 +370,9 @@
     wide_face = edge + ny + nx
     f32 = jnp.float32
     odd = lax.axis_index("gz") % 2 == 1
-    faces[0] = jnp.where(odd, inner_face[...], outer_face[...])
-    faces[1] = jnp.where(odd, outer_face[...], inner_face[...])
+    size = inner_face.shape[0]
+    faces[0] = jnp.where(odd, inner_face[...], outer_face[0:size])
+    faces[1] = jnp.where(odd, outer_face[0:size], inner_face[...])
     above, left = Square().low_sides()
     blank = jnp.zeros(grid.shape[:1] + grid.shape[2:], grid.dtype)
     grid[:, 0] = blank
@@ -735,7 +738,7 @@
     held = [((4, riders.size, 16, channels), bf16)] if riders.size else []
     outer, inner, *held = call(
         functools.partial(face_kernel, ny, nx, riders.size),
-        [face, face] + held,
+        [((face[0][0] + 2,) + face[0][1:], bf16), face] + held,
         [],
         field,
         y,

time: 57 us -> 55.5 us (0.974)
  starting transfers between devices: 19.8 us -> 18.3 us
    ppermute x3, starting transfers between devices: 5.95 us -> 4.78 us  [swap(): lax.ppermute(block, axis, [(i, i ^ mask) for i in range(lax.axis_size(axi...]
  transfers between devices with their start and end apart: 11 -> 11, of which waited for: 4 -> 4; matrix products, arithmetic and copies ran while one was open for 0% -> 0% of each run, Pallas kernels for 18% -> 19%
where the time goes in v17:
time: 55.5 us; the launch traced here: 55.3 us
  blocking collectives  19.2 us (35%)
  starting transfers between devices  18.3 us (33%)
  Pallas kernels  14.4 us (26%)
  waiting for transfers between devices  3.23 us (6%)
    all_to_all x2, blocking collectives, share(): return lax.all_to_all(stats, PART, 0, 0)  19.2 us
    pallas_call x9, Pallas kernels, call(): pl.pallas_call(kernel, out_shape=[jax.ShapeDtypeStruct(shape, dtype) for...  14.2 us
    ppermute x2, starting transfers between devices, halos(): corner = lax.ppermute(corners[0], 'yx', self.swap_route(3))  5.77 us
    ppermute x3, starting transfers between devices, swap(): lax.ppermute(block, axis, [(i, i ^ mask) for i in range(lax.axis_size(axi...  4.78 us
    ppermute x1, starting transfers between devices, swap_depth(): lax.ppermute(inner, 'gz', routes[0])  2.56 us
    ppermute x2, starting transfers between devices, halos(): x = lax.ppermute(x_edges[0], 'yx', self.swap_route(1))  2.42 us
    ppermute x2, starting transfers between devices, halos(): y = lax.ppermute(y_edges[0], 'yx', self.swap_route(2))  2.05 us
    ppermute x2, waiting for transfers between devices, halos(): y = lax.ppermute(y_edges[0], 'yx', self.swap_route(2))  1.59 us
  transfers between devices with their start and end apart: 11, of which 4 were waited for; matrix products, arithmetic and copies ran while one was open for 0% of the time, Pallas kernels for 19%

profile of v17, /device:TPU:0, one launch (start us, length us, event | category | flops | bytes accessed | tf_op | source)
XLA Modules:
  0.0 55.3 jit_solution(4740369685020385018)
XLA Ops:
  0.0 1.6 %shard_map.82 = (bf16[1,30,16,128]{3,2,1,0:T(8,128)(2,1)S(1)}, bf16[1,30,16,128]{3,2,1,0:T(8,128)(2,1)S(1)}, bf16[1,15,16,128]{3,2,1,0:T(8,128)(2,1)S(1)}, bf16[...) custom-call(bf16[16,16,16,128]{3,2,1,0:T(8,128)(2,1)} %x_in.1, bf16[27,128,128]{2,1,0:T(8,128)(2,1)} %bitcast.50, ...), custom_call_target="tpu_custom_call" | custom-call | bytes 5242880 | tf_op jit(solution)/shard_map/pallas_call | solution.py:105
  1.6 5.1 %collective-permute-start.2 = (bf16[15,16,128]{2,1,0:T(8,128)(2,1)S(1)}, bf16[15,16,128]{2,1,0:T(8,128)(2,1)S(1)}, u32[]{:S(2)}, u32[]{:S(2)}) collective-permute-start(bf16[15,16,128]{2,1,0:T(8,128)(2,1)S(1)} %bitcast.46), channel_id=1, source_target_pairs={{0,3},{1,2},{2,1},{3,0},{4,7},{5,6},{6,5},{7,4},{8,11},{9,10},{10,... | collective-permute-start | bytes 184328 | tf_op jit(solution)/shard_map/ppermute | solution.py:46
  6.7 0.0 collective-permute-start.1
  6.7 0.6 %collective-permute-start = (bf16[30,16,128]{2,1,0:T(8,128)(2,1)S(1)}, bf16[30,16,128]{2,1,0:T(8,128)(2,1)S(1)}, u32[]{:S(2)}, u32[]{:S(2)}) collective-permute-start(bf16[30,16,128]{2,1,0:T(8,128)(2,1)S(1)} %bitcast.44), channel_id=1, source_target_pairs={{0,2},{1,3},{2,0},{3,1},{4,6},{5,7},{6,4},{7,5},{8,10},{9,11},{10,... | collective-permute-start | bytes 368648 | tf_op jit(solution)/shard_map/ppermute | solution.py:44
  7.4 4.7 %shard_map.83 = (f32[16,16,16,128]{3,2,1,0:T(8,128)S(1)}, bf16[1152,384]{1,0:T(8,128)(2,1)S(1)}, bf16[1536,256]{1,0:T(8,128)(2,1)S(1)}, bf16[108,16,128]{2,1,0:T(8,128)(2,1)S(1)}) custom-call(bf16[108,16,128]{2,1,0:T(8,128)(2,1)} %bitcast.52, bf16[18,18,16,128]{3,2,1,0:T(8,128)(2,1)S(1)} %get-tuple-element.42.x.refs_0_, ...), custom_call_target="tpu_custom_call" | custom-call | flops 3623878656 | bytes 6291456 | tf_op jit(solution)/shard_map/pallas_call | solution.py:105
  12.1 0.0 collective-permute-done.2
  12.1 1.4 %collective-permute-done.1 = bf16[30,16,128]{2,1,0:T(8,128)(2,1)S(1)} collective-permute-done((bf16[30,16,128]{2,1,0:T(8,128)(2,1)S(1)}, bf16[30,16,128]{2,1,0:T(8,128)(2,1)S(1)}, u32[]{:S(2)}, u32[]{:S(2)}) %collective-permute-start.1) | collective-permute-done | bytes 122912 | tf_op jit(solution)/shard_map/ppermute | solution.py:45
  13.5 1.6 %collective-permute-done = bf16[30,16,128]{2,1,0:T(8,128)(2,1)S(1)} collective-permute-done((bf16[30,16,128]{2,1,0:T(8,128)(2,1)S(1)}, bf16[30,16,128]{2,1,0:T(8,128)(2,1)S(1)}, u32[]{:S(2)}, u32[]{:S(2)}) %collective-permute-start) | collective-permute-done | bytes 122912 | tf_op jit(solution)/shard_map/ppermute | solution.py:44
  15.1 0.1 shard_map.85
  15.2 0.7 %collective-permute-start.3 = (bf16[57,16,128]{2,1,0:T(8,128)(2,1)S(1)}, bf16[57,16,128]{2,1,0:T(8,128)(2,1)S(1)}, u32[]{:S(2)}, u32[]{:S(2)}) collective-permute-start(bf16[57,16,128]{2,1,0:T(8,128)(2,1)S(1)} %get-tuple-element.53), channel_id=1, source_target_pairs={{4,8},{8,4},{5,9},{9,5},{6,10},{10,6},{7,11},{11,7},{20,24},{24,20... | collective-permute-start | bytes 700424 | tf_op jit(solution)/shard_map/ppermute | solution.py:63
  15.8 1.6 %collective-permute-start.5 = (bf16[1,4,14,16,128]{4,3,2,1,0:T(8,128)(2,1)S(1)}, bf16[1,4,14,16,128]{4,3,2,1,0:T(8,128)(2,1)S(1)}, u32[]{:S(2)}, u32[]{:S(2)}) collective-permute-start(bf16[1,4,14,16,128]{4,3,2,1,0:T(8,128)(2,1)S(1)} %bitcast.35), channel_id=1, source_target_pairs={{0,16},{16,0},{1,17},{17,1},{2,18},{18,2},{3,19},{19,3},{4,20},{20... | collective-permute-start | bytes 688136 | tf_op jit(solution)/shard_map/ppermute | solution.py:94
  17.5 2.6 %collective-permute-start.4 = (bf16[55,16,128]{2,1,0:T(8,128)(2,1)S(1)}, bf16[55,16,128]{2,1,0:T(8,128)(2,1)S(1)}, u32[]{:S(2)}, u32[]{:S(2)}) collective-permute-start(bf16[55,16,128]{2,1,0:T(8,128)(2,1)S(1)} %get-tuple-element.54), channel_id=1, source_target_pairs={{0,4},{4,0},{8,12},{12,8},{1,5},{5,1},{9,13},{13,9},{2,6},{6,2},{1... | collective-permute-start | bytes 675848 | tf_op jit(solution)/shard_map/ppermute | solution.py:63
  20.0 1.0 %shard_map.84 = (f32[14,16,16,128]{3,2,1,0:T(8,128)S(1)}, f32[4,16,16,128]{3,2,1,0:T(8,128)S(1)}, f32[16,128]{1,0:T(8,128)S(1)}) custom-call(f32[16,16,16,128]{3,2,1,0:T(8,128)S(1)} %get-tuple-element.45.own, bf16[1,30,16,128]{3,2,1,0:T(8,128)(2,1)S(1)} %bitcast.32, bf16[1,30,16,128]{3,2,1,0:T(8,128)(2,1)S(1)} %bitcast.30, ...), custom_call_target="tpu_custom_call" | custom-call | tf_op jit(solution)/shard_map/pallas_call | solution.py:105
  21.1 0.1 collective-permute-done.4.refs_4_
  21.1 0.0 collective-permute-done.3.refs_3_
  21.1 2.0 %shard_map.86 = (f32[6,16,16,128]{3,2,1,0:T(8,128)S(1)}, f32[16,2,128]{2,1,0:T(2,128)S(1)}) custom-call(bf16[18,18,16,128]{3,2,1,0:T(8,128)(2,1)S(1)} %get-tuple-element.42.x.refs_0_, f32[16,128]{1,0:T(8,128)S(1)} %get-tuple-element.51.refs_1_, f32[4,16,16,128]{3,2,1,0:T(8,128)S(1)} %get-tuple-element.52.refs_2_, ...), custom_call_target="tpu_custom_call" | custom-call | tf_op jit(solution)/shard_map/pallas_call | solution.py:105
  23.1 0.0 copy-start.3
  23.1 0.0 copy-start.4
  23.2 0.0 collective-permute-done.5.refs_1_
  23.2 3.0 %collective-permute-start.6 = (bf16[2,3,14,16,128]{4,3,2,1,0:T(8,128)(2,1)S(1)}, bf16[2,3,14,16,128]{4,3,2,1,0:T(8,128)(2,1)S(1)}, u32[]{:S(2)}, u32[]{:S(2)}) collective-permute-start(bf16[2,3,14,16,128]{4,3,2,1,0:T(8,128)(2,1)S(1)} %bitcast.27), channel_id=1, source_target_pairs={{0,8},{4,12},{8,0},{12,4},{1,9},{5,13},{9,1},{13,5},{2,10},{6,14},... | collective-permute-start | bytes 1032200 | tf_op jit(solution)/shard_map/ppermute | solution.py:94
  26.2 9.2 %all_to_all.10.stats = f32[16,2,128]{2,1,0:T(2,128)S(1)} all-to-all(f32[16,2,128]{2,1,0:T(2,128)S(1)} %get-tuple-element.59), channel_id=1, replica_groups=mesh['cand'=2,'gz'=4,'yx'=4] {'gz','yx'}, dimensions={0} | all-to-all | bytes 32768 | tf_op jit(solution)/shard_map/all_to_all | solution.py:98
  35.4 0.0 collective-permute-done.6.refs_1_
  35.4 0.2 collective-permute-start.7
  35.6 0.0 copy-done.3
  35.6 0.0 copy-done.4
  35.6 1.1 %shard_map.88 = (bf16[16,16,16,128]{3,2,1,0:T(8,128)(2,1)S(1)}, f32[10,8,8,128]{3,2,1,0:T(8,128)S(1)}, bf16[1,80,128]{2,1,0:T(8,128)(2,1)S(1)}, bf16[1,80,128]{2,1,0:T(8,128)(2,1)S(1)}, f32[1,16,128]{2,1,0:T(8,128)S(1)}) custom-call(f32[14,16,16,128]{3,2,1,0:T(8,128)S(1)} %get-tuple-element.50.inner, f32[6,16,16,128]{3,2,1,0:T(8,128)S(1)} %get-tuple-element.56.ends, ...), custom_call_target="tpu_custom_call" | custom-call | flops 10485760 | bytes 3145728 | tf_op jit(solution)/shard_map/pallas_call | solution.py:105
  36.8 0.7 %collective-permute-start.10 = (f32[16,128]{1,0:T(8,128)S(1)}, f32[16,128]{1,0:T(8,128)S(1)}, u32[]{:S(2)}, u32[]{:S(2)}) collective-permute-start(f32[16,128]{1,0:T(8,128)S(1)} %bitcast.49), channel_id=1, source_target_pairs={{0,3},{1,2},{2,1},{3,0},{4,7},{5,6},{6,5},{7,4},{8,11},{9,10},{10,... | collective-permute-start | bytes 24584 | tf_op jit(solution)/shard_map/ppermute | solution.py:46
  37.4 1.4 %collective-permute-start.8 = (bf16[80,128]{1,0:T(8,128)(2,1)S(1)}, bf16[80,128]{1,0:T(8,128)(2,1)S(1)}, u32[]{:S(2)}, u32[]{:S(2)}) collective-permute-start(bf16[80,128]{1,0:T(8,128)(2,1)S(1)} %bitcast.48), channel_id=1, source_target_pairs={{0,2},{1,3},{2,0},{3,1},{4,6},{5,7},{6,4},{7,5},{8,10},{9,11},{10,... | collective-permute-start | bytes 61448 | tf_op jit(solution)/shard_map/ppermute | solution.py:44
  38.8 2.4 %collective-permute-start.9 = (bf16[80,128]{1,0:T(8,128)(2,1)S(1)}, bf16[80,128]{1,0:T(8,128)(2,1)S(1)}, u32[]{:S(2)}, u32[]{:S(2)}) collective-permute-start(bf16[80,128]{1,0:T(8,128)(2,1)S(1)} %bitcast.47), channel_id=1, source_target_pairs={{0,1},{1,0},{2,3},{3,2},{4,5},{5,4},{6,7},{7,6},{8,9},{9,8},{10,11... | collective-permute-start | bytes 61448 | tf_op jit(solution)/shard_map/ppermute | solution.py:45
  41.2 0.0 collective-permute-done.7.refs_1_
  41.2 0.1 shard_map.90
  41.3 1.4 %shard_map.91 = (f32[2,512,128]{2,1,0:T(8,128)S(1)}, bf16[4,108,16,128]{3,2,1,0:T(8,128)(2,1)S(1)}) custom-call(f32[10,8,8,128]{3,2,1,0:T(8,128)S(1)} %get-tuple-element.62.pooled, bf16[108,16,128]{2,1,0:T(8,128)(2,1)S(1)} %get-tuple-element.63.own, bf16[8,3,14,16,128]{4,3,2,1,0:T(8,128)(2,1)S(1)} %bitcast.26), custom_call_target="tpu_custom_call" | custom-call | flops 905969664 | bytes 4194304 | tf_op jit(solution)/shard_map/pallas_call | solution.py:105
  42.8 0.0 copy-start
  42.8 0.0 copy-start.1
  42.8 0.0 copy-start.2
  42.8 0.0 collective-permute-done.10
  42.8 0.0 collective-permute-done.8
  42.8 0.2 collective-permute-done.9
  43.0 0.7 %shard_map.92 = (f32[2,512,128]{2,1,0:T(8,128)S(1)}, f32[16,2,256]{2,1,0:T(2,128)S(1)}) custom-call(f32[2,512,128]{2,1,0:T(8,128)S(1)} %get-tuple-element.65.own, bf16[1,80,128]{2,1,0:T(8,128)(2,1)S(1)} %bitcast.37, bf16[1,80,128]{2,1,0:T(8,128)(2,1)S(1)} %bitcast.38, f32[1,16,128]{2,1,0:T(8,128)S(1)} %bitcast.39, ...), custom_call_target="tpu_custom_call" | custom-call | flops 67108864 | bytes 3145728 | tf_op jit(solution)/shard_map/pallas_call | solution.py:105
  43.7 10.0 %all_to_all.11.stats = f32[16,2,256]{2,1,0:T(2,128)S(1)} all-to-all(f32[16,2,256]{2,1,0:T(2,128)S(1)} %get-tuple-element.71), channel_id=1, replica_groups=mesh['cand'=2,'gz'=4,'yx'=4] {'gz','yx'}, dimensions={0} | all-to-all | bytes 65536 | tf_op jit(solution)/shard_map/all_to_all | solution.py:98
  53.8 0.0 copy-done
  53.8 0.0 copy-done.1
  53.8 0.0 copy-done.2
  53.8 1.5 %shard_map.93 = bf16[16,16,16,128]{3,2,1,0:T(8,128)(2,1)} custom-call(f32[2,512,128]{2,1,0:T(8,128)S(1)} %get-tuple-element.70.act, f32[16,2,256]{2,1,0:T(2,128)S(1)} %all_to_all.11.stats, f32[1,256]{1,0:T(1,128)S(1)} %bitcast.40, f32[1,256]{1,0:T(1,128)S(1)} %bitcast.41, bf16[256,128]{1,0:T(8,128)(2,1)S(1)} %copy-done, ...), custom_call_target="tpu_custom_call" | custom-call | flops 67108864 | bytes 3145728 | tf_op jit(solution)/shard_map/pallas_call | solution.py:105
  (2 shorter events, 0.1 us)
Async XLA Ops:
  1.6 10.5 %collective-permute-start.2 = (bf16[15,16,128]{2,1,0:T(8,128)(2,1)S(1)}, bf16[15,16,128]{2,1,0:T(8,128)(2,1)S(1)}, u32[]{:S(2)}, u32[]{:S(2)}) collective-permute-start(bf16[15,16,128]{2,1,0:T(8,128)(2,1)S(1)} %bitcast.46), channel_id=1, source_target_pairs={{0,3},{1,2},{2,1},{3,0},{4,7},{5,6},{6,5},{7,4},{8,11},{9,10},{10,... | collective-permute-start | bytes 184328 | tf_op jit(solution)/shard_map/ppermute | solution.py:46
  6.7 6.8 %collective-permute-start.1 = (bf16[30,16,128]{2,1,0:T(8,128)(2,1)S(1)}, bf16[30,16,128]{2,1,0:T(8,128)(2,1)S(1)}, u32[]{:S(2)}, u32[]{:S(2)}) collective-permute-start(bf16[30,16,128]{2,1,0:T(8,128)(2,1)S(1)} %bitcast.45), channel_id=1, source_target_pairs={{0,1},{1,0},{2,3},{3,2},{4,5},{5,4},{6,7},{7,6},{8,9},{9,8},{10,11... | collective-permute-start | bytes 368648 | tf_op jit(solution)/shard_map/ppermute | solution.py:45
  6.7 8.4 %collective-permute-start = (bf16[30,16,128]{2,1,0:T(8,128)(2,1)S(1)}, bf16[30,16,128]{2,1,0:T(8,128)(2,1)S(1)}, u32[]{:S(2)}, u32[]{:S(2)}) collective-permute-start(bf16[30,16,128]{2,1,0:T(8,128)(2,1)S(1)} %bitcast.44), channel_id=1, source_target_pairs={{0,2},{1,3},{2,0},{3,1},{4,6},{5,7},{6,4},{7,5},{8,10},{9,11},{10,... | collective-permute-start | bytes 368648 | tf_op jit(solution)/shard_map/ppermute | solution.py:44
  15.2 6.0 %collective-permute-start.3 = (bf16[57,16,128]{2,1,0:T(8,128)(2,1)S(1)}, bf16[57,16,128]{2,1,0:T(8,128)(2,1)S(1)}, u32[]{:S(2)}, u32[]{:S(2)}) collective-permute-start(bf16[57,16,128]{2,1,0:T(8,128)(2,1)S(1)} %get-tuple-element.53), channel_id=1, source_target_pairs={{4,8},{8,4},{5,9},{9,5},{6,10},{10,6},{7,11},{11,7},{20,24},{24,20... | collective-permute-start | bytes 700424 | tf_op jit(solution)/shard_map/ppermute | solution.py:63
  15.8 7.3 %collective-permute-start.5 = (bf16[1,4,14,16,128]{4,3,2,1,0:T(8,128)(2,1)S(1)}, bf16[1,4,14,16,128]{4,3,2,1,0:T(8,128)(2,1)S(1)}, u32[]{:S(2)}, u32[]{:S(2)}) collective-permute-start(bf16[1,4,14,16,128]{4,3,2,1,0:T(8,128)(2,1)S(1)} %bitcast.35), channel_id=1, source_target_pairs={{0,16},{16,0},{1,17},{17,1},{2,18},{18,2},{3,19},{19,3},{4,20},{20... | collective-permute-start | bytes 688136 | tf_op jit(solution)/shard_map/ppermute | solution.py:94
  17.5 3.7 %collective-permute-start.4 = (bf16[55,16,128]{2,1,0:T(8,128)(2,1)S(1)}, bf16[55,16,128]{2,1,0:T(8,128)(2,1)S(1)}, u32[]{:S(2)}, u32[]{:S(2)}) collective-permute-start(bf16[55,16,128]{2,1,0:T(8,128)(2,1)S(1)} %get-tuple-element.54), channel_id=1, source_target_pairs={{0,4},{4,0},{8,12},{12,8},{1,5},{5,1},{9,13},{13,9},{2,6},{6,2},{1... | collective-permute-start | bytes 675848 | tf_op jit(solution)/shard_map/ppermute | solution.py:63
  23.1 12.5 %copy-start.3 = (f32[128]{0:T(128)S(1)}, f32[128]{0:T(128)}, u32[]{:S(2)}) copy-start(f32[128]{0:T(128)} %param.10) | copy-start | bytes 1540
  23.1 12.5 %copy-start.4 = (f32[128]{0:T(128)S(1)}, f32[128]{0:T(128)}, u32[]{:S(2)}) copy-start(f32[128]{0:T(128)} %param.11) | copy-start | bytes 1540
  23.2 12.2 %collective-permute-start.6 = (bf16[2,3,14,16,128]{4,3,2,1,0:T(8,128)(2,1)S(1)}, bf16[2,3,14,16,128]{4,3,2,1,0:T(8,128)(2,1)S(1)}, u32[]{:S(2)}, u32[]{:S(2)}) collective-permute-start(bf16[2,3,14,16,128]{4,3,2,1,0:T(8,128)(2,1)S(1)} %bitcast.27), channel_id=1, source_target_pairs={{0,8},{4,12},{8,0},{12,4},{1,9},{5,13},{9,1},{13,5},{2,10},{6,14},... | collective-permute-start | bytes 1032200 | tf_op jit(solution)/shard_map/ppermute | solution.py:94
  35.4 5.8 %collective-permute-start.7 = (bf16[4,3,14,16,128]{4,3,2,1,0:T(8,128)(2,1)S(1)}, bf16[4,3,14,16,128]{4,3,2,1,0:T(8,128)(2,1)S(1)}, u32[]{:S(2)}, u32[]{:S(2)}) collective-permute-start(bf16[4,3,14,16,128]{4,3,2,1,0:T(8,128)(2,1)S(1)} %bitcast.24), channel_id=1, source_target_pairs={{0,4},{4,0},{8,12},{12,8},{1,5},{5,1},{9,13},{13,9},{2,6},{6,2},{1... | collective-permute-start | bytes 2064392 | tf_op jit(solution)/shard_map/ppermute | solution.py:94
  36.8 6.0 %collective-permute-start.10 = (f32[16,128]{1,0:T(8,128)S(1)}, f32[16,128]{1,0:T(8,128)S(1)}, u32[]{:S(2)}, u32[]{:S(2)}) collective-permute-start(f32[16,128]{1,0:T(8,128)S(1)} %bitcast.49), channel_id=1, source_target_pairs={{0,3},{1,2},{2,1},{3,0},{4,7},{5,6},{6,5},{7,4},{8,11},{9,10},{10,... | collective-permute-start | bytes 24584 | tf_op jit(solution)/shard_map/ppermute | solution.py:46
  37.4 5.4 %collective-permute-start.8 = (bf16[80,128]{1,0:T(8,128)(2,1)S(1)}, bf16[80,128]{1,0:T(8,128)(2,1)S(1)}, u32[]{:S(2)}, u32[]{:S(2)}) collective-permute-start(bf16[80,128]{1,0:T(8,128)(2,1)S(1)} %bitcast.48), channel_id=1, source_target_pairs={{0,2},{1,3},{2,0},{3,1},{4,6},{5,7},{6,4},{7,5},{8,10},{9,11},{10,... | collective-permute-start | bytes 61448 | tf_op jit(solution)/shard_map/ppermute | solution.py:44
  38.8 4.2 %collective-permute-start.9 = (bf16[80,128]{1,0:T(8,128)(2,1)S(1)}, bf16[80,128]{1,0:T(8,128)(2,1)S(1)}, u32[]{:S(2)}, u32[]{:S(2)}) collective-permute-start(bf16[80,128]{1,0:T(8,128)(2,1)S(1)} %bitcast.47), channel_id=1, source_target_pairs={{0,1},{1,0},{2,3},{3,2},{4,5},{5,4},{6,7},{7,6},{8,9},{9,8},{10,11... | collective-permute-start | bytes 61448 | tf_op jit(solution)/shard_map/ppermute | solution.py:45
  42.8 11.0 %copy-start = (bf16[256,128]{1,0:T(8,128)(2,1)S(1)}, bf16[256,128]{1,0:T(8,128)(2,1)}, u32[]{:S(2)}) copy-start(bf16[256,128]{1,0:T(8,128)(2,1)} %up.1) | copy-start | bytes 196612
  42.8 11.0 %copy-start.1 = (f32[256]{0:T(256)S(1)}, f32[256]{0:T(256)}, u32[]{:S(2)}) copy-start(f32[256]{0:T(256)} %param.13) | copy-start | bytes 3076
  42.8 11.0 %copy-start.2 = (f32[256]{0:T(256)S(1)}, f32[256]{0:T(256)}, u32[]{:S(2)}) copy-start(f32[256]{0:T(256)} %param.14) | copy-start | bytes 3076

commit v18 on v17

--- a/solution.py
+++ b/solution.py
@@ -364,68 +364,77 @@
     stats[8:16] = spread
 
 
-def end_kernel(ny, nx, *refs):
-    x, inner_stats, partial, outer_face, inner_face, taps, pairs, act, stats, faces, grid, column = refs
+def add_face(ny, nx, behind, face, x, taps, pairs, ends, three, grid, column):
     edge = x.shape[2]
     wide_face = edge + ny + nx
     f32 = jnp.float32
-    odd = lax.axis_index("gz") % 2 == 1
-    size = inner_face.shape[0]
-    faces[0] = jnp.where(odd, inner_face[...], outer_face[0:size])
-    faces[1] = jnp.where(odd, outer_face[0:size], inner_face[...])
     above, left = Square().low_sides()
+    end = pl.ds(jnp.where(behind, 3, 0), 3)
+    three[...] = ends[end]
     blank = jnp.zeros(grid.shape[:1] + grid.shape[2:], grid.dtype)
     grid[:, 0] = blank
     grid[:, edge + 1] = blank
-    gap = jnp.zeros((2, edge, 128), grid.dtype)
-    for side, halo_at, own_at, plane, at, beyond, own, beside, dz in (
-        (0, 0, 3, 1, 0, 0, 2, 2, 0),
-        (1, 1, 0, edge, 3, 4, 3, 1, 2),
-    ):
-        for k in range(3):
-            begin = k * wide_face
-            grid[halo_at + k, 1 : edge + 1] = faces[side, begin : begin + edge]
-        grid[own_at, 1 : edge + 1] = x[plane, 1 : edge + 1]
-
-        def put(z, new):
-            act[beyond + z : beyond + z + new.shape[0]] = new
-
-        convolve(grid, 2, taps, pairs, put)
-        stacked = jnp.concatenate(
-            [grid[beside, dy : dy + edge].reshape(edge * edge, 128) for dy in range(3)], axis=1
-        )
-        wide = jnp.dot(stacked, taps[dz * 384 : dz * 384 + 384, :], preferred_element_type=f32)
-        own_part = partial[1 if side == 0 else 2]
-        act[own] = own_part + join_x(wide.reshape(edge, edge, 384), edge)
-        near = 1 if side == 0 else 4
-        act[near] += partial[0 if side == 0 else 3]
-
-        def rim(row):
-            planes = [faces[side, k * wide_face + edge + row] for k in range(3)]
-            return jnp.stack(planes)
-
-        three = act.at[at : at + 3]
+    first = jnp.where(behind, 1, 0)
+    for k in range(3):
+        grid[first + k, 1 : edge + 1] = face[k * wide_face : k * wide_face + edge]
+    grid[jnp.where(behind, 0, 3), 1 : edge + 1] = x[jnp.where(behind, edge, 1), 1 : edge + 1]
+
+    def put(z, new):
+        three[pl.ds(first + z, new.shape[0])] += new
+
+    convolve(grid, 2, taps, pairs, put)
+    beside = jnp.where(behind, 1, 2)
+    lines = [grid[beside, dy : dy + edge].reshape(edge * edge, 128) for dy in range(3)]
+    rows = taps[pl.ds(pl.multiple_of(jnp.where(behind, 768, 0), 128), 384), :]
+    wide = jnp.dot(jnp.concatenate(lines, axis=1), rows, preferred_element_type=f32)
+    three[jnp.where(behind, 0, 2)] += join_x(wide.reshape(edge, edge, 384), edge)
+
+    def five(voxels):
+        gap = jnp.zeros((2,) + voxels.shape[1:], voxels.dtype)
+        return jnp.where(
+            behind,
+            jnp.concatenate([gap, voxels], axis=0),
+            jnp.concatenate([voxels, gap], axis=0),
+        )
+
+    def rim(row):
+        return five(jnp.stack([face[k * wide_face + edge + row] for k in range(3)]).astype(f32))
+
+    for i in range(ny):
+        terms = y_terms(rim(i).astype(jnp.bfloat16), above[i], taps)
+        three[:, jnp.where(above[i], 0, edge - 1)] += terms
+    for j in range(nx):
+        column[...] = jnp.zeros(column.shape, f32)
+        tails = []
         for i in range(ny):
-            line = [rim(i), gap] if side == 0 else [gap, rim(i)]
-            three[:, jnp.where(above[i], 0, edge - 1)] += y_terms(
-                jnp.concatenate(line, axis=0), above[i], taps
-            )
-        for j in range(nx):
-            column[...] = jnp.zeros(column.shape, f32)
-            ends = []
-            for i in range(ny):
-                tile = faces[side, 3 * wide_face + i * nx + j].astype(f32)
-                ends.append(tile[edge - 3 :] if side == 0 else tile[:3])
-            fill_column(column, 0 if side == 0 else 2, rim(ny + j), ends, above)
-            add_column(three, x_terms(column, taps), j, nx, left[j])
-
+            tile = face[3 * wide_face + i * nx + j].astype(f32)
+            tails.append(five(jnp.where(behind, tile[:3], tile[edge - 3 :])))
+        fill_column(column, 0, rim(ny + j), tails, above)
+        add_column(three, x_terms(column, taps), j, nx, left[j])
+    ends[end] = three[...]
+
+
+def inner_kernel(ny, nx, x, partial, face, taps, pairs, ends, three, grid, column):
+    blank = jnp.zeros(ends.shape[1:], jnp.float32)
+    ends[0] = blank
+    ends[1:5] = partial[...]
+    ends[5] = blank
+    behind = lax.axis_index("gz") % 2 == 0
+    add_face(ny, nx, behind, face, x, taps, pairs, ends, three, grid, column)
+
+
+def outer_kernel(ny, nx, x, middle_stats, ends, face, taps, pairs, act, stats, three, grid, column):
+    edge = x.shape[2]
+    act[...] = ends[...]
+    behind = lax.axis_index("gz") % 2 == 1
+    add_face(ny, nx, behind, face, x, taps, pairs, act, three, grid, column)
     mean, spread = moments(act.at[2:4])
     few, many = edge * edge // 4, (edge - 2) * edge * edge // 8
-    inner_mean, inner_spread = inner_stats[0:8], inner_stats[8:16]
-    off = inner_mean - mean
-    share_of = few / (few + many)
-    spread = spread + inner_spread + (many * share_of) * (off * off)
-    put_stats(stats, inner_mean - share_of * off, spread, few + many)
+    middle_mean, middle_spread = middle_stats[0:8], middle_stats[8:16]
+    off = middle_mean - mean
+    part = few / (few + many)
+    spread = spread + middle_spread + (many * part) * (off * off)
+    put_stats(stats, middle_mean - part * off, spread, few + many)
 
 
 def merge(mean, spread, rows, other_mean, other_spread):
@@ -767,19 +776,22 @@
         corner,
         taps,
     )
+    room = [
+        ((3, edge, edge, channels), f32),
+        ((4, edge + 2, edge, channels), bf16),
+        ((5,) + column, f32),
+    ]
+    (ends,) = call(
+        functools.partial(inner_kernel, ny, nx), [six], room, field, partial, inner, taps, pairs
+    )
     ends, stats = call(
-        functools.partial(end_kernel, ny, nx),
+        functools.partial(outer_kernel, ny, nx),
         [six, ((devices, 2, channels), f32)],
-        [
-            ((2,) + face[0], bf16),
-            ((4, edge + 2, edge, channels), bf16),
-            ((5,) + column, f32),
-        ],
+        room,
         field,
         stats,
-        partial,
+        ends,
         outer,
-        inner,
         taps,
         pairs,
     )

time: 55.5 us -> 54.8 us (0.987)
  starting transfers between devices: 18.3 us -> 17.1 us
    ppermute x3, starting transfers between devices: 4.78 us -> 3.64 us  [swap(): lax.ppermute(block, axis, [(i, i ^ mask) for i in range(lax.axis_size(axi...]
    pallas_call x9 -> x10, Pallas kernels: 14.2 us -> 14.6 us  [call(): pl.pallas_call(kernel, out_shape=[jax.ShapeDtypeStruct(shape, dtype) for...]
  transfers between devices with their start and end apart: 11 -> 11, of which waited for: 4 -> 4; matrix products, arithmetic and copies ran while one was open for 0% -> 0% of each run, Pallas kernels for 19% -> 20%
where the time goes in v18:
time: 54.8 us; the launch traced here: 54.5 us
  blocking collectives  19.2 us (35%)
  starting transfers between devices  17.1 us (31%)
  Pallas kernels  14.7 us (27%)
  waiting for transfers between devices  3.25 us (6%)
    all_to_all x2, blocking collectives, share(): return lax.all_to_all(stats, PART, 0, 0)  19.2 us
    pallas_call x10, Pallas kernels, call(): pl.pallas_call(kernel, out_shape=[jax.ShapeDtypeStruct(shape, dtype) for...  14.6 us
    ppermute x2, starting transfers between devices, halos(): corner = lax.ppermute(corners[0], 'yx', self.swap_route(3))  6.03 us
    ppermute x3, starting transfers between devices, swap(): lax.ppermute(block, axis, [(i, i ^ mask) for i in range(lax.axis_size(axi...  3.64 us
    ppermute x1, starting transfers between devices, swap_depth(): lax.ppermute(inner, 'gz', routes[0])  2.56 us
    ppermute x2, starting transfers between devices, halos(): x = lax.ppermute(x_edges[0], 'yx', self.swap_route(1))  2.42 us
    ppermute x2, starting transfers between devices, halos(): y = lax.ppermute(y_edges[0], 'yx', self.swap_route(2))  1.8 us
    ppermute x2, waiting for transfers between devices, halos(): y = lax.ppermute(y_edges[0], 'yx', self.swap_route(2))  1.59 us
  transfers between devices with their start and end apart: 11, of which 4 were waited for; matrix products, arithmetic and copies ran while one was open for 0% of the time, Pallas kernels for 20%

profile of v18, /device:TPU:0, one launch (start us, length us, event | category | flops | bytes accessed | tf_op | source)
XLA Modules:
  0.0 54.5 jit_solution(11859341147724359834)
XLA Ops:
  0.0 1.6 %shard_map.82 = (bf16[1,30,16,128]{3,2,1,0:T(8,128)(2,1)S(1)}, bf16[1,30,16,128]{3,2,1,0:T(8,128)(2,1)S(1)}, bf16[1,15,16,128]{3,2,1,0:T(8,128)(2,1)S(1)}, bf16[...) custom-call(bf16[16,16,16,128]{3,2,1,0:T(8,128)(2,1)} %x_in.1, bf16[27,128,128]{2,1,0:T(8,128)(2,1)} %bitcast.50, ...), custom_call_target="tpu_custom_call" | custom-call | bytes 5242880 | tf_op jit(solution)/shard_map/pallas_call | solution.py:105
  1.6 5.1 %collective-permute-start.2 = (bf16[15,16,128]{2,1,0:T(8,128)(2,1)S(1)}, bf16[15,16,128]{2,1,0:T(8,128)(2,1)S(1)}, u32[]{:S(2)}, u32[]{:S(2)}) collective-permute-start(bf16[15,16,128]{2,1,0:T(8,128)(2,1)S(1)} %bitcast.46), channel_id=1, source_target_pairs={{0,3},{1,2},{2,1},{3,0},{4,7},{5,6},{6,5},{7,4},{8,11},{9,10},{10,... | collective-permute-start | bytes 184328 | tf_op jit(solution)/shard_map/ppermute | solution.py:46
  6.7 0.0 collective-permute-start.1
  6.7 0.6 %collective-permute-start = (bf16[30,16,128]{2,1,0:T(8,128)(2,1)S(1)}, bf16[30,16,128]{2,1,0:T(8,128)(2,1)S(1)}, u32[]{:S(2)}, u32[]{:S(2)}) collective-permute-start(bf16[30,16,128]{2,1,0:T(8,128)(2,1)S(1)} %bitcast.44), channel_id=1, source_target_pairs={{0,2},{1,3},{2,0},{3,1},{4,6},{5,7},{6,4},{7,5},{8,10},{9,11},{10,... | collective-permute-start | bytes 368648 | tf_op jit(solution)/shard_map/ppermute | solution.py:44
  7.4 4.7 %shard_map.83 = (f32[16,16,16,128]{3,2,1,0:T(8,128)S(1)}, bf16[1152,384]{1,0:T(8,128)(2,1)S(1)}, bf16[1536,256]{1,0:T(8,128)(2,1)S(1)}, bf16[108,16,128]{2,1,0:T(8,128)(2,1)S(1)}) custom-call(bf16[108,16,128]{2,1,0:T(8,128)(2,1)} %bitcast.52, bf16[18,18,16,128]{3,2,1,0:T(8,128)(2,1)S(1)} %get-tuple-element.42.x, ...), custom_call_target="tpu_custom_call" | custom-call | flops 3623878656 | bytes 6291456 | tf_op jit(solution)/shard_map/pallas_call | solution.py:105
  12.1 0.0 collective-permute-done.2
  12.1 1.4 %collective-permute-done.1 = bf16[30,16,128]{2,1,0:T(8,128)(2,1)S(1)} collective-permute-done((bf16[30,16,128]{2,1,0:T(8,128)(2,1)S(1)}, bf16[30,16,128]{2,1,0:T(8,128)(2,1)S(1)}, u32[]{:S(2)}, u32[]{:S(2)}) %collective-permute-start.1) | collective-permute-done | bytes 122912 | tf_op jit(solution)/shard_map/ppermute | solution.py:45
  13.5 1.6 %collective-permute-done = bf16[30,16,128]{2,1,0:T(8,128)(2,1)S(1)} collective-permute-done((bf16[30,16,128]{2,1,0:T(8,128)(2,1)S(1)}, bf16[30,16,128]{2,1,0:T(8,128)(2,1)S(1)}, u32[]{:S(2)}, u32[]{:S(2)}) %collective-permute-start) | collective-permute-done | bytes 122912 | tf_op jit(solution)/shard_map/ppermute | solution.py:44
  15.1 0.1 shard_map.85
  15.2 0.7 %collective-permute-start.4 = (bf16[57,16,128]{2,1,0:T(8,128)(2,1)S(1)}, bf16[57,16,128]{2,1,0:T(8,128)(2,1)S(1)}, u32[]{:S(2)}, u32[]{:S(2)}) collective-permute-start(bf16[57,16,128]{2,1,0:T(8,128)(2,1)S(1)} %get-tuple-element.55), channel_id=1, source_target_pairs={{4,8},{8,4},{5,9},{9,5},{6,10},{10,6},{7,11},{11,7},{20,24},{24,20... | collective-permute-start | bytes 700424 | tf_op jit(solution)/shard_map/ppermute | solution.py:63
  15.8 1.6 %collective-permute-start.5 = (bf16[1,4,14,16,128]{4,3,2,1,0:T(8,128)(2,1)S(1)}, bf16[1,4,14,16,128]{4,3,2,1,0:T(8,128)(2,1)S(1)}, u32[]{:S(2)}, u32[]{:S(2)}) collective-permute-start(bf16[1,4,14,16,128]{4,3,2,1,0:T(8,128)(2,1)S(1)} %bitcast.35), channel_id=1, source_target_pairs={{0,16},{16,0},{1,17},{17,1},{2,18},{18,2},{3,19},{19,3},{4,20},{20... | collective-permute-start | bytes 688136 | tf_op jit(solution)/shard_map/ppermute | solution.py:94
  17.5 2.6 %collective-permute-start.3 = (bf16[55,16,128]{2,1,0:T(8,128)(2,1)S(1)}, bf16[55,16,128]{2,1,0:T(8,128)(2,1)S(1)}, u32[]{:S(2)}, u32[]{:S(2)}) collective-permute-start(bf16[55,16,128]{2,1,0:T(8,128)(2,1)S(1)} %get-tuple-element.53), channel_id=1, source_target_pairs={{0,4},{4,0},{8,12},{12,8},{1,5},{5,1},{9,13},{13,9},{2,6},{6,2},{1... | collective-permute-start | bytes 675848 | tf_op jit(solution)/shard_map/ppermute | solution.py:63
  20.0 1.0 %shard_map.84 = (f32[14,16,16,128]{3,2,1,0:T(8,128)S(1)}, f32[4,16,16,128]{3,2,1,0:T(8,128)S(1)}, f32[16,128]{1,0:T(8,128)S(1)}) custom-call(f32[16,16,16,128]{3,2,1,0:T(8,128)S(1)} %get-tuple-element.45.own, bf16[1,30,16,128]{3,2,1,0:T(8,128)(2,1)S(1)} %bitcast.32, bf16[1,30,16,128]{3,2,1,0:T(8,128)(2,1)S(1)} %bitcast.30, ...), custom_call_target="tpu_custom_call" | custom-call | tf_op jit(solution)/shard_map/pallas_call | solution.py:105
  21.1 0.1 collective-permute-done.3.face
  21.1 1.1 %shard_map.86.ends = f32[6,16,16,128]{3,2,1,0:T(8,128)S(1)} custom-call(bf16[18,18,16,128]{3,2,1,0:T(8,128)(2,1)S(1)} %get-tuple-element.42.x, f32[4,16,16,128]{3,2,1,0:T(8,128)S(1)} %get-tuple-element.52.partial, bf16[55,16,128]{2,1,0:T(8,128)(2,1)S(1)} %collective-permute-done.3.face, bf16[1152,384]{1,0:T(8,128)(2,1)S(1)} %get-tuple-element.49.taps, ...), custom_call_target="tpu_custom_call" | custom-call | tf_op jit(solution)/shard_map/pallas_call | solution.py:105
  22.3 0.0 collective-permute-done.4.face
  22.3 1.2 %shard_map.87 = (f32[6,16,16,128]{3,2,1,0:T(8,128)S(1)}, f32[16,2,128]{2,1,0:T(2,128)S(1)}) custom-call(bf16[18,18,16,128]{3,2,1,0:T(8,128)(2,1)S(1)} %get-tuple-element.42.x, f32[16,128]{1,0:T(8,128)S(1)} %get-tuple-element.51.middle_stats, f32[6,16,16,128]{3,2,1,0:T(8,128)S(1)} %shard_map.86.ends, bf16[57,16,128]{2,1,0:T(8,128)(2,1)S(1)} %collective-permute-done.4.face, ...), custom_call_target="tpu_custom_call" | custom-call | tf_op jit(solution)/shard_map/pallas_call | solution.py:105
  23.5 0.0 copy-start.3
  23.5 0.0 copy-start.4
  23.5 0.0 collective-permute-done.5.refs_1_
  23.6 1.9 %collective-permute-start.6 = (bf16[2,3,14,16,128]{4,3,2,1,0:T(8,128)(2,1)S(1)}, bf16[2,3,14,16,128]{4,3,2,1,0:T(8,128)(2,1)S(1)}, u32[]{:S(2)}, u32[]{:S(2)}) collective-permute-start(bf16[2,3,14,16,128]{4,3,2,1,0:T(8,128)(2,1)S(1)} %bitcast.27), channel_id=1, source_target_pairs={{0,8},{4,12},{8,0},{12,4},{1,9},{5,13},{9,1},{13,5},{2,10},{6,14},... | collective-permute-start | bytes 1032200 | tf_op jit(solution)/shard_map/ppermute | solution.py:94
  25.4 9.2 %all_to_all.10.stats = f32[16,2,128]{2,1,0:T(2,128)S(1)} all-to-all(f32[16,2,128]{2,1,0:T(2,128)S(1)} %get-tuple-element.59), channel_id=1, replica_groups=mesh['cand'=2,'gz'=4,'yx'=4] {'gz','yx'}, dimensions={0} | all-to-all | bytes 32768 | tf_op jit(solution)/shard_map/all_to_all | solution.py:98
  34.6 0.0 collective-permute-done.6.refs_1_
  34.7 0.2 collective-permute-start.7
  34.8 0.0 copy-done.3
  34.8 0.0 copy-done.4
  34.8 1.1 %shard_map.89 = (bf16[16,16,16,128]{3,2,1,0:T(8,128)(2,1)S(1)}, f32[10,8,8,128]{3,2,1,0:T(8,128)S(1)}, bf16[1,80,128]{2,1,0:T(8,128)(2,1)S(1)}, bf16[1,80,128]{2,1,0:T(8,128)(2,1)S(1)}, f32[1,16,128]{2,1,0:T(8,128)S(1)}) custom-call(f32[14,16,16,128]{3,2,1,0:T(8,128)S(1)} %get-tuple-element.50.inner, f32[6,16,16,128]{3,2,1,0:T(8,128)S(1)} %get-tuple-element.56.ends, ...), custom_call_target="tpu_custom_call" | custom-call | flops 10485760 | bytes 3145728 | tf_op jit(solution)/shard_map/pallas_call | solution.py:105
  36.0 0.9 %collective-permute-start.10 = (f32[16,128]{1,0:T(8,128)S(1)}, f32[16,128]{1,0:T(8,128)S(1)}, u32[]{:S(2)}, u32[]{:S(2)}) collective-permute-start(f32[16,128]{1,0:T(8,128)S(1)} %bitcast.49), channel_id=1, source_target_pairs={{0,3},{1,2},{2,1},{3,0},{4,7},{5,6},{6,5},{7,4},{8,11},{9,10},{10,... | collective-permute-start | bytes 24584 | tf_op jit(solution)/shard_map/ppermute | solution.py:46
  36.9 1.2 %collective-permute-start.8 = (bf16[80,128]{1,0:T(8,128)(2,1)S(1)}, bf16[80,128]{1,0:T(8,128)(2,1)S(1)}, u32[]{:S(2)}, u32[]{:S(2)}) collective-permute-start(bf16[80,128]{1,0:T(8,128)(2,1)S(1)} %bitcast.48), channel_id=1, source_target_pairs={{0,2},{1,3},{2,0},{3,1},{4,6},{5,7},{6,4},{7,5},{8,10},{9,11},{10,... | collective-permute-start | bytes 61448 | tf_op jit(solution)/shard_map/ppermute | solution.py:44
  38.1 2.4 %collective-permute-start.9 = (bf16[80,128]{1,0:T(8,128)(2,1)S(1)}, bf16[80,128]{1,0:T(8,128)(2,1)S(1)}, u32[]{:S(2)}, u32[]{:S(2)}) collective-permute-start(bf16[80,128]{1,0:T(8,128)(2,1)S(1)} %bitcast.47), channel_id=1, source_target_pairs={{0,1},{1,0},{2,3},{3,2},{4,5},{5,4},{6,7},{7,6},{8,9},{9,8},{10,11... | collective-permute-start | bytes 61448 | tf_op jit(solution)/shard_map/ppermute | solution.py:45
  40.5 0.0 collective-permute-done.7.refs_1_
  40.5 0.1 shard_map.91
  40.6 1.4 %shard_map.92 = (f32[2,512,128]{2,1,0:T(8,128)S(1)}, bf16[4,108,16,128]{3,2,1,0:T(8,128)(2,1)S(1)}) custom-call(f32[10,8,8,128]{3,2,1,0:T(8,128)S(1)} %get-tuple-element.62.pooled, bf16[108,16,128]{2,1,0:T(8,128)(2,1)S(1)} %get-tuple-element.63.own, bf16[8,3,14,16,128]{4,3,2,1,0:T(8,128)(2,1)S(1)} %bitcast.26), custom_call_target="tpu_custom_call" | custom-call | flops 905969664 | bytes 4194304 | tf_op jit(solution)/shard_map/pallas_call | solution.py:105
  42.0 0.0 copy-start
  42.0 0.0 copy-start.1
  42.0 0.0 copy-start.2
  42.0 0.0 collective-permute-done.10
  42.0 0.0 collective-permute-done.8
  42.1 0.2 collective-permute-done.9
  42.2 0.7 %shard_map.93 = (f32[2,512,128]{2,1,0:T(8,128)S(1)}, f32[16,2,256]{2,1,0:T(2,128)S(1)}) custom-call(f32[2,512,128]{2,1,0:T(8,128)S(1)} %get-tuple-element.65.own, bf16[1,80,128]{2,1,0:T(8,128)(2,1)S(1)} %bitcast.37, bf16[1,80,128]{2,1,0:T(8,128)(2,1)S(1)} %bitcast.38, f32[1,16,128]{2,1,0:T(8,128)S(1)} %bitcast.39, ...), custom_call_target="tpu_custom_call" | custom-call | flops 67108864 | bytes 3145728 | tf_op jit(solution)/shard_map/pallas_call | solution.py:105
  42.9 10.0 %all_to_all.11.stats = f32[16,2,256]{2,1,0:T(2,128)S(1)} all-to-all(f32[16,2,256]{2,1,0:T(2,128)S(1)} %get-tuple-element.71), channel_id=1, replica_groups=mesh['cand'=2,'gz'=4,'yx'=4] {'gz','yx'}, dimensions={0} | all-to-all | bytes 65536 | tf_op jit(solution)/shard_map/all_to_all | solution.py:98
  53.0 0.0 copy-done
  53.0 0.0 copy-done.1
  53.0 0.0 copy-done.2
  53.0 1.5 %shard_map.94 = bf16[16,16,16,128]{3,2,1,0:T(8,128)(2,1)} custom-call(f32[2,512,128]{2,1,0:T(8,128)S(1)} %get-tuple-element.70.act, f32[16,2,256]{2,1,0:T(2,128)S(1)} %all_to_all.11.stats, f32[1,256]{1,0:T(1,128)S(1)} %bitcast.40, f32[1,256]{1,0:T(1,128)S(1)} %bitcast.41, bf16[256,128]{1,0:T(8,128)(2,1)S(1)} %copy-done, ...), custom_call_target="tpu_custom_call" | custom-call | flops 67108864 | bytes 3145728 | tf_op jit(solution)/shard_map/pallas_call | solution.py:105
  (2 shorter events, 0.1 us)
Async XLA Ops:
  1.6 10.5 %collective-permute-start.2 = (bf16[15,16,128]{2,1,0:T(8,128)(2,1)S(1)}, bf16[15,16,128]{2,1,0:T(8,128)(2,1)S(1)}, u32[]{:S(2)}, u32[]{:S(2)}) collective-permute-start(bf16[15,16,128]{2,1,0:T(8,128)(2,1)S(1)} %bitcast.46), channel_id=1, source_target_pairs={{0,3},{1,2},{2,1},{3,0},{4,7},{5,6},{6,5},{7,4},{8,11},{9,10},{10,... | collective-permute-start | bytes 184328 | tf_op jit(solution)/shard_map/ppermute | solution.py:46
  6.7 6.8 %collective-permute-start.1 = (bf16[30,16,128]{2,1,0:T(8,128)(2,1)S(1)}, bf16[30,16,128]{2,1,0:T(8,128)(2,1)S(1)}, u32[]{:S(2)}, u32[]{:S(2)}) collective-permute-start(bf16[30,16,128]{2,1,0:T(8,128)(2,1)S(1)} %bitcast.45), channel_id=1, source_target_pairs={{0,1},{1,0},{2,3},{3,2},{4,5},{5,4},{6,7},{7,6},{8,9},{9,8},{10,11... | collective-permute-start | bytes 368648 | tf_op jit(solution)/shard_map/ppermute | solution.py:45
  6.7 8.4 %collective-permute-start = (bf16[30,16,128]{2,1,0:T(8,128)(2,1)S(1)}, bf16[30,16,128]{2,1,0:T(8,128)(2,1)S(1)}, u32[]{:S(2)}, u32[]{:S(2)}) collective-permute-start(bf16[30,16,128]{2,1,0:T(8,128)(2,1)S(1)} %bitcast.44), channel_id=1, source_target_pairs={{0,2},{1,3},{2,0},{3,1},{4,6},{5,7},{6,4},{7,5},{8,10},{9,11},{10,... | collective-permute-start | bytes 368648 | tf_op jit(solution)/shard_map/ppermute | solution.py:44
  15.2 7.1 %collective-permute-start.4 = (bf16[57,16,128]{2,1,0:T(8,128)(2,1)S(1)}, bf16[57,16,128]{2,1,0:T(8,128)(2,1)S(1)}, u32[]{:S(2)}, u32[]{:S(2)}) collective-permute-start(bf16[57,16,128]{2,1,0:T(8,128)(2,1)S(1)} %get-tuple-element.55), channel_id=1, source_target_pairs={{4,8},{8,4},{5,9},{9,5},{6,10},{10,6},{7,11},{11,7},{20,24},{24,20... | collective-permute-start | bytes 700424 | tf_op jit(solution)/shard_map/ppermute | solution.py:63
  15.8 7.7 %collective-permute-start.5 = (bf16[1,4,14,16,128]{4,3,2,1,0:T(8,128)(2,1)S(1)}, bf16[1,4,14,16,128]{4,3,2,1,0:T(8,128)(2,1)S(1)}, u32[]{:S(2)}, u32[]{:S(2)}) collective-permute-start(bf16[1,4,14,16,128]{4,3,2,1,0:T(8,128)(2,1)S(1)} %bitcast.35), channel_id=1, source_target_pairs={{0,16},{16,0},{1,17},{17,1},{2,18},{18,2},{3,19},{19,3},{4,20},{20... | collective-permute-start | bytes 688136 | tf_op jit(solution)/shard_map/ppermute | solution.py:94
  17.5 3.7 %collective-permute-start.3 = (bf16[55,16,128]{2,1,0:T(8,128)(2,1)S(1)}, bf16[55,16,128]{2,1,0:T(8,128)(2,1)S(1)}, u32[]{:S(2)}, u32[]{:S(2)}) collective-permute-start(bf16[55,16,128]{2,1,0:T(8,128)(2,1)S(1)} %get-tuple-element.53), channel_id=1, source_target_pairs={{0,4},{4,0},{8,12},{12,8},{1,5},{5,1},{9,13},{13,9},{2,6},{6,2},{1... | collective-permute-start | bytes 675848 | tf_op jit(solution)/shard_map/ppermute | solution.py:63
  23.5 11.3 %copy-start.3 = (f32[128]{0:T(128)S(1)}, f32[128]{0:T(128)}, u32[]{:S(2)}) copy-start(f32[128]{0:T(128)} %param.10) | copy-start | bytes 1540
  23.5 11.3 %copy-start.4 = (f32[128]{0:T(128)S(1)}, f32[128]{0:T(128)}, u32[]{:S(2)}) copy-start(f32[128]{0:T(128)} %param.11) | copy-start | bytes 1540
  23.6 11.0 %collective-permute-start.6 = (bf16[2,3,14,16,128]{4,3,2,1,0:T(8,128)(2,1)S(1)}, bf16[2,3,14,16,128]{4,3,2,1,0:T(8,128)(2,1)S(1)}, u32[]{:S(2)}, u32[]{:S(2)}) collective-permute-start(bf16[2,3,14,16,128]{4,3,2,1,0:T(8,128)(2,1)S(1)} %bitcast.27), channel_id=1, source_target_pairs={{0,8},{4,12},{8,0},{12,4},{1,9},{5,13},{9,1},{13,5},{2,10},{6,14},... | collective-permute-start | bytes 1032200 | tf_op jit(solution)/shard_map/ppermute | solution.py:94
  34.7 5.8 %collective-permute-start.7 = (bf16[4,3,14,16,128]{4,3,2,1,0:T(8,128)(2,1)S(1)}, bf16[4,3,14,16,128]{4,3,2,1,0:T(8,128)(2,1)S(1)}, u32[]{:S(2)}, u32[]{:S(2)}) collective-permute-start(bf16[4,3,14,16,128]{4,3,2,1,0:T(8,128)(2,1)S(1)} %bitcast.24), channel_id=1, source_target_pairs={{0,4},{4,0},{8,12},{12,8},{1,5},{5,1},{9,13},{13,9},{2,6},{6,2},{1... | collective-permute-start | bytes 2064392 | tf_op jit(solution)/shard_map/ppermute | solution.py:94
  36.0 6.0 %collective-permute-start.10 = (f32[16,128]{1,0:T(8,128)S(1)}, f32[16,128]{1,0:T(8,128)S(1)}, u32[]{:S(2)}, u32[]{:S(2)}) collective-permute-start(f32[16,128]{1,0:T(8,128)S(1)} %bitcast.49), channel_id=1, source_target_pairs={{0,3},{1,2},{2,1},{3,0},{4,7},{5,6},{6,5},{7,4},{8,11},{9,10},{10,... | collective-permute-start | bytes 24584 | tf_op jit(solution)/shard_map/ppermute | solution.py:46
  36.9 5.1 %collective-permute-start.8 = (bf16[80,128]{1,0:T(8,128)(2,1)S(1)}, bf16[80,128]{1,0:T(8,128)(2,1)S(1)}, u32[]{:S(2)}, u32[]{:S(2)}) collective-permute-start(bf16[80,128]{1,0:T(8,128)(2,1)S(1)} %bitcast.48), channel_id=1, source_target_pairs={{0,2},{1,3},{2,0},{3,1},{4,6},{5,7},{6,4},{7,5},{8,10},{9,11},{10,... | collective-permute-start | bytes 61448 | tf_op jit(solution)/shard_map/ppermute | solution.py:44
  38.1 4.2 %collective-permute-start.9 = (bf16[80,128]{1,0:T(8,128)(2,1)S(1)}, bf16[80,128]{1,0:T(8,128)(2,1)S(1)}, u32[]{:S(2)}, u32[]{:S(2)}) collective-permute-start(bf16[80,128]{1,0:T(8,128)(2,1)S(1)} %bitcast.47), channel_id=1, source_target_pairs={{0,1},{1,0},{2,3},{3,2},{4,5},{5,4},{6,7},{7,6},{8,9},{9,8},{10,11... | collective-permute-start | bytes 61448 | tf_op jit(solution)/shard_map/ppermute | solution.py:45
  42.0 11.0 %copy-start = (bf16[256,128]{1,0:T(8,128)(2,1)S(1)}, bf16[256,128]{1,0:T(8,128)(2,1)}, u32[]{:S(2)}) copy-start(bf16[256,128]{1,0:T(8,128)(2,1)} %up.1) | copy-start | bytes 196612
  42.0 11.0 %copy-start.1 = (f32[256]{0:T(256)S(1)}, f32[256]{0:T(256)}, u32[]{:S(2)}) copy-start(f32[256]{0:T(256)} %param.13) | copy-start | bytes 3076
  42.0 11.0 %copy-start.2 = (f32[256]{0:T(256)S(1)}, f32[256]{0:T(256)}, u32[]{:S(2)}) copy-start(f32[256]{0:T(256)} %param.14) | copy-start | bytes 3076

commit v19 on v18

--- a/solution.py
+++ b/solution.py
@@ -113,10 +113,10 @@
     )(*far, *near)
 
 
-def start_kernel(ny, nx, size, x_in, w_in, d_in, y_out, x_out, corners, x, w, lines, sems):
+def start_kernel(ny, size, x_in, w_in, d_in, y_out, rider, x, w, sems):
     edge = x_in.shape[0]
-    f32, bf16 = jnp.float32, jnp.bfloat16
-    above, left = Square().low_sides()
+    bf16 = jnp.bfloat16
+    above, _ = Square().low_sides()
     chunks = 4
     planes = edge // chunks
     first = [
@@ -130,13 +130,8 @@
     later = []
     if size:
         at = jnp.minimum(Riders.mine() * size, d_in.shape[0] - size)
-        for k, (out, begin) in enumerate(((y_out, edge), (x_out, edge), (corners, 1))):
-            later.append(
-                pltpu.make_async_copy(
-                    d_in.at[pl.ds(at, size)], out.at[0, pl.ds(begin, size)], sems.at[chunks + k]
-                )
-            )
-    later.append(pltpu.make_async_copy(w_in, w, sems.at[chunks + 3]))
+        later.append(pltpu.make_async_copy(d_in.at[pl.ds(at, size)], rider, sems.at[chunks]))
+    later.append(pltpu.make_async_copy(w_in, w, sems.at[chunks + 1]))
     for copy in first + later:
         copy.start()
     x[0] = jnp.zeros(x.shape[1:], bf16)
@@ -144,20 +139,34 @@
     blank = jnp.zeros((edge,) + x.shape[2:], bf16)
     x[1 : edge + 1, 0] = blank
     x[1 : edge + 1, edge + 1] = blank
-    flat = lines.reshape(nx * edge * edge * 8, 128)
-    part = planes * edge
+    if not size:
+        rider[...] = jnp.zeros(rider.shape, bf16)
     for k in range(chunks):
         first[k].wait()
         at, here = pl.ds(k * planes, planes), pl.ds(1 + k * planes, planes)
         for i in range(ny):
-            row = jnp.where(above[i], 1, edge)
-            y_out[i, at] = x[here, row]
+            y_out[i, at] = x[here, jnp.where(above[i], 1, edge)]
+    for copy in later:
+        copy.wait()
+    if size:
+        y_out[0, edge : edge + size] = rider[...]
+
+
+def flank_kernel(ny, nx, size, x, rider, after, x_out, corners, lines):
+    del after
+    edge = x.shape[2]
+    f32, bf16 = jnp.float32, jnp.bfloat16
+    above, left = Square().low_sides()
+    flat = lines.reshape(nx * edge * edge * 8, 128)
+    planes = edge // 4
+    part = planes * edge
+    for k in range(4):
+        at, here = pl.ds(k * planes, planes), pl.ds(1 + k * planes, planes)
         for j in range(nx):
             low = x[here, 1 : edge + 1, 0:8].astype(f32).reshape(part, 8, 128)
             high = x[here, 1 : edge + 1, edge - 8 : edge].astype(f32).reshape(part, 8, 128)
             high = pltpu.roll(high, 1, 1)
-            kept = jnp.where(left[j], low, high)
-            lines[j, k * part : k * part + part] = kept
+            lines[j, k * part : k * part + part] = jnp.where(left[j], low, high)
             begin = (j * edge * edge + k * part) * 8
             column = flat[pl.ds(begin, part, stride=8), :]
             x_out[j, at] = column.astype(bf16).reshape(planes, edge, 128)
@@ -166,10 +175,10 @@
             begin = j * edge * edge * 8
             low = flat[pl.ds(begin, edge, stride=8 * edge), :]
             high = flat[pl.ds(begin + 8 * (edge - 1), edge, stride=8 * edge), :]
-            kept = jnp.where(above[i], low, high)
-            corners[i * nx + j, 0] = kept.astype(bf16)
-    for copy in later:
-        copy.wait()
+            corners[i * nx + j, 0] = jnp.where(above[i], low, high).astype(bf16)
+    if size:
+        x_out[0, edge : edge + size] = rider[...]
+        corners[0, 1 : 1 + size] = rider[...]
 
 
 def face_kernel(ny, nx, size, x, y_halos, x_halos, corners, outer, inner, *riders):
@@ -258,18 +267,27 @@
         put(z, new.reshape(planes, edge, edge, 128))
 
 
-def conv_kernel(deep_in, x, weight, act, taps, pairs, deep_weight, sem):
+def near_kernel(deep_in, x, weight, act, taps, pairs, deep_weight, sem):
     copy = pltpu.make_async_copy(deep_in, deep_weight, sem)
     copy.start()
-    edge = act.shape[0]
     spread_taps(weight, taps)
     pair_taps(weight, pairs)
 
     def put(z, new):
         act[z : z + new.shape[0]] = new
 
-    convolve(x, edge, taps, pairs, put)
+    convolve(x, act.shape[0], taps, pairs, put)
     copy.wait()
+
+
+def far_kernel(x, taps, pairs, after, act):
+    del after
+    half = act.shape[0]
+
+    def put(z, new):
+        act[z : z + new.shape[0]] = new
+
+    convolve(x.at[half : 2 * half + 2], half, taps, pairs, put)
 
 
 def y_terms(line, low, taps):
@@ -340,11 +358,13 @@
     return mean, lax.fori_loop(0, count, spread_step, zero, unroll=True)
 
 
-def side_kernel(ny, nx, own, y_halos, x_halos, corners, taps, inner, ends, stats, act, column):
-    edge = own.shape[0]
+def side_kernel(ny, nx, near, far, y_halos, x_halos, corners, taps, inner, ends, stats, act, column):
+    edge = near.shape[1]
+    half = edge // 2
     act[0] = jnp.zeros(act.shape[1:], jnp.float32)
     act[edge + 1] = jnp.zeros(act.shape[1:], jnp.float32)
-    act[1 : edge + 1] = own[...]
+    act[1 : half + 1] = near[...]
+    act[half + 1 : edge + 1] = far[...]
     above, left = Square().low_sides()
     blank = jnp.zeros((2, edge, 128), jnp.bfloat16)
     for i in range(ny):
@@ -707,28 +727,27 @@
 
     own = jnp.moveaxis(deep_weight, 4, 3).reshape(-1, 16, channels)
     conv_weight = conv_weight.reshape(27, channels, channels)
-    *edges, field, conv_weight = call(
-        functools.partial(start_kernel, ny, nx, riders.size),
+    y, rider, field, conv_weight = call(
+        functools.partial(start_kernel, ny, riders.size),
         [
             ((ny, edge + riders.size, edge, channels), bf16),
-            ((nx, edge + riders.size, edge, channels), bf16),
-            ((ny * nx, 1 + riders.size, edge, channels), bf16),
+            ((max(riders.size, 1), 16, channels), bf16),
             ((edge + 2, edge + 2, edge, channels), bf16),
             (conv_weight.shape, bf16),
         ],
-        [((nx, edge * edge, 8, channels), f32), pltpu.SemaphoreType.DMA((8,))],
+        [pltpu.SemaphoreType.DMA((6,))],
         features,
         conv_weight,
         own,
         nbytes=5 << 20,
         in_hbm=3,
     )
-    halos = square.halos(*(list(piece) for piece in edges))
+    half_act = ((deep, edge, edge, channels), f32)
     conv_flops = 54 * channels * channels * edge**3
-    act, taps, pairs, own = call(
-        conv_kernel,
+    near, taps, pairs, own = call(
+        near_kernel,
         [
-            ((edge, edge, edge, channels), f32),
+            half_act,
             ((9 * channels, 3 * channels), bf16),
             ((12 * channels, 2 * channels), bf16),
             (own.shape, bf16),
@@ -737,11 +756,35 @@
         own,
         field,
         conv_weight,
-        flops=conv_flops,
-        nbytes=6 << 20,
+        flops=conv_flops // 2,
+        nbytes=4 << 20,
         in_hbm=1,
     )
-    (y, x, corner), act = lax.optimization_barrier((halos, act))
+    x, corner = call(
+        functools.partial(flank_kernel, ny, nx, riders.size),
+        [
+            ((nx, edge + riders.size, edge, channels), bf16),
+            ((ny * nx, 1 + riders.size, edge, channels), bf16),
+        ],
+        [((nx, edge * edge, 8, channels), f32)],
+        field,
+        rider,
+        taps,
+        nbytes=2 << 20,
+    )
+    halos = square.halos(list(y), list(x), list(corner))
+    (far,) = call(
+        far_kernel,
+        [half_act],
+        [],
+        field,
+        taps,
+        pairs,
+        corner,
+        flops=conv_flops // 2,
+        nbytes=4 << 20,
+    )
+    (y, x, corner), far = lax.optimization_barrier((halos, far))
     y, x, corner = jnp.stack(y), jnp.stack(x), jnp.stack(corner)
     face = ((3 * (edge + ny + nx) + ny * nx, edge, channels), bf16)
     held = [((4, riders.size, 16, channels), bf16)] if riders.size else []
@@ -770,7 +813,8 @@
             ((16, channels), f32),
         ],
         [((edge + 2, edge, edge, channels), f32), ((edge + 4,) + column, f32)],
-        act,
+        near,
+        far,
         y,
         x,
         corner,

time: 54.8 us -> 57.2 us (1.044)
  blocking collectives: 19.2 us -> 20.9 us
    ppermute x2, starting transfers between devices: 6.03 us -> 2.88 us  [halos(): corner = lax.ppermute(corners[0], 'yx', self.swap_route(3))]
    ppermute x2, starting transfers between devices: 1.8 us -> 4.71 us  [halos(): y = lax.ppermute(y_edges[0], 'yx', self.swap_route(2))]
    ppermute x2, waiting for transfers between devices: 0.01 us -> 2.69 us  [halos(): corner = lax.ppermute(corners[0], 'yx', self.swap_route(3))]
    all_to_all x2, blocking collectives: 19.2 us -> 20.9 us  [share(): return lax.all_to_all(stats, PART, 0, 0)]
    ppermute x2, waiting for transfers between devices: 1.59 us -> 0.1 us  [halos(): y = lax.ppermute(y_edges[0], 'yx', self.swap_route(2))]
    ppermute x2, waiting for transfers between devices: 1.58 us -> 0.69 us  [halos(): x = lax.ppermute(x_edges[0], 'yx', self.swap_route(1))]
    pallas_call x10 -> x12, Pallas kernels: 14.6 us -> 15.1 us  [call(): pl.pallas_call(kernel, out_shape=[jax.ShapeDtypeStruct(shape, dtype) for...]
where the time goes in v19:
time: 57.2 us; the launch traced here: 57 us
  blocking collectives  20.9 us (37%)
  starting transfers between devices  17.1 us (30%)
  Pallas kernels  15.2 us (27%)
  waiting for transfers between devices  3.49 us (6%)
    all_to_all x2, blocking collectives, share(): return lax.all_to_all(stats, PART, 0, 0)  20.9 us
    pallas_call x12, Pallas kernels, call(): pl.pallas_call(kernel, out_shape=[jax.ShapeDtypeStruct(shape, dtype) for...  15.1 us
    ppermute x2, starting transfers between devices, halos(): y = lax.ppermute(y_edges[0], 'yx', self.swap_route(2))  4.71 us
    ppermute x3, starting transfers between devices, swap(): lax.ppermute(block, axis, [(i, i ^ mask) for i in range(lax.axis_size(axi...  3.6 us
    ppermute x2, starting transfers between devices, halos(): corner = lax.ppermute(corners[0], 'yx', self.swap_route(3))  2.88 us
    ppermute x2, starting transfers between devices, halos(): x = lax.ppermute(x_edges[0], 'yx', self.swap_route(1))  2.72 us
    ppermute x2, waiting for transfers between devices, halos(): corner = lax.ppermute(corners[0], 'yx', self.swap_route(3))  2.69 us
    ppermute x1, starting transfers between devices, swap_depth(): lax.ppermute(inner, 'gz', routes[0])  2.56 us
  transfers between devices with their start and end apart: 11, of which 4 were waited for; matrix products, arithmetic and copies ran while one was open for 0% of the time, Pallas kernels for 20%

profile of v19, /device:TPU:0, one launch (start us, length us, event | category | flops | bytes accessed | tf_op | source)
XLA Modules:
  0.0 57.0 jit_solution(9060482938090935430)
XLA Ops:
  0.0 1.6 %shard_map.82 = (bf16[1,30,16,128]{3,2,1,0:T(8,128)(2,1)S(1)}, bf16[14,16,128]{2,1,0:T(8,128)(2,1)S(1)}, bf16[18,18,16,128]{3,2,1,0:T(8,128)(2,1)S(1)}, bf16[27,128,128]{2,1,0:T(8,128)(2,1)S(1)}) custom-call(bf16[16,16,16,128]{3,2,1,0:T(8,128)(2,1)} %x_in.1, bf16[27,128,128]{2,1,0:T(8,128)(2,1)} %bitcast.50, bf16[108,16,128]{2,1,0:T(8,128)(2,1)} %bitcast.51), custom_call_target="tpu_custom_call" | custom-call | bytes 5242880 | tf_op jit(solution)/shard_map/pallas_call | solution.py:105
  1.6 4.1 %collective-permute-start = (bf16[30,16,128]{2,1,0:T(8,128)(2,1)S(1)}, bf16[30,16,128]{2,1,0:T(8,128)(2,1)S(1)}, u32[]{:S(2)}, u32[]{:S(2)}) collective-permute-start(bf16[30,16,128]{2,1,0:T(8,128)(2,1)S(1)} %bitcast.44), channel_id=1, source_target_pairs={{0,2},{1,3},{2,0},{3,1},{4,6},{5,7},{6,4},{7,5},{8,10},{9,11},{10,... | collective-permute-start | bytes 368648 | tf_op jit(solution)/shard_map/ppermute | solution.py:44
  5.7 2.5 %shard_map.83 = (f32[8,16,16,128]{3,2,1,0:T(8,128)S(1)}, bf16[1152,384]{1,0:T(8,128)(2,1)S(1)}, bf16[1536,256]{1,0:T(8,128)(2,1)S(1)}, bf16[108,16,128]{2,1,0:T(8,128)(2,1)S(1)}) custom-call(bf16[108,16,128]{2,1,0:T(8,128)(2,1)} %bitcast.52, bf16[18,18,16,128]{3,2,1,0:T(8,128)(2,1)S(1)} %get-tuple-element.40.x, ...), custom_call_target="tpu_custom_call" | custom-call | flops 1811939328 | bytes 4194304 | tf_op jit(solution)/shard_map/pallas_call | solution.py:105
  8.2 0.3 shard_map.84
  8.5 1.4 %collective-permute-start.2 = (bf16[15,16,128]{2,1,0:T(8,128)(2,1)S(1)}, bf16[15,16,128]{2,1,0:T(8,128)(2,1)S(1)}, u32[]{:S(2)}, u32[]{:S(2)}) collective-permute-start(bf16[15,16,128]{2,1,0:T(8,128)(2,1)S(1)} %bitcast.46), channel_id=1, source_target_pairs={{0,3},{1,2},{2,1},{3,0},{4,7},{5,6},{6,5},{7,4},{8,11},{9,10},{10,... | collective-permute-start | bytes 184328 | tf_op jit(solution)/shard_map/ppermute | solution.py:46
  9.9 0.3 collective-permute-start.1
  10.2 2.3 %shard_map.85.far = f32[8,16,16,128]{3,2,1,0:T(8,128)S(1)} custom-call(bf16[18,18,16,128]{3,2,1,0:T(8,128)(2,1)S(1)} %get-tuple-element.40.x, bf16[1152,384]{1,0:T(8,128)(2,1)S(1)} %get-tuple-element.45.after.taps, bf16[1536,256]{1,0:T(8,128)(2,1)S(1)} %get-tuple-element.48.pairs, bf16[1,15,16,128]{3,2,1,0:T(8,128)(2,1)S(1)} %get-tuple-element.47.after), custom_call_target="tpu_custom_call" | custom-call | flops 1811939328 | bytes 4194304 | tf_op jit(solution)/shard_map/pallas_call | solution.py:105
  12.6 2.7 %collective-permute-done.2 = bf16[15,16,128]{2,1,0:T(8,128)(2,1)S(1)} collective-permute-done((bf16[15,16,128]{2,1,0:T(8,128)(2,1)S(1)}, bf16[15,16,128]{2,1,0:T(8,128)(2,1)S(1)}, u32[]{:S(2)}, u32[]{:S(2)}) %collective-permute-start.2) | collective-permute-done | bytes 61472 | tf_op jit(solution)/shard_map/ppermute | solution.py:46
  15.2 0.0 collective-permute-done
  15.2 0.5 collective-permute-done.1
  15.7 0.1 shard_map.87
  15.8 0.7 %collective-permute-start.4 = (bf16[57,16,128]{2,1,0:T(8,128)(2,1)S(1)}, bf16[57,16,128]{2,1,0:T(8,128)(2,1)S(1)}, u32[]{:S(2)}, u32[]{:S(2)}) collective-permute-start(bf16[57,16,128]{2,1,0:T(8,128)(2,1)S(1)} %get-tuple-element.57), channel_id=1, source_target_pairs={{4,8},{8,4},{5,9},{9,5},{6,10},{10,6},{7,11},{11,7},{20,24},{24,20... | collective-permute-start | bytes 700424 | tf_op jit(solution)/shard_map/ppermute | solution.py:63
  16.5 1.6 %collective-permute-start.5 = (bf16[1,4,14,16,128]{4,3,2,1,0:T(8,128)(2,1)S(1)}, bf16[1,4,14,16,128]{4,3,2,1,0:T(8,128)(2,1)S(1)}, u32[]{:S(2)}, u32[]{:S(2)}) collective-permute-start(bf16[1,4,14,16,128]{4,3,2,1,0:T(8,128)(2,1)S(1)} %bitcast.35), channel_id=1, source_target_pairs={{0,16},{16,0},{1,17},{17,1},{2,18},{18,2},{3,19},{19,3},{4,20},{20... | collective-permute-start | bytes 688136 | tf_op jit(solution)/shard_map/ppermute | solution.py:94
  18.1 2.6 %collective-permute-start.3 = (bf16[55,16,128]{2,1,0:T(8,128)(2,1)S(1)}, bf16[55,16,128]{2,1,0:T(8,128)(2,1)S(1)}, u32[]{:S(2)}, u32[]{:S(2)}) collective-permute-start(bf16[55,16,128]{2,1,0:T(8,128)(2,1)S(1)} %get-tuple-element.56), channel_id=1, source_target_pairs={{0,4},{4,0},{8,12},{12,8},{1,5},{5,1},{9,13},{13,9},{2,6},{6,2},{1... | collective-permute-start | bytes 675848 | tf_op jit(solution)/shard_map/ppermute | solution.py:63
  20.6 1.1 %shard_map.86 = (f32[14,16,16,128]{3,2,1,0:T(8,128)S(1)}, f32[4,16,16,128]{3,2,1,0:T(8,128)S(1)}, f32[16,128]{1,0:T(8,128)S(1)}) custom-call(f32[8,16,16,128]{3,2,1,0:T(8,128)S(1)} %get-tuple-element.42.near, f32[8,16,16,128]{3,2,1,0:T(8,128)S(1)} %shard_map.85.far, bf16[1,30,16,128]{3,2,1,0:T(8,128)(2,1)S(1)} %bitcast.30, ...), custom_call_target="tpu_custom_call" | custom-call | tf_op jit(solution)/shard_map/pallas_call | solution.py:105
  21.7 0.0 collective-permute-done.3.face
  21.7 1.1 %shard_map.88.ends = f32[6,16,16,128]{3,2,1,0:T(8,128)S(1)} custom-call(bf16[18,18,16,128]{3,2,1,0:T(8,128)(2,1)S(1)} %get-tuple-element.40.x, f32[4,16,16,128]{3,2,1,0:T(8,128)S(1)} %get-tuple-element.55.partial, bf16[55,16,128]{2,1,0:T(8,128)(2,1)S(1)} %collective-permute-done.3.face, bf16[1152,384]{1,0:T(8,128)(2,1)S(1)} %get-tuple-element.45.after.taps, ...), custom_call_target="tpu_custom_call" | custom-call | tf_op jit(solution)/shard_map/pallas_call | solution.py:105
  22.9 0.0 collective-permute-done.4.face
  22.9 1.3 %shard_map.89 = (f32[6,16,16,128]{3,2,1,0:T(8,128)S(1)}, f32[16,2,128]{2,1,0:T(2,128)S(1)}) custom-call(bf16[18,18,16,128]{3,2,1,0:T(8,128)(2,1)S(1)} %get-tuple-element.40.x, f32[16,128]{1,0:T(8,128)S(1)} %get-tuple-element.54.middle_stats, f32[6,16,16,128]{3,2,1,0:T(8,128)S(1)} %shard_map.88.ends, bf16[57,16,128]{2,1,0:T(8,128)(2,1)S(1)} %collective-permute-done.4.face, ...), custom_call_target="tpu_custom_call" | custom-call | tf_op jit(solution)/shard_map/pallas_call | solution.py:105
  24.2 0.0 copy-start.3
  24.2 0.0 copy-start.4
  24.2 0.0 collective-permute-done.5.refs_1_
  24.2 1.8 %collective-permute-start.6 = (bf16[2,3,14,16,128]{4,3,2,1,0:T(8,128)(2,1)S(1)}, bf16[2,3,14,16,128]{4,3,2,1,0:T(8,128)(2,1)S(1)}, u32[]{:S(2)}, u32[]{:S(2)}) collective-permute-start(bf16[2,3,14,16,128]{4,3,2,1,0:T(8,128)(2,1)S(1)} %bitcast.27), channel_id=1, source_target_pairs={{0,8},{4,12},{8,0},{12,4},{1,9},{5,13},{9,1},{13,5},{2,10},{6,14},... | collective-permute-start | bytes 1032200 | tf_op jit(solution)/shard_map/ppermute | solution.py:94
  26.1 11.0 %all_to_all.10.stats = f32[16,2,128]{2,1,0:T(2,128)S(1)} all-to-all(f32[16,2,128]{2,1,0:T(2,128)S(1)} %get-tuple-element.61), channel_id=1, replica_groups=mesh['cand'=2,'gz'=4,'yx'=4] {'gz','yx'}, dimensions={0} | all-to-all | bytes 32768 | tf_op jit(solution)/shard_map/all_to_all | solution.py:98
  37.1 0.0 collective-permute-done.6.refs_1_
  37.1 0.2 collective-permute-start.7
  37.3 0.0 copy-done.3
  37.3 0.0 copy-done.4
  37.3 1.1 %shard_map.91 = (bf16[16,16,16,128]{3,2,1,0:T(8,128)(2,1)S(1)}, f32[10,8,8,128]{3,2,1,0:T(8,128)S(1)}, bf16[1,80,128]{2,1,0:T(8,128)(2,1)S(1)}, bf16[1,80,128]{2,1,0:T(8,128)(2,1)S(1)}, f32[1,16,128]{2,1,0:T(8,128)S(1)}) custom-call(f32[14,16,16,128]{3,2,1,0:T(8,128)S(1)} %get-tuple-element.53.inner, f32[6,16,16,128]{3,2,1,0:T(8,128)S(1)} %get-tuple-element.58.ends, ...), custom_call_target="tpu_custom_call" | custom-call | flops 10485760 | bytes 3145728 | tf_op jit(solution)/shard_map/pallas_call | solution.py:105
  38.5 1.5 %collective-permute-start.10 = (f32[16,128]{1,0:T(8,128)S(1)}, f32[16,128]{1,0:T(8,128)S(1)}, u32[]{:S(2)}, u32[]{:S(2)}) collective-permute-start(f32[16,128]{1,0:T(8,128)S(1)} %bitcast.49), channel_id=1, source_target_pairs={{0,3},{1,2},{2,1},{3,0},{4,7},{5,6},{6,5},{7,4},{8,11},{9,10},{10,... | collective-permute-start | bytes 24584 | tf_op jit(solution)/shard_map/ppermute | solution.py:46
  39.9 0.6 %collective-permute-start.8 = (bf16[80,128]{1,0:T(8,128)(2,1)S(1)}, bf16[80,128]{1,0:T(8,128)(2,1)S(1)}, u32[]{:S(2)}, u32[]{:S(2)}) collective-permute-start(bf16[80,128]{1,0:T(8,128)(2,1)S(1)} %bitcast.48), channel_id=1, source_target_pairs={{0,2},{1,3},{2,0},{3,1},{4,6},{5,7},{6,4},{7,5},{8,10},{9,11},{10,... | collective-permute-start | bytes 61448 | tf_op jit(solution)/shard_map/ppermute | solution.py:44
  40.5 2.4 %collective-permute-start.9 = (bf16[80,128]{1,0:T(8,128)(2,1)S(1)}, bf16[80,128]{1,0:T(8,128)(2,1)S(1)}, u32[]{:S(2)}, u32[]{:S(2)}) collective-permute-start(bf16[80,128]{1,0:T(8,128)(2,1)S(1)} %bitcast.47), channel_id=1, source_target_pairs={{0,1},{1,0},{2,3},{3,2},{4,5},{5,4},{6,7},{7,6},{8,9},{9,8},{10,11... | collective-permute-start | bytes 61448 | tf_op jit(solution)/shard_map/ppermute | solution.py:45
  42.9 0.0 collective-permute-done.7.refs_1_
  42.9 0.1 shard_map.93
  43.0 1.4 %shard_map.94 = (f32[2,512,128]{2,1,0:T(8,128)S(1)}, bf16[4,108,16,128]{3,2,1,0:T(8,128)(2,1)S(1)}) custom-call(f32[10,8,8,128]{3,2,1,0:T(8,128)S(1)} %get-tuple-element.64.pooled, bf16[108,16,128]{2,1,0:T(8,128)(2,1)S(1)} %get-tuple-element.65.own, bf16[8,3,14,16,128]{4,3,2,1,0:T(8,128)(2,1)S(1)} %bitcast.26), custom_call_target="tpu_custom_call" | custom-call | flops 905969664 | bytes 4194304 | tf_op jit(solution)/shard_map/pallas_call | solution.py:105
  44.5 0.0 copy-start
  44.5 0.0 copy-start.1
  44.5 0.0 copy-start.2
  44.5 0.0 collective-permute-done.10
  44.5 0.1 collective-permute-done.8
  44.6 0.2 collective-permute-done.9
  44.8 0.7 %shard_map.95 = (f32[2,512,128]{2,1,0:T(8,128)S(1)}, f32[16,2,256]{2,1,0:T(2,128)S(1)}) custom-call(f32[2,512,128]{2,1,0:T(8,128)S(1)} %get-tuple-element.67.own, bf16[1,80,128]{2,1,0:T(8,128)(2,1)S(1)} %bitcast.37, bf16[1,80,128]{2,1,0:T(8,128)(2,1)S(1)} %bitcast.38, f32[1,16,128]{2,1,0:T(8,128)S(1)} %bitcast.39, ...), custom_call_target="tpu_custom_call" | custom-call | flops 67108864 | bytes 3145728 | tf_op jit(solution)/shard_map/pallas_call | solution.py:105
  45.5 9.9 %all_to_all.11.stats = f32[16,2,256]{2,1,0:T(2,128)S(1)} all-to-all(f32[16,2,256]{2,1,0:T(2,128)S(1)} %get-tuple-element.73), channel_id=1, replica_groups=mesh['cand'=2,'gz'=4,'yx'=4] {'gz','yx'}, dimensions={0} | all-to-all | bytes 65536 | tf_op jit(solution)/shard_map/all_to_all | solution.py:98
  55.5 0.0 copy-done
  55.5 0.0 copy-done.1
  55.5 0.0 copy-done.2
  55.5 1.5 %shard_map.96 = bf16[16,16,16,128]{3,2,1,0:T(8,128)(2,1)} custom-call(f32[2,512,128]{2,1,0:T(8,128)S(1)} %get-tuple-element.72.act, f32[16,2,256]{2,1,0:T(2,128)S(1)} %all_to_all.11.stats, f32[1,256]{1,0:T(1,128)S(1)} %bitcast.40, f32[1,256]{1,0:T(1,128)S(1)} %bitcast.41, bf16[256,128]{1,0:T(8,128)(2,1)S(1)} %copy-done, ...), custom_call_target="tpu_custom_call" | custom-call | flops 67108864 | bytes 3145728 | tf_op jit(solution)/shard_map/pallas_call | solution.py:105
  (2 shorter events, 0.1 us)
Async XLA Ops:
  1.6 13.7 %collective-permute-start = (bf16[30,16,128]{2,1,0:T(8,128)(2,1)S(1)}, bf16[30,16,128]{2,1,0:T(8,128)(2,1)S(1)}, u32[]{:S(2)}, u32[]{:S(2)}) collective-permute-start(bf16[30,16,128]{2,1,0:T(8,128)(2,1)S(1)} %bitcast.44), channel_id=1, source_target_pairs={{0,2},{1,3},{2,0},{3,1},{4,6},{5,7},{6,4},{7,5},{8,10},{9,11},{10,... | collective-permute-start | bytes 368648 | tf_op jit(solution)/shard_map/ppermute | solution.py:44
  8.5 6.7 %collective-permute-start.2 = (bf16[15,16,128]{2,1,0:T(8,128)(2,1)S(1)}, bf16[15,16,128]{2,1,0:T(8,128)(2,1)S(1)}, u32[]{:S(2)}, u32[]{:S(2)}) collective-permute-start(bf16[15,16,128]{2,1,0:T(8,128)(2,1)S(1)} %bitcast.46), channel_id=1, source_target_pairs={{0,3},{1,2},{2,1},{3,0},{4,7},{5,6},{6,5},{7,4},{8,11},{9,10},{10,... | collective-permute-start | bytes 184328 | tf_op jit(solution)/shard_map/ppermute | solution.py:46
  9.9 5.8 %collective-permute-start.1 = (bf16[30,16,128]{2,1,0:T(8,128)(2,1)S(1)}, bf16[30,16,128]{2,1,0:T(8,128)(2,1)S(1)}, u32[]{:S(2)}, u32[]{:S(2)}) collective-permute-start(bf16[30,16,128]{2,1,0:T(8,128)(2,1)S(1)} %bitcast.45), channel_id=1, source_target_pairs={{0,1},{1,0},{2,3},{3,2},{4,5},{5,4},{6,7},{7,6},{8,9},{9,8},{10,11... | collective-permute-start | bytes 368648 | tf_op jit(solution)/shard_map/ppermute | solution.py:45
  15.8 7.1 %collective-permute-start.4 = (bf16[57,16,128]{2,1,0:T(8,128)(2,1)S(1)}, bf16[57,16,128]{2,1,0:T(8,128)(2,1)S(1)}, u32[]{:S(2)}, u32[]{:S(2)}) collective-permute-start(bf16[57,16,128]{2,1,0:T(8,128)(2,1)S(1)} %get-tuple-element.57), channel_id=1, source_target_pairs={{4,8},{8,4},{5,9},{9,5},{6,10},{10,6},{7,11},{11,7},{20,24},{24,20... | collective-permute-start | bytes 700424 | tf_op jit(solution)/shard_map/ppermute | solution.py:63
  16.5 7.7 %collective-permute-start.5 = (bf16[1,4,14,16,128]{4,3,2,1,0:T(8,128)(2,1)S(1)}, bf16[1,4,14,16,128]{4,3,2,1,0:T(8,128)(2,1)S(1)}, u32[]{:S(2)}, u32[]{:S(2)}) collective-permute-start(bf16[1,4,14,16,128]{4,3,2,1,0:T(8,128)(2,1)S(1)} %bitcast.35), channel_id=1, source_target_pairs={{0,16},{16,0},{1,17},{17,1},{2,18},{18,2},{3,19},{19,3},{4,20},{20... | collective-permute-start | bytes 688136 | tf_op jit(solution)/shard_map/ppermute | solution.py:94
  18.1 3.7 %collective-permute-start.3 = (bf16[55,16,128]{2,1,0:T(8,128)(2,1)S(1)}, bf16[55,16,128]{2,1,0:T(8,128)(2,1)S(1)}, u32[]{:S(2)}, u32[]{:S(2)}) collective-permute-start(bf16[55,16,128]{2,1,0:T(8,128)(2,1)S(1)} %get-tuple-element.56), channel_id=1, source_target_pairs={{0,4},{4,0},{8,12},{12,8},{1,5},{5,1},{9,13},{13,9},{2,6},{6,2},{1... | collective-permute-start | bytes 675848 | tf_op jit(solution)/shard_map/ppermute | solution.py:63
  24.2 13.1 %copy-start.3 = (f32[128]{0:T(128)S(1)}, f32[128]{0:T(128)}, u32[]{:S(2)}) copy-start(f32[128]{0:T(128)} %param.10) | copy-start | bytes 1540
  24.2 13.1 %copy-start.4 = (f32[128]{0:T(128)S(1)}, f32[128]{0:T(128)}, u32[]{:S(2)}) copy-start(f32[128]{0:T(128)} %param.11) | copy-start | bytes 1540
  24.2 12.8 %collective-permute-start.6 = (bf16[2,3,14,16,128]{4,3,2,1,0:T(8,128)(2,1)S(1)}, bf16[2,3,14,16,128]{4,3,2,1,0:T(8,128)(2,1)S(1)}, u32[]{:S(2)}, u32[]{:S(2)}) collective-permute-start(bf16[2,3,14,16,128]{4,3,2,1,0:T(8,128)(2,1)S(1)} %bitcast.27), channel_id=1, source_target_pairs={{0,8},{4,12},{8,0},{12,4},{1,9},{5,13},{9,1},{13,5},{2,10},{6,14},... | collective-permute-start | bytes 1032200 | tf_op jit(solution)/shard_map/ppermute | solution.py:94
  37.1 5.8 %collective-permute-start.7 = (bf16[4,3,14,16,128]{4,3,2,1,0:T(8,128)(2,1)S(1)}, bf16[4,3,14,16,128]{4,3,2,1,0:T(8,128)(2,1)S(1)}, u32[]{:S(2)}, u32[]{:S(2)}) collective-permute-start(bf16[4,3,14,16,128]{4,3,2,1,0:T(8,128)(2,1)S(1)} %bitcast.24), channel_id=1, source_target_pairs={{0,4},{4,0},{8,12},{12,8},{1,5},{5,1},{9,13},{13,9},{2,6},{6,2},{1... | collective-permute-start | bytes 2064392 | tf_op jit(solution)/shard_map/ppermute | solution.py:94
  38.5 6.0 %collective-permute-start.10 = (f32[16,128]{1,0:T(8,128)S(1)}, f32[16,128]{1,0:T(8,128)S(1)}, u32[]{:S(2)}, u32[]{:S(2)}) collective-permute-start(f32[16,128]{1,0:T(8,128)S(1)} %bitcast.49), channel_id=1, source_target_pairs={{0,3},{1,2},{2,1},{3,0},{4,7},{5,6},{6,5},{7,4},{8,11},{9,10},{10,... | collective-permute-start | bytes 24584 | tf_op jit(solution)/shard_map/ppermute | solution.py:46
  39.9 4.7 %collective-permute-start.8 = (bf16[80,128]{1,0:T(8,128)(2,1)S(1)}, bf16[80,128]{1,0:T(8,128)(2,1)S(1)}, u32[]{:S(2)}, u32[]{:S(2)}) collective-permute-start(bf16[80,128]{1,0:T(8,128)(2,1)S(1)} %bitcast.48), channel_id=1, source_target_pairs={{0,2},{1,3},{2,0},{3,1},{4,6},{5,7},{6,4},{7,5},{8,10},{9,11},{10,... | collective-permute-start | bytes 61448 | tf_op jit(solution)/shard_map/ppermute | solution.py:44
  40.5 4.3 %collective-permute-start.9 = (bf16[80,128]{1,0:T(8,128)(2,1)S(1)}, bf16[80,128]{1,0:T(8,128)(2,1)S(1)}, u32[]{:S(2)}, u32[]{:S(2)}) collective-permute-start(bf16[80,128]{1,0:T(8,128)(2,1)S(1)} %bitcast.47), channel_id=1, source_target_pairs={{0,1},{1,0},{2,3},{3,2},{4,5},{5,4},{6,7},{7,6},{8,9},{9,8},{10,11... | collective-permute-start | bytes 61448 | tf_op jit(solution)/shard_map/ppermute | solution.py:45
  44.5 11.0 %copy-start = (bf16[256,128]{1,0:T(8,128)(2,1)S(1)}, bf16[256,128]{1,0:T(8,128)(2,1)}, u32[]{:S(2)}) copy-start(bf16[256,128]{1,0:T(8,128)(2,1)} %up.1) | copy-start | bytes 196612
  44.5 11.0 %copy-start.1 = (f32[256]{0:T(256)S(1)}, f32[256]{0:T(256)}, u32[]{:S(2)}) copy-start(f32[256]{0:T(256)} %param.13) | copy-start | bytes 3076
  44.5 11.0 %copy-start.2 = (f32[256]{0:T(256)S(1)}, f32[256]{0:T(256)}, u32[]{:S(2)}) copy-start(f32[256]{0:T(256)} %param.14) | copy-start | bytes 3076

commit v20 on v18

--- a/solution.py
+++ b/solution.py
@@ -784,6 +784,10 @@
     (ends,) = call(
         functools.partial(inner_kernel, ny, nx), [six], room, field, partial, inner, taps, pairs
     )
+    if riders.size:
+        ends, other = lax.optimization_barrier((ends, other))
+        held = stack(held, other, part=(1, 3)).reshape((2, 3) + held.shape[2:])
+        other = swap(held, *riders.STEPS[1])
     ends, stats = call(
         functools.partial(outer_kernel, ny, nx),
         [six, ((devices, 2, channels), f32)],
@@ -794,18 +798,14 @@
         outer,
         taps,
         pairs,
-    )
+        flops=conv_flops,
+    )
+    stats = share(stats)
     if riders.size:
-        stats, other = lax.optimization_barrier((stats, other))
-        held = stack(held, other, part=(1, 3)).reshape((2, 3) + held.shape[2:])
-        other = swap(held, *riders.STEPS[1])
-        stats = share(stats)
         stats, other = lax.optimization_barrier((stats, other))
         held = stack(held, other).reshape((-1,) + held.shape[1:])
         other = swap(held, *riders.STEPS[2])
         held = [stack(held, other).reshape((-1,) + held.shape[1:])]
-    else:
-        stats = share(stats)
     out, pooled, *edges = call(
         functools.partial(norm_kernel, ny, nx),
         [

time: 54.8 us -> 55.7 us (1.016)
  transfers between devices with their start and end apart: 11 -> 11, of which waited for: 4 -> 5; matrix products, arithmetic and copies ran while one was open for 0% -> 0% of each run, Pallas kernels for 20% -> 19%
where the time goes in v20:
time: 55.7 us; the launch traced here: 55.5 us
  blocking collectives  19.6 us (35%)
  starting transfers between devices  17.6 us (32%)
  Pallas kernels  14.7 us (26%)
  waiting for transfers between devices  3.45 us (6%)
    all_to_all x2, blocking collectives, share(): return lax.all_to_all(stats, PART, 0, 0)  19.6 us
    pallas_call x10, Pallas kernels, call(): pl.pallas_call(kernel, out_shape=[jax.ShapeDtypeStruct(shape, dtype) for...  14.6 us
    ppermute x2, starting transfers between devices, halos(): corner = lax.ppermute(corners[0], 'yx', self.swap_route(3))  5.77 us
    ppermute x3, starting transfers between devices, swap(): lax.ppermute(block, axis, [(i, i ^ mask) for i in range(lax.axis_size(axi...  4.1 us
    ppermute x1, starting transfers between devices, swap_depth(): lax.ppermute(inner, 'gz', routes[0])  2.56 us
    ppermute x2, starting transfers between devices, halos(): x = lax.ppermute(x_edges[0], 'yx', self.swap_route(1))  2.42 us
    ppermute x2, starting transfers between devices, halos(): y = lax.ppermute(y_edges[0], 'yx', self.swap_route(2))  2.05 us
    ppermute x2, waiting for transfers between devices, halos(): x = lax.ppermute(x_edges[0], 'yx', self.swap_route(1))  1.59 us
  transfers between devices with their start and end apart: 11, of which 5 were waited for; matrix products, arithmetic and copies ran while one was open for 0% of the time, Pallas kernels for 19%

profile of v20, /device:TPU:0, one launch (start us, length us, event | category | flops | bytes accessed | tf_op | source)
XLA Modules:
  0.0 55.5 jit_solution(8619451897363820921)
XLA Ops:
  0.0 1.6 %shard_map.82 = (bf16[1,30,16,128]{3,2,1,0:T(8,128)(2,1)S(1)}, bf16[1,30,16,128]{3,2,1,0:T(8,128)(2,1)S(1)}, bf16[1,15,16,128]{3,2,1,0:T(8,128)(2,1)S(1)}, bf16[...) custom-call(bf16[16,16,16,128]{3,2,1,0:T(8,128)(2,1)} %x_in.1, bf16[27,128,128]{2,1,0:T(8,128)(2,1)} %bitcast.50, ...), custom_call_target="tpu_custom_call" | custom-call | bytes 5242880 | tf_op jit(solution)/shard_map/pallas_call | solution.py:105
  1.6 5.1 %collective-permute-start.2 = (bf16[15,16,128]{2,1,0:T(8,128)(2,1)S(1)}, bf16[15,16,128]{2,1,0:T(8,128)(2,1)S(1)}, u32[]{:S(2)}, u32[]{:S(2)}) collective-permute-start(bf16[15,16,128]{2,1,0:T(8,128)(2,1)S(1)} %bitcast.46), channel_id=1, source_target_pairs={{0,3},{1,2},{2,1},{3,0},{4,7},{5,6},{6,5},{7,4},{8,11},{9,10},{10,... | collective-permute-start | bytes 184328 | tf_op jit(solution)/shard_map/ppermute | solution.py:46
  6.7 0.0 collective-permute-start.1
  6.7 0.6 %collective-permute-start = (bf16[30,16,128]{2,1,0:T(8,128)(2,1)S(1)}, bf16[30,16,128]{2,1,0:T(8,128)(2,1)S(1)}, u32[]{:S(2)}, u32[]{:S(2)}) collective-permute-start(bf16[30,16,128]{2,1,0:T(8,128)(2,1)S(1)} %bitcast.44), channel_id=1, source_target_pairs={{0,2},{1,3},{2,0},{3,1},{4,6},{5,7},{6,4},{7,5},{8,10},{9,11},{10,... | collective-permute-start | bytes 368648 | tf_op jit(solution)/shard_map/ppermute | solution.py:44
  7.4 4.7 %shard_map.83 = (f32[16,16,16,128]{3,2,1,0:T(8,128)S(1)}, bf16[1152,384]{1,0:T(8,128)(2,1)S(1)}, bf16[1536,256]{1,0:T(8,128)(2,1)S(1)}, bf16[108,16,128]{2,1,0:T(8,128)(2,1)S(1)}) custom-call(bf16[108,16,128]{2,1,0:T(8,128)(2,1)} %bitcast.52, bf16[18,18,16,128]{3,2,1,0:T(8,128)(2,1)S(1)} %get-tuple-element.42.x, ...), custom_call_target="tpu_custom_call" | custom-call | flops 3623878656 | bytes 6291456 | tf_op jit(solution)/shard_map/pallas_call | solution.py:105
  12.1 0.0 collective-permute-done.2
  12.1 1.4 %collective-permute-done.1 = bf16[30,16,128]{2,1,0:T(8,128)(2,1)S(1)} collective-permute-done((bf16[30,16,128]{2,1,0:T(8,128)(2,1)S(1)}, bf16[30,16,128]{2,1,0:T(8,128)(2,1)S(1)}, u32[]{:S(2)}, u32[]{:S(2)}) %collective-permute-start.1) | collective-permute-done | bytes 122912 | tf_op jit(solution)/shard_map/ppermute | solution.py:45
  13.5 1.6 %collective-permute-done = bf16[30,16,128]{2,1,0:T(8,128)(2,1)S(1)} collective-permute-done((bf16[30,16,128]{2,1,0:T(8,128)(2,1)S(1)}, bf16[30,16,128]{2,1,0:T(8,128)(2,1)S(1)}, u32[]{:S(2)}, u32[]{:S(2)}) %collective-permute-start) | collective-permute-done | bytes 122912 | tf_op jit(solution)/shard_map/ppermute | solution.py:44
  15.1 0.1 shard_map.85
  15.2 0.7 %collective-permute-start.5 = (bf16[57,16,128]{2,1,0:T(8,128)(2,1)S(1)}, bf16[57,16,128]{2,1,0:T(8,128)(2,1)S(1)}, u32[]{:S(2)}, u32[]{:S(2)}) collective-permute-start(bf16[57,16,128]{2,1,0:T(8,128)(2,1)S(1)} %get-tuple-element.57), channel_id=1, source_target_pairs={{4,8},{8,4},{5,9},{9,5},{6,10},{10,6},{7,11},{11,7},{20,24},{24,20... | collective-permute-start | bytes 700424 | tf_op jit(solution)/shard_map/ppermute | solution.py:63
  15.8 1.6 %collective-permute-start.4 = (bf16[1,4,14,16,128]{4,3,2,1,0:T(8,128)(2,1)S(1)}, bf16[1,4,14,16,128]{4,3,2,1,0:T(8,128)(2,1)S(1)}, u32[]{:S(2)}, u32[]{:S(2)}) collective-permute-start(bf16[1,4,14,16,128]{4,3,2,1,0:T(8,128)(2,1)S(1)} %bitcast.35), channel_id=1, source_target_pairs={{0,16},{16,0},{1,17},{17,1},{2,18},{18,2},{3,19},{19,3},{4,20},{20... | collective-permute-start | bytes 688136 | tf_op jit(solution)/shard_map/ppermute | solution.py:94
  17.5 2.6 %collective-permute-start.3 = (bf16[55,16,128]{2,1,0:T(8,128)(2,1)S(1)}, bf16[55,16,128]{2,1,0:T(8,128)(2,1)S(1)}, u32[]{:S(2)}, u32[]{:S(2)}) collective-permute-start(bf16[55,16,128]{2,1,0:T(8,128)(2,1)S(1)} %get-tuple-element.53), channel_id=1, source_target_pairs={{0,4},{4,0},{8,12},{12,8},{1,5},{5,1},{9,13},{13,9},{2,6},{6,2},{1... | collective-permute-start | bytes 675848 | tf_op jit(solution)/shard_map/ppermute | solution.py:63
  20.0 1.0 %shard_map.84 = (f32[14,16,16,128]{3,2,1,0:T(8,128)S(1)}, f32[4,16,16,128]{3,2,1,0:T(8,128)S(1)}, f32[16,128]{1,0:T(8,128)S(1)}) custom-call(f32[16,16,16,128]{3,2,1,0:T(8,128)S(1)} %get-tuple-element.45.own, bf16[1,30,16,128]{3,2,1,0:T(8,128)(2,1)S(1)} %bitcast.32, bf16[1,30,16,128]{3,2,1,0:T(8,128)(2,1)S(1)} %bitcast.30, ...), custom_call_target="tpu_custom_call" | custom-call | tf_op jit(solution)/shard_map/pallas_call | solution.py:105
  21.1 0.1 collective-permute-done.3.face
  21.1 1.1 %shard_map.86.ends = f32[6,16,16,128]{3,2,1,0:T(8,128)S(1)} custom-call(bf16[18,18,16,128]{3,2,1,0:T(8,128)(2,1)S(1)} %get-tuple-element.42.x, f32[4,16,16,128]{3,2,1,0:T(8,128)S(1)} %get-tuple-element.52.partial, bf16[55,16,128]{2,1,0:T(8,128)(2,1)S(1)} %collective-permute-done.3.face, bf16[1152,384]{1,0:T(8,128)(2,1)S(1)} %get-tuple-element.49.taps, ...), custom_call_target="tpu_custom_call" | custom-call | tf_op jit(solution)/shard_map/pallas_call | solution.py:105
  22.3 0.2 collective-permute-done.4.refs_1_
  22.5 2.3 %collective-permute-start.6 = (bf16[2,3,14,16,128]{4,3,2,1,0:T(8,128)(2,1)S(1)}, bf16[2,3,14,16,128]{4,3,2,1,0:T(8,128)(2,1)S(1)}, u32[]{:S(2)}, u32[]{:S(2)}) collective-permute-start(bf16[2,3,14,16,128]{4,3,2,1,0:T(8,128)(2,1)S(1)} %bitcast.27), channel_id=1, source_target_pairs={{0,8},{4,12},{8,0},{12,4},{1,9},{5,13},{9,1},{13,5},{2,10},{6,14},... | collective-permute-start | bytes 1032200 | tf_op jit(solution)/shard_map/ppermute | solution.py:94
  24.8 0.0 collective-permute-done.5.face
  24.8 0.0 copy-start.3
  24.8 0.0 copy-start.4
  24.8 1.2 %shard_map.87 = (f32[6,16,16,128]{3,2,1,0:T(8,128)S(1)}, f32[16,2,128]{2,1,0:T(2,128)S(1)}) custom-call(bf16[18,18,16,128]{3,2,1,0:T(8,128)(2,1)S(1)} %get-tuple-element.42.x, f32[16,128]{1,0:T(8,128)S(1)} %get-tuple-element.51.middle_stats, f32[6,16,16,128]{3,2,1,0:T(8,128)S(1)} %shard_map.86.ends, bf16[57,16,128]{2,1,0:T(8,128)(2,1)S(1)} %collective-permute-done.5.face, ...), custom_call_target="tpu_custom_call" | custom-call | flops 3623878656 | tf_op jit(solution)/shard_map/pallas_call | solution.py:105
  26.0 9.5 %all_to_all.10.stats = f32[16,2,128]{2,1,0:T(2,128)S(1)} all-to-all(f32[16,2,128]{2,1,0:T(2,128)S(1)} %get-tuple-element.59), channel_id=1, replica_groups=mesh['cand'=2,'gz'=4,'yx'=4] {'gz','yx'}, dimensions={0} | all-to-all | bytes 32768 | tf_op jit(solution)/shard_map/all_to_all | solution.py:98
  35.6 0.0 collective-permute-done.6.refs_1_
  35.6 0.2 collective-permute-start.7
  35.8 0.0 copy-done.3
  35.8 0.0 copy-done.4
  35.8 1.1 %shard_map.89 = (bf16[16,16,16,128]{3,2,1,0:T(8,128)(2,1)S(1)}, f32[10,8,8,128]{3,2,1,0:T(8,128)S(1)}, bf16[1,80,128]{2,1,0:T(8,128)(2,1)S(1)}, bf16[1,80,128]{2,1,0:T(8,128)(2,1)S(1)}, f32[1,16,128]{2,1,0:T(8,128)S(1)}) custom-call(f32[14,16,16,128]{3,2,1,0:T(8,128)S(1)} %get-tuple-element.50.inner, f32[6,16,16,128]{3,2,1,0:T(8,128)S(1)} %get-tuple-element.58.ends, ...), custom_call_target="tpu_custom_call" | custom-call | flops 10485760 | bytes 3145728 | tf_op jit(solution)/shard_map/pallas_call | solution.py:105
  37.0 0.7 %collective-permute-start.10 = (f32[16,128]{1,0:T(8,128)S(1)}, f32[16,128]{1,0:T(8,128)S(1)}, u32[]{:S(2)}, u32[]{:S(2)}) collective-permute-start(f32[16,128]{1,0:T(8,128)S(1)} %bitcast.49), channel_id=1, source_target_pairs={{0,3},{1,2},{2,1},{3,0},{4,7},{5,6},{6,5},{7,4},{8,11},{9,10},{10,... | collective-permute-start | bytes 24584 | tf_op jit(solution)/shard_map/ppermute | solution.py:46
  37.6 1.4 %collective-permute-start.8 = (bf16[80,128]{1,0:T(8,128)(2,1)S(1)}, bf16[80,128]{1,0:T(8,128)(2,1)S(1)}, u32[]{:S(2)}, u32[]{:S(2)}) collective-permute-start(bf16[80,128]{1,0:T(8,128)(2,1)S(1)} %bitcast.48), channel_id=1, source_target_pairs={{0,2},{1,3},{2,0},{3,1},{4,6},{5,7},{6,4},{7,5},{8,10},{9,11},{10,... | collective-permute-start | bytes 61448 | tf_op jit(solution)/shard_map/ppermute | solution.py:44
  39.0 2.4 %collective-permute-start.9 = (bf16[80,128]{1,0:T(8,128)(2,1)S(1)}, bf16[80,128]{1,0:T(8,128)(2,1)S(1)}, u32[]{:S(2)}, u32[]{:S(2)}) collective-permute-start(bf16[80,128]{1,0:T(8,128)(2,1)S(1)} %bitcast.47), channel_id=1, source_target_pairs={{0,1},{1,0},{2,3},{3,2},{4,5},{5,4},{6,7},{7,6},{8,9},{9,8},{10,11... | collective-permute-start | bytes 61448 | tf_op jit(solution)/shard_map/ppermute | solution.py:45
  41.5 0.0 collective-permute-done.7.refs_1_
  41.5 0.1 shard_map.91
  41.5 1.4 %shard_map.92 = (f32[2,512,128]{2,1,0:T(8,128)S(1)}, bf16[4,108,16,128]{3,2,1,0:T(8,128)(2,1)S(1)}) custom-call(f32[10,8,8,128]{3,2,1,0:T(8,128)S(1)} %get-tuple-element.62.pooled, bf16[108,16,128]{2,1,0:T(8,128)(2,1)S(1)} %get-tuple-element.63.own, bf16[8,3,14,16,128]{4,3,2,1,0:T(8,128)(2,1)S(1)} %bitcast.26), custom_call_target="tpu_custom_call" | custom-call | flops 905969664 | bytes 4194304 | tf_op jit(solution)/shard_map/pallas_call | solution.py:105
  43.0 0.0 copy-start
  43.0 0.0 copy-start.1
  43.0 0.0 copy-start.2
  43.0 0.0 collective-permute-done.10
  43.0 0.0 collective-permute-done.8
  43.0 0.2 collective-permute-done.9
  43.2 0.7 %shard_map.93 = (f32[2,512,128]{2,1,0:T(8,128)S(1)}, f32[16,2,256]{2,1,0:T(2,128)S(1)}) custom-call(f32[2,512,128]{2,1,0:T(8,128)S(1)} %get-tuple-element.65.own, bf16[1,80,128]{2,1,0:T(8,128)(2,1)S(1)} %bitcast.37, bf16[1,80,128]{2,1,0:T(8,128)(2,1)S(1)} %bitcast.38, f32[1,16,128]{2,1,0:T(8,128)S(1)} %bitcast.39, ...), custom_call_target="tpu_custom_call" | custom-call | flops 67108864 | bytes 3145728 | tf_op jit(solution)/shard_map/pallas_call | solution.py:105
  43.9 10.0 %all_to_all.11.stats = f32[16,2,256]{2,1,0:T(2,128)S(1)} all-to-all(f32[16,2,256]{2,1,0:T(2,128)S(1)} %get-tuple-element.71), channel_id=1, replica_groups=mesh['cand'=2,'gz'=4,'yx'=4] {'gz','yx'}, dimensions={0} | all-to-all | bytes 65536 | tf_op jit(solution)/shard_map/all_to_all | solution.py:98
  54.0 0.0 copy-done
  54.0 0.0 copy-done.1
  54.0 0.0 copy-done.2
  54.0 1.5 %shard_map.94 = bf16[16,16,16,128]{3,2,1,0:T(8,128)(2,1)} custom-call(f32[2,512,128]{2,1,0:T(8,128)S(1)} %get-tuple-element.70.act, f32[16,2,256]{2,1,0:T(2,128)S(1)} %all_to_all.11.stats, f32[1,256]{1,0:T(1,128)S(1)} %bitcast.40, f32[1,256]{1,0:T(1,128)S(1)} %bitcast.41, bf16[256,128]{1,0:T(8,128)(2,1)S(1)} %copy-done, ...), custom_call_target="tpu_custom_call" | custom-call | flops 67108864 | bytes 3145728 | tf_op jit(solution)/shard_map/pallas_call | solution.py:105
  (2 shorter events, 0.1 us)
Async XLA Ops:
  1.6 10.5 %collective-permute-start.2 = (bf16[15,16,128]{2,1,0:T(8,128)(2,1)S(1)}, bf16[15,16,128]{2,1,0:T(8,128)(2,1)S(1)}, u32[]{:S(2)}, u32[]{:S(2)}) collective-permute-start(bf16[15,16,128]{2,1,0:T(8,128)(2,1)S(1)} %bitcast.46), channel_id=1, source_target_pairs={{0,3},{1,2},{2,1},{3,0},{4,7},{5,6},{6,5},{7,4},{8,11},{9,10},{10,... | collective-permute-start | bytes 184328 | tf_op jit(solution)/shard_map/ppermute | solution.py:46
  6.7 6.8 %collective-permute-start.1 = (bf16[30,16,128]{2,1,0:T(8,128)(2,1)S(1)}, bf16[30,16,128]{2,1,0:T(8,128)(2,1)S(1)}, u32[]{:S(2)}, u32[]{:S(2)}) collective-permute-start(bf16[30,16,128]{2,1,0:T(8,128)(2,1)S(1)} %bitcast.45), channel_id=1, source_target_pairs={{0,1},{1,0},{2,3},{3,2},{4,5},{5,4},{6,7},{7,6},{8,9},{9,8},{10,11... | collective-permute-start | bytes 368648 | tf_op jit(solution)/shard_map/ppermute | solution.py:45
  6.7 8.4 %collective-permute-start = (bf16[30,16,128]{2,1,0:T(8,128)(2,1)S(1)}, bf16[30,16,128]{2,1,0:T(8,128)(2,1)S(1)}, u32[]{:S(2)}, u32[]{:S(2)}) collective-permute-start(bf16[30,16,128]{2,1,0:T(8,128)(2,1)S(1)} %bitcast.44), channel_id=1, source_target_pairs={{0,2},{1,3},{2,0},{3,1},{4,6},{5,7},{6,4},{7,5},{8,10},{9,11},{10,... | collective-permute-start | bytes 368648 | tf_op jit(solution)/shard_map/ppermute | solution.py:44
  15.2 9.6 %collective-permute-start.5 = (bf16[57,16,128]{2,1,0:T(8,128)(2,1)S(1)}, bf16[57,16,128]{2,1,0:T(8,128)(2,1)S(1)}, u32[]{:S(2)}, u32[]{:S(2)}) collective-permute-start(bf16[57,16,128]{2,1,0:T(8,128)(2,1)S(1)} %get-tuple-element.57), channel_id=1, source_target_pairs={{4,8},{8,4},{5,9},{9,5},{6,10},{10,6},{7,11},{11,7},{20,24},{24,20... | collective-permute-start | bytes 700424 | tf_op jit(solution)/shard_map/ppermute | solution.py:63
  15.8 6.6 %collective-permute-start.4 = (bf16[1,4,14,16,128]{4,3,2,1,0:T(8,128)(2,1)S(1)}, bf16[1,4,14,16,128]{4,3,2,1,0:T(8,128)(2,1)S(1)}, u32[]{:S(2)}, u32[]{:S(2)}) collective-permute-start(bf16[1,4,14,16,128]{4,3,2,1,0:T(8,128)(2,1)S(1)} %bitcast.35), channel_id=1, source_target_pairs={{0,16},{16,0},{1,17},{17,1},{2,18},{18,2},{3,19},{19,3},{4,20},{20... | collective-permute-start | bytes 688136 | tf_op jit(solution)/shard_map/ppermute | solution.py:94
  17.5 3.7 %collective-permute-start.3 = (bf16[55,16,128]{2,1,0:T(8,128)(2,1)S(1)}, bf16[55,16,128]{2,1,0:T(8,128)(2,1)S(1)}, u32[]{:S(2)}, u32[]{:S(2)}) collective-permute-start(bf16[55,16,128]{2,1,0:T(8,128)(2,1)S(1)} %get-tuple-element.53), channel_id=1, source_target_pairs={{0,4},{4,0},{8,12},{12,8},{1,5},{5,1},{9,13},{13,9},{2,6},{6,2},{1... | collective-permute-start | bytes 675848 | tf_op jit(solution)/shard_map/ppermute | solution.py:63
  22.5 13.1 %collective-permute-start.6 = (bf16[2,3,14,16,128]{4,3,2,1,0:T(8,128)(2,1)S(1)}, bf16[2,3,14,16,128]{4,3,2,1,0:T(8,128)(2,1)S(1)}, u32[]{:S(2)}, u32[]{:S(2)}) collective-permute-start(bf16[2,3,14,16,128]{4,3,2,1,0:T(8,128)(2,1)S(1)} %bitcast.27), channel_id=1, source_target_pairs={{0,8},{4,12},{8,0},{12,4},{1,9},{5,13},{9,1},{13,5},{2,10},{6,14},... | collective-permute-start | bytes 1032200 | tf_op jit(solution)/shard_map/ppermute | solution.py:94
  24.8 11.0 %copy-start.3 = (f32[128]{0:T(128)S(1)}, f32[128]{0:T(128)}, u32[]{:S(2)}) copy-start(f32[128]{0:T(128)} %param.10) | copy-start | bytes 1540
  24.8 11.0 %copy-start.4 = (f32[128]{0:T(128)S(1)}, f32[128]{0:T(128)}, u32[]{:S(2)}) copy-start(f32[128]{0:T(128)} %param.11) | copy-start | bytes 1540
  35.6 5.8 %collective-permute-start.7 = (bf16[4,3,14,16,128]{4,3,2,1,0:T(8,128)(2,1)S(1)}, bf16[4,3,14,16,128]{4,3,2,1,0:T(8,128)(2,1)S(1)}, u32[]{:S(2)}, u32[]{:S(2)}) collective-permute-start(bf16[4,3,14,16,128]{4,3,2,1,0:T(8,128)(2,1)S(1)} %bitcast.24), channel_id=1, source_target_pairs={{0,4},{4,0},{8,12},{12,8},{1,5},{5,1},{9,13},{13,9},{2,6},{6,2},{1... | collective-permute-start | bytes 2064392 | tf_op jit(solution)/shard_map/ppermute | solution.py:94
  37.0 6.0 %collective-permute-start.10 = (f32[16,128]{1,0:T(8,128)S(1)}, f32[16,128]{1,0:T(8,128)S(1)}, u32[]{:S(2)}, u32[]{:S(2)}) collective-permute-start(f32[16,128]{1,0:T(8,128)S(1)} %bitcast.49), channel_id=1, source_target_pairs={{0,3},{1,2},{2,1},{3,0},{4,7},{5,6},{6,5},{7,4},{8,11},{9,10},{10,... | collective-permute-start | bytes 24584 | tf_op jit(solution)/shard_map/ppermute | solution.py:46
  37.6 5.4 %collective-permute-start.8 = (bf16[80,128]{1,0:T(8,128)(2,1)S(1)}, bf16[80,128]{1,0:T(8,128)(2,1)S(1)}, u32[]{:S(2)}, u32[]{:S(2)}) collective-permute-start(bf16[80,128]{1,0:T(8,128)(2,1)S(1)} %bitcast.48), channel_id=1, source_target_pairs={{0,2},{1,3},{2,0},{3,1},{4,6},{5,7},{6,4},{7,5},{8,10},{9,11},{10,... | collective-permute-start | bytes 61448 | tf_op jit(solution)/shard_map/ppermute | solution.py:44
  39.0 4.2 %collective-permute-start.9 = (bf16[80,128]{1,0:T(8,128)(2,1)S(1)}, bf16[80,128]{1,0:T(8,128)(2,1)S(1)}, u32[]{:S(2)}, u32[]{:S(2)}) collective-permute-start(bf16[80,128]{1,0:T(8,128)(2,1)S(1)} %bitcast.47), channel_id=1, source_target_pairs={{0,1},{1,0},{2,3},{3,2},{4,5},{5,4},{6,7},{7,6},{8,9},{9,8},{10,11... | collective-permute-start | bytes 61448 | tf_op jit(solution)/shard_map/ppermute | solution.py:45
  43.0 11.0 %copy-start = (bf16[256,128]{1,0:T(8,128)(2,1)S(1)}, bf16[256,128]{1,0:T(8,128)(2,1)}, u32[]{:S(2)}) copy-start(bf16[256,128]{1,0:T(8,128)(2,1)} %up.1) | copy-start | bytes 196612
  43.0 11.0 %copy-start.1 = (f32[256]{0:T(256)S(1)}, f32[256]{0:T(256)}, u32[]{:S(2)}) copy-start(f32[256]{0:T(256)} %param.13) | copy-start | bytes 3076
  43.0 11.0 %copy-start.2 = (f32[256]{0:T(256)S(1)}, f32[256]{0:T(256)}, u32[]{:S(2)}) copy-start(f32[256]{0:T(256)} %param.14) | copy-start | bytes 3076

commit v21 on v18

--- a/solution.py
+++ b/solution.py
@@ -95,7 +95,7 @@
 
 
 def share(stats):
-    return lax.all_to_all(stats, PART, 0, 0)
+    return lax.all_gather(stats[0], PART)
 
 
 def call(kernel, outs, scratch, *arrays, flops=0, nbytes=0, in_hbm=0, out_hbm=False):

time: 54.8 us -> 95.1 us (1.74)
  blocking collectives: 19.2 us -> 59 us
    all_gather x0 -> x2, blocking collectives: none -> 59 us  [share(): return lax.all_gather(stats[0], PART)]
    all_to_all x2 -> x0, blocking collectives: 19.2 us -> none  [share(): return lax.all_to_all(stats, PART, 0, 0)]
    ppermute x2, starting transfers between devices: 1.8 us -> 3.04 us  [halos(): y = lax.ppermute(y_edges[0], 'yx', self.swap_route(2))]
    ppermute x2, starting transfers between devices: 2.42 us -> 1.3 us  [halos(): x = lax.ppermute(x_edges[0], 'yx', self.swap_route(1))]
  transfers between devices with their start and end apart: 11 -> 11, of which waited for: 4 -> 4; matrix products, arithmetic and copies ran while one was open for 0% -> 0% of each run, Pallas kernels for 20% -> 11%
where the time goes in v21:
time: 95.1 us; the launch traced here: 95 us
  blocking collectives  59 us (62%)
  starting transfers between devices  17 us (18%)
  Pallas kernels  14.8 us (16%)
  waiting for transfers between devices  3.98 us (4%)
    all_gather x2, blocking collectives, share(): return lax.all_gather(stats[0], PART)  59 us
    pallas_call x10, Pallas kernels, call(): pl.pallas_call(kernel, out_shape=[jax.ShapeDtypeStruct(shape, dtype) for...  14.6 us
    ppermute x2, starting transfers between devices, halos(): corner = lax.ppermute(corners[0], 'yx', self.swap_route(3))  5.87 us
    ppermute x3, starting transfers between devices, swap(): lax.ppermute(block, axis, [(i, i ^ mask) for i in range(lax.axis_size(axi...  3.53 us
    ppermute x2, starting transfers between devices, halos(): y = lax.ppermute(y_edges[0], 'yx', self.swap_route(2))  3.04 us
    ppermute x1, starting transfers between devices, swap_depth(): lax.ppermute(inner, 'gz', routes[0])  2.56 us
    ppermute x2, waiting for transfers between devices, halos(): x = lax.ppermute(x_edges[0], 'yx', self.swap_route(1))  2.3 us
  transfers between devices with their start and end apart: 11, of which 4 were waited for; matrix products, arithmetic and copies ran while one was open for 0% of the time, Pallas kernels for 11%

profile of v21, /device:TPU:0, one launch (start us, length us, event | category | flops | bytes accessed | tf_op | source)
XLA Modules:
  0.0 95.0 jit_solution(7420884606687365090)
XLA Ops:
  0.0 1.6 %shard_map.82 = (bf16[1,30,16,128]{3,2,1,0:T(8,128)(2,1)S(1)}, bf16[1,30,16,128]{3,2,1,0:T(8,128)(2,1)S(1)}, bf16[1,15,16,128]{3,2,1,0:T(8,128)(2,1)S(1)}, bf16[...) custom-call(bf16[16,16,16,128]{3,2,1,0:T(8,128)(2,1)} %x_in.1, bf16[27,128,128]{2,1,0:T(8,128)(2,1)} %bitcast.50, ...), custom_call_target="tpu_custom_call" | custom-call | bytes 5242880 | tf_op jit(solution)/shard_map/pallas_call | solution.py:105
  1.6 5.1 %collective-permute-start.2 = (bf16[15,16,128]{2,1,0:T(8,128)(2,1)S(1)}, bf16[15,16,128]{2,1,0:T(8,128)(2,1)S(1)}, u32[]{:S(2)}, u32[]{:S(2)}) collective-permute-start(bf16[15,16,128]{2,1,0:T(8,128)(2,1)S(1)} %bitcast.46), channel_id=1, source_target_pairs={{0,3},{1,2},{2,1},{3,0},{4,7},{5,6},{6,5},{7,4},{8,11},{9,10},{10,... | collective-permute-start | bytes 184328 | tf_op jit(solution)/shard_map/ppermute | solution.py:46
  6.7 0.0 collective-permute-start.1
  6.7 0.6 collective-permute-start
  7.4 4.7 %shard_map.83 = (f32[16,16,16,128]{3,2,1,0:T(8,128)S(1)}, bf16[1152,384]{1,0:T(8,128)(2,1)S(1)}, bf16[1536,256]{1,0:T(8,128)(2,1)S(1)}, bf16[108,16,128]{2,1,0:T(8,128)(2,1)S(1)}) custom-call(bf16[108,16,128]{2,1,0:T(8,128)(2,1)} %bitcast.52, bf16[18,18,16,128]{3,2,1,0:T(8,128)(2,1)S(1)} %get-tuple-element.42.x, ...), custom_call_target="tpu_custom_call" | custom-call | flops 3623878656 | bytes 6291456 | tf_op jit(solution)/shard_map/pallas_call | solution.py:105
  12.1 0.0 collective-permute-done.2
  12.1 1.4 %collective-permute-done.1 = bf16[30,16,128]{2,1,0:T(8,128)(2,1)S(1)} collective-permute-done((bf16[30,16,128]{2,1,0:T(8,128)(2,1)S(1)}, bf16[30,16,128]{2,1,0:T(8,128)(2,1)S(1)}, u32[]{:S(2)}, u32[]{:S(2)}) %collective-permute-start.1) | collective-permute-done | bytes 122912 | tf_op jit(solution)/shard_map/ppermute | solution.py:45
  13.5 1.6 %collective-permute-done = bf16[30,16,128]{2,1,0:T(8,128)(2,1)S(1)} collective-permute-done((bf16[30,16,128]{2,1,0:T(8,128)(2,1)S(1)}, bf16[30,16,128]{2,1,0:T(8,128)(2,1)S(1)}, u32[]{:S(2)}, u32[]{:S(2)}) %collective-permute-start) | collective-permute-done | bytes 122912 | tf_op jit(solution)/shard_map/ppermute | solution.py:44
  15.1 0.1 shard_map.85
  15.2 0.7 collective-permute-start.4
  15.8 1.6 %collective-permute-start.5 = (bf16[1,4,14,16,128]{4,3,2,1,0:T(8,128)(2,1)S(1)}, bf16[1,4,14,16,128]{4,3,2,1,0:T(8,128)(2,1)S(1)}, u32[]{:S(2)}, u32[]{:S(2)}) collective-permute-start(bf16[1,4,14,16,128]{4,3,2,1,0:T(8,128)(2,1)S(1)} %bitcast.35), channel_id=1, source_target_pairs={{0,16},{16,0},{1,17},{17,1},{2,18},{18,2},{3,19},{19,3},{4,20},{20... | collective-permute-start | bytes 688136 | tf_op jit(solution)/shard_map/ppermute | solution.py:94
  17.5 2.6 %collective-permute-start.3 = (bf16[55,16,128]{2,1,0:T(8,128)(2,1)S(1)}, bf16[55,16,128]{2,1,0:T(8,128)(2,1)S(1)}, u32[]{:S(2)}, u32[]{:S(2)}) collective-permute-start(bf16[55,16,128]{2,1,0:T(8,128)(2,1)S(1)} %get-tuple-element.53), channel_id=1, source_target_pairs={{0,4},{4,0},{8,12},{12,8},{1,5},{5,1},{9,13},{13,9},{2,6},{6,2},{1... | collective-permute-start | bytes 675848 | tf_op jit(solution)/shard_map/ppermute | solution.py:63
  20.0 1.0 %shard_map.84 = (f32[14,16,16,128]{3,2,1,0:T(8,128)S(1)}, f32[4,16,16,128]{3,2,1,0:T(8,128)S(1)}, f32[16,128]{1,0:T(8,128)S(1)}) custom-call(f32[16,16,16,128]{3,2,1,0:T(8,128)S(1)} %get-tuple-element.45.own, bf16[1,30,16,128]{3,2,1,0:T(8,128)(2,1)S(1)} %bitcast.32, bf16[1,30,16,128]{3,2,1,0:T(8,128)(2,1)S(1)} %bitcast.30, ...), custom_call_target="tpu_custom_call" | custom-call | tf_op jit(solution)/shard_map/pallas_call | solution.py:105
  21.1 0.1 collective-permute-done.3.face
  21.1 1.1 %shard_map.86.ends = f32[6,16,16,128]{3,2,1,0:T(8,128)S(1)} custom-call(bf16[18,18,16,128]{3,2,1,0:T(8,128)(2,1)S(1)} %get-tuple-element.42.x, f32[4,16,16,128]{3,2,1,0:T(8,128)S(1)} %get-tuple-element.52.partial, bf16[55,16,128]{2,1,0:T(8,128)(2,1)S(1)} %collective-permute-done.3.face, bf16[1152,384]{1,0:T(8,128)(2,1)S(1)} %get-tuple-element.49.taps, ...), custom_call_target="tpu_custom_call" | custom-call | tf_op jit(solution)/shard_map/pallas_call | solution.py:105
  22.3 0.0 collective-permute-done.4.face
  22.3 1.2 %shard_map.87 = (f32[6,16,16,128]{3,2,1,0:T(8,128)S(1)}, f32[16,2,128]{2,1,0:T(2,128)S(1)}) custom-call(bf16[18,18,16,128]{3,2,1,0:T(8,128)(2,1)S(1)} %get-tuple-element.42.x, f32[16,128]{1,0:T(8,128)S(1)} %get-tuple-element.51.middle_stats, f32[6,16,16,128]{3,2,1,0:T(8,128)S(1)} %shard_map.86.ends, bf16[57,16,128]{2,1,0:T(8,128)(2,1)S(1)} %collective-permute-done.4.face, ...), custom_call_target="tpu_custom_call" | custom-call | tf_op jit(solution)/shard_map/pallas_call | solution.py:105
  23.5 0.0 copy-start.3
  23.5 0.0 copy-start.4
  23.5 0.0 collective-permute-done.5.refs_1_
  23.6 1.9 %collective-permute-start.6 = (bf16[2,3,14,16,128]{4,3,2,1,0:T(8,128)(2,1)S(1)}, bf16[2,3,14,16,128]{4,3,2,1,0:T(8,128)(2,1)S(1)}, u32[]{:S(2)}, u32[]{:S(2)}) collective-permute-start(bf16[2,3,14,16,128]{4,3,2,1,0:T(8,128)(2,1)S(1)} %bitcast.27), channel_id=1, source_target_pairs={{0,8},{4,12},{8,0},{12,4},{1,9},{5,13},{9,1},{13,5},{2,10},{6,14},... | collective-permute-start | bytes 1032200 | tf_op jit(solution)/shard_map/ppermute | solution.py:94
  25.4 29.1 %all_gather.6.stats = f32[16,2,128]{2,1,0:T(2,128)S(1)} all-gather(f32[1,2,128]{2,1,0:T(2,128)S(1)} %slice.6), channel_id=1, replica_groups=mesh['cand'=2,'gz'=4,'yx'=4] {'gz','yx'}, dimensions={0}, use_global_device_ids=true | all-gather | bytes 17408 | tf_op jit(solution)/shard_map/all_gather | solution.py:98
  54.5 0.0 collective-permute-done.6.refs_1_
  54.6 0.1 collective-permute-start.7
  54.7 0.0 copy-done.3
  54.7 0.0 copy-done.4
  54.7 1.1 %shard_map.89 = (bf16[16,16,16,128]{3,2,1,0:T(8,128)(2,1)S(1)}, f32[10,8,8,128]{3,2,1,0:T(8,128)S(1)}, bf16[1,80,128]{2,1,0:T(8,128)(2,1)S(1)}, bf16[1,80,128]{2,1,0:T(8,128)(2,1)S(1)}, f32[1,16,128]{2,1,0:T(8,128)S(1)}) custom-call(f32[14,16,16,128]{3,2,1,0:T(8,128)S(1)} %get-tuple-element.50.inner, f32[6,16,16,128]{3,2,1,0:T(8,128)S(1)} %get-tuple-element.56.ends, ...), custom_call_target="tpu_custom_call" | custom-call | flops 10485760 | bytes 3145728 | tf_op jit(solution)/shard_map/pallas_call | solution.py:105
  55.9 0.8 collective-permute-start.10
  56.6 2.4 %collective-permute-start.8 = (bf16[80,128]{1,0:T(8,128)(2,1)S(1)}, bf16[80,128]{1,0:T(8,128)(2,1)S(1)}, u32[]{:S(2)}, u32[]{:S(2)}) collective-permute-start(bf16[80,128]{1,0:T(8,128)(2,1)S(1)} %bitcast.48), channel_id=1, source_target_pairs={{0,2},{1,3},{2,0},{3,1},{4,6},{5,7},{6,4},{7,5},{8,10},{9,11},{10,... | collective-permute-start | bytes 61448 | tf_op jit(solution)/shard_map/ppermute | solution.py:44
  59.0 1.3 %collective-permute-start.9 = (bf16[80,128]{1,0:T(8,128)(2,1)S(1)}, bf16[80,128]{1,0:T(8,128)(2,1)S(1)}, u32[]{:S(2)}, u32[]{:S(2)}) collective-permute-start(bf16[80,128]{1,0:T(8,128)(2,1)S(1)} %bitcast.47), channel_id=1, source_target_pairs={{0,1},{1,0},{2,3},{3,2},{4,5},{5,4},{6,7},{7,6},{8,9},{9,8},{10,11... | collective-permute-start | bytes 61448 | tf_op jit(solution)/shard_map/ppermute | solution.py:45
  60.3 0.0 collective-permute-done.7.refs_1_
  60.3 0.1 shard_map.91
  60.4 1.4 %shard_map.92 = (f32[2,512,128]{2,1,0:T(8,128)S(1)}, bf16[4,108,16,128]{3,2,1,0:T(8,128)(2,1)S(1)}) custom-call(f32[10,8,8,128]{3,2,1,0:T(8,128)S(1)} %get-tuple-element.62.pooled, bf16[108,16,128]{2,1,0:T(8,128)(2,1)S(1)} %get-tuple-element.63.own, bf16[8,3,14,16,128]{4,3,2,1,0:T(8,128)(2,1)S(1)} %bitcast.26), custom_call_target="tpu_custom_call" | custom-call | flops 905969664 | bytes 4194304 | tf_op jit(solution)/shard_map/pallas_call | solution.py:105
  61.8 0.0 copy-start
  61.8 0.0 copy-start.1
  61.9 0.0 copy-start.2
  61.9 0.0 collective-permute-done.10
  61.9 0.0 collective-permute-done.8
  61.9 0.9 collective-permute-done.9
  62.8 0.7 shard_map.93
  63.5 29.9 %all_gather.7.stats = f32[16,2,256]{2,1,0:T(2,128)S(1)} all-gather(f32[1,2,256]{2,1,0:T(2,128)S(1)} %slice.7), channel_id=1, replica_groups=mesh['cand'=2,'gz'=4,'yx'=4] {'gz','yx'}, dimensions={0}, use_global_device_ids=true | all-gather | bytes 34816 | tf_op jit(solution)/shard_map/all_gather | solution.py:98
  93.4 0.0 copy-done
  93.4 0.0 copy-done.1
  93.4 0.0 copy-done.2
  93.4 1.5 %shard_map.94 = bf16[16,16,16,128]{3,2,1,0:T(8,128)(2,1)} custom-call(f32[2,512,128]{2,1,0:T(8,128)S(1)} %get-tuple-element.70.act, f32[16,2,256]{2,1,0:T(2,128)S(1)} %all_gather.7.stats, f32[1,256]{1,0:T(1,128)S(1)} %bitcast.40, f32[1,256]{1,0:T(1,128)S(1)} %bitcast.41, bf16[256,128]{1,0:T(8,128)(2,1)S(1)} %copy-done, ...), custom_call_target="tpu_custom_call" | custom-call | flops 67108864 | bytes 3145728 | tf_op jit(solution)/shard_map/pallas_call | solution.py:105
  (4 shorter events, 0.1 us)
Async XLA Ops:
  1.6 10.5 %collective-permute-start.2 = (bf16[15,16,128]{2,1,0:T(8,128)(2,1)S(1)}, bf16[15,16,128]{2,1,0:T(8,128)(2,1)S(1)}, u32[]{:S(2)}, u32[]{:S(2)}) collective-permute-start(bf16[15,16,128]{2,1,0:T(8,128)(2,1)S(1)} %bitcast.46), channel_id=1, source_target_pairs={{0,3},{1,2},{2,1},{3,0},{4,7},{5,6},{6,5},{7,4},{8,11},{9,10},{10,... | collective-permute-start | bytes 184328 | tf_op jit(solution)/shard_map/ppermute | solution.py:46
  6.7 6.8 %collective-permute-start.1 = (bf16[30,16,128]{2,1,0:T(8,128)(2,1)S(1)}, bf16[30,16,128]{2,1,0:T(8,128)(2,1)S(1)}, u32[]{:S(2)}, u32[]{:S(2)}) collective-permute-start(bf16[30,16,128]{2,1,0:T(8,128)(2,1)S(1)} %bitcast.45), channel_id=1, source_target_pairs={{0,1},{1,0},{2,3},{3,2},{4,5},{5,4},{6,7},{7,6},{8,9},{9,8},{10,11... | collective-permute-start | bytes 368648 | tf_op jit(solution)/shard_map/ppermute | solution.py:45
  6.7 8.4 %collective-permute-start = (bf16[30,16,128]{2,1,0:T(8,128)(2,1)S(1)}, bf16[30,16,128]{2,1,0:T(8,128)(2,1)S(1)}, u32[]{:S(2)}, u32[]{:S(2)}) collective-permute-start(bf16[30,16,128]{2,1,0:T(8,128)(2,1)S(1)} %bitcast.44), channel_id=1, source_target_pairs={{0,2},{1,3},{2,0},{3,1},{4,6},{5,7},{6,4},{7,5},{8,10},{9,11},{10,... | collective-permute-start | bytes 368648 | tf_op jit(solution)/shard_map/ppermute | solution.py:44
  15.2 7.1 %collective-permute-start.4 = (bf16[57,16,128]{2,1,0:T(8,128)(2,1)S(1)}, bf16[57,16,128]{2,1,0:T(8,128)(2,1)S(1)}, u32[]{:S(2)}, u32[]{:S(2)}) collective-permute-start(bf16[57,16,128]{2,1,0:T(8,128)(2,1)S(1)} %get-tuple-element.55), channel_id=1, source_target_pairs={{4,8},{8,4},{5,9},{9,5},{6,10},{10,6},{7,11},{11,7},{20,24},{24,20... | collective-permute-start | bytes 700424 | tf_op jit(solution)/shard_map/ppermute | solution.py:63
  15.8 7.7 %collective-permute-start.5 = (bf16[1,4,14,16,128]{4,3,2,1,0:T(8,128)(2,1)S(1)}, bf16[1,4,14,16,128]{4,3,2,1,0:T(8,128)(2,1)S(1)}, u32[]{:S(2)}, u32[]{:S(2)}) collective-permute-start(bf16[1,4,14,16,128]{4,3,2,1,0:T(8,128)(2,1)S(1)} %bitcast.35), channel_id=1, source_target_pairs={{0,16},{16,0},{1,17},{17,1},{2,18},{18,2},{3,19},{19,3},{4,20},{20... | collective-permute-start | bytes 688136 | tf_op jit(solution)/shard_map/ppermute | solution.py:94
  17.5 3.7 %collective-permute-start.3 = (bf16[55,16,128]{2,1,0:T(8,128)(2,1)S(1)}, bf16[55,16,128]{2,1,0:T(8,128)(2,1)S(1)}, u32[]{:S(2)}, u32[]{:S(2)}) collective-permute-start(bf16[55,16,128]{2,1,0:T(8,128)(2,1)S(1)} %get-tuple-element.53), channel_id=1, source_target_pairs={{0,4},{4,0},{8,12},{12,8},{1,5},{5,1},{9,13},{13,9},{2,6},{6,2},{1... | collective-permute-start | bytes 675848 | tf_op jit(solution)/shard_map/ppermute | solution.py:63
  23.5 31.2 %copy-start.3 = (f32[128]{0:T(128)S(1)}, f32[128]{0:T(128)}, u32[]{:S(2)}) copy-start(f32[128]{0:T(128)} %param.10) | copy-start | bytes 1540
  23.5 31.2 %copy-start.4 = (f32[128]{0:T(128)S(1)}, f32[128]{0:T(128)}, u32[]{:S(2)}) copy-start(f32[128]{0:T(128)} %param.11) | copy-start | bytes 1540
  23.6 31.0 %collective-permute-start.6 = (bf16[2,3,14,16,128]{4,3,2,1,0:T(8,128)(2,1)S(1)}, bf16[2,3,14,16,128]{4,3,2,1,0:T(8,128)(2,1)S(1)}, u32[]{:S(2)}, u32[]{:S(2)}) collective-permute-start(bf16[2,3,14,16,128]{4,3,2,1,0:T(8,128)(2,1)S(1)} %bitcast.27), channel_id=1, source_target_pairs={{0,8},{4,12},{8,0},{12,4},{1,9},{5,13},{9,1},{13,5},{2,10},{6,14},... | collective-permute-start | bytes 1032200 | tf_op jit(solution)/shard_map/ppermute | solution.py:94
  54.6 5.7 %collective-permute-start.7 = (bf16[4,3,14,16,128]{4,3,2,1,0:T(8,128)(2,1)S(1)}, bf16[4,3,14,16,128]{4,3,2,1,0:T(8,128)(2,1)S(1)}, u32[]{:S(2)}, u32[]{:S(2)}) collective-permute-start(bf16[4,3,14,16,128]{4,3,2,1,0:T(8,128)(2,1)S(1)} %bitcast.24), channel_id=1, source_target_pairs={{0,4},{4,0},{8,12},{12,8},{1,5},{5,1},{9,13},{13,9},{2,6},{6,2},{1... | collective-permute-start | bytes 2064392 | tf_op jit(solution)/shard_map/ppermute | solution.py:94
  55.9 6.0 %collective-permute-start.10 = (f32[16,128]{1,0:T(8,128)S(1)}, f32[16,128]{1,0:T(8,128)S(1)}, u32[]{:S(2)}, u32[]{:S(2)}) collective-permute-start(f32[16,128]{1,0:T(8,128)S(1)} %bitcast.49), channel_id=1, source_target_pairs={{0,3},{1,2},{2,1},{3,0},{4,7},{5,6},{6,5},{7,4},{8,11},{9,10},{10,... | collective-permute-start | bytes 24584 | tf_op jit(solution)/shard_map/ppermute | solution.py:46
  56.6 5.3 %collective-permute-start.8 = (bf16[80,128]{1,0:T(8,128)(2,1)S(1)}, bf16[80,128]{1,0:T(8,128)(2,1)S(1)}, u32[]{:S(2)}, u32[]{:S(2)}) collective-permute-start(bf16[80,128]{1,0:T(8,128)(2,1)S(1)} %bitcast.48), channel_id=1, source_target_pairs={{0,2},{1,3},{2,0},{3,1},{4,6},{5,7},{6,4},{7,5},{8,10},{9,11},{10,... | collective-permute-start | bytes 61448 | tf_op jit(solution)/shard_map/ppermute | solution.py:44
  59.0 3.8 %collective-permute-start.9 = (bf16[80,128]{1,0:T(8,128)(2,1)S(1)}, bf16[80,128]{1,0:T(8,128)(2,1)S(1)}, u32[]{:S(2)}, u32[]{:S(2)}) collective-permute-start(bf16[80,128]{1,0:T(8,128)(2,1)S(1)} %bitcast.47), channel_id=1, source_target_pairs={{0,1},{1,0},{2,3},{3,2},{4,5},{5,4},{6,7},{7,6},{8,9},{9,8},{10,11... | collective-permute-start | bytes 61448 | tf_op jit(solution)/shard_map/ppermute | solution.py:45
  61.8 31.6 %copy-start = (bf16[256,128]{1,0:T(8,128)(2,1)S(1)}, bf16[256,128]{1,0:T(8,128)(2,1)}, u32[]{:S(2)}) copy-start(bf16[256,128]{1,0:T(8,128)(2,1)} %up.1) | copy-start | bytes 196612
  61.8 31.6 %copy-start.1 = (f32[256]{0:T(256)S(1)}, f32[256]{0:T(256)}, u32[]{:S(2)}) copy-start(f32[256]{0:T(256)} %param.13) | copy-start | bytes 3076
  61.9 31.6 %copy-start.2 = (f32[256]{0:T(256)S(1)}, f32[256]{0:T(256)}, u32[]{:S(2)}) copy-start(f32[256]{0:T(256)} %param.14) | copy-start | bytes 3076

commit v22 on v18

--- a/solution.py
+++ b/solution.py
@@ -364,7 +364,7 @@
     stats[8:16] = spread
 
 
-def add_face(ny, nx, behind, face, x, taps, pairs, ends, three, grid, column):
+def add_face(ny, nx, behind, face, x, taps, pairs, ends, three, grid, column, beyond=True):
     edge = x.shape[2]
     wide_face = edge + ny + nx
     f32 = jnp.float32
@@ -382,7 +382,8 @@
     def put(z, new):
         three[pl.ds(first + z, new.shape[0])] += new
 
-    convolve(grid, 2, taps, pairs, put)
+    if beyond:
+        convolve(grid, 2, taps, pairs, put)
     beside = jnp.where(behind, 1, 2)
     lines = [grid[beside, dy : dy + edge].reshape(edge * edge, 128) for dy in range(3)]
     rows = taps[pl.ds(pl.multiple_of(jnp.where(behind, 768, 0), 128), 384), :]
@@ -427,7 +428,7 @@
     edge = x.shape[2]
     act[...] = ends[...]
     behind = lax.axis_index("gz") % 2 == 1
-    add_face(ny, nx, behind, face, x, taps, pairs, act, three, grid, column)
+    add_face(ny, nx, behind, face, x, taps, pairs, act, three, grid, column, beyond=False)
     mean, spread = moments(act.at[2:4])
     few, many = edge * edge // 4, (edge - 2) * edge * edge // 8
     middle_mean, middle_spread = middle_stats[0:8], middle_stats[8:16]
@@ -435,6 +436,30 @@
     part = few / (few + many)
     spread = spread + middle_spread + (many * part) * (off * off)
     put_stats(stats, middle_mean - part * off, spread, few + many)
+
+
+def beyond_kernel(ny, nx, x, ends, face, taps, pairs, act, grid):
+    edge = x.shape[2]
+    wide_face = edge + ny + nx
+    depth_at = lax.axis_index("gz")
+    behind = depth_at % 2 == 1
+    act[...] = ends[...]
+
+    @pl.when(jnp.where(behind, depth_at < lax.axis_size("gz") - 1, depth_at > 0))
+    def _():
+        blank = jnp.zeros(grid.shape[:1] + grid.shape[2:], grid.dtype)
+        grid[:, 0] = blank
+        grid[:, edge + 1] = blank
+        first = jnp.where(behind, 1, 0)
+        for k in range(3):
+            grid[first + k, 1 : edge + 1] = face[k * wide_face : k * wide_face + edge]
+        own = jnp.where(behind, edge, 1)
+        grid[jnp.where(behind, 0, 3), 1 : edge + 1] = x[own, 1 : edge + 1]
+
+        def put(z, new):
+            act[pl.ds(jnp.where(behind, 4, 0) + z, new.shape[0])] += new
+
+        convolve(grid, 2, taps, pairs, put)
 
 
 def merge(mean, spread, rows, other_mean, other_spread):
@@ -799,13 +824,25 @@
         stats, other = lax.optimization_barrier((stats, other))
         held = stack(held, other, part=(1, 3)).reshape((2, 3) + held.shape[2:])
         other = swap(held, *riders.STEPS[1])
-        stats = share(stats)
+    (ends,) = call(
+        functools.partial(beyond_kernel, ny, nx),
+        [six],
+        room[1:2],
+        field,
+        ends,
+        outer,
+        taps,
+        pairs,
+        flops=conv_flops,
+        nbytes=4 << 20,
+    )
+    stats, ends = lax.optimization_barrier((stats, ends))
+    stats = share(stats)
+    if riders.size:
         stats, other = lax.optimization_barrier((stats, other))
         held = stack(held, other).reshape((-1,) + held.shape[1:])
         other = swap(held, *riders.STEPS[2])
         held = [stack(held, other).reshape((-1,) + held.shape[1:])]
-    else:
-        stats = share(stats)
     out, pooled, *edges = call(
         functools.partial(norm_kernel, ny, nx),
         [

time: 54.8 us -> 54.6 us (level)
    pallas_call x10 -> x11, Pallas kernels: 14.6 us -> 14 us  [call(): pl.pallas_call(kernel, out_shape=[jax.ShapeDtypeStruct(shape, dtype) for...]
  transfers between devices with their start and end apart: 11 -> 11, of which waited for: 4 -> 4; matrix products, arithmetic and copies ran while one was open for 0% -> 0% of each run, Pallas kernels for 20% -> 19%
where the time goes in v22:
time: 54.6 us; the launch traced here: 54.4 us
  blocking collectives  19.6 us (36%)
  starting transfers between devices  17.1 us (31%)
  Pallas kernels  14.2 us (26%)
  waiting for transfers between devices  3.26 us (6%)
    all_to_all x2, blocking collectives, share(): return lax.all_to_all(stats, PART, 0, 0)  19.6 us
    pallas_call x11, Pallas kernels, call(): pl.pallas_call(kernel, out_shape=[jax.ShapeDtypeStruct(shape, dtype) for...  14 us
    ppermute x2, starting transfers between devices, halos(): corner = lax.ppermute(corners[0], 'yx', self.swap_route(3))  5.86 us
    ppermute x3, starting transfers between devices, swap(): lax.ppermute(block, axis, [(i, i ^ mask) for i in range(lax.axis_size(axi...  3.63 us
    ppermute x1, starting transfers between devices, swap_depth(): lax.ppermute(inner, 'gz', routes[0])  2.56 us
    ppermute x2, starting transfers between devices, halos(): x = lax.ppermute(x_edges[0], 'yx', self.swap_route(1))  2.42 us
    ppermute x2, starting transfers between devices, halos(): y = lax.ppermute(y_edges[0], 'yx', self.swap_route(2))  1.96 us
    ppermute x2, waiting for transfers between devices, halos(): y = lax.ppermute(y_edges[0], 'yx', self.swap_route(2))  1.59 us
  transfers between devices with their start and end apart: 11, of which 4 were waited for; matrix products, arithmetic and copies ran while one was open for 0% of the time, Pallas kernels for 19%

profile of v22, /device:TPU:0, one launch (start us, length us, event | category | flops | bytes accessed | tf_op | source)
XLA Modules:
  0.0 54.4 jit_solution(6445003782387765110)
XLA Ops:
  0.0 1.6 %shard_map.82 = (bf16[1,30,16,128]{3,2,1,0:T(8,128)(2,1)S(1)}, bf16[1,30,16,128]{3,2,1,0:T(8,128)(2,1)S(1)}, bf16[1,15,16,128]{3,2,1,0:T(8,128)(2,1)S(1)}, bf16[...) custom-call(bf16[16,16,16,128]{3,2,1,0:T(8,128)(2,1)} %x_in.1, bf16[27,128,128]{2,1,0:T(8,128)(2,1)} %bitcast.50, ...), custom_call_target="tpu_custom_call" | custom-call | bytes 5242880 | tf_op jit(solution)/shard_map/pallas_call | solution.py:105
  1.6 5.1 %collective-permute-start.2 = (bf16[15,16,128]{2,1,0:T(8,128)(2,1)S(1)}, bf16[15,16,128]{2,1,0:T(8,128)(2,1)S(1)}, u32[]{:S(2)}, u32[]{:S(2)}) collective-permute-start(bf16[15,16,128]{2,1,0:T(8,128)(2,1)S(1)} %bitcast.46), channel_id=1, source_target_pairs={{0,3},{1,2},{2,1},{3,0},{4,7},{5,6},{6,5},{7,4},{8,11},{9,10},{10,... | collective-permute-start | bytes 184328 | tf_op jit(solution)/shard_map/ppermute | solution.py:46
  6.7 0.0 collective-permute-start.1
  6.7 0.6 %collective-permute-start = (bf16[30,16,128]{2,1,0:T(8,128)(2,1)S(1)}, bf16[30,16,128]{2,1,0:T(8,128)(2,1)S(1)}, u32[]{:S(2)}, u32[]{:S(2)}) collective-permute-start(bf16[30,16,128]{2,1,0:T(8,128)(2,1)S(1)} %bitcast.44), channel_id=1, source_target_pairs={{0,2},{1,3},{2,0},{3,1},{4,6},{5,7},{6,4},{7,5},{8,10},{9,11},{10,... | collective-permute-start | bytes 368648 | tf_op jit(solution)/shard_map/ppermute | solution.py:44
  7.4 4.7 %shard_map.83 = (f32[16,16,16,128]{3,2,1,0:T(8,128)S(1)}, bf16[1152,384]{1,0:T(8,128)(2,1)S(1)}, bf16[1536,256]{1,0:T(8,128)(2,1)S(1)}, bf16[108,16,128]{2,1,0:T(8,128)(2,1)S(1)}) custom-call(bf16[108,16,128]{2,1,0:T(8,128)(2,1)} %bitcast.52, bf16[18,18,16,128]{3,2,1,0:T(8,128)(2,1)S(1)} %get-tuple-element.44.x, ...), custom_call_target="tpu_custom_call" | custom-call | flops 3623878656 | bytes 6291456 | tf_op jit(solution)/shard_map/pallas_call | solution.py:105
  12.1 0.0 collective-permute-done.2
  12.1 1.4 %collective-permute-done.1 = bf16[30,16,128]{2,1,0:T(8,128)(2,1)S(1)} collective-permute-done((bf16[30,16,128]{2,1,0:T(8,128)(2,1)S(1)}, bf16[30,16,128]{2,1,0:T(8,128)(2,1)S(1)}, u32[]{:S(2)}, u32[]{:S(2)}) %collective-permute-start.1) | collective-permute-done | bytes 122912 | tf_op jit(solution)/shard_map/ppermute | solution.py:45
  13.5 1.6 %collective-permute-done = bf16[30,16,128]{2,1,0:T(8,128)(2,1)S(1)} collective-permute-done((bf16[30,16,128]{2,1,0:T(8,128)(2,1)S(1)}, bf16[30,16,128]{2,1,0:T(8,128)(2,1)S(1)}, u32[]{:S(2)}, u32[]{:S(2)}) %collective-permute-start) | collective-permute-done | bytes 122912 | tf_op jit(solution)/shard_map/ppermute | solution.py:44
  15.1 0.1 shard_map.85
  15.2 0.7 %collective-permute-start.4 = (bf16[57,16,128]{2,1,0:T(8,128)(2,1)S(1)}, bf16[57,16,128]{2,1,0:T(8,128)(2,1)S(1)}, u32[]{:S(2)}, u32[]{:S(2)}) collective-permute-start(bf16[57,16,128]{2,1,0:T(8,128)(2,1)S(1)} %get-tuple-element.57), channel_id=1, source_target_pairs={{4,8},{8,4},{5,9},{9,5},{6,10},{10,6},{7,11},{11,7},{20,24},{24,20... | collective-permute-start | bytes 700424 | tf_op jit(solution)/shard_map/ppermute | solution.py:63
  15.8 1.6 %collective-permute-start.5 = (bf16[1,4,14,16,128]{4,3,2,1,0:T(8,128)(2,1)S(1)}, bf16[1,4,14,16,128]{4,3,2,1,0:T(8,128)(2,1)S(1)}, u32[]{:S(2)}, u32[]{:S(2)}) collective-permute-start(bf16[1,4,14,16,128]{4,3,2,1,0:T(8,128)(2,1)S(1)} %bitcast.35), channel_id=1, source_target_pairs={{0,16},{16,0},{1,17},{17,1},{2,18},{18,2},{3,19},{19,3},{4,20},{20... | collective-permute-start | bytes 688136 | tf_op jit(solution)/shard_map/ppermute | solution.py:94
  17.5 2.6 %collective-permute-start.3 = (bf16[55,16,128]{2,1,0:T(8,128)(2,1)S(1)}, bf16[55,16,128]{2,1,0:T(8,128)(2,1)S(1)}, u32[]{:S(2)}, u32[]{:S(2)}) collective-permute-start(bf16[55,16,128]{2,1,0:T(8,128)(2,1)S(1)} %get-tuple-element.55), channel_id=1, source_target_pairs={{0,4},{4,0},{8,12},{12,8},{1,5},{5,1},{9,13},{13,9},{2,6},{6,2},{1... | collective-permute-start | bytes 675848 | tf_op jit(solution)/shard_map/ppermute | solution.py:63
  20.0 1.0 %shard_map.84 = (f32[14,16,16,128]{3,2,1,0:T(8,128)S(1)}, f32[4,16,16,128]{3,2,1,0:T(8,128)S(1)}, f32[16,128]{1,0:T(8,128)S(1)}) custom-call(f32[16,16,16,128]{3,2,1,0:T(8,128)S(1)} %get-tuple-element.47.own, bf16[1,30,16,128]{3,2,1,0:T(8,128)(2,1)S(1)} %bitcast.32, bf16[1,30,16,128]{3,2,1,0:T(8,128)(2,1)S(1)} %bitcast.30, ...), custom_call_target="tpu_custom_call" | custom-call | tf_op jit(solution)/shard_map/pallas_call | solution.py:105
  21.1 0.1 collective-permute-done.3.face
  21.1 1.1 %shard_map.86.ends = f32[6,16,16,128]{3,2,1,0:T(8,128)S(1)} custom-call(bf16[18,18,16,128]{3,2,1,0:T(8,128)(2,1)S(1)} %get-tuple-element.44.x, f32[4,16,16,128]{3,2,1,0:T(8,128)S(1)} %get-tuple-element.54.partial, bf16[55,16,128]{2,1,0:T(8,128)(2,1)S(1)} %collective-permute-done.3.face, bf16[1152,384]{1,0:T(8,128)(2,1)S(1)} %get-tuple-element.51.taps, ...), custom_call_target="tpu_custom_call" | custom-call | tf_op jit(solution)/shard_map/pallas_call | solution.py:105
  22.3 0.0 collective-permute-done.4.face
  22.3 0.6 %shard_map.87 = (f32[6,16,16,128]{3,2,1,0:T(8,128)S(1)}, f32[16,2,128]{2,1,0:T(2,128)S(1)}) custom-call(bf16[18,18,16,128]{3,2,1,0:T(8,128)(2,1)S(1)} %get-tuple-element.44.x, f32[16,128]{1,0:T(8,128)S(1)} %get-tuple-element.53.middle_stats, f32[6,16,16,128]{3,2,1,0:T(8,128)S(1)} %shard_map.86.ends, bf16[57,16,128]{2,1,0:T(8,128)(2,1)S(1)} %collective-permute-done.4.face, ...), custom_call_target="tpu_custom_call" | custom-call | tf_op jit(solution)/shard_map/pallas_call | solution.py:105
  22.9 0.0 collective-permute-done.5.refs_1_
  23.0 1.9 %collective-permute-start.6 = (bf16[2,3,14,16,128]{4,3,2,1,0:T(8,128)(2,1)S(1)}, bf16[2,3,14,16,128]{4,3,2,1,0:T(8,128)(2,1)S(1)}, u32[]{:S(2)}, u32[]{:S(2)}) collective-permute-start(bf16[2,3,14,16,128]{4,3,2,1,0:T(8,128)(2,1)S(1)} %bitcast.27), channel_id=1, source_target_pairs={{0,8},{4,12},{8,0},{12,4},{1,9},{5,13},{9,1},{13,5},{2,10},{6,14},... | collective-permute-start | bytes 1032200 | tf_op jit(solution)/shard_map/ppermute | solution.py:94
  24.8 0.0 copy-start.3
  24.8 0.0 copy-start.4
  24.8 0.1 shard_map.88.ends
  24.9 9.6 %all_to_all.10.stats = f32[16,2,128]{2,1,0:T(2,128)S(1)} all-to-all(f32[16,2,128]{2,1,0:T(2,128)S(1)} %get-tuple-element.63), channel_id=1, replica_groups=mesh['cand'=2,'gz'=4,'yx'=4] {'gz','yx'}, dimensions={0} | all-to-all | bytes 32768 | tf_op jit(solution)/shard_map/all_to_all | solution.py:98
  34.5 0.0 collective-permute-done.6.refs_1_
  34.5 0.2 collective-permute-start.7
  34.7 0.0 copy-done.3
  34.7 0.0 copy-done.4
  34.7 1.1 %shard_map.90 = (bf16[16,16,16,128]{3,2,1,0:T(8,128)(2,1)S(1)}, f32[10,8,8,128]{3,2,1,0:T(8,128)S(1)}, bf16[1,80,128]{2,1,0:T(8,128)(2,1)S(1)}, bf16[1,80,128]{2,1,0:T(8,128)(2,1)S(1)}, f32[1,16,128]{2,1,0:T(8,128)S(1)}) custom-call(f32[14,16,16,128]{3,2,1,0:T(8,128)S(1)} %get-tuple-element.52.inner, f32[6,16,16,128]{3,2,1,0:T(8,128)S(1)} %shard_map.88.ends, ...), custom_call_target="tpu_custom_call" | custom-call | flops 10485760 | bytes 3145728 | tf_op jit(solution)/shard_map/pallas_call | solution.py:105
  35.9 0.7 %collective-permute-start.10 = (f32[16,128]{1,0:T(8,128)S(1)}, f32[16,128]{1,0:T(8,128)S(1)}, u32[]{:S(2)}, u32[]{:S(2)}) collective-permute-start(f32[16,128]{1,0:T(8,128)S(1)} %bitcast.49), channel_id=1, source_target_pairs={{0,3},{1,2},{2,1},{3,0},{4,7},{5,6},{6,5},{7,4},{8,11},{9,10},{10,... | collective-permute-start | bytes 24584 | tf_op jit(solution)/shard_map/ppermute | solution.py:46
  36.6 1.3 %collective-permute-start.8 = (bf16[80,128]{1,0:T(8,128)(2,1)S(1)}, bf16[80,128]{1,0:T(8,128)(2,1)S(1)}, u32[]{:S(2)}, u32[]{:S(2)}) collective-permute-start(bf16[80,128]{1,0:T(8,128)(2,1)S(1)} %bitcast.48), channel_id=1, source_target_pairs={{0,2},{1,3},{2,0},{3,1},{4,6},{5,7},{6,4},{7,5},{8,10},{9,11},{10,... | collective-permute-start | bytes 61448 | tf_op jit(solution)/shard_map/ppermute | solution.py:44
  37.9 2.4 %collective-permute-start.9 = (bf16[80,128]{1,0:T(8,128)(2,1)S(1)}, bf16[80,128]{1,0:T(8,128)(2,1)S(1)}, u32[]{:S(2)}, u32[]{:S(2)}) collective-permute-start(bf16[80,128]{1,0:T(8,128)(2,1)S(1)} %bitcast.47), channel_id=1, source_target_pairs={{0,1},{1,0},{2,3},{3,2},{4,5},{5,4},{6,7},{7,6},{8,9},{9,8},{10,11... | collective-permute-start | bytes 61448 | tf_op jit(solution)/shard_map/ppermute | solution.py:45
  40.3 0.0 collective-permute-done.7.refs_1_
  40.3 0.1 shard_map.92
  40.4 1.4 %shard_map.93 = (f32[2,512,128]{2,1,0:T(8,128)S(1)}, bf16[4,108,16,128]{3,2,1,0:T(8,128)(2,1)S(1)}) custom-call(f32[10,8,8,128]{3,2,1,0:T(8,128)S(1)} %get-tuple-element.66.pooled, bf16[108,16,128]{2,1,0:T(8,128)(2,1)S(1)} %get-tuple-element.67.own, bf16[8,3,14,16,128]{4,3,2,1,0:T(8,128)(2,1)S(1)} %bitcast.26), custom_call_target="tpu_custom_call" | custom-call | flops 905969664 | bytes 4194304 | tf_op jit(solution)/shard_map/pallas_call | solution.py:105
  41.9 0.0 copy-start
  41.9 0.0 copy-start.1
  41.9 0.0 copy-start.2
  41.9 0.0 collective-permute-done.10
  41.9 0.0 collective-permute-done.8
  41.9 0.2 collective-permute-done.9
  42.1 0.7 %shard_map.94 = (f32[2,512,128]{2,1,0:T(8,128)S(1)}, f32[16,2,256]{2,1,0:T(2,128)S(1)}) custom-call(f32[2,512,128]{2,1,0:T(8,128)S(1)} %get-tuple-element.69.own, bf16[1,80,128]{2,1,0:T(8,128)(2,1)S(1)} %bitcast.37, bf16[1,80,128]{2,1,0:T(8,128)(2,1)S(1)} %bitcast.38, f32[1,16,128]{2,1,0:T(8,128)S(1)} %bitcast.39, ...), custom_call_target="tpu_custom_call" | custom-call | flops 67108864 | bytes 3145728 | tf_op jit(solution)/shard_map/pallas_call | solution.py:105
  42.8 10.0 %all_to_all.11.stats = f32[16,2,256]{2,1,0:T(2,128)S(1)} all-to-all(f32[16,2,256]{2,1,0:T(2,128)S(1)} %get-tuple-element.75), channel_id=1, replica_groups=mesh['cand'=2,'gz'=4,'yx'=4] {'gz','yx'}, dimensions={0} | all-to-all | bytes 65536 | tf_op jit(solution)/shard_map/all_to_all | solution.py:98
  52.9 0.0 copy-done
  52.9 0.0 copy-done.1
  52.9 0.0 copy-done.2
  52.9 1.5 %shard_map.95 = bf16[16,16,16,128]{3,2,1,0:T(8,128)(2,1)} custom-call(f32[2,512,128]{2,1,0:T(8,128)S(1)} %get-tuple-element.74.act, f32[16,2,256]{2,1,0:T(2,128)S(1)} %all_to_all.11.stats, f32[1,256]{1,0:T(1,128)S(1)} %bitcast.40, f32[1,256]{1,0:T(1,128)S(1)} %bitcast.41, bf16[256,128]{1,0:T(8,128)(2,1)S(1)} %copy-done, ...), custom_call_target="tpu_custom_call" | custom-call | flops 67108864 | bytes 3145728 | tf_op jit(solution)/shard_map/pallas_call | solution.py:105
  (2 shorter events, 0.1 us)
Async XLA Ops:
  1.6 10.5 %collective-permute-start.2 = (bf16[15,16,128]{2,1,0:T(8,128)(2,1)S(1)}, bf16[15,16,128]{2,1,0:T(8,128)(2,1)S(1)}, u32[]{:S(2)}, u32[]{:S(2)}) collective-permute-start(bf16[15,16,128]{2,1,0:T(8,128)(2,1)S(1)} %bitcast.46), channel_id=1, source_target_pairs={{0,3},{1,2},{2,1},{3,0},{4,7},{5,6},{6,5},{7,4},{8,11},{9,10},{10,... | collective-permute-start | bytes 184328 | tf_op jit(solution)/shard_map/ppermute | solution.py:46
  6.7 6.8 %collective-permute-start.1 = (bf16[30,16,128]{2,1,0:T(8,128)(2,1)S(1)}, bf16[30,16,128]{2,1,0:T(8,128)(2,1)S(1)}, u32[]{:S(2)}, u32[]{:S(2)}) collective-permute-start(bf16[30,16,128]{2,1,0:T(8,128)(2,1)S(1)} %bitcast.45), channel_id=1, source_target_pairs={{0,1},{1,0},{2,3},{3,2},{4,5},{5,4},{6,7},{7,6},{8,9},{9,8},{10,11... | collective-permute-start | bytes 368648 | tf_op jit(solution)/shard_map/ppermute | solution.py:45
  6.7 8.4 %collective-permute-start = (bf16[30,16,128]{2,1,0:T(8,128)(2,1)S(1)}, bf16[30,16,128]{2,1,0:T(8,128)(2,1)S(1)}, u32[]{:S(2)}, u32[]{:S(2)}) collective-permute-start(bf16[30,16,128]{2,1,0:T(8,128)(2,1)S(1)} %bitcast.44), channel_id=1, source_target_pairs={{0,2},{1,3},{2,0},{3,1},{4,6},{5,7},{6,4},{7,5},{8,10},{9,11},{10,... | collective-permute-start | bytes 368648 | tf_op jit(solution)/shard_map/ppermute | solution.py:44
  15.2 7.1 %collective-permute-start.4 = (bf16[57,16,128]{2,1,0:T(8,128)(2,1)S(1)}, bf16[57,16,128]{2,1,0:T(8,128)(2,1)S(1)}, u32[]{:S(2)}, u32[]{:S(2)}) collective-permute-start(bf16[57,16,128]{2,1,0:T(8,128)(2,1)S(1)} %get-tuple-element.57), channel_id=1, source_target_pairs={{4,8},{8,4},{5,9},{9,5},{6,10},{10,6},{7,11},{11,7},{20,24},{24,20... | collective-permute-start | bytes 700424 | tf_op jit(solution)/shard_map/ppermute | solution.py:63
  15.8 7.1 %collective-permute-start.5 = (bf16[1,4,14,16,128]{4,3,2,1,0:T(8,128)(2,1)S(1)}, bf16[1,4,14,16,128]{4,3,2,1,0:T(8,128)(2,1)S(1)}, u32[]{:S(2)}, u32[]{:S(2)}) collective-permute-start(bf16[1,4,14,16,128]{4,3,2,1,0:T(8,128)(2,1)S(1)} %bitcast.35), channel_id=1, source_target_pairs={{0,16},{16,0},{1,17},{17,1},{2,18},{18,2},{3,19},{19,3},{4,20},{20... | collective-permute-start | bytes 688136 | tf_op jit(solution)/shard_map/ppermute | solution.py:94
  17.5 3.7 %collective-permute-start.3 = (bf16[55,16,128]{2,1,0:T(8,128)(2,1)S(1)}, bf16[55,16,128]{2,1,0:T(8,128)(2,1)S(1)}, u32[]{:S(2)}, u32[]{:S(2)}) collective-permute-start(bf16[55,16,128]{2,1,0:T(8,128)(2,1)S(1)} %get-tuple-element.55), channel_id=1, source_target_pairs={{0,4},{4,0},{8,12},{12,8},{1,5},{5,1},{9,13},{13,9},{2,6},{6,2},{1... | collective-permute-start | bytes 675848 | tf_op jit(solution)/shard_map/ppermute | solution.py:63
  23.0 11.5 %collective-permute-start.6 = (bf16[2,3,14,16,128]{4,3,2,1,0:T(8,128)(2,1)S(1)}, bf16[2,3,14,16,128]{4,3,2,1,0:T(8,128)(2,1)S(1)}, u32[]{:S(2)}, u32[]{:S(2)}) collective-permute-start(bf16[2,3,14,16,128]{4,3,2,1,0:T(8,128)(2,1)S(1)} %bitcast.27), channel_id=1, source_target_pairs={{0,8},{4,12},{8,0},{12,4},{1,9},{5,13},{9,1},{13,5},{2,10},{6,14},... | collective-permute-start | bytes 1032200 | tf_op jit(solution)/shard_map/ppermute | solution.py:94
  24.8 9.9 %copy-start.3 = (f32[128]{0:T(128)S(1)}, f32[128]{0:T(128)}, u32[]{:S(2)}) copy-start(f32[128]{0:T(128)} %param.10) | copy-start | bytes 1540
  24.8 9.9 %copy-start.4 = (f32[128]{0:T(128)S(1)}, f32[128]{0:T(128)}, u32[]{:S(2)}) copy-start(f32[128]{0:T(128)} %param.11) | copy-start | bytes 1540
  34.5 5.8 %collective-permute-start.7 = (bf16[4,3,14,16,128]{4,3,2,1,0:T(8,128)(2,1)S(1)}, bf16[4,3,14,16,128]{4,3,2,1,0:T(8,128)(2,1)S(1)}, u32[]{:S(2)}, u32[]{:S(2)}) collective-permute-start(bf16[4,3,14,16,128]{4,3,2,1,0:T(8,128)(2,1)S(1)} %bitcast.24), channel_id=1, source_target_pairs={{0,4},{4,0},{8,12},{12,8},{1,5},{5,1},{9,13},{13,9},{2,6},{6,2},{1... | collective-permute-start | bytes 2064392 | tf_op jit(solution)/shard_map/ppermute | solution.py:94
  35.9 6.0 %collective-permute-start.10 = (f32[16,128]{1,0:T(8,128)S(1)}, f32[16,128]{1,0:T(8,128)S(1)}, u32[]{:S(2)}, u32[]{:S(2)}) collective-permute-start(f32[16,128]{1,0:T(8,128)S(1)} %bitcast.49), channel_id=1, source_target_pairs={{0,3},{1,2},{2,1},{3,0},{4,7},{5,6},{6,5},{7,4},{8,11},{9,10},{10,... | collective-permute-start | bytes 24584 | tf_op jit(solution)/shard_map/ppermute | solution.py:46
  36.6 5.3 %collective-permute-start.8 = (bf16[80,128]{1,0:T(8,128)(2,1)S(1)}, bf16[80,128]{1,0:T(8,128)(2,1)S(1)}, u32[]{:S(2)}, u32[]{:S(2)}) collective-permute-start(bf16[80,128]{1,0:T(8,128)(2,1)S(1)} %bitcast.48), channel_id=1, source_target_pairs={{0,2},{1,3},{2,0},{3,1},{4,6},{5,7},{6,4},{7,5},{8,10},{9,11},{10,... | collective-permute-start | bytes 61448 | tf_op jit(solution)/shard_map/ppermute | solution.py:44
  37.9 4.2 %collective-permute-start.9 = (bf16[80,128]{1,0:T(8,128)(2,1)S(1)}, bf16[80,128]{1,0:T(8,128)(2,1)S(1)}, u32[]{:S(2)}, u32[]{:S(2)}) collective-permute-start(bf16[80,128]{1,0:T(8,128)(2,1)S(1)} %bitcast.47), channel_id=1, source_target_pairs={{0,1},{1,0},{2,3},{3,2},{4,5},{5,4},{6,7},{7,6},{8,9},{9,8},{10,11... | collective-permute-start | bytes 61448 | tf_op jit(solution)/shard_map/ppermute | solution.py:45
  41.9 11.0 %copy-start = (bf16[256,128]{1,0:T(8,128)(2,1)S(1)}, bf16[256,128]{1,0:T(8,128)(2,1)}, u32[]{:S(2)}) copy-start(bf16[256,128]{1,0:T(8,128)(2,1)} %up.1) | copy-start | bytes 196612
  41.9 11.0 %copy-start.1 = (f32[256]{0:T(256)S(1)}, f32[256]{0:T(256)}, u32[]{:S(2)}) copy-start(f32[256]{0:T(256)} %param.13) | copy-start | bytes 3076
  41.9 11.0 %copy-start.2 = (f32[256]{0:T(256)S(1)}, f32[256]{0:T(256)}, u32[]{:S(2)}) copy-start(f32[256]{0:T(256)} %param.14) | copy-start | bytes 3076

commit v23 on v22

--- a/solution.py
+++ b/solution.py
@@ -137,8 +137,8 @@
                 )
             )
     later.append(pltpu.make_async_copy(w_in, w, sems.at[chunks + 3]))
-    for copy in first + later:
-        copy.start()
+    for k, copy in enumerate(first + later):
+        copy.start(priority=k % 2)
     x[0] = jnp.zeros(x.shape[1:], bf16)
     x[edge + 1] = jnp.zeros(x.shape[1:], bf16)
     blank = jnp.zeros((edge,) + x.shape[2:], bf16)
@@ -711,7 +711,7 @@
         old = mid[at].astype(f32).reshape(planes, 2, deep, 2, edge, 128)
         held[at] = (old + add).astype(jnp.bfloat16).reshape(2 * planes, edge, edge, 128)
         copy = pltpu.make_async_copy(held.at[at], out.at[at], sems.at[k // planes])
-        copy.start()
+        copy.start(priority=k // planes % 2)
         copies.append(copy)
     for copy in copies:
         copy.wait()

time: 54.6 us -> 54.6 us (level)
  no operation moved by 1% of the time
where the time goes in v23:
time: 54.6 us; the launch traced here: 54.4 us
  blocking collectives  19.6 us (36%)
  starting transfers between devices  17.1 us (31%)
  Pallas kernels  14.2 us (26%)
  waiting for transfers between devices  3.26 us (6%)
    all_to_all x2, blocking collectives, share(): return lax.all_to_all(stats, PART, 0, 0)  19.6 us
    pallas_call x11, Pallas kernels, call(): pl.pallas_call(kernel, out_shape=[jax.ShapeDtypeStruct(shape, dtype) for...  14 us
    ppermute x2, starting transfers between devices, halos(): corner = lax.ppermute(corners[0], 'yx', self.swap_route(3))  5.86 us
    ppermute x3, starting transfers between devices, swap(): lax.ppermute(block, axis, [(i, i ^ mask) for i in range(lax.axis_size(axi...  3.64 us
    ppermute x1, starting transfers between devices, swap_depth(): lax.ppermute(inner, 'gz', routes[0])  2.56 us
    ppermute x2, starting transfers between devices, halos(): x = lax.ppermute(x_edges[0], 'yx', self.swap_route(1))  2.42 us
    ppermute x2, starting transfers between devices, halos(): y = lax.ppermute(y_edges[0], 'yx', self.swap_route(2))  1.96 us
    ppermute x2, waiting for transfers between devices, halos(): y = lax.ppermute(y_edges[0], 'yx', self.swap_route(2))  1.59 us
  transfers between devices with their start and end apart: 11, of which 4 were waited for; matrix products, arithmetic and copies ran while one was open for 0% of the time, Pallas kernels for 19%

profile of v23, /device:TPU:0, one launch (start us, length us, event | category | flops | bytes accessed | tf_op | source)
XLA Modules:
  0.0 54.4 jit_solution(15199098553409543562)
XLA Ops:
  0.0 1.6 %shard_map.82 = (bf16[1,30,16,128]{3,2,1,0:T(8,128)(2,1)S(1)}, bf16[1,30,16,128]{3,2,1,0:T(8,128)(2,1)S(1)}, bf16[1,15,16,128]{3,2,1,0:T(8,128)(2,1)S(1)}, bf16[...) custom-call(bf16[16,16,16,128]{3,2,1,0:T(8,128)(2,1)} %x_in.1, bf16[27,128,128]{2,1,0:T(8,128)(2,1)} %bitcast.50, ...), custom_call_target="tpu_custom_call" | custom-call | bytes 5242880 | tf_op jit(solution)/shard_map/pallas_call | solution.py:105
  1.6 5.1 %collective-permute-start.2 = (bf16[15,16,128]{2,1,0:T(8,128)(2,1)S(1)}, bf16[15,16,128]{2,1,0:T(8,128)(2,1)S(1)}, u32[]{:S(2)}, u32[]{:S(2)}) collective-permute-start(bf16[15,16,128]{2,1,0:T(8,128)(2,1)S(1)} %bitcast.46), channel_id=1, source_target_pairs={{0,3},{1,2},{2,1},{3,0},{4,7},{5,6},{6,5},{7,4},{8,11},{9,10},{10,... | collective-permute-start | bytes 184328 | tf_op jit(solution)/shard_map/ppermute | solution.py:46
  6.7 0.0 collective-permute-start.1
  6.7 0.6 %collective-permute-start = (bf16[30,16,128]{2,1,0:T(8,128)(2,1)S(1)}, bf16[30,16,128]{2,1,0:T(8,128)(2,1)S(1)}, u32[]{:S(2)}, u32[]{:S(2)}) collective-permute-start(bf16[30,16,128]{2,1,0:T(8,128)(2,1)S(1)} %bitcast.44), channel_id=1, source_target_pairs={{0,2},{1,3},{2,0},{3,1},{4,6},{5,7},{6,4},{7,5},{8,10},{9,11},{10,... | collective-permute-start | bytes 368648 | tf_op jit(solution)/shard_map/ppermute | solution.py:44
  7.4 4.7 %shard_map.83 = (f32[16,16,16,128]{3,2,1,0:T(8,128)S(1)}, bf16[1152,384]{1,0:T(8,128)(2,1)S(1)}, bf16[1536,256]{1,0:T(8,128)(2,1)S(1)}, bf16[108,16,128]{2,1,0:T(8,128)(2,1)S(1)}) custom-call(bf16[108,16,128]{2,1,0:T(8,128)(2,1)} %bitcast.52, bf16[18,18,16,128]{3,2,1,0:T(8,128)(2,1)S(1)} %get-tuple-element.44.x, ...), custom_call_target="tpu_custom_call" | custom-call | flops 3623878656 | bytes 6291456 | tf_op jit(solution)/shard_map/pallas_call | solution.py:105
  12.1 0.0 collective-permute-done.2
  12.1 1.4 %collective-permute-done.1 = bf16[30,16,128]{2,1,0:T(8,128)(2,1)S(1)} collective-permute-done((bf16[30,16,128]{2,1,0:T(8,128)(2,1)S(1)}, bf16[30,16,128]{2,1,0:T(8,128)(2,1)S(1)}, u32[]{:S(2)}, u32[]{:S(2)}) %collective-permute-start.1) | collective-permute-done | bytes 122912 | tf_op jit(solution)/shard_map/ppermute | solution.py:45
  13.5 1.6 %collective-permute-done = bf16[30,16,128]{2,1,0:T(8,128)(2,1)S(1)} collective-permute-done((bf16[30,16,128]{2,1,0:T(8,128)(2,1)S(1)}, bf16[30,16,128]{2,1,0:T(8,128)(2,1)S(1)}, u32[]{:S(2)}, u32[]{:S(2)}) %collective-permute-start) | collective-permute-done | bytes 122912 | tf_op jit(solution)/shard_map/ppermute | solution.py:44
  15.1 0.1 shard_map.85
  15.1 0.7 %collective-permute-start.4 = (bf16[57,16,128]{2,1,0:T(8,128)(2,1)S(1)}, bf16[57,16,128]{2,1,0:T(8,128)(2,1)S(1)}, u32[]{:S(2)}, u32[]{:S(2)}) collective-permute-start(bf16[57,16,128]{2,1,0:T(8,128)(2,1)S(1)} %get-tuple-element.57), channel_id=1, source_target_pairs={{4,8},{8,4},{5,9},{9,5},{6,10},{10,6},{7,11},{11,7},{20,24},{24,20... | collective-permute-start | bytes 700424 | tf_op jit(solution)/shard_map/ppermute | solution.py:63
  15.8 1.6 %collective-permute-start.5 = (bf16[1,4,14,16,128]{4,3,2,1,0:T(8,128)(2,1)S(1)}, bf16[1,4,14,16,128]{4,3,2,1,0:T(8,128)(2,1)S(1)}, u32[]{:S(2)}, u32[]{:S(2)}) collective-permute-start(bf16[1,4,14,16,128]{4,3,2,1,0:T(8,128)(2,1)S(1)} %bitcast.35), channel_id=1, source_target_pairs={{0,16},{16,0},{1,17},{17,1},{2,18},{18,2},{3,19},{19,3},{4,20},{20... | collective-permute-start | bytes 688136 | tf_op jit(solution)/shard_map/ppermute | solution.py:94
  17.4 2.6 %collective-permute-start.3 = (bf16[55,16,128]{2,1,0:T(8,128)(2,1)S(1)}, bf16[55,16,128]{2,1,0:T(8,128)(2,1)S(1)}, u32[]{:S(2)}, u32[]{:S(2)}) collective-permute-start(bf16[55,16,128]{2,1,0:T(8,128)(2,1)S(1)} %get-tuple-element.55), channel_id=1, source_target_pairs={{0,4},{4,0},{8,12},{12,8},{1,5},{5,1},{9,13},{13,9},{2,6},{6,2},{1... | collective-permute-start | bytes 675848 | tf_op jit(solution)/shard_map/ppermute | solution.py:63
  20.0 1.0 %shard_map.84 = (f32[14,16,16,128]{3,2,1,0:T(8,128)S(1)}, f32[4,16,16,128]{3,2,1,0:T(8,128)S(1)}, f32[16,128]{1,0:T(8,128)S(1)}) custom-call(f32[16,16,16,128]{3,2,1,0:T(8,128)S(1)} %get-tuple-element.47.own, bf16[1,30,16,128]{3,2,1,0:T(8,128)(2,1)S(1)} %bitcast.32, bf16[1,30,16,128]{3,2,1,0:T(8,128)(2,1)S(1)} %bitcast.30, ...), custom_call_target="tpu_custom_call" | custom-call | tf_op jit(solution)/shard_map/pallas_call | solution.py:105
  21.0 0.1 collective-permute-done.3.face
  21.1 1.1 %shard_map.86.ends = f32[6,16,16,128]{3,2,1,0:T(8,128)S(1)} custom-call(bf16[18,18,16,128]{3,2,1,0:T(8,128)(2,1)S(1)} %get-tuple-element.44.x, f32[4,16,16,128]{3,2,1,0:T(8,128)S(1)} %get-tuple-element.54.partial, bf16[55,16,128]{2,1,0:T(8,128)(2,1)S(1)} %collective-permute-done.3.face, bf16[1152,384]{1,0:T(8,128)(2,1)S(1)} %get-tuple-element.51.taps, ...), custom_call_target="tpu_custom_call" | custom-call | tf_op jit(solution)/shard_map/pallas_call | solution.py:105
  22.2 0.0 collective-permute-done.4.face
  22.2 0.6 %shard_map.87 = (f32[6,16,16,128]{3,2,1,0:T(8,128)S(1)}, f32[16,2,128]{2,1,0:T(2,128)S(1)}) custom-call(bf16[18,18,16,128]{3,2,1,0:T(8,128)(2,1)S(1)} %get-tuple-element.44.x, f32[16,128]{1,0:T(8,128)S(1)} %get-tuple-element.53.middle_stats, f32[6,16,16,128]{3,2,1,0:T(8,128)S(1)} %shard_map.86.ends, bf16[57,16,128]{2,1,0:T(8,128)(2,1)S(1)} %collective-permute-done.4.face, ...), custom_call_target="tpu_custom_call" | custom-call | tf_op jit(solution)/shard_map/pallas_call | solution.py:105
  22.9 0.0 collective-permute-done.5.refs_1_
  22.9 1.9 %collective-permute-start.6 = (bf16[2,3,14,16,128]{4,3,2,1,0:T(8,128)(2,1)S(1)}, bf16[2,3,14,16,128]{4,3,2,1,0:T(8,128)(2,1)S(1)}, u32[]{:S(2)}, u32[]{:S(2)}) collective-permute-start(bf16[2,3,14,16,128]{4,3,2,1,0:T(8,128)(2,1)S(1)} %bitcast.27), channel_id=1, source_target_pairs={{0,8},{4,12},{8,0},{12,4},{1,9},{5,13},{9,1},{13,5},{2,10},{6,14},... | collective-permute-start | bytes 1032200 | tf_op jit(solution)/shard_map/ppermute | solution.py:94
  24.8 0.0 copy-start.3
  24.8 0.0 copy-start.4
  24.8 0.1 shard_map.88.ends
  24.8 9.6 %all_to_all.10.stats = f32[16,2,128]{2,1,0:T(2,128)S(1)} all-to-all(f32[16,2,128]{2,1,0:T(2,128)S(1)} %get-tuple-element.63), channel_id=1, replica_groups=mesh['cand'=2,'gz'=4,'yx'=4] {'gz','yx'}, dimensions={0} | all-to-all | bytes 32768 | tf_op jit(solution)/shard_map/all_to_all | solution.py:98
  34.5 0.0 collective-permute-done.6.refs_1_
  34.5 0.2 collective-permute-start.7
  34.7 0.0 copy-done.3
  34.7 0.0 copy-done.4
  34.7 1.1 %shard_map.90 = (bf16[16,16,16,128]{3,2,1,0:T(8,128)(2,1)S(1)}, f32[10,8,8,128]{3,2,1,0:T(8,128)S(1)}, bf16[1,80,128]{2,1,0:T(8,128)(2,1)S(1)}, bf16[1,80,128]{2,1,0:T(8,128)(2,1)S(1)}, f32[1,16,128]{2,1,0:T(8,128)S(1)}) custom-call(f32[14,16,16,128]{3,2,1,0:T(8,128)S(1)} %get-tuple-element.52.inner, f32[6,16,16,128]{3,2,1,0:T(8,128)S(1)} %shard_map.88.ends, ...), custom_call_target="tpu_custom_call" | custom-call | flops 10485760 | bytes 3145728 | tf_op jit(solution)/shard_map/pallas_call | solution.py:105
  35.8 0.7 %collective-permute-start.10 = (f32[16,128]{1,0:T(8,128)S(1)}, f32[16,128]{1,0:T(8,128)S(1)}, u32[]{:S(2)}, u32[]{:S(2)}) collective-permute-start(f32[16,128]{1,0:T(8,128)S(1)} %bitcast.49), channel_id=1, source_target_pairs={{0,3},{1,2},{2,1},{3,0},{4,7},{5,6},{6,5},{7,4},{8,11},{9,10},{10,... | collective-permute-start | bytes 24584 | tf_op jit(solution)/shard_map/ppermute | solution.py:46
  36.6 1.3 %collective-permute-start.8 = (bf16[80,128]{1,0:T(8,128)(2,1)S(1)}, bf16[80,128]{1,0:T(8,128)(2,1)S(1)}, u32[]{:S(2)}, u32[]{:S(2)}) collective-permute-start(bf16[80,128]{1,0:T(8,128)(2,1)S(1)} %bitcast.48), channel_id=1, source_target_pairs={{0,2},{1,3},{2,0},{3,1},{4,6},{5,7},{6,4},{7,5},{8,10},{9,11},{10,... | collective-permute-start | bytes 61448 | tf_op jit(solution)/shard_map/ppermute | solution.py:44
  37.9 2.4 %collective-permute-start.9 = (bf16[80,128]{1,0:T(8,128)(2,1)S(1)}, bf16[80,128]{1,0:T(8,128)(2,1)S(1)}, u32[]{:S(2)}, u32[]{:S(2)}) collective-permute-start(bf16[80,128]{1,0:T(8,128)(2,1)S(1)} %bitcast.47), channel_id=1, source_target_pairs={{0,1},{1,0},{2,3},{3,2},{4,5},{5,4},{6,7},{7,6},{8,9},{9,8},{10,11... | collective-permute-start | bytes 61448 | tf_op jit(solution)/shard_map/ppermute | solution.py:45
  40.3 0.0 collective-permute-done.7.refs_1_
  40.3 0.1 shard_map.92
  40.4 1.4 %shard_map.93 = (f32[2,512,128]{2,1,0:T(8,128)S(1)}, bf16[4,108,16,128]{3,2,1,0:T(8,128)(2,1)S(1)}) custom-call(f32[10,8,8,128]{3,2,1,0:T(8,128)S(1)} %get-tuple-element.66.pooled, bf16[108,16,128]{2,1,0:T(8,128)(2,1)S(1)} %get-tuple-element.67.own, bf16[8,3,14,16,128]{4,3,2,1,0:T(8,128)(2,1)S(1)} %bitcast.26), custom_call_target="tpu_custom_call" | custom-call | flops 905969664 | bytes 4194304 | tf_op jit(solution)/shard_map/pallas_call | solution.py:105
  41.8 0.0 copy-start
  41.9 0.0 copy-start.1
  41.9 0.0 copy-start.2
  41.9 0.0 collective-permute-done.10
  41.9 0.0 collective-permute-done.8
  41.9 0.2 collective-permute-done.9
  42.1 0.7 %shard_map.94 = (f32[2,512,128]{2,1,0:T(8,128)S(1)}, f32[16,2,256]{2,1,0:T(2,128)S(1)}) custom-call(f32[2,512,128]{2,1,0:T(8,128)S(1)} %get-tuple-element.69.own, bf16[1,80,128]{2,1,0:T(8,128)(2,1)S(1)} %bitcast.37, bf16[1,80,128]{2,1,0:T(8,128)(2,1)S(1)} %bitcast.38, f32[1,16,128]{2,1,0:T(8,128)S(1)} %bitcast.39, ...), custom_call_target="tpu_custom_call" | custom-call | flops 67108864 | bytes 3145728 | tf_op jit(solution)/shard_map/pallas_call | solution.py:105
  42.8 10.0 %all_to_all.11.stats = f32[16,2,256]{2,1,0:T(2,128)S(1)} all-to-all(f32[16,2,256]{2,1,0:T(2,128)S(1)} %get-tuple-element.75), channel_id=1, replica_groups=mesh['cand'=2,'gz'=4,'yx'=4] {'gz','yx'}, dimensions={0} | all-to-all | bytes 65536 | tf_op jit(solution)/shard_map/all_to_all | solution.py:98
  52.8 0.0 copy-done
  52.8 0.0 copy-done.1
  52.8 0.0 copy-done.2
  52.9 1.5 %shard_map.95 = bf16[16,16,16,128]{3,2,1,0:T(8,128)(2,1)} custom-call(f32[2,512,128]{2,1,0:T(8,128)S(1)} %get-tuple-element.74.act, f32[16,2,256]{2,1,0:T(2,128)S(1)} %all_to_all.11.stats, f32[1,256]{1,0:T(1,128)S(1)} %bitcast.40, f32[1,256]{1,0:T(1,128)S(1)} %bitcast.41, bf16[256,128]{1,0:T(8,128)(2,1)S(1)} %copy-done, ...), custom_call_target="tpu_custom_call" | custom-call | flops 67108864 | bytes 3145728 | tf_op jit(solution)/shard_map/pallas_call | solution.py:105
  (2 shorter events, 0.1 us)
Async XLA Ops:
  1.6 10.5 %collective-permute-start.2 = (bf16[15,16,128]{2,1,0:T(8,128)(2,1)S(1)}, bf16[15,16,128]{2,1,0:T(8,128)(2,1)S(1)}, u32[]{:S(2)}, u32[]{:S(2)}) collective-permute-start(bf16[15,16,128]{2,1,0:T(8,128)(2,1)S(1)} %bitcast.46), channel_id=1, source_target_pairs={{0,3},{1,2},{2,1},{3,0},{4,7},{5,6},{6,5},{7,4},{8,11},{9,10},{10,... | collective-permute-start | bytes 184328 | tf_op jit(solution)/shard_map/ppermute | solution.py:46
  6.7 6.8 %collective-permute-start.1 = (bf16[30,16,128]{2,1,0:T(8,128)(2,1)S(1)}, bf16[30,16,128]{2,1,0:T(8,128)(2,1)S(1)}, u32[]{:S(2)}, u32[]{:S(2)}) collective-permute-start(bf16[30,16,128]{2,1,0:T(8,128)(2,1)S(1)} %bitcast.45), channel_id=1, source_target_pairs={{0,1},{1,0},{2,3},{3,2},{4,5},{5,4},{6,7},{7,6},{8,9},{9,8},{10,11... | collective-permute-start | bytes 368648 | tf_op jit(solution)/shard_map/ppermute | solution.py:45
  6.7 8.4 %collective-permute-start = (bf16[30,16,128]{2,1,0:T(8,128)(2,1)S(1)}, bf16[30,16,128]{2,1,0:T(8,128)(2,1)S(1)}, u32[]{:S(2)}, u32[]{:S(2)}) collective-permute-start(bf16[30,16,128]{2,1,0:T(8,128)(2,1)S(1)} %bitcast.44), channel_id=1, source_target_pairs={{0,2},{1,3},{2,0},{3,1},{4,6},{5,7},{6,4},{7,5},{8,10},{9,11},{10,... | collective-permute-start | bytes 368648 | tf_op jit(solution)/shard_map/ppermute | solution.py:44
  15.1 7.1 %collective-permute-start.4 = (bf16[57,16,128]{2,1,0:T(8,128)(2,1)S(1)}, bf16[57,16,128]{2,1,0:T(8,128)(2,1)S(1)}, u32[]{:S(2)}, u32[]{:S(2)}) collective-permute-start(bf16[57,16,128]{2,1,0:T(8,128)(2,1)S(1)} %get-tuple-element.57), channel_id=1, source_target_pairs={{4,8},{8,4},{5,9},{9,5},{6,10},{10,6},{7,11},{11,7},{20,24},{24,20... | collective-permute-start | bytes 700424 | tf_op jit(solution)/shard_map/ppermute | solution.py:63
  15.8 7.1 %collective-permute-start.5 = (bf16[1,4,14,16,128]{4,3,2,1,0:T(8,128)(2,1)S(1)}, bf16[1,4,14,16,128]{4,3,2,1,0:T(8,128)(2,1)S(1)}, u32[]{:S(2)}, u32[]{:S(2)}) collective-permute-start(bf16[1,4,14,16,128]{4,3,2,1,0:T(8,128)(2,1)S(1)} %bitcast.35), channel_id=1, source_target_pairs={{0,16},{16,0},{1,17},{17,1},{2,18},{18,2},{3,19},{19,3},{4,20},{20... | collective-permute-start | bytes 688136 | tf_op jit(solution)/shard_map/ppermute | solution.py:94
  17.4 3.7 %collective-permute-start.3 = (bf16[55,16,128]{2,1,0:T(8,128)(2,1)S(1)}, bf16[55,16,128]{2,1,0:T(8,128)(2,1)S(1)}, u32[]{:S(2)}, u32[]{:S(2)}) collective-permute-start(bf16[55,16,128]{2,1,0:T(8,128)(2,1)S(1)} %get-tuple-element.55), channel_id=1, source_target_pairs={{0,4},{4,0},{8,12},{12,8},{1,5},{5,1},{9,13},{13,9},{2,6},{6,2},{1... | collective-permute-start | bytes 675848 | tf_op jit(solution)/shard_map/ppermute | solution.py:63
  22.9 11.5 %collective-permute-start.6 = (bf16[2,3,14,16,128]{4,3,2,1,0:T(8,128)(2,1)S(1)}, bf16[2,3,14,16,128]{4,3,2,1,0:T(8,128)(2,1)S(1)}, u32[]{:S(2)}, u32[]{:S(2)}) collective-permute-start(bf16[2,3,14,16,128]{4,3,2,1,0:T(8,128)(2,1)S(1)} %bitcast.27), channel_id=1, source_target_pairs={{0,8},{4,12},{8,0},{12,4},{1,9},{5,13},{9,1},{13,5},{2,10},{6,14},... | collective-permute-start | bytes 1032200 | tf_op jit(solution)/shard_map/ppermute | solution.py:94
  24.8 9.9 %copy-start.3 = (f32[128]{0:T(128)S(1)}, f32[128]{0:T(128)}, u32[]{:S(2)}) copy-start(f32[128]{0:T(128)} %param.10) | copy-start | bytes 1540
  24.8 9.9 %copy-start.4 = (f32[128]{0:T(128)S(1)}, f32[128]{0:T(128)}, u32[]{:S(2)}) copy-start(f32[128]{0:T(128)} %param.11) | copy-start | bytes 1540
  34.5 5.8 %collective-permute-start.7 = (bf16[4,3,14,16,128]{4,3,2,1,0:T(8,128)(2,1)S(1)}, bf16[4,3,14,16,128]{4,3,2,1,0:T(8,128)(2,1)S(1)}, u32[]{:S(2)}, u32[]{:S(2)}) collective-permute-start(bf16[4,3,14,16,128]{4,3,2,1,0:T(8,128)(2,1)S(1)} %bitcast.24), channel_id=1, source_target_pairs={{0,4},{4,0},{8,12},{12,8},{1,5},{5,1},{9,13},{13,9},{2,6},{6,2},{1... | collective-permute-start | bytes 2064392 | tf_op jit(solution)/shard_map/ppermute | solution.py:94
  35.8 6.0 %collective-permute-start.10 = (f32[16,128]{1,0:T(8,128)S(1)}, f32[16,128]{1,0:T(8,128)S(1)}, u32[]{:S(2)}, u32[]{:S(2)}) collective-permute-start(f32[16,128]{1,0:T(8,128)S(1)} %bitcast.49), channel_id=1, source_target_pairs={{0,3},{1,2},{2,1},{3,0},{4,7},{5,6},{6,5},{7,4},{8,11},{9,10},{10,... | collective-permute-start | bytes 24584 | tf_op jit(solution)/shard_map/ppermute | solution.py:46
  36.6 5.3 %collective-permute-start.8 = (bf16[80,128]{1,0:T(8,128)(2,1)S(1)}, bf16[80,128]{1,0:T(8,128)(2,1)S(1)}, u32[]{:S(2)}, u32[]{:S(2)}) collective-permute-start(bf16[80,128]{1,0:T(8,128)(2,1)S(1)} %bitcast.48), channel_id=1, source_target_pairs={{0,2},{1,3},{2,0},{3,1},{4,6},{5,7},{6,4},{7,5},{8,10},{9,11},{10,... | collective-permute-start | bytes 61448 | tf_op jit(solution)/shard_map/ppermute | solution.py:44
  37.9 4.2 %collective-permute-start.9 = (bf16[80,128]{1,0:T(8,128)(2,1)S(1)}, bf16[80,128]{1,0:T(8,128)(2,1)S(1)}, u32[]{:S(2)}, u32[]{:S(2)}) collective-permute-start(bf16[80,128]{1,0:T(8,128)(2,1)S(1)} %bitcast.47), channel_id=1, source_target_pairs={{0,1},{1,0},{2,3},{3,2},{4,5},{5,4},{6,7},{7,6},{8,9},{9,8},{10,11... | collective-permute-start | bytes 61448 | tf_op jit(solution)/shard_map/ppermute | solution.py:45
  41.8 11.0 %copy-start = (bf16[256,128]{1,0:T(8,128)(2,1)S(1)}, bf16[256,128]{1,0:T(8,128)(2,1)}, u32[]{:S(2)}) copy-start(bf16[256,128]{1,0:T(8,128)(2,1)} %up.1) | copy-start | bytes 196612
  41.9 11.0 %copy-start.1 = (f32[256]{0:T(256)S(1)}, f32[256]{0:T(256)}, u32[]{:S(2)}) copy-start(f32[256]{0:T(256)} %param.13) | copy-start | bytes 3076
  41.9 11.0 %copy-start.2 = (f32[256]{0:T(256)S(1)}, f32[256]{0:T(256)}, u32[]{:S(2)}) copy-start(f32[256]{0:T(256)} %param.14) | copy-start | bytes 3076

commit v24 on v22

--- a/solution.py
+++ b/solution.py
@@ -501,6 +501,11 @@
     return h + h * jnp.tanh(h)
 
 
+def sixteen(rows):
+    pad = jnp.zeros((16 - rows.shape[0], 128), rows.dtype)
+    return jnp.concatenate([rows, pad], axis=0).astype(jnp.bfloat16)
+
+
 def norm_kernel(ny, nx, inner, ends, stats, gain, offset, out, pooled, *refs):
     y_edges, x_edges, corners, half = refs
     depth, edge = inner.shape[0] + 6, inner.shape[1]
@@ -544,14 +549,15 @@
         above, left = above[0], left[0]
         y_edges[0] = jnp.where(above, first_y, last_y).astype(bf16)
         x_edges[0] = jnp.where(left, first_x, last_x).astype(bf16)
-        corners[0, 0:deep_depth] = jnp.where(
+        end = jnp.where(
             above, jnp.where(left, ends[0], ends[1]), jnp.where(left, ends[2], ends[3])
         )
+        corners[0, 0:16] = sixteen(end)
     else:
         y_edges[0], y_edges[1] = first_y.astype(bf16), last_y.astype(bf16)
         x_edges[0], x_edges[1] = first_x.astype(bf16), last_x.astype(bf16)
         for k in range(4):
-            corners[k, 0:deep_depth] = ends[k]
+            corners[k, 0:16] = sixteen(ends[k])
 
 
 def stack_kernel(*refs):
@@ -626,7 +632,7 @@
         act[half] = total[:, half * 128 : half * 128 + 128]
 
 
-def deep_rim_kernel(ny, nx, own, y_halos, x_halos, corners, weight, act, stats, line):
+def deep_rim_kernel(ny, nx, own, y_halos, corners, x_halos, weight, act, stats, line):
     depth, deep = line.shape[0], line.shape[1] - 16
     halves = act.shape[0]
     f32 = jnp.float32
@@ -649,7 +655,7 @@
         line[...] = jnp.zeros(line.shape, f32)
         line[:, 8 : 8 + deep] = y_halos[i].astype(f32).reshape(depth, deep, 128)
         for j in range(nx):
-            end = corners[i * nx + j, 0:depth]
+            end = corners[i * nx + j, 0:16].astype(f32)[:depth]
             first, last = jnp.where(left[j], end, 0.0), jnp.where(left[j], 0.0, end)
             if nx == 1 or j == 0:
                 flat[pl.ds(7, depth, stride=line.shape[1]), :] = first
@@ -850,7 +856,7 @@
             ((deep + 2, deep, deep, channels), f32),
             ((ny, (deep + 2) * deep, channels), bf16),
             ((nx, (deep + 2) * deep, channels), bf16),
-            ((ny * nx, 16, channels), f32),
+            ((ny * nx, (deep + 2) * deep, channels), bf16),
         ],
         [((deep + 2, deep * edge, channels), f32)],
         middle,
@@ -882,8 +888,8 @@
         [((deep + 2, 24, channels), f32)],
         deep_act,
         jnp.stack(y),
+        jnp.stack(corner),
         jnp.stack(x),
-        jnp.stack(corner),
         weight,
         flops=4 * channels * deep_channels * deep**3,
         nbytes=3 << 20,

time: 54.6 us -> 55 us (level)
  waiting for transfers between devices: 3.26 us -> 4.88 us
  starting transfers between devices: 17.1 us -> 16.2 us
    ppermute x2, waiting for transfers between devices: 0.01 us -> 1.81 us  [halos(): corner = lax.ppermute(corners[0], 'yx', self.swap_route(3))]
    ppermute x2, starting transfers between devices: 2.42 us -> 0.62 us  [halos(): x = lax.ppermute(x_edges[0], 'yx', self.swap_route(1))]
    ppermute x2, starting transfers between devices: 5.86 us -> 6.76 us  [halos(): corner = lax.ppermute(corners[0], 'yx', self.swap_route(3))]
where the time goes in v24:
time: 55 us; the launch traced here: 54.7 us
  blocking collectives  19.3 us (35%)
  starting transfers between devices  16.2 us (29%)
  Pallas kernels  14.2 us (26%)
  waiting for transfers between devices  4.88 us (9%)
    all_to_all x2, blocking collectives, share(): return lax.all_to_all(stats, PART, 0, 0)  19.3 us
    pallas_call x11, Pallas kernels, call(): pl.pallas_call(kernel, out_shape=[jax.ShapeDtypeStruct(shape, dtype) for...  14 us
    ppermute x2, starting transfers between devices, halos(): corner = lax.ppermute(corners[0], 'yx', self.swap_route(3))  6.76 us
    ppermute x3, starting transfers between devices, swap(): lax.ppermute(block, axis, [(i, i ^ mask) for i in range(lax.axis_size(axi...  3.63 us
    ppermute x1, starting transfers between devices, swap_depth(): lax.ppermute(inner, 'gz', routes[0])  2.56 us
    ppermute x2, starting transfers between devices, halos(): y = lax.ppermute(y_edges[0], 'yx', self.swap_route(2))  1.96 us
    ppermute x2, waiting for transfers between devices, halos(): corner = lax.ppermute(corners[0], 'yx', self.swap_route(3))  1.81 us
    ppermute x2, waiting for transfers between devices, halos(): y = lax.ppermute(y_edges[0], 'yx', self.swap_route(2))  1.59 us
  transfers between devices with their start and end apart: 11, of which 4 were waited for; matrix products, arithmetic and copies ran while one was open for 0% of the time, Pallas kernels for 19%

profile of v24, /device:TPU:0, one launch (start us, length us, event | category | flops | bytes accessed | tf_op | source)
XLA Modules:
  0.0 54.7 jit_solution(252739226349179553)
XLA Ops:
  0.0 1.6 %shard_map.82 = (bf16[1,30,16,128]{3,2,1,0:T(8,128)(2,1)S(1)}, bf16[1,30,16,128]{3,2,1,0:T(8,128)(2,1)S(1)}, bf16[1,15,16,128]{3,2,1,0:T(8,128)(2,1)S(1)}, bf16[...) custom-call(bf16[16,16,16,128]{3,2,1,0:T(8,128)(2,1)} %x_in.1, bf16[27,128,128]{2,1,0:T(8,128)(2,1)} %bitcast.50, ...), custom_call_target="tpu_custom_call" | custom-call | bytes 5242880 | tf_op jit(solution)/shard_map/pallas_call | solution.py:105
  1.6 5.1 %collective-permute-start.2 = (bf16[15,16,128]{2,1,0:T(8,128)(2,1)S(1)}, bf16[15,16,128]{2,1,0:T(8,128)(2,1)S(1)}, u32[]{:S(2)}, u32[]{:S(2)}) collective-permute-start(bf16[15,16,128]{2,1,0:T(8,128)(2,1)S(1)} %bitcast.46), channel_id=1, source_target_pairs={{0,3},{1,2},{2,1},{3,0},{4,7},{5,6},{6,5},{7,4},{8,11},{9,10},{10,... | collective-permute-start | bytes 184328 | tf_op jit(solution)/shard_map/ppermute | solution.py:46
  6.7 0.0 collective-permute-start.1
  6.7 0.6 %collective-permute-start = (bf16[30,16,128]{2,1,0:T(8,128)(2,1)S(1)}, bf16[30,16,128]{2,1,0:T(8,128)(2,1)S(1)}, u32[]{:S(2)}, u32[]{:S(2)}) collective-permute-start(bf16[30,16,128]{2,1,0:T(8,128)(2,1)S(1)} %bitcast.44), channel_id=1, source_target_pairs={{0,2},{1,3},{2,0},{3,1},{4,6},{5,7},{6,4},{7,5},{8,10},{9,11},{10,... | collective-permute-start | bytes 368648 | tf_op jit(solution)/shard_map/ppermute | solution.py:44
  7.4 4.7 %shard_map.83 = (f32[16,16,16,128]{3,2,1,0:T(8,128)S(1)}, bf16[1152,384]{1,0:T(8,128)(2,1)S(1)}, bf16[1536,256]{1,0:T(8,128)(2,1)S(1)}, bf16[108,16,128]{2,1,0:T(8,128)(2,1)S(1)}) custom-call(bf16[108,16,128]{2,1,0:T(8,128)(2,1)} %bitcast.52, bf16[18,18,16,128]{3,2,1,0:T(8,128)(2,1)S(1)} %get-tuple-element.44.x, ...), custom_call_target="tpu_custom_call" | custom-call | flops 3623878656 | bytes 6291456 | tf_op jit(solution)/shard_map/pallas_call | solution.py:105
  12.1 0.0 collective-permute-done.2
  12.1 1.4 %collective-permute-done.1 = bf16[30,16,128]{2,1,0:T(8,128)(2,1)S(1)} collective-permute-done((bf16[30,16,128]{2,1,0:T(8,128)(2,1)S(1)}, bf16[30,16,128]{2,1,0:T(8,128)(2,1)S(1)}, u32[]{:S(2)}, u32[]{:S(2)}) %collective-permute-start.1) | collective-permute-done | bytes 122912 | tf_op jit(solution)/shard_map/ppermute | solution.py:45
  13.5 1.6 %collective-permute-done = bf16[30,16,128]{2,1,0:T(8,128)(2,1)S(1)} collective-permute-done((bf16[30,16,128]{2,1,0:T(8,128)(2,1)S(1)}, bf16[30,16,128]{2,1,0:T(8,128)(2,1)S(1)}, u32[]{:S(2)}, u32[]{:S(2)}) %collective-permute-start) | collective-permute-done | bytes 122912 | tf_op jit(solution)/shard_map/ppermute | solution.py:44
  15.1 0.1 shard_map.85
  15.2 0.7 %collective-permute-start.4 = (bf16[57,16,128]{2,1,0:T(8,128)(2,1)S(1)}, bf16[57,16,128]{2,1,0:T(8,128)(2,1)S(1)}, u32[]{:S(2)}, u32[]{:S(2)}) collective-permute-start(bf16[57,16,128]{2,1,0:T(8,128)(2,1)S(1)} %get-tuple-element.57), channel_id=1, source_target_pairs={{4,8},{8,4},{5,9},{9,5},{6,10},{10,6},{7,11},{11,7},{20,24},{24,20... | collective-permute-start | bytes 700424 | tf_op jit(solution)/shard_map/ppermute | solution.py:63
  15.8 1.6 %collective-permute-start.5 = (bf16[1,4,14,16,128]{4,3,2,1,0:T(8,128)(2,1)S(1)}, bf16[1,4,14,16,128]{4,3,2,1,0:T(8,128)(2,1)S(1)}, u32[]{:S(2)}, u32[]{:S(2)}) collective-permute-start(bf16[1,4,14,16,128]{4,3,2,1,0:T(8,128)(2,1)S(1)} %bitcast.35), channel_id=1, source_target_pairs={{0,16},{16,0},{1,17},{17,1},{2,18},{18,2},{3,19},{19,3},{4,20},{20... | collective-permute-start | bytes 688136 | tf_op jit(solution)/shard_map/ppermute | solution.py:94
  17.5 2.6 %collective-permute-start.3 = (bf16[55,16,128]{2,1,0:T(8,128)(2,1)S(1)}, bf16[55,16,128]{2,1,0:T(8,128)(2,1)S(1)}, u32[]{:S(2)}, u32[]{:S(2)}) collective-permute-start(bf16[55,16,128]{2,1,0:T(8,128)(2,1)S(1)} %get-tuple-element.55), channel_id=1, source_target_pairs={{0,4},{4,0},{8,12},{12,8},{1,5},{5,1},{9,13},{13,9},{2,6},{6,2},{1... | collective-permute-start | bytes 675848 | tf_op jit(solution)/shard_map/ppermute | solution.py:63
  20.0 1.0 %shard_map.84 = (f32[14,16,16,128]{3,2,1,0:T(8,128)S(1)}, f32[4,16,16,128]{3,2,1,0:T(8,128)S(1)}, f32[16,128]{1,0:T(8,128)S(1)}) custom-call(f32[16,16,16,128]{3,2,1,0:T(8,128)S(1)} %get-tuple-element.47.own, bf16[1,30,16,128]{3,2,1,0:T(8,128)(2,1)S(1)} %bitcast.32, bf16[1,30,16,128]{3,2,1,0:T(8,128)(2,1)S(1)} %bitcast.30, ...), custom_call_target="tpu_custom_call" | custom-call | tf_op jit(solution)/shard_map/pallas_call | solution.py:105
  21.1 0.1 collective-permute-done.3.face
  21.1 1.1 %shard_map.86.ends = f32[6,16,16,128]{3,2,1,0:T(8,128)S(1)} custom-call(bf16[18,18,16,128]{3,2,1,0:T(8,128)(2,1)S(1)} %get-tuple-element.44.x, f32[4,16,16,128]{3,2,1,0:T(8,128)S(1)} %get-tuple-element.54.partial, bf16[55,16,128]{2,1,0:T(8,128)(2,1)S(1)} %collective-permute-done.3.face, bf16[1152,384]{1,0:T(8,128)(2,1)S(1)} %get-tuple-element.51.taps, ...), custom_call_target="tpu_custom_call" | custom-call | tf_op jit(solution)/shard_map/pallas_call | solution.py:105
  22.3 0.0 collective-permute-done.4.face
  22.3 0.6 %shard_map.87 = (f32[6,16,16,128]{3,2,1,0:T(8,128)S(1)}, f32[16,2,128]{2,1,0:T(2,128)S(1)}) custom-call(bf16[18,18,16,128]{3,2,1,0:T(8,128)(2,1)S(1)} %get-tuple-element.44.x, f32[16,128]{1,0:T(8,128)S(1)} %get-tuple-element.53.middle_stats, f32[6,16,16,128]{3,2,1,0:T(8,128)S(1)} %shard_map.86.ends, bf16[57,16,128]{2,1,0:T(8,128)(2,1)S(1)} %collective-permute-done.4.face, ...), custom_call_target="tpu_custom_call" | custom-call | tf_op jit(solution)/shard_map/pallas_call | solution.py:105
  22.9 0.0 collective-permute-done.5.refs_1_
  23.0 1.9 %collective-permute-start.6 = (bf16[2,3,14,16,128]{4,3,2,1,0:T(8,128)(2,1)S(1)}, bf16[2,3,14,16,128]{4,3,2,1,0:T(8,128)(2,1)S(1)}, u32[]{:S(2)}, u32[]{:S(2)}) collective-permute-start(bf16[2,3,14,16,128]{4,3,2,1,0:T(8,128)(2,1)S(1)} %bitcast.27), channel_id=1, source_target_pairs={{0,8},{4,12},{8,0},{12,4},{1,9},{5,13},{9,1},{13,5},{2,10},{6,14},... | collective-permute-start | bytes 1032200 | tf_op jit(solution)/shard_map/ppermute | solution.py:94
  24.8 0.0 copy-start.3
  24.8 0.0 copy-start.4
  24.8 0.1 shard_map.88.ends
  24.9 9.6 %all_to_all.10.stats = f32[16,2,128]{2,1,0:T(2,128)S(1)} all-to-all(f32[16,2,128]{2,1,0:T(2,128)S(1)} %get-tuple-element.63), channel_id=1, replica_groups=mesh['cand'=2,'gz'=4,'yx'=4] {'gz','yx'}, dimensions={0} | all-to-all | bytes 32768 | tf_op jit(solution)/shard_map/all_to_all | solution.py:98
  34.5 0.0 collective-permute-done.6.refs_1_
  34.5 0.2 collective-permute-start.7
  34.7 0.0 copy-done.3
  34.7 0.0 copy-done.4
  34.7 1.1 %shard_map.90 = (bf16[16,16,16,128]{3,2,1,0:T(8,128)(2,1)S(1)}, f32[10,8,8,128]{3,2,1,0:T(8,128)S(1)}, bf16[1,80,128]{2,1,0:T(8,128)(2,1)S(1)}, bf16[1,80,128]{2,1,0:T(8,128)(2,1)S(1)}, bf16[1,80,128]{2,1,0:T(8,128)(2,1)S(1)}) custom-call(f32[14,16,16,128]{3,2,1,0:T(8,128)S(1)} %get-tuple-element.52.inner, f32[6,16,16,128]{3,2,1,0:T(8,128)S(1)} %shard_map.88.ends, ...), custom_call_target="tpu_custom_call" | custom-call | flops 10485760 | bytes 3145728 | tf_op jit(solution)/shard_map/pallas_call | solution.py:105
  35.8 1.3 %collective-permute-start.8 = (bf16[80,128]{1,0:T(8,128)(2,1)S(1)}, bf16[80,128]{1,0:T(8,128)(2,1)S(1)}, u32[]{:S(2)}, u32[]{:S(2)}) collective-permute-start(bf16[80,128]{1,0:T(8,128)(2,1)S(1)} %bitcast.49), channel_id=1, source_target_pairs={{0,2},{1,3},{2,0},{3,1},{4,6},{5,7},{6,4},{7,5},{8,10},{9,11},{10,... | collective-permute-start | bytes 61448 | tf_op jit(solution)/shard_map/ppermute | solution.py:44
  37.2 1.6 %collective-permute-start.9 = (bf16[80,128]{1,0:T(8,128)(2,1)S(1)}, bf16[80,128]{1,0:T(8,128)(2,1)S(1)}, u32[]{:S(2)}, u32[]{:S(2)}) collective-permute-start(bf16[80,128]{1,0:T(8,128)(2,1)S(1)} %bitcast.48), channel_id=1, source_target_pairs={{0,3},{1,2},{2,1},{3,0},{4,7},{5,6},{6,5},{7,4},{8,11},{9,10},{10,... | collective-permute-start | bytes 61448 | tf_op jit(solution)/shard_map/ppermute | solution.py:46
  38.8 0.6 %collective-permute-start.10 = (bf16[80,128]{1,0:T(8,128)(2,1)S(1)}, bf16[80,128]{1,0:T(8,128)(2,1)S(1)}, u32[]{:S(2)}, u32[]{:S(2)}) collective-permute-start(bf16[80,128]{1,0:T(8,128)(2,1)S(1)} %bitcast.47), channel_id=1, source_target_pairs={{0,1},{1,0},{2,3},{3,2},{4,5},{5,4},{6,7},{7,6},{8,9},{9,8},{10,11... | collective-permute-start | bytes 61448 | tf_op jit(solution)/shard_map/ppermute | solution.py:45
  39.4 0.0 collective-permute-done.7.refs_1_
  39.4 0.1 shard_map.92
  39.5 1.4 %shard_map.93 = (f32[2,512,128]{2,1,0:T(8,128)S(1)}, bf16[4,108,16,128]{3,2,1,0:T(8,128)(2,1)S(1)}) custom-call(f32[10,8,8,128]{3,2,1,0:T(8,128)S(1)} %get-tuple-element.66.pooled, bf16[108,16,128]{2,1,0:T(8,128)(2,1)S(1)} %get-tuple-element.67.own, bf16[8,3,14,16,128]{4,3,2,1,0:T(8,128)(2,1)S(1)} %bitcast.26), custom_call_target="tpu_custom_call" | custom-call | flops 905969664 | bytes 4194304 | tf_op jit(solution)/shard_map/pallas_call | solution.py:105
  41.0 0.0 copy-start
  41.0 0.0 copy-start.1
  41.0 0.0 copy-start.2
  41.0 0.0 collective-permute-done.8
  41.0 1.8 %collective-permute-done.9 = bf16[80,128]{1,0:T(8,128)(2,1)S(1)} collective-permute-done((bf16[80,128]{1,0:T(8,128)(2,1)S(1)}, bf16[80,128]{1,0:T(8,128)(2,1)S(1)}, u32[]{:S(2)}, u32[]{:S(2)}) %collective-permute-start.9) | collective-permute-done | bytes 20512 | tf_op jit(solution)/shard_map/ppermute | solution.py:46
  42.8 0.0 collective-permute-done.10
  42.8 0.7 %shard_map.94 = (f32[2,512,128]{2,1,0:T(8,128)S(1)}, f32[16,2,256]{2,1,0:T(2,128)S(1)}) custom-call(f32[2,512,128]{2,1,0:T(8,128)S(1)} %get-tuple-element.69.own, bf16[1,80,128]{2,1,0:T(8,128)(2,1)S(1)} %bitcast.37, bf16[1,80,128]{2,1,0:T(8,128)(2,1)S(1)} %bitcast.38, bf16[1,80,128]{2,1,0:T(8,128)(2,1)S(1)} %bitcast.39, ...), custom_call_target="tpu_custom_call" | custom-call | flops 67108864 | bytes 3145728 | tf_op jit(solution)/shard_map/pallas_call | solution.py:105
  43.5 9.7 %all_to_all.11.stats = f32[16,2,256]{2,1,0:T(2,128)S(1)} all-to-all(f32[16,2,256]{2,1,0:T(2,128)S(1)} %get-tuple-element.75), channel_id=1, replica_groups=mesh['cand'=2,'gz'=4,'yx'=4] {'gz','yx'}, dimensions={0} | all-to-all | bytes 65536 | tf_op jit(solution)/shard_map/all_to_all | solution.py:98
  53.2 0.0 copy-done
  53.2 0.0 copy-done.1
  53.2 0.0 copy-done.2
  53.2 1.5 %shard_map.95 = bf16[16,16,16,128]{3,2,1,0:T(8,128)(2,1)} custom-call(f32[2,512,128]{2,1,0:T(8,128)S(1)} %get-tuple-element.74.act, f32[16,2,256]{2,1,0:T(2,128)S(1)} %all_to_all.11.stats, f32[1,256]{1,0:T(1,128)S(1)} %bitcast.40, f32[1,256]{1,0:T(1,128)S(1)} %bitcast.41, bf16[256,128]{1,0:T(8,128)(2,1)S(1)} %copy-done, ...), custom_call_target="tpu_custom_call" | custom-call | flops 67108864 | bytes 3145728 | tf_op jit(solution)/shard_map/pallas_call | solution.py:105
  (2 shorter events, 0.1 us)
Async XLA Ops:
  1.6 10.5 %collective-permute-start.2 = (bf16[15,16,128]{2,1,0:T(8,128)(2,1)S(1)}, bf16[15,16,128]{2,1,0:T(8,128)(2,1)S(1)}, u32[]{:S(2)}, u32[]{:S(2)}) collective-permute-start(bf16[15,16,128]{2,1,0:T(8,128)(2,1)S(1)} %bitcast.46), channel_id=1, source_target_pairs={{0,3},{1,2},{2,1},{3,0},{4,7},{5,6},{6,5},{7,4},{8,11},{9,10},{10,... | collective-permute-start | bytes 184328 | tf_op jit(solution)/shard_map/ppermute | solution.py:46
  6.7 6.8 %collective-permute-start.1 = (bf16[30,16,128]{2,1,0:T(8,128)(2,1)S(1)}, bf16[30,16,128]{2,1,0:T(8,128)(2,1)S(1)}, u32[]{:S(2)}, u32[]{:S(2)}) collective-permute-start(bf16[30,16,128]{2,1,0:T(8,128)(2,1)S(1)} %bitcast.45), channel_id=1, source_target_pairs={{0,1},{1,0},{2,3},{3,2},{4,5},{5,4},{6,7},{7,6},{8,9},{9,8},{10,11... | collective-permute-start | bytes 368648 | tf_op jit(solution)/shard_map/ppermute | solution.py:45
  6.7 8.4 %collective-permute-start = (bf16[30,16,128]{2,1,0:T(8,128)(2,1)S(1)}, bf16[30,16,128]{2,1,0:T(8,128)(2,1)S(1)}, u32[]{:S(2)}, u32[]{:S(2)}) collective-permute-start(bf16[30,16,128]{2,1,0:T(8,128)(2,1)S(1)} %bitcast.44), channel_id=1, source_target_pairs={{0,2},{1,3},{2,0},{3,1},{4,6},{5,7},{6,4},{7,5},{8,10},{9,11},{10,... | collective-permute-start | bytes 368648 | tf_op jit(solution)/shard_map/ppermute | solution.py:44
  15.2 7.1 %collective-permute-start.4 = (bf16[57,16,128]{2,1,0:T(8,128)(2,1)S(1)}, bf16[57,16,128]{2,1,0:T(8,128)(2,1)S(1)}, u32[]{:S(2)}, u32[]{:S(2)}) collective-permute-start(bf16[57,16,128]{2,1,0:T(8,128)(2,1)S(1)} %get-tuple-element.57), channel_id=1, source_target_pairs={{4,8},{8,4},{5,9},{9,5},{6,10},{10,6},{7,11},{11,7},{20,24},{24,20... | collective-permute-start | bytes 700424 | tf_op jit(solution)/shard_map/ppermute | solution.py:63
  15.8 7.1 %collective-permute-start.5 = (bf16[1,4,14,16,128]{4,3,2,1,0:T(8,128)(2,1)S(1)}, bf16[1,4,14,16,128]{4,3,2,1,0:T(8,128)(2,1)S(1)}, u32[]{:S(2)}, u32[]{:S(2)}) collective-permute-start(bf16[1,4,14,16,128]{4,3,2,1,0:T(8,128)(2,1)S(1)} %bitcast.35), channel_id=1, source_target_pairs={{0,16},{16,0},{1,17},{17,1},{2,18},{18,2},{3,19},{19,3},{4,20},{20... | collective-permute-start | bytes 688136 | tf_op jit(solution)/shard_map/ppermute | solution.py:94
  17.5 3.7 %collective-permute-start.3 = (bf16[55,16,128]{2,1,0:T(8,128)(2,1)S(1)}, bf16[55,16,128]{2,1,0:T(8,128)(2,1)S(1)}, u32[]{:S(2)}, u32[]{:S(2)}) collective-permute-start(bf16[55,16,128]{2,1,0:T(8,128)(2,1)S(1)} %get-tuple-element.55), channel_id=1, source_target_pairs={{0,4},{4,0},{8,12},{12,8},{1,5},{5,1},{9,13},{13,9},{2,6},{6,2},{1... | collective-permute-start | bytes 675848 | tf_op jit(solution)/shard_map/ppermute | solution.py:63
  23.0 11.5 %collective-permute-start.6 = (bf16[2,3,14,16,128]{4,3,2,1,0:T(8,128)(2,1)S(1)}, bf16[2,3,14,16,128]{4,3,2,1,0:T(8,128)(2,1)S(1)}, u32[]{:S(2)}, u32[]{:S(2)}) collective-permute-start(bf16[2,3,14,16,128]{4,3,2,1,0:T(8,128)(2,1)S(1)} %bitcast.27), channel_id=1, source_target_pairs={{0,8},{4,12},{8,0},{12,4},{1,9},{5,13},{9,1},{13,5},{2,10},{6,14},... | collective-permute-start | bytes 1032200 | tf_op jit(solution)/shard_map/ppermute | solution.py:94
  24.8 9.9 %copy-start.3 = (f32[128]{0:T(128)S(1)}, f32[128]{0:T(128)}, u32[]{:S(2)}) copy-start(f32[128]{0:T(128)} %param.10) | copy-start | bytes 1540
  24.8 9.9 %copy-start.4 = (f32[128]{0:T(128)S(1)}, f32[128]{0:T(128)}, u32[]{:S(2)}) copy-start(f32[128]{0:T(128)} %param.11) | copy-start | bytes 1540
  34.5 4.9 %collective-permute-start.7 = (bf16[4,3,14,16,128]{4,3,2,1,0:T(8,128)(2,1)S(1)}, bf16[4,3,14,16,128]{4,3,2,1,0:T(8,128)(2,1)S(1)}, u32[]{:S(2)}, u32[]{:S(2)}) collective-permute-start(bf16[4,3,14,16,128]{4,3,2,1,0:T(8,128)(2,1)S(1)} %bitcast.24), channel_id=1, source_target_pairs={{0,4},{4,0},{8,12},{12,8},{1,5},{5,1},{9,13},{13,9},{2,6},{6,2},{1... | collective-permute-start | bytes 2064392 | tf_op jit(solution)/shard_map/ppermute | solution.py:94
  35.8 5.2 %collective-permute-start.8 = (bf16[80,128]{1,0:T(8,128)(2,1)S(1)}, bf16[80,128]{1,0:T(8,128)(2,1)S(1)}, u32[]{:S(2)}, u32[]{:S(2)}) collective-permute-start(bf16[80,128]{1,0:T(8,128)(2,1)S(1)} %bitcast.49), channel_id=1, source_target_pairs={{0,2},{1,3},{2,0},{3,1},{4,6},{5,7},{6,4},{7,5},{8,10},{9,11},{10,... | collective-permute-start | bytes 61448 | tf_op jit(solution)/shard_map/ppermute | solution.py:44
  37.2 5.6 %collective-permute-start.9 = (bf16[80,128]{1,0:T(8,128)(2,1)S(1)}, bf16[80,128]{1,0:T(8,128)(2,1)S(1)}, u32[]{:S(2)}, u32[]{:S(2)}) collective-permute-start(bf16[80,128]{1,0:T(8,128)(2,1)S(1)} %bitcast.48), channel_id=1, source_target_pairs={{0,3},{1,2},{2,1},{3,0},{4,7},{5,6},{6,5},{7,4},{8,11},{9,10},{10,... | collective-permute-start | bytes 61448 | tf_op jit(solution)/shard_map/ppermute | solution.py:46
  38.8 4.0 %collective-permute-start.10 = (bf16[80,128]{1,0:T(8,128)(2,1)S(1)}, bf16[80,128]{1,0:T(8,128)(2,1)S(1)}, u32[]{:S(2)}, u32[]{:S(2)}) collective-permute-start(bf16[80,128]{1,0:T(8,128)(2,1)S(1)} %bitcast.47), channel_id=1, source_target_pairs={{0,1},{1,0},{2,3},{3,2},{4,5},{5,4},{6,7},{7,6},{8,9},{9,8},{10,11... | collective-permute-start | bytes 61448 | tf_op jit(solution)/shard_map/ppermute | solution.py:45
  41.0 12.2 %copy-start = (bf16[256,128]{1,0:T(8,128)(2,1)S(1)}, bf16[256,128]{1,0:T(8,128)(2,1)}, u32[]{:S(2)}) copy-start(bf16[256,128]{1,0:T(8,128)(2,1)} %up.1) | copy-start | bytes 196612
  41.0 12.2 %copy-start.1 = (f32[256]{0:T(256)S(1)}, f32[256]{0:T(256)}, u32[]{:S(2)}) copy-start(f32[256]{0:T(256)} %param.13) | copy-start | bytes 3076
  41.0 12.2 %copy-start.2 = (f32[256]{0:T(256)S(1)}, f32[256]{0:T(256)}, u32[]{:S(2)}) copy-start(f32[256]{0:T(256)} %param.14) | copy-start | bytes 3076

commit v25 on v22

--- a/solution.py
+++ b/solution.py
@@ -626,7 +626,7 @@
         act[half] = total[:, half * 128 : half * 128 + 128]
 
 
-def deep_rim_kernel(ny, nx, own, y_halos, x_halos, corners, weight, act, stats, line):
+def deep_rim_kernel(ny, nx, own, x_halos, y_halos, corners, weight, act, stats, line):
     depth, deep = line.shape[0], line.shape[1] - 16
     halves = act.shape[0]
     f32 = jnp.float32
@@ -881,8 +881,8 @@
         [halves, ((devices, 2, deep_channels), f32)],
         [((deep + 2, 24, channels), f32)],
         deep_act,
+        jnp.stack(x),
         jnp.stack(y),
-        jnp.stack(x),
         jnp.stack(corner),
         weight,
         flops=4 * channels * deep_channels * deep**3,

time: 54.6 us -> 55.2 us (1.011)
    ppermute x2, starting transfers between devices: 1.96 us -> 3.24 us  [halos(): y = lax.ppermute(y_edges[0], 'yx', self.swap_route(2))]
    ppermute x2, starting transfers between devices: 2.42 us -> 1.14 us  [halos(): x = lax.ppermute(x_edges[0], 'yx', self.swap_route(1))]
where the time goes in v25:
time: 55.2 us; the launch traced here: 55 us
  blocking collectives  19.9 us (36%)
  starting transfers between devices  17.1 us (31%)
  Pallas kernels  14.2 us (26%)
  waiting for transfers between devices  3.58 us (6%)
    all_to_all x2, blocking collectives, share(): return lax.all_to_all(stats, PART, 0, 0)  19.9 us
    pallas_call x11, Pallas kernels, call(): pl.pallas_call(kernel, out_shape=[jax.ShapeDtypeStruct(shape, dtype) for...  14 us
    ppermute x2, starting transfers between devices, halos(): corner = lax.ppermute(corners[0], 'yx', self.swap_route(3))  5.86 us
    ppermute x3, starting transfers between devices, swap(): lax.ppermute(block, axis, [(i, i ^ mask) for i in range(lax.axis_size(axi...  3.63 us
    ppermute x2, starting transfers between devices, halos(): y = lax.ppermute(y_edges[0], 'yx', self.swap_route(2))  3.24 us
    ppermute x1, starting transfers between devices, swap_depth(): lax.ppermute(inner, 'gz', routes[0])  2.56 us
    ppermute x2, waiting for transfers between devices, halos(): y = lax.ppermute(y_edges[0], 'yx', self.swap_route(2))  2.1 us
    ppermute x2, waiting for transfers between devices, halos(): x = lax.ppermute(x_edges[0], 'yx', self.swap_route(1))  1.4 us
  transfers between devices with their start and end apart: 11, of which 4 were waited for; matrix products, arithmetic and copies ran while one was open for 0% of the time, Pallas kernels for 19%

profile of v25, /device:TPU:0, one launch (start us, length us, event | category | flops | bytes accessed | tf_op | source)
XLA Modules:
  0.0 55.0 jit_solution(12428232775937798173)
XLA Ops:
  0.0 1.6 %shard_map.82 = (bf16[1,30,16,128]{3,2,1,0:T(8,128)(2,1)S(1)}, bf16[1,30,16,128]{3,2,1,0:T(8,128)(2,1)S(1)}, bf16[1,15,16,128]{3,2,1,0:T(8,128)(2,1)S(1)}, bf16[...) custom-call(bf16[16,16,16,128]{3,2,1,0:T(8,128)(2,1)} %x_in.1, bf16[27,128,128]{2,1,0:T(8,128)(2,1)} %bitcast.50, ...), custom_call_target="tpu_custom_call" | custom-call | bytes 5242880 | tf_op jit(solution)/shard_map/pallas_call | solution.py:105
  1.6 5.1 %collective-permute-start.2 = (bf16[15,16,128]{2,1,0:T(8,128)(2,1)S(1)}, bf16[15,16,128]{2,1,0:T(8,128)(2,1)S(1)}, u32[]{:S(2)}, u32[]{:S(2)}) collective-permute-start(bf16[15,16,128]{2,1,0:T(8,128)(2,1)S(1)} %bitcast.46), channel_id=1, source_target_pairs={{0,3},{1,2},{2,1},{3,0},{4,7},{5,6},{6,5},{7,4},{8,11},{9,10},{10,... | collective-permute-start | bytes 184328 | tf_op jit(solution)/shard_map/ppermute | solution.py:46
  6.7 0.0 collective-permute-start.1
  6.7 0.6 %collective-permute-start = (bf16[30,16,128]{2,1,0:T(8,128)(2,1)S(1)}, bf16[30,16,128]{2,1,0:T(8,128)(2,1)S(1)}, u32[]{:S(2)}, u32[]{:S(2)}) collective-permute-start(bf16[30,16,128]{2,1,0:T(8,128)(2,1)S(1)} %bitcast.44), channel_id=1, source_target_pairs={{0,2},{1,3},{2,0},{3,1},{4,6},{5,7},{6,4},{7,5},{8,10},{9,11},{10,... | collective-permute-start | bytes 368648 | tf_op jit(solution)/shard_map/ppermute | solution.py:44
  7.4 4.7 %shard_map.83 = (f32[16,16,16,128]{3,2,1,0:T(8,128)S(1)}, bf16[1152,384]{1,0:T(8,128)(2,1)S(1)}, bf16[1536,256]{1,0:T(8,128)(2,1)S(1)}, bf16[108,16,128]{2,1,0:T(8,128)(2,1)S(1)}) custom-call(bf16[108,16,128]{2,1,0:T(8,128)(2,1)} %bitcast.52, bf16[18,18,16,128]{3,2,1,0:T(8,128)(2,1)S(1)} %get-tuple-element.44.x, ...), custom_call_target="tpu_custom_call" | custom-call | flops 3623878656 | bytes 6291456 | tf_op jit(solution)/shard_map/pallas_call | solution.py:105
  12.1 0.0 collective-permute-done.2
  12.1 1.4 %collective-permute-done.1 = bf16[30,16,128]{2,1,0:T(8,128)(2,1)S(1)} collective-permute-done((bf16[30,16,128]{2,1,0:T(8,128)(2,1)S(1)}, bf16[30,16,128]{2,1,0:T(8,128)(2,1)S(1)}, u32[]{:S(2)}, u32[]{:S(2)}) %collective-permute-start.1) | collective-permute-done | bytes 122912 | tf_op jit(solution)/shard_map/ppermute | solution.py:45
  13.5 1.6 %collective-permute-done = bf16[30,16,128]{2,1,0:T(8,128)(2,1)S(1)} collective-permute-done((bf16[30,16,128]{2,1,0:T(8,128)(2,1)S(1)}, bf16[30,16,128]{2,1,0:T(8,128)(2,1)S(1)}, u32[]{:S(2)}, u32[]{:S(2)}) %collective-permute-start) | collective-permute-done | bytes 122912 | tf_op jit(solution)/shard_map/ppermute | solution.py:44
  15.1 0.1 shard_map.85
  15.2 0.7 %collective-permute-start.4 = (bf16[57,16,128]{2,1,0:T(8,128)(2,1)S(1)}, bf16[57,16,128]{2,1,0:T(8,128)(2,1)S(1)}, u32[]{:S(2)}, u32[]{:S(2)}) collective-permute-start(bf16[57,16,128]{2,1,0:T(8,128)(2,1)S(1)} %get-tuple-element.57), channel_id=1, source_target_pairs={{4,8},{8,4},{5,9},{9,5},{6,10},{10,6},{7,11},{11,7},{20,24},{24,20... | collective-permute-start | bytes 700424 | tf_op jit(solution)/shard_map/ppermute | solution.py:63
  15.8 1.6 %collective-permute-start.5 = (bf16[1,4,14,16,128]{4,3,2,1,0:T(8,128)(2,1)S(1)}, bf16[1,4,14,16,128]{4,3,2,1,0:T(8,128)(2,1)S(1)}, u32[]{:S(2)}, u32[]{:S(2)}) collective-permute-start(bf16[1,4,14,16,128]{4,3,2,1,0:T(8,128)(2,1)S(1)} %bitcast.35), channel_id=1, source_target_pairs={{0,16},{16,0},{1,17},{17,1},{2,18},{18,2},{3,19},{19,3},{4,20},{20... | collective-permute-start | bytes 688136 | tf_op jit(solution)/shard_map/ppermute | solution.py:94
  17.5 2.6 %collective-permute-start.3 = (bf16[55,16,128]{2,1,0:T(8,128)(2,1)S(1)}, bf16[55,16,128]{2,1,0:T(8,128)(2,1)S(1)}, u32[]{:S(2)}, u32[]{:S(2)}) collective-permute-start(bf16[55,16,128]{2,1,0:T(8,128)(2,1)S(1)} %get-tuple-element.55), channel_id=1, source_target_pairs={{0,4},{4,0},{8,12},{12,8},{1,5},{5,1},{9,13},{13,9},{2,6},{6,2},{1... | collective-permute-start | bytes 675848 | tf_op jit(solution)/shard_map/ppermute | solution.py:63
  20.0 1.0 %shard_map.84 = (f32[14,16,16,128]{3,2,1,0:T(8,128)S(1)}, f32[4,16,16,128]{3,2,1,0:T(8,128)S(1)}, f32[16,128]{1,0:T(8,128)S(1)}) custom-call(f32[16,16,16,128]{3,2,1,0:T(8,128)S(1)} %get-tuple-element.47.own, bf16[1,30,16,128]{3,2,1,0:T(8,128)(2,1)S(1)} %bitcast.32, bf16[1,30,16,128]{3,2,1,0:T(8,128)(2,1)S(1)} %bitcast.30, ...), custom_call_target="tpu_custom_call" | custom-call | tf_op jit(solution)/shard_map/pallas_call | solution.py:105
  21.1 0.1 collective-permute-done.3.face
  21.1 1.1 %shard_map.86.ends = f32[6,16,16,128]{3,2,1,0:T(8,128)S(1)} custom-call(bf16[18,18,16,128]{3,2,1,0:T(8,128)(2,1)S(1)} %get-tuple-element.44.x, f32[4,16,16,128]{3,2,1,0:T(8,128)S(1)} %get-tuple-element.54.partial, bf16[55,16,128]{2,1,0:T(8,128)(2,1)S(1)} %collective-permute-done.3.face, bf16[1152,384]{1,0:T(8,128)(2,1)S(1)} %get-tuple-element.51.taps, ...), custom_call_target="tpu_custom_call" | custom-call | tf_op jit(solution)/shard_map/pallas_call | solution.py:105
  22.3 0.0 collective-permute-done.4.face
  22.3 0.6 %shard_map.87 = (f32[6,16,16,128]{3,2,1,0:T(8,128)S(1)}, f32[16,2,128]{2,1,0:T(2,128)S(1)}) custom-call(bf16[18,18,16,128]{3,2,1,0:T(8,128)(2,1)S(1)} %get-tuple-element.44.x, f32[16,128]{1,0:T(8,128)S(1)} %get-tuple-element.53.middle_stats, f32[6,16,16,128]{3,2,1,0:T(8,128)S(1)} %shard_map.86.ends, bf16[57,16,128]{2,1,0:T(8,128)(2,1)S(1)} %collective-permute-done.4.face, ...), custom_call_target="tpu_custom_call" | custom-call | tf_op jit(solution)/shard_map/pallas_call | solution.py:105
  22.9 0.0 collective-permute-done.5.refs_1_
  23.0 1.9 %collective-permute-start.6 = (bf16[2,3,14,16,128]{4,3,2,1,0:T(8,128)(2,1)S(1)}, bf16[2,3,14,16,128]{4,3,2,1,0:T(8,128)(2,1)S(1)}, u32[]{:S(2)}, u32[]{:S(2)}) collective-permute-start(bf16[2,3,14,16,128]{4,3,2,1,0:T(8,128)(2,1)S(1)} %bitcast.27), channel_id=1, source_target_pairs={{0,8},{4,12},{8,0},{12,4},{1,9},{5,13},{9,1},{13,5},{2,10},{6,14},... | collective-permute-start | bytes 1032200 | tf_op jit(solution)/shard_map/ppermute | solution.py:94
  24.8 0.0 copy-start.3
  24.8 0.0 copy-start.4
  24.8 0.1 shard_map.88.ends
  24.9 9.6 %all_to_all.10.stats = f32[16,2,128]{2,1,0:T(2,128)S(1)} all-to-all(f32[16,2,128]{2,1,0:T(2,128)S(1)} %get-tuple-element.63), channel_id=1, replica_groups=mesh['cand'=2,'gz'=4,'yx'=4] {'gz','yx'}, dimensions={0} | all-to-all | bytes 32768 | tf_op jit(solution)/shard_map/all_to_all | solution.py:98
  34.5 0.0 collective-permute-done.6.refs_1_
  34.5 0.2 collective-permute-start.7
  34.7 0.0 copy-done.3
  34.7 0.0 copy-done.4
  34.7 1.1 %shard_map.90 = (bf16[16,16,16,128]{3,2,1,0:T(8,128)(2,1)S(1)}, f32[10,8,8,128]{3,2,1,0:T(8,128)S(1)}, bf16[1,80,128]{2,1,0:T(8,128)(2,1)S(1)}, bf16[1,80,128]{2,1,0:T(8,128)(2,1)S(1)}, f32[1,16,128]{2,1,0:T(8,128)S(1)}) custom-call(f32[14,16,16,128]{3,2,1,0:T(8,128)S(1)} %get-tuple-element.52.inner, f32[6,16,16,128]{3,2,1,0:T(8,128)S(1)} %shard_map.88.ends, ...), custom_call_target="tpu_custom_call" | custom-call | flops 10485760 | bytes 3145728 | tf_op jit(solution)/shard_map/pallas_call | solution.py:105
  35.9 0.7 %collective-permute-start.10 = (f32[16,128]{1,0:T(8,128)S(1)}, f32[16,128]{1,0:T(8,128)S(1)}, u32[]{:S(2)}, u32[]{:S(2)}) collective-permute-start(f32[16,128]{1,0:T(8,128)S(1)} %bitcast.49), channel_id=1, source_target_pairs={{0,3},{1,2},{2,1},{3,0},{4,7},{5,6},{6,5},{7,4},{8,11},{9,10},{10,... | collective-permute-start | bytes 24584 | tf_op jit(solution)/shard_map/ppermute | solution.py:46
  36.6 1.1 %collective-permute-start.8 = (bf16[80,128]{1,0:T(8,128)(2,1)S(1)}, bf16[80,128]{1,0:T(8,128)(2,1)S(1)}, u32[]{:S(2)}, u32[]{:S(2)}) collective-permute-start(bf16[80,128]{1,0:T(8,128)(2,1)S(1)} %bitcast.48), channel_id=1, source_target_pairs={{0,1},{1,0},{2,3},{3,2},{4,5},{5,4},{6,7},{7,6},{8,9},{9,8},{10,11... | collective-permute-start | bytes 61448 | tf_op jit(solution)/shard_map/ppermute | solution.py:45
  37.7 2.6 %collective-permute-start.9 = (bf16[80,128]{1,0:T(8,128)(2,1)S(1)}, bf16[80,128]{1,0:T(8,128)(2,1)S(1)}, u32[]{:S(2)}, u32[]{:S(2)}) collective-permute-start(bf16[80,128]{1,0:T(8,128)(2,1)S(1)} %bitcast.47), channel_id=1, source_target_pairs={{0,2},{1,3},{2,0},{3,1},{4,6},{5,7},{6,4},{7,5},{8,10},{9,11},{10,... | collective-permute-start | bytes 61448 | tf_op jit(solution)/shard_map/ppermute | solution.py:44
  40.3 0.0 collective-permute-done.7.refs_1_
  40.3 0.1 shard_map.92
  40.4 1.4 %shard_map.93 = (f32[2,512,128]{2,1,0:T(8,128)S(1)}, bf16[4,108,16,128]{3,2,1,0:T(8,128)(2,1)S(1)}) custom-call(f32[10,8,8,128]{3,2,1,0:T(8,128)S(1)} %get-tuple-element.66.pooled, bf16[108,16,128]{2,1,0:T(8,128)(2,1)S(1)} %get-tuple-element.67.own, bf16[8,3,14,16,128]{4,3,2,1,0:T(8,128)(2,1)S(1)} %bitcast.26), custom_call_target="tpu_custom_call" | custom-call | flops 905969664 | bytes 4194304 | tf_op jit(solution)/shard_map/pallas_call | solution.py:105
  41.9 0.0 copy-start
  41.9 0.0 copy-start.1
  41.9 0.0 copy-start.2
  41.9 0.0 collective-permute-done.10
  41.9 0.0 collective-permute-done.8
  41.9 0.5 collective-permute-done.9
  42.4 0.7 %shard_map.94 = (f32[2,512,128]{2,1,0:T(8,128)S(1)}, f32[16,2,256]{2,1,0:T(2,128)S(1)}) custom-call(f32[2,512,128]{2,1,0:T(8,128)S(1)} %get-tuple-element.69.own, bf16[1,80,128]{2,1,0:T(8,128)(2,1)S(1)} %bitcast.37, bf16[1,80,128]{2,1,0:T(8,128)(2,1)S(1)} %bitcast.38, f32[1,16,128]{2,1,0:T(8,128)S(1)} %bitcast.39, ...), custom_call_target="tpu_custom_call" | custom-call | flops 67108864 | bytes 3145728 | tf_op jit(solution)/shard_map/pallas_call | solution.py:105
  43.1 10.3 %all_to_all.11.stats = f32[16,2,256]{2,1,0:T(2,128)S(1)} all-to-all(f32[16,2,256]{2,1,0:T(2,128)S(1)} %get-tuple-element.75), channel_id=1, replica_groups=mesh['cand'=2,'gz'=4,'yx'=4] {'gz','yx'}, dimensions={0} | all-to-all | bytes 65536 | tf_op jit(solution)/shard_map/all_to_all | solution.py:98
  53.4 0.0 copy-done
  53.4 0.0 copy-done.1
  53.4 0.0 copy-done.2
  53.4 1.5 %shard_map.95 = bf16[16,16,16,128]{3,2,1,0:T(8,128)(2,1)} custom-call(f32[2,512,128]{2,1,0:T(8,128)S(1)} %get-tuple-element.74.act, f32[16,2,256]{2,1,0:T(2,128)S(1)} %all_to_all.11.stats, f32[1,256]{1,0:T(1,128)S(1)} %bitcast.40, f32[1,256]{1,0:T(1,128)S(1)} %bitcast.41, bf16[256,128]{1,0:T(8,128)(2,1)S(1)} %copy-done, ...), custom_call_target="tpu_custom_call" | custom-call | flops 67108864 | bytes 3145728 | tf_op jit(solution)/shard_map/pallas_call | solution.py:105
  (2 shorter events, 0.1 us)
Async XLA Ops:
  1.6 10.5 %collective-permute-start.2 = (bf16[15,16,128]{2,1,0:T(8,128)(2,1)S(1)}, bf16[15,16,128]{2,1,0:T(8,128)(2,1)S(1)}, u32[]{:S(2)}, u32[]{:S(2)}) collective-permute-start(bf16[15,16,128]{2,1,0:T(8,128)(2,1)S(1)} %bitcast.46), channel_id=1, source_target_pairs={{0,3},{1,2},{2,1},{3,0},{4,7},{5,6},{6,5},{7,4},{8,11},{9,10},{10,... | collective-permute-start | bytes 184328 | tf_op jit(solution)/shard_map/ppermute | solution.py:46
  6.7 6.8 %collective-permute-start.1 = (bf16[30,16,128]{2,1,0:T(8,128)(2,1)S(1)}, bf16[30,16,128]{2,1,0:T(8,128)(2,1)S(1)}, u32[]{:S(2)}, u32[]{:S(2)}) collective-permute-start(bf16[30,16,128]{2,1,0:T(8,128)(2,1)S(1)} %bitcast.45), channel_id=1, source_target_pairs={{0,1},{1,0},{2,3},{3,2},{4,5},{5,4},{6,7},{7,6},{8,9},{9,8},{10,11... | collective-permute-start | bytes 368648 | tf_op jit(solution)/shard_map/ppermute | solution.py:45
  6.7 8.4 %collective-permute-start = (bf16[30,16,128]{2,1,0:T(8,128)(2,1)S(1)}, bf16[30,16,128]{2,1,0:T(8,128)(2,1)S(1)}, u32[]{:S(2)}, u32[]{:S(2)}) collective-permute-start(bf16[30,16,128]{2,1,0:T(8,128)(2,1)S(1)} %bitcast.44), channel_id=1, source_target_pairs={{0,2},{1,3},{2,0},{3,1},{4,6},{5,7},{6,4},{7,5},{8,10},{9,11},{10,... | collective-permute-start | bytes 368648 | tf_op jit(solution)/shard_map/ppermute | solution.py:44
  15.2 7.1 %collective-permute-start.4 = (bf16[57,16,128]{2,1,0:T(8,128)(2,1)S(1)}, bf16[57,16,128]{2,1,0:T(8,128)(2,1)S(1)}, u32[]{:S(2)}, u32[]{:S(2)}) collective-permute-start(bf16[57,16,128]{2,1,0:T(8,128)(2,1)S(1)} %get-tuple-element.57), channel_id=1, source_target_pairs={{4,8},{8,4},{5,9},{9,5},{6,10},{10,6},{7,11},{11,7},{20,24},{24,20... | collective-permute-start | bytes 700424 | tf_op jit(solution)/shard_map/ppermute | solution.py:63
  15.8 7.1 %collective-permute-start.5 = (bf16[1,4,14,16,128]{4,3,2,1,0:T(8,128)(2,1)S(1)}, bf16[1,4,14,16,128]{4,3,2,1,0:T(8,128)(2,1)S(1)}, u32[]{:S(2)}, u32[]{:S(2)}) collective-permute-start(bf16[1,4,14,16,128]{4,3,2,1,0:T(8,128)(2,1)S(1)} %bitcast.35), channel_id=1, source_target_pairs={{0,16},{16,0},{1,17},{17,1},{2,18},{18,2},{3,19},{19,3},{4,20},{20... | collective-permute-start | bytes 688136 | tf_op jit(solution)/shard_map/ppermute | solution.py:94
  17.5 3.7 %collective-permute-start.3 = (bf16[55,16,128]{2,1,0:T(8,128)(2,1)S(1)}, bf16[55,16,128]{2,1,0:T(8,128)(2,1)S(1)}, u32[]{:S(2)}, u32[]{:S(2)}) collective-permute-start(bf16[55,16,128]{2,1,0:T(8,128)(2,1)S(1)} %get-tuple-element.55), channel_id=1, source_target_pairs={{0,4},{4,0},{8,12},{12,8},{1,5},{5,1},{9,13},{13,9},{2,6},{6,2},{1... | collective-permute-start | bytes 675848 | tf_op jit(solution)/shard_map/ppermute | solution.py:63
  23.0 11.5 %collective-permute-start.6 = (bf16[2,3,14,16,128]{4,3,2,1,0:T(8,128)(2,1)S(1)}, bf16[2,3,14,16,128]{4,3,2,1,0:T(8,128)(2,1)S(1)}, u32[]{:S(2)}, u32[]{:S(2)}) collective-permute-start(bf16[2,3,14,16,128]{4,3,2,1,0:T(8,128)(2,1)S(1)} %bitcast.27), channel_id=1, source_target_pairs={{0,8},{4,12},{8,0},{12,4},{1,9},{5,13},{9,1},{13,5},{2,10},{6,14},... | collective-permute-start | bytes 1032200 | tf_op jit(solution)/shard_map/ppermute | solution.py:94
  24.8 9.9 %copy-start.3 = (f32[128]{0:T(128)S(1)}, f32[128]{0:T(128)}, u32[]{:S(2)}) copy-start(f32[128]{0:T(128)} %param.10) | copy-start | bytes 1540
  24.8 9.9 %copy-start.4 = (f32[128]{0:T(128)S(1)}, f32[128]{0:T(128)}, u32[]{:S(2)}) copy-start(f32[128]{0:T(128)} %param.11) | copy-start | bytes 1540
  34.5 5.8 %collective-permute-start.7 = (bf16[4,3,14,16,128]{4,3,2,1,0:T(8,128)(2,1)S(1)}, bf16[4,3,14,16,128]{4,3,2,1,0:T(8,128)(2,1)S(1)}, u32[]{:S(2)}, u32[]{:S(2)}) collective-permute-start(bf16[4,3,14,16,128]{4,3,2,1,0:T(8,128)(2,1)S(1)} %bitcast.24), channel_id=1, source_target_pairs={{0,4},{4,0},{8,12},{12,8},{1,5},{5,1},{9,13},{13,9},{2,6},{6,2},{1... | collective-permute-start | bytes 2064392 | tf_op jit(solution)/shard_map/ppermute | solution.py:94
  35.9 6.0 %collective-permute-start.10 = (f32[16,128]{1,0:T(8,128)S(1)}, f32[16,128]{1,0:T(8,128)S(1)}, u32[]{:S(2)}, u32[]{:S(2)}) collective-permute-start(f32[16,128]{1,0:T(8,128)S(1)} %bitcast.49), channel_id=1, source_target_pairs={{0,3},{1,2},{2,1},{3,0},{4,7},{5,6},{6,5},{7,4},{8,11},{9,10},{10,... | collective-permute-start | bytes 24584 | tf_op jit(solution)/shard_map/ppermute | solution.py:46
  36.6 5.3 %collective-permute-start.8 = (bf16[80,128]{1,0:T(8,128)(2,1)S(1)}, bf16[80,128]{1,0:T(8,128)(2,1)S(1)}, u32[]{:S(2)}, u32[]{:S(2)}) collective-permute-start(bf16[80,128]{1,0:T(8,128)(2,1)S(1)} %bitcast.48), channel_id=1, source_target_pairs={{0,1},{1,0},{2,3},{3,2},{4,5},{5,4},{6,7},{7,6},{8,9},{9,8},{10,11... | collective-permute-start | bytes 61448 | tf_op jit(solution)/shard_map/ppermute | solution.py:45
  37.7 4.7 %collective-permute-start.9 = (bf16[80,128]{1,0:T(8,128)(2,1)S(1)}, bf16[80,128]{1,0:T(8,128)(2,1)S(1)}, u32[]{:S(2)}, u32[]{:S(2)}) collective-permute-start(bf16[80,128]{1,0:T(8,128)(2,1)S(1)} %bitcast.47), channel_id=1, source_target_pairs={{0,2},{1,3},{2,0},{3,1},{4,6},{5,7},{6,4},{7,5},{8,10},{9,11},{10,... | collective-permute-start | bytes 61448 | tf_op jit(solution)/shard_map/ppermute | solution.py:44
  41.9 11.6 %copy-start = (bf16[256,128]{1,0:T(8,128)(2,1)S(1)}, bf16[256,128]{1,0:T(8,128)(2,1)}, u32[]{:S(2)}) copy-start(bf16[256,128]{1,0:T(8,128)(2,1)} %up.1) | copy-start | bytes 196612
  41.9 11.5 %copy-start.1 = (f32[256]{0:T(256)S(1)}, f32[256]{0:T(256)}, u32[]{:S(2)}) copy-start(f32[256]{0:T(256)} %param.13) | copy-start | bytes 3076
  41.9 11.5 %copy-start.2 = (f32[256]{0:T(256)S(1)}, f32[256]{0:T(256)}, u32[]{:S(2)}) copy-start(f32[256]{0:T(256)} %param.14) | copy-start | bytes 3076
